TPU v7x, 32 devices: a whole 2x2x4 slice. The times are simulated.
32 devices in a mesh: dom: 32 (over z, y, x, core).
Axes of the slice: x: 2, y: 2, z: 4, core: 2. Of those that a mesh axis runs over, the one named last changes fastest.
Arguments:
- strips: float32 [16384, 256], P('dom')
- columns: int32 [256, 4], P('dom'), may hold values from 0 to 39, as said below
- send_list: int32 [32, 4, 8], P('dom'), may hold values from 0 to 7, each once within a row
- send_count: int32 [32, 4], P('dom'), may hold values from 1 to 8, as said below
- shifts: float32 [4], replicated, may hold values from 0.25 to 1
- prev_basis: float32 [3, 32, 16384], P(None, None, 'dom')
- mix: float32 [3, 32], replicated, may hold values from -1 to 1
Outputs:
- new_basis: float32 [3, 4, 16384], P(None, None, 'dom')
- factors: float32 [3, 36, 4], replicated
Inputs may be any that keep to these rules, and one draw needn't show every extreme that they name: `columns`: entry 0 of block row r of a partition is r itself. An entry e below 8 names the partition's own block row e; an entry e of 8 or more names ghost slot (e - 8) % 8 of link (e - 8) // 8. `send_count`: slot j of a link carries data when j is below the sender's count for that link, zeros otherwise. `send_list`: each partition's list for one link names each of its 8 block rows once.
All inputs are finite; a program needn't handle non-finite values.
Results may differ from a plain program's by a relative error of at most 0.013.
Values sent between devices are 32-bit elements; how exact they have to be, the bound alone decides.
No kernel may reach another device: no remote copies, remote signals or barrier semaphores. Data moves between devices by JAX's collectives and lax.ppermute only.
A program may use at most 64 MiB of HBM per device.

v0:
```python
import jax
import jax.numpy as jnp
from jax import lax
from jax.sharding import PartitionSpec as P

BLOCK = 64
S = 4


link_steps = (1, -1, 8, -8)


def shifted(shard, axis, by):
    length = lax.axis_size(axis)
    pairs = [(i, i + by) for i in range(length) if 0 <= i + by < length]
    return lax.ppermute(shard, axis, pairs)


def local(strips, columns, send_list, send_count, shifts, prev_basis, mix):
    comps, count_prev, rows = prev_basis.shape
    blocks = columns.shape[0]
    width = strips.shape[1]
    matrix = strips.reshape(blocks, BLOCK, width)
    flat_columns = columns.reshape(-1)
    slots = jnp.arange(blocks, dtype=jnp.int32)
    start = jnp.einsum("cp,cpn->cn", mix, prev_basis, precision=lax.Precision.HIGHEST)
    vec = start.reshape(comps, blocks, BLOCK)
    vectors = []
    for step in range(S):
        received = []
        for link, fetch_step in enumerate(link_steps):
            packed = jnp.take(vec, send_list[0, link], axis=1)
            live = slots[None, :, None] < send_count[0, link]
            packed = jnp.where(live, packed, jnp.zeros_like(packed)).reshape(comps, blocks * BLOCK)
            moved = shifted(packed, "dom", fetch_step)
            received.append(moved.reshape(comps, blocks, BLOCK))
        ghosts = jnp.concatenate(received, axis=1)
        picked = jnp.take(jnp.concatenate([vec, ghosts], axis=1), flat_columns, axis=1).reshape(
            comps, blocks, width
        )
        image = jnp.einsum("rik,crk->cri", matrix, picked, precision=lax.Precision.HIGHEST)
        vec = image - shifts[step] * vec
        vectors.append(vec.reshape(comps, rows))
    basis = jnp.stack(vectors, axis=1)
    total = float(lax.axis_size("dom") * rows)
    partial_value = jnp.einsum("cpn,csn->cps", prev_basis, basis, precision=lax.Precision.HIGHEST)
    coef = lax.psum(partial_value, "dom") / total
    projected = basis - jnp.einsum(
        "cps,cpn->csn", coef, prev_basis, precision=lax.Precision.HIGHEST
    )
    local_gram = jnp.einsum("csn,ctn->cst", projected, projected, precision=lax.Precision.HIGHEST)
    gram = lax.psum(local_gram, "dom") / total
    lower = jnp.linalg.cholesky(gram)
    new_basis = lax.linalg.triangular_solve(lower, projected, left_side=True, lower=True)
    factors = jnp.concatenate([coef, jnp.swapaxes(lower, 1, 2)], axis=1)
    return (new_basis, factors)


def solution(mesh):
    in_specs = (
        P("dom", None),
        P("dom", None),
        P("dom", None, None),
        P("dom", None),
        P(),
        P(None, None, "dom"),
        P(),
    )
    out_specs = (P(None, None, "dom"), P())
    return jax.shard_map(local, mesh=mesh, in_specs=in_specs, out_specs=out_specs, check_vma=False)
```

profile of v0, /device:TPU:0, one launch (start us, length us, event | category | flops | bytes accessed | tf_op | source)
XLA Modules:
  0.0 175.6 jit_solution(3281067117631960281)
XLA Ops:
  0.6 1.4 fusion.17
  2.1 0.6 iota_compare_fusion.5
  2.8 0.7 copy-done.5
  3.4 1.1 fusion.12
  4.7 0.6 gather_fusion
  5.4 2.3 %collective-permute-start = (f32[3,512]{1,0:T(4,128)S(1)}, f32[3,512]{1,0:T(4,128)S(1)}, u32[]{:S(2)}, u32[]{:S(2)}) collective-permute-start(f32[3,512]{1,0:T(4,128)S(1)} %reshape.162), channel_id=1, source_target_pairs={{0,1},{1,2},{2,3},{3,4},{4,5},{5,6},{6,7},{7,8},{8,9},{9,10},{10,1... | collective-permute-start | bytes 18440 | tf_op jit(solution)/shard_map/ppermute | solution.py:16
  7.8 0.7 iota_compare_fusion.2
  8.5 0.6 gather_fusion.3
  9.2 1.3 collective-permute-start.3
  10.5 0.7 iota_compare_fusion.4
  11.2 0.6 gather_fusion.1
  11.9 1.3 collective-permute-start.1
  13.2 0.6 iota_compare_fusion.3
  13.9 0.6 gather_fusion.2
  14.6 8.6 %collective-permute-start.2 = (f32[3,512]{1,0:T(4,128)S(1)}, f32[3,512]{1,0:T(4,128)S(1)}, u32[]{:S(2)}, u32[]{:S(2)}) collective-permute-start(f32[3,512]{1,0:T(4,128)S(1)} %reshape.166), channel_id=1, source_target_pairs={{0,8},{1,9},{2,10},{3,11},{4,12},{5,13},{6,14},{7,15},{8,16},{9,17... | collective-permute-start | bytes 18440 | tf_op jit(solution)/shard_map/ppermute | solution.py:16
  23.5 0.6 copy-done.2
  24.1 0.6 fusion.16
  25.2 0.6 gather_fusion.4
  26.0 1.1 constant_dynamic-update-slice_fusion.9
  27.1 0.6 gather_fusion.8
  27.6 0.6 gather_fusion.7
  28.2 0.6 gather_fusion.6
  28.8 0.6 gather_fusion.5
  29.7 1.3 collective-permute-start.4
  31.4 1.3 collective-permute-start.5
  32.7 9.0 %collective-permute-start.6 = (f32[3,512]{1,0:T(4,128)S(1)}, f32[3,512]{1,0:T(4,128)S(1)}, u32[]{:S(2)}, u32[]{:S(2)}) collective-permute-start(f32[3,512]{1,0:T(4,128)S(1)} %reshape.177), channel_id=1, source_target_pairs={{0,8},{1,9},{2,10},{3,11},{4,12},{5,13},{6,14},{7,15},{8,16},{9,17... | collective-permute-start | bytes 18440 | tf_op jit(solution)/shard_map/ppermute | solution.py:16
  41.8 1.3 collective-permute-start.7
  43.4 3.9 %collective-permute-done.7 = f32[3,512]{1,0:T(4,128)S(1)} collective-permute-done((f32[3,512]{1,0:T(4,128)S(1)}, f32[3,512]{1,0:T(4,128)S(1)}, u32[]{:S(2)}, u32[]{:S(2)}) %collective-permute-start.7) | collective-permute-done | bytes 6176 | tf_op jit(solution)/shard_map/ppermute | solution.py:16
  47.4 0.6 gather_fusion.9
  48.2 1.2 constant_dynamic-update-slice_fusion.14
  49.4 0.6 gather_fusion.13
  50.0 0.6 gather_fusion.12
  50.6 0.6 gather_fusion.11
  51.1 0.6 gather_fusion.10
  52.1 1.3 collective-permute-start.8
  53.8 1.3 collective-permute-start.9
  55.1 8.6 %collective-permute-start.10 = (f32[3,512]{1,0:T(4,128)S(1)}, f32[3,512]{1,0:T(4,128)S(1)}, u32[]{:S(2)}, u32[]{:S(2)}) collective-permute-start(f32[3,512]{1,0:T(4,128)S(1)} %reshape.186), channel_id=1, source_target_pairs={{0,8},{1,9},{2,10},{3,11},{4,12},{5,13},{6,14},{7,15},{8,16},{9,17... | collective-permute-start | bytes 18440 | tf_op jit(solution)/shard_map/ppermute | solution.py:16
  63.7 1.3 collective-permute-start.11
  65.3 3.9 %collective-permute-done.11 = f32[3,512]{1,0:T(4,128)S(1)} collective-permute-done((f32[3,512]{1,0:T(4,128)S(1)}, f32[3,512]{1,0:T(4,128)S(1)}, u32[]{:S(2)}, u32[]{:S(2)}) %collective-permute-start.11) | collective-permute-done | bytes 6176 | tf_op jit(solution)/shard_map/ppermute | solution.py:16
  69.4 0.6 gather_fusion.14
  70.2 1.1 constant_dynamic-update-slice_fusion.19
  71.3 0.6 gather_fusion.18
  71.9 0.6 gather_fusion.17
  72.5 0.6 gather_fusion.16
  73.0 0.6 gather_fusion.15
  73.6 0.1 bitcast_select_fusion.2
  73.8 1.3 collective-permute-start.12
  75.6 1.3 collective-permute-start.13
  76.9 8.3 %collective-permute-start.14 = (f32[3,512]{1,0:T(4,128)S(1)}, f32[3,512]{1,0:T(4,128)S(1)}, u32[]{:S(2)}, u32[]{:S(2)}) collective-permute-start(f32[3,512]{1,0:T(4,128)S(1)} %reshape.195), channel_id=1, source_target_pairs={{0,8},{1,9},{2,10},{3,11},{4,12},{5,13},{6,14},{7,15},{8,16},{9,17... | collective-permute-start | bytes 18440 | tf_op jit(solution)/shard_map/ppermute | solution.py:16
  85.1 1.3 collective-permute-start.15
  86.7 3.9 %collective-permute-done.15 = f32[3,512]{1,0:T(4,128)S(1)} collective-permute-done((f32[3,512]{1,0:T(4,128)S(1)}, f32[3,512]{1,0:T(4,128)S(1)}, u32[]{:S(2)}, u32[]{:S(2)}) %collective-permute-start.15) | collective-permute-done | bytes 6176 | tf_op jit(solution)/shard_map/ppermute | solution.py:16
  90.8 0.6 gather_fusion.19
  91.6 1.2 fusion
  92.9 0.3 convolution_bitcast_fusion.4
  93.1 37.8 %psum.14 = f32[3,32,4]{1,2,0:T(4,128)S(1)} all-reduce(f32[3,32,4]{1,2,0:T(4,128)S(1)} %convolution_bitcast_fusion.4), channel_id=1, replica_groups=mesh['dom'=32] {'dom'}, use_global_device_ids=true, to_apply=%region_0.3 | all-reduce | flops 384 | bytes 3072 | tf_op jit(solution)/shard_map/psum | solution.py:47
  131.0 0.2 convolution_subtract_fusion
  131.2 0.2 fusion.18
  131.4 40.2 %psum.15 = f32[3,4,4]{1,2,0:T(4,128)S(1)} all-reduce(f32[3,4,4]{1,2,0:T(4,128)S(1)} %fusion.18), channel_id=1, replica_groups=mesh['dom'=32] {'dom'}, use_global_device_ids=true, to_apply=%region_1.4 | all-reduce | flops 48 | bytes 384 | tf_op jit(solution)/shard_map/psum | solution.py:52
  171.6 0.1 copy.178
  171.7 1.1 custom-call.7
  172.9 0.1 compare_reduce_fusion
  173.1 1.0 custom-call.8
  174.1 0.9 fusion.8
  174.9 0.7 pad_maximum_fusion.1
  (140 shorter events, 5.6 us)
Async XLA Ops:
  0.6 25.3 %copy-start = (f32[512,256]{1,0:T(8,128)S(1)}, f32[512,256]{1,0:T(8,128)}, u32[]{:S(2)}) copy-start(f32[512,256]{1,0:T(8,128)} %param.11) | copy-start | bytes 1572868
  2.1 0.7 copy-start.3
  2.7 0.7 copy-start.5
  5.4 19.3 %collective-permute-start = (f32[3,512]{1,0:T(4,128)S(1)}, f32[3,512]{1,0:T(4,128)S(1)}, u32[]{:S(2)}, u32[]{:S(2)}) collective-permute-start(f32[3,512]{1,0:T(4,128)S(1)} %reshape.162), channel_id=1, source_target_pairs={{0,1},{1,2},{2,3},{3,4},{4,5},{5,6},{6,7},{7,8},{8,9},{9,10},{10,1... | collective-permute-start | bytes 18440 | tf_op jit(solution)/shard_map/ppermute | solution.py:16
  9.2 15.8 %collective-permute-start.3 = (f32[3,512]{1,0:T(4,128)S(1)}, f32[3,512]{1,0:T(4,128)S(1)}, u32[]{:S(2)}, u32[]{:S(2)}) collective-permute-start(f32[3,512]{1,0:T(4,128)S(1)} %reshape.168), channel_id=1, source_target_pairs={{8,0},{9,1},{10,2},{11,3},{12,4},{13,5},{14,6},{15,7},{16,8},{17,9... | collective-permute-start | bytes 18440 | tf_op jit(solution)/shard_map/ppermute | solution.py:16
  11.9 12.9 %collective-permute-start.1 = (f32[3,512]{1,0:T(4,128)S(1)}, f32[3,512]{1,0:T(4,128)S(1)}, u32[]{:S(2)}, u32[]{:S(2)}) collective-permute-start(f32[3,512]{1,0:T(4,128)S(1)} %reshape.164), channel_id=1, source_target_pairs={{1,0},{2,1},{3,2},{4,3},{5,4},{6,5},{7,6},{8,7},{9,8},{10,9},{11,1... | collective-permute-start | bytes 18440 | tf_op jit(solution)/shard_map/ppermute | solution.py:16
  14.5 8.7 %copy-start.4 = (s32[8,4]{0,1:T(4,128)S(1)}, s32[8,4]{0,1:T(4,128)}, u32[]{:S(2)}) copy-start(s32[8,4]{0,1:T(4,128)} %param.12) | copy-start | bytes 388
  14.6 10.3 %collective-permute-start.2 = (f32[3,512]{1,0:T(4,128)S(1)}, f32[3,512]{1,0:T(4,128)S(1)}, u32[]{:S(2)}, u32[]{:S(2)}) collective-permute-start(f32[3,512]{1,0:T(4,128)S(1)} %reshape.166), channel_id=1, source_target_pairs={{0,8},{1,9},{2,10},{3,11},{4,12},{5,13},{6,14},{7,15},{8,16},{9,17... | collective-permute-start | bytes 18440 | tf_op jit(solution)/shard_map/ppermute | solution.py:16
  23.5 0.7 copy-start.2
  29.7 13.4 %collective-permute-start.4 = (f32[3,512]{1,0:T(4,128)S(1)}, f32[3,512]{1,0:T(4,128)S(1)}, u32[]{:S(2)}, u32[]{:S(2)}) collective-permute-start(f32[3,512]{1,0:T(4,128)S(1)} %reshape.173), channel_id=1, source_target_pairs={{0,1},{1,2},{2,3},{3,4},{4,5},{5,6},{6,7},{7,8},{8,9},{9,10},{10,1... | collective-permute-start | bytes 18440 | tf_op jit(solution)/shard_map/ppermute | solution.py:16
  31.4 11.8 %collective-permute-start.5 = (f32[3,512]{1,0:T(4,128)S(1)}, f32[3,512]{1,0:T(4,128)S(1)}, u32[]{:S(2)}, u32[]{:S(2)}) collective-permute-start(f32[3,512]{1,0:T(4,128)S(1)} %reshape.175), channel_id=1, source_target_pairs={{1,0},{2,1},{3,2},{4,3},{5,4},{6,5},{7,6},{8,7},{9,8},{10,9},{11,1... | collective-permute-start | bytes 18440 | tf_op jit(solution)/shard_map/ppermute | solution.py:16
  32.7 10.6 %collective-permute-start.6 = (f32[3,512]{1,0:T(4,128)S(1)}, f32[3,512]{1,0:T(4,128)S(1)}, u32[]{:S(2)}, u32[]{:S(2)}) collective-permute-start(f32[3,512]{1,0:T(4,128)S(1)} %reshape.177), channel_id=1, source_target_pairs={{0,8},{1,9},{2,10},{3,11},{4,12},{5,13},{6,14},{7,15},{8,16},{9,17... | collective-permute-start | bytes 18440 | tf_op jit(solution)/shard_map/ppermute | solution.py:16
  41.8 5.5 %collective-permute-start.7 = (f32[3,512]{1,0:T(4,128)S(1)}, f32[3,512]{1,0:T(4,128)S(1)}, u32[]{:S(2)}, u32[]{:S(2)}) collective-permute-start(f32[3,512]{1,0:T(4,128)S(1)} %reshape.179), channel_id=1, source_target_pairs={{8,0},{9,1},{10,2},{11,3},{12,4},{13,5},{14,6},{15,7},{16,8},{17,9... | collective-permute-start | bytes 18440 | tf_op jit(solution)/shard_map/ppermute | solution.py:16
  52.1 12.9 %collective-permute-start.8 = (f32[3,512]{1,0:T(4,128)S(1)}, f32[3,512]{1,0:T(4,128)S(1)}, u32[]{:S(2)}, u32[]{:S(2)}) collective-permute-start(f32[3,512]{1,0:T(4,128)S(1)} %reshape.182), channel_id=1, source_target_pairs={{0,1},{1,2},{2,3},{3,4},{4,5},{5,6},{6,7},{7,8},{8,9},{9,10},{10,1... | collective-permute-start | bytes 18440 | tf_op jit(solution)/shard_map/ppermute | solution.py:16
  53.8 11.3 %collective-permute-start.9 = (f32[3,512]{1,0:T(4,128)S(1)}, f32[3,512]{1,0:T(4,128)S(1)}, u32[]{:S(2)}, u32[]{:S(2)}) collective-permute-start(f32[3,512]{1,0:T(4,128)S(1)} %reshape.184), channel_id=1, source_target_pairs={{1,0},{2,1},{3,2},{4,3},{5,4},{6,5},{7,6},{8,7},{9,8},{10,9},{11,1... | collective-permute-start | bytes 18440 | tf_op jit(solution)/shard_map/ppermute | solution.py:16
  55.1 10.1 %collective-permute-start.10 = (f32[3,512]{1,0:T(4,128)S(1)}, f32[3,512]{1,0:T(4,128)S(1)}, u32[]{:S(2)}, u32[]{:S(2)}) collective-permute-start(f32[3,512]{1,0:T(4,128)S(1)} %reshape.186), channel_id=1, source_target_pairs={{0,8},{1,9},{2,10},{3,11},{4,12},{5,13},{6,14},{7,15},{8,16},{9,17... | collective-permute-start | bytes 18440 | tf_op jit(solution)/shard_map/ppermute | solution.py:16
  63.7 5.5 %collective-permute-start.11 = (f32[3,512]{1,0:T(4,128)S(1)}, f32[3,512]{1,0:T(4,128)S(1)}, u32[]{:S(2)}, u32[]{:S(2)}) collective-permute-start(f32[3,512]{1,0:T(4,128)S(1)} %reshape.188), channel_id=1, source_target_pairs={{8,0},{9,1},{10,2},{11,3},{12,4},{13,5},{14,6},{15,7},{16,8},{17,9... | collective-permute-start | bytes 18440 | tf_op jit(solution)/shard_map/ppermute | solution.py:16
  73.8 12.6 %collective-permute-start.12 = (f32[3,512]{1,0:T(4,128)S(1)}, f32[3,512]{1,0:T(4,128)S(1)}, u32[]{:S(2)}, u32[]{:S(2)}) collective-permute-start(f32[3,512]{1,0:T(4,128)S(1)} %reshape.191), channel_id=1, source_target_pairs={{0,1},{1,2},{2,3},{3,4},{4,5},{5,6},{6,7},{7,8},{8,9},{9,10},{10,1... | collective-permute-start | bytes 18440 | tf_op jit(solution)/shard_map/ppermute | solution.py:16
  75.6 11.0 %collective-permute-start.13 = (f32[3,512]{1,0:T(4,128)S(1)}, f32[3,512]{1,0:T(4,128)S(1)}, u32[]{:S(2)}, u32[]{:S(2)}) collective-permute-start(f32[3,512]{1,0:T(4,128)S(1)} %reshape.193), channel_id=1, source_target_pairs={{1,0},{2,1},{3,2},{4,3},{5,4},{6,5},{7,6},{8,7},{9,8},{10,9},{11,1... | collective-permute-start | bytes 18440 | tf_op jit(solution)/shard_map/ppermute | solution.py:16
  76.9 9.8 %collective-permute-start.14 = (f32[3,512]{1,0:T(4,128)S(1)}, f32[3,512]{1,0:T(4,128)S(1)}, u32[]{:S(2)}, u32[]{:S(2)}) collective-permute-start(f32[3,512]{1,0:T(4,128)S(1)} %reshape.195), channel_id=1, source_target_pairs={{0,8},{1,9},{2,10},{3,11},{4,12},{5,13},{6,14},{7,15},{8,16},{9,17... | collective-permute-start | bytes 18440 | tf_op jit(solution)/shard_map/ppermute | solution.py:16
  85.1 5.5 %collective-permute-start.15 = (f32[3,512]{1,0:T(4,128)S(1)}, f32[3,512]{1,0:T(4,128)S(1)}, u32[]{:S(2)}, u32[]{:S(2)}) collective-permute-start(f32[3,512]{1,0:T(4,128)S(1)} %reshape.197), channel_id=1, source_target_pairs={{8,0},{9,1},{10,2},{11,3},{12,4},{13,5},{14,6},{15,7},{16,8},{17,9... | collective-permute-start | bytes 18440 | tf_op jit(solution)/shard_map/ppermute | solution.py:16
  91.6 1.3 copy-start.1
where the time goes:
time: 176 us
  blocking collectives  78 us (44%)
  starting transfers between devices  51 us (29%)
  local copies, waits for them, and re-layouts  18.9 us (11%)
  waiting for transfers between devices  11.8 us (7%)
  matrix products  7.28 us (4%)
  other arithmetic  7.22 us (4%)
    ppermute x16, starting transfers between devices, shifted(): return lax.ppermute(shard, axis, pairs)  51 us
    psum x1, blocking collectives, local(): gram = lax.psum(local_gram, 'dom') / total  40.2 us
    psum x1, blocking collectives, local(): coef = lax.psum(partial_value, 'dom') / total  37.8 us
    ppermute x16, waiting for transfers between devices, shifted(): return lax.ppermute(shard, axis, pairs)  11.8 us
    gather x16, local copies, waits for them, and re-layouts, local(): packed = jnp.take(vec, send_list[0, link], axis=1)  9.23 us
    dot_general x4, matrix products, local(): jnp.einsum('rik,crk->cri', matrix, picked, precision=lax.Precision.HIGHEST)  4.59 us
  transfers between devices with their start and end apart: 16, of which 3 were waited for; matrix products, arithmetic and copies ran while one was open for 4% of the time, Pallas kernels for 0%

commit v1 on v0

v1 whole, which is shorter than its diff:
```python
import jax
import jax.numpy as jnp
from jax import lax
from jax.experimental import pallas as pl
from jax.experimental.pallas import tpu as pltpu
from jax.sharding import PartitionSpec as P

BLOCK = 64
S = 4
FAR = 8
DEAD = 1000.0
HIGHEST = lax.Precision.HIGHEST
NN = (((1,), (0,)), ((), ()))
NT = (((1,), (1,)), ((), ()))


def dot(a, b, dims=NN, precision=None):
    return lax.dot_general(a, b, dims, precision=precision, preferred_element_type=jnp.float32)


def iota(shape, axis):
    return lax.broadcasted_iota(jnp.int32, shape, axis)


def split(x):
    high = x.astype(jnp.bfloat16)
    return high, (x - high.astype(jnp.float32)).astype(jnp.bfloat16)


def own_lanes(blocks):
    shape = (blocks, blocks * BLOCK)
    return iota(shape, 1) // BLOCK == iota(shape, 0)


def fold(masked):
    total = masked[:, :128]
    for t in range(1, masked.shape[1] // 128):
        total = total + masked[:, t * 128 : (t + 1) * 128]
    return total + pltpu.roll(total, BLOCK, 1)


def doubled(tile, comp):
    part = tile[:, (comp // 2) * 128 : (comp // 2 + 1) * 128]
    turned = pltpu.roll(part, BLOCK, 1)
    low = iota(part.shape, 1) < BLOCK
    return jnp.where(low, part, turned) if comp % 2 == 0 else jnp.where(low, turned, part)


def joined(parts, tail):
    low = iota(parts[0].shape, 1) < BLOCK
    return jnp.concatenate([jnp.where(low, parts[0], parts[1]), jnp.where(low, parts[2], tail)], axis=1)


def start_kernel(prev_ref, mix_ref, list_ref, count_ref, out_ref):
    comps, vecs, rows = prev_ref.shape
    blocks = rows // BLOCK
    prev = prev_ref[...].reshape(comps * vecs, rows)
    mix = jnp.concatenate([mix_ref[...]] * comps, axis=1)
    mix = jnp.where(iota(mix.shape, 1) // vecs == iota(mix.shape, 0), mix, 0.0)
    start = dot(mix, prev, precision=HIGHEST)
    own = own_lanes(blocks)
    parts = [
        fold(jnp.where(own, jnp.broadcast_to(start[c : c + 1], own.shape), 0.0)) for c in range(comps)
    ]
    square = (blocks, blocks)
    tail = jnp.zeros((blocks, 128), jnp.float32)
    for link in range(4):
        order = jnp.broadcast_to(list_ref[0, link : link + 1, :], square)
        live = iota(square, 1) < jnp.broadcast_to(count_ref[0:1, link : link + 1], square)
        order = jnp.where(live, order.astype(jnp.float32), DEAD)
        column = jnp.sum(jnp.where(iota(square, 0) == iota(square, 1), order, 0.0), axis=1, keepdims=True)
        tail = jnp.where(iota(tail.shape, 1) == BLOCK + link, column, tail)
    out_ref[...] = joined(parts, tail)


def prepare_kernel(strips_ref, high_ref, low_ref):
    high, low = split(strips_ref[...].T)
    high_ref[...] = high
    low_ref[...] = low


def previous_gram_kernel(prev_ref, out_ref):
    comps, vecs, rows = prev_ref.shape
    prev = prev_ref[...].reshape(comps * vecs, rows)
    full = dot(prev, prev, NT, HIGHEST)
    owner = iota((vecs, comps * vecs), 1) // vecs
    total = jnp.where(owner == 0, full[:vecs], 0.0)
    for c in range(1, comps):
        total = total + jnp.where(owner == c, full[c * vecs : (c + 1) * vecs], 0.0)
    out_ref[...] = jnp.concatenate([total, jnp.zeros((vecs, 128 - comps * vecs), jnp.float32)], axis=1)


def selection(columns, pieces, place):
    blocks, count = columns.shape
    rows = [(iota((blocks, 128), 0) == iota((blocks, 128), 1)).astype(jnp.float32)]
    even, even_far = lax.rem(place, 2) == 0, lax.rem(place // FAR, 2) == 0
    slots = [
        (jnp.where(even, 2, 1), (pieces[2], pieces[1]), even),
        (jnp.where(even, 1, 2), (pieces[1], pieces[2]), even),
        (jnp.where(even_far, 4, 3), (pieces[4], pieces[3]), even_far),
        (jnp.where(even_far, 3, 4), (pieces[3], pieces[4]), even_far),
    ]
    for link, (slot, (when, other), test) in enumerate(slots):
        lane = 192 + link
        order = jnp.where(test, when[:, lane : lane + 1], other[:, lane : lane + 1])
        at = order.astype(jnp.int32) + slot * blocks
        rows.append((iota((blocks, 128), 1) == at).astype(jnp.float32))
    rows.append(jnp.zeros((128 - 5 * blocks, 128), jnp.float32))
    table = jnp.concatenate(rows, axis=0).astype(jnp.bfloat16)
    picks = [
        (iota((blocks, 128), 1) == columns[:, k : k + 1]).astype(jnp.float32) for k in range(count)
    ]
    return dot(jnp.concatenate(picks, axis=0).astype(jnp.bfloat16), table)


def multiply(choose, pieces, shift, high, low):
    blocks = pieces[0].shape[0]
    count = choose.shape[0] // blocks
    comps = 3
    ext = jnp.concatenate(pieces + [jnp.zeros((128 - 5 * blocks, 256), jnp.float32)], axis=0)
    picked = dot(choose.astype(jnp.bfloat16), jnp.concatenate(split(ext), axis=1))
    halves = []
    for half in range(2):
        for c in range(comps):
            lane = half * 256 + c * BLOCK
            halves.append(
                jnp.concatenate(
                    [picked[k * blocks : (k + 1) * blocks, lane : lane + BLOCK] for k in range(count)],
                    axis=1,
                )
            )
    left = jnp.concatenate(halves, axis=0).astype(jnp.bfloat16)
    both = dot(left, high) + dot(left, low)
    image = both[: comps * blocks] + both[comps * blocks :]
    own = own_lanes(blocks)
    parts, lines = [], []
    for c in range(comps):
        part = fold(jnp.where(own, image[c * blocks : (c + 1) * blocks], 0.0))
        part = part - shift * doubled(pieces[0], c)
        parts.append(part)
        wide = jnp.concatenate([part] * (blocks // 2), axis=1)
        lines.append(jnp.sum(jnp.where(own, wide, 0.0), axis=0, keepdims=True))
    return joined(parts, jnp.zeros_like(parts[0])), lines


def spread(lines, old):
    where = iota(old.shape, 0)
    for c, line in enumerate(lines):
        old = jnp.where(where == c, jnp.broadcast_to(line, old.shape), old)
    return old


def first_kernel(own, a, b, c, d, columns, shifts, high, low, tile_ref, lines_ref, choose_ref):
    pieces = [ref[...] for ref in (own, a, b, c, d)]
    choose = selection(columns[...], pieces, lax.axis_index("dom"))
    choose_ref[...] = choose
    tile, lines = multiply(choose, pieces, shifts[0], high[...], low[...])
    tile_ref[...] = tile
    lines_ref[...] = spread(lines, jnp.zeros(lines_ref.shape, jnp.float32))


def middle_kernel(step, own, a, b, c, d, choose, shifts, high, low, tile_ref, lines_ref):
    pieces = [ref[...] for ref in (own, a, b, c, d)]
    tile, lines = multiply(choose[...], pieces, shifts[step], high[...], low[...])
    tile_ref[...] = tile
    lines_ref[...] = spread(lines, jnp.zeros(lines_ref.shape, jnp.float32))


def last_kernel(
    own, a, b, c, d, choose, shifts, high, low, l0, l1, l2, prev_ref, prev_gram, lines_ref, gram_ref
):
    pieces = [ref[...] for ref in (own, a, b, c, d)]
    _, lines = multiply(choose[...], pieces, shifts[S - 1], high[...], low[...])
    comps, vecs, rows = prev_ref.shape
    last = spread(lines, jnp.zeros(lines_ref.shape, jnp.float32))
    lines_ref[...] = last
    basis = jnp.concatenate([l0[...], l1[...], l2[...], last], axis=0)
    prev = prev_ref[...].reshape(comps * vecs, rows)
    with_prev = dot(basis, prev, NT, HIGHEST)
    with_basis = dot(basis, basis, NT, HIGHEST)
    gram = jnp.concatenate([with_prev, with_basis], axis=1)
    lane = iota((8, 128), 1)
    comp = iota((8, 128), 0)
    mine = jnp.where(lane < comps * vecs, lane // vecs, lax.rem(lane, 8)) == comp
    result = jnp.zeros((8, 128), jnp.float32)
    for k in range(S):
        line = jnp.sum(jnp.where(mine, gram[k * 8 : (k + 1) * 8], 0.0), axis=0, keepdims=True)
        result = jnp.where(comp == k, jnp.broadcast_to(line, result.shape), result)
    gram_ref[...] = jnp.concatenate([prev_gram[...], result], axis=0)


def finish_kernel(total, gram_ref, prev_ref, l0, l1, l2, l3, basis_ref, factors_ref):
    comps, vecs, rows = prev_ref.shape
    width = comps * vecs
    gram = gram_ref[...] * (1.0 / total)
    small = gram[vecs:]
    lane, comp = iota((8, 128), 1), iota((8, 128), 0)
    in_prev = (lane < width) & (lane // vecs == comp)
    coef, cross = [], []
    for k in range(S):
        line = jnp.broadcast_to(small[k : k + 1], (8, 128))
        coef.append(jnp.where(in_prev, line, 0.0))
        cross.append([jnp.where(lane == width + 8 * l + comp, line, 0.0) for l in range(k + 1)])
    coefs = jnp.concatenate(coef, axis=0)
    prev = prev_ref[...].reshape(width, rows)
    basis = jnp.concatenate([l0[...], l1[...], l2[...], l3[...]], axis=0)
    projected = basis - dot(coefs[:, :width], prev, precision=HIGHEST)
    square = jnp.concatenate([gram[:vecs]] * comps, axis=0)
    r, q = iota(square.shape, 0), iota(square.shape, 1)
    square = jnp.where(r // vecs == q // vecs, square, 0.0) - jnp.where(r == q, 2.0, 0.0)
    turned = dot(coefs[:, :width], square, precision=HIGHEST)
    entry = {}
    for k in range(S):
        for l in range(k + 1):
            value = turned[k * 8 : (k + 1) * 8] * coef[l] + cross[k][l]
            entry[k, l] = jnp.sum(value, axis=1, keepdims=True)
    lower = {}
    for k in range(S):
        for l in range(k + 1):
            value = entry[k, l]
            for m in range(l):
                value = value - lower[k, m] * lower[l, m]
            lower[k, l] = jnp.sqrt(value) if l == k else value / lower[l, l]
    vectors = []
    for k in range(S):
        value = projected[k * 8 : (k + 1) * 8]
        for l in range(k):
            value = value - lower[k, l] * vectors[l]
        value = value / lower[k, k]
        vectors.append(value)
        for c in range(comps):
            basis_ref[c, k : k + 1, :] = value[c : c + 1]
    across = jnp.concatenate([small] * 16, axis=0).T
    for c in range(comps):
        factors_ref[c, :vecs, :] = across[c * vecs : (c + 1) * vecs, :S]
    for k in range(S):
        line = jnp.zeros((8, 128), jnp.float32)
        for l in range(k, S):
            line = jnp.where(lane == l, lower[l, k], line)
        for c in range(comps):
            factors_ref[c, vecs + k : vecs + k + 1, :] = line[c : c + 1, :S]


VMEM = pl.BlockSpec(memory_space=pltpu.VMEM)
SMEM = pl.BlockSpec(memory_space=pltpu.SMEM)


def call(kernel, outs, specs, flops, moved):
    shapes = [jax.ShapeDtypeStruct(shape, kind) for shape, kind in outs]
    return pl.pallas_call(
        kernel,
        out_shape=shapes if len(shapes) > 1 else shapes[0],
        in_specs=specs,
        out_specs=[VMEM] * len(shapes) if len(shapes) > 1 else VMEM,
        compiler_params=pltpu.CompilerParams(vmem_limit_bytes=24 * 1024 * 1024),
        cost_estimate=pl.CostEstimate(flops=flops, bytes_accessed=moved, transcendentals=0),
    )


def pairs_of(length, step, odd):
    firsts = [d for d in range(length - step) if (d // step) % 2 == odd]
    return [(d, d + step) for d in firsts] + [(d + step, d) for d in firsts]


def ghosts(tile):
    length = lax.axis_size("dom")
    return [
        lax.ppermute(tile, "dom", pairs_of(length, step, odd)) for step in (1, FAR) for odd in (0, 1)
    ]


def summed(value):
    length = lax.axis_size("dom")
    step = 1
    while step < length:
        value = value + lax.ppermute(value, "dom", [(d, d ^ step) for d in range(length)])
        step *= 2
    return value


def local(strips, columns, send_list, send_count, shifts, prev_basis, mix):
    comps, vecs, rows = prev_basis.shape
    blocks = columns.shape[0]
    width = strips.shape[1]
    f32, bf16 = jnp.float32, jnp.bfloat16
    tile_out, lines_out = ((blocks, 256), f32), ((8, rows), f32)
    tile = call(start_kernel, [tile_out], [VMEM] * 4, 600000, 250000)(
        prev_basis, mix, send_list, send_count
    )
    high, low = call(
        prepare_kernel, [((width, rows), bf16), ((width, rows), bf16)], [VMEM], 1000000, 1000000
    )(strips)
    prev_gram = call(previous_gram_kernel, [((vecs, 128), f32)], [VMEM], 60000000, 250000)(prev_basis)
    step_specs = [VMEM] * 6 + [SMEM, VMEM, VMEM]
    tile, l0, choose = call(
        first_kernel,
        [tile_out, lines_out, ((4 * blocks, 128), f32)],
        step_specs,
        50000000,
        600000,
    )(tile, *ghosts(tile), columns, shifts, high, low)
    middle = []
    for step in (1, 2):
        tile, line = call(
            lambda *refs, step=step: middle_kernel(step, *refs),
            [tile_out, lines_out],
            step_specs,
            50000000,
            600000,
        )(tile, *ghosts(tile), choose, shifts, high, low)
        middle.append(line)
    l1, l2 = middle
    l3, gram = call(
        last_kernel,
        [lines_out, ((vecs + 8, 128), f32)],
        step_specs + [VMEM] * 5,
        80000000,
        900000,
    )(tile, *ghosts(tile), choose, shifts, high, low, l0, l1, l2, prev_basis, prev_gram)
    gram = summed(gram)
    total = float(lax.axis_size("dom") * rows)
    return call(
        lambda *refs: finish_kernel(total, *refs),
        [((comps, S, rows), f32), ((comps, vecs + S, S), f32)],
        [VMEM] * 6,
        50000000,
        400000,
    )(gram, prev_basis, l0, l1, l2, l3)


def solution(mesh):
    in_specs = (
        P("dom", None),
        P("dom", None),
        P("dom", None, None),
        P("dom", None),
        P(),
        P(None, None, "dom"),
        P(),
    )
    out_specs = (P(None, None, "dom"), P())
    return jax.shard_map(local, mesh=mesh, in_specs=in_specs, out_specs=out_specs, check_vma=False)
```

time: 176 us -> 69.2 us (0.39)
  blocking collectives: 78 us -> 0 us
  local copies, waits for them, and re-layouts: 18.9 us -> 5.41 us
  matrix products: 7.28 us -> 0 us
  other arithmetic: 7.22 us -> 0.02 us
  starting transfers between devices: 51 us -> 44.1 us
  Pallas kernels: 0 us -> 6.42 us
    psum x2 -> x0, blocking collectives: 78 us -> none  [the longest x1 40.2 us: local(): gram = lax.psum(local_gram, 'dom') / total]
    gather x20 -> x0, local copies, waits for them, and re-layouts: 11.7 us -> none  [the longest x16 9.23 us: local(): packed = jnp.take(vec, send_list[0, link], axis=1)]
    ppermute x16 -> x21, starting transfers between devices: 51 us -> 44.1 us  [the longest x16 33.1 us: ghosts(): lax.ppermute(tile, 'dom', pairs_of(length, step, odd))]
    pallas_call x0 -> x8, Pallas kernels: none -> 6.42 us  [the longest x2 1.96 us: local(): call(lambda *refs, step=step: middle_kernel(step, *refs), [tile_out, line...]
    dot_general x8 -> x0, matrix products: 6.4 us -> none  [the longest x4 4.59 us: local(): jnp.einsum('rik,crk->cri', matrix, picked, precision=lax.Precision.HIGHEST)]
    unnamed x25 -> x17, local copies, waits for them, and re-layouts: 1.67 us -> 4.72 us
    reshape x39 -> x0, local copies, waits for them, and re-layouts: 3 us -> none  [the longest x16 1.27 us: local(): jnp.where(live, packed, jnp.zeros_like(packed))]
    lt x4 -> x0, other arithmetic: 2.51 us -> none  [local(): live = slots[None, :, None] < send_count[0, link]]
  transfers between devices with their start and end apart: 16 -> 21, of which waited for: 3 -> 10; matrix products, arithmetic and copies ran while one was open for 4% -> 0% of each run, Pallas kernels for 0% -> 1%
where the time goes in v1:
time: 69.2 us; the launch traced here: 68.7 us
  starting transfers between devices  44.1 us (64%)
  waiting for transfers between devices  12 us (17%)
  Pallas kernels  6.42 us (9%)
  local copies, waits for them, and re-layouts  5.41 us (8%)
  between operations  0.86 us (1%)
    ppermute x16, starting transfers between devices, ghosts(): lax.ppermute(tile, 'dom', pairs_of(length, step, odd))  33.1 us
    ppermute x5, starting transfers between devices, summed(): lax.ppermute(value, 'dom', [(d, d ^ step) for d in range(length)])  11 us
    ppermute x5, waiting for transfers between devices, summed(): lax.ppermute(value, 'dom', [(d, d ^ step) for d in range(length)])  9.16 us
    unnamed x17, local copies, waits for them, and re-layouts  4.72 us
    ppermute x16, waiting for transfers between devices, ghosts(): lax.ppermute(tile, 'dom', pairs_of(length, step, odd))  2.81 us
    pallas_call x2, Pallas kernels, local(): call(lambda *refs, step=step: middle_kernel(step, *refs), [tile_out, line...  1.96 us
    pallas_call x1, Pallas kernels, local(): call(last_kernel, [lines_out, ((vecs + 8, 128), f32)], step_specs + [VMEM...  1.41 us
  transfers between devices with their start and end apart: 21, of which 10 were waited for; matrix products, arithmetic and copies ran while one was open for 0% of the time, Pallas kernels for 1%

profile of v1, /device:TPU:0, one launch (start us, length us, event | category | flops | bytes accessed | tf_op | source)
XLA Modules:
  0.0 68.7 jit_solution(4294552101148445985)
XLA Ops:
  0.6 0.0 copy-start
  0.6 0.9 %copy-done = f32[3,32,512]{2,1,0:T(8,128)S(1)} copy-done((f32[3,32,512]{2,1,0:T(8,128)S(1)}, f32[3,32,512]{2,1,0:T(8,128)}, u32[]{:S(2)}) %copy-start) | copy-done | bytes 196632
  1.6 0.0 copy-start.4
  1.6 0.7 copy-done.4
  2.2 0.7 copy-done.5
  2.9 0.7 copy-done.6
  3.6 0.3 shard_map.86.own
  3.9 0.7 collective-permute-start.3
  4.6 5.9 %collective-permute-start.2 = (f32[8,256]{1,0:T(8,128)S(1)}, f32[8,256]{1,0:T(8,128)S(1)}, u32[]{:S(2)}, u32[]{:S(2)}) collective-permute-start(f32[8,256]{1,0:T(8,128)S(1)} %shard_map.86.own), channel_id=1, source_target_pairs={{0,8},{1,9},{2,10},{3,11},{4,12},{5,13},{6,14},{7,15},{16,24},{17,... | collective-permute-start | bytes 24584 | tf_op jit(solution)/shard_map/ppermute | solution.py:268
  10.5 0.6 collective-permute-start.1
  11.2 2.9 %collective-permute-start = (f32[8,256]{1,0:T(8,128)S(1)}, f32[8,256]{1,0:T(8,128)S(1)}, u32[]{:S(2)}, u32[]{:S(2)}) collective-permute-start(f32[8,256]{1,0:T(8,128)S(1)} %shard_map.86.own), channel_id=1, source_target_pairs={{0,1},{2,3},{4,5},{6,7},{8,9},{10,11},{12,13},{14,15},{16,17},{18,... | collective-permute-start | bytes 24584 | tf_op jit(solution)/shard_map/ppermute | solution.py:268
  14.1 0.0 copy-done.7
  14.1 0.1 copy.9.columns
  14.2 1.0 %copy-done.2 = f32[512,256]{1,0:T(8,128)S(1)} copy-done((f32[512,256]{1,0:T(8,128)S(1)}, f32[512,256]{1,0:T(8,128)}, u32[]{:S(2)}) %copy-start.2) | copy-done | bytes 524312
  15.2 0.2 shard_map.87
  15.4 0.0 collective-permute-done.3.d
  15.4 0.0 collective-permute-done.2.c
  15.4 0.0 collective-permute-done.1.b
  15.5 0.0 collective-permute-done.a
  15.5 0.0 copy-start.3
  15.5 0.6 copy-done.3
  16.1 1.2 %shard_map.88 = (f32[8,256]{1,0:T(8,128)S(1)}, f32[8,512]{1,0:T(8,128)S(1)}, f32[32,128]{1,0:T(8,128)S(1)}) custom-call(f32[8,256]{1,0:T(8,128)S(1)} %shard_map.86.own, f32[8,256]{1,0:T(8,128)S(1)} %collective-permute-done.a, f32[8,256]{1,0:T(8,128)S(1)} %collective-permute-done.1.b, f32[8,256]{1,0:T(8,128)S(1)} %collective-permute-done.2.c, ...), custom_call_target="tpu_custom_call" | custom-call | flops 50000000 | bytes 600000 | tf_op jit(solution)/shard_map/pallas_call | solution.py:295
  17.3 0.7 collective-permute-start.7
  18.0 3.6 %collective-permute-start.6 = (f32[8,256]{1,0:T(8,128)S(1)}, f32[8,256]{1,0:T(8,128)S(1)}, u32[]{:S(2)}, u32[]{:S(2)}) collective-permute-start(f32[8,256]{1,0:T(8,128)S(1)} %get-tuple-element.15.refs_0_), channel_id=1, source_target_pairs={{0,8},{1,9},{2,10},{3,11},{4,12},{5,13},{6,14},{7,15},{16,24},{17,... | collective-permute-start | bytes 24584 | tf_op jit(solution)/shard_map/ppermute | solution.py:268
  21.6 0.6 collective-permute-start.5
  22.2 1.1 %collective-permute-start.4 = (f32[8,256]{1,0:T(8,128)S(1)}, f32[8,256]{1,0:T(8,128)S(1)}, u32[]{:S(2)}, u32[]{:S(2)}) collective-permute-start(f32[8,256]{1,0:T(8,128)S(1)} %get-tuple-element.15.refs_0_), channel_id=1, source_target_pairs={{0,1},{2,3},{4,5},{6,7},{8,9},{10,11},{12,13},{14,15},{16,17},{18,... | collective-permute-start | bytes 24584 | tf_op jit(solution)/shard_map/ppermute | solution.py:268
  23.4 0.0 collective-permute-done.7.refs_4_
  23.4 0.0 collective-permute-done.6.refs_3_
  23.4 0.0 collective-permute-done.5.refs_2_
  23.4 0.8 %collective-permute-done.4.refs_1_ = f32[8,256]{1,0:T(8,128)S(1)} collective-permute-done((f32[8,256]{1,0:T(8,128)S(1)}, f32[8,256]{1,0:T(8,128)S(1)}, u32[]{:S(2)}, u32[]{:S(2)}) %collective-permute-start.4) | collective-permute-done | bytes 8224 | tf_op jit(solution)/shard_map/ppermute | solution.py:268
  24.2 1.0 %shard_map.89 = (f32[8,256]{1,0:T(8,128)S(1)}, f32[8,512]{1,0:T(8,128)S(1)}) custom-call(f32[8,256]{1,0:T(8,128)S(1)} %get-tuple-element.15.refs_0_, f32[8,256]{1,0:T(8,128)S(1)} %collective-permute-done.4.refs_1_, f32[8,256]{1,0:T(8,128)S(1)} %collective-permute-done.5.refs_2_, f32[8,256]{1,0:T(8,128)S(1)} %collective-permute-done.6.refs_3_, ...), custom_call_target="tpu_custom_call" | custom-call | flops 50000000 | bytes 600000 | tf_op jit(solution)/shard_map/pallas_call | solution.py:304
  25.2 0.0 copy-start.1
  25.2 0.8 %collective-permute-start.11 = (f32[8,256]{1,0:T(8,128)S(1)}, f32[8,256]{1,0:T(8,128)S(1)}, u32[]{:S(2)}, u32[]{:S(2)}) collective-permute-start(f32[8,256]{1,0:T(8,128)S(1)} %get-tuple-element.17.refs_0_), channel_id=1, source_target_pairs={{8,16},{9,17},{10,18},{11,19},{12,20},{13,21},{14,22},{15,23},{16,... | collective-permute-start | bytes 24584 | tf_op jit(solution)/shard_map/ppermute | solution.py:268
  26.0 7.1 %collective-permute-start.10 = (f32[8,256]{1,0:T(8,128)S(1)}, f32[8,256]{1,0:T(8,128)S(1)}, u32[]{:S(2)}, u32[]{:S(2)}) collective-permute-start(f32[8,256]{1,0:T(8,128)S(1)} %get-tuple-element.17.refs_0_), channel_id=1, source_target_pairs={{0,8},{1,9},{2,10},{3,11},{4,12},{5,13},{6,14},{7,15},{16,24},{17,... | collective-permute-start | bytes 24584 | tf_op jit(solution)/shard_map/ppermute | solution.py:268
  33.1 0.6 collective-permute-start.9
  33.7 0.1 collective-permute-start.8
  33.8 0.0 collective-permute-done.11.refs_4_
  33.8 0.9 %collective-permute-done.10.refs_3_ = f32[8,256]{1,0:T(8,128)S(1)} collective-permute-done((f32[8,256]{1,0:T(8,128)S(1)}, f32[8,256]{1,0:T(8,128)S(1)}, u32[]{:S(2)}, u32[]{:S(2)}) %collective-permute-start.10) | collective-permute-done | bytes 8224 | tf_op jit(solution)/shard_map/ppermute | solution.py:268
  34.7 0.0 collective-permute-done.9.refs_2_
  34.7 0.3 collective-permute-done.8.refs_1_
  35.0 1.0 %shard_map.90 = (f32[8,256]{1,0:T(8,128)S(1)}, f32[8,512]{1,0:T(8,128)S(1)}) custom-call(f32[8,256]{1,0:T(8,128)S(1)} %get-tuple-element.17.refs_0_, f32[8,256]{1,0:T(8,128)S(1)} %collective-permute-done.8.refs_1_, f32[8,256]{1,0:T(8,128)S(1)} %collective-permute-done.9.refs_2_, f32[8,256]{1,0:T(8,128)S(1)} %collective-permute-done.10.refs_3_, ...), custom_call_target="tpu_custom_call" | custom-call | flops 50000000 | bytes 600000 | tf_op jit(solution)/shard_map/pallas_call | solution.py:304
  35.9 0.7 collective-permute-start.15
  36.6 6.9 %collective-permute-start.14 = (f32[8,256]{1,0:T(8,128)S(1)}, f32[8,256]{1,0:T(8,128)S(1)}, u32[]{:S(2)}, u32[]{:S(2)}) collective-permute-start(f32[8,256]{1,0:T(8,128)S(1)} %get-tuple-element.18.own), channel_id=1, source_target_pairs={{0,8},{1,9},{2,10},{3,11},{4,12},{5,13},{6,14},{7,15},{16,24},{17,... | collective-permute-start | bytes 24584 | tf_op jit(solution)/shard_map/ppermute | solution.py:268
  43.5 0.6 collective-permute-start.13
  44.2 0.1 collective-permute-start.12
  44.3 0.0 copy-done.1
  44.3 0.3 shard_map.91.prev_gram
  44.6 0.0 collective-permute-done.15.d
  44.6 0.6 collective-permute-done.14.c
  45.2 0.0 collective-permute-done.13.b
  45.2 0.3 collective-permute-done.12.a
  45.4 1.4 %shard_map.92 = (f32[8,512]{1,0:T(8,128)S(1)}, f32[40,128]{1,0:T(8,128)S(1)}) custom-call(f32[8,256]{1,0:T(8,128)S(1)} %get-tuple-element.18.own, f32[8,256]{1,0:T(8,128)S(1)} %collective-permute-done.12.a, f32[8,256]{1,0:T(8,128)S(1)} %collective-permute-done.13.b, f32[8,256]{1,0:T(8,128)S(1)} %collective-permute-done.14.c, ...), custom_call_target="tpu_custom_call" | custom-call | flops 80000000 | bytes 900000 | tf_op jit(solution)/shard_map/pallas_call | solution.py:313
  46.9 0.9 %collective-permute-start.16 = (f32[40,128]{1,0:T(8,128)S(1)}, f32[40,128]{1,0:T(8,128)S(1)}, u32[]{:S(2)}, u32[]{:S(2)}) collective-permute-start(f32[40,128]{1,0:T(8,128)S(1)} %get-tuple-element.22), channel_id=1, source_target_pairs={{0,1},{1,0},{2,3},{3,2},{4,5},{5,4},{6,7},{7,6},{8,9},{9,8},{10,11... | collective-permute-start | bytes 61448 | tf_op jit(solution)/shard_map/ppermute | solution.py:276
  47.8 0.8 %collective-permute-done.16 = f32[40,128]{1,0:T(8,128)S(1)} collective-permute-done((f32[40,128]{1,0:T(8,128)S(1)}, f32[40,128]{1,0:T(8,128)S(1)}, u32[]{:S(2)}, u32[]{:S(2)}) %collective-permute-start.16) | collective-permute-done | bytes 20512 | tf_op jit(solution)/shard_map/ppermute | solution.py:276
  48.6 0.9 %collective-permute-start.17 = (f32[40,128]{1,0:T(8,128)S(1)}, f32[40,128]{1,0:T(8,128)S(1)}, u32[]{:S(2)}, u32[]{:S(2)}) collective-permute-start(f32[40,128]{1,0:T(8,128)S(1)} %add.15), channel_id=1, source_target_pairs={{0,2},{1,3},{2,0},{3,1},{4,6},{5,7},{6,4},{7,5},{8,10},{9,11},{10,... | collective-permute-start | bytes 61448 | tf_op jit(solution)/shard_map/ppermute | solution.py:276
  49.5 2.9 %collective-permute-done.17 = f32[40,128]{1,0:T(8,128)S(1)} collective-permute-done((f32[40,128]{1,0:T(8,128)S(1)}, f32[40,128]{1,0:T(8,128)S(1)}, u32[]{:S(2)}, u32[]{:S(2)}) %collective-permute-start.17) | collective-permute-done | bytes 20512 | tf_op jit(solution)/shard_map/ppermute | solution.py:276
  52.4 3.2 %collective-permute-start.18 = (f32[40,128]{1,0:T(8,128)S(1)}, f32[40,128]{1,0:T(8,128)S(1)}, u32[]{:S(2)}, u32[]{:S(2)}) collective-permute-start(f32[40,128]{1,0:T(8,128)S(1)} %add.16), channel_id=1, source_target_pairs={{0,4},{1,5},{2,6},{3,7},{4,0},{5,1},{6,2},{7,3},{8,12},{9,13},{10,... | collective-permute-start | bytes 61448 | tf_op jit(solution)/shard_map/ppermute | solution.py:276
  55.6 1.8 %collective-permute-done.18 = f32[40,128]{1,0:T(8,128)S(1)} collective-permute-done((f32[40,128]{1,0:T(8,128)S(1)}, f32[40,128]{1,0:T(8,128)S(1)}, u32[]{:S(2)}, u32[]{:S(2)}) %collective-permute-start.18) | collective-permute-done | bytes 20512 | tf_op jit(solution)/shard_map/ppermute | solution.py:276
  57.3 3.2 %collective-permute-start.19 = (f32[40,128]{1,0:T(8,128)S(1)}, f32[40,128]{1,0:T(8,128)S(1)}, u32[]{:S(2)}, u32[]{:S(2)}) collective-permute-start(f32[40,128]{1,0:T(8,128)S(1)} %add.17), channel_id=1, source_target_pairs={{0,8},{1,9},{2,10},{3,11},{4,12},{5,13},{6,14},{7,15},{8,0},{9,1},... | collective-permute-start | bytes 61448 | tf_op jit(solution)/shard_map/ppermute | solution.py:276
  60.6 1.8 %collective-permute-done.19 = f32[40,128]{1,0:T(8,128)S(1)} collective-permute-done((f32[40,128]{1,0:T(8,128)S(1)}, f32[40,128]{1,0:T(8,128)S(1)}, u32[]{:S(2)}, u32[]{:S(2)}) %collective-permute-start.19) | collective-permute-done | bytes 20512 | tf_op jit(solution)/shard_map/ppermute | solution.py:276
  62.4 2.8 %collective-permute-start.20 = (f32[40,128]{1,0:T(8,128)S(1)}, f32[40,128]{1,0:T(8,128)S(1)}, u32[]{:S(2)}, u32[]{:S(2)}) collective-permute-start(f32[40,128]{1,0:T(8,128)S(1)} %add.18), channel_id=1, source_target_pairs={{0,16},{1,17},{2,18},{3,19},{4,20},{5,21},{6,22},{7,23},{8,24},{9,... | collective-permute-start | bytes 61448 | tf_op jit(solution)/shard_map/ppermute | solution.py:276
  65.1 1.9 %collective-permute-done.20 = f32[40,128]{1,0:T(8,128)S(1)} collective-permute-done((f32[40,128]{1,0:T(8,128)S(1)}, f32[40,128]{1,0:T(8,128)S(1)}, u32[]{:S(2)}, u32[]{:S(2)}) %collective-permute-start.20) | collective-permute-done | bytes 20512 | tf_op jit(solution)/shard_map/ppermute | solution.py:276
  67.0 1.0 %shard_map.93 = (f32[3,4,512]{2,1,0:T(4,128)}, f32[3,36,4]{2,1,0:T(8,128)S(1)}) custom-call(f32[40,128]{1,0:T(8,128)S(1)} %add.19.refs_0_, f32[3,32,512]{2,1,0:T(8,128)S(1)} %copy-done.1, f32[8,512]{1,0:T(8,128)S(1)} %get-tuple-element.19.l0.refs_2_, f32[8,512]{1,0:T(8,128)S(1)} %get-tuple-element.20.l1.refs_3_, f32[8,512]{1,0:T(8,128)S(1)} %get-tuple-element.21.l2.refs_4_, ...), custom_call_target="tpu_custom_call" | custom-call | flops 50000000 | bytes 400000 | tf_op jit(solution)/shard_map/pallas_call | solution.py:322
  68.1 0.7 copy.10
  (9 shorter events, 0.0 us)
Async XLA Ops:
  0.6 0.9 %copy-start = (f32[3,32,512]{2,1,0:T(8,128)S(1)}, f32[3,32,512]{2,1,0:T(8,128)}, u32[]{:S(2)}) copy-start(f32[3,32,512]{2,1,0:T(8,128)} %refs_1_.1) | copy-start | bytes 589828
  1.6 0.7 copy-start.4
  2.2 0.7 copy-start.5
  2.9 0.7 copy-start.6
  3.6 10.5 %copy-start.7 = (s32[8,4]{0,1:T(4,128)S(1)}, s32[8,4]{0,1:T(4,128)}, u32[]{:S(2)}) copy-start(s32[8,4]{0,1:T(4,128)} %param.8) | copy-start | bytes 388
  3.9 11.5 %collective-permute-start.3 = (f32[8,256]{1,0:T(8,128)S(1)}, f32[8,256]{1,0:T(8,128)S(1)}, u32[]{:S(2)}, u32[]{:S(2)}) collective-permute-start(f32[8,256]{1,0:T(8,128)S(1)} %shard_map.86.own), channel_id=1, source_target_pairs={{8,16},{9,17},{10,18},{11,19},{12,20},{13,21},{14,22},{15,23},{16,... | collective-permute-start | bytes 24584 | tf_op jit(solution)/shard_map/ppermute | solution.py:268
  4.6 10.8 %collective-permute-start.2 = (f32[8,256]{1,0:T(8,128)S(1)}, f32[8,256]{1,0:T(8,128)S(1)}, u32[]{:S(2)}, u32[]{:S(2)}) collective-permute-start(f32[8,256]{1,0:T(8,128)S(1)} %shard_map.86.own), channel_id=1, source_target_pairs={{0,8},{1,9},{2,10},{3,11},{4,12},{5,13},{6,14},{7,15},{16,24},{17,... | collective-permute-start | bytes 24584 | tf_op jit(solution)/shard_map/ppermute | solution.py:268
  10.5 4.9 %collective-permute-start.1 = (f32[8,256]{1,0:T(8,128)S(1)}, f32[8,256]{1,0:T(8,128)S(1)}, u32[]{:S(2)}, u32[]{:S(2)}) collective-permute-start(f32[8,256]{1,0:T(8,128)S(1)} %shard_map.86.own), channel_id=1, source_target_pairs={{1,2},{3,4},{5,6},{7,8},{9,10},{11,12},{13,14},{15,16},{17,18},{19... | collective-permute-start | bytes 24584 | tf_op jit(solution)/shard_map/ppermute | solution.py:268
  11.2 4.3 %collective-permute-start = (f32[8,256]{1,0:T(8,128)S(1)}, f32[8,256]{1,0:T(8,128)S(1)}, u32[]{:S(2)}, u32[]{:S(2)}) collective-permute-start(f32[8,256]{1,0:T(8,128)S(1)} %shard_map.86.own), channel_id=1, source_target_pairs={{0,1},{2,3},{4,5},{6,7},{8,9},{10,11},{12,13},{14,15},{16,17},{18,... | collective-permute-start | bytes 24584 | tf_op jit(solution)/shard_map/ppermute | solution.py:268
  14.2 1.0 %copy-start.2 = (f32[512,256]{1,0:T(8,128)S(1)}, f32[512,256]{1,0:T(8,128)}, u32[]{:S(2)}) copy-start(f32[512,256]{1,0:T(8,128)} %strips_ref.1) | copy-start | bytes 1572868
  15.5 0.7 copy-start.3
  17.3 6.0 %collective-permute-start.7 = (f32[8,256]{1,0:T(8,128)S(1)}, f32[8,256]{1,0:T(8,128)S(1)}, u32[]{:S(2)}, u32[]{:S(2)}) collective-permute-start(f32[8,256]{1,0:T(8,128)S(1)} %get-tuple-element.15.refs_0_), channel_id=1, source_target_pairs={{8,16},{9,17},{10,18},{11,19},{12,20},{13,21},{14,22},{15,23},{16,... | collective-permute-start | bytes 24584 | tf_op jit(solution)/shard_map/ppermute | solution.py:268
  18.0 5.4 %collective-permute-start.6 = (f32[8,256]{1,0:T(8,128)S(1)}, f32[8,256]{1,0:T(8,128)S(1)}, u32[]{:S(2)}, u32[]{:S(2)}) collective-permute-start(f32[8,256]{1,0:T(8,128)S(1)} %get-tuple-element.15.refs_0_), channel_id=1, source_target_pairs={{0,8},{1,9},{2,10},{3,11},{4,12},{5,13},{6,14},{7,15},{16,24},{17,... | collective-permute-start | bytes 24584 | tf_op jit(solution)/shard_map/ppermute | solution.py:268
  21.6 1.8 %collective-permute-start.5 = (f32[8,256]{1,0:T(8,128)S(1)}, f32[8,256]{1,0:T(8,128)S(1)}, u32[]{:S(2)}, u32[]{:S(2)}) collective-permute-start(f32[8,256]{1,0:T(8,128)S(1)} %get-tuple-element.15.refs_0_), channel_id=1, source_target_pairs={{1,2},{3,4},{5,6},{7,8},{9,10},{11,12},{13,14},{15,16},{17,18},{19... | collective-permute-start | bytes 24584 | tf_op jit(solution)/shard_map/ppermute | solution.py:268
  22.2 1.9 %collective-permute-start.4 = (f32[8,256]{1,0:T(8,128)S(1)}, f32[8,256]{1,0:T(8,128)S(1)}, u32[]{:S(2)}, u32[]{:S(2)}) collective-permute-start(f32[8,256]{1,0:T(8,128)S(1)} %get-tuple-element.15.refs_0_), channel_id=1, source_target_pairs={{0,1},{2,3},{4,5},{6,7},{8,9},{10,11},{12,13},{14,15},{16,17},{18,... | collective-permute-start | bytes 24584 | tf_op jit(solution)/shard_map/ppermute | solution.py:268
  25.2 19.1 %copy-start.1 = (f32[3,32,512]{2,1,0:T(8,128)S(1)}, f32[3,32,512]{2,1,0:T(8,128)}, u32[]{:S(2)}) copy-start(f32[3,32,512]{2,1,0:T(8,128)} %refs_1_.1) | copy-start | bytes 589828
  25.2 8.6 %collective-permute-start.11 = (f32[8,256]{1,0:T(8,128)S(1)}, f32[8,256]{1,0:T(8,128)S(1)}, u32[]{:S(2)}, u32[]{:S(2)}) collective-permute-start(f32[8,256]{1,0:T(8,128)S(1)} %get-tuple-element.17.refs_0_), channel_id=1, source_target_pairs={{8,16},{9,17},{10,18},{11,19},{12,20},{13,21},{14,22},{15,23},{16,... | collective-permute-start | bytes 24584 | tf_op jit(solution)/shard_map/ppermute | solution.py:268
  26.0 8.7 %collective-permute-start.10 = (f32[8,256]{1,0:T(8,128)S(1)}, f32[8,256]{1,0:T(8,128)S(1)}, u32[]{:S(2)}, u32[]{:S(2)}) collective-permute-start(f32[8,256]{1,0:T(8,128)S(1)} %get-tuple-element.17.refs_0_), channel_id=1, source_target_pairs={{0,8},{1,9},{2,10},{3,11},{4,12},{5,13},{6,14},{7,15},{16,24},{17,... | collective-permute-start | bytes 24584 | tf_op jit(solution)/shard_map/ppermute | solution.py:268
  33.1 1.6 %collective-permute-start.9 = (f32[8,256]{1,0:T(8,128)S(1)}, f32[8,256]{1,0:T(8,128)S(1)}, u32[]{:S(2)}, u32[]{:S(2)}) collective-permute-start(f32[8,256]{1,0:T(8,128)S(1)} %get-tuple-element.17.refs_0_), channel_id=1, source_target_pairs={{1,2},{3,4},{5,6},{7,8},{9,10},{11,12},{13,14},{15,16},{17,18},{19... | collective-permute-start | bytes 24584 | tf_op jit(solution)/shard_map/ppermute | solution.py:268
  33.7 1.2 %collective-permute-start.8 = (f32[8,256]{1,0:T(8,128)S(1)}, f32[8,256]{1,0:T(8,128)S(1)}, u32[]{:S(2)}, u32[]{:S(2)}) collective-permute-start(f32[8,256]{1,0:T(8,128)S(1)} %get-tuple-element.17.refs_0_), channel_id=1, source_target_pairs={{0,1},{2,3},{4,5},{6,7},{8,9},{10,11},{12,13},{14,15},{16,17},{18,... | collective-permute-start | bytes 24584 | tf_op jit(solution)/shard_map/ppermute | solution.py:268
  35.9 8.7 %collective-permute-start.15 = (f32[8,256]{1,0:T(8,128)S(1)}, f32[8,256]{1,0:T(8,128)S(1)}, u32[]{:S(2)}, u32[]{:S(2)}) collective-permute-start(f32[8,256]{1,0:T(8,128)S(1)} %get-tuple-element.18.own), channel_id=1, source_target_pairs={{8,16},{9,17},{10,18},{11,19},{12,20},{13,21},{14,22},{15,23},{16,... | collective-permute-start | bytes 24584 | tf_op jit(solution)/shard_map/ppermute | solution.py:268
  36.6 8.6 %collective-permute-start.14 = (f32[8,256]{1,0:T(8,128)S(1)}, f32[8,256]{1,0:T(8,128)S(1)}, u32[]{:S(2)}, u32[]{:S(2)}) collective-permute-start(f32[8,256]{1,0:T(8,128)S(1)} %get-tuple-element.18.own), channel_id=1, source_target_pairs={{0,8},{1,9},{2,10},{3,11},{4,12},{5,13},{6,14},{7,15},{16,24},{17,... | collective-permute-start | bytes 24584 | tf_op jit(solution)/shard_map/ppermute | solution.py:268
  43.5 1.6 %collective-permute-start.13 = (f32[8,256]{1,0:T(8,128)S(1)}, f32[8,256]{1,0:T(8,128)S(1)}, u32[]{:S(2)}, u32[]{:S(2)}) collective-permute-start(f32[8,256]{1,0:T(8,128)S(1)} %get-tuple-element.18.own), channel_id=1, source_target_pairs={{1,2},{3,4},{5,6},{7,8},{9,10},{11,12},{13,14},{15,16},{17,18},{19... | collective-permute-start | bytes 24584 | tf_op jit(solution)/shard_map/ppermute | solution.py:268
  44.2 1.2 %collective-permute-start.12 = (f32[8,256]{1,0:T(8,128)S(1)}, f32[8,256]{1,0:T(8,128)S(1)}, u32[]{:S(2)}, u32[]{:S(2)}) collective-permute-start(f32[8,256]{1,0:T(8,128)S(1)} %get-tuple-element.18.own), channel_id=1, source_target_pairs={{0,1},{2,3},{4,5},{6,7},{8,9},{10,11},{12,13},{14,15},{16,17},{18,... | collective-permute-start | bytes 24584 | tf_op jit(solution)/shard_map/ppermute | solution.py:268
  46.9 1.8 %collective-permute-start.16 = (f32[40,128]{1,0:T(8,128)S(1)}, f32[40,128]{1,0:T(8,128)S(1)}, u32[]{:S(2)}, u32[]{:S(2)}) collective-permute-start(f32[40,128]{1,0:T(8,128)S(1)} %get-tuple-element.22), channel_id=1, source_target_pairs={{0,1},{1,0},{2,3},{3,2},{4,5},{5,4},{6,7},{7,6},{8,9},{9,8},{10,11... | collective-permute-start | bytes 61448 | tf_op jit(solution)/shard_map/ppermute | solution.py:276
  48.6 3.8 %collective-permute-start.17 = (f32[40,128]{1,0:T(8,128)S(1)}, f32[40,128]{1,0:T(8,128)S(1)}, u32[]{:S(2)}, u32[]{:S(2)}) collective-permute-start(f32[40,128]{1,0:T(8,128)S(1)} %add.15), channel_id=1, source_target_pairs={{0,2},{1,3},{2,0},{3,1},{4,6},{5,7},{6,4},{7,5},{8,10},{9,11},{10,... | collective-permute-start | bytes 61448 | tf_op jit(solution)/shard_map/ppermute | solution.py:276
  52.4 4.9 %collective-permute-start.18 = (f32[40,128]{1,0:T(8,128)S(1)}, f32[40,128]{1,0:T(8,128)S(1)}, u32[]{:S(2)}, u32[]{:S(2)}) collective-permute-start(f32[40,128]{1,0:T(8,128)S(1)} %add.16), channel_id=1, source_target_pairs={{0,4},{1,5},{2,6},{3,7},{4,0},{5,1},{6,2},{7,3},{8,12},{9,13},{10,... | collective-permute-start | bytes 61448 | tf_op jit(solution)/shard_map/ppermute | solution.py:276
  57.3 5.0 %collective-permute-start.19 = (f32[40,128]{1,0:T(8,128)S(1)}, f32[40,128]{1,0:T(8,128)S(1)}, u32[]{:S(2)}, u32[]{:S(2)}) collective-permute-start(f32[40,128]{1,0:T(8,128)S(1)} %add.17), channel_id=1, source_target_pairs={{0,8},{1,9},{2,10},{3,11},{4,12},{5,13},{6,14},{7,15},{8,0},{9,1},... | collective-permute-start | bytes 61448 | tf_op jit(solution)/shard_map/ppermute | solution.py:276
  62.4 4.7 %collective-permute-start.20 = (f32[40,128]{1,0:T(8,128)S(1)}, f32[40,128]{1,0:T(8,128)S(1)}, u32[]{:S(2)}, u32[]{:S(2)}) collective-permute-start(f32[40,128]{1,0:T(8,128)S(1)} %add.18), channel_id=1, source_target_pairs={{0,16},{1,17},{2,18},{3,19},{4,20},{5,21},{6,22},{7,23},{8,24},{9,... | collective-permute-start | bytes 61448 | tf_op jit(solution)/shard_map/ppermute | solution.py:276

commit v2 on v1

--- a/solution.py
+++ b/solution.py
@@ -270,12 +270,7 @@
 
 
 def summed(value):
-    length = lax.axis_size("dom")
-    step = 1
-    while step < length:
-        value = value + lax.ppermute(value, "dom", [(d, d ^ step) for d in range(length)])
-        step *= 2
-    return value
+    return jnp.sum(lax.all_gather(value, "dom"), axis=0)
 
 
 def local(strips, columns, send_list, send_count, shifts, prev_basis, mix):

time: 69.2 us -> 91.3 us (1.32)
  blocking collectives: 0 us -> 42.2 us
  starting transfers between devices: 44.1 us -> 33.1 us
  waiting for transfers between devices: 12 us -> 2.81 us
    all_gather x0 -> x1, blocking collectives: none -> 42.2 us  [summed(): return jnp.sum(lax.all_gather(value, 'dom'), axis=0)]
    ppermute x5 -> x0, starting transfers between devices: 11 us -> none  [summed(): lax.ppermute(value, 'dom', [(d, d ^ step) for d in range(length)])]
    ppermute x5 -> x0, waiting for transfers between devices: 9.16 us -> none  [summed(): lax.ppermute(value, 'dom', [(d, d ^ step) for d in range(length)])]
  transfers between devices with their start and end apart: 21 -> 16, of which waited for: 10 -> 5; matrix products, arithmetic and copies ran while one was open for 0% -> 0% of each run, Pallas kernels for 1% -> 1%
where the time goes in v2:
time: 91.3 us; the launch traced here: 90.8 us
  blocking collectives  42.2 us (46%)
  starting transfers between devices  33.1 us (36%)
  Pallas kernels  6.42 us (7%)
  local copies, waits for them, and re-layouts  5.41 us (6%)
  waiting for transfers between devices  2.81 us (3%)
    all_gather x1, blocking collectives, summed(): return jnp.sum(lax.all_gather(value, 'dom'), axis=0)  42.2 us
    ppermute x16, starting transfers between devices, ghosts(): lax.ppermute(tile, 'dom', pairs_of(length, step, odd))  33.1 us
    unnamed x17, local copies, waits for them, and re-layouts  4.72 us
    ppermute x16, waiting for transfers between devices, ghosts(): lax.ppermute(tile, 'dom', pairs_of(length, step, odd))  2.81 us
    pallas_call x2, Pallas kernels, local(): call(lambda *refs, step=step: middle_kernel(step, *refs), [tile_out, line...  1.96 us
  transfers between devices with their start and end apart: 16, of which 5 were waited for; matrix products, arithmetic and copies ran while one was open for 0% of the time, Pallas kernels for 1%

profile of v2, /device:TPU:0, one launch (start us, length us, event | category | flops | bytes accessed | tf_op | source)
XLA Modules:
  0.0 90.8 jit_solution(5459006522640302287)
XLA Ops:
  0.6 0.0 copy-start
  0.6 0.9 %copy-done = f32[3,32,512]{2,1,0:T(8,128)S(1)} copy-done((f32[3,32,512]{2,1,0:T(8,128)S(1)}, f32[3,32,512]{2,1,0:T(8,128)}, u32[]{:S(2)}) %copy-start) | copy-done | bytes 196632
  1.6 0.0 copy-start.4
  1.6 0.7 copy-done.4
  2.2 0.0 copy-start.5
  2.2 0.7 copy-done.5
  2.9 0.0 copy-start.6
  2.9 0.7 copy-done.6
  3.6 0.0 copy-start.7
  3.6 0.3 shard_map.86.own
  3.9 0.7 collective-permute-start.3
  4.6 5.9 %collective-permute-start.2 = (f32[8,256]{1,0:T(8,128)S(1)}, f32[8,256]{1,0:T(8,128)S(1)}, u32[]{:S(2)}, u32[]{:S(2)}) collective-permute-start(f32[8,256]{1,0:T(8,128)S(1)} %shard_map.86.own), channel_id=1, source_target_pairs={{0,8},{1,9},{2,10},{3,11},{4,12},{5,13},{6,14},{7,15},{16,24},{17,... | collective-permute-start | bytes 24584 | tf_op jit(solution)/shard_map/ppermute | solution.py:268
  10.5 0.6 collective-permute-start.1
  11.2 2.9 %collective-permute-start = (f32[8,256]{1,0:T(8,128)S(1)}, f32[8,256]{1,0:T(8,128)S(1)}, u32[]{:S(2)}, u32[]{:S(2)}) collective-permute-start(f32[8,256]{1,0:T(8,128)S(1)} %shard_map.86.own), channel_id=1, source_target_pairs={{0,1},{2,3},{4,5},{6,7},{8,9},{10,11},{12,13},{14,15},{16,17},{18,... | collective-permute-start | bytes 24584 | tf_op jit(solution)/shard_map/ppermute | solution.py:268
  14.1 0.0 copy-done.7
  14.1 0.1 copy.9.columns
  14.2 0.0 copy-start.2
  14.2 1.0 %copy-done.2 = f32[512,256]{1,0:T(8,128)S(1)} copy-done((f32[512,256]{1,0:T(8,128)S(1)}, f32[512,256]{1,0:T(8,128)}, u32[]{:S(2)}) %copy-start.2) | copy-done | bytes 524312
  15.2 0.2 shard_map.87
  15.4 0.0 collective-permute-done.3.d
  15.4 0.0 collective-permute-done.2.c
  15.4 0.0 collective-permute-done.1.b
  15.5 0.0 collective-permute-done.a
  15.5 0.0 copy-start.3
  15.5 0.6 copy-done.3
  16.1 1.2 %shard_map.88 = (f32[8,256]{1,0:T(8,128)S(1)}, f32[8,512]{1,0:T(8,128)S(1)}, f32[32,128]{1,0:T(8,128)S(1)}) custom-call(f32[8,256]{1,0:T(8,128)S(1)} %shard_map.86.own, f32[8,256]{1,0:T(8,128)S(1)} %collective-permute-done.a, f32[8,256]{1,0:T(8,128)S(1)} %collective-permute-done.1.b, f32[8,256]{1,0:T(8,128)S(1)} %collective-permute-done.2.c, ...), custom_call_target="tpu_custom_call" | custom-call | flops 50000000 | bytes 600000 | tf_op jit(solution)/shard_map/pallas_call | solution.py:290
  17.3 0.7 collective-permute-start.7
  18.0 3.6 %collective-permute-start.6 = (f32[8,256]{1,0:T(8,128)S(1)}, f32[8,256]{1,0:T(8,128)S(1)}, u32[]{:S(2)}, u32[]{:S(2)}) collective-permute-start(f32[8,256]{1,0:T(8,128)S(1)} %get-tuple-element.15.refs_0_), channel_id=1, source_target_pairs={{0,8},{1,9},{2,10},{3,11},{4,12},{5,13},{6,14},{7,15},{16,24},{17,... | collective-permute-start | bytes 24584 | tf_op jit(solution)/shard_map/ppermute | solution.py:268
  21.6 0.6 collective-permute-start.5
  22.2 1.1 %collective-permute-start.4 = (f32[8,256]{1,0:T(8,128)S(1)}, f32[8,256]{1,0:T(8,128)S(1)}, u32[]{:S(2)}, u32[]{:S(2)}) collective-permute-start(f32[8,256]{1,0:T(8,128)S(1)} %get-tuple-element.15.refs_0_), channel_id=1, source_target_pairs={{0,1},{2,3},{4,5},{6,7},{8,9},{10,11},{12,13},{14,15},{16,17},{18,... | collective-permute-start | bytes 24584 | tf_op jit(solution)/shard_map/ppermute | solution.py:268
  23.4 0.0 collective-permute-done.7.refs_4_
  23.4 0.0 collective-permute-done.6.refs_3_
  23.4 0.0 collective-permute-done.5.refs_2_
  23.4 0.8 collective-permute-done.4.refs_1_
  24.2 1.0 %shard_map.89 = (f32[8,256]{1,0:T(8,128)S(1)}, f32[8,512]{1,0:T(8,128)S(1)}) custom-call(f32[8,256]{1,0:T(8,128)S(1)} %get-tuple-element.15.refs_0_, f32[8,256]{1,0:T(8,128)S(1)} %collective-permute-done.4.refs_1_, f32[8,256]{1,0:T(8,128)S(1)} %collective-permute-done.5.refs_2_, f32[8,256]{1,0:T(8,128)S(1)} %collective-permute-done.6.refs_3_, ...), custom_call_target="tpu_custom_call" | custom-call | flops 50000000 | bytes 600000 | tf_op jit(solution)/shard_map/pallas_call | solution.py:299
  25.2 0.0 copy-start.1
  25.2 0.8 collective-permute-start.11
  26.0 7.1 %collective-permute-start.10 = (f32[8,256]{1,0:T(8,128)S(1)}, f32[8,256]{1,0:T(8,128)S(1)}, u32[]{:S(2)}, u32[]{:S(2)}) collective-permute-start(f32[8,256]{1,0:T(8,128)S(1)} %get-tuple-element.17.refs_0_), channel_id=1, source_target_pairs={{0,8},{1,9},{2,10},{3,11},{4,12},{5,13},{6,14},{7,15},{16,24},{17,... | collective-permute-start | bytes 24584 | tf_op jit(solution)/shard_map/ppermute | solution.py:268
  33.1 0.6 collective-permute-start.9
  33.7 0.1 collective-permute-start.8
  33.8 0.0 collective-permute-done.11.refs_4_
  33.8 0.9 collective-permute-done.10.refs_3_
  34.7 0.0 collective-permute-done.9.refs_2_
  34.7 0.3 collective-permute-done.8.refs_1_
  35.0 1.0 %shard_map.90 = (f32[8,256]{1,0:T(8,128)S(1)}, f32[8,512]{1,0:T(8,128)S(1)}) custom-call(f32[8,256]{1,0:T(8,128)S(1)} %get-tuple-element.17.refs_0_, f32[8,256]{1,0:T(8,128)S(1)} %collective-permute-done.8.refs_1_, f32[8,256]{1,0:T(8,128)S(1)} %collective-permute-done.9.refs_2_, f32[8,256]{1,0:T(8,128)S(1)} %collective-permute-done.10.refs_3_, ...), custom_call_target="tpu_custom_call" | custom-call | flops 50000000 | bytes 600000 | tf_op jit(solution)/shard_map/pallas_call | solution.py:299
  35.9 0.7 collective-permute-start.15
  36.6 6.9 %collective-permute-start.14 = (f32[8,256]{1,0:T(8,128)S(1)}, f32[8,256]{1,0:T(8,128)S(1)}, u32[]{:S(2)}, u32[]{:S(2)}) collective-permute-start(f32[8,256]{1,0:T(8,128)S(1)} %get-tuple-element.18.own), channel_id=1, source_target_pairs={{0,8},{1,9},{2,10},{3,11},{4,12},{5,13},{6,14},{7,15},{16,24},{17,... | collective-permute-start | bytes 24584 | tf_op jit(solution)/shard_map/ppermute | solution.py:268
  43.5 0.6 collective-permute-start.13
  44.2 0.1 collective-permute-start.12
  44.3 0.0 copy-done.1
  44.3 0.3 shard_map.91.prev_gram
  44.6 0.0 collective-permute-done.15.d
  44.6 0.6 collective-permute-done.14.c
  45.2 0.0 collective-permute-done.13.b
  45.2 0.3 collective-permute-done.12.a
  45.4 1.4 %shard_map.92 = (f32[8,512]{1,0:T(8,128)S(1)}, f32[40,128]{1,0:T(8,128)S(1)}) custom-call(f32[8,256]{1,0:T(8,128)S(1)} %get-tuple-element.18.own, f32[8,256]{1,0:T(8,128)S(1)} %collective-permute-done.12.a, f32[8,256]{1,0:T(8,128)S(1)} %collective-permute-done.13.b, f32[8,256]{1,0:T(8,128)S(1)} %collective-permute-done.14.c, ...), custom_call_target="tpu_custom_call" | custom-call | flops 80000000 | bytes 900000 | tf_op jit(solution)/shard_map/pallas_call | solution.py:308
  46.9 42.2 %all-gather = f32[1280,128]{1,0:T(8,128)S(1)} all-gather(f32[40,128]{1,0:T(8,128)S(1)} %get-tuple-element.22), channel_id=2, replica_groups=mesh['dom'=32] {'dom'}, dimensions={0}, use_global_device_ids=true | all-gather | bytes 675840 | tf_op jit(solution)/shard_map/all_gather | solution.py:273
  89.1 0.1 reduce_sum.9.refs_0_
  89.1 1.0 %shard_map.93 = (f32[3,4,512]{2,1,0:T(4,128)}, f32[3,36,4]{2,1,0:T(8,128)S(1)}) custom-call(f32[40,128]{1,0:T(8,128)S(1)} %reduce_sum.9.refs_0_, f32[3,32,512]{2,1,0:T(8,128)S(1)} %copy-done.1, f32[8,512]{1,0:T(8,128)S(1)} %get-tuple-element.19.l0.refs_2_, f32[8,512]{1,0:T(8,128)S(1)} %get-tuple-element.20.l1.refs_3_, ...), custom_call_target="tpu_custom_call" | custom-call | flops 50000000 | bytes 400000 | tf_op jit(solution)/shard_map/pallas_call | solution.py:317
  90.2 0.7 copy.10
Async XLA Ops:
  0.6 0.9 %copy-start = (f32[3,32,512]{2,1,0:T(8,128)S(1)}, f32[3,32,512]{2,1,0:T(8,128)}, u32[]{:S(2)}) copy-start(f32[3,32,512]{2,1,0:T(8,128)} %refs_1_.1) | copy-start | bytes 589828
  1.6 0.7 copy-start.4
  2.2 0.7 copy-start.5
  2.9 0.7 copy-start.6
  3.6 10.5 %copy-start.7 = (s32[8,4]{0,1:T(4,128)S(1)}, s32[8,4]{0,1:T(4,128)}, u32[]{:S(2)}) copy-start(s32[8,4]{0,1:T(4,128)} %param.8) | copy-start | bytes 388
  3.9 11.5 %collective-permute-start.3 = (f32[8,256]{1,0:T(8,128)S(1)}, f32[8,256]{1,0:T(8,128)S(1)}, u32[]{:S(2)}, u32[]{:S(2)}) collective-permute-start(f32[8,256]{1,0:T(8,128)S(1)} %shard_map.86.own), channel_id=1, source_target_pairs={{8,16},{9,17},{10,18},{11,19},{12,20},{13,21},{14,22},{15,23},{16,... | collective-permute-start | bytes 24584 | tf_op jit(solution)/shard_map/ppermute | solution.py:268
  4.6 10.8 %collective-permute-start.2 = (f32[8,256]{1,0:T(8,128)S(1)}, f32[8,256]{1,0:T(8,128)S(1)}, u32[]{:S(2)}, u32[]{:S(2)}) collective-permute-start(f32[8,256]{1,0:T(8,128)S(1)} %shard_map.86.own), channel_id=1, source_target_pairs={{0,8},{1,9},{2,10},{3,11},{4,12},{5,13},{6,14},{7,15},{16,24},{17,... | collective-permute-start | bytes 24584 | tf_op jit(solution)/shard_map/ppermute | solution.py:268
  10.5 4.9 %collective-permute-start.1 = (f32[8,256]{1,0:T(8,128)S(1)}, f32[8,256]{1,0:T(8,128)S(1)}, u32[]{:S(2)}, u32[]{:S(2)}) collective-permute-start(f32[8,256]{1,0:T(8,128)S(1)} %shard_map.86.own), channel_id=1, source_target_pairs={{1,2},{3,4},{5,6},{7,8},{9,10},{11,12},{13,14},{15,16},{17,18},{19... | collective-permute-start | bytes 24584 | tf_op jit(solution)/shard_map/ppermute | solution.py:268
  11.2 4.3 %collective-permute-start = (f32[8,256]{1,0:T(8,128)S(1)}, f32[8,256]{1,0:T(8,128)S(1)}, u32[]{:S(2)}, u32[]{:S(2)}) collective-permute-start(f32[8,256]{1,0:T(8,128)S(1)} %shard_map.86.own), channel_id=1, source_target_pairs={{0,1},{2,3},{4,5},{6,7},{8,9},{10,11},{12,13},{14,15},{16,17},{18,... | collective-permute-start | bytes 24584 | tf_op jit(solution)/shard_map/ppermute | solution.py:268
  14.2 1.0 %copy-start.2 = (f32[512,256]{1,0:T(8,128)S(1)}, f32[512,256]{1,0:T(8,128)}, u32[]{:S(2)}) copy-start(f32[512,256]{1,0:T(8,128)} %strips_ref.1) | copy-start | bytes 1572868
  15.5 0.7 copy-start.3
  17.3 6.0 %collective-permute-start.7 = (f32[8,256]{1,0:T(8,128)S(1)}, f32[8,256]{1,0:T(8,128)S(1)}, u32[]{:S(2)}, u32[]{:S(2)}) collective-permute-start(f32[8,256]{1,0:T(8,128)S(1)} %get-tuple-element.15.refs_0_), channel_id=1, source_target_pairs={{8,16},{9,17},{10,18},{11,19},{12,20},{13,21},{14,22},{15,23},{16,... | collective-permute-start | bytes 24584 | tf_op jit(solution)/shard_map/ppermute | solution.py:268
  18.0 5.4 %collective-permute-start.6 = (f32[8,256]{1,0:T(8,128)S(1)}, f32[8,256]{1,0:T(8,128)S(1)}, u32[]{:S(2)}, u32[]{:S(2)}) collective-permute-start(f32[8,256]{1,0:T(8,128)S(1)} %get-tuple-element.15.refs_0_), channel_id=1, source_target_pairs={{0,8},{1,9},{2,10},{3,11},{4,12},{5,13},{6,14},{7,15},{16,24},{17,... | collective-permute-start | bytes 24584 | tf_op jit(solution)/shard_map/ppermute | solution.py:268
  21.6 1.8 %collective-permute-start.5 = (f32[8,256]{1,0:T(8,128)S(1)}, f32[8,256]{1,0:T(8,128)S(1)}, u32[]{:S(2)}, u32[]{:S(2)}) collective-permute-start(f32[8,256]{1,0:T(8,128)S(1)} %get-tuple-element.15.refs_0_), channel_id=1, source_target_pairs={{1,2},{3,4},{5,6},{7,8},{9,10},{11,12},{13,14},{15,16},{17,18},{19... | collective-permute-start | bytes 24584 | tf_op jit(solution)/shard_map/ppermute | solution.py:268
  22.2 1.9 %collective-permute-start.4 = (f32[8,256]{1,0:T(8,128)S(1)}, f32[8,256]{1,0:T(8,128)S(1)}, u32[]{:S(2)}, u32[]{:S(2)}) collective-permute-start(f32[8,256]{1,0:T(8,128)S(1)} %get-tuple-element.15.refs_0_), channel_id=1, source_target_pairs={{0,1},{2,3},{4,5},{6,7},{8,9},{10,11},{12,13},{14,15},{16,17},{18,... | collective-permute-start | bytes 24584 | tf_op jit(solution)/shard_map/ppermute | solution.py:268
  25.2 19.1 %copy-start.1 = (f32[3,32,512]{2,1,0:T(8,128)S(1)}, f32[3,32,512]{2,1,0:T(8,128)}, u32[]{:S(2)}) copy-start(f32[3,32,512]{2,1,0:T(8,128)} %refs_1_.1) | copy-start | bytes 589828
  25.2 8.6 %collective-permute-start.11 = (f32[8,256]{1,0:T(8,128)S(1)}, f32[8,256]{1,0:T(8,128)S(1)}, u32[]{:S(2)}, u32[]{:S(2)}) collective-permute-start(f32[8,256]{1,0:T(8,128)S(1)} %get-tuple-element.17.refs_0_), channel_id=1, source_target_pairs={{8,16},{9,17},{10,18},{11,19},{12,20},{13,21},{14,22},{15,23},{16,... | collective-permute-start | bytes 24584 | tf_op jit(solution)/shard_map/ppermute | solution.py:268
  26.0 8.7 %collective-permute-start.10 = (f32[8,256]{1,0:T(8,128)S(1)}, f32[8,256]{1,0:T(8,128)S(1)}, u32[]{:S(2)}, u32[]{:S(2)}) collective-permute-start(f32[8,256]{1,0:T(8,128)S(1)} %get-tuple-element.17.refs_0_), channel_id=1, source_target_pairs={{0,8},{1,9},{2,10},{3,11},{4,12},{5,13},{6,14},{7,15},{16,24},{17,... | collective-permute-start | bytes 24584 | tf_op jit(solution)/shard_map/ppermute | solution.py:268
  33.1 1.6 %collective-permute-start.9 = (f32[8,256]{1,0:T(8,128)S(1)}, f32[8,256]{1,0:T(8,128)S(1)}, u32[]{:S(2)}, u32[]{:S(2)}) collective-permute-start(f32[8,256]{1,0:T(8,128)S(1)} %get-tuple-element.17.refs_0_), channel_id=1, source_target_pairs={{1,2},{3,4},{5,6},{7,8},{9,10},{11,12},{13,14},{15,16},{17,18},{19... | collective-permute-start | bytes 24584 | tf_op jit(solution)/shard_map/ppermute | solution.py:268
  33.7 1.2 %collective-permute-start.8 = (f32[8,256]{1,0:T(8,128)S(1)}, f32[8,256]{1,0:T(8,128)S(1)}, u32[]{:S(2)}, u32[]{:S(2)}) collective-permute-start(f32[8,256]{1,0:T(8,128)S(1)} %get-tuple-element.17.refs_0_), channel_id=1, source_target_pairs={{0,1},{2,3},{4,5},{6,7},{8,9},{10,11},{12,13},{14,15},{16,17},{18,... | collective-permute-start | bytes 24584 | tf_op jit(solution)/shard_map/ppermute | solution.py:268
  35.9 8.7 %collective-permute-start.15 = (f32[8,256]{1,0:T(8,128)S(1)}, f32[8,256]{1,0:T(8,128)S(1)}, u32[]{:S(2)}, u32[]{:S(2)}) collective-permute-start(f32[8,256]{1,0:T(8,128)S(1)} %get-tuple-element.18.own), channel_id=1, source_target_pairs={{8,16},{9,17},{10,18},{11,19},{12,20},{13,21},{14,22},{15,23},{16,... | collective-permute-start | bytes 24584 | tf_op jit(solution)/shard_map/ppermute | solution.py:268
  36.6 8.6 %collective-permute-start.14 = (f32[8,256]{1,0:T(8,128)S(1)}, f32[8,256]{1,0:T(8,128)S(1)}, u32[]{:S(2)}, u32[]{:S(2)}) collective-permute-start(f32[8,256]{1,0:T(8,128)S(1)} %get-tuple-element.18.own), channel_id=1, source_target_pairs={{0,8},{1,9},{2,10},{3,11},{4,12},{5,13},{6,14},{7,15},{16,24},{17,... | collective-permute-start | bytes 24584 | tf_op jit(solution)/shard_map/ppermute | solution.py:268
  43.5 1.6 %collective-permute-start.13 = (f32[8,256]{1,0:T(8,128)S(1)}, f32[8,256]{1,0:T(8,128)S(1)}, u32[]{:S(2)}, u32[]{:S(2)}) collective-permute-start(f32[8,256]{1,0:T(8,128)S(1)} %get-tuple-element.18.own), channel_id=1, source_target_pairs={{1,2},{3,4},{5,6},{7,8},{9,10},{11,12},{13,14},{15,16},{17,18},{19... | collective-permute-start | bytes 24584 | tf_op jit(solution)/shard_map/ppermute | solution.py:268
  44.2 1.2 %collective-permute-start.12 = (f32[8,256]{1,0:T(8,128)S(1)}, f32[8,256]{1,0:T(8,128)S(1)}, u32[]{:S(2)}, u32[]{:S(2)}) collective-permute-start(f32[8,256]{1,0:T(8,128)S(1)} %get-tuple-element.18.own), channel_id=1, source_target_pairs={{0,1},{2,3},{4,5},{6,7},{8,9},{10,11},{12,13},{14,15},{16,17},{18,... | collective-permute-start | bytes 24584 | tf_op jit(solution)/shard_map/ppermute | solution.py:268

commit v3 on v0

v3 whole, which is shorter than its diff:
```python
import jax
import jax.numpy as jnp
from jax import lax
from jax.experimental import pallas as pl
from jax.experimental.pallas import tpu as pltpu
from jax.sharding import PartitionSpec as P

BLOCK = 64
S = 4
FAR = 8
COMPS = 3
DEAD = 1000.0
HIGHEST = lax.Precision.HIGHEST
NN = (((1,), (0,)), ((), ()))
NT = (((1,), (1,)), ((), ()))


def dot(a, b, dims=NN, precision=None):
    return lax.dot_general(a, b, dims, precision=precision, preferred_element_type=jnp.float32)


def iota(shape, axis):
    return lax.broadcasted_iota(jnp.int32, shape, axis)


def own_lanes(rows, width):
    return iota((rows, width), 1) // BLOCK == iota((rows, width), 0) % 8


def fold(masked):
    total = masked[:, :128]
    for t in range(1, masked.shape[1] // 128):
        total = total + masked[:, t * 128 : (t + 1) * 128]
    return total + pltpu.roll(total, BLOCK, 1)


def lines_of(tile, width):
    wide = jnp.concatenate([tile] * (width // 128), axis=1)
    wide = jnp.where(own_lanes(wide.shape[0], width), wide, 0.0)
    where = iota((8, width), 0)
    result = jnp.zeros((8, width), jnp.float32)
    for c in range(COMPS):
        line = jnp.sum(wide[c * 8 : (c + 1) * 8], axis=0, keepdims=True)
        result = jnp.where(where == c, jnp.broadcast_to(line, result.shape), result)
    return result


def fetch(pairs, sems):
    copies = [pltpu.make_async_copy(src, dst, sems.at[i]) for i, (src, dst) in enumerate(pairs)]
    for copy in copies:
        copy.start()
    return copies


def start_kernel(prev_in, mix_in, list_in, count_in, out_ref, prev_ref, mix_ref, list_ref, count_ref, sems):
    copies = fetch(
        [(prev_in, prev_ref), (mix_in, mix_ref), (list_in, list_ref), (count_in, count_ref)], sems
    )
    for copy in copies[1:]:
        copy.wait()
    comps, vecs, rows = prev_ref.shape
    mix = jnp.concatenate([mix_ref[...]] * comps, axis=1)
    mix = jnp.where(iota(mix.shape, 1) // vecs == iota(mix.shape, 0), mix, 0.0)
    order = list_ref[0].astype(jnp.float32)
    order = jnp.concatenate([order, jnp.zeros((4, 120), jnp.float32)], axis=1)
    meta = jnp.zeros((8, 128), jnp.float32)
    slot = iota((1, 128), 1)
    for link in range(4):
        live = slot < jnp.broadcast_to(count_ref[0:1, link : link + 1], slot.shape)
        line = jnp.where(live, order[link : link + 1], DEAD)
        line = pltpu.roll(jnp.broadcast_to(line, (8, 128)), 8 + 8 * link, 1)
        meta = jnp.where(iota((8, 128), 1) // 8 == link + 1, line, meta)
    out_ref[8 * comps :, :] = meta
    copies[0].wait()
    start = dot(mix, prev_ref[...].reshape(comps * vecs, rows), precision=HIGHEST)
    own = own_lanes(8, rows)
    for c in range(comps):
        line = jnp.broadcast_to(start[c : c + 1], own.shape)
        out_ref[c * 8 : (c + 1) * 8, :] = fold(jnp.where(own, line, 0.0))


def prepare_kernel(strips_in, columns_in, shifts_in, high_ref, low_ref, aux_ref, strips, columns, shifts, sems):
    parts = strips.shape[0]
    depth = strips.shape[1]
    pairs = [(columns_in, columns), (shifts_in, shifts)]
    pairs += [(strips_in.at[pl.ds(p * depth, depth)], strips.at[p]) for p in range(parts)]
    copies = fetch(pairs, sems)
    copies[0].wait()
    copies[1].wait()
    where = iota((8, 128), 1)
    table = jnp.zeros((8, 128), jnp.float32)
    eye = iota((8, 8), 0) == iota((8, 8), 1)
    for k in range(columns.shape[0]):
        line = jnp.broadcast_to(columns[k : k + 1, :].astype(jnp.float32), (8, 8))
        column = jnp.sum(jnp.where(eye, line, 0.0), axis=1, keepdims=True)
        table = jnp.where(where == k, column, table)
    for k in range(S):
        aux_ref[8 * k : 8 * k + 8, :] = jnp.full((8, 128), shifts[k], jnp.float32)
    aux_ref[8 * S :, :] = table
    for p in range(parts):
        copies[2 + p].wait()
        turned = strips[p].T
        high = turned.astype(jnp.bfloat16)
        high_ref[:, p * depth : (p + 1) * depth] = high
        low_ref[:, p * depth : (p + 1) * depth] = (turned - high.astype(jnp.float32)).astype(jnp.bfloat16)


def selection(table, metas, place):
    even, even_far = lax.rem(place, 2) == 0, lax.rem(place // FAR, 2) == 0
    slots = [
        (jnp.where(even, 48.0, 24.0), metas[1], metas[0], even),
        (jnp.where(even, 24.0, 48.0), metas[0], metas[1], even),
        (jnp.where(even_far, 96.0, 72.0), metas[3], metas[2], even_far),
        (jnp.where(even_far, 72.0, 96.0), metas[2], metas[3], even_far),
    ]
    lane = iota((1, 128), 1)
    target = lane.astype(jnp.float32)
    for link, (base, when, other, test) in enumerate(slots):
        target = jnp.where(lane // 8 == link + 1, jnp.where(test, when, other) + base, target)
    target = jnp.broadcast_to(target, (8, 128))
    lane = iota((8, 128), 1).astype(jnp.float32)
    at = [
        jnp.sum(jnp.where(lane == table[:, k : k + 1], target, 0.0), axis=1, keepdims=True)
        for k in range(4)
    ]
    lane = iota((8, 256), 1).astype(jnp.float32)
    groups = []
    for pair in range(2):
        for c in range(COMPS):
            first = lane == at[2 * pair] + float(8 * c)
            second = lane == at[2 * pair + 1] + float(8 * c + 120)
            groups.append((first | second).astype(jnp.float32))
    return jnp.concatenate(groups, axis=0)


def multiply(choose, pieces, shift, high, low):
    rows = 8 * COMPS
    ext = jnp.concatenate(pieces, axis=0)
    front = iota(ext.shape, 1) < BLOCK
    top = ext.astype(jnp.bfloat16).astype(jnp.float32)
    rest = ext - top
    zero = jnp.zeros_like(ext)
    picked = jnp.concatenate(
        [
            jnp.concatenate([jnp.where(front, top, zero), jnp.where(front, rest, zero)], axis=1),
            jnp.concatenate([jnp.where(front, zero, top), jnp.where(front, zero, rest)], axis=1),
            jnp.zeros((256 - 2 * ext.shape[0], 256), jnp.float32),
        ],
        axis=0,
    ).astype(jnp.bfloat16)
    x = dot(choose.astype(jnp.bfloat16), picked)
    left = jnp.concatenate(
        [
            jnp.concatenate([x[:rows, :128], x[rows:, :128]], axis=1),
            jnp.concatenate([x[:rows, 128:], x[rows:, 128:]], axis=1),
        ],
        axis=0,
    ).astype(jnp.bfloat16)
    both = dot(left, high) + dot(left, low)
    image = both[:rows] + both[rows:]
    image = fold(jnp.where(own_lanes(rows, image.shape[1]), image, 0.0))
    return image - jnp.concatenate([shift] * COMPS, axis=0) * pieces[0]


def first_kernel(own, a, b, c, d, aux, high, low, tile_ref, choose_ref):
    rows = 8 * COMPS
    refs = (own, a, b, c, d)
    pieces = [ref[:rows, :] for ref in refs]
    metas = [ref[rows : rows + 1, :] for ref in refs[1:]]
    choose = selection(aux[8 * S :, :], metas, lax.axis_index("dom"))
    choose_ref[...] = choose
    tile_ref[...] = multiply(choose, pieces, aux[:8, :], high[...], low[...])


def middle_kernel(step, own, a, b, c, d, choose, aux, high, low, tile_ref):
    pieces = [ref[...] for ref in (own, a, b, c, d)]
    tile_ref[...] = multiply(choose[...], pieces, aux[8 * step : 8 * step + 8, :], high[...], low[...])


def collect(gram, width, vecs):
    lane, comp = iota(gram.shape, 1), iota(gram.shape, 0)
    mine = jnp.where(lane < width, lane // vecs, lane % 8) == comp
    return jnp.sum(jnp.where(mine, gram, 0.0), axis=0, keepdims=True)


def early_kernel(prev_ref, t0, t1, t2, lines_ref, gram_ref):
    comps, vecs, rows = prev_ref.shape
    width = comps * vecs
    lines = jnp.concatenate([lines_of(t[...], rows) for t in (t0, t1, t2)], axis=0)
    lines_ref[...] = lines
    prev = prev_ref[...].reshape(width, rows)
    full = dot(prev, prev, NT, HIGHEST)
    owner = iota((vecs, width), 1) // vecs
    total = jnp.where(owner == 0, full[:vecs], 0.0)
    for c in range(1, comps):
        total = total + jnp.where(owner == c, full[c * vecs : (c + 1) * vecs], 0.0)
    gram_ref[:vecs, :] = jnp.concatenate([total, jnp.zeros((vecs, 128 - width), jnp.float32)], axis=1)
    against = jnp.concatenate([prev, lines, jnp.zeros((8, rows), jnp.float32)], axis=0)
    gram = dot(lines, against, NT, HIGHEST)
    result = jnp.zeros((8, 128), jnp.float32)
    for k in range(S - 1):
        line = collect(gram[k * 8 : (k + 1) * 8], width, vecs)
        result = jnp.where(iota((8, 128), 0) == k, jnp.broadcast_to(line, result.shape), result)
    gram_ref[vecs:, :] = result


def last_kernel(own, a, b, c, d, choose, aux, high, low, lines, prev_ref, early, line_ref, gram_ref):
    pieces = [ref[...] for ref in (own, a, b, c, d)]
    tile = multiply(choose[...], pieces, aux[8 * S - 8 : 8 * S, :], high[...], low[...])
    comps, vecs, rows = prev_ref.shape
    width = comps * vecs
    last = lines_of(tile, rows)
    line_ref[...] = last
    against = jnp.concatenate([prev_ref[...].reshape(width, rows), lines[...], last], axis=0)
    line = collect(dot(last, against, NT, HIGHEST), width, vecs)
    gram_ref[:vecs, :] = early[:vecs, :]
    gram_ref[vecs:, :] = jnp.where(
        iota((8, 128), 0) == S - 1, jnp.broadcast_to(line, (8, 128)), early[vecs:, :]
    )


def finish_kernel(total, mine_ref, other_ref, prev_ref, lines, last, basis_ref, factors_ref):
    comps, vecs, rows = prev_ref.shape
    width = comps * vecs
    odd = lax.rem(lax.axis_index("dom"), 2) == 1
    gram = jnp.where(odd, mine_ref[...], other_ref[...]) * (1.0 / total)
    small = gram[vecs:]
    lane, comp = iota((8, 128), 1), iota((8, 128), 0)
    in_prev = (lane < width) & (lane // vecs == comp)
    coef, cross = [], []
    for k in range(S):
        line = jnp.broadcast_to(small[k : k + 1], (8, 128))
        coef.append(jnp.where(in_prev, line, 0.0))
        cross.append([jnp.where(lane == width + 8 * l + comp, line, 0.0) for l in range(k + 1)])
    coefs = jnp.concatenate(coef, axis=0)
    prev = prev_ref[...].reshape(width, rows)
    basis = jnp.concatenate([lines[...], last[...]], axis=0)
    projected = basis - dot(coefs[:, :width], prev, precision=HIGHEST)
    square = jnp.concatenate([gram[:vecs]] * comps, axis=0)
    r, q = iota(square.shape, 0), iota(square.shape, 1)
    square = jnp.where(r // vecs == q // vecs, square, 0.0) - jnp.where(r == q, 2.0, 0.0)
    turned = dot(coefs[:, :width], square, precision=HIGHEST)
    entry = {}
    for k in range(S):
        for l in range(k + 1):
            value = turned[k * 8 : (k + 1) * 8] * coef[l] + cross[k][l]
            entry[k, l] = jnp.sum(value, axis=1, keepdims=True)
    lower = {}
    for k in range(S):
        for l in range(k + 1):
            value = entry[k, l]
            for m in range(l):
                value = value - lower[k, m] * lower[l, m]
            lower[k, l] = jnp.sqrt(value) if l == k else value / lower[l, l]
    vectors = []
    for k in range(S):
        value = projected[k * 8 : (k + 1) * 8]
        for l in range(k):
            value = value - lower[k, l] * vectors[l]
        value = value / lower[k, k]
        vectors.append(value)
        for c in range(comps):
            basis_ref[c, k : k + 1, :] = value[c : c + 1]
    for c in range(comps):
        factors_ref[c, :, :vecs] = small[:S, c * vecs : (c + 1) * vecs]
    for k in range(S):
        line = jnp.zeros((8, 128), jnp.float32)
        for l in range(k + 1):
            line = jnp.where(lane == l, lower[k, l], line)
        for c in range(comps):
            factors_ref[c, k : k + 1, vecs:] = line[c : c + 1, :S]


VMEM = pl.BlockSpec(memory_space=pltpu.VMEM)
HBM = pl.BlockSpec(memory_space=pltpu.HBM)


def in_hbm(*arrays):
    return [pltpu.with_memory_space_constraint(x, pltpu.HBM) for x in arrays]


def call(kernel, outs, specs, flops, moved, scratch=()):
    shapes = [jax.ShapeDtypeStruct(shape, kind) for shape, kind in outs]
    return pl.pallas_call(
        kernel,
        out_shape=shapes if len(shapes) > 1 else shapes[0],
        in_specs=specs,
        out_specs=[VMEM] * len(shapes) if len(shapes) > 1 else VMEM,
        scratch_shapes=list(scratch),
        compiler_params=pltpu.CompilerParams(vmem_limit_bytes=24 * 1024 * 1024),
        cost_estimate=pl.CostEstimate(flops=flops, bytes_accessed=moved, transcendentals=0),
    )


def pairs_of(length, step, odd):
    firsts = [d for d in range(length - step) if (d // step) % 2 == odd]
    return [(d, d + step) for d in firsts] + [(d + step, d) for d in firsts]


def ghosts(tile):
    length = lax.axis_size("dom")
    near = lax.ppermute(tile, "dom", pairs_of(length, 1, 0))
    far_odd = lax.ppermute(tile, "dom", pairs_of(length, FAR, 1))
    far_even = lax.ppermute(tile, "dom", pairs_of(length, FAR, 0))
    across = lax.ppermute(tile, "dom", pairs_of(length, 1, 1))
    return near, across, far_even, far_odd


def summed(value):
    length = lax.axis_size("dom")
    value = value + lax.ppermute(value, "dom", [(d, d ^ 1) for d in range(length)])
    step = 2
    while step < length:
        value = value + lax.ppermute(value, "dom", [(d, d ^ step) for d in range(1, length, 2)])
        step *= 2
    return value, lax.ppermute(value, "dom", [(d, d ^ 1) for d in range(length)])


def local(strips, columns, send_list, send_count, shifts, prev_basis, mix):
    comps, vecs, rows = prev_basis.shape
    blocks = columns.shape[0]
    width = strips.shape[1]
    f32, bf16, dma = jnp.float32, jnp.bfloat16, pltpu.SemaphoreType.DMA
    tile_out = ((comps * blocks, 128), f32)
    tile = call(
        start_kernel,
        [((comps * blocks + 8, 128), f32)],
        [HBM] * 4,
        600000,
        250000,
        [
            pltpu.VMEM(prev_basis.shape, f32),
            pltpu.VMEM(mix.shape, f32),
            pltpu.VMEM(send_list.shape, jnp.int32),
            pltpu.VMEM(send_count.shape, jnp.int32),
            dma((4,)),
        ],
    )(*in_hbm(prev_basis, mix, send_list, send_count))
    high, low, aux = call(
        prepare_kernel,
        [((width, rows), bf16), ((width, rows), bf16), ((8 * S + 8, 128), f32)],
        [HBM] * 3,
        1000000,
        1000000,
        [
            pltpu.VMEM((4, rows // 4, width), f32),
            pltpu.VMEM(columns.shape[::-1], jnp.int32),
            pltpu.SMEM(shifts.shape, f32),
            dma((6,)),
        ],
    )(*in_hbm(strips, columns.T, shifts))
    tiles = []
    tile, choose = call(
        first_kernel, [tile_out, ((2 * comps * blocks, 256), f32)], [VMEM] * 8, 50000000, 600000
    )(tile, *ghosts(tile), aux, high, low)
    tiles.append(tile)
    for step in (1, 2):
        tile = call(
            lambda *refs, step=step: middle_kernel(step, *refs), [tile_out], [VMEM] * 9, 50000000, 600000
        )(tile, *ghosts(tile), choose, aux, high, low)
        tiles.append(tile)
    received = ghosts(tile)
    gram_out = ((vecs + 8, 128), f32)
    lines, early = call(
        early_kernel, [((8 * S - 8, rows), f32), gram_out], [VMEM] * 4, 60000000, 250000
    )(prev_basis, *tiles)
    last, gram = call(
        last_kernel, [((8, rows), f32), gram_out], [VMEM] * 12, 80000000, 900000
    )(tile, *received, choose, aux, high, low, lines, prev_basis, early)
    total = float(lax.axis_size("dom") * rows)
    basis, factors = call(
        lambda *refs: finish_kernel(total, *refs),
        [((comps, S, rows), f32), ((comps, S, vecs + S), f32)],
        [VMEM] * 5,
        50000000,
        400000,
    )(*summed(gram), prev_basis, lines, last)
    return basis, jnp.swapaxes(factors, 1, 2)


def solution(mesh):
    in_specs = (
        P("dom", None),
        P("dom", None),
        P("dom", None, None),
        P("dom", None),
        P(),
        P(None, None, "dom"),
        P(),
    )
    out_specs = (P(None, None, "dom"), P())
    return jax.shard_map(local, mesh=mesh, in_specs=in_specs, out_specs=out_specs, check_vma=False)
```

time: 176 us -> 68 us (0.39)
  blocking collectives: 78 us -> 0 us
  local copies, waits for them, and re-layouts: 18.9 us -> 0.01 us
  waiting for transfers between devices: 11.8 us -> 4.34 us
  matrix products: 7.28 us -> 0 us
  other arithmetic: 7.22 us -> 0.03 us
  Pallas kernels: 0 us -> 6.44 us
  starting transfers between devices: 51 us -> 55.8 us
    psum x2 -> x0, blocking collectives: 78 us -> none  [the longest x1 40.2 us: local(): gram = lax.psum(local_gram, 'dom') / total]
    gather x20 -> x0, local copies, waits for them, and re-layouts: 11.7 us -> none  [the longest x16 9.23 us: local(): packed = jnp.take(vec, send_list[0, link], axis=1)]
    ppermute x16 -> x22, waiting for transfers between devices: 11.8 us -> 4.34 us  [the longest x2 1.69 us: summed(): lax.ppermute(value, 'dom', [(d, d ^ 1) for d in range(length)])]
    pallas_call x0 -> x8, Pallas kernels: none -> 6.44 us  [the longest x1 1.39 us: local(): call(prepare_kernel, [((width, rows), bf16), ((width, rows), bf16), ((8 *...]
    dot_general x8 -> x0, matrix products: 6.4 us -> none  [the longest x4 4.59 us: local(): jnp.einsum('rik,crk->cri', matrix, picked, precision=lax.Precision.HIGHEST)]
    ppermute x16 -> x22, starting transfers between devices: 51 us -> 55.8 us  [the longest x4 23.6 us: ghosts(): far_even = lax.ppermute(tile, 'dom', pairs_of(length, FAR, 0))]
    reshape x39 -> x0, local copies, waits for them, and re-layouts: 3 us -> none  [the longest x16 1.27 us: local(): jnp.where(live, packed, jnp.zeros_like(packed))]
    lt x4 -> x0, other arithmetic: 2.51 us -> none  [local(): live = slots[None, :, None] < send_count[0, link]]
  transfers between devices with their start and end apart: 16 -> 22, of which waited for: 3 -> 7; matrix products, arithmetic and copies ran while one was open for 4% -> 0% of each run, Pallas kernels for 0% -> 3%
where the time goes in v3:
time: 68 us; the launch traced here: 67.5 us
  starting transfers between devices  55.8 us (82%)
  Pallas kernels  6.44 us (9%)
  waiting for transfers between devices  4.34 us (6%)
  between operations  0.9 us (1%)
    ppermute x4, starting transfers between devices, ghosts(): far_even = lax.ppermute(tile, 'dom', pairs_of(length, FAR, 0))  23.6 us
    ppermute x2, starting transfers between devices, summed(): lax.ppermute(value, 'dom', [(d, d ^ 1) for d in range(length)])  20 us
    ppermute x4, starting transfers between devices, ghosts(): near = lax.ppermute(tile, 'dom', pairs_of(length, 1, 0))  4.18 us
    ppermute x4, starting transfers between devices, ghosts(): far_odd = lax.ppermute(tile, 'dom', pairs_of(length, FAR, 1))  2.77 us
    ppermute x4, starting transfers between devices, summed(): lax.ppermute(value, 'dom', [(d, d ^ step) for d in range(1, length, 2)])  2.64 us
    ppermute x4, starting transfers between devices, ghosts(): across = lax.ppermute(tile, 'dom', pairs_of(length, 1, 1))  2.6 us
    ppermute x2, waiting for transfers between devices, summed(): lax.ppermute(value, 'dom', [(d, d ^ 1) for d in range(length)])  1.69 us
    pallas_call x1, Pallas kernels, local(): call(prepare_kernel, [((width, rows), bf16), ((width, rows), bf16), ((8 *...  1.39 us
  transfers between devices with their start and end apart: 22, of which 7 were waited for; matrix products, arithmetic and copies ran while one was open for 0% of the time, Pallas kernels for 3%

profile of v3, /device:TPU:0, one launch (start us, length us, event | category | flops | bytes accessed | tf_op | source)
XLA Modules:
  0.0 67.5 jit_solution(5877927639035531595)
XLA Ops:
  0.6 1.3 %shard_map.86.own = f32[32,128]{1,0:T(8,128)S(1)} custom-call(f32[3,32,512]{2,1,0:T(8,128)} %refs_2_.1, f32[3,32]{1,0:T(4,128)} %mix_in.1, s32[1,4,8]{2,1,0:T(4,128)} %list_in.1, s32[1,4]{1,0:T(1,128)} %count_in.1), custom_call_target="tpu_custom_call" | custom-call | flops 600000 | bytes 250000 | tf_op jit(solution)/shard_map/pallas_call | solution.py:325
  1.9 0.7 collective-permute-start.3
  2.6 5.9 %collective-permute-start.2 = (f32[32,128]{1,0:T(8,128)S(1)}, f32[32,128]{1,0:T(8,128)S(1)}, u32[]{:S(2)}, u32[]{:S(2)}) collective-permute-start(f32[32,128]{1,0:T(8,128)S(1)} %shard_map.86.own), channel_id=1, source_target_pairs={{0,8},{1,9},{2,10},{3,11},{4,12},{5,13},{6,14},{7,15},{16,24},{17,... | collective-permute-start | bytes 49160 | tf_op jit(solution)/shard_map/ppermute | solution.py:304
  8.5 0.7 collective-permute-start.1
  9.1 2.9 %collective-permute-start = (f32[32,128]{1,0:T(8,128)S(1)}, f32[32,128]{1,0:T(8,128)S(1)}, u32[]{:S(2)}, u32[]{:S(2)}) collective-permute-start(f32[32,128]{1,0:T(8,128)S(1)} %shard_map.86.own), channel_id=1, source_target_pairs={{0,1},{2,3},{4,5},{6,7},{8,9},{10,11},{12,13},{14,15},{16,17},{18,... | collective-permute-start | bytes 49160 | tf_op jit(solution)/shard_map/ppermute | solution.py:302
  12.1 1.4 %shard_map.87 = (bf16[256,512]{1,0:T(8,128)(2,1)S(1)}, bf16[256,512]{1,0:T(8,128)(2,1)S(1)}, f32[40,128]{1,0:T(8,128)S(1)}) custom-call(f32[512,256]{1,0:T(8,128)} %strips_in.1, s32[4,8]{1,0:T(4,128)} %bitcast.2, f32[4]{0:T(128)} %shifts_in.1), custom_call_target="tpu_custom_call" | custom-call | flops 1000000 | bytes 1000000 | tf_op jit(solution)/shard_map/pallas_call | solution.py:339
  13.5 0.0 collective-permute-done.3.d
  13.5 0.0 collective-permute-done.2.c
  13.5 0.0 collective-permute-done.1.b
  13.5 0.0 collective-permute-done.a
  13.5 0.6 shard_map.88
  14.1 0.7 collective-permute-start.7
  14.7 3.6 %collective-permute-start.6 = (f32[24,128]{1,0:T(8,128)S(1)}, f32[24,128]{1,0:T(8,128)S(1)}, u32[]{:S(2)}, u32[]{:S(2)}) collective-permute-start(f32[24,128]{1,0:T(8,128)S(1)} %get-tuple-element.16.refs_0_.t0), channel_id=1, source_target_pairs={{0,8},{1,9},{2,10},{3,11},{4,12},{5,13},{6,14},{7,15},{16,24},{17,... | collective-permute-start | bytes 36872 | tf_op jit(solution)/shard_map/ppermute | solution.py:304
  18.3 0.7 collective-permute-start.5
  19.0 1.1 %collective-permute-start.4 = (f32[24,128]{1,0:T(8,128)S(1)}, f32[24,128]{1,0:T(8,128)S(1)}, u32[]{:S(2)}, u32[]{:S(2)}) collective-permute-start(f32[24,128]{1,0:T(8,128)S(1)} %get-tuple-element.16.refs_0_.t0), channel_id=1, source_target_pairs={{0,1},{2,3},{4,5},{6,7},{8,9},{10,11},{12,13},{14,15},{16,17},{18,... | collective-permute-start | bytes 36872 | tf_op jit(solution)/shard_map/ppermute | solution.py:302
  20.1 0.0 collective-permute-done.7.refs_4_
  20.1 0.0 collective-permute-done.6.refs_3_
  20.1 0.0 collective-permute-done.5.refs_2_
  20.1 0.8 %collective-permute-done.4.refs_1_ = f32[24,128]{1,0:T(8,128)S(1)} collective-permute-done((f32[24,128]{1,0:T(8,128)S(1)}, f32[24,128]{1,0:T(8,128)S(1)}, u32[]{:S(2)}, u32[]{:S(2)}) %collective-permute-start.4) | collective-permute-done | bytes 12320 | tf_op jit(solution)/shard_map/ppermute | solution.py:302
  20.9 0.4 shard_map.89.refs_0_.t1
  21.4 0.0 copy-start
  21.4 0.8 %collective-permute-start.11 = (f32[24,128]{1,0:T(8,128)S(1)}, f32[24,128]{1,0:T(8,128)S(1)}, u32[]{:S(2)}, u32[]{:S(2)}) collective-permute-start(f32[24,128]{1,0:T(8,128)S(1)} %shard_map.89.refs_0_.t1), channel_id=1, source_target_pairs={{8,16},{9,17},{10,18},{11,19},{12,20},{13,21},{14,22},{15,23},{16,... | collective-permute-start | bytes 36872 | tf_op jit(solution)/shard_map/ppermute | solution.py:303
  22.2 7.1 %collective-permute-start.10 = (f32[24,128]{1,0:T(8,128)S(1)}, f32[24,128]{1,0:T(8,128)S(1)}, u32[]{:S(2)}, u32[]{:S(2)}) collective-permute-start(f32[24,128]{1,0:T(8,128)S(1)} %shard_map.89.refs_0_.t1), channel_id=1, source_target_pairs={{0,8},{1,9},{2,10},{3,11},{4,12},{5,13},{6,14},{7,15},{16,24},{17,... | collective-permute-start | bytes 36872 | tf_op jit(solution)/shard_map/ppermute | solution.py:304
  29.3 0.7 collective-permute-start.9
  29.9 0.1 collective-permute-start.8
  30.0 0.0 collective-permute-done.11.refs_4_
  30.0 0.9 %collective-permute-done.10.refs_3_ = f32[24,128]{1,0:T(8,128)S(1)} collective-permute-done((f32[24,128]{1,0:T(8,128)S(1)}, f32[24,128]{1,0:T(8,128)S(1)}, u32[]{:S(2)}, u32[]{:S(2)}) %collective-permute-start.10) | collective-permute-done | bytes 12320 | tf_op jit(solution)/shard_map/ppermute | solution.py:304
  31.0 0.0 collective-permute-done.9.refs_2_
  31.0 0.2 collective-permute-done.8.refs_1_
  31.2 0.4 shard_map.90.t2.own
  31.6 0.7 collective-permute-start.15
  32.3 7.0 %collective-permute-start.14 = (f32[24,128]{1,0:T(8,128)S(1)}, f32[24,128]{1,0:T(8,128)S(1)}, u32[]{:S(2)}, u32[]{:S(2)}) collective-permute-start(f32[24,128]{1,0:T(8,128)S(1)} %shard_map.90.t2.own), channel_id=1, source_target_pairs={{0,8},{1,9},{2,10},{3,11},{4,12},{5,13},{6,14},{7,15},{16,24},{17,... | collective-permute-start | bytes 36872 | tf_op jit(solution)/shard_map/ppermute | solution.py:304
  39.3 0.7 collective-permute-start.13
  39.9 0.1 collective-permute-start.12
  40.0 0.0 copy-done
  40.0 0.5 shard_map.91
  40.5 0.0 collective-permute-done.15.d
  40.5 0.4 collective-permute-done.14.c
  40.9 0.0 collective-permute-done.13.b
  40.9 0.2 collective-permute-done.12.a
  41.2 0.8 %shard_map.92 = (f32[8,512]{1,0:T(8,128)S(1)}, f32[40,128]{1,0:T(8,128)S(1)}) custom-call(f32[24,128]{1,0:T(8,128)S(1)} %shard_map.90.t2.own, f32[24,128]{1,0:T(8,128)S(1)} %collective-permute-done.12.a, f32[24,128]{1,0:T(8,128)S(1)} %collective-permute-done.13.b, f32[24,128]{1,0:T(8,128)S(1)} %collective-permute-done.14.c, ...), custom_call_target="tpu_custom_call" | custom-call | flops 80000000 | bytes 900000 | tf_op jit(solution)/shard_map/pallas_call | solution.py:367
  42.0 0.9 %collective-permute-start.16 = (f32[40,128]{1,0:T(8,128)S(1)}, f32[40,128]{1,0:T(8,128)S(1)}, u32[]{:S(2)}, u32[]{:S(2)}) collective-permute-start(f32[40,128]{1,0:T(8,128)S(1)} %get-tuple-element.20), channel_id=1, source_target_pairs={{0,1},{1,0},{2,3},{3,2},{4,5},{5,4},{6,7},{7,6},{8,9},{9,8},{10,11... | collective-permute-start | bytes 61448 | tf_op jit(solution)/shard_map/ppermute | solution.py:311
  42.8 0.8 %collective-permute-done.16 = f32[40,128]{1,0:T(8,128)S(1)} collective-permute-done((f32[40,128]{1,0:T(8,128)S(1)}, f32[40,128]{1,0:T(8,128)S(1)}, u32[]{:S(2)}, u32[]{:S(2)}) %collective-permute-start.16) | collective-permute-done | bytes 20512 | tf_op jit(solution)/shard_map/ppermute | solution.py:311
  43.7 0.7 collective-permute-start.17
  44.3 0.0 collective-permute-done.17
  44.4 0.7 collective-permute-start.18
  45.0 0.0 collective-permute-done.18
  45.1 0.7 collective-permute-start.19
  45.7 0.0 collective-permute-done.19
  45.8 0.7 collective-permute-start.20
  46.4 0.0 collective-permute-done.20
  46.5 19.2 %collective-permute-start.21 = (f32[40,128]{1,0:T(8,128)S(1)}, f32[40,128]{1,0:T(8,128)S(1)}, u32[]{:S(2)}, u32[]{:S(2)}) collective-permute-start(f32[40,128]{1,0:T(8,128)S(1)} %add.19.refs_0_), channel_id=1, source_target_pairs={{0,1},{1,0},{2,3},{3,2},{4,5},{5,4},{6,7},{7,6},{8,9},{9,8},{10,11... | collective-permute-start | bytes 61448 | tf_op jit(solution)/shard_map/ppermute | solution.py:316
  65.6 0.8 %collective-permute-done.21.refs_1_ = f32[40,128]{1,0:T(8,128)S(1)} collective-permute-done((f32[40,128]{1,0:T(8,128)S(1)}, f32[40,128]{1,0:T(8,128)S(1)}, u32[]{:S(2)}, u32[]{:S(2)}) %collective-permute-start.21) | collective-permute-done | bytes 20512 | tf_op jit(solution)/shard_map/ppermute | solution.py:316
  66.5 1.1 %shard_map.93 = (f32[3,4,512]{2,1,0:T(4,128)}, f32[3,4,36]{2,1,0:T(4,128)}) custom-call(f32[40,128]{1,0:T(8,128)S(1)} %add.19.refs_0_, f32[40,128]{1,0:T(8,128)S(1)} %collective-permute-done.21.refs_1_, f32[3,32,512]{2,1,0:T(8,128)S(1)} %copy-done, f32[24,512]{1,0:T(8,128)S(1)} %get-tuple-element.18.lines.refs_3_, f32[8,512]{1,0:T(8,128)S(1)} %get-tuple-element.21.refs_4_), custom_call_target="tpu_custom_call" | custom-call | flops 50000000 | bytes 400000 | tf_op jit(solution)/shard_map/pallas_call | solution.py:371
  (5 shorter events, 0.0 us)
Async XLA Ops:
  1.9 11.6 %collective-permute-start.3 = (f32[32,128]{1,0:T(8,128)S(1)}, f32[32,128]{1,0:T(8,128)S(1)}, u32[]{:S(2)}, u32[]{:S(2)}) collective-permute-start(f32[32,128]{1,0:T(8,128)S(1)} %shard_map.86.own), channel_id=1, source_target_pairs={{8,16},{9,17},{10,18},{11,19},{12,20},{13,21},{14,22},{15,23},{16,... | collective-permute-start | bytes 49160 | tf_op jit(solution)/shard_map/ppermute | solution.py:303
  2.6 10.9 %collective-permute-start.2 = (f32[32,128]{1,0:T(8,128)S(1)}, f32[32,128]{1,0:T(8,128)S(1)}, u32[]{:S(2)}, u32[]{:S(2)}) collective-permute-start(f32[32,128]{1,0:T(8,128)S(1)} %shard_map.86.own), channel_id=1, source_target_pairs={{0,8},{1,9},{2,10},{3,11},{4,12},{5,13},{6,14},{7,15},{16,24},{17,... | collective-permute-start | bytes 49160 | tf_op jit(solution)/shard_map/ppermute | solution.py:304
  8.5 5.0 %collective-permute-start.1 = (f32[32,128]{1,0:T(8,128)S(1)}, f32[32,128]{1,0:T(8,128)S(1)}, u32[]{:S(2)}, u32[]{:S(2)}) collective-permute-start(f32[32,128]{1,0:T(8,128)S(1)} %shard_map.86.own), channel_id=1, source_target_pairs={{1,2},{3,4},{5,6},{7,8},{9,10},{11,12},{13,14},{15,16},{17,18},{19... | collective-permute-start | bytes 49160 | tf_op jit(solution)/shard_map/ppermute | solution.py:305
  9.1 4.4 %collective-permute-start = (f32[32,128]{1,0:T(8,128)S(1)}, f32[32,128]{1,0:T(8,128)S(1)}, u32[]{:S(2)}, u32[]{:S(2)}) collective-permute-start(f32[32,128]{1,0:T(8,128)S(1)} %shard_map.86.own), channel_id=1, source_target_pairs={{0,1},{2,3},{4,5},{6,7},{8,9},{10,11},{12,13},{14,15},{16,17},{18,... | collective-permute-start | bytes 49160 | tf_op jit(solution)/shard_map/ppermute | solution.py:302
  14.1 6.1 %collective-permute-start.7 = (f32[24,128]{1,0:T(8,128)S(1)}, f32[24,128]{1,0:T(8,128)S(1)}, u32[]{:S(2)}, u32[]{:S(2)}) collective-permute-start(f32[24,128]{1,0:T(8,128)S(1)} %get-tuple-element.16.refs_0_.t0), channel_id=1, source_target_pairs={{8,16},{9,17},{10,18},{11,19},{12,20},{13,21},{14,22},{15,23},{16,... | collective-permute-start | bytes 36872 | tf_op jit(solution)/shard_map/ppermute | solution.py:303
  14.7 5.4 %collective-permute-start.6 = (f32[24,128]{1,0:T(8,128)S(1)}, f32[24,128]{1,0:T(8,128)S(1)}, u32[]{:S(2)}, u32[]{:S(2)}) collective-permute-start(f32[24,128]{1,0:T(8,128)S(1)} %get-tuple-element.16.refs_0_.t0), channel_id=1, source_target_pairs={{0,8},{1,9},{2,10},{3,11},{4,12},{5,13},{6,14},{7,15},{16,24},{17,... | collective-permute-start | bytes 36872 | tf_op jit(solution)/shard_map/ppermute | solution.py:304
  18.3 1.8 %collective-permute-start.5 = (f32[24,128]{1,0:T(8,128)S(1)}, f32[24,128]{1,0:T(8,128)S(1)}, u32[]{:S(2)}, u32[]{:S(2)}) collective-permute-start(f32[24,128]{1,0:T(8,128)S(1)} %get-tuple-element.16.refs_0_.t0), channel_id=1, source_target_pairs={{1,2},{3,4},{5,6},{7,8},{9,10},{11,12},{13,14},{15,16},{17,18},{19... | collective-permute-start | bytes 36872 | tf_op jit(solution)/shard_map/ppermute | solution.py:305
  19.0 2.0 %collective-permute-start.4 = (f32[24,128]{1,0:T(8,128)S(1)}, f32[24,128]{1,0:T(8,128)S(1)}, u32[]{:S(2)}, u32[]{:S(2)}) collective-permute-start(f32[24,128]{1,0:T(8,128)S(1)} %get-tuple-element.16.refs_0_.t0), channel_id=1, source_target_pairs={{0,1},{2,3},{4,5},{6,7},{8,9},{10,11},{12,13},{14,15},{16,17},{18,... | collective-permute-start | bytes 36872 | tf_op jit(solution)/shard_map/ppermute | solution.py:302
  21.4 18.6 %copy-start = (f32[3,32,512]{2,1,0:T(8,128)S(1)}, f32[3,32,512]{2,1,0:T(8,128)}, u32[]{:S(2)}) copy-start(f32[3,32,512]{2,1,0:T(8,128)} %refs_2_.1) | copy-start | bytes 589828
  21.4 8.6 %collective-permute-start.11 = (f32[24,128]{1,0:T(8,128)S(1)}, f32[24,128]{1,0:T(8,128)S(1)}, u32[]{:S(2)}, u32[]{:S(2)}) collective-permute-start(f32[24,128]{1,0:T(8,128)S(1)} %shard_map.89.refs_0_.t1), channel_id=1, source_target_pairs={{8,16},{9,17},{10,18},{11,19},{12,20},{13,21},{14,22},{15,23},{16,... | collective-permute-start | bytes 36872 | tf_op jit(solution)/shard_map/ppermute | solution.py:303
  22.2 8.8 %collective-permute-start.10 = (f32[24,128]{1,0:T(8,128)S(1)}, f32[24,128]{1,0:T(8,128)S(1)}, u32[]{:S(2)}, u32[]{:S(2)}) collective-permute-start(f32[24,128]{1,0:T(8,128)S(1)} %shard_map.89.refs_0_.t1), channel_id=1, source_target_pairs={{0,8},{1,9},{2,10},{3,11},{4,12},{5,13},{6,14},{7,15},{16,24},{17,... | collective-permute-start | bytes 36872 | tf_op jit(solution)/shard_map/ppermute | solution.py:304
  29.3 1.7 %collective-permute-start.9 = (f32[24,128]{1,0:T(8,128)S(1)}, f32[24,128]{1,0:T(8,128)S(1)}, u32[]{:S(2)}, u32[]{:S(2)}) collective-permute-start(f32[24,128]{1,0:T(8,128)S(1)} %shard_map.89.refs_0_.t1), channel_id=1, source_target_pairs={{1,2},{3,4},{5,6},{7,8},{9,10},{11,12},{13,14},{15,16},{17,18},{19... | collective-permute-start | bytes 36872 | tf_op jit(solution)/shard_map/ppermute | solution.py:305
  29.9 1.2 %collective-permute-start.8 = (f32[24,128]{1,0:T(8,128)S(1)}, f32[24,128]{1,0:T(8,128)S(1)}, u32[]{:S(2)}, u32[]{:S(2)}) collective-permute-start(f32[24,128]{1,0:T(8,128)S(1)} %shard_map.89.refs_0_.t1), channel_id=1, source_target_pairs={{0,1},{2,3},{4,5},{6,7},{8,9},{10,11},{12,13},{14,15},{16,17},{18,... | collective-permute-start | bytes 36872 | tf_op jit(solution)/shard_map/ppermute | solution.py:302
  31.6 8.9 %collective-permute-start.15 = (f32[24,128]{1,0:T(8,128)S(1)}, f32[24,128]{1,0:T(8,128)S(1)}, u32[]{:S(2)}, u32[]{:S(2)}) collective-permute-start(f32[24,128]{1,0:T(8,128)S(1)} %shard_map.90.t2.own), channel_id=1, source_target_pairs={{8,16},{9,17},{10,18},{11,19},{12,20},{13,21},{14,22},{15,23},{16,... | collective-permute-start | bytes 36872 | tf_op jit(solution)/shard_map/ppermute | solution.py:303
  32.3 8.6 %collective-permute-start.14 = (f32[24,128]{1,0:T(8,128)S(1)}, f32[24,128]{1,0:T(8,128)S(1)}, u32[]{:S(2)}, u32[]{:S(2)}) collective-permute-start(f32[24,128]{1,0:T(8,128)S(1)} %shard_map.90.t2.own), channel_id=1, source_target_pairs={{0,8},{1,9},{2,10},{3,11},{4,12},{5,13},{6,14},{7,15},{16,24},{17,... | collective-permute-start | bytes 36872 | tf_op jit(solution)/shard_map/ppermute | solution.py:304
  39.3 1.7 %collective-permute-start.13 = (f32[24,128]{1,0:T(8,128)S(1)}, f32[24,128]{1,0:T(8,128)S(1)}, u32[]{:S(2)}, u32[]{:S(2)}) collective-permute-start(f32[24,128]{1,0:T(8,128)S(1)} %shard_map.90.t2.own), channel_id=1, source_target_pairs={{1,2},{3,4},{5,6},{7,8},{9,10},{11,12},{13,14},{15,16},{17,18},{19... | collective-permute-start | bytes 36872 | tf_op jit(solution)/shard_map/ppermute | solution.py:305
  39.9 1.2 %collective-permute-start.12 = (f32[24,128]{1,0:T(8,128)S(1)}, f32[24,128]{1,0:T(8,128)S(1)}, u32[]{:S(2)}, u32[]{:S(2)}) collective-permute-start(f32[24,128]{1,0:T(8,128)S(1)} %shard_map.90.t2.own), channel_id=1, source_target_pairs={{0,1},{2,3},{4,5},{6,7},{8,9},{10,11},{12,13},{14,15},{16,17},{18,... | collective-permute-start | bytes 36872 | tf_op jit(solution)/shard_map/ppermute | solution.py:302
  42.0 1.7 %collective-permute-start.16 = (f32[40,128]{1,0:T(8,128)S(1)}, f32[40,128]{1,0:T(8,128)S(1)}, u32[]{:S(2)}, u32[]{:S(2)}) collective-permute-start(f32[40,128]{1,0:T(8,128)S(1)} %get-tuple-element.20), channel_id=1, source_target_pairs={{0,1},{1,0},{2,3},{3,2},{4,5},{5,4},{6,7},{7,6},{8,9},{9,8},{10,11... | collective-permute-start | bytes 61448 | tf_op jit(solution)/shard_map/ppermute | solution.py:311
  43.7 0.7 collective-permute-start.17
  44.4 0.7 collective-permute-start.18
  45.1 0.7 collective-permute-start.19
  45.8 0.7 collective-permute-start.20
  46.5 20.0 %collective-permute-start.21 = (f32[40,128]{1,0:T(8,128)S(1)}, f32[40,128]{1,0:T(8,128)S(1)}, u32[]{:S(2)}, u32[]{:S(2)}) collective-permute-start(f32[40,128]{1,0:T(8,128)S(1)} %add.19.refs_0_), channel_id=1, source_target_pairs={{0,1},{1,0},{2,3},{3,2},{4,5},{5,4},{6,7},{7,6},{8,9},{9,8},{10,11... | collective-permute-start | bytes 61448 | tf_op jit(solution)/shard_map/ppermute | solution.py:316

commit v4 on v3

--- a/solution.py
+++ b/solution.py
@@ -105,18 +105,20 @@
         low_ref[:, p * depth : (p + 1) * depth] = (turned - high.astype(jnp.float32)).astype(jnp.bfloat16)
 
 
-def selection(table, metas, place):
+def selection(table, metas, place, length):
     even, even_far = lax.rem(place, 2) == 0, lax.rem(place // FAR, 2) == 0
+    near, far_odd, far_even, across = metas
     slots = [
-        (jnp.where(even, 48.0, 24.0), metas[1], metas[0], even),
-        (jnp.where(even, 24.0, 48.0), metas[0], metas[1], even),
-        (jnp.where(even_far, 96.0, 72.0), metas[3], metas[2], even_far),
-        (jnp.where(even_far, 72.0, 96.0), metas[2], metas[3], even_far),
+        (place >= 1, jnp.where(even, 96.0, 24.0), jnp.where(even, across, near)),
+        (place < length - 1, jnp.where(even, 24.0, 96.0), jnp.where(even, near, across)),
+        (place >= FAR, jnp.where(even_far, 48.0, 72.0), jnp.where(even_far, far_odd, far_even)),
+        (place < length - FAR, jnp.where(even_far, 72.0, 48.0), jnp.where(even_far, far_even, far_odd)),
     ]
     lane = iota((1, 128), 1)
     target = lane.astype(jnp.float32)
-    for link, (base, when, other, test) in enumerate(slots):
-        target = jnp.where(lane // 8 == link + 1, jnp.where(test, when, other) + base, target)
+    for link, (valid, base, order) in enumerate(slots):
+        order = order + jnp.where(valid, base, DEAD)
+        target = jnp.where(lane // 8 == link + 1, order, target)
     target = jnp.broadcast_to(target, (8, 128))
     lane = iota((8, 128), 1).astype(jnp.float32)
     at = [
@@ -162,12 +164,12 @@
     return image - jnp.concatenate([shift] * COMPS, axis=0) * pieces[0]
 
 
-def first_kernel(own, a, b, c, d, aux, high, low, tile_ref, choose_ref):
+def first_kernel(length, own, a, b, c, d, aux, high, low, tile_ref, choose_ref):
     rows = 8 * COMPS
     refs = (own, a, b, c, d)
     pieces = [ref[:rows, :] for ref in refs]
     metas = [ref[rows : rows + 1, :] for ref in refs[1:]]
-    choose = selection(aux[8 * S :, :], metas, lax.axis_index("dom"))
+    choose = selection(aux[8 * S :, :], metas, lax.axis_index("dom"), length)
     choose_ref[...] = choose
     tile_ref[...] = multiply(choose, pieces, aux[:8, :], high[...], low[...])
 
@@ -292,28 +294,31 @@
     )
 
 
-def pairs_of(length, step, odd):
-    firsts = [d for d in range(length - step) if (d // step) % 2 == odd]
-    return [(d, d + step) for d in firsts] + [(d + step, d) for d in firsts]
+def swap(value, partner):
+    return lax.ppermute(value, "dom", [(d, partner(d)) for d in range(lax.axis_size("dom"))])
+
+
+def linked(step, odd):
+    length = lax.axis_size("dom")
+
+    def partner(d):
+        other = d + step if (d // step) % 2 == odd else d - step
+        return other if 0 <= other < length else d
+
+    return partner
 
 
 def ghosts(tile):
-    length = lax.axis_size("dom")
-    near = lax.ppermute(tile, "dom", pairs_of(length, 1, 0))
-    far_odd = lax.ppermute(tile, "dom", pairs_of(length, FAR, 1))
-    far_even = lax.ppermute(tile, "dom", pairs_of(length, FAR, 0))
-    across = lax.ppermute(tile, "dom", pairs_of(length, 1, 1))
-    return near, across, far_even, far_odd
+    return [swap(tile, linked(step, odd)) for step, odd in ((1, 0), (FAR, 1), (FAR, 0), (1, 1))]
 
 
 def summed(value):
-    length = lax.axis_size("dom")
-    value = value + lax.ppermute(value, "dom", [(d, d ^ 1) for d in range(length)])
+    value = value + swap(value, lambda d: d ^ 1)
     step = 2
-    while step < length:
-        value = value + lax.ppermute(value, "dom", [(d, d ^ step) for d in range(1, length, 2)])
+    while step < lax.axis_size("dom"):
+        value = value + swap(value, lambda d: d ^ step if d % 2 else d)
         step *= 2
-    return value, lax.ppermute(value, "dom", [(d, d ^ 1) for d in range(length)])
+    return value, swap(value, lambda d: d ^ 1)
 
 
 def local(strips, columns, send_list, send_count, shifts, prev_basis, mix):
@@ -350,8 +355,13 @@
         ],
     )(*in_hbm(strips, columns.T, shifts))
     tiles = []
+    length = lax.axis_size("dom")
     tile, choose = call(
-        first_kernel, [tile_out, ((2 * comps * blocks, 256), f32)], [VMEM] * 8, 50000000, 600000
+        lambda *refs: first_kernel(length, *refs),
+        [tile_out, ((2 * comps * blocks, 256), f32)],
+        [VMEM] * 8,
+        50000000,
+        600000,
     )(tile, *ghosts(tile), aux, high, low)
     tiles.append(tile)
     for step in (1, 2):
@@ -367,7 +377,7 @@
     last, gram = call(
         last_kernel, [((8, rows), f32), gram_out], [VMEM] * 12, 80000000, 900000
     )(tile, *received, choose, aux, high, low, lines, prev_basis, early)
-    total = float(lax.axis_size("dom") * rows)
+    total = float(length * rows)
     basis, factors = call(
         lambda *refs: finish_kernel(total, *refs),
         [((comps, S, rows), f32), ((comps, S, vecs + S), f32)],

time: 68 us -> 65.5 us (0.963)
  starting transfers between devices: 55.8 us -> 53.4 us
    ppermute x22, starting transfers between devices: 55.8 us -> 53.4 us  [swap(): lax.ppermute(value, 'dom', [(d, partner(d)) for d in range(lax.axis_size(...]
  transfers between devices with their start and end apart: 22 -> 22, of which waited for: 7 -> 8; matrix products, arithmetic and copies ran while one was open for 0% -> 0% of each run, Pallas kernels for 3% -> 3%
where the time goes in v4:
time: 65.5 us; the launch traced here: 65.1 us
  starting transfers between devices  53.4 us (82%)
  Pallas kernels  6.45 us (10%)
  waiting for transfers between devices  4.33 us (7%)
  between operations  0.89 us (1%)
    ppermute x22, starting transfers between devices, swap(): lax.ppermute(value, 'dom', [(d, partner(d)) for d in range(lax.axis_size(...  53.4 us
    ppermute x22, waiting for transfers between devices, swap(): lax.ppermute(value, 'dom', [(d, partner(d)) for d in range(lax.axis_size(...  4.33 us
    pallas_call x1, Pallas kernels, local(): call(prepare_kernel, [((width, rows), bf16), ((width, rows), bf16), ((8 *...  1.4 us
  transfers between devices with their start and end apart: 22, of which 8 were waited for; matrix products, arithmetic and copies ran while one was open for 0% of the time, Pallas kernels for 3%

profile of v4, /device:TPU:0, one launch (start us, length us, event | category | flops | bytes accessed | tf_op | source)
XLA Modules:
  0.0 65.1 jit_solution(13704600370682649311)
XLA Ops:
  0.6 1.3 %shard_map.86.refs_0_ = f32[32,128]{1,0:T(8,128)S(1)} custom-call(f32[3,32,512]{2,1,0:T(8,128)} %refs_2_.1, f32[3,32]{1,0:T(4,128)} %mix_in.1, s32[1,4,8]{2,1,0:T(4,128)} %list_in.1, s32[1,4]{1,0:T(1,128)} %count_in.1), custom_call_target="tpu_custom_call" | custom-call | flops 600000 | bytes 250000 | tf_op jit(solution)/shard_map/pallas_call | solution.py:330
  1.9 0.7 %collective-permute-start.3 = (f32[32,128]{1,0:T(8,128)S(1)}, f32[32,128]{1,0:T(8,128)S(1)}, u32[]{:S(2)}, u32[]{:S(2)}) collective-permute-start(f32[32,128]{1,0:T(8,128)S(1)} %shard_map.86.refs_0_), channel_id=1, source_target_pairs={{0,0},{1,2},{2,1},{3,4},{4,3},{5,6},{6,5},{7,8},{8,7},{9,10},{10,9... | collective-permute-start | bytes 49160 | tf_op jit(solution)/shard_map/ppermute | solution.py:298
  2.6 6.1 %collective-permute-start.2 = (f32[32,128]{1,0:T(8,128)S(1)}, f32[32,128]{1,0:T(8,128)S(1)}, u32[]{:S(2)}, u32[]{:S(2)}) collective-permute-start(f32[32,128]{1,0:T(8,128)S(1)} %shard_map.86.refs_0_), channel_id=1, source_target_pairs={{0,8},{1,9},{2,10},{3,11},{4,12},{5,13},{6,14},{7,15},{8,0},{9,1},... | collective-permute-start | bytes 49160 | tf_op jit(solution)/shard_map/ppermute | solution.py:298
  8.7 0.7 collective-permute-start.1
  9.3 0.1 collective-permute-start
  9.4 1.4 %shard_map.87 = (bf16[256,512]{1,0:T(8,128)(2,1)S(1)}, bf16[256,512]{1,0:T(8,128)(2,1)S(1)}, f32[40,128]{1,0:T(8,128)S(1)}) custom-call(f32[512,256]{1,0:T(8,128)} %strips_in.1, s32[4,8]{1,0:T(4,128)} %bitcast.2, f32[4]{0:T(128)} %shifts_in.1), custom_call_target="tpu_custom_call" | custom-call | flops 1000000 | bytes 1000000 | tf_op jit(solution)/shard_map/pallas_call | solution.py:344
  10.8 0.0 collective-permute-done.3.refs_4_
  10.8 0.0 collective-permute-done.2.refs_3_
  10.8 0.0 collective-permute-done.1.refs_2_
  10.9 0.0 collective-permute-done.refs_1_
  10.9 0.6 shard_map.88
  11.4 0.7 %collective-permute-start.7 = (f32[24,128]{1,0:T(8,128)S(1)}, f32[24,128]{1,0:T(8,128)S(1)}, u32[]{:S(2)}, u32[]{:S(2)}) collective-permute-start(f32[24,128]{1,0:T(8,128)S(1)} %get-tuple-element.16.refs_0_.t0), channel_id=1, source_target_pairs={{0,0},{1,2},{2,1},{3,4},{4,3},{5,6},{6,5},{7,8},{8,7},{9,10},{10,9... | collective-permute-start | bytes 36872 | tf_op jit(solution)/shard_map/ppermute | solution.py:298
  12.1 5.9 %collective-permute-start.6 = (f32[24,128]{1,0:T(8,128)S(1)}, f32[24,128]{1,0:T(8,128)S(1)}, u32[]{:S(2)}, u32[]{:S(2)}) collective-permute-start(f32[24,128]{1,0:T(8,128)S(1)} %get-tuple-element.16.refs_0_.t0), channel_id=1, source_target_pairs={{0,8},{1,9},{2,10},{3,11},{4,12},{5,13},{6,14},{7,15},{8,0},{9,1},... | collective-permute-start | bytes 36872 | tf_op jit(solution)/shard_map/ppermute | solution.py:298
  18.0 0.7 collective-permute-start.5
  18.6 0.5 collective-permute-start.4
  19.1 0.0 collective-permute-done.7.refs_4_
  19.1 0.7 %collective-permute-done.6.refs_3_ = f32[24,128]{1,0:T(8,128)S(1)} collective-permute-done((f32[24,128]{1,0:T(8,128)S(1)}, f32[24,128]{1,0:T(8,128)S(1)}, u32[]{:S(2)}, u32[]{:S(2)}) %collective-permute-start.6) | collective-permute-done | bytes 12320 | tf_op jit(solution)/shard_map/ppermute | solution.py:298
  19.8 0.0 collective-permute-done.5.refs_2_
  19.8 0.1 collective-permute-done.4.refs_1_
  19.9 0.4 shard_map.89.refs_0_.t1
  20.4 0.0 copy-start
  20.4 0.8 %collective-permute-start.11 = (f32[24,128]{1,0:T(8,128)S(1)}, f32[24,128]{1,0:T(8,128)S(1)}, u32[]{:S(2)}, u32[]{:S(2)}) collective-permute-start(f32[24,128]{1,0:T(8,128)S(1)} %shard_map.89.refs_0_.t1), channel_id=1, source_target_pairs={{0,0},{1,2},{2,1},{3,4},{4,3},{5,6},{6,5},{7,8},{8,7},{9,10},{10,9... | collective-permute-start | bytes 36872 | tf_op jit(solution)/shard_map/ppermute | solution.py:298
  21.2 6.5 %collective-permute-start.10 = (f32[24,128]{1,0:T(8,128)S(1)}, f32[24,128]{1,0:T(8,128)S(1)}, u32[]{:S(2)}, u32[]{:S(2)}) collective-permute-start(f32[24,128]{1,0:T(8,128)S(1)} %shard_map.89.refs_0_.t1), channel_id=1, source_target_pairs={{0,8},{1,9},{2,10},{3,11},{4,12},{5,13},{6,14},{7,15},{8,0},{9,1},... | collective-permute-start | bytes 36872 | tf_op jit(solution)/shard_map/ppermute | solution.py:298
  27.7 0.7 collective-permute-start.9
  28.4 0.3 collective-permute-start.8
  28.6 0.0 collective-permute-done.11.refs_4_
  28.6 0.8 %collective-permute-done.10.refs_3_ = f32[24,128]{1,0:T(8,128)S(1)} collective-permute-done((f32[24,128]{1,0:T(8,128)S(1)}, f32[24,128]{1,0:T(8,128)S(1)}, u32[]{:S(2)}, u32[]{:S(2)}) %collective-permute-start.10) | collective-permute-done | bytes 12320 | tf_op jit(solution)/shard_map/ppermute | solution.py:298
  29.4 0.0 collective-permute-done.9.refs_2_
  29.4 0.2 collective-permute-done.8.refs_1_
  29.6 0.4 shard_map.90.t2.own
  30.0 0.7 %collective-permute-start.15 = (f32[24,128]{1,0:T(8,128)S(1)}, f32[24,128]{1,0:T(8,128)S(1)}, u32[]{:S(2)}, u32[]{:S(2)}) collective-permute-start(f32[24,128]{1,0:T(8,128)S(1)} %shard_map.90.t2.own), channel_id=1, source_target_pairs={{0,0},{1,2},{2,1},{3,4},{4,3},{5,6},{6,5},{7,8},{8,7},{9,10},{10,9... | collective-permute-start | bytes 36872 | tf_op jit(solution)/shard_map/ppermute | solution.py:298
  30.7 6.3 %collective-permute-start.14 = (f32[24,128]{1,0:T(8,128)S(1)}, f32[24,128]{1,0:T(8,128)S(1)}, u32[]{:S(2)}, u32[]{:S(2)}) collective-permute-start(f32[24,128]{1,0:T(8,128)S(1)} %shard_map.90.t2.own), channel_id=1, source_target_pairs={{0,8},{1,9},{2,10},{3,11},{4,12},{5,13},{6,14},{7,15},{8,0},{9,1},... | collective-permute-start | bytes 36872 | tf_op jit(solution)/shard_map/ppermute | solution.py:298
  37.0 0.7 collective-permute-start.13
  37.6 0.1 collective-permute-start.12
  37.7 0.0 copy-done
  37.7 0.5 shard_map.91
  38.2 0.0 collective-permute-done.15.d
  38.2 0.5 collective-permute-done.14.c
  38.7 0.0 collective-permute-done.13.b
  38.7 0.2 collective-permute-done.12.a
  38.9 0.8 %shard_map.92 = (f32[8,512]{1,0:T(8,128)S(1)}, f32[40,128]{1,0:T(8,128)S(1)}) custom-call(f32[24,128]{1,0:T(8,128)S(1)} %shard_map.90.t2.own, f32[24,128]{1,0:T(8,128)S(1)} %collective-permute-done.12.a, f32[24,128]{1,0:T(8,128)S(1)} %collective-permute-done.13.b, f32[24,128]{1,0:T(8,128)S(1)} %collective-permute-done.14.c, ...), custom_call_target="tpu_custom_call" | custom-call | flops 80000000 | bytes 900000 | tf_op jit(solution)/shard_map/pallas_call | solution.py:377
  39.7 0.2 collective-permute-start.16
  39.9 1.0 %collective-permute-done.16 = f32[40,128]{1,0:T(8,128)S(1)} collective-permute-done((f32[40,128]{1,0:T(8,128)S(1)}, f32[40,128]{1,0:T(8,128)S(1)}, u32[]{:S(2)}, u32[]{:S(2)}) %collective-permute-start.16) | collective-permute-done | bytes 20512 | tf_op jit(solution)/shard_map/ppermute | solution.py:298
  40.9 0.7 %collective-permute-start.17 = (f32[40,128]{1,0:T(8,128)S(1)}, f32[40,128]{1,0:T(8,128)S(1)}, u32[]{:S(2)}, u32[]{:S(2)}) collective-permute-start(f32[40,128]{1,0:T(8,128)S(1)} %add.15), channel_id=1, source_target_pairs={{0,0},{1,3},{2,2},{3,1},{4,4},{5,7},{6,6},{7,5},{8,8},{9,11},{10,1... | collective-permute-start | bytes 61448 | tf_op jit(solution)/shard_map/ppermute | solution.py:298
  41.6 0.0 collective-permute-done.17
  41.6 0.7 %collective-permute-start.18 = (f32[40,128]{1,0:T(8,128)S(1)}, f32[40,128]{1,0:T(8,128)S(1)}, u32[]{:S(2)}, u32[]{:S(2)}) collective-permute-start(f32[40,128]{1,0:T(8,128)S(1)} %add.16), channel_id=1, source_target_pairs={{0,0},{1,5},{2,2},{3,7},{4,4},{5,1},{6,6},{7,3},{8,8},{9,13},{10,1... | collective-permute-start | bytes 61448 | tf_op jit(solution)/shard_map/ppermute | solution.py:298
  42.3 0.0 collective-permute-done.18
  42.3 0.7 %collective-permute-start.19 = (f32[40,128]{1,0:T(8,128)S(1)}, f32[40,128]{1,0:T(8,128)S(1)}, u32[]{:S(2)}, u32[]{:S(2)}) collective-permute-start(f32[40,128]{1,0:T(8,128)S(1)} %add.17), channel_id=1, source_target_pairs={{0,0},{1,9},{2,2},{3,11},{4,4},{5,13},{6,6},{7,15},{8,8},{9,1},{10... | collective-permute-start | bytes 61448 | tf_op jit(solution)/shard_map/ppermute | solution.py:298
  43.0 0.0 collective-permute-done.19
  43.0 0.7 %collective-permute-start.20 = (f32[40,128]{1,0:T(8,128)S(1)}, f32[40,128]{1,0:T(8,128)S(1)}, u32[]{:S(2)}, u32[]{:S(2)}) collective-permute-start(f32[40,128]{1,0:T(8,128)S(1)} %add.18), channel_id=1, source_target_pairs={{0,0},{1,17},{2,2},{3,19},{4,4},{5,21},{6,6},{7,23},{8,8},{9,25},{... | collective-permute-start | bytes 61448 | tf_op jit(solution)/shard_map/ppermute | solution.py:298
  43.7 0.0 collective-permute-done.20
  43.7 19.5 %collective-permute-start.21 = (f32[40,128]{1,0:T(8,128)S(1)}, f32[40,128]{1,0:T(8,128)S(1)}, u32[]{:S(2)}, u32[]{:S(2)}) collective-permute-start(f32[40,128]{1,0:T(8,128)S(1)} %add.19.refs_0_), channel_id=1, source_target_pairs={{0,1},{1,0},{2,3},{3,2},{4,5},{5,4},{6,7},{7,6},{8,9},{9,8},{10,11... | collective-permute-start | bytes 61448 | tf_op jit(solution)/shard_map/ppermute | solution.py:298
  63.2 0.8 %collective-permute-done.21.refs_1_ = f32[40,128]{1,0:T(8,128)S(1)} collective-permute-done((f32[40,128]{1,0:T(8,128)S(1)}, f32[40,128]{1,0:T(8,128)S(1)}, u32[]{:S(2)}, u32[]{:S(2)}) %collective-permute-start.21) | collective-permute-done | bytes 20512 | tf_op jit(solution)/shard_map/ppermute | solution.py:298
  64.0 1.1 %shard_map.93 = (f32[3,4,512]{2,1,0:T(4,128)}, f32[3,4,36]{2,1,0:T(4,128)}) custom-call(f32[40,128]{1,0:T(8,128)S(1)} %add.19.refs_0_, f32[40,128]{1,0:T(8,128)S(1)} %collective-permute-done.21.refs_1_, f32[3,32,512]{2,1,0:T(8,128)S(1)} %copy-done, f32[24,512]{1,0:T(8,128)S(1)} %get-tuple-element.18.lines.refs_3_, f32[8,512]{1,0:T(8,128)S(1)} %get-tuple-element.21.refs_4_), custom_call_target="tpu_custom_call" | custom-call | flops 50000000 | bytes 400000 | tf_op jit(solution)/shard_map/pallas_call | solution.py:381
  (5 shorter events, 0.0 us)
Async XLA Ops:
  1.9 8.9 %collective-permute-start.3 = (f32[32,128]{1,0:T(8,128)S(1)}, f32[32,128]{1,0:T(8,128)S(1)}, u32[]{:S(2)}, u32[]{:S(2)}) collective-permute-start(f32[32,128]{1,0:T(8,128)S(1)} %shard_map.86.refs_0_), channel_id=1, source_target_pairs={{0,0},{1,2},{2,1},{3,4},{4,3},{5,6},{6,5},{7,8},{8,7},{9,10},{10,9... | collective-permute-start | bytes 49160 | tf_op jit(solution)/shard_map/ppermute | solution.py:298
  2.6 8.3 %collective-permute-start.2 = (f32[32,128]{1,0:T(8,128)S(1)}, f32[32,128]{1,0:T(8,128)S(1)}, u32[]{:S(2)}, u32[]{:S(2)}) collective-permute-start(f32[32,128]{1,0:T(8,128)S(1)} %shard_map.86.refs_0_), channel_id=1, source_target_pairs={{0,8},{1,9},{2,10},{3,11},{4,12},{5,13},{6,14},{7,15},{8,0},{9,1},... | collective-permute-start | bytes 49160 | tf_op jit(solution)/shard_map/ppermute | solution.py:298
  8.7 2.2 %collective-permute-start.1 = (f32[32,128]{1,0:T(8,128)S(1)}, f32[32,128]{1,0:T(8,128)S(1)}, u32[]{:S(2)}, u32[]{:S(2)}) collective-permute-start(f32[32,128]{1,0:T(8,128)S(1)} %shard_map.86.refs_0_), channel_id=1, source_target_pairs={{0,0},{1,1},{2,2},{3,3},{4,4},{5,5},{6,6},{7,7},{8,16},{9,17},{10,... | collective-permute-start | bytes 49160 | tf_op jit(solution)/shard_map/ppermute | solution.py:298
  9.3 1.5 %collective-permute-start = (f32[32,128]{1,0:T(8,128)S(1)}, f32[32,128]{1,0:T(8,128)S(1)}, u32[]{:S(2)}, u32[]{:S(2)}) collective-permute-start(f32[32,128]{1,0:T(8,128)S(1)} %shard_map.86.refs_0_), channel_id=1, source_target_pairs={{0,1},{1,0},{2,3},{3,2},{4,5},{5,4},{6,7},{7,6},{8,9},{9,8},{10,11... | collective-permute-start | bytes 49160 | tf_op jit(solution)/shard_map/ppermute | solution.py:298
  11.4 7.7 %collective-permute-start.7 = (f32[24,128]{1,0:T(8,128)S(1)}, f32[24,128]{1,0:T(8,128)S(1)}, u32[]{:S(2)}, u32[]{:S(2)}) collective-permute-start(f32[24,128]{1,0:T(8,128)S(1)} %get-tuple-element.16.refs_0_.t0), channel_id=1, source_target_pairs={{0,0},{1,2},{2,1},{3,4},{4,3},{5,6},{6,5},{7,8},{8,7},{9,10},{10,9... | collective-permute-start | bytes 36872 | tf_op jit(solution)/shard_map/ppermute | solution.py:298
  12.1 7.7 %collective-permute-start.6 = (f32[24,128]{1,0:T(8,128)S(1)}, f32[24,128]{1,0:T(8,128)S(1)}, u32[]{:S(2)}, u32[]{:S(2)}) collective-permute-start(f32[24,128]{1,0:T(8,128)S(1)} %get-tuple-element.16.refs_0_.t0), channel_id=1, source_target_pairs={{0,8},{1,9},{2,10},{3,11},{4,12},{5,13},{6,14},{7,15},{8,0},{9,1},... | collective-permute-start | bytes 36872 | tf_op jit(solution)/shard_map/ppermute | solution.py:298
  18.0 1.8 %collective-permute-start.5 = (f32[24,128]{1,0:T(8,128)S(1)}, f32[24,128]{1,0:T(8,128)S(1)}, u32[]{:S(2)}, u32[]{:S(2)}) collective-permute-start(f32[24,128]{1,0:T(8,128)S(1)} %get-tuple-element.16.refs_0_.t0), channel_id=1, source_target_pairs={{0,0},{1,1},{2,2},{3,3},{4,4},{5,5},{6,6},{7,7},{8,16},{9,17},{10,... | collective-permute-start | bytes 36872 | tf_op jit(solution)/shard_map/ppermute | solution.py:298
  18.6 1.3 %collective-permute-start.4 = (f32[24,128]{1,0:T(8,128)S(1)}, f32[24,128]{1,0:T(8,128)S(1)}, u32[]{:S(2)}, u32[]{:S(2)}) collective-permute-start(f32[24,128]{1,0:T(8,128)S(1)} %get-tuple-element.16.refs_0_.t0), channel_id=1, source_target_pairs={{0,1},{1,0},{2,3},{3,2},{4,5},{5,4},{6,7},{7,6},{8,9},{9,8},{10,11... | collective-permute-start | bytes 36872 | tf_op jit(solution)/shard_map/ppermute | solution.py:298
  20.4 17.4 %copy-start = (f32[3,32,512]{2,1,0:T(8,128)S(1)}, f32[3,32,512]{2,1,0:T(8,128)}, u32[]{:S(2)}) copy-start(f32[3,32,512]{2,1,0:T(8,128)} %refs_2_.1) | copy-start | bytes 589828
  20.4 8.3 %collective-permute-start.11 = (f32[24,128]{1,0:T(8,128)S(1)}, f32[24,128]{1,0:T(8,128)S(1)}, u32[]{:S(2)}, u32[]{:S(2)}) collective-permute-start(f32[24,128]{1,0:T(8,128)S(1)} %shard_map.89.refs_0_.t1), channel_id=1, source_target_pairs={{0,0},{1,2},{2,1},{3,4},{4,3},{5,6},{6,5},{7,8},{8,7},{9,10},{10,9... | collective-permute-start | bytes 36872 | tf_op jit(solution)/shard_map/ppermute | solution.py:298
  21.2 8.3 %collective-permute-start.10 = (f32[24,128]{1,0:T(8,128)S(1)}, f32[24,128]{1,0:T(8,128)S(1)}, u32[]{:S(2)}, u32[]{:S(2)}) collective-permute-start(f32[24,128]{1,0:T(8,128)S(1)} %shard_map.89.refs_0_.t1), channel_id=1, source_target_pairs={{0,8},{1,9},{2,10},{3,11},{4,12},{5,13},{6,14},{7,15},{8,0},{9,1},... | collective-permute-start | bytes 36872 | tf_op jit(solution)/shard_map/ppermute | solution.py:298
  27.7 1.7 %collective-permute-start.9 = (f32[24,128]{1,0:T(8,128)S(1)}, f32[24,128]{1,0:T(8,128)S(1)}, u32[]{:S(2)}, u32[]{:S(2)}) collective-permute-start(f32[24,128]{1,0:T(8,128)S(1)} %shard_map.89.refs_0_.t1), channel_id=1, source_target_pairs={{0,0},{1,1},{2,2},{3,3},{4,4},{5,5},{6,6},{7,7},{8,16},{9,17},{10,... | collective-permute-start | bytes 36872 | tf_op jit(solution)/shard_map/ppermute | solution.py:298
  28.4 1.2 %collective-permute-start.8 = (f32[24,128]{1,0:T(8,128)S(1)}, f32[24,128]{1,0:T(8,128)S(1)}, u32[]{:S(2)}, u32[]{:S(2)}) collective-permute-start(f32[24,128]{1,0:T(8,128)S(1)} %shard_map.89.refs_0_.t1), channel_id=1, source_target_pairs={{0,1},{1,0},{2,3},{3,2},{4,5},{5,4},{6,7},{7,6},{8,9},{9,8},{10,11... | collective-permute-start | bytes 36872 | tf_op jit(solution)/shard_map/ppermute | solution.py:298
  30.0 8.2 %collective-permute-start.15 = (f32[24,128]{1,0:T(8,128)S(1)}, f32[24,128]{1,0:T(8,128)S(1)}, u32[]{:S(2)}, u32[]{:S(2)}) collective-permute-start(f32[24,128]{1,0:T(8,128)S(1)} %shard_map.90.t2.own), channel_id=1, source_target_pairs={{0,0},{1,2},{2,1},{3,4},{4,3},{5,6},{6,5},{7,8},{8,7},{9,10},{10,9... | collective-permute-start | bytes 36872 | tf_op jit(solution)/shard_map/ppermute | solution.py:298
  30.7 8.0 %collective-permute-start.14 = (f32[24,128]{1,0:T(8,128)S(1)}, f32[24,128]{1,0:T(8,128)S(1)}, u32[]{:S(2)}, u32[]{:S(2)}) collective-permute-start(f32[24,128]{1,0:T(8,128)S(1)} %shard_map.90.t2.own), channel_id=1, source_target_pairs={{0,8},{1,9},{2,10},{3,11},{4,12},{5,13},{6,14},{7,15},{8,0},{9,1},... | collective-permute-start | bytes 36872 | tf_op jit(solution)/shard_map/ppermute | solution.py:298
  37.0 1.7 %collective-permute-start.13 = (f32[24,128]{1,0:T(8,128)S(1)}, f32[24,128]{1,0:T(8,128)S(1)}, u32[]{:S(2)}, u32[]{:S(2)}) collective-permute-start(f32[24,128]{1,0:T(8,128)S(1)} %shard_map.90.t2.own), channel_id=1, source_target_pairs={{0,0},{1,1},{2,2},{3,3},{4,4},{5,5},{6,6},{7,7},{8,16},{9,17},{10,... | collective-permute-start | bytes 36872 | tf_op jit(solution)/shard_map/ppermute | solution.py:298
  37.6 1.2 %collective-permute-start.12 = (f32[24,128]{1,0:T(8,128)S(1)}, f32[24,128]{1,0:T(8,128)S(1)}, u32[]{:S(2)}, u32[]{:S(2)}) collective-permute-start(f32[24,128]{1,0:T(8,128)S(1)} %shard_map.90.t2.own), channel_id=1, source_target_pairs={{0,1},{1,0},{2,3},{3,2},{4,5},{5,4},{6,7},{7,6},{8,9},{9,8},{10,11... | collective-permute-start | bytes 36872 | tf_op jit(solution)/shard_map/ppermute | solution.py:298
  39.7 1.2 %collective-permute-start.16 = (f32[40,128]{1,0:T(8,128)S(1)}, f32[40,128]{1,0:T(8,128)S(1)}, u32[]{:S(2)}, u32[]{:S(2)}) collective-permute-start(f32[40,128]{1,0:T(8,128)S(1)} %get-tuple-element.20), channel_id=1, source_target_pairs={{0,1},{1,0},{2,3},{3,2},{4,5},{5,4},{6,7},{7,6},{8,9},{9,8},{10,11... | collective-permute-start | bytes 61448 | tf_op jit(solution)/shard_map/ppermute | solution.py:298
  40.9 0.7 %collective-permute-start.17 = (f32[40,128]{1,0:T(8,128)S(1)}, f32[40,128]{1,0:T(8,128)S(1)}, u32[]{:S(2)}, u32[]{:S(2)}) collective-permute-start(f32[40,128]{1,0:T(8,128)S(1)} %add.15), channel_id=1, source_target_pairs={{0,0},{1,3},{2,2},{3,1},{4,4},{5,7},{6,6},{7,5},{8,8},{9,11},{10,1... | collective-permute-start | bytes 61448 | tf_op jit(solution)/shard_map/ppermute | solution.py:298
  41.6 0.7 %collective-permute-start.18 = (f32[40,128]{1,0:T(8,128)S(1)}, f32[40,128]{1,0:T(8,128)S(1)}, u32[]{:S(2)}, u32[]{:S(2)}) collective-permute-start(f32[40,128]{1,0:T(8,128)S(1)} %add.16), channel_id=1, source_target_pairs={{0,0},{1,5},{2,2},{3,7},{4,4},{5,1},{6,6},{7,3},{8,8},{9,13},{10,1... | collective-permute-start | bytes 61448 | tf_op jit(solution)/shard_map/ppermute | solution.py:298
  42.3 0.7 %collective-permute-start.19 = (f32[40,128]{1,0:T(8,128)S(1)}, f32[40,128]{1,0:T(8,128)S(1)}, u32[]{:S(2)}, u32[]{:S(2)}) collective-permute-start(f32[40,128]{1,0:T(8,128)S(1)} %add.17), channel_id=1, source_target_pairs={{0,0},{1,9},{2,2},{3,11},{4,4},{5,13},{6,6},{7,15},{8,8},{9,1},{10... | collective-permute-start | bytes 61448 | tf_op jit(solution)/shard_map/ppermute | solution.py:298
  43.0 0.7 %collective-permute-start.20 = (f32[40,128]{1,0:T(8,128)S(1)}, f32[40,128]{1,0:T(8,128)S(1)}, u32[]{:S(2)}, u32[]{:S(2)}) collective-permute-start(f32[40,128]{1,0:T(8,128)S(1)} %add.18), channel_id=1, source_target_pairs={{0,0},{1,17},{2,2},{3,19},{4,4},{5,21},{6,6},{7,23},{8,8},{9,25},{... | collective-permute-start | bytes 61448 | tf_op jit(solution)/shard_map/ppermute | solution.py:298
  43.7 20.4 %collective-permute-start.21 = (f32[40,128]{1,0:T(8,128)S(1)}, f32[40,128]{1,0:T(8,128)S(1)}, u32[]{:S(2)}, u32[]{:S(2)}) collective-permute-start(f32[40,128]{1,0:T(8,128)S(1)} %add.19.refs_0_), channel_id=1, source_target_pairs={{0,1},{1,0},{2,3},{3,2},{4,5},{5,4},{6,7},{7,6},{8,9},{9,8},{10,11... | collective-permute-start | bytes 61448 | tf_op jit(solution)/shard_map/ppermute | solution.py:298

commit v5 on v4

--- a/solution.py
+++ b/solution.py
@@ -108,9 +108,12 @@
 def selection(table, metas, place, length):
     even, even_far = lax.rem(place, 2) == 0, lax.rem(place // FAR, 2) == 0
     near, far_odd, far_even, across = metas
+    moved = (place == 1) | (place == length - 2)
+    across = jnp.where(moved, far_odd, across)
+    circle = jnp.where(moved, 48.0, 96.0)
     slots = [
-        (place >= 1, jnp.where(even, 96.0, 24.0), jnp.where(even, across, near)),
-        (place < length - 1, jnp.where(even, 24.0, 96.0), jnp.where(even, near, across)),
+        (place >= 1, jnp.where(even, circle, 24.0), jnp.where(even, across, near)),
+        (place < length - 1, jnp.where(even, 24.0, circle), jnp.where(even, near, across)),
         (place >= FAR, jnp.where(even_far, 48.0, 72.0), jnp.where(even_far, far_odd, far_even)),
         (place < length - FAR, jnp.where(even_far, 72.0, 48.0), jnp.where(even_far, far_even, far_odd)),
     ]
@@ -221,11 +224,10 @@
     )
 
 
-def finish_kernel(total, mine_ref, other_ref, prev_ref, lines, last, basis_ref, factors_ref):
+def finish_kernel(total, gram_in, prev_ref, lines, last, basis_ref, factors_ref):
     comps, vecs, rows = prev_ref.shape
     width = comps * vecs
-    odd = lax.rem(lax.axis_index("dom"), 2) == 1
-    gram = jnp.where(odd, mine_ref[...], other_ref[...]) * (1.0 / total)
+    gram = gram_in[...] * (1.0 / total)
     small = gram[vecs:]
     lane, comp = iota((8, 128), 1), iota((8, 128), 0)
     in_prev = (lane < width) & (lane // vecs == comp)
@@ -294,31 +296,38 @@
     )
 
 
-def swap(value, partner):
-    return lax.ppermute(value, "dom", [(d, partner(d)) for d in range(lax.axis_size("dom"))])
-
-
-def linked(step, odd):
+def send(value, target):
+    return lax.ppermute(value, "dom", [(d, target[d]) for d in range(lax.axis_size("dom"))])
+
+
+def neighbours(length, step, odd):
+    target = {}
+    for d in range(length):
+        other = d + step if (d // step) % 2 == odd else d - step
+        target[d] = other if 0 <= other < length else None
+    return target
+
+
+def ghosts(tile):
     length = lax.axis_size("dom")
-
-    def partner(d):
-        other = d + step if (d // step) % 2 == odd else d - step
-        return other if 0 <= other < length else d
-
-    return partner
-
-
-def ghosts(tile):
-    return [swap(tile, linked(step, odd)) for step, odd in ((1, 0), (FAR, 1), (FAR, 0), (1, 1))]
+    last = length - 1
+    near, across = neighbours(length, 1, 0), neighbours(length, 1, 1)
+    far_even, far_odd = neighbours(length, FAR, 0), neighbours(length, FAR, 1)
+    across.update({0: 1, 1: 2, 2: 0, last: last - 1, last - 1: last - 2, last - 2: last})
+    for d in range(length):
+        if far_odd[d] is None:
+            far_odd[d] = d ^ 1
+    far_odd.update({0: 3, 3: 0, 1: 2, 2: 1})
+    far_odd.update({last: last - 3, last - 3: last, last - 1: last - 2, last - 2: last - 1})
+    return [send(tile, target) for target in (near, far_odd, far_even, across)]
 
 
 def summed(value):
-    value = value + swap(value, lambda d: d ^ 1)
-    step = 2
+    step = 1
     while step < lax.axis_size("dom"):
-        value = value + swap(value, lambda d: d ^ step if d % 2 else d)
+        value = value + send(value, {d: d ^ (step | 1) for d in range(lax.axis_size("dom"))})
         step *= 2
-    return value, swap(value, lambda d: d ^ 1)
+    return value
 
 
 def local(strips, columns, send_list, send_count, shifts, prev_basis, mix):
@@ -381,10 +390,10 @@
     basis, factors = call(
         lambda *refs: finish_kernel(total, *refs),
         [((comps, S, rows), f32), ((comps, S, vecs + S), f32)],
-        [VMEM] * 5,
+        [VMEM] * 4,
         50000000,
         400000,
-    )(*summed(gram), prev_basis, lines, last)
+    )(summed(gram), prev_basis, lines, last)
     return basis, jnp.swapaxes(factors, 1, 2)
 
 

time: 65.5 us -> 44.8 us (0.68)
  starting transfers between devices: 53.4 us -> 20.5 us
  waiting for transfers between devices: 4.33 us -> 16.9 us
    ppermute x22 -> x21, starting transfers between devices: 53.4 us -> 20.5 us  [send(): lax.ppermute(value, 'dom', [(d, target[d]) for d in range(lax.axis_size('...]
    ppermute x22 -> x21, waiting for transfers between devices: 4.33 us -> 16.9 us  [send(): lax.ppermute(value, 'dom', [(d, target[d]) for d in range(lax.axis_size('...]
  transfers between devices with their start and end apart: 22 -> 21, of which waited for: 8 -> 13; matrix products, arithmetic and copies ran while one was open for 0% -> 0% of each run, Pallas kernels for 3% -> 4%
where the time goes in v5:
time: 44.8 us; the launch traced here: 44.6 us
  starting transfers between devices  20.5 us (46%)
  waiting for transfers between devices  16.9 us (38%)
  Pallas kernels  6.45 us (14%)
  between operations  0.71 us (2%)
    ppermute x21, starting transfers between devices, send(): lax.ppermute(value, 'dom', [(d, target[d]) for d in range(lax.axis_size('...  20.5 us
    ppermute x21, waiting for transfers between devices, send(): lax.ppermute(value, 'dom', [(d, target[d]) for d in range(lax.axis_size('...  16.9 us
    pallas_call x1, Pallas kernels, local(): call(prepare_kernel, [((width, rows), bf16), ((width, rows), bf16), ((8 *...  1.39 us
    pallas_call x1, Pallas kernels, local(): call(start_kernel, [((comps * blocks + 8, 128), f32)], [HBM] * 4, 600000,...  1.26 us
    pallas_call x1, Pallas kernels, local(): call(lambda *refs: finish_kernel(total, *refs), [((comps, S, rows), f32),...  1.06 us
  transfers between devices with their start and end apart: 21, of which 13 were waited for; matrix products, arithmetic and copies ran while one was open for 0% of the time, Pallas kernels for 4%

profile of v5, /device:TPU:0, one launch (start us, length us, event | category | flops | bytes accessed | tf_op | source)
XLA Modules:
  0.0 44.6 jit_solution(471580801611017840)
XLA Ops:
  0.6 1.3 %shard_map.86.refs_0_ = f32[32,128]{1,0:T(8,128)S(1)} custom-call(f32[3,32,512]{2,1,0:T(8,128)} %refs_1_.1, f32[3,32]{1,0:T(4,128)} %mix_in.1, s32[1,4,8]{2,1,0:T(4,128)} %list_in.1, s32[1,4]{1,0:T(1,128)} %count_in.1), custom_call_target="tpu_custom_call" | custom-call | flops 600000 | bytes 250000 | tf_op jit(solution)/shard_map/pallas_call | solution.py:339
  1.9 0.5 %collective-permute-start.3 = (f32[32,128]{1,0:T(8,128)S(1)}, f32[32,128]{1,0:T(8,128)S(1)}, u32[]{:S(2)}, u32[]{:S(2)}) collective-permute-start(f32[32,128]{1,0:T(8,128)S(1)} %shard_map.86.refs_0_), channel_id=1, source_target_pairs={{0,1},{1,2},{2,0},{3,4},{4,3},{5,6},{6,5},{7,8},{8,7},{9,10},{10,9... | collective-permute-start | bytes 49160 | tf_op jit(solution)/shard_map/ppermute | solution.py:300
  2.4 4.3 %collective-permute-start.2 = (f32[32,128]{1,0:T(8,128)S(1)}, f32[32,128]{1,0:T(8,128)S(1)}, u32[]{:S(2)}, u32[]{:S(2)}) collective-permute-start(f32[32,128]{1,0:T(8,128)S(1)} %shard_map.86.refs_0_), channel_id=1, source_target_pairs={{0,8},{1,9},{2,10},{3,11},{4,12},{5,13},{6,14},{7,15},{8,0},{9,1},... | collective-permute-start | bytes 49160 | tf_op jit(solution)/shard_map/ppermute | solution.py:300
  6.7 0.7 %collective-permute-start.1 = (f32[32,128]{1,0:T(8,128)S(1)}, f32[32,128]{1,0:T(8,128)S(1)}, u32[]{:S(2)}, u32[]{:S(2)}) collective-permute-start(f32[32,128]{1,0:T(8,128)S(1)} %shard_map.86.refs_0_), channel_id=1, source_target_pairs={{0,3},{1,2},{2,1},{3,0},{4,5},{5,4},{6,7},{7,6},{8,16},{9,17},{10,... | collective-permute-start | bytes 49160 | tf_op jit(solution)/shard_map/ppermute | solution.py:300
  7.4 0.0 collective-permute-start
  7.4 1.4 %shard_map.87 = (bf16[256,512]{1,0:T(8,128)(2,1)S(1)}, bf16[256,512]{1,0:T(8,128)(2,1)S(1)}, f32[40,128]{1,0:T(8,128)S(1)}) custom-call(f32[512,256]{1,0:T(8,128)} %strips_in.1, s32[4,8]{1,0:T(4,128)} %bitcast.2, f32[4]{0:T(128)} %shifts_in.1), custom_call_target="tpu_custom_call" | custom-call | flops 1000000 | bytes 1000000 | tf_op jit(solution)/shard_map/pallas_call | solution.py:353
  8.8 0.0 collective-permute-done.3.refs_4_
  8.8 0.0 collective-permute-done.2.refs_3_
  8.8 1.1 %collective-permute-done.1.refs_2_ = f32[32,128]{1,0:T(8,128)S(1)} collective-permute-done((f32[32,128]{1,0:T(8,128)S(1)}, f32[32,128]{1,0:T(8,128)S(1)}, u32[]{:S(2)}, u32[]{:S(2)}) %collective-permute-start.1) | collective-permute-done | bytes 16416 | tf_op jit(solution)/shard_map/ppermute | solution.py:300
  9.9 0.0 collective-permute-done.refs_1_
  9.9 0.5 %shard_map.88 = (f32[24,128]{1,0:T(8,128)S(1)}, f32[48,256]{1,0:T(8,128)S(1)}) custom-call(f32[32,128]{1,0:T(8,128)S(1)} %shard_map.86.refs_0_, f32[32,128]{1,0:T(8,128)S(1)} %collective-permute-done.refs_1_, f32[32,128]{1,0:T(8,128)S(1)} %collective-permute-done.1.refs_2_, f32[32,128]{1,0:T(8,128)S(1)} %collective-permute-done.2.refs_3_, ...), custom_call_target="tpu_custom_call" | custom-call | flops 50000000 | bytes 600000 | tf_op jit(solution)/shard_map/pallas_call | solution.py:368
  10.5 0.0 collective-permute-start.7
  10.5 1.9 %collective-permute-start.6 = (f32[24,128]{1,0:T(8,128)S(1)}, f32[24,128]{1,0:T(8,128)S(1)}, u32[]{:S(2)}, u32[]{:S(2)}) collective-permute-start(f32[24,128]{1,0:T(8,128)S(1)} %get-tuple-element.16.refs_0_.t0), channel_id=1, source_target_pairs={{0,8},{1,9},{2,10},{3,11},{4,12},{5,13},{6,14},{7,15},{8,0},{9,1},... | collective-permute-start | bytes 36872 | tf_op jit(solution)/shard_map/ppermute | solution.py:300
  12.3 1.4 %collective-permute-start.5 = (f32[24,128]{1,0:T(8,128)S(1)}, f32[24,128]{1,0:T(8,128)S(1)}, u32[]{:S(2)}, u32[]{:S(2)}) collective-permute-start(f32[24,128]{1,0:T(8,128)S(1)} %get-tuple-element.16.refs_0_.t0), channel_id=1, source_target_pairs={{0,3},{1,2},{2,1},{3,0},{4,5},{5,4},{6,7},{7,6},{8,16},{9,17},{10,... | collective-permute-start | bytes 36872 | tf_op jit(solution)/shard_map/ppermute | solution.py:300
  13.7 0.5 %collective-permute-start.4 = (f32[24,128]{1,0:T(8,128)S(1)}, f32[24,128]{1,0:T(8,128)S(1)}, u32[]{:S(2)}, u32[]{:S(2)}) collective-permute-start(f32[24,128]{1,0:T(8,128)S(1)} %get-tuple-element.16.refs_0_.t0), channel_id=1, source_target_pairs={{0,1},{1,0},{2,3},{3,2},{4,5},{5,4},{6,7},{7,6},{8,9},{9,8},{10,11... | collective-permute-start | bytes 36872 | tf_op jit(solution)/shard_map/ppermute | solution.py:300
  14.2 0.0 collective-permute-done.7.refs_4_
  14.2 0.1 collective-permute-done.6.refs_3_
  14.2 1.2 %collective-permute-done.5.refs_2_ = f32[24,128]{1,0:T(8,128)S(1)} collective-permute-done((f32[24,128]{1,0:T(8,128)S(1)}, f32[24,128]{1,0:T(8,128)S(1)}, u32[]{:S(2)}, u32[]{:S(2)}) %collective-permute-start.5) | collective-permute-done | bytes 12320 | tf_op jit(solution)/shard_map/ppermute | solution.py:300
  15.4 0.0 collective-permute-done.4.refs_1_
  15.5 0.4 shard_map.89.refs_0_.t1
  15.9 0.0 copy-start
  15.9 0.2 collective-permute-start.11
  16.1 3.2 %collective-permute-start.10 = (f32[24,128]{1,0:T(8,128)S(1)}, f32[24,128]{1,0:T(8,128)S(1)}, u32[]{:S(2)}, u32[]{:S(2)}) collective-permute-start(f32[24,128]{1,0:T(8,128)S(1)} %shard_map.89.refs_0_.t1), channel_id=1, source_target_pairs={{0,8},{1,9},{2,10},{3,11},{4,12},{5,13},{6,14},{7,15},{8,0},{9,1},... | collective-permute-start | bytes 36872 | tf_op jit(solution)/shard_map/ppermute | solution.py:300
  19.3 0.4 collective-permute-start.9
  19.7 0.0 collective-permute-start.8
  19.7 0.0 collective-permute-done.11.refs_4_
  19.7 1.4 %collective-permute-done.10.refs_3_ = f32[24,128]{1,0:T(8,128)S(1)} collective-permute-done((f32[24,128]{1,0:T(8,128)S(1)}, f32[24,128]{1,0:T(8,128)S(1)}, u32[]{:S(2)}, u32[]{:S(2)}) %collective-permute-start.10) | collective-permute-done | bytes 12320 | tf_op jit(solution)/shard_map/ppermute | solution.py:300
  21.1 1.3 %collective-permute-done.9.refs_2_ = f32[24,128]{1,0:T(8,128)S(1)} collective-permute-done((f32[24,128]{1,0:T(8,128)S(1)}, f32[24,128]{1,0:T(8,128)S(1)}, u32[]{:S(2)}, u32[]{:S(2)}) %collective-permute-start.9) | collective-permute-done | bytes 12320 | tf_op jit(solution)/shard_map/ppermute | solution.py:300
  22.4 0.0 collective-permute-done.8.refs_1_
  22.4 0.4 shard_map.90.t2.own
  22.8 0.0 collective-permute-start.15
  22.8 1.8 %collective-permute-start.14 = (f32[24,128]{1,0:T(8,128)S(1)}, f32[24,128]{1,0:T(8,128)S(1)}, u32[]{:S(2)}, u32[]{:S(2)}) collective-permute-start(f32[24,128]{1,0:T(8,128)S(1)} %shard_map.90.t2.own), channel_id=1, source_target_pairs={{0,8},{1,9},{2,10},{3,11},{4,12},{5,13},{6,14},{7,15},{8,0},{9,1},... | collective-permute-start | bytes 36872 | tf_op jit(solution)/shard_map/ppermute | solution.py:300
  24.6 1.2 %collective-permute-start.13 = (f32[24,128]{1,0:T(8,128)S(1)}, f32[24,128]{1,0:T(8,128)S(1)}, u32[]{:S(2)}, u32[]{:S(2)}) collective-permute-start(f32[24,128]{1,0:T(8,128)S(1)} %shard_map.90.t2.own), channel_id=1, source_target_pairs={{0,3},{1,2},{2,1},{3,0},{4,5},{5,4},{6,7},{7,6},{8,16},{9,17},{10,... | collective-permute-start | bytes 36872 | tf_op jit(solution)/shard_map/ppermute | solution.py:300
  25.9 0.0 collective-permute-start.12
  25.9 0.0 copy-done
  25.9 0.5 %shard_map.91 = (f32[24,512]{1,0:T(8,128)S(1)}, f32[40,128]{1,0:T(8,128)S(1)}) custom-call(f32[3,32,512]{2,1,0:T(8,128)S(1)} %copy-done, f32[24,128]{1,0:T(8,128)S(1)} %get-tuple-element.16.refs_0_.t0, f32[24,128]{1,0:T(8,128)S(1)} %shard_map.89.refs_0_.t1, f32[24,128]{1,0:T(8,128)S(1)} %shard_map.90.t2.own), custom_call_target="tpu_custom_call" | custom-call | flops 60000000 | bytes 250000 | tf_op jit(solution)/shard_map/pallas_call | solution.py:383
  26.4 0.1 collective-permute-done.15.d
  26.5 0.1 collective-permute-done.14.c
  26.6 1.2 %collective-permute-done.13.b = f32[24,128]{1,0:T(8,128)S(1)} collective-permute-done((f32[24,128]{1,0:T(8,128)S(1)}, f32[24,128]{1,0:T(8,128)S(1)}, u32[]{:S(2)}, u32[]{:S(2)}) %collective-permute-start.13) | collective-permute-done | bytes 12320 | tf_op jit(solution)/shard_map/ppermute | solution.py:300
  27.8 0.0 collective-permute-done.12.a
  27.8 0.8 %shard_map.92 = (f32[8,512]{1,0:T(8,128)S(1)}, f32[40,128]{1,0:T(8,128)S(1)}) custom-call(f32[24,128]{1,0:T(8,128)S(1)} %shard_map.90.t2.own, f32[24,128]{1,0:T(8,128)S(1)} %collective-permute-done.12.a, f32[24,128]{1,0:T(8,128)S(1)} %collective-permute-done.13.b, f32[24,128]{1,0:T(8,128)S(1)} %collective-permute-done.14.c, ...), custom_call_target="tpu_custom_call" | custom-call | flops 80000000 | bytes 900000 | tf_op jit(solution)/shard_map/pallas_call | solution.py:386
  28.6 0.0 collective-permute-start.16
  28.6 1.2 %collective-permute-done.16 = f32[40,128]{1,0:T(8,128)S(1)} collective-permute-done((f32[40,128]{1,0:T(8,128)S(1)}, f32[40,128]{1,0:T(8,128)S(1)}, u32[]{:S(2)}, u32[]{:S(2)}) %collective-permute-start.16) | collective-permute-done | bytes 20512 | tf_op jit(solution)/shard_map/ppermute | solution.py:300
  29.8 1.2 %collective-permute-start.17 = (f32[40,128]{1,0:T(8,128)S(1)}, f32[40,128]{1,0:T(8,128)S(1)}, u32[]{:S(2)}, u32[]{:S(2)}) collective-permute-start(f32[40,128]{1,0:T(8,128)S(1)} %add.15), channel_id=1, source_target_pairs={{0,3},{1,2},{2,1},{3,0},{4,7},{5,6},{6,5},{7,4},{8,11},{9,10},{10,... | collective-permute-start | bytes 61448 | tf_op jit(solution)/shard_map/ppermute | solution.py:300
  31.0 2.0 %collective-permute-done.17 = f32[40,128]{1,0:T(8,128)S(1)} collective-permute-done((f32[40,128]{1,0:T(8,128)S(1)}, f32[40,128]{1,0:T(8,128)S(1)}, u32[]{:S(2)}, u32[]{:S(2)}) %collective-permute-start.17) | collective-permute-done | bytes 20512 | tf_op jit(solution)/shard_map/ppermute | solution.py:300
  33.0 0.4 collective-permute-start.18
  33.4 2.8 %collective-permute-done.18 = f32[40,128]{1,0:T(8,128)S(1)} collective-permute-done((f32[40,128]{1,0:T(8,128)S(1)}, f32[40,128]{1,0:T(8,128)S(1)}, u32[]{:S(2)}, u32[]{:S(2)}) %collective-permute-start.18) | collective-permute-done | bytes 20512 | tf_op jit(solution)/shard_map/ppermute | solution.py:300
  36.2 0.8 %collective-permute-start.19 = (f32[40,128]{1,0:T(8,128)S(1)}, f32[40,128]{1,0:T(8,128)S(1)}, u32[]{:S(2)}, u32[]{:S(2)}) collective-permute-start(f32[40,128]{1,0:T(8,128)S(1)} %add.17), channel_id=1, source_target_pairs={{0,9},{1,8},{2,11},{3,10},{4,13},{5,12},{6,15},{7,14},{8,1},{9,0},... | collective-permute-start | bytes 61448 | tf_op jit(solution)/shard_map/ppermute | solution.py:300
  37.0 2.4 %collective-permute-done.19 = f32[40,128]{1,0:T(8,128)S(1)} collective-permute-done((f32[40,128]{1,0:T(8,128)S(1)}, f32[40,128]{1,0:T(8,128)S(1)}, u32[]{:S(2)}, u32[]{:S(2)}) %collective-permute-start.19) | collective-permute-done | bytes 20512 | tf_op jit(solution)/shard_map/ppermute | solution.py:300
  39.4 2.1 %collective-permute-start.20 = (f32[40,128]{1,0:T(8,128)S(1)}, f32[40,128]{1,0:T(8,128)S(1)}, u32[]{:S(2)}, u32[]{:S(2)}) collective-permute-start(f32[40,128]{1,0:T(8,128)S(1)} %add.18), channel_id=1, source_target_pairs={{0,17},{1,16},{2,19},{3,18},{4,21},{5,20},{6,23},{7,22},{8,25},{9,... | collective-permute-start | bytes 61448 | tf_op jit(solution)/shard_map/ppermute | solution.py:300
  41.5 2.0 %collective-permute-done.20 = f32[40,128]{1,0:T(8,128)S(1)} collective-permute-done((f32[40,128]{1,0:T(8,128)S(1)}, f32[40,128]{1,0:T(8,128)S(1)}, u32[]{:S(2)}, u32[]{:S(2)}) %collective-permute-start.20) | collective-permute-done | bytes 20512 | tf_op jit(solution)/shard_map/ppermute | solution.py:300
  43.5 1.1 %shard_map.93 = (f32[3,4,512]{2,1,0:T(4,128)}, f32[3,4,36]{2,1,0:T(4,128)}) custom-call(f32[40,128]{1,0:T(8,128)S(1)} %add.19.refs_0_, f32[3,32,512]{2,1,0:T(8,128)S(1)} %copy-done, f32[24,512]{1,0:T(8,128)S(1)} %get-tuple-element.18.lines.refs_2_, f32[8,512]{1,0:T(8,128)S(1)} %get-tuple-element.21.refs_3_), custom_call_target="tpu_custom_call" | custom-call | flops 50000000 | bytes 400000 | tf_op jit(solution)/shard_map/pallas_call | solution.py:390
  (5 shorter events, 0.0 us)
Async XLA Ops:
  1.9 6.9 %collective-permute-start.3 = (f32[32,128]{1,0:T(8,128)S(1)}, f32[32,128]{1,0:T(8,128)S(1)}, u32[]{:S(2)}, u32[]{:S(2)}) collective-permute-start(f32[32,128]{1,0:T(8,128)S(1)} %shard_map.86.refs_0_), channel_id=1, source_target_pairs={{0,1},{1,2},{2,0},{3,4},{4,3},{5,6},{6,5},{7,8},{8,7},{9,10},{10,9... | collective-permute-start | bytes 49160 | tf_op jit(solution)/shard_map/ppermute | solution.py:300
  2.4 6.4 %collective-permute-start.2 = (f32[32,128]{1,0:T(8,128)S(1)}, f32[32,128]{1,0:T(8,128)S(1)}, u32[]{:S(2)}, u32[]{:S(2)}) collective-permute-start(f32[32,128]{1,0:T(8,128)S(1)} %shard_map.86.refs_0_), channel_id=1, source_target_pairs={{0,8},{1,9},{2,10},{3,11},{4,12},{5,13},{6,14},{7,15},{8,0},{9,1},... | collective-permute-start | bytes 49160 | tf_op jit(solution)/shard_map/ppermute | solution.py:300
  6.7 3.2 %collective-permute-start.1 = (f32[32,128]{1,0:T(8,128)S(1)}, f32[32,128]{1,0:T(8,128)S(1)}, u32[]{:S(2)}, u32[]{:S(2)}) collective-permute-start(f32[32,128]{1,0:T(8,128)S(1)} %shard_map.86.refs_0_), channel_id=1, source_target_pairs={{0,3},{1,2},{2,1},{3,0},{4,5},{5,4},{6,7},{7,6},{8,16},{9,17},{10,... | collective-permute-start | bytes 49160 | tf_op jit(solution)/shard_map/ppermute | solution.py:300
  7.4 2.5 %collective-permute-start = (f32[32,128]{1,0:T(8,128)S(1)}, f32[32,128]{1,0:T(8,128)S(1)}, u32[]{:S(2)}, u32[]{:S(2)}) collective-permute-start(f32[32,128]{1,0:T(8,128)S(1)} %shard_map.86.refs_0_), channel_id=1, source_target_pairs={{0,1},{1,0},{2,3},{3,2},{4,5},{5,4},{6,7},{7,6},{8,9},{9,8},{10,11... | collective-permute-start | bytes 49160 | tf_op jit(solution)/shard_map/ppermute | solution.py:300
  10.5 3.7 %collective-permute-start.7 = (f32[24,128]{1,0:T(8,128)S(1)}, f32[24,128]{1,0:T(8,128)S(1)}, u32[]{:S(2)}, u32[]{:S(2)}) collective-permute-start(f32[24,128]{1,0:T(8,128)S(1)} %get-tuple-element.16.refs_0_.t0), channel_id=1, source_target_pairs={{0,1},{1,2},{2,0},{3,4},{4,3},{5,6},{6,5},{7,8},{8,7},{9,10},{10,9... | collective-permute-start | bytes 36872 | tf_op jit(solution)/shard_map/ppermute | solution.py:300
  10.5 3.8 %collective-permute-start.6 = (f32[24,128]{1,0:T(8,128)S(1)}, f32[24,128]{1,0:T(8,128)S(1)}, u32[]{:S(2)}, u32[]{:S(2)}) collective-permute-start(f32[24,128]{1,0:T(8,128)S(1)} %get-tuple-element.16.refs_0_.t0), channel_id=1, source_target_pairs={{0,8},{1,9},{2,10},{3,11},{4,12},{5,13},{6,14},{7,15},{8,0},{9,1},... | collective-permute-start | bytes 36872 | tf_op jit(solution)/shard_map/ppermute | solution.py:300
  12.3 3.1 %collective-permute-start.5 = (f32[24,128]{1,0:T(8,128)S(1)}, f32[24,128]{1,0:T(8,128)S(1)}, u32[]{:S(2)}, u32[]{:S(2)}) collective-permute-start(f32[24,128]{1,0:T(8,128)S(1)} %get-tuple-element.16.refs_0_.t0), channel_id=1, source_target_pairs={{0,3},{1,2},{2,1},{3,0},{4,5},{5,4},{6,7},{7,6},{8,16},{9,17},{10,... | collective-permute-start | bytes 36872 | tf_op jit(solution)/shard_map/ppermute | solution.py:300
  13.7 1.8 %collective-permute-start.4 = (f32[24,128]{1,0:T(8,128)S(1)}, f32[24,128]{1,0:T(8,128)S(1)}, u32[]{:S(2)}, u32[]{:S(2)}) collective-permute-start(f32[24,128]{1,0:T(8,128)S(1)} %get-tuple-element.16.refs_0_.t0), channel_id=1, source_target_pairs={{0,1},{1,0},{2,3},{3,2},{4,5},{5,4},{6,7},{7,6},{8,9},{9,8},{10,11... | collective-permute-start | bytes 36872 | tf_op jit(solution)/shard_map/ppermute | solution.py:300
  15.9 10.0 %copy-start = (f32[3,32,512]{2,1,0:T(8,128)S(1)}, f32[3,32,512]{2,1,0:T(8,128)}, u32[]{:S(2)}) copy-start(f32[3,32,512]{2,1,0:T(8,128)} %refs_1_.1) | copy-start | bytes 589828
  15.9 3.8 %collective-permute-start.11 = (f32[24,128]{1,0:T(8,128)S(1)}, f32[24,128]{1,0:T(8,128)S(1)}, u32[]{:S(2)}, u32[]{:S(2)}) collective-permute-start(f32[24,128]{1,0:T(8,128)S(1)} %shard_map.89.refs_0_.t1), channel_id=1, source_target_pairs={{0,1},{1,2},{2,0},{3,4},{4,3},{5,6},{6,5},{7,8},{8,7},{9,10},{10,9... | collective-permute-start | bytes 36872 | tf_op jit(solution)/shard_map/ppermute | solution.py:300
  16.1 5.0 %collective-permute-start.10 = (f32[24,128]{1,0:T(8,128)S(1)}, f32[24,128]{1,0:T(8,128)S(1)}, u32[]{:S(2)}, u32[]{:S(2)}) collective-permute-start(f32[24,128]{1,0:T(8,128)S(1)} %shard_map.89.refs_0_.t1), channel_id=1, source_target_pairs={{0,8},{1,9},{2,10},{3,11},{4,12},{5,13},{6,14},{7,15},{8,0},{9,1},... | collective-permute-start | bytes 36872 | tf_op jit(solution)/shard_map/ppermute | solution.py:300
  19.3 3.1 %collective-permute-start.9 = (f32[24,128]{1,0:T(8,128)S(1)}, f32[24,128]{1,0:T(8,128)S(1)}, u32[]{:S(2)}, u32[]{:S(2)}) collective-permute-start(f32[24,128]{1,0:T(8,128)S(1)} %shard_map.89.refs_0_.t1), channel_id=1, source_target_pairs={{0,3},{1,2},{2,1},{3,0},{4,5},{5,4},{6,7},{7,6},{8,16},{9,17},{10,... | collective-permute-start | bytes 36872 | tf_op jit(solution)/shard_map/ppermute | solution.py:300
  19.7 2.7 %collective-permute-start.8 = (f32[24,128]{1,0:T(8,128)S(1)}, f32[24,128]{1,0:T(8,128)S(1)}, u32[]{:S(2)}, u32[]{:S(2)}) collective-permute-start(f32[24,128]{1,0:T(8,128)S(1)} %shard_map.89.refs_0_.t1), channel_id=1, source_target_pairs={{0,1},{1,0},{2,3},{3,2},{4,5},{5,4},{6,7},{7,6},{8,9},{9,8},{10,11... | collective-permute-start | bytes 36872 | tf_op jit(solution)/shard_map/ppermute | solution.py:300
  22.8 3.7 %collective-permute-start.15 = (f32[24,128]{1,0:T(8,128)S(1)}, f32[24,128]{1,0:T(8,128)S(1)}, u32[]{:S(2)}, u32[]{:S(2)}) collective-permute-start(f32[24,128]{1,0:T(8,128)S(1)} %shard_map.90.t2.own), channel_id=1, source_target_pairs={{0,1},{1,2},{2,0},{3,4},{4,3},{5,6},{6,5},{7,8},{8,7},{9,10},{10,9... | collective-permute-start | bytes 36872 | tf_op jit(solution)/shard_map/ppermute | solution.py:300
  22.8 3.8 %collective-permute-start.14 = (f32[24,128]{1,0:T(8,128)S(1)}, f32[24,128]{1,0:T(8,128)S(1)}, u32[]{:S(2)}, u32[]{:S(2)}) collective-permute-start(f32[24,128]{1,0:T(8,128)S(1)} %shard_map.90.t2.own), channel_id=1, source_target_pairs={{0,8},{1,9},{2,10},{3,11},{4,12},{5,13},{6,14},{7,15},{8,0},{9,1},... | collective-permute-start | bytes 36872 | tf_op jit(solution)/shard_map/ppermute | solution.py:300
  24.6 3.1 %collective-permute-start.13 = (f32[24,128]{1,0:T(8,128)S(1)}, f32[24,128]{1,0:T(8,128)S(1)}, u32[]{:S(2)}, u32[]{:S(2)}) collective-permute-start(f32[24,128]{1,0:T(8,128)S(1)} %shard_map.90.t2.own), channel_id=1, source_target_pairs={{0,3},{1,2},{2,1},{3,0},{4,5},{5,4},{6,7},{7,6},{8,16},{9,17},{10,... | collective-permute-start | bytes 36872 | tf_op jit(solution)/shard_map/ppermute | solution.py:300
  25.9 1.9 %collective-permute-start.12 = (f32[24,128]{1,0:T(8,128)S(1)}, f32[24,128]{1,0:T(8,128)S(1)}, u32[]{:S(2)}, u32[]{:S(2)}) collective-permute-start(f32[24,128]{1,0:T(8,128)S(1)} %shard_map.90.t2.own), channel_id=1, source_target_pairs={{0,1},{1,0},{2,3},{3,2},{4,5},{5,4},{6,7},{7,6},{8,9},{9,8},{10,11... | collective-permute-start | bytes 36872 | tf_op jit(solution)/shard_map/ppermute | solution.py:300
  28.6 1.2 %collective-permute-start.16 = (f32[40,128]{1,0:T(8,128)S(1)}, f32[40,128]{1,0:T(8,128)S(1)}, u32[]{:S(2)}, u32[]{:S(2)}) collective-permute-start(f32[40,128]{1,0:T(8,128)S(1)} %get-tuple-element.20), channel_id=1, source_target_pairs={{0,1},{1,0},{2,3},{3,2},{4,5},{5,4},{6,7},{7,6},{8,9},{9,8},{10,11... | collective-permute-start | bytes 61448 | tf_op jit(solution)/shard_map/ppermute | solution.py:300
  29.8 3.2 %collective-permute-start.17 = (f32[40,128]{1,0:T(8,128)S(1)}, f32[40,128]{1,0:T(8,128)S(1)}, u32[]{:S(2)}, u32[]{:S(2)}) collective-permute-start(f32[40,128]{1,0:T(8,128)S(1)} %add.15), channel_id=1, source_target_pairs={{0,3},{1,2},{2,1},{3,0},{4,7},{5,6},{6,5},{7,4},{8,11},{9,10},{10,... | collective-permute-start | bytes 61448 | tf_op jit(solution)/shard_map/ppermute | solution.py:300
  33.0 3.2 %collective-permute-start.18 = (f32[40,128]{1,0:T(8,128)S(1)}, f32[40,128]{1,0:T(8,128)S(1)}, u32[]{:S(2)}, u32[]{:S(2)}) collective-permute-start(f32[40,128]{1,0:T(8,128)S(1)} %add.16), channel_id=1, source_target_pairs={{0,5},{1,4},{2,7},{3,6},{4,1},{5,0},{6,3},{7,2},{8,13},{9,12},{10,... | collective-permute-start | bytes 61448 | tf_op jit(solution)/shard_map/ppermute | solution.py:300
  36.2 3.2 %collective-permute-start.19 = (f32[40,128]{1,0:T(8,128)S(1)}, f32[40,128]{1,0:T(8,128)S(1)}, u32[]{:S(2)}, u32[]{:S(2)}) collective-permute-start(f32[40,128]{1,0:T(8,128)S(1)} %add.17), channel_id=1, source_target_pairs={{0,9},{1,8},{2,11},{3,10},{4,13},{5,12},{6,15},{7,14},{8,1},{9,0},... | collective-permute-start | bytes 61448 | tf_op jit(solution)/shard_map/ppermute | solution.py:300
  39.4 4.1 %collective-permute-start.20 = (f32[40,128]{1,0:T(8,128)S(1)}, f32[40,128]{1,0:T(8,128)S(1)}, u32[]{:S(2)}, u32[]{:S(2)}) collective-permute-start(f32[40,128]{1,0:T(8,128)S(1)} %add.18), channel_id=1, source_target_pairs={{0,17},{1,16},{2,19},{3,18},{4,21},{5,20},{6,23},{7,22},{8,25},{9,... | collective-permute-start | bytes 61448 | tf_op jit(solution)/shard_map/ppermute | solution.py:300

commit v6 on v5

--- a/solution.py
+++ b/solution.py
@@ -43,6 +43,14 @@
         line = jnp.sum(wide[c * 8 : (c + 1) * 8], axis=0, keepdims=True)
         result = jnp.where(where == c, jnp.broadcast_to(line, result.shape), result)
     return result
+
+
+def split(x):
+    parts = []
+    for _ in range(3):
+        parts.append(x.astype(jnp.bfloat16))
+        x = x - parts[-1].astype(jnp.float32)
+    return parts
 
 
 def fetch(pairs, sems):
@@ -188,7 +196,7 @@
     return jnp.sum(jnp.where(mine, gram, 0.0), axis=0, keepdims=True)
 
 
-def early_kernel(prev_ref, t0, t1, t2, lines_ref, gram_ref):
+def early_kernel(prev_ref, t0, t1, t2, lines_ref, gram_ref, *turned_refs):
     comps, vecs, rows = prev_ref.shape
     width = comps * vecs
     lines = jnp.concatenate([lines_of(t[...], rows) for t in (t0, t1, t2)], axis=0)
@@ -201,6 +209,8 @@
         total = total + jnp.where(owner == c, full[c * vecs : (c + 1) * vecs], 0.0)
     gram_ref[:vecs, :] = jnp.concatenate([total, jnp.zeros((vecs, 128 - width), jnp.float32)], axis=1)
     against = jnp.concatenate([prev, lines, jnp.zeros((8, rows), jnp.float32)], axis=0)
+    for ref, part in zip(turned_refs, split(against.T)):
+        ref[...] = part
     gram = dot(lines, against, NT, HIGHEST)
     result = jnp.zeros((8, 128), jnp.float32)
     for k in range(S - 1):
@@ -209,15 +219,21 @@
     gram_ref[vecs:, :] = result
 
 
-def last_kernel(own, a, b, c, d, choose, aux, high, low, lines, prev_ref, early, line_ref, gram_ref):
+def last_kernel(own, a, b, c, d, choose, aux, high, low, early, t0, t1, t2, line_ref, gram_ref):
     pieces = [ref[...] for ref in (own, a, b, c, d)]
     tile = multiply(choose[...], pieces, aux[8 * S - 8 : 8 * S, :], high[...], low[...])
-    comps, vecs, rows = prev_ref.shape
-    width = comps * vecs
+    rows = line_ref.shape[1]
+    vecs = early.shape[0] - 8
+    width = COMPS * vecs
     last = lines_of(tile, rows)
     line_ref[...] = last
-    against = jnp.concatenate([prev_ref[...].reshape(width, rows), lines[...], last], axis=0)
-    line = collect(dot(last, against, NT, HIGHEST), width, vecs)
+    parts = [part.astype(jnp.float32) for part in split(last)]
+    left = jnp.concatenate(parts + [jnp.zeros_like(last)], axis=0).astype(jnp.bfloat16)
+    products = dot(left, t0[...]) + dot(left, t1[...]) + dot(left, t2[...])
+    gram = products[:8] + (products[8:16] + products[16:24])
+    square = jnp.sum(last * last, axis=1, keepdims=True)
+    gram = jnp.where(iota(gram.shape, 1) == width + 8 * (S - 1) + iota(gram.shape, 0), square, gram)
+    line = collect(gram, width, vecs)
     gram_ref[:vecs, :] = early[:vecs, :]
     gram_ref[vecs:, :] = jnp.where(
         iota((8, 128), 0) == S - 1, jnp.broadcast_to(line, (8, 128)), early[vecs:, :]
@@ -237,32 +253,33 @@
         coef.append(jnp.where(in_prev, line, 0.0))
         cross.append([jnp.where(lane == width + 8 * l + comp, line, 0.0) for l in range(k + 1)])
     coefs = jnp.concatenate(coef, axis=0)
-    prev = prev_ref[...].reshape(width, rows)
-    basis = jnp.concatenate([lines[...], last[...]], axis=0)
-    projected = basis - dot(coefs[:, :width], prev, precision=HIGHEST)
     square = jnp.concatenate([gram[:vecs]] * comps, axis=0)
     r, q = iota(square.shape, 0), iota(square.shape, 1)
     square = jnp.where(r // vecs == q // vecs, square, 0.0) - jnp.where(r == q, 2.0, 0.0)
     turned = dot(coefs[:, :width], square, precision=HIGHEST)
-    entry = {}
-    for k in range(S):
-        for l in range(k + 1):
+    prev = prev_ref[...].reshape(width, rows)
+    basis = jnp.concatenate([lines[...], last[...]], axis=0)
+    projected = basis - dot(coefs[:, :width], prev, precision=HIGHEST)
+    unit, scale = {}, {}
+    for l in range(S):
+        for k in range(l, S):
             value = turned[k * 8 : (k + 1) * 8] * coef[l] + cross[k][l]
-            entry[k, l] = jnp.sum(value, axis=1, keepdims=True)
-    lower = {}
-    for k in range(S):
-        for l in range(k + 1):
-            value = entry[k, l]
+            value = jnp.sum(value, axis=1, keepdims=True)
             for m in range(l):
-                value = value - lower[k, m] * lower[l, m]
-            lower[k, l] = jnp.sqrt(value) if l == k else value / lower[l, l]
+                value = value - (unit[k, m] * scale[m]) * unit[l, m]
+            if k == l:
+                scale[l] = value
+            else:
+                unit[k, l] = value / scale[l]
+    roots = [jnp.sqrt(scale[k]) for k in range(S)]
+    lower = {(k, l): unit[k, l] * roots[l] if l < k else roots[k] for k in range(S) for l in range(k + 1)}
     vectors = []
     for k in range(S):
         value = projected[k * 8 : (k + 1) * 8]
         for l in range(k):
-            value = value - lower[k, l] * vectors[l]
-        value = value / lower[k, k]
+            value = value - unit[k, l] * vectors[l]
         vectors.append(value)
+        value = value / roots[k]
         for c in range(comps):
             basis_ref[c, k : k + 1, :] = value[c : c + 1]
     for c in range(comps):
@@ -323,10 +340,21 @@
 
 
 def summed(value):
-    step = 1
-    while step < lax.axis_size("dom"):
-        value = value + send(value, {d: d ^ (step | 1) for d in range(lax.axis_size("dom"))})
-        step *= 2
+    length = lax.axis_size("dom")
+
+    def fetched(step):
+        return send(value, {d: d ^ (step | 1) for d in range(length)})
+
+    value = value + fetched(1)
+    step = 2
+    while step < length:
+        if 2 * step < length:
+            farthest = fetched(3 * step)
+            first, second = fetched(step), fetched(2 * step)
+            value = (value + first) + (second + farthest)
+        else:
+            value = value + fetched(step)
+        step *= 4
     return value
 
 
@@ -380,12 +408,16 @@
         tiles.append(tile)
     received = ghosts(tile)
     gram_out = ((vecs + 8, 128), f32)
-    lines, early = call(
-        early_kernel, [((8 * S - 8, rows), f32), gram_out], [VMEM] * 4, 60000000, 250000
+    lines, early, *turned = call(
+        early_kernel,
+        [((8 * S - 8, rows), f32), gram_out] + [((rows, 128), bf16)] * 3,
+        [VMEM] * 4,
+        60000000,
+        250000,
     )(prev_basis, *tiles)
     last, gram = call(
-        last_kernel, [((8, rows), f32), gram_out], [VMEM] * 12, 80000000, 900000
-    )(tile, *received, choose, aux, high, low, lines, prev_basis, early)
+        last_kernel, [((8, rows), f32), gram_out], [VMEM] * 13, 80000000, 900000
+    )(tile, *received, choose, aux, high, low, early, *turned)
     total = float(length * rows)
     basis, factors = call(
         lambda *refs: finish_kernel(total, *refs),

time: 44.8 us -> 42.8 us (0.955)
  waiting for transfers between devices: 16.9 us -> 12.6 us
  starting transfers between devices: 20.5 us -> 23.2 us
    ppermute x21 -> x23, waiting for transfers between devices: 16.9 us -> 12.6 us  [send(): lax.ppermute(value, 'dom', [(d, target[d]) for d in range(lax.axis_size('...]
    ppermute x21 -> x23, starting transfers between devices: 20.5 us -> 23.2 us  [send(): lax.ppermute(value, 'dom', [(d, target[d]) for d in range(lax.axis_size('...]
  transfers between devices with their start and end apart: 21 -> 23, of which waited for: 13 -> 15; matrix products, arithmetic and copies ran while one was open for 0% -> 0% of each run, Pallas kernels for 4% -> 4%
where the time goes in v6:
time: 42.8 us; the launch traced here: 42.7 us
  starting transfers between devices  23.2 us (54%)
  waiting for transfers between devices  12.6 us (29%)
  Pallas kernels  6.13 us (14%)
  between operations  0.72 us (2%)
    ppermute x23, starting transfers between devices, send(): lax.ppermute(value, 'dom', [(d, target[d]) for d in range(lax.axis_size('...  23.2 us
    ppermute x23, waiting for transfers between devices, send(): lax.ppermute(value, 'dom', [(d, target[d]) for d in range(lax.axis_size('...  12.6 us
    pallas_call x1, Pallas kernels, local(): call(prepare_kernel, [((width, rows), bf16), ((width, rows), bf16), ((8 *...  1.39 us
    pallas_call x1, Pallas kernels, local(): call(start_kernel, [((comps * blocks + 8, 128), f32)], [HBM] * 4, 600000,...  1.26 us
    pallas_call x1, Pallas kernels, local(): call(lambda *refs: finish_kernel(total, *refs), [((comps, S, rows), f32),...  0.95 us
    pallas_call x2, Pallas kernels, local(): call(lambda *refs, step=step: middle_kernel(step, *refs), [tile_out], [VM...  0.87 us
  transfers between devices with their start and end apart: 23, of which 15 were waited for; matrix products, arithmetic and copies ran while one was open for 0% of the time, Pallas kernels for 4%

profile of v6, /device:TPU:0, one launch (start us, length us, event | category | flops | bytes accessed | tf_op | source)
XLA Modules:
  0.0 42.7 jit_solution(1170750041003576828)
XLA Ops:
  0.6 1.3 %shard_map.86.refs_0_ = f32[32,128]{1,0:T(8,128)S(1)} custom-call(f32[3,32,512]{2,1,0:T(8,128)} %refs_1_.1, f32[3,32]{1,0:T(4,128)} %mix_in.1, s32[1,4,8]{2,1,0:T(4,128)} %list_in.1, s32[1,4]{1,0:T(1,128)} %count_in.1), custom_call_target="tpu_custom_call" | custom-call | flops 600000 | bytes 250000 | tf_op jit(solution)/shard_map/pallas_call | solution.py:367
  1.9 0.5 %collective-permute-start.3 = (f32[32,128]{1,0:T(8,128)S(1)}, f32[32,128]{1,0:T(8,128)S(1)}, u32[]{:S(2)}, u32[]{:S(2)}) collective-permute-start(f32[32,128]{1,0:T(8,128)S(1)} %shard_map.86.refs_0_), channel_id=1, source_target_pairs={{0,1},{1,2},{2,0},{3,4},{4,3},{5,6},{6,5},{7,8},{8,7},{9,10},{10,9... | collective-permute-start | bytes 49160 | tf_op jit(solution)/shard_map/ppermute | solution.py:317
  2.4 4.3 %collective-permute-start.2 = (f32[32,128]{1,0:T(8,128)S(1)}, f32[32,128]{1,0:T(8,128)S(1)}, u32[]{:S(2)}, u32[]{:S(2)}) collective-permute-start(f32[32,128]{1,0:T(8,128)S(1)} %shard_map.86.refs_0_), channel_id=1, source_target_pairs={{0,8},{1,9},{2,10},{3,11},{4,12},{5,13},{6,14},{7,15},{8,0},{9,1},... | collective-permute-start | bytes 49160 | tf_op jit(solution)/shard_map/ppermute | solution.py:317
  6.7 0.7 %collective-permute-start.1 = (f32[32,128]{1,0:T(8,128)S(1)}, f32[32,128]{1,0:T(8,128)S(1)}, u32[]{:S(2)}, u32[]{:S(2)}) collective-permute-start(f32[32,128]{1,0:T(8,128)S(1)} %shard_map.86.refs_0_), channel_id=1, source_target_pairs={{0,3},{1,2},{2,1},{3,0},{4,5},{5,4},{6,7},{7,6},{8,16},{9,17},{10,... | collective-permute-start | bytes 49160 | tf_op jit(solution)/shard_map/ppermute | solution.py:317
  7.4 0.0 collective-permute-start
  7.4 1.4 %shard_map.87 = (bf16[256,512]{1,0:T(8,128)(2,1)S(1)}, bf16[256,512]{1,0:T(8,128)(2,1)S(1)}, f32[40,128]{1,0:T(8,128)S(1)}) custom-call(f32[512,256]{1,0:T(8,128)} %strips_in.1, s32[4,8]{1,0:T(4,128)} %bitcast.2, f32[4]{0:T(128)} %shifts_in.1), custom_call_target="tpu_custom_call" | custom-call | flops 1000000 | bytes 1000000 | tf_op jit(solution)/shard_map/pallas_call | solution.py:381
  8.8 0.0 collective-permute-done.3.refs_4_
  8.8 0.0 collective-permute-done.2.refs_3_
  8.8 1.1 %collective-permute-done.1.refs_2_ = f32[32,128]{1,0:T(8,128)S(1)} collective-permute-done((f32[32,128]{1,0:T(8,128)S(1)}, f32[32,128]{1,0:T(8,128)S(1)}, u32[]{:S(2)}, u32[]{:S(2)}) %collective-permute-start.1) | collective-permute-done | bytes 16416 | tf_op jit(solution)/shard_map/ppermute | solution.py:317
  9.9 0.0 collective-permute-done.refs_1_
  9.9 0.5 %shard_map.88 = (f32[24,128]{1,0:T(8,128)S(1)}, f32[48,256]{1,0:T(8,128)S(1)}) custom-call(f32[32,128]{1,0:T(8,128)S(1)} %shard_map.86.refs_0_, f32[32,128]{1,0:T(8,128)S(1)} %collective-permute-done.refs_1_, f32[32,128]{1,0:T(8,128)S(1)} %collective-permute-done.1.refs_2_, f32[32,128]{1,0:T(8,128)S(1)} %collective-permute-done.2.refs_3_, ...), custom_call_target="tpu_custom_call" | custom-call | flops 50000000 | bytes 600000 | tf_op jit(solution)/shard_map/pallas_call | solution.py:396
  10.5 0.0 collective-permute-start.7
  10.5 1.9 %collective-permute-start.6 = (f32[24,128]{1,0:T(8,128)S(1)}, f32[24,128]{1,0:T(8,128)S(1)}, u32[]{:S(2)}, u32[]{:S(2)}) collective-permute-start(f32[24,128]{1,0:T(8,128)S(1)} %get-tuple-element.19.refs_0_.t0), channel_id=1, source_target_pairs={{0,8},{1,9},{2,10},{3,11},{4,12},{5,13},{6,14},{7,15},{8,0},{9,1},... | collective-permute-start | bytes 36872 | tf_op jit(solution)/shard_map/ppermute | solution.py:317
  12.3 1.4 %collective-permute-start.5 = (f32[24,128]{1,0:T(8,128)S(1)}, f32[24,128]{1,0:T(8,128)S(1)}, u32[]{:S(2)}, u32[]{:S(2)}) collective-permute-start(f32[24,128]{1,0:T(8,128)S(1)} %get-tuple-element.19.refs_0_.t0), channel_id=1, source_target_pairs={{0,3},{1,2},{2,1},{3,0},{4,5},{5,4},{6,7},{7,6},{8,16},{9,17},{10,... | collective-permute-start | bytes 36872 | tf_op jit(solution)/shard_map/ppermute | solution.py:317
  13.7 0.5 %collective-permute-start.4 = (f32[24,128]{1,0:T(8,128)S(1)}, f32[24,128]{1,0:T(8,128)S(1)}, u32[]{:S(2)}, u32[]{:S(2)}) collective-permute-start(f32[24,128]{1,0:T(8,128)S(1)} %get-tuple-element.19.refs_0_.t0), channel_id=1, source_target_pairs={{0,1},{1,0},{2,3},{3,2},{4,5},{5,4},{6,7},{7,6},{8,9},{9,8},{10,11... | collective-permute-start | bytes 36872 | tf_op jit(solution)/shard_map/ppermute | solution.py:317
  14.2 0.0 collective-permute-done.7.refs_4_
  14.2 0.1 collective-permute-done.6.refs_3_
  14.2 1.2 %collective-permute-done.5.refs_2_ = f32[24,128]{1,0:T(8,128)S(1)} collective-permute-done((f32[24,128]{1,0:T(8,128)S(1)}, f32[24,128]{1,0:T(8,128)S(1)}, u32[]{:S(2)}, u32[]{:S(2)}) %collective-permute-start.5) | collective-permute-done | bytes 12320 | tf_op jit(solution)/shard_map/ppermute | solution.py:317
  15.4 0.0 collective-permute-done.4.refs_1_
  15.5 0.4 %shard_map.89.refs_0_.t1 = f32[24,128]{1,0:T(8,128)S(1)} custom-call(f32[24,128]{1,0:T(8,128)S(1)} %get-tuple-element.19.refs_0_.t0, f32[24,128]{1,0:T(8,128)S(1)} %collective-permute-done.4.refs_1_, f32[24,128]{1,0:T(8,128)S(1)} %collective-permute-done.5.refs_2_, f32[24,128]{1,0:T(8,128)S(1)} %collective-permute-done.6.refs_3_, ...), custom_call_target="tpu_custom_call" | custom-call | flops 50000000 | bytes 600000 | tf_op jit(solution)/shard_map/pallas_call | solution.py:405
  15.9 0.0 copy-start
  15.9 0.2 collective-permute-start.11
  16.1 3.2 %collective-permute-start.10 = (f32[24,128]{1,0:T(8,128)S(1)}, f32[24,128]{1,0:T(8,128)S(1)}, u32[]{:S(2)}, u32[]{:S(2)}) collective-permute-start(f32[24,128]{1,0:T(8,128)S(1)} %shard_map.89.refs_0_.t1), channel_id=1, source_target_pairs={{0,8},{1,9},{2,10},{3,11},{4,12},{5,13},{6,14},{7,15},{8,0},{9,1},... | collective-permute-start | bytes 36872 | tf_op jit(solution)/shard_map/ppermute | solution.py:317
  19.3 0.4 collective-permute-start.9
  19.7 0.0 collective-permute-start.8
  19.7 0.0 collective-permute-done.11.refs_4_
  19.7 1.4 %collective-permute-done.10.refs_3_ = f32[24,128]{1,0:T(8,128)S(1)} collective-permute-done((f32[24,128]{1,0:T(8,128)S(1)}, f32[24,128]{1,0:T(8,128)S(1)}, u32[]{:S(2)}, u32[]{:S(2)}) %collective-permute-start.10) | collective-permute-done | bytes 12320 | tf_op jit(solution)/shard_map/ppermute | solution.py:317
  21.1 1.3 %collective-permute-done.9.refs_2_ = f32[24,128]{1,0:T(8,128)S(1)} collective-permute-done((f32[24,128]{1,0:T(8,128)S(1)}, f32[24,128]{1,0:T(8,128)S(1)}, u32[]{:S(2)}, u32[]{:S(2)}) %collective-permute-start.9) | collective-permute-done | bytes 12320 | tf_op jit(solution)/shard_map/ppermute | solution.py:317
  22.4 0.0 collective-permute-done.8.refs_1_
  22.4 0.4 %shard_map.90.t2.own = f32[24,128]{1,0:T(8,128)S(1)} custom-call(f32[24,128]{1,0:T(8,128)S(1)} %shard_map.89.refs_0_.t1, f32[24,128]{1,0:T(8,128)S(1)} %collective-permute-done.8.refs_1_, f32[24,128]{1,0:T(8,128)S(1)} %collective-permute-done.9.refs_2_, f32[24,128]{1,0:T(8,128)S(1)} %collective-permute-done.10.refs_3_, ...), custom_call_target="tpu_custom_call" | custom-call | flops 50000000 | bytes 600000 | tf_op jit(solution)/shard_map/pallas_call | solution.py:405
  22.8 0.0 collective-permute-start.15
  22.8 1.8 %collective-permute-start.14 = (f32[24,128]{1,0:T(8,128)S(1)}, f32[24,128]{1,0:T(8,128)S(1)}, u32[]{:S(2)}, u32[]{:S(2)}) collective-permute-start(f32[24,128]{1,0:T(8,128)S(1)} %shard_map.90.t2.own), channel_id=1, source_target_pairs={{0,8},{1,9},{2,10},{3,11},{4,12},{5,13},{6,14},{7,15},{8,0},{9,1},... | collective-permute-start | bytes 36872 | tf_op jit(solution)/shard_map/ppermute | solution.py:317
  24.6 1.2 %collective-permute-start.13 = (f32[24,128]{1,0:T(8,128)S(1)}, f32[24,128]{1,0:T(8,128)S(1)}, u32[]{:S(2)}, u32[]{:S(2)}) collective-permute-start(f32[24,128]{1,0:T(8,128)S(1)} %shard_map.90.t2.own), channel_id=1, source_target_pairs={{0,3},{1,2},{2,1},{3,0},{4,5},{5,4},{6,7},{7,6},{8,16},{9,17},{10,... | collective-permute-start | bytes 36872 | tf_op jit(solution)/shard_map/ppermute | solution.py:317
  25.9 0.0 collective-permute-start.12
  25.9 0.0 copy-done
  25.9 0.5 %shard_map.91 = (f32[24,512]{1,0:T(8,128)S(1)}, f32[40,128]{1,0:T(8,128)S(1)}, bf16[512,128]{1,0:T(8,128)(2,1)S(1)}, bf16[512,128]{1,0:T(8,128)(2,1)S(1)}, bf16[512,128]{1,0:T(8,128)(2,1)S(1)}) custom-call(f32[3,32,512]{2,1,0:T(8,128)S(1)} %copy-done, f32[24,128]{1,0:T(8,128)S(1)} %get-tuple-element.19.refs_0_.t0, f32[24,128]{1,0:T(8,128)S(1)} %shard_map.89.refs_0_.t1, ...), custom_call_target="tpu_custom_call" | custom-call | flops 60000000 | bytes 250000 | tf_op jit(solution)/shard_map/pallas_call | solution.py:411
  26.4 0.1 collective-permute-done.15.d
  26.5 0.1 collective-permute-done.14.c
  26.6 1.2 %collective-permute-done.13.b = f32[24,128]{1,0:T(8,128)S(1)} collective-permute-done((f32[24,128]{1,0:T(8,128)S(1)}, f32[24,128]{1,0:T(8,128)S(1)}, u32[]{:S(2)}, u32[]{:S(2)}) %collective-permute-start.13) | collective-permute-done | bytes 12320 | tf_op jit(solution)/shard_map/ppermute | solution.py:317
  27.7 0.0 collective-permute-done.12.a
  27.7 0.6 %shard_map.92 = (f32[8,512]{1,0:T(8,128)S(1)}, f32[40,128]{1,0:T(8,128)S(1)}) custom-call(f32[24,128]{1,0:T(8,128)S(1)} %shard_map.90.t2.own, f32[24,128]{1,0:T(8,128)S(1)} %collective-permute-done.12.a, f32[24,128]{1,0:T(8,128)S(1)} %collective-permute-done.13.b, f32[24,128]{1,0:T(8,128)S(1)} %collective-permute-done.14.c, ...), custom_call_target="tpu_custom_call" | custom-call | flops 80000000 | bytes 900000 | tf_op jit(solution)/shard_map/pallas_call | solution.py:418
  28.4 0.1 collective-permute-start.16
  28.4 1.2 %collective-permute-done.16 = f32[40,128]{1,0:T(8,128)S(1)} collective-permute-done((f32[40,128]{1,0:T(8,128)S(1)}, f32[40,128]{1,0:T(8,128)S(1)}, u32[]{:S(2)}, u32[]{:S(2)}) %collective-permute-start.16) | collective-permute-done | bytes 20512 | tf_op jit(solution)/shard_map/ppermute | solution.py:317
  29.6 1.0 %collective-permute-start.19 = (f32[40,128]{1,0:T(8,128)S(1)}, f32[40,128]{1,0:T(8,128)S(1)}, u32[]{:S(2)}, u32[]{:S(2)}) collective-permute-start(f32[40,128]{1,0:T(8,128)S(1)} %add.21), channel_id=1, source_target_pairs={{0,7},{1,6},{2,5},{3,4},{4,3},{5,2},{6,1},{7,0},{8,15},{9,14},{10,... | collective-permute-start | bytes 61448 | tf_op jit(solution)/shard_map/ppermute | solution.py:317
  30.6 1.5 %collective-permute-start.18 = (f32[40,128]{1,0:T(8,128)S(1)}, f32[40,128]{1,0:T(8,128)S(1)}, u32[]{:S(2)}, u32[]{:S(2)}) collective-permute-start(f32[40,128]{1,0:T(8,128)S(1)} %add.21), channel_id=1, source_target_pairs={{0,5},{1,4},{2,7},{3,6},{4,1},{5,0},{6,3},{7,2},{8,13},{9,12},{10,... | collective-permute-start | bytes 61448 | tf_op jit(solution)/shard_map/ppermute | solution.py:317
  32.1 0.5 %collective-permute-start.17 = (f32[40,128]{1,0:T(8,128)S(1)}, f32[40,128]{1,0:T(8,128)S(1)}, u32[]{:S(2)}, u32[]{:S(2)}) collective-permute-start(f32[40,128]{1,0:T(8,128)S(1)} %add.21), channel_id=1, source_target_pairs={{0,3},{1,2},{2,1},{3,0},{4,7},{5,6},{6,5},{7,4},{8,11},{9,10},{10,... | collective-permute-start | bytes 61448 | tf_op jit(solution)/shard_map/ppermute | solution.py:317
  32.6 1.1 %collective-permute-done.19 = f32[40,128]{1,0:T(8,128)S(1)} collective-permute-done((f32[40,128]{1,0:T(8,128)S(1)}, f32[40,128]{1,0:T(8,128)S(1)}, u32[]{:S(2)}, u32[]{:S(2)}) %collective-permute-start.19) | collective-permute-done | bytes 20512 | tf_op jit(solution)/shard_map/ppermute | solution.py:317
  33.7 0.5 %collective-permute-done.18 = f32[40,128]{1,0:T(8,128)S(1)} collective-permute-done((f32[40,128]{1,0:T(8,128)S(1)}, f32[40,128]{1,0:T(8,128)S(1)}, u32[]{:S(2)}, u32[]{:S(2)}) %collective-permute-start.18) | collective-permute-done | bytes 20512 | tf_op jit(solution)/shard_map/ppermute | solution.py:317
  34.2 1.1 %collective-permute-done.17 = f32[40,128]{1,0:T(8,128)S(1)} collective-permute-done((f32[40,128]{1,0:T(8,128)S(1)}, f32[40,128]{1,0:T(8,128)S(1)}, u32[]{:S(2)}, u32[]{:S(2)}) %collective-permute-start.17) | collective-permute-done | bytes 20512 | tf_op jit(solution)/shard_map/ppermute | solution.py:317
  35.3 1.1 %collective-permute-start.22 = (f32[40,128]{1,0:T(8,128)S(1)}, f32[40,128]{1,0:T(8,128)S(1)}, u32[]{:S(2)}, u32[]{:S(2)}) collective-permute-start(f32[40,128]{1,0:T(8,128)S(1)} %add_add_fusion.1), channel_id=1, source_target_pairs={{0,25},{1,24},{2,27},{3,26},{4,29},{5,28},{6,31},{7,30},{8,17},{9,... | collective-permute-start | bytes 61448 | tf_op jit(solution)/shard_map/ppermute | solution.py:317
  36.4 1.7 %collective-permute-start.21 = (f32[40,128]{1,0:T(8,128)S(1)}, f32[40,128]{1,0:T(8,128)S(1)}, u32[]{:S(2)}, u32[]{:S(2)}) collective-permute-start(f32[40,128]{1,0:T(8,128)S(1)} %add_add_fusion.1), channel_id=1, source_target_pairs={{0,17},{1,16},{2,19},{3,18},{4,21},{5,20},{6,23},{7,22},{8,25},{9,... | collective-permute-start | bytes 61448 | tf_op jit(solution)/shard_map/ppermute | solution.py:317
  38.1 1.3 %collective-permute-start.20 = (f32[40,128]{1,0:T(8,128)S(1)}, f32[40,128]{1,0:T(8,128)S(1)}, u32[]{:S(2)}, u32[]{:S(2)}) collective-permute-start(f32[40,128]{1,0:T(8,128)S(1)} %add_add_fusion.1), channel_id=1, source_target_pairs={{0,9},{1,8},{2,11},{3,10},{4,13},{5,12},{6,15},{7,14},{8,1},{9,0},... | collective-permute-start | bytes 61448 | tf_op jit(solution)/shard_map/ppermute | solution.py:317
  39.4 1.0 %collective-permute-done.22 = f32[40,128]{1,0:T(8,128)S(1)} collective-permute-done((f32[40,128]{1,0:T(8,128)S(1)}, f32[40,128]{1,0:T(8,128)S(1)}, u32[]{:S(2)}, u32[]{:S(2)}) %collective-permute-start.22) | collective-permute-done | bytes 20512 | tf_op jit(solution)/shard_map/ppermute | solution.py:317
  40.4 1.1 %collective-permute-done.21 = f32[40,128]{1,0:T(8,128)S(1)} collective-permute-done((f32[40,128]{1,0:T(8,128)S(1)}, f32[40,128]{1,0:T(8,128)S(1)}, u32[]{:S(2)}, u32[]{:S(2)}) %collective-permute-start.21) | collective-permute-done | bytes 20512 | tf_op jit(solution)/shard_map/ppermute | solution.py:317
  41.5 0.2 collective-permute-done.20
  41.7 0.9 %shard_map.93 = (f32[3,4,512]{2,1,0:T(4,128)}, f32[3,4,36]{2,1,0:T(4,128)}) custom-call(f32[40,128]{1,0:T(8,128)S(1)} %add_add_fusion.refs_0_, f32[3,32,512]{2,1,0:T(8,128)S(1)} %copy-done, f32[24,512]{1,0:T(8,128)S(1)} %get-tuple-element.26.refs_2_, f32[8,512]{1,0:T(8,128)S(1)} %get-tuple-element.27.refs_3_), custom_call_target="tpu_custom_call" | custom-call | flops 50000000 | bytes 400000 | tf_op jit(solution)/shard_map/pallas_call | solution.py:422
  (3 shorter events, 0.0 us)
Async XLA Ops:
  1.9 6.9 %collective-permute-start.3 = (f32[32,128]{1,0:T(8,128)S(1)}, f32[32,128]{1,0:T(8,128)S(1)}, u32[]{:S(2)}, u32[]{:S(2)}) collective-permute-start(f32[32,128]{1,0:T(8,128)S(1)} %shard_map.86.refs_0_), channel_id=1, source_target_pairs={{0,1},{1,2},{2,0},{3,4},{4,3},{5,6},{6,5},{7,8},{8,7},{9,10},{10,9... | collective-permute-start | bytes 49160 | tf_op jit(solution)/shard_map/ppermute | solution.py:317
  2.4 6.4 %collective-permute-start.2 = (f32[32,128]{1,0:T(8,128)S(1)}, f32[32,128]{1,0:T(8,128)S(1)}, u32[]{:S(2)}, u32[]{:S(2)}) collective-permute-start(f32[32,128]{1,0:T(8,128)S(1)} %shard_map.86.refs_0_), channel_id=1, source_target_pairs={{0,8},{1,9},{2,10},{3,11},{4,12},{5,13},{6,14},{7,15},{8,0},{9,1},... | collective-permute-start | bytes 49160 | tf_op jit(solution)/shard_map/ppermute | solution.py:317
  6.7 3.2 %collective-permute-start.1 = (f32[32,128]{1,0:T(8,128)S(1)}, f32[32,128]{1,0:T(8,128)S(1)}, u32[]{:S(2)}, u32[]{:S(2)}) collective-permute-start(f32[32,128]{1,0:T(8,128)S(1)} %shard_map.86.refs_0_), channel_id=1, source_target_pairs={{0,3},{1,2},{2,1},{3,0},{4,5},{5,4},{6,7},{7,6},{8,16},{9,17},{10,... | collective-permute-start | bytes 49160 | tf_op jit(solution)/shard_map/ppermute | solution.py:317
  7.4 2.5 %collective-permute-start = (f32[32,128]{1,0:T(8,128)S(1)}, f32[32,128]{1,0:T(8,128)S(1)}, u32[]{:S(2)}, u32[]{:S(2)}) collective-permute-start(f32[32,128]{1,0:T(8,128)S(1)} %shard_map.86.refs_0_), channel_id=1, source_target_pairs={{0,1},{1,0},{2,3},{3,2},{4,5},{5,4},{6,7},{7,6},{8,9},{9,8},{10,11... | collective-permute-start | bytes 49160 | tf_op jit(solution)/shard_map/ppermute | solution.py:317
  10.5 3.7 %collective-permute-start.7 = (f32[24,128]{1,0:T(8,128)S(1)}, f32[24,128]{1,0:T(8,128)S(1)}, u32[]{:S(2)}, u32[]{:S(2)}) collective-permute-start(f32[24,128]{1,0:T(8,128)S(1)} %get-tuple-element.19.refs_0_.t0), channel_id=1, source_target_pairs={{0,1},{1,2},{2,0},{3,4},{4,3},{5,6},{6,5},{7,8},{8,7},{9,10},{10,9... | collective-permute-start | bytes 36872 | tf_op jit(solution)/shard_map/ppermute | solution.py:317
  10.5 3.8 %collective-permute-start.6 = (f32[24,128]{1,0:T(8,128)S(1)}, f32[24,128]{1,0:T(8,128)S(1)}, u32[]{:S(2)}, u32[]{:S(2)}) collective-permute-start(f32[24,128]{1,0:T(8,128)S(1)} %get-tuple-element.19.refs_0_.t0), channel_id=1, source_target_pairs={{0,8},{1,9},{2,10},{3,11},{4,12},{5,13},{6,14},{7,15},{8,0},{9,1},... | collective-permute-start | bytes 36872 | tf_op jit(solution)/shard_map/ppermute | solution.py:317
  12.3 3.1 %collective-permute-start.5 = (f32[24,128]{1,0:T(8,128)S(1)}, f32[24,128]{1,0:T(8,128)S(1)}, u32[]{:S(2)}, u32[]{:S(2)}) collective-permute-start(f32[24,128]{1,0:T(8,128)S(1)} %get-tuple-element.19.refs_0_.t0), channel_id=1, source_target_pairs={{0,3},{1,2},{2,1},{3,0},{4,5},{5,4},{6,7},{7,6},{8,16},{9,17},{10,... | collective-permute-start | bytes 36872 | tf_op jit(solution)/shard_map/ppermute | solution.py:317
  13.7 1.8 %collective-permute-start.4 = (f32[24,128]{1,0:T(8,128)S(1)}, f32[24,128]{1,0:T(8,128)S(1)}, u32[]{:S(2)}, u32[]{:S(2)}) collective-permute-start(f32[24,128]{1,0:T(8,128)S(1)} %get-tuple-element.19.refs_0_.t0), channel_id=1, source_target_pairs={{0,1},{1,0},{2,3},{3,2},{4,5},{5,4},{6,7},{7,6},{8,9},{9,8},{10,11... | collective-permute-start | bytes 36872 | tf_op jit(solution)/shard_map/ppermute | solution.py:317
  15.9 10.0 %copy-start = (f32[3,32,512]{2,1,0:T(8,128)S(1)}, f32[3,32,512]{2,1,0:T(8,128)}, u32[]{:S(2)}) copy-start(f32[3,32,512]{2,1,0:T(8,128)} %refs_1_.1) | copy-start | bytes 589828
  15.9 3.8 %collective-permute-start.11 = (f32[24,128]{1,0:T(8,128)S(1)}, f32[24,128]{1,0:T(8,128)S(1)}, u32[]{:S(2)}, u32[]{:S(2)}) collective-permute-start(f32[24,128]{1,0:T(8,128)S(1)} %shard_map.89.refs_0_.t1), channel_id=1, source_target_pairs={{0,1},{1,2},{2,0},{3,4},{4,3},{5,6},{6,5},{7,8},{8,7},{9,10},{10,9... | collective-permute-start | bytes 36872 | tf_op jit(solution)/shard_map/ppermute | solution.py:317
  16.1 5.0 %collective-permute-start.10 = (f32[24,128]{1,0:T(8,128)S(1)}, f32[24,128]{1,0:T(8,128)S(1)}, u32[]{:S(2)}, u32[]{:S(2)}) collective-permute-start(f32[24,128]{1,0:T(8,128)S(1)} %shard_map.89.refs_0_.t1), channel_id=1, source_target_pairs={{0,8},{1,9},{2,10},{3,11},{4,12},{5,13},{6,14},{7,15},{8,0},{9,1},... | collective-permute-start | bytes 36872 | tf_op jit(solution)/shard_map/ppermute | solution.py:317
  19.3 3.1 %collective-permute-start.9 = (f32[24,128]{1,0:T(8,128)S(1)}, f32[24,128]{1,0:T(8,128)S(1)}, u32[]{:S(2)}, u32[]{:S(2)}) collective-permute-start(f32[24,128]{1,0:T(8,128)S(1)} %shard_map.89.refs_0_.t1), channel_id=1, source_target_pairs={{0,3},{1,2},{2,1},{3,0},{4,5},{5,4},{6,7},{7,6},{8,16},{9,17},{10,... | collective-permute-start | bytes 36872 | tf_op jit(solution)/shard_map/ppermute | solution.py:317
  19.7 2.7 %collective-permute-start.8 = (f32[24,128]{1,0:T(8,128)S(1)}, f32[24,128]{1,0:T(8,128)S(1)}, u32[]{:S(2)}, u32[]{:S(2)}) collective-permute-start(f32[24,128]{1,0:T(8,128)S(1)} %shard_map.89.refs_0_.t1), channel_id=1, source_target_pairs={{0,1},{1,0},{2,3},{3,2},{4,5},{5,4},{6,7},{7,6},{8,9},{9,8},{10,11... | collective-permute-start | bytes 36872 | tf_op jit(solution)/shard_map/ppermute | solution.py:317
  22.8 3.7 %collective-permute-start.15 = (f32[24,128]{1,0:T(8,128)S(1)}, f32[24,128]{1,0:T(8,128)S(1)}, u32[]{:S(2)}, u32[]{:S(2)}) collective-permute-start(f32[24,128]{1,0:T(8,128)S(1)} %shard_map.90.t2.own), channel_id=1, source_target_pairs={{0,1},{1,2},{2,0},{3,4},{4,3},{5,6},{6,5},{7,8},{8,7},{9,10},{10,9... | collective-permute-start | bytes 36872 | tf_op jit(solution)/shard_map/ppermute | solution.py:317
  22.8 3.8 %collective-permute-start.14 = (f32[24,128]{1,0:T(8,128)S(1)}, f32[24,128]{1,0:T(8,128)S(1)}, u32[]{:S(2)}, u32[]{:S(2)}) collective-permute-start(f32[24,128]{1,0:T(8,128)S(1)} %shard_map.90.t2.own), channel_id=1, source_target_pairs={{0,8},{1,9},{2,10},{3,11},{4,12},{5,13},{6,14},{7,15},{8,0},{9,1},... | collective-permute-start | bytes 36872 | tf_op jit(solution)/shard_map/ppermute | solution.py:317
  24.6 3.1 %collective-permute-start.13 = (f32[24,128]{1,0:T(8,128)S(1)}, f32[24,128]{1,0:T(8,128)S(1)}, u32[]{:S(2)}, u32[]{:S(2)}) collective-permute-start(f32[24,128]{1,0:T(8,128)S(1)} %shard_map.90.t2.own), channel_id=1, source_target_pairs={{0,3},{1,2},{2,1},{3,0},{4,5},{5,4},{6,7},{7,6},{8,16},{9,17},{10,... | collective-permute-start | bytes 36872 | tf_op jit(solution)/shard_map/ppermute | solution.py:317
  25.9 1.9 %collective-permute-start.12 = (f32[24,128]{1,0:T(8,128)S(1)}, f32[24,128]{1,0:T(8,128)S(1)}, u32[]{:S(2)}, u32[]{:S(2)}) collective-permute-start(f32[24,128]{1,0:T(8,128)S(1)} %shard_map.90.t2.own), channel_id=1, source_target_pairs={{0,1},{1,0},{2,3},{3,2},{4,5},{5,4},{6,7},{7,6},{8,9},{9,8},{10,11... | collective-permute-start | bytes 36872 | tf_op jit(solution)/shard_map/ppermute | solution.py:317
  28.4 1.3 %collective-permute-start.16 = (f32[40,128]{1,0:T(8,128)S(1)}, f32[40,128]{1,0:T(8,128)S(1)}, u32[]{:S(2)}, u32[]{:S(2)}) collective-permute-start(f32[40,128]{1,0:T(8,128)S(1)} %get-tuple-element.25), channel_id=1, source_target_pairs={{0,1},{1,0},{2,3},{3,2},{4,5},{5,4},{6,7},{7,6},{8,9},{9,8},{10,11... | collective-permute-start | bytes 61448 | tf_op jit(solution)/shard_map/ppermute | solution.py:317
  29.6 4.1 %collective-permute-start.19 = (f32[40,128]{1,0:T(8,128)S(1)}, f32[40,128]{1,0:T(8,128)S(1)}, u32[]{:S(2)}, u32[]{:S(2)}) collective-permute-start(f32[40,128]{1,0:T(8,128)S(1)} %add.21), channel_id=1, source_target_pairs={{0,7},{1,6},{2,5},{3,4},{4,3},{5,2},{6,1},{7,0},{8,15},{9,14},{10,... | collective-permute-start | bytes 61448 | tf_op jit(solution)/shard_map/ppermute | solution.py:317
  30.6 3.6 %collective-permute-start.18 = (f32[40,128]{1,0:T(8,128)S(1)}, f32[40,128]{1,0:T(8,128)S(1)}, u32[]{:S(2)}, u32[]{:S(2)}) collective-permute-start(f32[40,128]{1,0:T(8,128)S(1)} %add.21), channel_id=1, source_target_pairs={{0,5},{1,4},{2,7},{3,6},{4,1},{5,0},{6,3},{7,2},{8,13},{9,12},{10,... | collective-permute-start | bytes 61448 | tf_op jit(solution)/shard_map/ppermute | solution.py:317
  32.1 3.2 %collective-permute-start.17 = (f32[40,128]{1,0:T(8,128)S(1)}, f32[40,128]{1,0:T(8,128)S(1)}, u32[]{:S(2)}, u32[]{:S(2)}) collective-permute-start(f32[40,128]{1,0:T(8,128)S(1)} %add.21), channel_id=1, source_target_pairs={{0,3},{1,2},{2,1},{3,0},{4,7},{5,6},{6,5},{7,4},{8,11},{9,10},{10,... | collective-permute-start | bytes 61448 | tf_op jit(solution)/shard_map/ppermute | solution.py:317
  35.3 5.1 %collective-permute-start.22 = (f32[40,128]{1,0:T(8,128)S(1)}, f32[40,128]{1,0:T(8,128)S(1)}, u32[]{:S(2)}, u32[]{:S(2)}) collective-permute-start(f32[40,128]{1,0:T(8,128)S(1)} %add_add_fusion.1), channel_id=1, source_target_pairs={{0,25},{1,24},{2,27},{3,26},{4,29},{5,28},{6,31},{7,30},{8,17},{9,... | collective-permute-start | bytes 61448 | tf_op jit(solution)/shard_map/ppermute | solution.py:317
  36.4 5.1 %collective-permute-start.21 = (f32[40,128]{1,0:T(8,128)S(1)}, f32[40,128]{1,0:T(8,128)S(1)}, u32[]{:S(2)}, u32[]{:S(2)}) collective-permute-start(f32[40,128]{1,0:T(8,128)S(1)} %add_add_fusion.1), channel_id=1, source_target_pairs={{0,17},{1,16},{2,19},{3,18},{4,21},{5,20},{6,23},{7,22},{8,25},{9,... | collective-permute-start | bytes 61448 | tf_op jit(solution)/shard_map/ppermute | solution.py:317
  38.1 3.6 %collective-permute-start.20 = (f32[40,128]{1,0:T(8,128)S(1)}, f32[40,128]{1,0:T(8,128)S(1)}, u32[]{:S(2)}, u32[]{:S(2)}) collective-permute-start(f32[40,128]{1,0:T(8,128)S(1)} %add_add_fusion.1), channel_id=1, source_target_pairs={{0,9},{1,8},{2,11},{3,10},{4,13},{5,12},{6,15},{7,14},{8,1},{9,0},... | collective-permute-start | bytes 61448 | tf_op jit(solution)/shard_map/ppermute | solution.py:317

commit v7 on v6

--- a/solution.py
+++ b/solution.py
@@ -67,8 +67,11 @@
     for copy in copies[1:]:
         copy.wait()
     comps, vecs, rows = prev_ref.shape
-    mix = jnp.concatenate([mix_ref[...]] * comps, axis=1)
-    mix = jnp.where(iota(mix.shape, 1) // vecs == iota(mix.shape, 0), mix, 0.0)
+    eye = iota((vecs, vecs), 0) == iota((vecs, vecs), 1)
+    weights = []
+    for c in range(comps):
+        line = jnp.broadcast_to(mix_ref[c : c + 1, :], eye.shape)
+        weights.append(jnp.sum(jnp.where(eye, line, 0.0), axis=1, keepdims=True))
     order = list_ref[0].astype(jnp.float32)
     order = jnp.concatenate([order, jnp.zeros((4, 120), jnp.float32)], axis=1)
     meta = jnp.zeros((8, 128), jnp.float32)
@@ -80,10 +83,10 @@
         meta = jnp.where(iota((8, 128), 1) // 8 == link + 1, line, meta)
     out_ref[8 * comps :, :] = meta
     copies[0].wait()
-    start = dot(mix, prev_ref[...].reshape(comps * vecs, rows), precision=HIGHEST)
     own = own_lanes(8, rows)
     for c in range(comps):
-        line = jnp.broadcast_to(start[c : c + 1], own.shape)
+        start = jnp.sum(weights[c] * prev_ref[c], axis=0, keepdims=True)
+        line = jnp.broadcast_to(start, own.shape)
         out_ref[c * 8 : (c + 1) * 8, :] = fold(jnp.where(own, line, 0.0))
 
 
@@ -136,36 +139,24 @@
         jnp.sum(jnp.where(lane == table[:, k : k + 1], target, 0.0), axis=1, keepdims=True)
         for k in range(4)
     ]
-    lane = iota((8, 256), 1).astype(jnp.float32)
-    groups = []
-    for pair in range(2):
-        for c in range(COMPS):
-            first = lane == at[2 * pair] + float(8 * c)
-            second = lane == at[2 * pair + 1] + float(8 * c + 120)
-            groups.append((first | second).astype(jnp.float32))
-    return jnp.concatenate(groups, axis=0)
+    groups = [(lane == at[k] + float(8 * c)).astype(jnp.float32) for k in range(4) for c in range(COMPS)]
+    return jnp.concatenate(groups, axis=0).astype(jnp.bfloat16)
 
 
 def multiply(choose, pieces, shift, high, low):
     rows = 8 * COMPS
-    ext = jnp.concatenate(pieces, axis=0)
-    front = iota(ext.shape, 1) < BLOCK
+    ext = jnp.concatenate(pieces + [jnp.zeros((128 - 5 * rows, 128), jnp.float32)], axis=0)
     top = ext.astype(jnp.bfloat16).astype(jnp.float32)
-    rest = ext - top
-    zero = jnp.zeros_like(ext)
-    picked = jnp.concatenate(
-        [
-            jnp.concatenate([jnp.where(front, top, zero), jnp.where(front, rest, zero)], axis=1),
-            jnp.concatenate([jnp.where(front, zero, top), jnp.where(front, zero, rest)], axis=1),
-            jnp.zeros((256 - 2 * ext.shape[0], 256), jnp.float32),
-        ],
-        axis=0,
-    ).astype(jnp.bfloat16)
-    x = dot(choose.astype(jnp.bfloat16), picked)
+    x = dot(choose, jnp.concatenate([top, ext - top], axis=1).astype(jnp.bfloat16))
+    front = iota((rows, 256), 1) % 128 < BLOCK
+    pairs = [
+        jnp.where(front, x[2 * t * rows : (2 * t + 1) * rows], x[(2 * t + 1) * rows : (2 * t + 2) * rows])
+        for t in range(2)
+    ]
     left = jnp.concatenate(
         [
-            jnp.concatenate([x[:rows, :128], x[rows:, :128]], axis=1),
-            jnp.concatenate([x[:rows, 128:], x[rows:, 128:]], axis=1),
+            jnp.concatenate([pair[:, half * 128 : (half + 1) * 128] for pair in pairs], axis=1)
+            for half in range(2)
         ],
         axis=0,
     ).astype(jnp.bfloat16)
@@ -395,7 +386,7 @@
     length = lax.axis_size("dom")
     tile, choose = call(
         lambda *refs: first_kernel(length, *refs),
-        [tile_out, ((2 * comps * blocks, 256), f32)],
+        [tile_out, ((4 * comps * blocks, 128), bf16)],
         [VMEM] * 8,
         50000000,
         600000,

time: 42.8 us -> 42.5 us (level)
  no operation moved by 1% of the time
where the time goes in v7:
time: 42.5 us; the launch traced here: 42.4 us
  starting transfers between devices  23.2 us (55%)
  waiting for transfers between devices  12.6 us (30%)
  Pallas kernels  5.84 us (14%)
  between operations  0.72 us (2%)
    ppermute x23, starting transfers between devices, send(): lax.ppermute(value, 'dom', [(d, target[d]) for d in range(lax.axis_size('...  23.2 us
    ppermute x23, waiting for transfers between devices, send(): lax.ppermute(value, 'dom', [(d, target[d]) for d in range(lax.axis_size('...  12.6 us
    pallas_call x1, Pallas kernels, local(): call(prepare_kernel, [((width, rows), bf16), ((width, rows), bf16), ((8 *...  1.39 us
    pallas_call x1, Pallas kernels, local(): call(start_kernel, [((comps * blocks + 8, 128), f32)], [HBM] * 4, 600000,...  1.08 us
    pallas_call x1, Pallas kernels, local(): call(lambda *refs: finish_kernel(total, *refs), [((comps, S, rows), f32),...  0.95 us
  transfers between devices with their start and end apart: 23, of which 15 were waited for; matrix products, arithmetic and copies ran while one was open for 0% of the time, Pallas kernels for 4%

profile of v7, /device:TPU:0, one launch (start us, length us, event | category | flops | bytes accessed | tf_op | source)
XLA Modules:
  0.0 42.4 jit_solution(4321533947921622594)
XLA Ops:
  0.6 1.1 %shard_map.86.refs_0_ = f32[32,128]{1,0:T(8,128)S(1)} custom-call(f32[3,32,512]{2,1,0:T(8,128)} %refs_1_.1, f32[3,32]{1,0:T(4,128)} %mix_in.1, s32[1,4,8]{2,1,0:T(4,128)} %list_in.1, s32[1,4]{1,0:T(1,128)} %count_in.1), custom_call_target="tpu_custom_call" | custom-call | flops 600000 | bytes 250000 | tf_op jit(solution)/shard_map/pallas_call | solution.py:358
  1.7 0.5 %collective-permute-start.3 = (f32[32,128]{1,0:T(8,128)S(1)}, f32[32,128]{1,0:T(8,128)S(1)}, u32[]{:S(2)}, u32[]{:S(2)}) collective-permute-start(f32[32,128]{1,0:T(8,128)S(1)} %shard_map.86.refs_0_), channel_id=1, source_target_pairs={{0,1},{1,2},{2,0},{3,4},{4,3},{5,6},{6,5},{7,8},{8,7},{9,10},{10,9... | collective-permute-start | bytes 49160 | tf_op jit(solution)/shard_map/ppermute | solution.py:308
  2.2 4.3 %collective-permute-start.2 = (f32[32,128]{1,0:T(8,128)S(1)}, f32[32,128]{1,0:T(8,128)S(1)}, u32[]{:S(2)}, u32[]{:S(2)}) collective-permute-start(f32[32,128]{1,0:T(8,128)S(1)} %shard_map.86.refs_0_), channel_id=1, source_target_pairs={{0,8},{1,9},{2,10},{3,11},{4,12},{5,13},{6,14},{7,15},{8,0},{9,1},... | collective-permute-start | bytes 49160 | tf_op jit(solution)/shard_map/ppermute | solution.py:308
  6.6 0.7 %collective-permute-start.1 = (f32[32,128]{1,0:T(8,128)S(1)}, f32[32,128]{1,0:T(8,128)S(1)}, u32[]{:S(2)}, u32[]{:S(2)}) collective-permute-start(f32[32,128]{1,0:T(8,128)S(1)} %shard_map.86.refs_0_), channel_id=1, source_target_pairs={{0,3},{1,2},{2,1},{3,0},{4,5},{5,4},{6,7},{7,6},{8,16},{9,17},{10,... | collective-permute-start | bytes 49160 | tf_op jit(solution)/shard_map/ppermute | solution.py:308
  7.2 0.0 collective-permute-start
  7.2 1.4 %shard_map.87 = (bf16[256,512]{1,0:T(8,128)(2,1)S(1)}, bf16[256,512]{1,0:T(8,128)(2,1)S(1)}, f32[40,128]{1,0:T(8,128)S(1)}) custom-call(f32[512,256]{1,0:T(8,128)} %strips_in.1, s32[4,8]{1,0:T(4,128)} %bitcast.2, f32[4]{0:T(128)} %shifts_in.1), custom_call_target="tpu_custom_call" | custom-call | flops 1000000 | bytes 1000000 | tf_op jit(solution)/shard_map/pallas_call | solution.py:372
  8.6 0.0 collective-permute-done.3.refs_4_
  8.6 0.0 collective-permute-done.2.refs_3_
  8.6 1.1 %collective-permute-done.1.refs_2_ = f32[32,128]{1,0:T(8,128)S(1)} collective-permute-done((f32[32,128]{1,0:T(8,128)S(1)}, f32[32,128]{1,0:T(8,128)S(1)}, u32[]{:S(2)}, u32[]{:S(2)}) %collective-permute-start.1) | collective-permute-done | bytes 16416 | tf_op jit(solution)/shard_map/ppermute | solution.py:308
  9.7 0.0 collective-permute-done.refs_1_
  9.7 0.5 %shard_map.88 = (f32[24,128]{1,0:T(8,128)S(1)}, bf16[96,128]{1,0:T(8,128)(2,1)S(1)}) custom-call(f32[32,128]{1,0:T(8,128)S(1)} %shard_map.86.refs_0_, f32[32,128]{1,0:T(8,128)S(1)} %collective-permute-done.refs_1_, f32[32,128]{1,0:T(8,128)S(1)} %collective-permute-done.1.refs_2_, f32[32,128]{1,0:T(8,128)S(1)} %collective-permute-done.2.refs_3_, ...), custom_call_target="tpu_custom_call" | custom-call | flops 50000000 | bytes 600000 | tf_op jit(solution)/shard_map/pallas_call | solution.py:387
  10.3 0.0 collective-permute-start.7
  10.3 1.9 %collective-permute-start.6 = (f32[24,128]{1,0:T(8,128)S(1)}, f32[24,128]{1,0:T(8,128)S(1)}, u32[]{:S(2)}, u32[]{:S(2)}) collective-permute-start(f32[24,128]{1,0:T(8,128)S(1)} %get-tuple-element.19.refs_0_.t0), channel_id=1, source_target_pairs={{0,8},{1,9},{2,10},{3,11},{4,12},{5,13},{6,14},{7,15},{8,0},{9,1},... | collective-permute-start | bytes 36872 | tf_op jit(solution)/shard_map/ppermute | solution.py:308
  12.1 1.4 %collective-permute-start.5 = (f32[24,128]{1,0:T(8,128)S(1)}, f32[24,128]{1,0:T(8,128)S(1)}, u32[]{:S(2)}, u32[]{:S(2)}) collective-permute-start(f32[24,128]{1,0:T(8,128)S(1)} %get-tuple-element.19.refs_0_.t0), channel_id=1, source_target_pairs={{0,3},{1,2},{2,1},{3,0},{4,5},{5,4},{6,7},{7,6},{8,16},{9,17},{10,... | collective-permute-start | bytes 36872 | tf_op jit(solution)/shard_map/ppermute | solution.py:308
  13.5 0.5 %collective-permute-start.4 = (f32[24,128]{1,0:T(8,128)S(1)}, f32[24,128]{1,0:T(8,128)S(1)}, u32[]{:S(2)}, u32[]{:S(2)}) collective-permute-start(f32[24,128]{1,0:T(8,128)S(1)} %get-tuple-element.19.refs_0_.t0), channel_id=1, source_target_pairs={{0,1},{1,0},{2,3},{3,2},{4,5},{5,4},{6,7},{7,6},{8,9},{9,8},{10,11... | collective-permute-start | bytes 36872 | tf_op jit(solution)/shard_map/ppermute | solution.py:308
  13.9 0.0 collective-permute-done.7.refs_4_
  14.0 0.1 collective-permute-done.6.refs_3_
  14.0 1.2 %collective-permute-done.5.refs_2_ = f32[24,128]{1,0:T(8,128)S(1)} collective-permute-done((f32[24,128]{1,0:T(8,128)S(1)}, f32[24,128]{1,0:T(8,128)S(1)}, u32[]{:S(2)}, u32[]{:S(2)}) %collective-permute-start.5) | collective-permute-done | bytes 12320 | tf_op jit(solution)/shard_map/ppermute | solution.py:308
  15.2 0.0 collective-permute-done.4.refs_1_
  15.2 0.4 shard_map.89.refs_0_.t1
  15.6 0.0 copy-start
  15.6 0.2 collective-permute-start.11
  15.8 3.2 %collective-permute-start.10 = (f32[24,128]{1,0:T(8,128)S(1)}, f32[24,128]{1,0:T(8,128)S(1)}, u32[]{:S(2)}, u32[]{:S(2)}) collective-permute-start(f32[24,128]{1,0:T(8,128)S(1)} %shard_map.89.refs_0_.t1), channel_id=1, source_target_pairs={{0,8},{1,9},{2,10},{3,11},{4,12},{5,13},{6,14},{7,15},{8,0},{9,1},... | collective-permute-start | bytes 36872 | tf_op jit(solution)/shard_map/ppermute | solution.py:308
  19.0 0.4 collective-permute-start.9
  19.4 0.0 collective-permute-start.8
  19.4 0.0 collective-permute-done.11.refs_4_
  19.4 1.4 %collective-permute-done.10.refs_3_ = f32[24,128]{1,0:T(8,128)S(1)} collective-permute-done((f32[24,128]{1,0:T(8,128)S(1)}, f32[24,128]{1,0:T(8,128)S(1)}, u32[]{:S(2)}, u32[]{:S(2)}) %collective-permute-start.10) | collective-permute-done | bytes 12320 | tf_op jit(solution)/shard_map/ppermute | solution.py:308
  20.8 1.3 %collective-permute-done.9.refs_2_ = f32[24,128]{1,0:T(8,128)S(1)} collective-permute-done((f32[24,128]{1,0:T(8,128)S(1)}, f32[24,128]{1,0:T(8,128)S(1)}, u32[]{:S(2)}, u32[]{:S(2)}) %collective-permute-start.9) | collective-permute-done | bytes 12320 | tf_op jit(solution)/shard_map/ppermute | solution.py:308
  22.1 0.0 collective-permute-done.8.refs_1_
  22.1 0.4 shard_map.90.t2.own
  22.5 0.0 collective-permute-start.15
  22.5 1.8 %collective-permute-start.14 = (f32[24,128]{1,0:T(8,128)S(1)}, f32[24,128]{1,0:T(8,128)S(1)}, u32[]{:S(2)}, u32[]{:S(2)}) collective-permute-start(f32[24,128]{1,0:T(8,128)S(1)} %shard_map.90.t2.own), channel_id=1, source_target_pairs={{0,8},{1,9},{2,10},{3,11},{4,12},{5,13},{6,14},{7,15},{8,0},{9,1},... | collective-permute-start | bytes 36872 | tf_op jit(solution)/shard_map/ppermute | solution.py:308
  24.4 1.2 %collective-permute-start.13 = (f32[24,128]{1,0:T(8,128)S(1)}, f32[24,128]{1,0:T(8,128)S(1)}, u32[]{:S(2)}, u32[]{:S(2)}) collective-permute-start(f32[24,128]{1,0:T(8,128)S(1)} %shard_map.90.t2.own), channel_id=1, source_target_pairs={{0,3},{1,2},{2,1},{3,0},{4,5},{5,4},{6,7},{7,6},{8,16},{9,17},{10,... | collective-permute-start | bytes 36872 | tf_op jit(solution)/shard_map/ppermute | solution.py:308
  25.6 0.0 collective-permute-start.12
  25.6 0.0 copy-done
  25.6 0.5 %shard_map.91 = (f32[24,512]{1,0:T(8,128)S(1)}, f32[40,128]{1,0:T(8,128)S(1)}, bf16[512,128]{1,0:T(8,128)(2,1)S(1)}, bf16[512,128]{1,0:T(8,128)(2,1)S(1)}, bf16[512,128]{1,0:T(8,128)(2,1)S(1)}) custom-call(f32[3,32,512]{2,1,0:T(8,128)S(1)} %copy-done, f32[24,128]{1,0:T(8,128)S(1)} %get-tuple-element.19.refs_0_.t0, f32[24,128]{1,0:T(8,128)S(1)} %shard_map.89.refs_0_.t1, ...), custom_call_target="tpu_custom_call" | custom-call | flops 60000000 | bytes 250000 | tf_op jit(solution)/shard_map/pallas_call | solution.py:402
  26.1 0.1 collective-permute-done.15.d
  26.2 0.1 collective-permute-done.14.c
  26.3 1.2 %collective-permute-done.13.b = f32[24,128]{1,0:T(8,128)S(1)} collective-permute-done((f32[24,128]{1,0:T(8,128)S(1)}, f32[24,128]{1,0:T(8,128)S(1)}, u32[]{:S(2)}, u32[]{:S(2)}) %collective-permute-start.13) | collective-permute-done | bytes 12320 | tf_op jit(solution)/shard_map/ppermute | solution.py:308
  27.5 0.0 collective-permute-done.12.a
  27.5 0.6 %shard_map.92 = (f32[8,512]{1,0:T(8,128)S(1)}, f32[40,128]{1,0:T(8,128)S(1)}) custom-call(f32[24,128]{1,0:T(8,128)S(1)} %shard_map.90.t2.own, f32[24,128]{1,0:T(8,128)S(1)} %collective-permute-done.12.a, f32[24,128]{1,0:T(8,128)S(1)} %collective-permute-done.13.b, f32[24,128]{1,0:T(8,128)S(1)} %collective-permute-done.14.c, ...), custom_call_target="tpu_custom_call" | custom-call | flops 80000000 | bytes 900000 | tf_op jit(solution)/shard_map/pallas_call | solution.py:409
  28.1 0.1 collective-permute-start.16
  28.2 1.2 %collective-permute-done.16 = f32[40,128]{1,0:T(8,128)S(1)} collective-permute-done((f32[40,128]{1,0:T(8,128)S(1)}, f32[40,128]{1,0:T(8,128)S(1)}, u32[]{:S(2)}, u32[]{:S(2)}) %collective-permute-start.16) | collective-permute-done | bytes 20512 | tf_op jit(solution)/shard_map/ppermute | solution.py:308
  29.3 1.0 %collective-permute-start.19 = (f32[40,128]{1,0:T(8,128)S(1)}, f32[40,128]{1,0:T(8,128)S(1)}, u32[]{:S(2)}, u32[]{:S(2)}) collective-permute-start(f32[40,128]{1,0:T(8,128)S(1)} %add.21), channel_id=1, source_target_pairs={{0,7},{1,6},{2,5},{3,4},{4,3},{5,2},{6,1},{7,0},{8,15},{9,14},{10,... | collective-permute-start | bytes 61448 | tf_op jit(solution)/shard_map/ppermute | solution.py:308
  30.4 1.5 %collective-permute-start.18 = (f32[40,128]{1,0:T(8,128)S(1)}, f32[40,128]{1,0:T(8,128)S(1)}, u32[]{:S(2)}, u32[]{:S(2)}) collective-permute-start(f32[40,128]{1,0:T(8,128)S(1)} %add.21), channel_id=1, source_target_pairs={{0,5},{1,4},{2,7},{3,6},{4,1},{5,0},{6,3},{7,2},{8,13},{9,12},{10,... | collective-permute-start | bytes 61448 | tf_op jit(solution)/shard_map/ppermute | solution.py:308
  31.8 0.5 %collective-permute-start.17 = (f32[40,128]{1,0:T(8,128)S(1)}, f32[40,128]{1,0:T(8,128)S(1)}, u32[]{:S(2)}, u32[]{:S(2)}) collective-permute-start(f32[40,128]{1,0:T(8,128)S(1)} %add.21), channel_id=1, source_target_pairs={{0,3},{1,2},{2,1},{3,0},{4,7},{5,6},{6,5},{7,4},{8,11},{9,10},{10,... | collective-permute-start | bytes 61448 | tf_op jit(solution)/shard_map/ppermute | solution.py:308
  32.3 1.1 %collective-permute-done.19 = f32[40,128]{1,0:T(8,128)S(1)} collective-permute-done((f32[40,128]{1,0:T(8,128)S(1)}, f32[40,128]{1,0:T(8,128)S(1)}, u32[]{:S(2)}, u32[]{:S(2)}) %collective-permute-start.19) | collective-permute-done | bytes 20512 | tf_op jit(solution)/shard_map/ppermute | solution.py:308
  33.5 0.4 %collective-permute-done.18 = f32[40,128]{1,0:T(8,128)S(1)} collective-permute-done((f32[40,128]{1,0:T(8,128)S(1)}, f32[40,128]{1,0:T(8,128)S(1)}, u32[]{:S(2)}, u32[]{:S(2)}) %collective-permute-start.18) | collective-permute-done | bytes 20512 | tf_op jit(solution)/shard_map/ppermute | solution.py:308
  33.9 1.1 %collective-permute-done.17 = f32[40,128]{1,0:T(8,128)S(1)} collective-permute-done((f32[40,128]{1,0:T(8,128)S(1)}, f32[40,128]{1,0:T(8,128)S(1)}, u32[]{:S(2)}, u32[]{:S(2)}) %collective-permute-start.17) | collective-permute-done | bytes 20512 | tf_op jit(solution)/shard_map/ppermute | solution.py:308
  35.0 1.1 %collective-permute-start.22 = (f32[40,128]{1,0:T(8,128)S(1)}, f32[40,128]{1,0:T(8,128)S(1)}, u32[]{:S(2)}, u32[]{:S(2)}) collective-permute-start(f32[40,128]{1,0:T(8,128)S(1)} %add_add_fusion.1), channel_id=1, source_target_pairs={{0,25},{1,24},{2,27},{3,26},{4,29},{5,28},{6,31},{7,30},{8,17},{9,... | collective-permute-start | bytes 61448 | tf_op jit(solution)/shard_map/ppermute | solution.py:308
  36.1 1.7 %collective-permute-start.21 = (f32[40,128]{1,0:T(8,128)S(1)}, f32[40,128]{1,0:T(8,128)S(1)}, u32[]{:S(2)}, u32[]{:S(2)}) collective-permute-start(f32[40,128]{1,0:T(8,128)S(1)} %add_add_fusion.1), channel_id=1, source_target_pairs={{0,17},{1,16},{2,19},{3,18},{4,21},{5,20},{6,23},{7,22},{8,25},{9,... | collective-permute-start | bytes 61448 | tf_op jit(solution)/shard_map/ppermute | solution.py:308
  37.8 1.3 %collective-permute-start.20 = (f32[40,128]{1,0:T(8,128)S(1)}, f32[40,128]{1,0:T(8,128)S(1)}, u32[]{:S(2)}, u32[]{:S(2)}) collective-permute-start(f32[40,128]{1,0:T(8,128)S(1)} %add_add_fusion.1), channel_id=1, source_target_pairs={{0,9},{1,8},{2,11},{3,10},{4,13},{5,12},{6,15},{7,14},{8,1},{9,0},... | collective-permute-start | bytes 61448 | tf_op jit(solution)/shard_map/ppermute | solution.py:308
  39.2 1.0 %collective-permute-done.22 = f32[40,128]{1,0:T(8,128)S(1)} collective-permute-done((f32[40,128]{1,0:T(8,128)S(1)}, f32[40,128]{1,0:T(8,128)S(1)}, u32[]{:S(2)}, u32[]{:S(2)}) %collective-permute-start.22) | collective-permute-done | bytes 20512 | tf_op jit(solution)/shard_map/ppermute | solution.py:308
  40.1 1.1 %collective-permute-done.21 = f32[40,128]{1,0:T(8,128)S(1)} collective-permute-done((f32[40,128]{1,0:T(8,128)S(1)}, f32[40,128]{1,0:T(8,128)S(1)}, u32[]{:S(2)}, u32[]{:S(2)}) %collective-permute-start.21) | collective-permute-done | bytes 20512 | tf_op jit(solution)/shard_map/ppermute | solution.py:308
  41.2 0.2 collective-permute-done.20
  41.4 0.9 %shard_map.93 = (f32[3,4,512]{2,1,0:T(4,128)}, f32[3,4,36]{2,1,0:T(4,128)}) custom-call(f32[40,128]{1,0:T(8,128)S(1)} %add_add_fusion.refs_0_, f32[3,32,512]{2,1,0:T(8,128)S(1)} %copy-done, f32[24,512]{1,0:T(8,128)S(1)} %get-tuple-element.26.refs_2_, f32[8,512]{1,0:T(8,128)S(1)} %get-tuple-element.27.refs_3_), custom_call_target="tpu_custom_call" | custom-call | flops 50000000 | bytes 400000 | tf_op jit(solution)/shard_map/pallas_call | solution.py:413
  (3 shorter events, 0.0 us)
Async XLA Ops:
  1.7 6.9 %collective-permute-start.3 = (f32[32,128]{1,0:T(8,128)S(1)}, f32[32,128]{1,0:T(8,128)S(1)}, u32[]{:S(2)}, u32[]{:S(2)}) collective-permute-start(f32[32,128]{1,0:T(8,128)S(1)} %shard_map.86.refs_0_), channel_id=1, source_target_pairs={{0,1},{1,2},{2,0},{3,4},{4,3},{5,6},{6,5},{7,8},{8,7},{9,10},{10,9... | collective-permute-start | bytes 49160 | tf_op jit(solution)/shard_map/ppermute | solution.py:308
  2.2 6.4 %collective-permute-start.2 = (f32[32,128]{1,0:T(8,128)S(1)}, f32[32,128]{1,0:T(8,128)S(1)}, u32[]{:S(2)}, u32[]{:S(2)}) collective-permute-start(f32[32,128]{1,0:T(8,128)S(1)} %shard_map.86.refs_0_), channel_id=1, source_target_pairs={{0,8},{1,9},{2,10},{3,11},{4,12},{5,13},{6,14},{7,15},{8,0},{9,1},... | collective-permute-start | bytes 49160 | tf_op jit(solution)/shard_map/ppermute | solution.py:308
  6.6 3.2 %collective-permute-start.1 = (f32[32,128]{1,0:T(8,128)S(1)}, f32[32,128]{1,0:T(8,128)S(1)}, u32[]{:S(2)}, u32[]{:S(2)}) collective-permute-start(f32[32,128]{1,0:T(8,128)S(1)} %shard_map.86.refs_0_), channel_id=1, source_target_pairs={{0,3},{1,2},{2,1},{3,0},{4,5},{5,4},{6,7},{7,6},{8,16},{9,17},{10,... | collective-permute-start | bytes 49160 | tf_op jit(solution)/shard_map/ppermute | solution.py:308
  7.2 2.5 %collective-permute-start = (f32[32,128]{1,0:T(8,128)S(1)}, f32[32,128]{1,0:T(8,128)S(1)}, u32[]{:S(2)}, u32[]{:S(2)}) collective-permute-start(f32[32,128]{1,0:T(8,128)S(1)} %shard_map.86.refs_0_), channel_id=1, source_target_pairs={{0,1},{1,0},{2,3},{3,2},{4,5},{5,4},{6,7},{7,6},{8,9},{9,8},{10,11... | collective-permute-start | bytes 49160 | tf_op jit(solution)/shard_map/ppermute | solution.py:308
  10.3 3.7 %collective-permute-start.7 = (f32[24,128]{1,0:T(8,128)S(1)}, f32[24,128]{1,0:T(8,128)S(1)}, u32[]{:S(2)}, u32[]{:S(2)}) collective-permute-start(f32[24,128]{1,0:T(8,128)S(1)} %get-tuple-element.19.refs_0_.t0), channel_id=1, source_target_pairs={{0,1},{1,2},{2,0},{3,4},{4,3},{5,6},{6,5},{7,8},{8,7},{9,10},{10,9... | collective-permute-start | bytes 36872 | tf_op jit(solution)/shard_map/ppermute | solution.py:308
  10.3 3.8 %collective-permute-start.6 = (f32[24,128]{1,0:T(8,128)S(1)}, f32[24,128]{1,0:T(8,128)S(1)}, u32[]{:S(2)}, u32[]{:S(2)}) collective-permute-start(f32[24,128]{1,0:T(8,128)S(1)} %get-tuple-element.19.refs_0_.t0), channel_id=1, source_target_pairs={{0,8},{1,9},{2,10},{3,11},{4,12},{5,13},{6,14},{7,15},{8,0},{9,1},... | collective-permute-start | bytes 36872 | tf_op jit(solution)/shard_map/ppermute | solution.py:308
  12.1 3.1 %collective-permute-start.5 = (f32[24,128]{1,0:T(8,128)S(1)}, f32[24,128]{1,0:T(8,128)S(1)}, u32[]{:S(2)}, u32[]{:S(2)}) collective-permute-start(f32[24,128]{1,0:T(8,128)S(1)} %get-tuple-element.19.refs_0_.t0), channel_id=1, source_target_pairs={{0,3},{1,2},{2,1},{3,0},{4,5},{5,4},{6,7},{7,6},{8,16},{9,17},{10,... | collective-permute-start | bytes 36872 | tf_op jit(solution)/shard_map/ppermute | solution.py:308
  13.5 1.8 %collective-permute-start.4 = (f32[24,128]{1,0:T(8,128)S(1)}, f32[24,128]{1,0:T(8,128)S(1)}, u32[]{:S(2)}, u32[]{:S(2)}) collective-permute-start(f32[24,128]{1,0:T(8,128)S(1)} %get-tuple-element.19.refs_0_.t0), channel_id=1, source_target_pairs={{0,1},{1,0},{2,3},{3,2},{4,5},{5,4},{6,7},{7,6},{8,9},{9,8},{10,11... | collective-permute-start | bytes 36872 | tf_op jit(solution)/shard_map/ppermute | solution.py:308
  15.6 10.0 %copy-start = (f32[3,32,512]{2,1,0:T(8,128)S(1)}, f32[3,32,512]{2,1,0:T(8,128)}, u32[]{:S(2)}) copy-start(f32[3,32,512]{2,1,0:T(8,128)} %refs_1_.1) | copy-start | bytes 589828
  15.6 3.8 %collective-permute-start.11 = (f32[24,128]{1,0:T(8,128)S(1)}, f32[24,128]{1,0:T(8,128)S(1)}, u32[]{:S(2)}, u32[]{:S(2)}) collective-permute-start(f32[24,128]{1,0:T(8,128)S(1)} %shard_map.89.refs_0_.t1), channel_id=1, source_target_pairs={{0,1},{1,2},{2,0},{3,4},{4,3},{5,6},{6,5},{7,8},{8,7},{9,10},{10,9... | collective-permute-start | bytes 36872 | tf_op jit(solution)/shard_map/ppermute | solution.py:308
  15.8 5.0 %collective-permute-start.10 = (f32[24,128]{1,0:T(8,128)S(1)}, f32[24,128]{1,0:T(8,128)S(1)}, u32[]{:S(2)}, u32[]{:S(2)}) collective-permute-start(f32[24,128]{1,0:T(8,128)S(1)} %shard_map.89.refs_0_.t1), channel_id=1, source_target_pairs={{0,8},{1,9},{2,10},{3,11},{4,12},{5,13},{6,14},{7,15},{8,0},{9,1},... | collective-permute-start | bytes 36872 | tf_op jit(solution)/shard_map/ppermute | solution.py:308
  19.0 3.1 %collective-permute-start.9 = (f32[24,128]{1,0:T(8,128)S(1)}, f32[24,128]{1,0:T(8,128)S(1)}, u32[]{:S(2)}, u32[]{:S(2)}) collective-permute-start(f32[24,128]{1,0:T(8,128)S(1)} %shard_map.89.refs_0_.t1), channel_id=1, source_target_pairs={{0,3},{1,2},{2,1},{3,0},{4,5},{5,4},{6,7},{7,6},{8,16},{9,17},{10,... | collective-permute-start | bytes 36872 | tf_op jit(solution)/shard_map/ppermute | solution.py:308
  19.4 2.7 %collective-permute-start.8 = (f32[24,128]{1,0:T(8,128)S(1)}, f32[24,128]{1,0:T(8,128)S(1)}, u32[]{:S(2)}, u32[]{:S(2)}) collective-permute-start(f32[24,128]{1,0:T(8,128)S(1)} %shard_map.89.refs_0_.t1), channel_id=1, source_target_pairs={{0,1},{1,0},{2,3},{3,2},{4,5},{5,4},{6,7},{7,6},{8,9},{9,8},{10,11... | collective-permute-start | bytes 36872 | tf_op jit(solution)/shard_map/ppermute | solution.py:308
  22.5 3.7 %collective-permute-start.15 = (f32[24,128]{1,0:T(8,128)S(1)}, f32[24,128]{1,0:T(8,128)S(1)}, u32[]{:S(2)}, u32[]{:S(2)}) collective-permute-start(f32[24,128]{1,0:T(8,128)S(1)} %shard_map.90.t2.own), channel_id=1, source_target_pairs={{0,1},{1,2},{2,0},{3,4},{4,3},{5,6},{6,5},{7,8},{8,7},{9,10},{10,9... | collective-permute-start | bytes 36872 | tf_op jit(solution)/shard_map/ppermute | solution.py:308
  22.5 3.8 %collective-permute-start.14 = (f32[24,128]{1,0:T(8,128)S(1)}, f32[24,128]{1,0:T(8,128)S(1)}, u32[]{:S(2)}, u32[]{:S(2)}) collective-permute-start(f32[24,128]{1,0:T(8,128)S(1)} %shard_map.90.t2.own), channel_id=1, source_target_pairs={{0,8},{1,9},{2,10},{3,11},{4,12},{5,13},{6,14},{7,15},{8,0},{9,1},... | collective-permute-start | bytes 36872 | tf_op jit(solution)/shard_map/ppermute | solution.py:308
  24.4 3.1 %collective-permute-start.13 = (f32[24,128]{1,0:T(8,128)S(1)}, f32[24,128]{1,0:T(8,128)S(1)}, u32[]{:S(2)}, u32[]{:S(2)}) collective-permute-start(f32[24,128]{1,0:T(8,128)S(1)} %shard_map.90.t2.own), channel_id=1, source_target_pairs={{0,3},{1,2},{2,1},{3,0},{4,5},{5,4},{6,7},{7,6},{8,16},{9,17},{10,... | collective-permute-start | bytes 36872 | tf_op jit(solution)/shard_map/ppermute | solution.py:308
  25.6 1.9 %collective-permute-start.12 = (f32[24,128]{1,0:T(8,128)S(1)}, f32[24,128]{1,0:T(8,128)S(1)}, u32[]{:S(2)}, u32[]{:S(2)}) collective-permute-start(f32[24,128]{1,0:T(8,128)S(1)} %shard_map.90.t2.own), channel_id=1, source_target_pairs={{0,1},{1,0},{2,3},{3,2},{4,5},{5,4},{6,7},{7,6},{8,9},{9,8},{10,11... | collective-permute-start | bytes 36872 | tf_op jit(solution)/shard_map/ppermute | solution.py:308
  28.1 1.3 %collective-permute-start.16 = (f32[40,128]{1,0:T(8,128)S(1)}, f32[40,128]{1,0:T(8,128)S(1)}, u32[]{:S(2)}, u32[]{:S(2)}) collective-permute-start(f32[40,128]{1,0:T(8,128)S(1)} %get-tuple-element.25), channel_id=1, source_target_pairs={{0,1},{1,0},{2,3},{3,2},{4,5},{5,4},{6,7},{7,6},{8,9},{9,8},{10,11... | collective-permute-start | bytes 61448 | tf_op jit(solution)/shard_map/ppermute | solution.py:308
  29.3 4.1 %collective-permute-start.19 = (f32[40,128]{1,0:T(8,128)S(1)}, f32[40,128]{1,0:T(8,128)S(1)}, u32[]{:S(2)}, u32[]{:S(2)}) collective-permute-start(f32[40,128]{1,0:T(8,128)S(1)} %add.21), channel_id=1, source_target_pairs={{0,7},{1,6},{2,5},{3,4},{4,3},{5,2},{6,1},{7,0},{8,15},{9,14},{10,... | collective-permute-start | bytes 61448 | tf_op jit(solution)/shard_map/ppermute | solution.py:308
  30.4 3.6 %collective-permute-start.18 = (f32[40,128]{1,0:T(8,128)S(1)}, f32[40,128]{1,0:T(8,128)S(1)}, u32[]{:S(2)}, u32[]{:S(2)}) collective-permute-start(f32[40,128]{1,0:T(8,128)S(1)} %add.21), channel_id=1, source_target_pairs={{0,5},{1,4},{2,7},{3,6},{4,1},{5,0},{6,3},{7,2},{8,13},{9,12},{10,... | collective-permute-start | bytes 61448 | tf_op jit(solution)/shard_map/ppermute | solution.py:308
  31.8 3.2 %collective-permute-start.17 = (f32[40,128]{1,0:T(8,128)S(1)}, f32[40,128]{1,0:T(8,128)S(1)}, u32[]{:S(2)}, u32[]{:S(2)}) collective-permute-start(f32[40,128]{1,0:T(8,128)S(1)} %add.21), channel_id=1, source_target_pairs={{0,3},{1,2},{2,1},{3,0},{4,7},{5,6},{6,5},{7,4},{8,11},{9,10},{10,... | collective-permute-start | bytes 61448 | tf_op jit(solution)/shard_map/ppermute | solution.py:308
  35.0 5.1 %collective-permute-start.22 = (f32[40,128]{1,0:T(8,128)S(1)}, f32[40,128]{1,0:T(8,128)S(1)}, u32[]{:S(2)}, u32[]{:S(2)}) collective-permute-start(f32[40,128]{1,0:T(8,128)S(1)} %add_add_fusion.1), channel_id=1, source_target_pairs={{0,25},{1,24},{2,27},{3,26},{4,29},{5,28},{6,31},{7,30},{8,17},{9,... | collective-permute-start | bytes 61448 | tf_op jit(solution)/shard_map/ppermute | solution.py:308
  36.1 5.1 %collective-permute-start.21 = (f32[40,128]{1,0:T(8,128)S(1)}, f32[40,128]{1,0:T(8,128)S(1)}, u32[]{:S(2)}, u32[]{:S(2)}) collective-permute-start(f32[40,128]{1,0:T(8,128)S(1)} %add_add_fusion.1), channel_id=1, source_target_pairs={{0,17},{1,16},{2,19},{3,18},{4,21},{5,20},{6,23},{7,22},{8,25},{9,... | collective-permute-start | bytes 61448 | tf_op jit(solution)/shard_map/ppermute | solution.py:308
  37.8 3.6 %collective-permute-start.20 = (f32[40,128]{1,0:T(8,128)S(1)}, f32[40,128]{1,0:T(8,128)S(1)}, u32[]{:S(2)}, u32[]{:S(2)}) collective-permute-start(f32[40,128]{1,0:T(8,128)S(1)} %add_add_fusion.1), channel_id=1, source_target_pairs={{0,9},{1,8},{2,11},{3,10},{4,13},{5,12},{6,15},{7,14},{8,1},{9,0},... | collective-permute-start | bytes 61448 | tf_op jit(solution)/shard_map/ppermute | solution.py:308

commit v8 on v7

--- a/solution.py
+++ b/solution.py
@@ -332,20 +332,21 @@
 
 def summed(value):
     length = lax.axis_size("dom")
-
-    def fetched(step):
-        return send(value, {d: d ^ (step | 1) for d in range(length)})
-
-    value = value + fetched(1)
+    value = value + send(value, {d: d ^ 1 for d in range(length)})
     step = 2
     while step < length:
-        if 2 * step < length:
-            farthest = fetched(3 * step)
-            first, second = fetched(step), fetched(2 * step)
-            value = (value + first) + (second + farthest)
-        else:
-            value = value + fetched(step)
-        step *= 4
+        size = min(4, length // step)
+        groups = [
+            [low + step * k for k in range(size)]
+            for low in range(length)
+            if low // step % size == 0
+        ]
+        parts = jnp.broadcast_to(value, (size,) + value.shape)
+        parts = lax.all_to_all(parts, "dom", 0, 0, axis_index_groups=groups)
+        value = parts[0] + parts[1]
+        if size == 4:
+            value = value + (parts[2] + parts[3])
+        step *= size
     return value
 
 

time: 42.5 us -> 47.1 us (1.11)
  blocking collectives: 0 us -> 16.6 us
  starting transfers between devices: 23.2 us -> 16.1 us
  waiting for transfers between devices: 12.6 us -> 7.65 us
    all_to_all x0 -> x2, blocking collectives: none -> 16.6 us  [summed(): parts = lax.all_to_all(parts, 'dom', 0, 0, axis_index_groups=groups)]
    ppermute x23 -> x17, starting transfers between devices: 23.2 us -> 16.1 us  [send(): lax.ppermute(value, 'dom', [(d, target[d]) for d in range(lax.axis_size('...]
    ppermute x23 -> x17, waiting for transfers between devices: 12.6 us -> 7.65 us  [send(): lax.ppermute(value, 'dom', [(d, target[d]) for d in range(lax.axis_size('...]
  transfers between devices with their start and end apart: 23 -> 17, of which waited for: 15 -> 9; matrix products, arithmetic and copies ran while one was open for 0% -> 0% of each run, Pallas kernels for 4% -> 4%
where the time goes in v8:
time: 47.1 us; the launch traced here: 46.9 us
  blocking collectives  16.6 us (35%)
  starting transfers between devices  16.1 us (34%)
  waiting for transfers between devices  7.65 us (16%)
  Pallas kernels  5.84 us (12%)
  between operations  0.72 us (2%)
    all_to_all x2, blocking collectives, summed(): parts = lax.all_to_all(parts, 'dom', 0, 0, axis_index_groups=groups)  16.6 us
    ppermute x17, starting transfers between devices, send(): lax.ppermute(value, 'dom', [(d, target[d]) for d in range(lax.axis_size('...  16.1 us
    ppermute x17, waiting for transfers between devices, send(): lax.ppermute(value, 'dom', [(d, target[d]) for d in range(lax.axis_size('...  7.65 us
    pallas_call x1, Pallas kernels, local(): call(prepare_kernel, [((width, rows), bf16), ((width, rows), bf16), ((8 *...  1.39 us
    pallas_call x1, Pallas kernels, local(): call(start_kernel, [((comps * blocks + 8, 128), f32)], [HBM] * 4, 600000,...  1.08 us
    pallas_call x1, Pallas kernels, local(): call(lambda *refs: finish_kernel(total, *refs), [((comps, S, rows), f32),...  0.95 us
  transfers between devices with their start and end apart: 17, of which 9 were waited for; matrix products, arithmetic and copies ran while one was open for 0% of the time, Pallas kernels for 4%

profile of v8, /device:TPU:0, one launch (start us, length us, event | category | flops | bytes accessed | tf_op | source)
XLA Modules:
  0.0 46.9 jit_solution(4994575171740375340)
XLA Ops:
  0.6 1.1 %shard_map.86.refs_0_ = f32[32,128]{1,0:T(8,128)S(1)} custom-call(f32[3,32,512]{2,1,0:T(8,128)} %refs_1_.1, f32[3,32]{1,0:T(4,128)} %mix_in.1, s32[1,4,8]{2,1,0:T(4,128)} %list_in.1, s32[1,4]{1,0:T(1,128)} %count_in.1), custom_call_target="tpu_custom_call" | custom-call | flops 600000 | bytes 250000 | tf_op jit(solution)/shard_map/pallas_call | solution.py:359
  1.7 0.5 %collective-permute-start.3 = (f32[32,128]{1,0:T(8,128)S(1)}, f32[32,128]{1,0:T(8,128)S(1)}, u32[]{:S(2)}, u32[]{:S(2)}) collective-permute-start(f32[32,128]{1,0:T(8,128)S(1)} %shard_map.86.refs_0_), channel_id=1, source_target_pairs={{0,1},{1,2},{2,0},{3,4},{4,3},{5,6},{6,5},{7,8},{8,7},{9,10},{10,9... | collective-permute-start | bytes 49160 | tf_op jit(solution)/shard_map/ppermute | solution.py:308
  2.2 4.3 %collective-permute-start.2 = (f32[32,128]{1,0:T(8,128)S(1)}, f32[32,128]{1,0:T(8,128)S(1)}, u32[]{:S(2)}, u32[]{:S(2)}) collective-permute-start(f32[32,128]{1,0:T(8,128)S(1)} %shard_map.86.refs_0_), channel_id=1, source_target_pairs={{0,8},{1,9},{2,10},{3,11},{4,12},{5,13},{6,14},{7,15},{8,0},{9,1},... | collective-permute-start | bytes 49160 | tf_op jit(solution)/shard_map/ppermute | solution.py:308
  6.6 0.7 %collective-permute-start.1 = (f32[32,128]{1,0:T(8,128)S(1)}, f32[32,128]{1,0:T(8,128)S(1)}, u32[]{:S(2)}, u32[]{:S(2)}) collective-permute-start(f32[32,128]{1,0:T(8,128)S(1)} %shard_map.86.refs_0_), channel_id=1, source_target_pairs={{0,3},{1,2},{2,1},{3,0},{4,5},{5,4},{6,7},{7,6},{8,16},{9,17},{10,... | collective-permute-start | bytes 49160 | tf_op jit(solution)/shard_map/ppermute | solution.py:308
  7.2 0.0 collective-permute-start
  7.2 1.4 %shard_map.87 = (bf16[256,512]{1,0:T(8,128)(2,1)S(1)}, bf16[256,512]{1,0:T(8,128)(2,1)S(1)}, f32[40,128]{1,0:T(8,128)S(1)}) custom-call(f32[512,256]{1,0:T(8,128)} %strips_in.1, s32[4,8]{1,0:T(4,128)} %bitcast.6, f32[4]{0:T(128)} %shifts_in.1), custom_call_target="tpu_custom_call" | custom-call | flops 1000000 | bytes 1000000 | tf_op jit(solution)/shard_map/pallas_call | solution.py:373
  8.6 0.0 collective-permute-done.3.refs_4_
  8.6 0.0 collective-permute-done.2.refs_3_
  8.6 1.1 %collective-permute-done.1.refs_2_ = f32[32,128]{1,0:T(8,128)S(1)} collective-permute-done((f32[32,128]{1,0:T(8,128)S(1)}, f32[32,128]{1,0:T(8,128)S(1)}, u32[]{:S(2)}, u32[]{:S(2)}) %collective-permute-start.1) | collective-permute-done | bytes 16416 | tf_op jit(solution)/shard_map/ppermute | solution.py:308
  9.7 0.0 collective-permute-done.refs_1_
  9.7 0.5 %shard_map.88 = (f32[24,128]{1,0:T(8,128)S(1)}, bf16[96,128]{1,0:T(8,128)(2,1)S(1)}) custom-call(f32[32,128]{1,0:T(8,128)S(1)} %shard_map.86.refs_0_, f32[32,128]{1,0:T(8,128)S(1)} %collective-permute-done.refs_1_, f32[32,128]{1,0:T(8,128)S(1)} %collective-permute-done.1.refs_2_, f32[32,128]{1,0:T(8,128)S(1)} %collective-permute-done.2.refs_3_, ...), custom_call_target="tpu_custom_call" | custom-call | flops 50000000 | bytes 600000 | tf_op jit(solution)/shard_map/pallas_call | solution.py:388
  10.3 0.0 collective-permute-start.7
  10.3 1.9 %collective-permute-start.6 = (f32[24,128]{1,0:T(8,128)S(1)}, f32[24,128]{1,0:T(8,128)S(1)}, u32[]{:S(2)}, u32[]{:S(2)}) collective-permute-start(f32[24,128]{1,0:T(8,128)S(1)} %get-tuple-element.19.refs_0_.t0), channel_id=1, source_target_pairs={{0,8},{1,9},{2,10},{3,11},{4,12},{5,13},{6,14},{7,15},{8,0},{9,1},... | collective-permute-start | bytes 36872 | tf_op jit(solution)/shard_map/ppermute | solution.py:308
  12.1 1.4 %collective-permute-start.5 = (f32[24,128]{1,0:T(8,128)S(1)}, f32[24,128]{1,0:T(8,128)S(1)}, u32[]{:S(2)}, u32[]{:S(2)}) collective-permute-start(f32[24,128]{1,0:T(8,128)S(1)} %get-tuple-element.19.refs_0_.t0), channel_id=1, source_target_pairs={{0,3},{1,2},{2,1},{3,0},{4,5},{5,4},{6,7},{7,6},{8,16},{9,17},{10,... | collective-permute-start | bytes 36872 | tf_op jit(solution)/shard_map/ppermute | solution.py:308
  13.5 0.5 collective-permute-start.4
  13.9 0.0 collective-permute-done.7.refs_4_
  14.0 0.1 collective-permute-done.6.refs_3_
  14.0 1.2 %collective-permute-done.5.refs_2_ = f32[24,128]{1,0:T(8,128)S(1)} collective-permute-done((f32[24,128]{1,0:T(8,128)S(1)}, f32[24,128]{1,0:T(8,128)S(1)}, u32[]{:S(2)}, u32[]{:S(2)}) %collective-permute-start.5) | collective-permute-done | bytes 12320 | tf_op jit(solution)/shard_map/ppermute | solution.py:308
  15.2 0.0 collective-permute-done.4.refs_1_
  15.2 0.4 shard_map.89.refs_0_.t1
  15.6 0.0 copy-start
  15.6 0.2 collective-permute-start.11
  15.8 3.2 %collective-permute-start.10 = (f32[24,128]{1,0:T(8,128)S(1)}, f32[24,128]{1,0:T(8,128)S(1)}, u32[]{:S(2)}, u32[]{:S(2)}) collective-permute-start(f32[24,128]{1,0:T(8,128)S(1)} %shard_map.89.refs_0_.t1), channel_id=1, source_target_pairs={{0,8},{1,9},{2,10},{3,11},{4,12},{5,13},{6,14},{7,15},{8,0},{9,1},... | collective-permute-start | bytes 36872 | tf_op jit(solution)/shard_map/ppermute | solution.py:308
  19.0 0.4 collective-permute-start.9
  19.4 0.0 collective-permute-start.8
  19.4 0.0 collective-permute-done.11.refs_4_
  19.4 1.4 %collective-permute-done.10.refs_3_ = f32[24,128]{1,0:T(8,128)S(1)} collective-permute-done((f32[24,128]{1,0:T(8,128)S(1)}, f32[24,128]{1,0:T(8,128)S(1)}, u32[]{:S(2)}, u32[]{:S(2)}) %collective-permute-start.10) | collective-permute-done | bytes 12320 | tf_op jit(solution)/shard_map/ppermute | solution.py:308
  20.8 1.3 %collective-permute-done.9.refs_2_ = f32[24,128]{1,0:T(8,128)S(1)} collective-permute-done((f32[24,128]{1,0:T(8,128)S(1)}, f32[24,128]{1,0:T(8,128)S(1)}, u32[]{:S(2)}, u32[]{:S(2)}) %collective-permute-start.9) | collective-permute-done | bytes 12320 | tf_op jit(solution)/shard_map/ppermute | solution.py:308
  22.1 0.0 collective-permute-done.8.refs_1_
  22.1 0.4 shard_map.90.t2.own
  22.5 0.0 collective-permute-start.15
  22.5 1.8 %collective-permute-start.14 = (f32[24,128]{1,0:T(8,128)S(1)}, f32[24,128]{1,0:T(8,128)S(1)}, u32[]{:S(2)}, u32[]{:S(2)}) collective-permute-start(f32[24,128]{1,0:T(8,128)S(1)} %shard_map.90.t2.own), channel_id=1, source_target_pairs={{0,8},{1,9},{2,10},{3,11},{4,12},{5,13},{6,14},{7,15},{8,0},{9,1},... | collective-permute-start | bytes 36872 | tf_op jit(solution)/shard_map/ppermute | solution.py:308
  24.4 1.2 %collective-permute-start.13 = (f32[24,128]{1,0:T(8,128)S(1)}, f32[24,128]{1,0:T(8,128)S(1)}, u32[]{:S(2)}, u32[]{:S(2)}) collective-permute-start(f32[24,128]{1,0:T(8,128)S(1)} %shard_map.90.t2.own), channel_id=1, source_target_pairs={{0,3},{1,2},{2,1},{3,0},{4,5},{5,4},{6,7},{7,6},{8,16},{9,17},{10,... | collective-permute-start | bytes 36872 | tf_op jit(solution)/shard_map/ppermute | solution.py:308
  25.6 0.0 collective-permute-start.12
  25.6 0.0 copy-done
  25.6 0.5 %shard_map.91 = (f32[24,512]{1,0:T(8,128)S(1)}, f32[40,128]{1,0:T(8,128)S(1)}, bf16[512,128]{1,0:T(8,128)(2,1)S(1)}, bf16[512,128]{1,0:T(8,128)(2,1)S(1)}, bf16[512,128]{1,0:T(8,128)(2,1)S(1)}) custom-call(f32[3,32,512]{2,1,0:T(8,128)S(1)} %copy-done, f32[24,128]{1,0:T(8,128)S(1)} %get-tuple-element.19.refs_0_.t0, f32[24,128]{1,0:T(8,128)S(1)} %shard_map.89.refs_0_.t1, ...), custom_call_target="tpu_custom_call" | custom-call | flops 60000000 | bytes 250000 | tf_op jit(solution)/shard_map/pallas_call | solution.py:403
  26.1 0.1 collective-permute-done.15.d
  26.2 0.1 collective-permute-done.14.c
  26.3 1.2 %collective-permute-done.13.b = f32[24,128]{1,0:T(8,128)S(1)} collective-permute-done((f32[24,128]{1,0:T(8,128)S(1)}, f32[24,128]{1,0:T(8,128)S(1)}, u32[]{:S(2)}, u32[]{:S(2)}) %collective-permute-start.13) | collective-permute-done | bytes 12320 | tf_op jit(solution)/shard_map/ppermute | solution.py:308
  27.5 0.0 collective-permute-done.12.a
  27.5 0.6 %shard_map.92 = (f32[8,512]{1,0:T(8,128)S(1)}, f32[40,128]{1,0:T(8,128)S(1)}) custom-call(f32[24,128]{1,0:T(8,128)S(1)} %shard_map.90.t2.own, f32[24,128]{1,0:T(8,128)S(1)} %collective-permute-done.12.a, f32[24,128]{1,0:T(8,128)S(1)} %collective-permute-done.13.b, f32[24,128]{1,0:T(8,128)S(1)} %collective-permute-done.14.c, ...), custom_call_target="tpu_custom_call" | custom-call | flops 80000000 | bytes 900000 | tf_op jit(solution)/shard_map/pallas_call | solution.py:410
  28.1 0.1 collective-permute-start.16
  28.2 1.2 %collective-permute-done.16 = f32[40,128]{1,0:T(8,128)S(1)} collective-permute-done((f32[40,128]{1,0:T(8,128)S(1)}, f32[40,128]{1,0:T(8,128)S(1)}, u32[]{:S(2)}, u32[]{:S(2)}) %collective-permute-start.16) | collective-permute-done | bytes 20512 | tf_op jit(solution)/shard_map/ppermute | solution.py:308
  29.4 7.3 %all_to_all.10 = f32[4,40,128]{2,1,0:T(8,128)S(1)} all-to-all(f32[4,40,128]{2,1,0:T(8,128)S(1)} %broadcast_in_dim.6), channel_id=1, replica_groups={{0,2,4,6},{1,3,5,7},{8,10,12,14},{9,11,13,15},{16,18,20,22},{17,19,21,2..., dimensions={0} | all-to-all | bytes 163840 | tf_op jit(solution)/shard_map/all_to_all | solution.py:345
  36.6 9.3 %all_to_all.11 = f32[4,40,128]{2,1,0:T(8,128)S(1)} all-to-all(f32[4,40,128]{2,1,0:T(8,128)S(1)} %broadcast_in_dim.7), channel_id=1, replica_groups={{0,8,16,24},{1,9,17,25},{2,10,18,26},{3,11,19,27},{4,12,20,28},{5,13,21..., dimensions={0} | all-to-all | bytes 163840 | tf_op jit(solution)/shard_map/all_to_all | solution.py:345
  45.9 0.9 %shard_map.93 = (f32[3,4,512]{2,1,0:T(4,128)}, f32[3,4,36]{2,1,0:T(4,128)}) custom-call(f32[40,128]{1,0:T(8,128)S(1)} %fusion.1.refs_0_, f32[3,32,512]{2,1,0:T(8,128)S(1)} %copy-done, f32[24,512]{1,0:T(8,128)S(1)} %get-tuple-element.26.refs_2_, f32[8,512]{1,0:T(8,128)S(1)} %get-tuple-element.27.refs_3_), custom_call_target="tpu_custom_call" | custom-call | flops 50000000 | bytes 400000 | tf_op jit(solution)/shard_map/pallas_call | solution.py:414
  (5 shorter events, 0.0 us)
Async XLA Ops:
  1.7 6.9 %collective-permute-start.3 = (f32[32,128]{1,0:T(8,128)S(1)}, f32[32,128]{1,0:T(8,128)S(1)}, u32[]{:S(2)}, u32[]{:S(2)}) collective-permute-start(f32[32,128]{1,0:T(8,128)S(1)} %shard_map.86.refs_0_), channel_id=1, source_target_pairs={{0,1},{1,2},{2,0},{3,4},{4,3},{5,6},{6,5},{7,8},{8,7},{9,10},{10,9... | collective-permute-start | bytes 49160 | tf_op jit(solution)/shard_map/ppermute | solution.py:308
  2.2 6.4 %collective-permute-start.2 = (f32[32,128]{1,0:T(8,128)S(1)}, f32[32,128]{1,0:T(8,128)S(1)}, u32[]{:S(2)}, u32[]{:S(2)}) collective-permute-start(f32[32,128]{1,0:T(8,128)S(1)} %shard_map.86.refs_0_), channel_id=1, source_target_pairs={{0,8},{1,9},{2,10},{3,11},{4,12},{5,13},{6,14},{7,15},{8,0},{9,1},... | collective-permute-start | bytes 49160 | tf_op jit(solution)/shard_map/ppermute | solution.py:308
  6.6 3.2 %collective-permute-start.1 = (f32[32,128]{1,0:T(8,128)S(1)}, f32[32,128]{1,0:T(8,128)S(1)}, u32[]{:S(2)}, u32[]{:S(2)}) collective-permute-start(f32[32,128]{1,0:T(8,128)S(1)} %shard_map.86.refs_0_), channel_id=1, source_target_pairs={{0,3},{1,2},{2,1},{3,0},{4,5},{5,4},{6,7},{7,6},{8,16},{9,17},{10,... | collective-permute-start | bytes 49160 | tf_op jit(solution)/shard_map/ppermute | solution.py:308
  7.2 2.5 %collective-permute-start = (f32[32,128]{1,0:T(8,128)S(1)}, f32[32,128]{1,0:T(8,128)S(1)}, u32[]{:S(2)}, u32[]{:S(2)}) collective-permute-start(f32[32,128]{1,0:T(8,128)S(1)} %shard_map.86.refs_0_), channel_id=1, source_target_pairs={{0,1},{1,0},{2,3},{3,2},{4,5},{5,4},{6,7},{7,6},{8,9},{9,8},{10,11... | collective-permute-start | bytes 49160 | tf_op jit(solution)/shard_map/ppermute | solution.py:308
  10.3 3.7 %collective-permute-start.7 = (f32[24,128]{1,0:T(8,128)S(1)}, f32[24,128]{1,0:T(8,128)S(1)}, u32[]{:S(2)}, u32[]{:S(2)}) collective-permute-start(f32[24,128]{1,0:T(8,128)S(1)} %get-tuple-element.19.refs_0_.t0), channel_id=1, source_target_pairs={{0,1},{1,2},{2,0},{3,4},{4,3},{5,6},{6,5},{7,8},{8,7},{9,10},{10,9... | collective-permute-start | bytes 36872 | tf_op jit(solution)/shard_map/ppermute | solution.py:308
  10.3 3.8 %collective-permute-start.6 = (f32[24,128]{1,0:T(8,128)S(1)}, f32[24,128]{1,0:T(8,128)S(1)}, u32[]{:S(2)}, u32[]{:S(2)}) collective-permute-start(f32[24,128]{1,0:T(8,128)S(1)} %get-tuple-element.19.refs_0_.t0), channel_id=1, source_target_pairs={{0,8},{1,9},{2,10},{3,11},{4,12},{5,13},{6,14},{7,15},{8,0},{9,1},... | collective-permute-start | bytes 36872 | tf_op jit(solution)/shard_map/ppermute | solution.py:308
  12.1 3.1 %collective-permute-start.5 = (f32[24,128]{1,0:T(8,128)S(1)}, f32[24,128]{1,0:T(8,128)S(1)}, u32[]{:S(2)}, u32[]{:S(2)}) collective-permute-start(f32[24,128]{1,0:T(8,128)S(1)} %get-tuple-element.19.refs_0_.t0), channel_id=1, source_target_pairs={{0,3},{1,2},{2,1},{3,0},{4,5},{5,4},{6,7},{7,6},{8,16},{9,17},{10,... | collective-permute-start | bytes 36872 | tf_op jit(solution)/shard_map/ppermute | solution.py:308
  13.5 1.8 %collective-permute-start.4 = (f32[24,128]{1,0:T(8,128)S(1)}, f32[24,128]{1,0:T(8,128)S(1)}, u32[]{:S(2)}, u32[]{:S(2)}) collective-permute-start(f32[24,128]{1,0:T(8,128)S(1)} %get-tuple-element.19.refs_0_.t0), channel_id=1, source_target_pairs={{0,1},{1,0},{2,3},{3,2},{4,5},{5,4},{6,7},{7,6},{8,9},{9,8},{10,11... | collective-permute-start | bytes 36872 | tf_op jit(solution)/shard_map/ppermute | solution.py:308
  15.6 10.0 %copy-start = (f32[3,32,512]{2,1,0:T(8,128)S(1)}, f32[3,32,512]{2,1,0:T(8,128)}, u32[]{:S(2)}) copy-start(f32[3,32,512]{2,1,0:T(8,128)} %refs_1_.1) | copy-start | bytes 589828
  15.6 3.8 %collective-permute-start.11 = (f32[24,128]{1,0:T(8,128)S(1)}, f32[24,128]{1,0:T(8,128)S(1)}, u32[]{:S(2)}, u32[]{:S(2)}) collective-permute-start(f32[24,128]{1,0:T(8,128)S(1)} %shard_map.89.refs_0_.t1), channel_id=1, source_target_pairs={{0,1},{1,2},{2,0},{3,4},{4,3},{5,6},{6,5},{7,8},{8,7},{9,10},{10,9... | collective-permute-start | bytes 36872 | tf_op jit(solution)/shard_map/ppermute | solution.py:308
  15.8 5.0 %collective-permute-start.10 = (f32[24,128]{1,0:T(8,128)S(1)}, f32[24,128]{1,0:T(8,128)S(1)}, u32[]{:S(2)}, u32[]{:S(2)}) collective-permute-start(f32[24,128]{1,0:T(8,128)S(1)} %shard_map.89.refs_0_.t1), channel_id=1, source_target_pairs={{0,8},{1,9},{2,10},{3,11},{4,12},{5,13},{6,14},{7,15},{8,0},{9,1},... | collective-permute-start | bytes 36872 | tf_op jit(solution)/shard_map/ppermute | solution.py:308
  19.0 3.1 %collective-permute-start.9 = (f32[24,128]{1,0:T(8,128)S(1)}, f32[24,128]{1,0:T(8,128)S(1)}, u32[]{:S(2)}, u32[]{:S(2)}) collective-permute-start(f32[24,128]{1,0:T(8,128)S(1)} %shard_map.89.refs_0_.t1), channel_id=1, source_target_pairs={{0,3},{1,2},{2,1},{3,0},{4,5},{5,4},{6,7},{7,6},{8,16},{9,17},{10,... | collective-permute-start | bytes 36872 | tf_op jit(solution)/shard_map/ppermute | solution.py:308
  19.4 2.7 %collective-permute-start.8 = (f32[24,128]{1,0:T(8,128)S(1)}, f32[24,128]{1,0:T(8,128)S(1)}, u32[]{:S(2)}, u32[]{:S(2)}) collective-permute-start(f32[24,128]{1,0:T(8,128)S(1)} %shard_map.89.refs_0_.t1), channel_id=1, source_target_pairs={{0,1},{1,0},{2,3},{3,2},{4,5},{5,4},{6,7},{7,6},{8,9},{9,8},{10,11... | collective-permute-start | bytes 36872 | tf_op jit(solution)/shard_map/ppermute | solution.py:308
  22.5 3.7 %collective-permute-start.15 = (f32[24,128]{1,0:T(8,128)S(1)}, f32[24,128]{1,0:T(8,128)S(1)}, u32[]{:S(2)}, u32[]{:S(2)}) collective-permute-start(f32[24,128]{1,0:T(8,128)S(1)} %shard_map.90.t2.own), channel_id=1, source_target_pairs={{0,1},{1,2},{2,0},{3,4},{4,3},{5,6},{6,5},{7,8},{8,7},{9,10},{10,9... | collective-permute-start | bytes 36872 | tf_op jit(solution)/shard_map/ppermute | solution.py:308
  22.5 3.8 %collective-permute-start.14 = (f32[24,128]{1,0:T(8,128)S(1)}, f32[24,128]{1,0:T(8,128)S(1)}, u32[]{:S(2)}, u32[]{:S(2)}) collective-permute-start(f32[24,128]{1,0:T(8,128)S(1)} %shard_map.90.t2.own), channel_id=1, source_target_pairs={{0,8},{1,9},{2,10},{3,11},{4,12},{5,13},{6,14},{7,15},{8,0},{9,1},... | collective-permute-start | bytes 36872 | tf_op jit(solution)/shard_map/ppermute | solution.py:308
  24.4 3.1 %collective-permute-start.13 = (f32[24,128]{1,0:T(8,128)S(1)}, f32[24,128]{1,0:T(8,128)S(1)}, u32[]{:S(2)}, u32[]{:S(2)}) collective-permute-start(f32[24,128]{1,0:T(8,128)S(1)} %shard_map.90.t2.own), channel_id=1, source_target_pairs={{0,3},{1,2},{2,1},{3,0},{4,5},{5,4},{6,7},{7,6},{8,16},{9,17},{10,... | collective-permute-start | bytes 36872 | tf_op jit(solution)/shard_map/ppermute | solution.py:308
  25.6 1.9 %collective-permute-start.12 = (f32[24,128]{1,0:T(8,128)S(1)}, f32[24,128]{1,0:T(8,128)S(1)}, u32[]{:S(2)}, u32[]{:S(2)}) collective-permute-start(f32[24,128]{1,0:T(8,128)S(1)} %shard_map.90.t2.own), channel_id=1, source_target_pairs={{0,1},{1,0},{2,3},{3,2},{4,5},{5,4},{6,7},{7,6},{8,9},{9,8},{10,11... | collective-permute-start | bytes 36872 | tf_op jit(solution)/shard_map/ppermute | solution.py:308
  28.1 1.3 %collective-permute-start.16 = (f32[40,128]{1,0:T(8,128)S(1)}, f32[40,128]{1,0:T(8,128)S(1)}, u32[]{:S(2)}, u32[]{:S(2)}) collective-permute-start(f32[40,128]{1,0:T(8,128)S(1)} %get-tuple-element.25), channel_id=1, source_target_pairs={{0,1},{1,0},{2,3},{3,2},{4,5},{5,4},{6,7},{7,6},{8,9},{9,8},{10,11... | collective-permute-start | bytes 61448 | tf_op jit(solution)/shard_map/ppermute | solution.py:308

commit v9 on v7

--- a/solution.py
+++ b/solution.py
@@ -21,6 +21,36 @@
 
 def iota(shape, axis):
     return lax.broadcasted_iota(jnp.int32, shape, axis)
+
+
+def packed(tile, tail=None):
+    low = iota((8, 128), 1) < BLOCK
+    last = tile[16:] if tail is None else jnp.where(low, tile[16:], tail)
+    return jnp.concatenate([jnp.where(low, tile[:8], tile[8:16]), last], axis=0)
+
+
+def unpacked(sent):
+    low = iota((8, 128), 1) < BLOCK
+    pair, last = sent[:8], sent[8:]
+    turned, rest = pltpu.roll(pair, BLOCK, 1), pltpu.roll(last, BLOCK, 1)
+    parts = [jnp.where(low, pair, turned), jnp.where(low, turned, pair), jnp.where(low, last, rest)]
+    return jnp.concatenate(parts, axis=0), rest
+
+
+PLACES = {
+    (0, 0): (0, 0),
+    (0, 1): (0, 32),
+    (0, 2): (0, 56),
+    (0, 3): (0, 72),
+    (1, 0): (0, 80),
+    (1, 2): (0, 112),
+    (1, 1): (1, 0),
+    (1, 3): (1, 24),
+    (2, 0): (1, 32),
+    (2, 1): (1, 64),
+    (2, 2): (1, 88),
+    (2, 3): (1, 104),
+}
 
 
 def own_lanes(rows, width):
@@ -60,7 +90,7 @@
     return copies
 
 
-def start_kernel(prev_in, mix_in, list_in, count_in, out_ref, prev_ref, mix_ref, list_ref, count_ref, sems):
+def start_kernel(prev_in, mix_in, list_in, count_in, sent_ref, tile_ref, prev_ref, mix_ref, list_ref, count_ref, sems):
     copies = fetch(
         [(prev_in, prev_ref), (mix_in, mix_ref), (list_in, list_ref), (count_in, count_ref)], sems
     )
@@ -79,15 +109,18 @@
     for link in range(4):
         live = slot < jnp.broadcast_to(count_ref[0:1, link : link + 1], slot.shape)
         line = jnp.where(live, order[link : link + 1], DEAD)
-        line = pltpu.roll(jnp.broadcast_to(line, (8, 128)), 8 + 8 * link, 1)
-        meta = jnp.where(iota((8, 128), 1) // 8 == link + 1, line, meta)
-    out_ref[8 * comps :, :] = meta
+        line = pltpu.roll(jnp.broadcast_to(line, (8, 128)), BLOCK + 8 + 8 * link, 1)
+        meta = jnp.where(iota((8, 128), 1) // 8 == BLOCK // 8 + link + 1, line, meta)
     copies[0].wait()
     own = own_lanes(8, rows)
+    parts = []
     for c in range(comps):
         start = jnp.sum(weights[c] * prev_ref[c], axis=0, keepdims=True)
         line = jnp.broadcast_to(start, own.shape)
-        out_ref[c * 8 : (c + 1) * 8, :] = fold(jnp.where(own, line, 0.0))
+        parts.append(fold(jnp.where(own, line, 0.0)))
+    tile = jnp.concatenate(parts, axis=0)
+    tile_ref[...] = tile
+    sent_ref[...] = packed(tile, meta)
 
 
 def prepare_kernel(strips_in, columns_in, shifts_in, high_ref, low_ref, aux_ref, strips, columns, shifts, sems):
@@ -166,19 +199,22 @@
     return image - jnp.concatenate([shift] * COMPS, axis=0) * pieces[0]
 
 
-def first_kernel(length, own, a, b, c, d, aux, high, low, tile_ref, choose_ref):
-    rows = 8 * COMPS
-    refs = (own, a, b, c, d)
-    pieces = [ref[:rows, :] for ref in refs]
-    metas = [ref[rows : rows + 1, :] for ref in refs[1:]]
+def first_kernel(length, own, a, b, c, d, aux, high, low, sent_ref, tile_ref, choose_ref):
+    received = [unpacked(ref[...]) for ref in (a, b, c, d)]
+    metas = [rest[:1] for _, rest in received]
     choose = selection(aux[8 * S :, :], metas, lax.axis_index("dom"), length)
     choose_ref[...] = choose
-    tile_ref[...] = multiply(choose, pieces, aux[:8, :], high[...], low[...])
-
-
-def middle_kernel(step, own, a, b, c, d, choose, aux, high, low, tile_ref):
-    pieces = [ref[...] for ref in (own, a, b, c, d)]
-    tile_ref[...] = multiply(choose[...], pieces, aux[8 * step : 8 * step + 8, :], high[...], low[...])
+    pieces = [own[...]] + [tile for tile, _ in received]
+    tile = multiply(choose, pieces, aux[:8, :], high[...], low[...])
+    tile_ref[...] = tile
+    sent_ref[...] = packed(tile)
+
+
+def middle_kernel(step, own, a, b, c, d, choose, aux, high, low, sent_ref, tile_ref):
+    pieces = [own[...]] + [unpacked(ref[...])[0] for ref in (a, b, c, d)]
+    tile = multiply(choose[...], pieces, aux[8 * step : 8 * step + 8, :], high[...], low[...])
+    tile_ref[...] = tile
+    sent_ref[...] = packed(tile)
 
 
 def collect(gram, width, vecs):
@@ -194,11 +230,14 @@
     lines_ref[...] = lines
     prev = prev_ref[...].reshape(width, rows)
     full = dot(prev, prev, NT, HIGHEST)
-    owner = iota((vecs, width), 1) // vecs
-    total = jnp.where(owner == 0, full[:vecs], 0.0)
-    for c in range(1, comps):
-        total = total + jnp.where(owner == c, full[c * vecs : (c + 1) * vecs], 0.0)
-    gram_ref[:vecs, :] = jnp.concatenate([total, jnp.zeros((vecs, 128 - width), jnp.float32)], axis=1)
+    full = jnp.concatenate([full, jnp.zeros((width, 128 - width), jnp.float32)], axis=1)
+    lane = iota((8, 128), 1)
+    tiles = [jnp.zeros((8, 128), jnp.float32)] * 2
+    for (c, g), (t, first) in PLACES.items():
+        at = c * vecs + 8 * g
+        piece = pltpu.roll(full[at : at + 8], (first - at) % 128, 1)
+        tiles[t] = jnp.where((lane >= first) & (lane < first + vecs - 8 * g), piece, tiles[t])
+    gram_ref[:16, :] = jnp.concatenate(tiles, axis=0)
     against = jnp.concatenate([prev, lines, jnp.zeros((8, rows), jnp.float32)], axis=0)
     for ref, part in zip(turned_refs, split(against.T)):
         ref[...] = part
@@ -207,14 +246,13 @@
     for k in range(S - 1):
         line = collect(gram[k * 8 : (k + 1) * 8], width, vecs)
         result = jnp.where(iota((8, 128), 0) == k, jnp.broadcast_to(line, result.shape), result)
-    gram_ref[vecs:, :] = result
-
-
-def last_kernel(own, a, b, c, d, choose, aux, high, low, early, t0, t1, t2, line_ref, gram_ref):
-    pieces = [ref[...] for ref in (own, a, b, c, d)]
+    gram_ref[16:, :] = result
+
+
+def last_kernel(vecs, own, a, b, c, d, choose, aux, high, low, early, t0, t1, t2, line_ref, gram_ref):
+    pieces = [own[...]] + [unpacked(ref[...])[0] for ref in (a, b, c, d)]
     tile = multiply(choose[...], pieces, aux[8 * S - 8 : 8 * S, :], high[...], low[...])
     rows = line_ref.shape[1]
-    vecs = early.shape[0] - 8
     width = COMPS * vecs
     last = lines_of(tile, rows)
     line_ref[...] = last
@@ -225,9 +263,9 @@
     square = jnp.sum(last * last, axis=1, keepdims=True)
     gram = jnp.where(iota(gram.shape, 1) == width + 8 * (S - 1) + iota(gram.shape, 0), square, gram)
     line = collect(gram, width, vecs)
-    gram_ref[:vecs, :] = early[:vecs, :]
-    gram_ref[vecs:, :] = jnp.where(
-        iota((8, 128), 0) == S - 1, jnp.broadcast_to(line, (8, 128)), early[vecs:, :]
+    gram_ref[:16, :] = early[:16, :]
+    gram_ref[16:, :] = jnp.where(
+        iota((8, 128), 0) == S - 1, jnp.broadcast_to(line, (8, 128)), early[16:, :]
     )
 
 
@@ -235,7 +273,7 @@
     comps, vecs, rows = prev_ref.shape
     width = comps * vecs
     gram = gram_in[...] * (1.0 / total)
-    small = gram[vecs:]
+    small = gram[16:]
     lane, comp = iota((8, 128), 1), iota((8, 128), 0)
     in_prev = (lane < width) & (lane // vecs == comp)
     coef, cross = [], []
@@ -244,17 +282,24 @@
         coef.append(jnp.where(in_prev, line, 0.0))
         cross.append([jnp.where(lane == width + 8 * l + comp, line, 0.0) for l in range(k + 1)])
     coefs = jnp.concatenate(coef, axis=0)
-    square = jnp.concatenate([gram[:vecs]] * comps, axis=0)
-    r, q = iota(square.shape, 0), iota(square.shape, 1)
-    square = jnp.where(r // vecs == q // vecs, square, 0.0) - jnp.where(r == q, 2.0, 0.0)
-    turned = dot(coefs[:, :width], square, precision=HIGHEST)
+    pieces = []
+    for c in range(comps):
+        for g in range(vecs // 8):
+            t, first = PLACES[c, g]
+            at = c * vecs + 8 * g
+            piece = pltpu.roll(gram[8 * t : 8 * t + 8], (at - first) % 128, 1)
+            piece = jnp.where(lane < at + 8, 0.5 * piece, piece)
+            piece = jnp.where((lane >= at) & (lane < (c + 1) * vecs), piece, 0.0)
+            pieces.append(piece - jnp.where(lane == at + comp, 1.0, 0.0))
+    half = jnp.concatenate(pieces, axis=0)
+    turned = dot(coefs[:, :width], half, precision=HIGHEST)
     prev = prev_ref[...].reshape(width, rows)
     basis = jnp.concatenate([lines[...], last[...]], axis=0)
     projected = basis - dot(coefs[:, :width], prev, precision=HIGHEST)
     unit, scale = {}, {}
     for l in range(S):
         for k in range(l, S):
-            value = turned[k * 8 : (k + 1) * 8] * coef[l] + cross[k][l]
+            value = turned[k * 8 : (k + 1) * 8] * coef[l] + turned[l * 8 : (l + 1) * 8] * coef[k] + cross[k][l]
             value = jnp.sum(value, axis=1, keepdims=True)
             for m in range(l):
                 value = value - (unit[k, m] * scale[m]) * unit[l, m]
@@ -355,9 +400,10 @@
     width = strips.shape[1]
     f32, bf16, dma = jnp.float32, jnp.bfloat16, pltpu.SemaphoreType.DMA
     tile_out = ((comps * blocks, 128), f32)
-    tile = call(
+    sent_out = ((16, 128), f32)
+    sent, tile = call(
         start_kernel,
-        [((comps * blocks + 8, 128), f32)],
+        [sent_out, tile_out],
         [HBM] * 4,
         600000,
         250000,
@@ -384,21 +430,25 @@
     )(*in_hbm(strips, columns.T, shifts))
     tiles = []
     length = lax.axis_size("dom")
-    tile, choose = call(
+    sent, tile, choose = call(
         lambda *refs: first_kernel(length, *refs),
-        [tile_out, ((4 * comps * blocks, 128), bf16)],
+        [sent_out, tile_out, ((4 * comps * blocks, 128), bf16)],
         [VMEM] * 8,
         50000000,
         600000,
-    )(tile, *ghosts(tile), aux, high, low)
+    )(tile, *ghosts(sent), aux, high, low)
     tiles.append(tile)
     for step in (1, 2):
-        tile = call(
-            lambda *refs, step=step: middle_kernel(step, *refs), [tile_out], [VMEM] * 9, 50000000, 600000
-        )(tile, *ghosts(tile), choose, aux, high, low)
+        sent, tile = call(
+            lambda *refs, step=step: middle_kernel(step, *refs),
+            [sent_out, tile_out],
+            [VMEM] * 9,
+            50000000,
+            600000,
+        )(tile, *ghosts(sent), choose, aux, high, low)
         tiles.append(tile)
-    received = ghosts(tile)
-    gram_out = ((vecs + 8, 128), f32)
+    received = ghosts(sent)
+    gram_out = ((24, 128), f32)
     lines, early, *turned = call(
         early_kernel,
         [((8 * S - 8, rows), f32), gram_out] + [((rows, 128), bf16)] * 3,
@@ -407,7 +457,11 @@
         250000,
     )(prev_basis, *tiles)
     last, gram = call(
-        last_kernel, [((8, rows), f32), gram_out], [VMEM] * 13, 80000000, 900000
+        lambda *refs: last_kernel(vecs, *refs),
+        [((8, rows), f32), gram_out],
+        [VMEM] * 13,
+        80000000,
+        900000,
     )(tile, *received, choose, aux, high, low, early, *turned)
     total = float(length * rows)
     basis, factors = call(

time: 42.5 us -> 42 us (0.988)
  waiting for transfers between devices: 12.6 us -> 11.7 us
    ppermute x23, waiting for transfers between devices: 12.6 us -> 11.7 us  [send(): lax.ppermute(value, 'dom', [(d, target[d]) for d in range(lax.axis_size('...]
  transfers between devices with their start and end apart: 23 -> 23, of which waited for: 15 -> 10; matrix products, arithmetic and copies ran while one was open for 0% -> 0% of each run, Pallas kernels for 4% -> 5%
where the time goes in v9:
time: 42 us; the launch traced here: 41.8 us
  starting transfers between devices  23.2 us (55%)
  waiting for transfers between devices  11.7 us (28%)
  Pallas kernels  6.19 us (15%)
  between operations  0.73 us (2%)
    ppermute x23, starting transfers between devices, send(): lax.ppermute(value, 'dom', [(d, target[d]) for d in range(lax.axis_size('...  23.2 us
    ppermute x23, waiting for transfers between devices, send(): lax.ppermute(value, 'dom', [(d, target[d]) for d in range(lax.axis_size('...  11.7 us
    pallas_call x1, Pallas kernels, local(): call(prepare_kernel, [((width, rows), bf16), ((width, rows), bf16), ((8 *...  1.39 us
    pallas_call x1, Pallas kernels, local(): call(start_kernel, [sent_out, tile_out], [HBM] * 4, 600000, 250000, [pltp...  1.08 us
    pallas_call x1, Pallas kernels, local(): call(lambda *refs: finish_kernel(total, *refs), [((comps, S, rows), f32),...  1.02 us
    pallas_call x2, Pallas kernels, local(): call(lambda *refs, step=step: middle_kernel(step, *refs), [sent_out, tile...  0.93 us
  transfers between devices with their start and end apart: 23, of which 10 were waited for; matrix products, arithmetic and copies ran while one was open for 0% of the time, Pallas kernels for 5%

profile of v9, /device:TPU:0, one launch (start us, length us, event | category | flops | bytes accessed | tf_op | source)
XLA Modules:
  0.0 41.8 jit_solution(15606159778702028190)
XLA Ops:
  0.6 1.1 %shard_map.86 = (f32[16,128]{1,0:T(8,128)S(1)}, f32[24,128]{1,0:T(8,128)S(1)}) custom-call(f32[3,32,512]{2,1,0:T(8,128)} %refs_1_.1, f32[3,32]{1,0:T(4,128)} %mix_in.1, s32[1,4,8]{2,1,0:T(4,128)} %list_in.1, s32[1,4]{1,0:T(1,128)} %count_in.1), custom_call_target="tpu_custom_call" | custom-call | flops 600000 | bytes 250000 | tf_op jit(solution)/shard_map/pallas_call | solution.py:404
  1.7 0.5 %collective-permute-start.3 = (f32[16,128]{1,0:T(8,128)S(1)}, f32[16,128]{1,0:T(8,128)S(1)}, u32[]{:S(2)}, u32[]{:S(2)}) collective-permute-start(f32[16,128]{1,0:T(8,128)S(1)} %get-tuple-element.24), channel_id=1, source_target_pairs={{0,1},{1,2},{2,0},{3,4},{4,3},{5,6},{6,5},{7,8},{8,7},{9,10},{10,9... | collective-permute-start | bytes 24584 | tf_op jit(solution)/shard_map/ppermute | solution.py:353
  2.2 4.3 %collective-permute-start.2 = (f32[16,128]{1,0:T(8,128)S(1)}, f32[16,128]{1,0:T(8,128)S(1)}, u32[]{:S(2)}, u32[]{:S(2)}) collective-permute-start(f32[16,128]{1,0:T(8,128)S(1)} %get-tuple-element.24), channel_id=1, source_target_pairs={{0,8},{1,9},{2,10},{3,11},{4,12},{5,13},{6,14},{7,15},{8,0},{9,1},... | collective-permute-start | bytes 24584 | tf_op jit(solution)/shard_map/ppermute | solution.py:353
  6.6 0.7 %collective-permute-start.1 = (f32[16,128]{1,0:T(8,128)S(1)}, f32[16,128]{1,0:T(8,128)S(1)}, u32[]{:S(2)}, u32[]{:S(2)}) collective-permute-start(f32[16,128]{1,0:T(8,128)S(1)} %get-tuple-element.24), channel_id=1, source_target_pairs={{0,3},{1,2},{2,1},{3,0},{4,5},{5,4},{6,7},{7,6},{8,16},{9,17},{10,... | collective-permute-start | bytes 24584 | tf_op jit(solution)/shard_map/ppermute | solution.py:353
  7.2 0.0 collective-permute-start
  7.2 1.4 %shard_map.87 = (bf16[256,512]{1,0:T(8,128)(2,1)S(1)}, bf16[256,512]{1,0:T(8,128)(2,1)S(1)}, f32[40,128]{1,0:T(8,128)S(1)}) custom-call(f32[512,256]{1,0:T(8,128)} %strips_in.1, s32[4,8]{1,0:T(4,128)} %bitcast.2, f32[4]{0:T(128)} %shifts_in.1), custom_call_target="tpu_custom_call" | custom-call | flops 1000000 | bytes 1000000 | tf_op jit(solution)/shard_map/pallas_call | solution.py:418
  8.6 0.0 collective-permute-done.3.refs_4_
  8.6 0.0 collective-permute-done.2.refs_3_
  8.6 1.0 %collective-permute-done.1.refs_2_ = f32[16,128]{1,0:T(8,128)S(1)} collective-permute-done((f32[16,128]{1,0:T(8,128)S(1)}, f32[16,128]{1,0:T(8,128)S(1)}, u32[]{:S(2)}, u32[]{:S(2)}) %collective-permute-start.1) | collective-permute-done | bytes 8224 | tf_op jit(solution)/shard_map/ppermute | solution.py:353
  9.6 0.0 collective-permute-done.refs_1_
  9.6 0.5 %shard_map.88 = (f32[16,128]{1,0:T(8,128)S(1)}, f32[24,128]{1,0:T(8,128)S(1)}, bf16[96,128]{1,0:T(8,128)(2,1)S(1)}) custom-call(f32[24,128]{1,0:T(8,128)S(1)} %get-tuple-element.23.refs_0_, f32[16,128]{1,0:T(8,128)S(1)} %collective-permute-done.refs_1_, f32[16,128]{1,0:T(8,128)S(1)} %collective-permute-done.1.refs_2_, ...), custom_call_target="tpu_custom_call" | custom-call | flops 50000000 | bytes 600000 | tf_op jit(solution)/shard_map/pallas_call | solution.py:433
  10.2 0.0 collective-permute-start.7
  10.2 1.9 %collective-permute-start.6 = (f32[16,128]{1,0:T(8,128)S(1)}, f32[16,128]{1,0:T(8,128)S(1)}, u32[]{:S(2)}, u32[]{:S(2)}) collective-permute-start(f32[16,128]{1,0:T(8,128)S(1)} %get-tuple-element.29), channel_id=1, source_target_pairs={{0,8},{1,9},{2,10},{3,11},{4,12},{5,13},{6,14},{7,15},{8,0},{9,1},... | collective-permute-start | bytes 24584 | tf_op jit(solution)/shard_map/ppermute | solution.py:353
  12.1 1.3 %collective-permute-start.5 = (f32[16,128]{1,0:T(8,128)S(1)}, f32[16,128]{1,0:T(8,128)S(1)}, u32[]{:S(2)}, u32[]{:S(2)}) collective-permute-start(f32[16,128]{1,0:T(8,128)S(1)} %get-tuple-element.29), channel_id=1, source_target_pairs={{0,3},{1,2},{2,1},{3,0},{4,5},{5,4},{6,7},{7,6},{8,16},{9,17},{10,... | collective-permute-start | bytes 24584 | tf_op jit(solution)/shard_map/ppermute | solution.py:353
  13.4 0.5 %collective-permute-start.4 = (f32[16,128]{1,0:T(8,128)S(1)}, f32[16,128]{1,0:T(8,128)S(1)}, u32[]{:S(2)}, u32[]{:S(2)}) collective-permute-start(f32[16,128]{1,0:T(8,128)S(1)} %get-tuple-element.29), channel_id=1, source_target_pairs={{0,1},{1,0},{2,3},{3,2},{4,5},{5,4},{6,7},{7,6},{8,9},{9,8},{10,11... | collective-permute-start | bytes 24584 | tf_op jit(solution)/shard_map/ppermute | solution.py:353
  14.0 0.0 collective-permute-done.7.refs_4_
  14.0 0.0 collective-permute-done.6.refs_3_
  14.0 1.2 %collective-permute-done.5.refs_2_ = f32[16,128]{1,0:T(8,128)S(1)} collective-permute-done((f32[16,128]{1,0:T(8,128)S(1)}, f32[16,128]{1,0:T(8,128)S(1)}, u32[]{:S(2)}, u32[]{:S(2)}) %collective-permute-start.5) | collective-permute-done | bytes 8224 | tf_op jit(solution)/shard_map/ppermute | solution.py:353
  15.2 0.0 collective-permute-done.4.refs_1_
  15.2 0.5 %shard_map.89 = (f32[16,128]{1,0:T(8,128)S(1)}, f32[24,128]{1,0:T(8,128)S(1)}) custom-call(f32[24,128]{1,0:T(8,128)S(1)} %get-tuple-element.28.refs_0_.t0, f32[16,128]{1,0:T(8,128)S(1)} %collective-permute-done.4.refs_1_, f32[16,128]{1,0:T(8,128)S(1)} %collective-permute-done.5.refs_2_, f32[16,128]{1,0:T(8,128)S(1)} %collective-permute-done.6.refs_3_, ...), custom_call_target="tpu_custom_call" | custom-call | flops 50000000 | bytes 600000 | tf_op jit(solution)/shard_map/pallas_call | solution.py:442
  15.7 0.2 collective-permute-start.11
  15.9 3.1 %collective-permute-start.10 = (f32[16,128]{1,0:T(8,128)S(1)}, f32[16,128]{1,0:T(8,128)S(1)}, u32[]{:S(2)}, u32[]{:S(2)}) collective-permute-start(f32[16,128]{1,0:T(8,128)S(1)} %get-tuple-element.32), channel_id=1, source_target_pairs={{0,8},{1,9},{2,10},{3,11},{4,12},{5,13},{6,14},{7,15},{8,0},{9,1},... | collective-permute-start | bytes 24584 | tf_op jit(solution)/shard_map/ppermute | solution.py:353
  19.0 0.4 collective-permute-start.9
  19.4 0.0 collective-permute-start.8
  19.4 0.0 collective-permute-done.11.refs_4_
  19.4 1.3 %collective-permute-done.10.refs_3_ = f32[16,128]{1,0:T(8,128)S(1)} collective-permute-done((f32[16,128]{1,0:T(8,128)S(1)}, f32[16,128]{1,0:T(8,128)S(1)}, u32[]{:S(2)}, u32[]{:S(2)}) %collective-permute-start.10) | collective-permute-done | bytes 8224 | tf_op jit(solution)/shard_map/ppermute | solution.py:353
  20.7 1.4 %collective-permute-done.9.refs_2_ = f32[16,128]{1,0:T(8,128)S(1)} collective-permute-done((f32[16,128]{1,0:T(8,128)S(1)}, f32[16,128]{1,0:T(8,128)S(1)}, u32[]{:S(2)}, u32[]{:S(2)}) %collective-permute-start.9) | collective-permute-done | bytes 8224 | tf_op jit(solution)/shard_map/ppermute | solution.py:353
  22.1 0.0 collective-permute-done.8.refs_1_
  22.1 0.0 copy-start
  22.1 0.5 %shard_map.90 = (f32[16,128]{1,0:T(8,128)S(1)}, f32[24,128]{1,0:T(8,128)S(1)}) custom-call(f32[24,128]{1,0:T(8,128)S(1)} %get-tuple-element.31.refs_0_.t1, f32[16,128]{1,0:T(8,128)S(1)} %collective-permute-done.8.refs_1_, f32[16,128]{1,0:T(8,128)S(1)} %collective-permute-done.9.refs_2_, f32[16,128]{1,0:T(8,128)S(1)} %collective-permute-done.10.refs_3_, ...), custom_call_target="tpu_custom_call" | custom-call | flops 50000000 | bytes 600000 | tf_op jit(solution)/shard_map/pallas_call | solution.py:442
  22.5 0.0 collective-permute-start.15
  22.5 1.8 %collective-permute-start.14 = (f32[16,128]{1,0:T(8,128)S(1)}, f32[16,128]{1,0:T(8,128)S(1)}, u32[]{:S(2)}, u32[]{:S(2)}) collective-permute-start(f32[16,128]{1,0:T(8,128)S(1)} %get-tuple-element.34), channel_id=1, source_target_pairs={{0,8},{1,9},{2,10},{3,11},{4,12},{5,13},{6,14},{7,15},{8,0},{9,1},... | collective-permute-start | bytes 24584 | tf_op jit(solution)/shard_map/ppermute | solution.py:353
  24.4 1.3 %collective-permute-start.13 = (f32[16,128]{1,0:T(8,128)S(1)}, f32[16,128]{1,0:T(8,128)S(1)}, u32[]{:S(2)}, u32[]{:S(2)}) collective-permute-start(f32[16,128]{1,0:T(8,128)S(1)} %get-tuple-element.34), channel_id=1, source_target_pairs={{0,3},{1,2},{2,1},{3,0},{4,5},{5,4},{6,7},{7,6},{8,16},{9,17},{10,... | collective-permute-start | bytes 24584 | tf_op jit(solution)/shard_map/ppermute | solution.py:353
  25.6 0.0 collective-permute-start.12
  25.6 0.0 copy-done
  25.6 0.6 %shard_map.91 = (f32[24,512]{1,0:T(8,128)S(1)}, f32[24,128]{1,0:T(8,128)S(1)}, bf16[512,128]{1,0:T(8,128)(2,1)S(1)}, bf16[512,128]{1,0:T(8,128)(2,1)S(1)}, bf16[512,128]{1,0:T(8,128)(2,1)S(1)}) custom-call(f32[3,32,512]{2,1,0:T(8,128)S(1)} %copy-done, f32[24,128]{1,0:T(8,128)S(1)} %get-tuple-element.28.refs_0_.t0, ...), custom_call_target="tpu_custom_call" | custom-call | flops 60000000 | bytes 250000 | tf_op jit(solution)/shard_map/pallas_call | solution.py:452
  26.2 0.0 collective-permute-done.15.refs_4_
  26.2 0.0 collective-permute-done.14.refs_3_
  26.3 1.2 %collective-permute-done.13.refs_2_ = f32[16,128]{1,0:T(8,128)S(1)} collective-permute-done((f32[16,128]{1,0:T(8,128)S(1)}, f32[16,128]{1,0:T(8,128)S(1)}, u32[]{:S(2)}, u32[]{:S(2)}) %collective-permute-start.13) | collective-permute-done | bytes 8224 | tf_op jit(solution)/shard_map/ppermute | solution.py:353
  27.4 0.0 collective-permute-done.12.refs_1_
  27.4 0.7 %shard_map.92 = (f32[8,512]{1,0:T(8,128)S(1)}, f32[24,128]{1,0:T(8,128)S(1)}) custom-call(f32[24,128]{1,0:T(8,128)S(1)} %get-tuple-element.33.t2.refs_0_, f32[16,128]{1,0:T(8,128)S(1)} %collective-permute-done.12.refs_1_, f32[16,128]{1,0:T(8,128)S(1)} %collective-permute-done.13.refs_2_, f32[16,128]{1,0:T(8,128)S(1)} %collective-permute-done.14.refs_3_, ...), custom_call_target="tpu_custom_call" | custom-call | flops 80000000 | bytes 900000 | tf_op jit(solution)/shard_map/pallas_call | solution.py:459
  28.1 0.1 collective-permute-start.16
  28.2 1.2 %collective-permute-done.16 = f32[24,128]{1,0:T(8,128)S(1)} collective-permute-done((f32[24,128]{1,0:T(8,128)S(1)}, f32[24,128]{1,0:T(8,128)S(1)}, u32[]{:S(2)}, u32[]{:S(2)}) %collective-permute-start.16) | collective-permute-done | bytes 12320 | tf_op jit(solution)/shard_map/ppermute | solution.py:353
  29.4 0.7 %collective-permute-start.19 = (f32[24,128]{1,0:T(8,128)S(1)}, f32[24,128]{1,0:T(8,128)S(1)}, u32[]{:S(2)}, u32[]{:S(2)}) collective-permute-start(f32[24,128]{1,0:T(8,128)S(1)} %add.21), channel_id=1, source_target_pairs={{0,7},{1,6},{2,5},{3,4},{4,3},{5,2},{6,1},{7,0},{8,15},{9,14},{10,... | collective-permute-start | bytes 36872 | tf_op jit(solution)/shard_map/ppermute | solution.py:353
  30.0 1.8 %collective-permute-start.18 = (f32[24,128]{1,0:T(8,128)S(1)}, f32[24,128]{1,0:T(8,128)S(1)}, u32[]{:S(2)}, u32[]{:S(2)}) collective-permute-start(f32[24,128]{1,0:T(8,128)S(1)} %add.21), channel_id=1, source_target_pairs={{0,5},{1,4},{2,7},{3,6},{4,1},{5,0},{6,3},{7,2},{8,13},{9,12},{10,... | collective-permute-start | bytes 36872 | tf_op jit(solution)/shard_map/ppermute | solution.py:353
  31.9 0.5 %collective-permute-start.17 = (f32[24,128]{1,0:T(8,128)S(1)}, f32[24,128]{1,0:T(8,128)S(1)}, u32[]{:S(2)}, u32[]{:S(2)}) collective-permute-start(f32[24,128]{1,0:T(8,128)S(1)} %add.21), channel_id=1, source_target_pairs={{0,3},{1,2},{2,1},{3,0},{4,7},{5,6},{6,5},{7,4},{8,11},{9,10},{10,... | collective-permute-start | bytes 36872 | tf_op jit(solution)/shard_map/ppermute | solution.py:353
  32.3 1.0 %collective-permute-done.19 = f32[24,128]{1,0:T(8,128)S(1)} collective-permute-done((f32[24,128]{1,0:T(8,128)S(1)}, f32[24,128]{1,0:T(8,128)S(1)}, u32[]{:S(2)}, u32[]{:S(2)}) %collective-permute-start.19) | collective-permute-done | bytes 12320 | tf_op jit(solution)/shard_map/ppermute | solution.py:353
  33.4 0.0 collective-permute-done.18
  33.4 1.6 %collective-permute-done.17 = f32[24,128]{1,0:T(8,128)S(1)} collective-permute-done((f32[24,128]{1,0:T(8,128)S(1)}, f32[24,128]{1,0:T(8,128)S(1)}, u32[]{:S(2)}, u32[]{:S(2)}) %collective-permute-start.17) | collective-permute-done | bytes 12320 | tf_op jit(solution)/shard_map/ppermute | solution.py:353
  35.0 0.7 %collective-permute-start.22 = (f32[24,128]{1,0:T(8,128)S(1)}, f32[24,128]{1,0:T(8,128)S(1)}, u32[]{:S(2)}, u32[]{:S(2)}) collective-permute-start(f32[24,128]{1,0:T(8,128)S(1)} %add_add_fusion.1), channel_id=1, source_target_pairs={{0,25},{1,24},{2,27},{3,26},{4,29},{5,28},{6,31},{7,30},{8,17},{9,... | collective-permute-start | bytes 36872 | tf_op jit(solution)/shard_map/ppermute | solution.py:353
  35.7 2.0 %collective-permute-start.21 = (f32[24,128]{1,0:T(8,128)S(1)}, f32[24,128]{1,0:T(8,128)S(1)}, u32[]{:S(2)}, u32[]{:S(2)}) collective-permute-start(f32[24,128]{1,0:T(8,128)S(1)} %add_add_fusion.1), channel_id=1, source_target_pairs={{0,17},{1,16},{2,19},{3,18},{4,21},{5,20},{6,23},{7,22},{8,25},{9,... | collective-permute-start | bytes 36872 | tf_op jit(solution)/shard_map/ppermute | solution.py:353
  37.7 1.4 %collective-permute-start.20 = (f32[24,128]{1,0:T(8,128)S(1)}, f32[24,128]{1,0:T(8,128)S(1)}, u32[]{:S(2)}, u32[]{:S(2)}) collective-permute-start(f32[24,128]{1,0:T(8,128)S(1)} %add_add_fusion.1), channel_id=1, source_target_pairs={{0,9},{1,8},{2,11},{3,10},{4,13},{5,12},{6,15},{7,14},{8,1},{9,0},... | collective-permute-start | bytes 36872 | tf_op jit(solution)/shard_map/ppermute | solution.py:353
  39.1 0.9 %collective-permute-done.22 = f32[24,128]{1,0:T(8,128)S(1)} collective-permute-done((f32[24,128]{1,0:T(8,128)S(1)}, f32[24,128]{1,0:T(8,128)S(1)}, u32[]{:S(2)}, u32[]{:S(2)}) %collective-permute-start.22) | collective-permute-done | bytes 12320 | tf_op jit(solution)/shard_map/ppermute | solution.py:353
  39.9 0.0 collective-permute-done.21
  39.9 0.9 %collective-permute-done.20 = f32[24,128]{1,0:T(8,128)S(1)} collective-permute-done((f32[24,128]{1,0:T(8,128)S(1)}, f32[24,128]{1,0:T(8,128)S(1)}, u32[]{:S(2)}, u32[]{:S(2)}) %collective-permute-start.20) | collective-permute-done | bytes 12320 | tf_op jit(solution)/shard_map/ppermute | solution.py:353
  40.8 1.0 %shard_map.93 = (f32[3,4,512]{2,1,0:T(4,128)}, f32[3,4,36]{2,1,0:T(4,128)}) custom-call(f32[24,128]{1,0:T(8,128)S(1)} %add_add_fusion.refs_0_, f32[3,32,512]{2,1,0:T(8,128)S(1)} %copy-done, f32[24,512]{1,0:T(8,128)S(1)} %get-tuple-element.40.refs_2_, f32[8,512]{1,0:T(8,128)S(1)} %get-tuple-element.41.refs_3_), custom_call_target="tpu_custom_call" | custom-call | flops 50000000 | bytes 400000 | tf_op jit(solution)/shard_map/pallas_call | solution.py:467
  (3 shorter events, 0.0 us)
Async XLA Ops:
  1.7 6.9 %collective-permute-start.3 = (f32[16,128]{1,0:T(8,128)S(1)}, f32[16,128]{1,0:T(8,128)S(1)}, u32[]{:S(2)}, u32[]{:S(2)}) collective-permute-start(f32[16,128]{1,0:T(8,128)S(1)} %get-tuple-element.24), channel_id=1, source_target_pairs={{0,1},{1,2},{2,0},{3,4},{4,3},{5,6},{6,5},{7,8},{8,7},{9,10},{10,9... | collective-permute-start | bytes 24584 | tf_op jit(solution)/shard_map/ppermute | solution.py:353
  2.2 6.4 %collective-permute-start.2 = (f32[16,128]{1,0:T(8,128)S(1)}, f32[16,128]{1,0:T(8,128)S(1)}, u32[]{:S(2)}, u32[]{:S(2)}) collective-permute-start(f32[16,128]{1,0:T(8,128)S(1)} %get-tuple-element.24), channel_id=1, source_target_pairs={{0,8},{1,9},{2,10},{3,11},{4,12},{5,13},{6,14},{7,15},{8,0},{9,1},... | collective-permute-start | bytes 24584 | tf_op jit(solution)/shard_map/ppermute | solution.py:353
  6.6 3.1 %collective-permute-start.1 = (f32[16,128]{1,0:T(8,128)S(1)}, f32[16,128]{1,0:T(8,128)S(1)}, u32[]{:S(2)}, u32[]{:S(2)}) collective-permute-start(f32[16,128]{1,0:T(8,128)S(1)} %get-tuple-element.24), channel_id=1, source_target_pairs={{0,3},{1,2},{2,1},{3,0},{4,5},{5,4},{6,7},{7,6},{8,16},{9,17},{10,... | collective-permute-start | bytes 24584 | tf_op jit(solution)/shard_map/ppermute | solution.py:353
  7.2 2.4 %collective-permute-start = (f32[16,128]{1,0:T(8,128)S(1)}, f32[16,128]{1,0:T(8,128)S(1)}, u32[]{:S(2)}, u32[]{:S(2)}) collective-permute-start(f32[16,128]{1,0:T(8,128)S(1)} %get-tuple-element.24), channel_id=1, source_target_pairs={{0,1},{1,0},{2,3},{3,2},{4,5},{5,4},{6,7},{7,6},{8,9},{9,8},{10,11... | collective-permute-start | bytes 24584 | tf_op jit(solution)/shard_map/ppermute | solution.py:353
  10.2 3.8 %collective-permute-start.7 = (f32[16,128]{1,0:T(8,128)S(1)}, f32[16,128]{1,0:T(8,128)S(1)}, u32[]{:S(2)}, u32[]{:S(2)}) collective-permute-start(f32[16,128]{1,0:T(8,128)S(1)} %get-tuple-element.29), channel_id=1, source_target_pairs={{0,1},{1,2},{2,0},{3,4},{4,3},{5,6},{6,5},{7,8},{8,7},{9,10},{10,9... | collective-permute-start | bytes 24584 | tf_op jit(solution)/shard_map/ppermute | solution.py:353
  10.2 3.8 %collective-permute-start.6 = (f32[16,128]{1,0:T(8,128)S(1)}, f32[16,128]{1,0:T(8,128)S(1)}, u32[]{:S(2)}, u32[]{:S(2)}) collective-permute-start(f32[16,128]{1,0:T(8,128)S(1)} %get-tuple-element.29), channel_id=1, source_target_pairs={{0,8},{1,9},{2,10},{3,11},{4,12},{5,13},{6,14},{7,15},{8,0},{9,1},... | collective-permute-start | bytes 24584 | tf_op jit(solution)/shard_map/ppermute | solution.py:353
  12.1 3.1 %collective-permute-start.5 = (f32[16,128]{1,0:T(8,128)S(1)}, f32[16,128]{1,0:T(8,128)S(1)}, u32[]{:S(2)}, u32[]{:S(2)}) collective-permute-start(f32[16,128]{1,0:T(8,128)S(1)} %get-tuple-element.29), channel_id=1, source_target_pairs={{0,3},{1,2},{2,1},{3,0},{4,5},{5,4},{6,7},{7,6},{8,16},{9,17},{10,... | collective-permute-start | bytes 24584 | tf_op jit(solution)/shard_map/ppermute | solution.py:353
  13.4 1.8 %collective-permute-start.4 = (f32[16,128]{1,0:T(8,128)S(1)}, f32[16,128]{1,0:T(8,128)S(1)}, u32[]{:S(2)}, u32[]{:S(2)}) collective-permute-start(f32[16,128]{1,0:T(8,128)S(1)} %get-tuple-element.29), channel_id=1, source_target_pairs={{0,1},{1,0},{2,3},{3,2},{4,5},{5,4},{6,7},{7,6},{8,9},{9,8},{10,11... | collective-permute-start | bytes 24584 | tf_op jit(solution)/shard_map/ppermute | solution.py:353
  15.7 3.7 %collective-permute-start.11 = (f32[16,128]{1,0:T(8,128)S(1)}, f32[16,128]{1,0:T(8,128)S(1)}, u32[]{:S(2)}, u32[]{:S(2)}) collective-permute-start(f32[16,128]{1,0:T(8,128)S(1)} %get-tuple-element.32), channel_id=1, source_target_pairs={{0,1},{1,2},{2,0},{3,4},{4,3},{5,6},{6,5},{7,8},{8,7},{9,10},{10,9... | collective-permute-start | bytes 24584 | tf_op jit(solution)/shard_map/ppermute | solution.py:353
  15.9 4.8 %collective-permute-start.10 = (f32[16,128]{1,0:T(8,128)S(1)}, f32[16,128]{1,0:T(8,128)S(1)}, u32[]{:S(2)}, u32[]{:S(2)}) collective-permute-start(f32[16,128]{1,0:T(8,128)S(1)} %get-tuple-element.32), channel_id=1, source_target_pairs={{0,8},{1,9},{2,10},{3,11},{4,12},{5,13},{6,14},{7,15},{8,0},{9,1},... | collective-permute-start | bytes 24584 | tf_op jit(solution)/shard_map/ppermute | solution.py:353
  19.0 3.1 %collective-permute-start.9 = (f32[16,128]{1,0:T(8,128)S(1)}, f32[16,128]{1,0:T(8,128)S(1)}, u32[]{:S(2)}, u32[]{:S(2)}) collective-permute-start(f32[16,128]{1,0:T(8,128)S(1)} %get-tuple-element.32), channel_id=1, source_target_pairs={{0,3},{1,2},{2,1},{3,0},{4,5},{5,4},{6,7},{7,6},{8,16},{9,17},{10,... | collective-permute-start | bytes 24584 | tf_op jit(solution)/shard_map/ppermute | solution.py:353
  19.4 2.7 %collective-permute-start.8 = (f32[16,128]{1,0:T(8,128)S(1)}, f32[16,128]{1,0:T(8,128)S(1)}, u32[]{:S(2)}, u32[]{:S(2)}) collective-permute-start(f32[16,128]{1,0:T(8,128)S(1)} %get-tuple-element.32), channel_id=1, source_target_pairs={{0,1},{1,0},{2,3},{3,2},{4,5},{5,4},{6,7},{7,6},{8,9},{9,8},{10,11... | collective-permute-start | bytes 24584 | tf_op jit(solution)/shard_map/ppermute | solution.py:353
  22.1 3.6 %copy-start = (f32[3,32,512]{2,1,0:T(8,128)S(1)}, f32[3,32,512]{2,1,0:T(8,128)}, u32[]{:S(2)}) copy-start(f32[3,32,512]{2,1,0:T(8,128)} %refs_1_.1) | copy-start | bytes 589828
  22.5 3.7 %collective-permute-start.15 = (f32[16,128]{1,0:T(8,128)S(1)}, f32[16,128]{1,0:T(8,128)S(1)}, u32[]{:S(2)}, u32[]{:S(2)}) collective-permute-start(f32[16,128]{1,0:T(8,128)S(1)} %get-tuple-element.34), channel_id=1, source_target_pairs={{0,1},{1,2},{2,0},{3,4},{4,3},{5,6},{6,5},{7,8},{8,7},{9,10},{10,9... | collective-permute-start | bytes 24584 | tf_op jit(solution)/shard_map/ppermute | solution.py:353
  22.5 3.7 %collective-permute-start.14 = (f32[16,128]{1,0:T(8,128)S(1)}, f32[16,128]{1,0:T(8,128)S(1)}, u32[]{:S(2)}, u32[]{:S(2)}) collective-permute-start(f32[16,128]{1,0:T(8,128)S(1)} %get-tuple-element.34), channel_id=1, source_target_pairs={{0,8},{1,9},{2,10},{3,11},{4,12},{5,13},{6,14},{7,15},{8,0},{9,1},... | collective-permute-start | bytes 24584 | tf_op jit(solution)/shard_map/ppermute | solution.py:353
  24.4 3.1 %collective-permute-start.13 = (f32[16,128]{1,0:T(8,128)S(1)}, f32[16,128]{1,0:T(8,128)S(1)}, u32[]{:S(2)}, u32[]{:S(2)}) collective-permute-start(f32[16,128]{1,0:T(8,128)S(1)} %get-tuple-element.34), channel_id=1, source_target_pairs={{0,3},{1,2},{2,1},{3,0},{4,5},{5,4},{6,7},{7,6},{8,16},{9,17},{10,... | collective-permute-start | bytes 24584 | tf_op jit(solution)/shard_map/ppermute | solution.py:353
  25.6 1.8 %collective-permute-start.12 = (f32[16,128]{1,0:T(8,128)S(1)}, f32[16,128]{1,0:T(8,128)S(1)}, u32[]{:S(2)}, u32[]{:S(2)}) collective-permute-start(f32[16,128]{1,0:T(8,128)S(1)} %get-tuple-element.34), channel_id=1, source_target_pairs={{0,1},{1,0},{2,3},{3,2},{4,5},{5,4},{6,7},{7,6},{8,9},{9,8},{10,11... | collective-permute-start | bytes 24584 | tf_op jit(solution)/shard_map/ppermute | solution.py:353
  28.1 1.2 %collective-permute-start.16 = (f32[24,128]{1,0:T(8,128)S(1)}, f32[24,128]{1,0:T(8,128)S(1)}, u32[]{:S(2)}, u32[]{:S(2)}) collective-permute-start(f32[24,128]{1,0:T(8,128)S(1)} %get-tuple-element.39), channel_id=1, source_target_pairs={{0,1},{1,0},{2,3},{3,2},{4,5},{5,4},{6,7},{7,6},{8,9},{9,8},{10,11... | collective-permute-start | bytes 36872 | tf_op jit(solution)/shard_map/ppermute | solution.py:353
  29.4 4.0 %collective-permute-start.19 = (f32[24,128]{1,0:T(8,128)S(1)}, f32[24,128]{1,0:T(8,128)S(1)}, u32[]{:S(2)}, u32[]{:S(2)}) collective-permute-start(f32[24,128]{1,0:T(8,128)S(1)} %add.21), channel_id=1, source_target_pairs={{0,7},{1,6},{2,5},{3,4},{4,3},{5,2},{6,1},{7,0},{8,15},{9,14},{10,... | collective-permute-start | bytes 36872 | tf_op jit(solution)/shard_map/ppermute | solution.py:353
  30.0 3.3 %collective-permute-start.18 = (f32[24,128]{1,0:T(8,128)S(1)}, f32[24,128]{1,0:T(8,128)S(1)}, u32[]{:S(2)}, u32[]{:S(2)}) collective-permute-start(f32[24,128]{1,0:T(8,128)S(1)} %add.21), channel_id=1, source_target_pairs={{0,5},{1,4},{2,7},{3,6},{4,1},{5,0},{6,3},{7,2},{8,13},{9,12},{10,... | collective-permute-start | bytes 36872 | tf_op jit(solution)/shard_map/ppermute | solution.py:353
  31.9 3.1 %collective-permute-start.17 = (f32[24,128]{1,0:T(8,128)S(1)}, f32[24,128]{1,0:T(8,128)S(1)}, u32[]{:S(2)}, u32[]{:S(2)}) collective-permute-start(f32[24,128]{1,0:T(8,128)S(1)} %add.21), channel_id=1, source_target_pairs={{0,3},{1,2},{2,1},{3,0},{4,7},{5,6},{6,5},{7,4},{8,11},{9,10},{10,... | collective-permute-start | bytes 36872 | tf_op jit(solution)/shard_map/ppermute | solution.py:353
  35.0 4.9 %collective-permute-start.22 = (f32[24,128]{1,0:T(8,128)S(1)}, f32[24,128]{1,0:T(8,128)S(1)}, u32[]{:S(2)}, u32[]{:S(2)}) collective-permute-start(f32[24,128]{1,0:T(8,128)S(1)} %add_add_fusion.1), channel_id=1, source_target_pairs={{0,25},{1,24},{2,27},{3,26},{4,29},{5,28},{6,31},{7,30},{8,17},{9,... | collective-permute-start | bytes 36872 | tf_op jit(solution)/shard_map/ppermute | solution.py:353
  35.7 4.3 %collective-permute-start.21 = (f32[24,128]{1,0:T(8,128)S(1)}, f32[24,128]{1,0:T(8,128)S(1)}, u32[]{:S(2)}, u32[]{:S(2)}) collective-permute-start(f32[24,128]{1,0:T(8,128)S(1)} %add_add_fusion.1), channel_id=1, source_target_pairs={{0,17},{1,16},{2,19},{3,18},{4,21},{5,20},{6,23},{7,22},{8,25},{9,... | collective-permute-start | bytes 36872 | tf_op jit(solution)/shard_map/ppermute | solution.py:353
  37.7 3.1 %collective-permute-start.20 = (f32[24,128]{1,0:T(8,128)S(1)}, f32[24,128]{1,0:T(8,128)S(1)}, u32[]{:S(2)}, u32[]{:S(2)}) collective-permute-start(f32[24,128]{1,0:T(8,128)S(1)} %add_add_fusion.1), channel_id=1, source_target_pairs={{0,9},{1,8},{2,11},{3,10},{4,13},{5,12},{6,15},{7,14},{8,1},{9,0},... | collective-permute-start | bytes 36872 | tf_op jit(solution)/shard_map/ppermute | solution.py:353

commit v10 on v7

--- a/solution.py
+++ b/solution.py
@@ -21,6 +21,22 @@
 
 def iota(shape, axis):
     return lax.broadcasted_iota(jnp.int32, shape, axis)
+
+
+PLACES = {
+    (0, 0): (0, 0),
+    (0, 1): (0, 32),
+    (0, 2): (0, 56),
+    (0, 3): (0, 72),
+    (1, 0): (0, 80),
+    (1, 2): (0, 112),
+    (1, 1): (1, 0),
+    (1, 3): (1, 24),
+    (2, 0): (1, 32),
+    (2, 1): (1, 64),
+    (2, 2): (1, 88),
+    (2, 3): (1, 104),
+}
 
 
 def own_lanes(rows, width):
@@ -51,6 +67,15 @@
         parts.append(x.astype(jnp.bfloat16))
         x = x - parts[-1].astype(jnp.float32)
     return parts
+
+
+def split_dot(x, parts):
+    left = [part.astype(jnp.float32) for part in split(x)]
+    left.append(jnp.zeros((-3 * x.shape[0] % 16, x.shape[1]), jnp.float32))
+    left = jnp.concatenate([part for part in left if part.shape[0]], axis=0).astype(jnp.bfloat16)
+    products = dot(left, parts[0]) + dot(left, parts[1]) + dot(left, parts[2])
+    rows = x.shape[0]
+    return products[:rows] + (products[rows : 2 * rows] + products[2 * rows : 3 * rows])
 
 
 def fetch(pairs, sems):
@@ -119,7 +144,7 @@
 def selection(table, metas, place, length):
     even, even_far = lax.rem(place, 2) == 0, lax.rem(place // FAR, 2) == 0
     near, far_odd, far_even, across = metas
-    moved = (place == 1) | (place == length - 2)
+    moved = (place == 2) | (place == length - 3)
     across = jnp.where(moved, far_odd, across)
     circle = jnp.where(moved, 48.0, 96.0)
     slots = [
@@ -187,55 +212,54 @@
     return jnp.sum(jnp.where(mine, gram, 0.0), axis=0, keepdims=True)
 
 
-def early_kernel(prev_ref, t0, t1, t2, lines_ref, gram_ref, *turned_refs):
+def early_kernel(prev_ref, t0, t1, t2, lines_ref, gram_ref, *split_refs):
     comps, vecs, rows = prev_ref.shape
     width = comps * vecs
     lines = jnp.concatenate([lines_of(t[...], rows) for t in (t0, t1, t2)], axis=0)
     lines_ref[...] = lines
     prev = prev_ref[...].reshape(width, rows)
     full = dot(prev, prev, NT, HIGHEST)
-    owner = iota((vecs, width), 1) // vecs
-    total = jnp.where(owner == 0, full[:vecs], 0.0)
-    for c in range(1, comps):
-        total = total + jnp.where(owner == c, full[c * vecs : (c + 1) * vecs], 0.0)
-    gram_ref[:vecs, :] = jnp.concatenate([total, jnp.zeros((vecs, 128 - width), jnp.float32)], axis=1)
+    full = jnp.concatenate([full, jnp.zeros((width, 128 - width), jnp.float32)], axis=1)
+    lane = iota((8, 128), 1)
+    tiles = [jnp.zeros((8, 128), jnp.float32)] * 2
+    for (c, g), (t, first) in PLACES.items():
+        at = c * vecs + 8 * g
+        piece = pltpu.roll(full[at : at + 8], (first - at) % 128, 1)
+        tiles[t] = jnp.where((lane >= first) & (lane < first + vecs - 8 * g), piece, tiles[t])
+    gram_ref[:16, :] = jnp.concatenate(tiles, axis=0)
     against = jnp.concatenate([prev, lines, jnp.zeros((8, rows), jnp.float32)], axis=0)
-    for ref, part in zip(turned_refs, split(against.T)):
+    for ref, part in zip(split_refs, split(against.T) + split(prev)):
         ref[...] = part
     gram = dot(lines, against, NT, HIGHEST)
     result = jnp.zeros((8, 128), jnp.float32)
     for k in range(S - 1):
         line = collect(gram[k * 8 : (k + 1) * 8], width, vecs)
         result = jnp.where(iota((8, 128), 0) == k, jnp.broadcast_to(line, result.shape), result)
-    gram_ref[vecs:, :] = result
-
-
-def last_kernel(own, a, b, c, d, choose, aux, high, low, early, t0, t1, t2, line_ref, gram_ref):
+    gram_ref[16:, :] = result
+
+
+def last_kernel(vecs, own, a, b, c, d, choose, aux, high, low, early, t0, t1, t2, line_ref, gram_ref):
     pieces = [ref[...] for ref in (own, a, b, c, d)]
     tile = multiply(choose[...], pieces, aux[8 * S - 8 : 8 * S, :], high[...], low[...])
     rows = line_ref.shape[1]
-    vecs = early.shape[0] - 8
     width = COMPS * vecs
     last = lines_of(tile, rows)
     line_ref[...] = last
-    parts = [part.astype(jnp.float32) for part in split(last)]
-    left = jnp.concatenate(parts + [jnp.zeros_like(last)], axis=0).astype(jnp.bfloat16)
-    products = dot(left, t0[...]) + dot(left, t1[...]) + dot(left, t2[...])
-    gram = products[:8] + (products[8:16] + products[16:24])
+    gram = split_dot(last, (t0[...], t1[...], t2[...]))
     square = jnp.sum(last * last, axis=1, keepdims=True)
     gram = jnp.where(iota(gram.shape, 1) == width + 8 * (S - 1) + iota(gram.shape, 0), square, gram)
     line = collect(gram, width, vecs)
-    gram_ref[:vecs, :] = early[:vecs, :]
-    gram_ref[vecs:, :] = jnp.where(
-        iota((8, 128), 0) == S - 1, jnp.broadcast_to(line, (8, 128)), early[vecs:, :]
+    gram_ref[:16, :] = early[:16, :]
+    gram_ref[16:, :] = jnp.where(
+        iota((8, 128), 0) == S - 1, jnp.broadcast_to(line, (8, 128)), early[16:, :]
     )
 
 
-def finish_kernel(total, gram_in, prev_ref, lines, last, basis_ref, factors_ref):
-    comps, vecs, rows = prev_ref.shape
+def finish_kernel(total, vecs, gram_in, p0, p1, p2, lines, last, basis_ref, factors_ref):
+    comps = COMPS
     width = comps * vecs
     gram = gram_in[...] * (1.0 / total)
-    small = gram[vecs:]
+    small = gram[16:]
     lane, comp = iota((8, 128), 1), iota((8, 128), 0)
     in_prev = (lane < width) & (lane // vecs == comp)
     coef, cross = [], []
@@ -244,17 +268,23 @@
         coef.append(jnp.where(in_prev, line, 0.0))
         cross.append([jnp.where(lane == width + 8 * l + comp, line, 0.0) for l in range(k + 1)])
     coefs = jnp.concatenate(coef, axis=0)
-    square = jnp.concatenate([gram[:vecs]] * comps, axis=0)
-    r, q = iota(square.shape, 0), iota(square.shape, 1)
-    square = jnp.where(r // vecs == q // vecs, square, 0.0) - jnp.where(r == q, 2.0, 0.0)
-    turned = dot(coefs[:, :width], square, precision=HIGHEST)
-    prev = prev_ref[...].reshape(width, rows)
+    pieces = []
+    for c in range(comps):
+        for g in range(vecs // 8):
+            t, first = PLACES[c, g]
+            at = c * vecs + 8 * g
+            piece = pltpu.roll(gram[8 * t : 8 * t + 8], (at - first) % 128, 1)
+            piece = jnp.where(lane < at + 8, 0.5 * piece, piece)
+            piece = jnp.where((lane >= at) & (lane < (c + 1) * vecs), piece, 0.0)
+            pieces.append(piece - jnp.where(lane == at + comp, 1.0, 0.0))
+    half = split(jnp.concatenate(pieces, axis=0))
+    turned = split_dot(coefs[:, :width], half)
     basis = jnp.concatenate([lines[...], last[...]], axis=0)
-    projected = basis - dot(coefs[:, :width], prev, precision=HIGHEST)
+    projected = basis - split_dot(coefs[:, :width], (p0[...], p1[...], p2[...]))
     unit, scale = {}, {}
     for l in range(S):
         for k in range(l, S):
-            value = turned[k * 8 : (k + 1) * 8] * coef[l] + cross[k][l]
+            value = turned[k * 8 : (k + 1) * 8] * coef[l] + turned[l * 8 : (l + 1) * 8] * coef[k] + cross[k][l]
             value = jnp.sum(value, axis=1, keepdims=True)
             for m in range(l):
                 value = value - (unit[k, m] * scale[m]) * unit[l, m]
@@ -321,12 +351,12 @@
     last = length - 1
     near, across = neighbours(length, 1, 0), neighbours(length, 1, 1)
     far_even, far_odd = neighbours(length, FAR, 0), neighbours(length, FAR, 1)
-    across.update({0: 1, 1: 2, 2: 0, last: last - 1, last - 1: last - 2, last - 2: last})
+    across.update({0: 2, 2: 1, 1: 0, last: last - 2, last - 2: last - 1, last - 1: last})
     for d in range(length):
         if far_odd[d] is None:
             far_odd[d] = d ^ 1
-    far_odd.update({0: 3, 3: 0, 1: 2, 2: 1})
-    far_odd.update({last: last - 3, last - 3: last, last - 1: last - 2, last - 2: last - 1})
+    far_odd.update({1: 2, 2: 3, 3: 0, 0: 1})
+    far_odd.update({last - 1: last - 2, last - 2: last - 3, last - 3: last, last: last - 1})
     return [send(tile, target) for target in (near, far_odd, far_even, across)]
 
 
@@ -398,25 +428,29 @@
         )(tile, *ghosts(tile), choose, aux, high, low)
         tiles.append(tile)
     received = ghosts(tile)
-    gram_out = ((vecs + 8, 128), f32)
-    lines, early, *turned = call(
+    gram_out = ((24, 128), f32)
+    lines, early, *parts = call(
         early_kernel,
-        [((8 * S - 8, rows), f32), gram_out] + [((rows, 128), bf16)] * 3,
+        [((8 * S - 8, rows), f32), gram_out] + [((rows, 128), bf16)] * 3 + [((comps * vecs, rows), bf16)] * 3,
         [VMEM] * 4,
         60000000,
         250000,
     )(prev_basis, *tiles)
     last, gram = call(
-        last_kernel, [((8, rows), f32), gram_out], [VMEM] * 13, 80000000, 900000
-    )(tile, *received, choose, aux, high, low, early, *turned)
+        lambda *refs: last_kernel(vecs, *refs),
+        [((8, rows), f32), gram_out],
+        [VMEM] * 13,
+        80000000,
+        900000,
+    )(tile, *received, choose, aux, high, low, early, *parts[:3])
     total = float(length * rows)
     basis, factors = call(
-        lambda *refs: finish_kernel(total, *refs),
+        lambda *refs: finish_kernel(total, vecs, *refs),
         [((comps, S, rows), f32), ((comps, S, vecs + S), f32)],
-        [VMEM] * 4,
+        [VMEM] * 6,
         50000000,
         400000,
-    )(summed(gram), prev_basis, lines, last)
+    )(summed(gram), *parts[3:], lines, last)
     return basis, jnp.swapaxes(factors, 1, 2)
 
 

time: 42.5 us -> 41.4 us (0.974)
  starting transfers between devices: 23.2 us -> 21.1 us
  waiting for transfers between devices: 12.6 us -> 13.4 us
    ppermute x23, starting transfers between devices: 23.2 us -> 21.1 us  [send(): lax.ppermute(value, 'dom', [(d, target[d]) for d in range(lax.axis_size('...]
    ppermute x23, waiting for transfers between devices: 12.6 us -> 13.4 us  [send(): lax.ppermute(value, 'dom', [(d, target[d]) for d in range(lax.axis_size('...]
  transfers between devices with their start and end apart: 23 -> 23, of which waited for: 15 -> 14; matrix products, arithmetic and copies ran while one was open for 0% -> 0% of each run, Pallas kernels for 4% -> 5%
where the time goes in v10:
time: 41.4 us; the launch traced here: 41.2 us
  starting transfers between devices  21.1 us (51%)
  waiting for transfers between devices  13.4 us (32%)
  Pallas kernels  6.04 us (15%)
  between operations  0.72 us (2%)
    ppermute x23, starting transfers between devices, send(): lax.ppermute(value, 'dom', [(d, target[d]) for d in range(lax.axis_size('...  21.1 us
    ppermute x23, waiting for transfers between devices, send(): lax.ppermute(value, 'dom', [(d, target[d]) for d in range(lax.axis_size('...  13.4 us
    pallas_call x1, Pallas kernels, local(): call(prepare_kernel, [((width, rows), bf16), ((width, rows), bf16), ((8 *...  1.39 us
    pallas_call x1, Pallas kernels, local(): call(start_kernel, [((comps * blocks + 8, 128), f32)], [HBM] * 4, 600000,...  1.08 us
    pallas_call x1, Pallas kernels, local(): call(lambda *refs: finish_kernel(total, vecs, *refs), [((comps, S, rows),...  1.06 us
  transfers between devices with their start and end apart: 23, of which 14 were waited for; matrix products, arithmetic and copies ran while one was open for 0% of the time, Pallas kernels for 5%

profile of v10, /device:TPU:0, one launch (start us, length us, event | category | flops | bytes accessed | tf_op | source)
XLA Modules:
  0.0 41.2 jit_solution(13828214706002827410)
XLA Ops:
  0.6 1.1 %shard_map.86.refs_0_ = f32[32,128]{1,0:T(8,128)S(1)} custom-call(f32[3,32,512]{2,1,0:T(8,128)} %prev_ref.1, f32[3,32]{1,0:T(4,128)} %mix_in.1, s32[1,4,8]{2,1,0:T(4,128)} %list_in.1, s32[1,4]{1,0:T(1,128)} %count_in.1), custom_call_target="tpu_custom_call" | custom-call | flops 600000 | bytes 250000 | tf_op jit(solution)/shard_map/pallas_call | solution.py:388
  1.7 3.0 %collective-permute-start.3 = (f32[32,128]{1,0:T(8,128)S(1)}, f32[32,128]{1,0:T(8,128)S(1)}, u32[]{:S(2)}, u32[]{:S(2)}) collective-permute-start(f32[32,128]{1,0:T(8,128)S(1)} %shard_map.86.refs_0_), channel_id=1, source_target_pairs={{0,2},{1,0},{2,1},{3,4},{4,3},{5,6},{6,5},{7,8},{8,7},{9,10},{10,9... | collective-permute-start | bytes 49160 | tf_op jit(solution)/shard_map/ppermute | solution.py:338
  4.7 1.9 %collective-permute-start.2 = (f32[32,128]{1,0:T(8,128)S(1)}, f32[32,128]{1,0:T(8,128)S(1)}, u32[]{:S(2)}, u32[]{:S(2)}) collective-permute-start(f32[32,128]{1,0:T(8,128)S(1)} %shard_map.86.refs_0_), channel_id=1, source_target_pairs={{0,8},{1,9},{2,10},{3,11},{4,12},{5,13},{6,14},{7,15},{8,0},{9,1},... | collective-permute-start | bytes 49160 | tf_op jit(solution)/shard_map/ppermute | solution.py:338
  6.6 0.0 collective-permute-start.1
  6.6 0.0 collective-permute-start
  6.6 1.4 %shard_map.87 = (bf16[256,512]{1,0:T(8,128)(2,1)S(1)}, bf16[256,512]{1,0:T(8,128)(2,1)S(1)}, f32[40,128]{1,0:T(8,128)S(1)}) custom-call(f32[512,256]{1,0:T(8,128)} %strips_in.1, s32[4,8]{1,0:T(4,128)} %bitcast.2, f32[4]{0:T(128)} %shifts_in.1), custom_call_target="tpu_custom_call" | custom-call | flops 1000000 | bytes 1000000 | tf_op jit(solution)/shard_map/pallas_call | solution.py:402
  8.0 0.0 collective-permute-done.3.refs_4_
  8.0 0.5 %collective-permute-done.2.refs_3_ = f32[32,128]{1,0:T(8,128)S(1)} collective-permute-done((f32[32,128]{1,0:T(8,128)S(1)}, f32[32,128]{1,0:T(8,128)S(1)}, u32[]{:S(2)}, u32[]{:S(2)}) %collective-permute-start.2) | collective-permute-done | bytes 16416 | tf_op jit(solution)/shard_map/ppermute | solution.py:338
  8.5 1.3 %collective-permute-done.1.refs_2_ = f32[32,128]{1,0:T(8,128)S(1)} collective-permute-done((f32[32,128]{1,0:T(8,128)S(1)}, f32[32,128]{1,0:T(8,128)S(1)}, u32[]{:S(2)}, u32[]{:S(2)}) %collective-permute-start.1) | collective-permute-done | bytes 16416 | tf_op jit(solution)/shard_map/ppermute | solution.py:338
  9.7 0.0 collective-permute-done.refs_1_
  9.7 0.5 %shard_map.88 = (f32[24,128]{1,0:T(8,128)S(1)}, bf16[96,128]{1,0:T(8,128)(2,1)S(1)}) custom-call(f32[32,128]{1,0:T(8,128)S(1)} %shard_map.86.refs_0_, f32[32,128]{1,0:T(8,128)S(1)} %collective-permute-done.refs_1_, f32[32,128]{1,0:T(8,128)S(1)} %collective-permute-done.1.refs_2_, f32[32,128]{1,0:T(8,128)S(1)} %collective-permute-done.2.refs_3_, ...), custom_call_target="tpu_custom_call" | custom-call | flops 50000000 | bytes 600000 | tf_op jit(solution)/shard_map/pallas_call | solution.py:417
  10.3 0.4 %collective-permute-start.7 = (f32[24,128]{1,0:T(8,128)S(1)}, f32[24,128]{1,0:T(8,128)S(1)}, u32[]{:S(2)}, u32[]{:S(2)}) collective-permute-start(f32[24,128]{1,0:T(8,128)S(1)} %get-tuple-element.22.refs_0_.t0), channel_id=1, source_target_pairs={{0,2},{1,0},{2,1},{3,4},{4,3},{5,6},{6,5},{7,8},{8,7},{9,10},{10,9... | collective-permute-start | bytes 36872 | tf_op jit(solution)/shard_map/ppermute | solution.py:338
  10.7 1.4 %collective-permute-start.6 = (f32[24,128]{1,0:T(8,128)S(1)}, f32[24,128]{1,0:T(8,128)S(1)}, u32[]{:S(2)}, u32[]{:S(2)}) collective-permute-start(f32[24,128]{1,0:T(8,128)S(1)} %get-tuple-element.22.refs_0_.t0), channel_id=1, source_target_pairs={{0,8},{1,9},{2,10},{3,11},{4,12},{5,13},{6,14},{7,15},{8,0},{9,1},... | collective-permute-start | bytes 36872 | tf_op jit(solution)/shard_map/ppermute | solution.py:338
  12.1 0.2 collective-permute-start.5
  12.3 1.7 %collective-permute-start.4 = (f32[24,128]{1,0:T(8,128)S(1)}, f32[24,128]{1,0:T(8,128)S(1)}, u32[]{:S(2)}, u32[]{:S(2)}) collective-permute-start(f32[24,128]{1,0:T(8,128)S(1)} %get-tuple-element.22.refs_0_.t0), channel_id=1, source_target_pairs={{0,1},{1,0},{2,3},{3,2},{4,5},{5,4},{6,7},{7,6},{8,9},{9,8},{10,11... | collective-permute-start | bytes 36872 | tf_op jit(solution)/shard_map/ppermute | solution.py:338
  13.9 0.0 collective-permute-done.7.refs_4_
  14.0 0.4 %collective-permute-done.6.refs_3_ = f32[24,128]{1,0:T(8,128)S(1)} collective-permute-done((f32[24,128]{1,0:T(8,128)S(1)}, f32[24,128]{1,0:T(8,128)S(1)}, u32[]{:S(2)}, u32[]{:S(2)}) %collective-permute-start.6) | collective-permute-done | bytes 12320 | tf_op jit(solution)/shard_map/ppermute | solution.py:338
  14.4 0.9 %collective-permute-done.5.refs_2_ = f32[24,128]{1,0:T(8,128)S(1)} collective-permute-done((f32[24,128]{1,0:T(8,128)S(1)}, f32[24,128]{1,0:T(8,128)S(1)}, u32[]{:S(2)}, u32[]{:S(2)}) %collective-permute-start.5) | collective-permute-done | bytes 12320 | tf_op jit(solution)/shard_map/ppermute | solution.py:338
  15.2 0.0 collective-permute-done.4.refs_1_
  15.2 0.4 shard_map.89.refs_0_.t1
  15.6 0.0 copy-start
  15.6 1.7 %collective-permute-start.11 = (f32[24,128]{1,0:T(8,128)S(1)}, f32[24,128]{1,0:T(8,128)S(1)}, u32[]{:S(2)}, u32[]{:S(2)}) collective-permute-start(f32[24,128]{1,0:T(8,128)S(1)} %shard_map.89.refs_0_.t1), channel_id=1, source_target_pairs={{0,2},{1,0},{2,1},{3,4},{4,3},{5,6},{6,5},{7,8},{8,7},{9,10},{10,9... | collective-permute-start | bytes 36872 | tf_op jit(solution)/shard_map/ppermute | solution.py:338
  17.4 1.6 %collective-permute-start.10 = (f32[24,128]{1,0:T(8,128)S(1)}, f32[24,128]{1,0:T(8,128)S(1)}, u32[]{:S(2)}, u32[]{:S(2)}) collective-permute-start(f32[24,128]{1,0:T(8,128)S(1)} %shard_map.89.refs_0_.t1), channel_id=1, source_target_pairs={{0,8},{1,9},{2,10},{3,11},{4,12},{5,13},{6,14},{7,15},{8,0},{9,1},... | collective-permute-start | bytes 36872 | tf_op jit(solution)/shard_map/ppermute | solution.py:338
  19.0 0.0 collective-permute-start.9
  19.0 0.0 collective-permute-start.8
  19.0 0.0 collective-permute-done.11.refs_4_
  19.0 2.0 %collective-permute-done.10.refs_3_ = f32[24,128]{1,0:T(8,128)S(1)} collective-permute-done((f32[24,128]{1,0:T(8,128)S(1)}, f32[24,128]{1,0:T(8,128)S(1)}, u32[]{:S(2)}, u32[]{:S(2)}) %collective-permute-start.10) | collective-permute-done | bytes 12320 | tf_op jit(solution)/shard_map/ppermute | solution.py:338
  21.1 1.1 %collective-permute-done.9.refs_2_ = f32[24,128]{1,0:T(8,128)S(1)} collective-permute-done((f32[24,128]{1,0:T(8,128)S(1)}, f32[24,128]{1,0:T(8,128)S(1)}, u32[]{:S(2)}, u32[]{:S(2)}) %collective-permute-start.9) | collective-permute-done | bytes 12320 | tf_op jit(solution)/shard_map/ppermute | solution.py:338
  22.1 0.0 collective-permute-done.8.refs_1_
  22.1 0.4 shard_map.90.t2.refs_0_
  22.5 0.0 collective-permute-start.15
  22.5 1.8 %collective-permute-start.14 = (f32[24,128]{1,0:T(8,128)S(1)}, f32[24,128]{1,0:T(8,128)S(1)}, u32[]{:S(2)}, u32[]{:S(2)}) collective-permute-start(f32[24,128]{1,0:T(8,128)S(1)} %shard_map.90.t2.refs_0_), channel_id=1, source_target_pairs={{0,8},{1,9},{2,10},{3,11},{4,12},{5,13},{6,14},{7,15},{8,0},{9,1},... | collective-permute-start | bytes 36872 | tf_op jit(solution)/shard_map/ppermute | solution.py:338
  24.4 0.0 collective-permute-start.13
  24.4 0.4 collective-permute-start.12
  24.8 0.0 copy-done
  24.8 0.6 %shard_map.91 = (f32[24,512]{1,0:T(8,128)S(1)}, f32[24,128]{1,0:T(8,128)S(1)}, bf16[512,128]{1,0:T(8,128)(2,1)S(1)}, bf16[512,128]{1,0:T(8,128)(2,1)S(1)}, bf16[...) custom-call(f32[3,32,512]{2,1,0:T(8,128)S(1)} %copy-done, ...), custom_call_target="tpu_custom_call" | custom-call | flops 60000000 | bytes 250000 | tf_op jit(solution)/shard_map/pallas_call | solution.py:432
  25.4 0.0 collective-permute-done.15.refs_4_
  25.4 0.9 %collective-permute-done.14.refs_3_ = f32[24,128]{1,0:T(8,128)S(1)} collective-permute-done((f32[24,128]{1,0:T(8,128)S(1)}, f32[24,128]{1,0:T(8,128)S(1)}, u32[]{:S(2)}, u32[]{:S(2)}) %collective-permute-start.14) | collective-permute-done | bytes 12320 | tf_op jit(solution)/shard_map/ppermute | solution.py:338
  26.3 1.2 %collective-permute-done.13.refs_2_ = f32[24,128]{1,0:T(8,128)S(1)} collective-permute-done((f32[24,128]{1,0:T(8,128)S(1)}, f32[24,128]{1,0:T(8,128)S(1)}, u32[]{:S(2)}, u32[]{:S(2)}) %collective-permute-start.13) | collective-permute-done | bytes 12320 | tf_op jit(solution)/shard_map/ppermute | solution.py:338
  27.5 0.0 collective-permute-done.12.refs_1_
  27.5 0.6 %shard_map.92 = (f32[8,512]{1,0:T(8,128)S(1)}, f32[24,128]{1,0:T(8,128)S(1)}) custom-call(f32[24,128]{1,0:T(8,128)S(1)} %shard_map.90.t2.refs_0_, f32[24,128]{1,0:T(8,128)S(1)} %collective-permute-done.12.refs_1_, f32[24,128]{1,0:T(8,128)S(1)} %collective-permute-done.13.refs_2_, f32[24,128]{1,0:T(8,128)S(1)} %collective-permute-done.14.refs_3_, ...), custom_call_target="tpu_custom_call" | custom-call | flops 80000000 | bytes 900000 | tf_op jit(solution)/shard_map/pallas_call | solution.py:439
  28.1 0.1 collective-permute-start.16
  28.2 1.2 %collective-permute-done.16 = f32[24,128]{1,0:T(8,128)S(1)} collective-permute-done((f32[24,128]{1,0:T(8,128)S(1)}, f32[24,128]{1,0:T(8,128)S(1)}, u32[]{:S(2)}, u32[]{:S(2)}) %collective-permute-start.16) | collective-permute-done | bytes 12320 | tf_op jit(solution)/shard_map/ppermute | solution.py:338
  29.4 1.0 %collective-permute-start.19 = (f32[24,128]{1,0:T(8,128)S(1)}, f32[24,128]{1,0:T(8,128)S(1)}, u32[]{:S(2)}, u32[]{:S(2)}) collective-permute-start(f32[24,128]{1,0:T(8,128)S(1)} %add.21), channel_id=1, source_target_pairs={{0,7},{1,6},{2,5},{3,4},{4,3},{5,2},{6,1},{7,0},{8,15},{9,14},{10,... | collective-permute-start | bytes 36872 | tf_op jit(solution)/shard_map/ppermute | solution.py:338
  30.4 0.4 %collective-permute-start.18 = (f32[24,128]{1,0:T(8,128)S(1)}, f32[24,128]{1,0:T(8,128)S(1)}, u32[]{:S(2)}, u32[]{:S(2)}) collective-permute-start(f32[24,128]{1,0:T(8,128)S(1)} %add.21), channel_id=1, source_target_pairs={{0,5},{1,4},{2,7},{3,6},{4,1},{5,0},{6,3},{7,2},{8,13},{9,12},{10,... | collective-permute-start | bytes 36872 | tf_op jit(solution)/shard_map/ppermute | solution.py:338
  30.8 1.5 %collective-permute-start.17 = (f32[24,128]{1,0:T(8,128)S(1)}, f32[24,128]{1,0:T(8,128)S(1)}, u32[]{:S(2)}, u32[]{:S(2)}) collective-permute-start(f32[24,128]{1,0:T(8,128)S(1)} %add.21), channel_id=1, source_target_pairs={{0,3},{1,2},{2,1},{3,0},{4,7},{5,6},{6,5},{7,4},{8,11},{9,10},{10,... | collective-permute-start | bytes 36872 | tf_op jit(solution)/shard_map/ppermute | solution.py:338
  32.4 1.0 %collective-permute-done.19 = f32[24,128]{1,0:T(8,128)S(1)} collective-permute-done((f32[24,128]{1,0:T(8,128)S(1)}, f32[24,128]{1,0:T(8,128)S(1)}, u32[]{:S(2)}, u32[]{:S(2)}) %collective-permute-start.19) | collective-permute-done | bytes 12320 | tf_op jit(solution)/shard_map/ppermute | solution.py:338
  33.4 0.1 collective-permute-done.18
  33.5 0.4 %collective-permute-done.17 = f32[24,128]{1,0:T(8,128)S(1)} collective-permute-done((f32[24,128]{1,0:T(8,128)S(1)}, f32[24,128]{1,0:T(8,128)S(1)}, u32[]{:S(2)}, u32[]{:S(2)}) %collective-permute-start.17) | collective-permute-done | bytes 12320 | tf_op jit(solution)/shard_map/ppermute | solution.py:338
  34.0 2.1 %collective-permute-start.22 = (f32[24,128]{1,0:T(8,128)S(1)}, f32[24,128]{1,0:T(8,128)S(1)}, u32[]{:S(2)}, u32[]{:S(2)}) collective-permute-start(f32[24,128]{1,0:T(8,128)S(1)} %add_add_fusion.1), channel_id=1, source_target_pairs={{0,25},{1,24},{2,27},{3,26},{4,29},{5,28},{6,31},{7,30},{8,17},{9,... | collective-permute-start | bytes 36872 | tf_op jit(solution)/shard_map/ppermute | solution.py:338
  36.1 0.2 collective-permute-start.21
  36.3 1.6 %collective-permute-start.20 = (f32[24,128]{1,0:T(8,128)S(1)}, f32[24,128]{1,0:T(8,128)S(1)}, u32[]{:S(2)}, u32[]{:S(2)}) collective-permute-start(f32[24,128]{1,0:T(8,128)S(1)} %add_add_fusion.1), channel_id=1, source_target_pairs={{0,9},{1,8},{2,11},{3,10},{4,13},{5,12},{6,15},{7,14},{8,1},{9,0},... | collective-permute-start | bytes 36872 | tf_op jit(solution)/shard_map/ppermute | solution.py:338
  37.9 1.0 %collective-permute-done.22 = f32[24,128]{1,0:T(8,128)S(1)} collective-permute-done((f32[24,128]{1,0:T(8,128)S(1)}, f32[24,128]{1,0:T(8,128)S(1)}, u32[]{:S(2)}, u32[]{:S(2)}) %collective-permute-start.22) | collective-permute-done | bytes 12320 | tf_op jit(solution)/shard_map/ppermute | solution.py:338
  38.9 1.3 %collective-permute-done.21 = f32[24,128]{1,0:T(8,128)S(1)} collective-permute-done((f32[24,128]{1,0:T(8,128)S(1)}, f32[24,128]{1,0:T(8,128)S(1)}, u32[]{:S(2)}, u32[]{:S(2)}) %collective-permute-start.21) | collective-permute-done | bytes 12320 | tf_op jit(solution)/shard_map/ppermute | solution.py:338
  40.2 0.0 collective-permute-done.20
  40.2 1.1 %shard_map.93 = (f32[3,4,512]{2,1,0:T(4,128)}, f32[3,4,36]{2,1,0:T(4,128)}) custom-call(f32[24,128]{1,0:T(8,128)S(1)} %add_add_fusion.refs_0_, bf16[96,512]{1,0:T(8,128)(2,1)S(1)} %get-tuple-element.29.refs_1_, bf16[96,512]{1,0:T(8,128)(2,1)S(1)} %get-tuple-element.30.refs_2_, bf16[96,512]{1,0:T(8,128)(2,1)S(1)} %get-tuple-element.31.refs_3_, ...), custom_call_target="tpu_custom_call" | custom-call | flops 50000000 | bytes 400000 | tf_op jit(solution)/shard_map/pallas_call | solution.py:447
  (3 shorter events, 0.0 us)
Async XLA Ops:
  1.7 6.3 %collective-permute-start.3 = (f32[32,128]{1,0:T(8,128)S(1)}, f32[32,128]{1,0:T(8,128)S(1)}, u32[]{:S(2)}, u32[]{:S(2)}) collective-permute-start(f32[32,128]{1,0:T(8,128)S(1)} %shard_map.86.refs_0_), channel_id=1, source_target_pairs={{0,2},{1,0},{2,1},{3,4},{4,3},{5,6},{6,5},{7,8},{8,7},{9,10},{10,9... | collective-permute-start | bytes 49160 | tf_op jit(solution)/shard_map/ppermute | solution.py:338
  4.7 3.7 %collective-permute-start.2 = (f32[32,128]{1,0:T(8,128)S(1)}, f32[32,128]{1,0:T(8,128)S(1)}, u32[]{:S(2)}, u32[]{:S(2)}) collective-permute-start(f32[32,128]{1,0:T(8,128)S(1)} %shard_map.86.refs_0_), channel_id=1, source_target_pairs={{0,8},{1,9},{2,10},{3,11},{4,12},{5,13},{6,14},{7,15},{8,0},{9,1},... | collective-permute-start | bytes 49160 | tf_op jit(solution)/shard_map/ppermute | solution.py:338
  6.6 3.2 %collective-permute-start.1 = (f32[32,128]{1,0:T(8,128)S(1)}, f32[32,128]{1,0:T(8,128)S(1)}, u32[]{:S(2)}, u32[]{:S(2)}) collective-permute-start(f32[32,128]{1,0:T(8,128)S(1)} %shard_map.86.refs_0_), channel_id=1, source_target_pairs={{0,1},{1,2},{2,3},{3,0},{4,5},{5,4},{6,7},{7,6},{8,16},{9,17},{10,... | collective-permute-start | bytes 49160 | tf_op jit(solution)/shard_map/ppermute | solution.py:338
  6.6 3.2 %collective-permute-start = (f32[32,128]{1,0:T(8,128)S(1)}, f32[32,128]{1,0:T(8,128)S(1)}, u32[]{:S(2)}, u32[]{:S(2)}) collective-permute-start(f32[32,128]{1,0:T(8,128)S(1)} %shard_map.86.refs_0_), channel_id=1, source_target_pairs={{0,1},{1,0},{2,3},{3,2},{4,5},{5,4},{6,7},{7,6},{8,9},{9,8},{10,11... | collective-permute-start | bytes 49160 | tf_op jit(solution)/shard_map/ppermute | solution.py:338
  10.3 3.7 %collective-permute-start.7 = (f32[24,128]{1,0:T(8,128)S(1)}, f32[24,128]{1,0:T(8,128)S(1)}, u32[]{:S(2)}, u32[]{:S(2)}) collective-permute-start(f32[24,128]{1,0:T(8,128)S(1)} %get-tuple-element.22.refs_0_.t0), channel_id=1, source_target_pairs={{0,2},{1,0},{2,1},{3,4},{4,3},{5,6},{6,5},{7,8},{8,7},{9,10},{10,9... | collective-permute-start | bytes 36872 | tf_op jit(solution)/shard_map/ppermute | solution.py:338
  10.7 3.7 %collective-permute-start.6 = (f32[24,128]{1,0:T(8,128)S(1)}, f32[24,128]{1,0:T(8,128)S(1)}, u32[]{:S(2)}, u32[]{:S(2)}) collective-permute-start(f32[24,128]{1,0:T(8,128)S(1)} %get-tuple-element.22.refs_0_.t0), channel_id=1, source_target_pairs={{0,8},{1,9},{2,10},{3,11},{4,12},{5,13},{6,14},{7,15},{8,0},{9,1},... | collective-permute-start | bytes 36872 | tf_op jit(solution)/shard_map/ppermute | solution.py:338
  12.1 3.1 %collective-permute-start.5 = (f32[24,128]{1,0:T(8,128)S(1)}, f32[24,128]{1,0:T(8,128)S(1)}, u32[]{:S(2)}, u32[]{:S(2)}) collective-permute-start(f32[24,128]{1,0:T(8,128)S(1)} %get-tuple-element.22.refs_0_.t0), channel_id=1, source_target_pairs={{0,1},{1,2},{2,3},{3,0},{4,5},{5,4},{6,7},{7,6},{8,16},{9,17},{10,... | collective-permute-start | bytes 36872 | tf_op jit(solution)/shard_map/ppermute | solution.py:338
  12.3 2.9 %collective-permute-start.4 = (f32[24,128]{1,0:T(8,128)S(1)}, f32[24,128]{1,0:T(8,128)S(1)}, u32[]{:S(2)}, u32[]{:S(2)}) collective-permute-start(f32[24,128]{1,0:T(8,128)S(1)} %get-tuple-element.22.refs_0_.t0), channel_id=1, source_target_pairs={{0,1},{1,0},{2,3},{3,2},{4,5},{5,4},{6,7},{7,6},{8,9},{9,8},{10,11... | collective-permute-start | bytes 36872 | tf_op jit(solution)/shard_map/ppermute | solution.py:338
  15.6 9.1 %copy-start = (f32[3,32,512]{2,1,0:T(8,128)S(1)}, f32[3,32,512]{2,1,0:T(8,128)}, u32[]{:S(2)}) copy-start(f32[3,32,512]{2,1,0:T(8,128)} %prev_ref.1) | copy-start | bytes 589828
  15.6 3.4 %collective-permute-start.11 = (f32[24,128]{1,0:T(8,128)S(1)}, f32[24,128]{1,0:T(8,128)S(1)}, u32[]{:S(2)}, u32[]{:S(2)}) collective-permute-start(f32[24,128]{1,0:T(8,128)S(1)} %shard_map.89.refs_0_.t1), channel_id=1, source_target_pairs={{0,2},{1,0},{2,1},{3,4},{4,3},{5,6},{6,5},{7,8},{8,7},{9,10},{10,9... | collective-permute-start | bytes 36872 | tf_op jit(solution)/shard_map/ppermute | solution.py:338
  17.4 3.7 %collective-permute-start.10 = (f32[24,128]{1,0:T(8,128)S(1)}, f32[24,128]{1,0:T(8,128)S(1)}, u32[]{:S(2)}, u32[]{:S(2)}) collective-permute-start(f32[24,128]{1,0:T(8,128)S(1)} %shard_map.89.refs_0_.t1), channel_id=1, source_target_pairs={{0,8},{1,9},{2,10},{3,11},{4,12},{5,13},{6,14},{7,15},{8,0},{9,1},... | collective-permute-start | bytes 36872 | tf_op jit(solution)/shard_map/ppermute | solution.py:338
  19.0 3.1 %collective-permute-start.9 = (f32[24,128]{1,0:T(8,128)S(1)}, f32[24,128]{1,0:T(8,128)S(1)}, u32[]{:S(2)}, u32[]{:S(2)}) collective-permute-start(f32[24,128]{1,0:T(8,128)S(1)} %shard_map.89.refs_0_.t1), channel_id=1, source_target_pairs={{0,1},{1,2},{2,3},{3,0},{4,5},{5,4},{6,7},{7,6},{8,16},{9,17},{10,... | collective-permute-start | bytes 36872 | tf_op jit(solution)/shard_map/ppermute | solution.py:338
  19.0 3.1 %collective-permute-start.8 = (f32[24,128]{1,0:T(8,128)S(1)}, f32[24,128]{1,0:T(8,128)S(1)}, u32[]{:S(2)}, u32[]{:S(2)}) collective-permute-start(f32[24,128]{1,0:T(8,128)S(1)} %shard_map.89.refs_0_.t1), channel_id=1, source_target_pairs={{0,1},{1,0},{2,3},{3,2},{4,5},{5,4},{6,7},{7,6},{8,9},{9,8},{10,11... | collective-permute-start | bytes 36872 | tf_op jit(solution)/shard_map/ppermute | solution.py:338
  22.5 2.8 %collective-permute-start.15 = (f32[24,128]{1,0:T(8,128)S(1)}, f32[24,128]{1,0:T(8,128)S(1)}, u32[]{:S(2)}, u32[]{:S(2)}) collective-permute-start(f32[24,128]{1,0:T(8,128)S(1)} %shard_map.90.t2.refs_0_), channel_id=1, source_target_pairs={{0,2},{1,0},{2,1},{3,4},{4,3},{5,6},{6,5},{7,8},{8,7},{9,10},{10,9... | collective-permute-start | bytes 36872 | tf_op jit(solution)/shard_map/ppermute | solution.py:338
  22.5 3.8 %collective-permute-start.14 = (f32[24,128]{1,0:T(8,128)S(1)}, f32[24,128]{1,0:T(8,128)S(1)}, u32[]{:S(2)}, u32[]{:S(2)}) collective-permute-start(f32[24,128]{1,0:T(8,128)S(1)} %shard_map.90.t2.refs_0_), channel_id=1, source_target_pairs={{0,8},{1,9},{2,10},{3,11},{4,12},{5,13},{6,14},{7,15},{8,0},{9,1},... | collective-permute-start | bytes 36872 | tf_op jit(solution)/shard_map/ppermute | solution.py:338
  24.4 3.1 %collective-permute-start.13 = (f32[24,128]{1,0:T(8,128)S(1)}, f32[24,128]{1,0:T(8,128)S(1)}, u32[]{:S(2)}, u32[]{:S(2)}) collective-permute-start(f32[24,128]{1,0:T(8,128)S(1)} %shard_map.90.t2.refs_0_), channel_id=1, source_target_pairs={{0,1},{1,2},{2,3},{3,0},{4,5},{5,4},{6,7},{7,6},{8,16},{9,17},{10,... | collective-permute-start | bytes 36872 | tf_op jit(solution)/shard_map/ppermute | solution.py:338
  24.4 3.1 %collective-permute-start.12 = (f32[24,128]{1,0:T(8,128)S(1)}, f32[24,128]{1,0:T(8,128)S(1)}, u32[]{:S(2)}, u32[]{:S(2)}) collective-permute-start(f32[24,128]{1,0:T(8,128)S(1)} %shard_map.90.t2.refs_0_), channel_id=1, source_target_pairs={{0,1},{1,0},{2,3},{3,2},{4,5},{5,4},{6,7},{7,6},{8,9},{9,8},{10,11... | collective-permute-start | bytes 36872 | tf_op jit(solution)/shard_map/ppermute | solution.py:338
  28.1 1.2 %collective-permute-start.16 = (f32[24,128]{1,0:T(8,128)S(1)}, f32[24,128]{1,0:T(8,128)S(1)}, u32[]{:S(2)}, u32[]{:S(2)}) collective-permute-start(f32[24,128]{1,0:T(8,128)S(1)} %get-tuple-element.28), channel_id=1, source_target_pairs={{0,1},{1,0},{2,3},{3,2},{4,5},{5,4},{6,7},{7,6},{8,9},{9,8},{10,11... | collective-permute-start | bytes 36872 | tf_op jit(solution)/shard_map/ppermute | solution.py:338
  29.4 4.0 %collective-permute-start.19 = (f32[24,128]{1,0:T(8,128)S(1)}, f32[24,128]{1,0:T(8,128)S(1)}, u32[]{:S(2)}, u32[]{:S(2)}) collective-permute-start(f32[24,128]{1,0:T(8,128)S(1)} %add.21), channel_id=1, source_target_pairs={{0,7},{1,6},{2,5},{3,4},{4,3},{5,2},{6,1},{7,0},{8,15},{9,14},{10,... | collective-permute-start | bytes 36872 | tf_op jit(solution)/shard_map/ppermute | solution.py:338
  30.4 3.1 %collective-permute-start.18 = (f32[24,128]{1,0:T(8,128)S(1)}, f32[24,128]{1,0:T(8,128)S(1)}, u32[]{:S(2)}, u32[]{:S(2)}) collective-permute-start(f32[24,128]{1,0:T(8,128)S(1)} %add.21), channel_id=1, source_target_pairs={{0,5},{1,4},{2,7},{3,6},{4,1},{5,0},{6,3},{7,2},{8,13},{9,12},{10,... | collective-permute-start | bytes 36872 | tf_op jit(solution)/shard_map/ppermute | solution.py:338
  30.8 3.1 %collective-permute-start.17 = (f32[24,128]{1,0:T(8,128)S(1)}, f32[24,128]{1,0:T(8,128)S(1)}, u32[]{:S(2)}, u32[]{:S(2)}) collective-permute-start(f32[24,128]{1,0:T(8,128)S(1)} %add.21), channel_id=1, source_target_pairs={{0,3},{1,2},{2,1},{3,0},{4,7},{5,6},{6,5},{7,4},{8,11},{9,10},{10,... | collective-permute-start | bytes 36872 | tf_op jit(solution)/shard_map/ppermute | solution.py:338
  34.0 4.9 %collective-permute-start.22 = (f32[24,128]{1,0:T(8,128)S(1)}, f32[24,128]{1,0:T(8,128)S(1)}, u32[]{:S(2)}, u32[]{:S(2)}) collective-permute-start(f32[24,128]{1,0:T(8,128)S(1)} %add_add_fusion.1), channel_id=1, source_target_pairs={{0,25},{1,24},{2,27},{3,26},{4,29},{5,28},{6,31},{7,30},{8,17},{9,... | collective-permute-start | bytes 36872 | tf_op jit(solution)/shard_map/ppermute | solution.py:338
  36.1 4.1 %collective-permute-start.21 = (f32[24,128]{1,0:T(8,128)S(1)}, f32[24,128]{1,0:T(8,128)S(1)}, u32[]{:S(2)}, u32[]{:S(2)}) collective-permute-start(f32[24,128]{1,0:T(8,128)S(1)} %add_add_fusion.1), channel_id=1, source_target_pairs={{0,17},{1,16},{2,19},{3,18},{4,21},{5,20},{6,23},{7,22},{8,25},{9,... | collective-permute-start | bytes 36872 | tf_op jit(solution)/shard_map/ppermute | solution.py:338
  36.3 3.9 %collective-permute-start.20 = (f32[24,128]{1,0:T(8,128)S(1)}, f32[24,128]{1,0:T(8,128)S(1)}, u32[]{:S(2)}, u32[]{:S(2)}) collective-permute-start(f32[24,128]{1,0:T(8,128)S(1)} %add_add_fusion.1), channel_id=1, source_target_pairs={{0,9},{1,8},{2,11},{3,10},{4,13},{5,12},{6,15},{7,14},{8,1},{9,0},... | collective-permute-start | bytes 36872 | tf_op jit(solution)/shard_map/ppermute | solution.py:338

commit v11 on v10

--- a/solution.py
+++ b/solution.py
@@ -23,20 +23,26 @@
     return lax.broadcasted_iota(jnp.int32, shape, axis)
 
 
-PLACES = {
-    (0, 0): (0, 0),
-    (0, 1): (0, 32),
-    (0, 2): (0, 56),
-    (0, 3): (0, 72),
-    (1, 0): (0, 80),
-    (1, 2): (0, 112),
-    (1, 1): (1, 0),
-    (1, 3): (1, 24),
-    (2, 0): (1, 32),
-    (2, 1): (1, 64),
-    (2, 2): (1, 88),
-    (2, 3): (1, 104),
-}
+def packed(parts, tail=None):
+    low = iota((8, 128), 1) < BLOCK
+    last = parts[2] if tail is None else jnp.where(low, parts[2], tail)
+    return jnp.concatenate([jnp.where(low, parts[0], parts[1]), last], axis=0)
+
+
+def parts_of(tile):
+    low = iota((8, 128), 1) < BLOCK
+    turned = pltpu.roll(tile[:8], BLOCK, 1)
+    return [jnp.where(low, tile[:8], turned), jnp.where(low, turned, tile[:8]), tile[8:]]
+
+
+def opened(tile):
+    low = iota((8, 128), 1) < BLOCK
+    turned = pltpu.roll(tile[8:], BLOCK, 1)
+    return jnp.concatenate([tile[:8], jnp.where(low, tile[8:], turned)], axis=0), turned[:1]
+
+
+PLACES = {(c, g): (g % 2, (0, 8, 0, 0)[g] + 32 * c) for c in range(COMPS) for g in range(4)}
+PLACES.update({(0, 2): (0, 96), (1, 2): (0, 112), (2, 2): (1, 96)})
 
 
 def own_lanes(rows, width):
@@ -51,7 +57,7 @@
 
 
 def lines_of(tile, width):
-    wide = jnp.concatenate([tile] * (width // 128), axis=1)
+    wide = jnp.concatenate([jnp.concatenate(parts_of(tile), axis=0)] * (width // 128), axis=1)
     wide = jnp.where(own_lanes(wide.shape[0], width), wide, 0.0)
     where = iota((8, width), 0)
     result = jnp.zeros((8, width), jnp.float32)
@@ -69,15 +75,6 @@
     return parts
 
 
-def split_dot(x, parts):
-    left = [part.astype(jnp.float32) for part in split(x)]
-    left.append(jnp.zeros((-3 * x.shape[0] % 16, x.shape[1]), jnp.float32))
-    left = jnp.concatenate([part for part in left if part.shape[0]], axis=0).astype(jnp.bfloat16)
-    products = dot(left, parts[0]) + dot(left, parts[1]) + dot(left, parts[2])
-    rows = x.shape[0]
-    return products[:rows] + (products[rows : 2 * rows] + products[2 * rows : 3 * rows])
-
-
 def fetch(pairs, sems):
     copies = [pltpu.make_async_copy(src, dst, sems.at[i]) for i, (src, dst) in enumerate(pairs)]
     for copy in copies:
@@ -85,13 +82,14 @@
     return copies
 
 
-def start_kernel(prev_in, mix_in, list_in, count_in, out_ref, prev_ref, mix_ref, list_ref, count_ref, sems):
-    copies = fetch(
-        [(prev_in, prev_ref), (mix_in, mix_ref), (list_in, list_ref), (count_in, count_ref)], sems
-    )
-    for copy in copies[1:]:
+def start_kernel(prev_in, mix_in, list_in, count_in, tile_ref, prev_ref, mix_ref, list_ref, count_ref, sems):
+    comps, vecs, rows = prev_ref.shape
+    pairs = [(mix_in, mix_ref), (list_in, list_ref), (count_in, count_ref)]
+    halves = [(c, pl.ds(h * (vecs // 2), vecs // 2)) for c in range(comps) for h in range(2)]
+    pairs += [(prev_in.at[c, part], prev_ref.at[c, part]) for c, part in halves]
+    copies = fetch(pairs, sems)
+    for copy in copies[:3]:
         copy.wait()
-    comps, vecs, rows = prev_ref.shape
     eye = iota((vecs, vecs), 0) == iota((vecs, vecs), 1)
     weights = []
     for c in range(comps):
@@ -104,15 +102,17 @@
     for link in range(4):
         live = slot < jnp.broadcast_to(count_ref[0:1, link : link + 1], slot.shape)
         line = jnp.where(live, order[link : link + 1], DEAD)
-        line = pltpu.roll(jnp.broadcast_to(line, (8, 128)), 8 + 8 * link, 1)
-        meta = jnp.where(iota((8, 128), 1) // 8 == link + 1, line, meta)
-    out_ref[8 * comps :, :] = meta
-    copies[0].wait()
+        line = pltpu.roll(jnp.broadcast_to(line, (8, 128)), BLOCK + 8 + 8 * link, 1)
+        meta = jnp.where(iota((8, 128), 1) // 8 == BLOCK // 8 + link + 1, line, meta)
     own = own_lanes(8, rows)
+    parts = []
     for c in range(comps):
+        copies[3 + 2 * c].wait()
+        copies[4 + 2 * c].wait()
         start = jnp.sum(weights[c] * prev_ref[c], axis=0, keepdims=True)
         line = jnp.broadcast_to(start, own.shape)
-        out_ref[c * 8 : (c + 1) * 8, :] = fold(jnp.where(own, line, 0.0))
+        parts.append(fold(jnp.where(own, line, 0.0)))
+    tile_ref[...] = packed(parts, meta)
 
 
 def prepare_kernel(strips_in, columns_in, shifts_in, high_ref, low_ref, aux_ref, strips, columns, shifts, sems):
@@ -146,12 +146,12 @@
     near, far_odd, far_even, across = metas
     moved = (place == 2) | (place == length - 3)
     across = jnp.where(moved, far_odd, across)
-    circle = jnp.where(moved, 48.0, 96.0)
+    circle = jnp.where(moved, 32.0, 64.0)
     slots = [
-        (place >= 1, jnp.where(even, circle, 24.0), jnp.where(even, across, near)),
-        (place < length - 1, jnp.where(even, 24.0, circle), jnp.where(even, near, across)),
-        (place >= FAR, jnp.where(even_far, 48.0, 72.0), jnp.where(even_far, far_odd, far_even)),
-        (place < length - FAR, jnp.where(even_far, 72.0, 48.0), jnp.where(even_far, far_even, far_odd)),
+        (place >= 1, jnp.where(even, circle, 16.0), jnp.where(even, across, near)),
+        (place < length - 1, jnp.where(even, 16.0, circle), jnp.where(even, near, across)),
+        (place >= FAR, jnp.where(even_far, 32.0, 48.0), jnp.where(even_far, far_odd, far_even)),
+        (place < length - FAR, jnp.where(even_far, 48.0, 32.0), jnp.where(even_far, far_even, far_odd)),
     ]
     lane = iota((1, 128), 1)
     target = lane.astype(jnp.float32)
@@ -164,40 +164,39 @@
         jnp.sum(jnp.where(lane == table[:, k : k + 1], target, 0.0), axis=1, keepdims=True)
         for k in range(4)
     ]
-    groups = [(lane == at[k] + float(8 * c)).astype(jnp.float32) for k in range(4) for c in range(COMPS)]
+    groups = [(lane == at[k] + float(8 * c)).astype(jnp.float32) for k in range(4) for c in range(2)]
     return jnp.concatenate(groups, axis=0).astype(jnp.bfloat16)
 
 
 def multiply(choose, pieces, shift, high, low):
-    rows = 8 * COMPS
-    ext = jnp.concatenate(pieces + [jnp.zeros((128 - 5 * rows, 128), jnp.float32)], axis=0)
+    ext = jnp.concatenate(pieces + [jnp.zeros((48, 128), jnp.float32)], axis=0)
     top = ext.astype(jnp.bfloat16).astype(jnp.float32)
     x = dot(choose, jnp.concatenate([top, ext - top], axis=1).astype(jnp.bfloat16))
-    front = iota((rows, 256), 1) % 128 < BLOCK
-    pairs = [
-        jnp.where(front, x[2 * t * rows : (2 * t + 1) * rows], x[(2 * t + 1) * rows : (2 * t + 2) * rows])
-        for t in range(2)
-    ]
-    left = jnp.concatenate(
-        [
-            jnp.concatenate([pair[:, half * 128 : (half + 1) * 128] for pair in pairs], axis=1)
-            for half in range(2)
-        ],
-        axis=0,
-    ).astype(jnp.bfloat16)
+    front = iota((8, 128), 1) < BLOCK
+    halves = []
+    for half in range(2):
+        columns = []
+        for t in range(2):
+            a, b = [x[k * 16 : (k + 1) * 16, half * 128 : (half + 1) * 128] for k in (2 * t, 2 * t + 1)]
+            one = jnp.where(front, a[:8], pltpu.roll(b[:8], BLOCK, 1))
+            two = jnp.where(front, pltpu.roll(a[:8], BLOCK, 1), b[:8])
+            columns.append(jnp.concatenate([one, two, jnp.where(front, a[8:], b[8:])], axis=0))
+        halves.append(jnp.concatenate(columns, axis=1))
+    left = jnp.concatenate(halves, axis=0).astype(jnp.bfloat16)
     both = dot(left, high) + dot(left, low)
+    rows = 8 * COMPS
     image = both[:rows] + both[rows:]
     image = fold(jnp.where(own_lanes(rows, image.shape[1]), image, 0.0))
-    return image - jnp.concatenate([shift] * COMPS, axis=0) * pieces[0]
+    image = packed([image[c * 8 : (c + 1) * 8] for c in range(COMPS)])
+    return image - jnp.concatenate([shift] * 2, axis=0) * pieces[0]
 
 
 def first_kernel(length, own, a, b, c, d, aux, high, low, tile_ref, choose_ref):
-    rows = 8 * COMPS
-    refs = (own, a, b, c, d)
-    pieces = [ref[:rows, :] for ref in refs]
-    metas = [ref[rows : rows + 1, :] for ref in refs[1:]]
+    tiles = [opened(ref[...]) for ref in (own, a, b, c, d)]
+    metas = [meta for _, meta in tiles[1:]]
     choose = selection(aux[8 * S :, :], metas, lax.axis_index("dom"), length)
     choose_ref[...] = choose
+    pieces = [tile for tile, _ in tiles]
     tile_ref[...] = multiply(choose, pieces, aux[:8, :], high[...], low[...])
 
 
@@ -212,7 +211,7 @@
     return jnp.sum(jnp.where(mine, gram, 0.0), axis=0, keepdims=True)
 
 
-def early_kernel(prev_ref, t0, t1, t2, lines_ref, gram_ref, *split_refs):
+def early_kernel(prev_ref, t0, t1, t2, lines_ref, gram_ref, *turned_refs):
     comps, vecs, rows = prev_ref.shape
     width = comps * vecs
     lines = jnp.concatenate([lines_of(t[...], rows) for t in (t0, t1, t2)], axis=0)
@@ -228,7 +227,7 @@
         tiles[t] = jnp.where((lane >= first) & (lane < first + vecs - 8 * g), piece, tiles[t])
     gram_ref[:16, :] = jnp.concatenate(tiles, axis=0)
     against = jnp.concatenate([prev, lines, jnp.zeros((8, rows), jnp.float32)], axis=0)
-    for ref, part in zip(split_refs, split(against.T) + split(prev)):
+    for ref, part in zip(turned_refs, split(against.T)):
         ref[...] = part
     gram = dot(lines, against, NT, HIGHEST)
     result = jnp.zeros((8, 128), jnp.float32)
@@ -245,7 +244,10 @@
     width = COMPS * vecs
     last = lines_of(tile, rows)
     line_ref[...] = last
-    gram = split_dot(last, (t0[...], t1[...], t2[...]))
+    parts = [part.astype(jnp.float32) for part in split(last)]
+    left = jnp.concatenate(parts + [jnp.zeros_like(last)], axis=0).astype(jnp.bfloat16)
+    products = dot(left, t0[...]) + dot(left, t1[...]) + dot(left, t2[...])
+    gram = products[:8] + (products[8:16] + products[16:24])
     square = jnp.sum(last * last, axis=1, keepdims=True)
     gram = jnp.where(iota(gram.shape, 1) == width + 8 * (S - 1) + iota(gram.shape, 0), square, gram)
     line = collect(gram, width, vecs)
@@ -255,8 +257,8 @@
     )
 
 
-def finish_kernel(total, vecs, gram_in, p0, p1, p2, lines, last, basis_ref, factors_ref):
-    comps = COMPS
+def finish_kernel(total, gram_in, prev_ref, lines, last, basis_ref, factors_ref):
+    comps, vecs, rows = prev_ref.shape
     width = comps * vecs
     gram = gram_in[...] * (1.0 / total)
     small = gram[16:]
@@ -268,19 +270,24 @@
         coef.append(jnp.where(in_prev, line, 0.0))
         cross.append([jnp.where(lane == width + 8 * l + comp, line, 0.0) for l in range(k + 1)])
     coefs = jnp.concatenate(coef, axis=0)
-    pieces = []
+    pieces, turns = [], {}
     for c in range(comps):
         for g in range(vecs // 8):
             t, first = PLACES[c, g]
             at = c * vecs + 8 * g
-            piece = pltpu.roll(gram[8 * t : 8 * t + 8], (at - first) % 128, 1)
+            turn = t, (at - first) % 128
+            if turn not in turns:
+                piece = gram[8 * t : 8 * t + 8]
+                turns[turn] = pltpu.roll(piece, turn[1], 1) if turn[1] else piece
+            piece = turns[turn]
             piece = jnp.where(lane < at + 8, 0.5 * piece, piece)
             piece = jnp.where((lane >= at) & (lane < (c + 1) * vecs), piece, 0.0)
             pieces.append(piece - jnp.where(lane == at + comp, 1.0, 0.0))
-    half = split(jnp.concatenate(pieces, axis=0))
-    turned = split_dot(coefs[:, :width], half)
+    half = jnp.concatenate(pieces, axis=0)
+    turned = dot(coefs[:, :width], half, precision=HIGHEST)
+    prev = prev_ref[...].reshape(width, rows)
     basis = jnp.concatenate([lines[...], last[...]], axis=0)
-    projected = basis - split_dot(coefs[:, :width], (p0[...], p1[...], p2[...]))
+    projected = basis - dot(coefs[:, :width], prev, precision=HIGHEST)
     unit, scale = {}, {}
     for l in range(S):
         for k in range(l, S):
@@ -384,10 +391,10 @@
     blocks = columns.shape[0]
     width = strips.shape[1]
     f32, bf16, dma = jnp.float32, jnp.bfloat16, pltpu.SemaphoreType.DMA
-    tile_out = ((comps * blocks, 128), f32)
+    tile_out = ((2 * blocks, 128), f32)
     tile = call(
         start_kernel,
-        [((comps * blocks + 8, 128), f32)],
+        [tile_out],
         [HBM] * 4,
         600000,
         250000,
@@ -396,7 +403,7 @@
             pltpu.VMEM(mix.shape, f32),
             pltpu.VMEM(send_list.shape, jnp.int32),
             pltpu.VMEM(send_count.shape, jnp.int32),
-            dma((4,)),
+            dma((9,)),
         ],
     )(*in_hbm(prev_basis, mix, send_list, send_count))
     high, low, aux = call(
@@ -416,7 +423,7 @@
     length = lax.axis_size("dom")
     tile, choose = call(
         lambda *refs: first_kernel(length, *refs),
-        [tile_out, ((4 * comps * blocks, 128), bf16)],
+        [tile_out, ((8 * blocks, 128), bf16)],
         [VMEM] * 8,
         50000000,
         600000,
@@ -429,9 +436,9 @@
         tiles.append(tile)
     received = ghosts(tile)
     gram_out = ((24, 128), f32)
-    lines, early, *parts = call(
+    lines, early, *turned = call(
         early_kernel,
-        [((8 * S - 8, rows), f32), gram_out] + [((rows, 128), bf16)] * 3 + [((comps * vecs, rows), bf16)] * 3,
+        [((8 * S - 8, rows), f32), gram_out] + [((rows, 128), bf16)] * 3,
         [VMEM] * 4,
         60000000,
         250000,
@@ -442,15 +449,15 @@
         [VMEM] * 13,
         80000000,
         900000,
-    )(tile, *received, choose, aux, high, low, early, *parts[:3])
+    )(tile, *received, choose, aux, high, low, early, *turned)
     total = float(length * rows)
     basis, factors = call(
-        lambda *refs: finish_kernel(total, vecs, *refs),
+        lambda *refs: finish_kernel(total, *refs),
         [((comps, S, rows), f32), ((comps, S, vecs + S), f32)],
-        [VMEM] * 6,
+        [VMEM] * 4,
         50000000,
         400000,
-    )(summed(gram), *parts[3:], lines, last)
+    )(summed(gram), prev_basis, lines, last)
     return basis, jnp.swapaxes(factors, 1, 2)
 
 

time: 41.4 us -> 41.5 us (level)
  no operation moved by 1% of the time
where the time goes in v11:
time: 41.5 us; the launch traced here: 41.3 us
  starting transfers between devices  21.1 us (51%)
  waiting for transfers between devices  13.1 us (32%)
  Pallas kernels  6.4 us (15%)
  between operations  0.72 us (2%)
    ppermute x23, starting transfers between devices, send(): lax.ppermute(value, 'dom', [(d, target[d]) for d in range(lax.axis_size('...  21.1 us
    ppermute x23, waiting for transfers between devices, send(): lax.ppermute(value, 'dom', [(d, target[d]) for d in range(lax.axis_size('...  13.1 us
    pallas_call x1, Pallas kernels, local(): call(prepare_kernel, [((width, rows), bf16), ((width, rows), bf16), ((8 *...  1.39 us
    pallas_call x1, Pallas kernels, local(): call(start_kernel, [tile_out], [HBM] * 4, 600000, 250000, [pltpu.VMEM(pre...  1.18 us
    pallas_call x1, Pallas kernels, local(): call(lambda *refs: finish_kernel(total, *refs), [((comps, S, rows), f32),...  1.02 us
    pallas_call x2, Pallas kernels, local(): call(lambda *refs, step=step: middle_kernel(step, *refs), [tile_out], [VM...  0.92 us
  transfers between devices with their start and end apart: 23, of which 14 were waited for; matrix products, arithmetic and copies ran while one was open for 0% of the time, Pallas kernels for 5%

profile of v11, /device:TPU:0, one launch (start us, length us, event | category | flops | bytes accessed | tf_op | source)
XLA Modules:
  0.0 41.3 jit_solution(6215499075909394453)
XLA Ops:
  0.6 1.2 %shard_map.86.refs_0_ = f32[16,128]{1,0:T(8,128)S(1)} custom-call(f32[3,32,512]{2,1,0:T(8,128)} %refs_1_.1, f32[3,32]{1,0:T(4,128)} %mix_in.1, s32[1,4,8]{2,1,0:T(4,128)} %list_in.1, s32[1,4]{1,0:T(1,128)} %count_in.1), custom_call_target="tpu_custom_call" | custom-call | flops 600000 | bytes 250000 | tf_op jit(solution)/shard_map/pallas_call | solution.py:395
  1.8 3.0 %collective-permute-start.3 = (f32[16,128]{1,0:T(8,128)S(1)}, f32[16,128]{1,0:T(8,128)S(1)}, u32[]{:S(2)}, u32[]{:S(2)}) collective-permute-start(f32[16,128]{1,0:T(8,128)S(1)} %shard_map.86.refs_0_), channel_id=1, source_target_pairs={{0,2},{1,0},{2,1},{3,4},{4,3},{5,6},{6,5},{7,8},{8,7},{9,10},{10,9... | collective-permute-start | bytes 24584 | tf_op jit(solution)/shard_map/ppermute | solution.py:345
  4.8 1.9 %collective-permute-start.2 = (f32[16,128]{1,0:T(8,128)S(1)}, f32[16,128]{1,0:T(8,128)S(1)}, u32[]{:S(2)}, u32[]{:S(2)}) collective-permute-start(f32[16,128]{1,0:T(8,128)S(1)} %shard_map.86.refs_0_), channel_id=1, source_target_pairs={{0,8},{1,9},{2,10},{3,11},{4,12},{5,13},{6,14},{7,15},{8,0},{9,1},... | collective-permute-start | bytes 24584 | tf_op jit(solution)/shard_map/ppermute | solution.py:345
  6.7 0.0 collective-permute-start.1
  6.7 0.0 collective-permute-start
  6.7 1.4 %shard_map.87 = (bf16[256,512]{1,0:T(8,128)(2,1)S(1)}, bf16[256,512]{1,0:T(8,128)(2,1)S(1)}, f32[40,128]{1,0:T(8,128)S(1)}) custom-call(f32[512,256]{1,0:T(8,128)} %strips_in.1, s32[4,8]{1,0:T(4,128)} %bitcast.2, f32[4]{0:T(128)} %shifts_in.1), custom_call_target="tpu_custom_call" | custom-call | flops 1000000 | bytes 1000000 | tf_op jit(solution)/shard_map/pallas_call | solution.py:409
  8.1 0.0 collective-permute-done.3.refs_4_
  8.1 0.4 collective-permute-done.2.refs_3_
  8.5 1.3 %collective-permute-done.1.refs_2_ = f32[16,128]{1,0:T(8,128)S(1)} collective-permute-done((f32[16,128]{1,0:T(8,128)S(1)}, f32[16,128]{1,0:T(8,128)S(1)}, u32[]{:S(2)}, u32[]{:S(2)}) %collective-permute-start.1) | collective-permute-done | bytes 8224 | tf_op jit(solution)/shard_map/ppermute | solution.py:345
  9.7 0.0 collective-permute-done.refs_1_
  9.7 0.6 %shard_map.88 = (f32[16,128]{1,0:T(8,128)S(1)}, bf16[64,128]{1,0:T(8,128)(2,1)S(1)}) custom-call(f32[16,128]{1,0:T(8,128)S(1)} %shard_map.86.refs_0_, f32[16,128]{1,0:T(8,128)S(1)} %collective-permute-done.refs_1_, f32[16,128]{1,0:T(8,128)S(1)} %collective-permute-done.1.refs_2_, f32[16,128]{1,0:T(8,128)S(1)} %collective-permute-done.2.refs_3_, ...), custom_call_target="tpu_custom_call" | custom-call | flops 50000000 | bytes 600000 | tf_op jit(solution)/shard_map/pallas_call | solution.py:424
  10.3 0.5 %collective-permute-start.7 = (f32[16,128]{1,0:T(8,128)S(1)}, f32[16,128]{1,0:T(8,128)S(1)}, u32[]{:S(2)}, u32[]{:S(2)}) collective-permute-start(f32[16,128]{1,0:T(8,128)S(1)} %get-tuple-element.19.refs_0_.t0), channel_id=1, source_target_pairs={{0,2},{1,0},{2,1},{3,4},{4,3},{5,6},{6,5},{7,8},{8,7},{9,10},{10,9... | collective-permute-start | bytes 24584 | tf_op jit(solution)/shard_map/ppermute | solution.py:345
  10.9 1.4 %collective-permute-start.6 = (f32[16,128]{1,0:T(8,128)S(1)}, f32[16,128]{1,0:T(8,128)S(1)}, u32[]{:S(2)}, u32[]{:S(2)}) collective-permute-start(f32[16,128]{1,0:T(8,128)S(1)} %get-tuple-element.19.refs_0_.t0), channel_id=1, source_target_pairs={{0,8},{1,9},{2,10},{3,11},{4,12},{5,13},{6,14},{7,15},{8,0},{9,1},... | collective-permute-start | bytes 24584 | tf_op jit(solution)/shard_map/ppermute | solution.py:345
  12.3 0.2 collective-permute-start.5
  12.5 1.7 %collective-permute-start.4 = (f32[16,128]{1,0:T(8,128)S(1)}, f32[16,128]{1,0:T(8,128)S(1)}, u32[]{:S(2)}, u32[]{:S(2)}) collective-permute-start(f32[16,128]{1,0:T(8,128)S(1)} %get-tuple-element.19.refs_0_.t0), channel_id=1, source_target_pairs={{0,1},{1,0},{2,3},{3,2},{4,5},{5,4},{6,7},{7,6},{8,9},{9,8},{10,11... | collective-permute-start | bytes 24584 | tf_op jit(solution)/shard_map/ppermute | solution.py:345
  14.1 0.0 collective-permute-done.7.refs_4_
  14.1 0.4 collective-permute-done.6.refs_3_
  14.5 0.9 %collective-permute-done.5.refs_2_ = f32[16,128]{1,0:T(8,128)S(1)} collective-permute-done((f32[16,128]{1,0:T(8,128)S(1)}, f32[16,128]{1,0:T(8,128)S(1)}, u32[]{:S(2)}, u32[]{:S(2)}) %collective-permute-start.5) | collective-permute-done | bytes 8224 | tf_op jit(solution)/shard_map/ppermute | solution.py:345
  15.4 0.0 collective-permute-done.4.refs_1_
  15.4 0.5 %shard_map.89.refs_0_.t1 = f32[16,128]{1,0:T(8,128)S(1)} custom-call(f32[16,128]{1,0:T(8,128)S(1)} %get-tuple-element.19.refs_0_.t0, f32[16,128]{1,0:T(8,128)S(1)} %collective-permute-done.4.refs_1_, f32[16,128]{1,0:T(8,128)S(1)} %collective-permute-done.5.refs_2_, f32[16,128]{1,0:T(8,128)S(1)} %collective-permute-done.6.refs_3_, ...), custom_call_target="tpu_custom_call" | custom-call | flops 50000000 | bytes 600000 | tf_op jit(solution)/shard_map/pallas_call | solution.py:433
  15.8 0.0 copy-start
  15.8 1.7 %collective-permute-start.11 = (f32[16,128]{1,0:T(8,128)S(1)}, f32[16,128]{1,0:T(8,128)S(1)}, u32[]{:S(2)}, u32[]{:S(2)}) collective-permute-start(f32[16,128]{1,0:T(8,128)S(1)} %shard_map.89.refs_0_.t1), channel_id=1, source_target_pairs={{0,2},{1,0},{2,1},{3,4},{4,3},{5,6},{6,5},{7,8},{8,7},{9,10},{10,9... | collective-permute-start | bytes 24584 | tf_op jit(solution)/shard_map/ppermute | solution.py:345
  17.6 1.6 %collective-permute-start.10 = (f32[16,128]{1,0:T(8,128)S(1)}, f32[16,128]{1,0:T(8,128)S(1)}, u32[]{:S(2)}, u32[]{:S(2)}) collective-permute-start(f32[16,128]{1,0:T(8,128)S(1)} %shard_map.89.refs_0_.t1), channel_id=1, source_target_pairs={{0,8},{1,9},{2,10},{3,11},{4,12},{5,13},{6,14},{7,15},{8,0},{9,1},... | collective-permute-start | bytes 24584 | tf_op jit(solution)/shard_map/ppermute | solution.py:345
  19.1 0.0 collective-permute-start.9
  19.1 0.0 collective-permute-start.8
  19.1 0.0 collective-permute-done.11.refs_4_
  19.2 2.0 %collective-permute-done.10.refs_3_ = f32[16,128]{1,0:T(8,128)S(1)} collective-permute-done((f32[16,128]{1,0:T(8,128)S(1)}, f32[16,128]{1,0:T(8,128)S(1)}, u32[]{:S(2)}, u32[]{:S(2)}) %collective-permute-start.10) | collective-permute-done | bytes 8224 | tf_op jit(solution)/shard_map/ppermute | solution.py:345
  21.2 1.0 %collective-permute-done.9.refs_2_ = f32[16,128]{1,0:T(8,128)S(1)} collective-permute-done((f32[16,128]{1,0:T(8,128)S(1)}, f32[16,128]{1,0:T(8,128)S(1)}, u32[]{:S(2)}, u32[]{:S(2)}) %collective-permute-start.9) | collective-permute-done | bytes 8224 | tf_op jit(solution)/shard_map/ppermute | solution.py:345
  22.2 0.0 collective-permute-done.8.refs_1_
  22.2 0.5 %shard_map.90.t2.refs_0_ = f32[16,128]{1,0:T(8,128)S(1)} custom-call(f32[16,128]{1,0:T(8,128)S(1)} %shard_map.89.refs_0_.t1, f32[16,128]{1,0:T(8,128)S(1)} %collective-permute-done.8.refs_1_, f32[16,128]{1,0:T(8,128)S(1)} %collective-permute-done.9.refs_2_, f32[16,128]{1,0:T(8,128)S(1)} %collective-permute-done.10.refs_3_, ...), custom_call_target="tpu_custom_call" | custom-call | flops 50000000 | bytes 600000 | tf_op jit(solution)/shard_map/pallas_call | solution.py:433
  22.7 0.0 collective-permute-start.15
  22.7 1.8 %collective-permute-start.14 = (f32[16,128]{1,0:T(8,128)S(1)}, f32[16,128]{1,0:T(8,128)S(1)}, u32[]{:S(2)}, u32[]{:S(2)}) collective-permute-start(f32[16,128]{1,0:T(8,128)S(1)} %shard_map.90.t2.refs_0_), channel_id=1, source_target_pairs={{0,8},{1,9},{2,10},{3,11},{4,12},{5,13},{6,14},{7,15},{8,0},{9,1},... | collective-permute-start | bytes 24584 | tf_op jit(solution)/shard_map/ppermute | solution.py:345
  24.5 0.0 collective-permute-start.13
  24.5 0.4 collective-permute-start.12
  24.9 0.0 copy-done
  24.9 0.6 %shard_map.91 = (f32[24,512]{1,0:T(8,128)S(1)}, f32[24,128]{1,0:T(8,128)S(1)}, bf16[512,128]{1,0:T(8,128)(2,1)S(1)}, bf16[512,128]{1,0:T(8,128)(2,1)S(1)}, bf16[512,128]{1,0:T(8,128)(2,1)S(1)}) custom-call(f32[3,32,512]{2,1,0:T(8,128)S(1)} %copy-done, f32[16,128]{1,0:T(8,128)S(1)} %get-tuple-element.19.refs_0_.t0, f32[16,128]{1,0:T(8,128)S(1)} %shard_map.89.refs_0_.t1, ...), custom_call_target="tpu_custom_call" | custom-call | flops 60000000 | bytes 250000 | tf_op jit(solution)/shard_map/pallas_call | solution.py:439
  25.5 0.0 collective-permute-done.15.refs_4_
  25.5 0.9 %collective-permute-done.14.refs_3_ = f32[16,128]{1,0:T(8,128)S(1)} collective-permute-done((f32[16,128]{1,0:T(8,128)S(1)}, f32[16,128]{1,0:T(8,128)S(1)}, u32[]{:S(2)}, u32[]{:S(2)}) %collective-permute-start.14) | collective-permute-done | bytes 8224 | tf_op jit(solution)/shard_map/ppermute | solution.py:345
  26.4 1.2 %collective-permute-done.13.refs_2_ = f32[16,128]{1,0:T(8,128)S(1)} collective-permute-done((f32[16,128]{1,0:T(8,128)S(1)}, f32[16,128]{1,0:T(8,128)S(1)}, u32[]{:S(2)}, u32[]{:S(2)}) %collective-permute-start.13) | collective-permute-done | bytes 8224 | tf_op jit(solution)/shard_map/ppermute | solution.py:345
  27.6 0.0 collective-permute-done.12.refs_1_
  27.6 0.7 %shard_map.92 = (f32[8,512]{1,0:T(8,128)S(1)}, f32[24,128]{1,0:T(8,128)S(1)}) custom-call(f32[16,128]{1,0:T(8,128)S(1)} %shard_map.90.t2.refs_0_, f32[16,128]{1,0:T(8,128)S(1)} %collective-permute-done.12.refs_1_, f32[16,128]{1,0:T(8,128)S(1)} %collective-permute-done.13.refs_2_, f32[16,128]{1,0:T(8,128)S(1)} %collective-permute-done.14.refs_3_, ...), custom_call_target="tpu_custom_call" | custom-call | flops 80000000 | bytes 900000 | tf_op jit(solution)/shard_map/pallas_call | solution.py:446
  28.3 0.1 collective-permute-start.16
  28.4 1.2 %collective-permute-done.16 = f32[24,128]{1,0:T(8,128)S(1)} collective-permute-done((f32[24,128]{1,0:T(8,128)S(1)}, f32[24,128]{1,0:T(8,128)S(1)}, u32[]{:S(2)}, u32[]{:S(2)}) %collective-permute-start.16) | collective-permute-done | bytes 12320 | tf_op jit(solution)/shard_map/ppermute | solution.py:345
  29.6 1.0 %collective-permute-start.19 = (f32[24,128]{1,0:T(8,128)S(1)}, f32[24,128]{1,0:T(8,128)S(1)}, u32[]{:S(2)}, u32[]{:S(2)}) collective-permute-start(f32[24,128]{1,0:T(8,128)S(1)} %add.21), channel_id=1, source_target_pairs={{0,7},{1,6},{2,5},{3,4},{4,3},{5,2},{6,1},{7,0},{8,15},{9,14},{10,... | collective-permute-start | bytes 36872 | tf_op jit(solution)/shard_map/ppermute | solution.py:345
  30.6 0.4 %collective-permute-start.18 = (f32[24,128]{1,0:T(8,128)S(1)}, f32[24,128]{1,0:T(8,128)S(1)}, u32[]{:S(2)}, u32[]{:S(2)}) collective-permute-start(f32[24,128]{1,0:T(8,128)S(1)} %add.21), channel_id=1, source_target_pairs={{0,5},{1,4},{2,7},{3,6},{4,1},{5,0},{6,3},{7,2},{8,13},{9,12},{10,... | collective-permute-start | bytes 36872 | tf_op jit(solution)/shard_map/ppermute | solution.py:345
  31.0 1.5 %collective-permute-start.17 = (f32[24,128]{1,0:T(8,128)S(1)}, f32[24,128]{1,0:T(8,128)S(1)}, u32[]{:S(2)}, u32[]{:S(2)}) collective-permute-start(f32[24,128]{1,0:T(8,128)S(1)} %add.21), channel_id=1, source_target_pairs={{0,3},{1,2},{2,1},{3,0},{4,7},{5,6},{6,5},{7,4},{8,11},{9,10},{10,... | collective-permute-start | bytes 36872 | tf_op jit(solution)/shard_map/ppermute | solution.py:345
  32.5 1.0 %collective-permute-done.19 = f32[24,128]{1,0:T(8,128)S(1)} collective-permute-done((f32[24,128]{1,0:T(8,128)S(1)}, f32[24,128]{1,0:T(8,128)S(1)}, u32[]{:S(2)}, u32[]{:S(2)}) %collective-permute-start.19) | collective-permute-done | bytes 12320 | tf_op jit(solution)/shard_map/ppermute | solution.py:345
  33.6 0.1 collective-permute-done.18
  33.7 0.4 %collective-permute-done.17 = f32[24,128]{1,0:T(8,128)S(1)} collective-permute-done((f32[24,128]{1,0:T(8,128)S(1)}, f32[24,128]{1,0:T(8,128)S(1)}, u32[]{:S(2)}, u32[]{:S(2)}) %collective-permute-start.17) | collective-permute-done | bytes 12320 | tf_op jit(solution)/shard_map/ppermute | solution.py:345
  34.1 2.0 %collective-permute-start.22 = (f32[24,128]{1,0:T(8,128)S(1)}, f32[24,128]{1,0:T(8,128)S(1)}, u32[]{:S(2)}, u32[]{:S(2)}) collective-permute-start(f32[24,128]{1,0:T(8,128)S(1)} %add_add_fusion.1), channel_id=1, source_target_pairs={{0,25},{1,24},{2,27},{3,26},{4,29},{5,28},{6,31},{7,30},{8,17},{9,... | collective-permute-start | bytes 36872 | tf_op jit(solution)/shard_map/ppermute | solution.py:345
  36.2 0.2 collective-permute-start.21
  36.4 1.6 %collective-permute-start.20 = (f32[24,128]{1,0:T(8,128)S(1)}, f32[24,128]{1,0:T(8,128)S(1)}, u32[]{:S(2)}, u32[]{:S(2)}) collective-permute-start(f32[24,128]{1,0:T(8,128)S(1)} %add_add_fusion.1), channel_id=1, source_target_pairs={{0,9},{1,8},{2,11},{3,10},{4,13},{5,12},{6,15},{7,14},{8,1},{9,0},... | collective-permute-start | bytes 36872 | tf_op jit(solution)/shard_map/ppermute | solution.py:345
  38.0 1.0 %collective-permute-done.22 = f32[24,128]{1,0:T(8,128)S(1)} collective-permute-done((f32[24,128]{1,0:T(8,128)S(1)}, f32[24,128]{1,0:T(8,128)S(1)}, u32[]{:S(2)}, u32[]{:S(2)}) %collective-permute-start.22) | collective-permute-done | bytes 12320 | tf_op jit(solution)/shard_map/ppermute | solution.py:345
  39.1 1.2 %collective-permute-done.21 = f32[24,128]{1,0:T(8,128)S(1)} collective-permute-done((f32[24,128]{1,0:T(8,128)S(1)}, f32[24,128]{1,0:T(8,128)S(1)}, u32[]{:S(2)}, u32[]{:S(2)}) %collective-permute-start.21) | collective-permute-done | bytes 12320 | tf_op jit(solution)/shard_map/ppermute | solution.py:345
  40.3 0.0 collective-permute-done.20
  40.3 1.0 %shard_map.93 = (f32[3,4,512]{2,1,0:T(4,128)}, f32[3,4,36]{2,1,0:T(4,128)}) custom-call(f32[24,128]{1,0:T(8,128)S(1)} %add_add_fusion.refs_0_, f32[3,32,512]{2,1,0:T(8,128)S(1)} %copy-done, f32[24,512]{1,0:T(8,128)S(1)} %get-tuple-element.26.refs_2_, f32[8,512]{1,0:T(8,128)S(1)} %get-tuple-element.27.refs_3_), custom_call_target="tpu_custom_call" | custom-call | flops 50000000 | bytes 400000 | tf_op jit(solution)/shard_map/pallas_call | solution.py:454
  (3 shorter events, 0.0 us)
Async XLA Ops:
  1.8 6.3 %collective-permute-start.3 = (f32[16,128]{1,0:T(8,128)S(1)}, f32[16,128]{1,0:T(8,128)S(1)}, u32[]{:S(2)}, u32[]{:S(2)}) collective-permute-start(f32[16,128]{1,0:T(8,128)S(1)} %shard_map.86.refs_0_), channel_id=1, source_target_pairs={{0,2},{1,0},{2,1},{3,4},{4,3},{5,6},{6,5},{7,8},{8,7},{9,10},{10,9... | collective-permute-start | bytes 24584 | tf_op jit(solution)/shard_map/ppermute | solution.py:345
  4.8 3.7 %collective-permute-start.2 = (f32[16,128]{1,0:T(8,128)S(1)}, f32[16,128]{1,0:T(8,128)S(1)}, u32[]{:S(2)}, u32[]{:S(2)}) collective-permute-start(f32[16,128]{1,0:T(8,128)S(1)} %shard_map.86.refs_0_), channel_id=1, source_target_pairs={{0,8},{1,9},{2,10},{3,11},{4,12},{5,13},{6,14},{7,15},{8,0},{9,1},... | collective-permute-start | bytes 24584 | tf_op jit(solution)/shard_map/ppermute | solution.py:345
  6.7 3.1 %collective-permute-start.1 = (f32[16,128]{1,0:T(8,128)S(1)}, f32[16,128]{1,0:T(8,128)S(1)}, u32[]{:S(2)}, u32[]{:S(2)}) collective-permute-start(f32[16,128]{1,0:T(8,128)S(1)} %shard_map.86.refs_0_), channel_id=1, source_target_pairs={{0,1},{1,2},{2,3},{3,0},{4,5},{5,4},{6,7},{7,6},{8,16},{9,17},{10,... | collective-permute-start | bytes 24584 | tf_op jit(solution)/shard_map/ppermute | solution.py:345
  6.7 3.1 %collective-permute-start = (f32[16,128]{1,0:T(8,128)S(1)}, f32[16,128]{1,0:T(8,128)S(1)}, u32[]{:S(2)}, u32[]{:S(2)}) collective-permute-start(f32[16,128]{1,0:T(8,128)S(1)} %shard_map.86.refs_0_), channel_id=1, source_target_pairs={{0,1},{1,0},{2,3},{3,2},{4,5},{5,4},{6,7},{7,6},{8,9},{9,8},{10,11... | collective-permute-start | bytes 24584 | tf_op jit(solution)/shard_map/ppermute | solution.py:345
  10.3 3.8 %collective-permute-start.7 = (f32[16,128]{1,0:T(8,128)S(1)}, f32[16,128]{1,0:T(8,128)S(1)}, u32[]{:S(2)}, u32[]{:S(2)}) collective-permute-start(f32[16,128]{1,0:T(8,128)S(1)} %get-tuple-element.19.refs_0_.t0), channel_id=1, source_target_pairs={{0,2},{1,0},{2,1},{3,4},{4,3},{5,6},{6,5},{7,8},{8,7},{9,10},{10,9... | collective-permute-start | bytes 24584 | tf_op jit(solution)/shard_map/ppermute | solution.py:345
  10.9 3.7 %collective-permute-start.6 = (f32[16,128]{1,0:T(8,128)S(1)}, f32[16,128]{1,0:T(8,128)S(1)}, u32[]{:S(2)}, u32[]{:S(2)}) collective-permute-start(f32[16,128]{1,0:T(8,128)S(1)} %get-tuple-element.19.refs_0_.t0), channel_id=1, source_target_pairs={{0,8},{1,9},{2,10},{3,11},{4,12},{5,13},{6,14},{7,15},{8,0},{9,1},... | collective-permute-start | bytes 24584 | tf_op jit(solution)/shard_map/ppermute | solution.py:345
  12.3 3.1 %collective-permute-start.5 = (f32[16,128]{1,0:T(8,128)S(1)}, f32[16,128]{1,0:T(8,128)S(1)}, u32[]{:S(2)}, u32[]{:S(2)}) collective-permute-start(f32[16,128]{1,0:T(8,128)S(1)} %get-tuple-element.19.refs_0_.t0), channel_id=1, source_target_pairs={{0,1},{1,2},{2,3},{3,0},{4,5},{5,4},{6,7},{7,6},{8,16},{9,17},{10,... | collective-permute-start | bytes 24584 | tf_op jit(solution)/shard_map/ppermute | solution.py:345
  12.5 2.9 %collective-permute-start.4 = (f32[16,128]{1,0:T(8,128)S(1)}, f32[16,128]{1,0:T(8,128)S(1)}, u32[]{:S(2)}, u32[]{:S(2)}) collective-permute-start(f32[16,128]{1,0:T(8,128)S(1)} %get-tuple-element.19.refs_0_.t0), channel_id=1, source_target_pairs={{0,1},{1,0},{2,3},{3,2},{4,5},{5,4},{6,7},{7,6},{8,9},{9,8},{10,11... | collective-permute-start | bytes 24584 | tf_op jit(solution)/shard_map/ppermute | solution.py:345
  15.8 9.1 %copy-start = (f32[3,32,512]{2,1,0:T(8,128)S(1)}, f32[3,32,512]{2,1,0:T(8,128)}, u32[]{:S(2)}) copy-start(f32[3,32,512]{2,1,0:T(8,128)} %refs_1_.1) | copy-start | bytes 589828
  15.8 3.3 %collective-permute-start.11 = (f32[16,128]{1,0:T(8,128)S(1)}, f32[16,128]{1,0:T(8,128)S(1)}, u32[]{:S(2)}, u32[]{:S(2)}) collective-permute-start(f32[16,128]{1,0:T(8,128)S(1)} %shard_map.89.refs_0_.t1), channel_id=1, source_target_pairs={{0,2},{1,0},{2,1},{3,4},{4,3},{5,6},{6,5},{7,8},{8,7},{9,10},{10,9... | collective-permute-start | bytes 24584 | tf_op jit(solution)/shard_map/ppermute | solution.py:345
  17.6 3.7 %collective-permute-start.10 = (f32[16,128]{1,0:T(8,128)S(1)}, f32[16,128]{1,0:T(8,128)S(1)}, u32[]{:S(2)}, u32[]{:S(2)}) collective-permute-start(f32[16,128]{1,0:T(8,128)S(1)} %shard_map.89.refs_0_.t1), channel_id=1, source_target_pairs={{0,8},{1,9},{2,10},{3,11},{4,12},{5,13},{6,14},{7,15},{8,0},{9,1},... | collective-permute-start | bytes 24584 | tf_op jit(solution)/shard_map/ppermute | solution.py:345
  19.1 3.1 %collective-permute-start.9 = (f32[16,128]{1,0:T(8,128)S(1)}, f32[16,128]{1,0:T(8,128)S(1)}, u32[]{:S(2)}, u32[]{:S(2)}) collective-permute-start(f32[16,128]{1,0:T(8,128)S(1)} %shard_map.89.refs_0_.t1), channel_id=1, source_target_pairs={{0,1},{1,2},{2,3},{3,0},{4,5},{5,4},{6,7},{7,6},{8,16},{9,17},{10,... | collective-permute-start | bytes 24584 | tf_op jit(solution)/shard_map/ppermute | solution.py:345
  19.1 3.1 %collective-permute-start.8 = (f32[16,128]{1,0:T(8,128)S(1)}, f32[16,128]{1,0:T(8,128)S(1)}, u32[]{:S(2)}, u32[]{:S(2)}) collective-permute-start(f32[16,128]{1,0:T(8,128)S(1)} %shard_map.89.refs_0_.t1), channel_id=1, source_target_pairs={{0,1},{1,0},{2,3},{3,2},{4,5},{5,4},{6,7},{7,6},{8,9},{9,8},{10,11... | collective-permute-start | bytes 24584 | tf_op jit(solution)/shard_map/ppermute | solution.py:345
  22.7 2.8 %collective-permute-start.15 = (f32[16,128]{1,0:T(8,128)S(1)}, f32[16,128]{1,0:T(8,128)S(1)}, u32[]{:S(2)}, u32[]{:S(2)}) collective-permute-start(f32[16,128]{1,0:T(8,128)S(1)} %shard_map.90.t2.refs_0_), channel_id=1, source_target_pairs={{0,2},{1,0},{2,1},{3,4},{4,3},{5,6},{6,5},{7,8},{8,7},{9,10},{10,9... | collective-permute-start | bytes 24584 | tf_op jit(solution)/shard_map/ppermute | solution.py:345
  22.7 3.7 %collective-permute-start.14 = (f32[16,128]{1,0:T(8,128)S(1)}, f32[16,128]{1,0:T(8,128)S(1)}, u32[]{:S(2)}, u32[]{:S(2)}) collective-permute-start(f32[16,128]{1,0:T(8,128)S(1)} %shard_map.90.t2.refs_0_), channel_id=1, source_target_pairs={{0,8},{1,9},{2,10},{3,11},{4,12},{5,13},{6,14},{7,15},{8,0},{9,1},... | collective-permute-start | bytes 24584 | tf_op jit(solution)/shard_map/ppermute | solution.py:345
  24.5 3.1 %collective-permute-start.13 = (f32[16,128]{1,0:T(8,128)S(1)}, f32[16,128]{1,0:T(8,128)S(1)}, u32[]{:S(2)}, u32[]{:S(2)}) collective-permute-start(f32[16,128]{1,0:T(8,128)S(1)} %shard_map.90.t2.refs_0_), channel_id=1, source_target_pairs={{0,1},{1,2},{2,3},{3,0},{4,5},{5,4},{6,7},{7,6},{8,16},{9,17},{10,... | collective-permute-start | bytes 24584 | tf_op jit(solution)/shard_map/ppermute | solution.py:345
  24.5 3.1 %collective-permute-start.12 = (f32[16,128]{1,0:T(8,128)S(1)}, f32[16,128]{1,0:T(8,128)S(1)}, u32[]{:S(2)}, u32[]{:S(2)}) collective-permute-start(f32[16,128]{1,0:T(8,128)S(1)} %shard_map.90.t2.refs_0_), channel_id=1, source_target_pairs={{0,1},{1,0},{2,3},{3,2},{4,5},{5,4},{6,7},{7,6},{8,9},{9,8},{10,11... | collective-permute-start | bytes 24584 | tf_op jit(solution)/shard_map/ppermute | solution.py:345
  28.3 1.2 %collective-permute-start.16 = (f32[24,128]{1,0:T(8,128)S(1)}, f32[24,128]{1,0:T(8,128)S(1)}, u32[]{:S(2)}, u32[]{:S(2)}) collective-permute-start(f32[24,128]{1,0:T(8,128)S(1)} %get-tuple-element.25), channel_id=1, source_target_pairs={{0,1},{1,0},{2,3},{3,2},{4,5},{5,4},{6,7},{7,6},{8,9},{9,8},{10,11... | collective-permute-start | bytes 36872 | tf_op jit(solution)/shard_map/ppermute | solution.py:345
  29.6 4.0 %collective-permute-start.19 = (f32[24,128]{1,0:T(8,128)S(1)}, f32[24,128]{1,0:T(8,128)S(1)}, u32[]{:S(2)}, u32[]{:S(2)}) collective-permute-start(f32[24,128]{1,0:T(8,128)S(1)} %add.21), channel_id=1, source_target_pairs={{0,7},{1,6},{2,5},{3,4},{4,3},{5,2},{6,1},{7,0},{8,15},{9,14},{10,... | collective-permute-start | bytes 36872 | tf_op jit(solution)/shard_map/ppermute | solution.py:345
  30.6 3.1 %collective-permute-start.18 = (f32[24,128]{1,0:T(8,128)S(1)}, f32[24,128]{1,0:T(8,128)S(1)}, u32[]{:S(2)}, u32[]{:S(2)}) collective-permute-start(f32[24,128]{1,0:T(8,128)S(1)} %add.21), channel_id=1, source_target_pairs={{0,5},{1,4},{2,7},{3,6},{4,1},{5,0},{6,3},{7,2},{8,13},{9,12},{10,... | collective-permute-start | bytes 36872 | tf_op jit(solution)/shard_map/ppermute | solution.py:345
  31.0 3.1 %collective-permute-start.17 = (f32[24,128]{1,0:T(8,128)S(1)}, f32[24,128]{1,0:T(8,128)S(1)}, u32[]{:S(2)}, u32[]{:S(2)}) collective-permute-start(f32[24,128]{1,0:T(8,128)S(1)} %add.21), channel_id=1, source_target_pairs={{0,3},{1,2},{2,1},{3,0},{4,7},{5,6},{6,5},{7,4},{8,11},{9,10},{10,... | collective-permute-start | bytes 36872 | tf_op jit(solution)/shard_map/ppermute | solution.py:345
  34.1 4.9 %collective-permute-start.22 = (f32[24,128]{1,0:T(8,128)S(1)}, f32[24,128]{1,0:T(8,128)S(1)}, u32[]{:S(2)}, u32[]{:S(2)}) collective-permute-start(f32[24,128]{1,0:T(8,128)S(1)} %add_add_fusion.1), channel_id=1, source_target_pairs={{0,25},{1,24},{2,27},{3,26},{4,29},{5,28},{6,31},{7,30},{8,17},{9,... | collective-permute-start | bytes 36872 | tf_op jit(solution)/shard_map/ppermute | solution.py:345
  36.2 4.1 %collective-permute-start.21 = (f32[24,128]{1,0:T(8,128)S(1)}, f32[24,128]{1,0:T(8,128)S(1)}, u32[]{:S(2)}, u32[]{:S(2)}) collective-permute-start(f32[24,128]{1,0:T(8,128)S(1)} %add_add_fusion.1), channel_id=1, source_target_pairs={{0,17},{1,16},{2,19},{3,18},{4,21},{5,20},{6,23},{7,22},{8,25},{9,... | collective-permute-start | bytes 36872 | tf_op jit(solution)/shard_map/ppermute | solution.py:345
  36.4 3.9 %collective-permute-start.20 = (f32[24,128]{1,0:T(8,128)S(1)}, f32[24,128]{1,0:T(8,128)S(1)}, u32[]{:S(2)}, u32[]{:S(2)}) collective-permute-start(f32[24,128]{1,0:T(8,128)S(1)} %add_add_fusion.1), channel_id=1, source_target_pairs={{0,9},{1,8},{2,11},{3,10},{4,13},{5,12},{6,15},{7,14},{8,1},{9,0},... | collective-permute-start | bytes 36872 | tf_op jit(solution)/shard_map/ppermute | solution.py:345

commit v12 on v10

--- a/solution.py
+++ b/solution.py
@@ -23,20 +23,8 @@
     return lax.broadcasted_iota(jnp.int32, shape, axis)
 
 
-PLACES = {
-    (0, 0): (0, 0),
-    (0, 1): (0, 32),
-    (0, 2): (0, 56),
-    (0, 3): (0, 72),
-    (1, 0): (0, 80),
-    (1, 2): (0, 112),
-    (1, 1): (1, 0),
-    (1, 3): (1, 24),
-    (2, 0): (1, 32),
-    (2, 1): (1, 64),
-    (2, 2): (1, 88),
-    (2, 3): (1, 104),
-}
+PLACES = {(c, g): (g % 2, (0, 8, 0, 0)[g] + 32 * c) for c in range(COMPS) for g in range(4)}
+PLACES.update({(0, 2): (0, 96), (1, 2): (0, 112), (2, 2): (1, 96)})
 
 
 def own_lanes(rows, width):
@@ -146,12 +134,12 @@
     near, far_odd, far_even, across = metas
     moved = (place == 2) | (place == length - 3)
     across = jnp.where(moved, far_odd, across)
-    circle = jnp.where(moved, 48.0, 96.0)
+    circle = jnp.where(moved, 16.0, 32.0)
     slots = [
-        (place >= 1, jnp.where(even, circle, 24.0), jnp.where(even, across, near)),
-        (place < length - 1, jnp.where(even, 24.0, circle), jnp.where(even, near, across)),
-        (place >= FAR, jnp.where(even_far, 48.0, 72.0), jnp.where(even_far, far_odd, far_even)),
-        (place < length - FAR, jnp.where(even_far, 72.0, 48.0), jnp.where(even_far, far_even, far_odd)),
+        (place >= 1, jnp.where(even, circle, 8.0), jnp.where(even, across, near)),
+        (place < length - 1, jnp.where(even, 8.0, circle), jnp.where(even, near, across)),
+        (place >= FAR, jnp.where(even_far, 16.0, 24.0), jnp.where(even_far, far_odd, far_even)),
+        (place < length - FAR, jnp.where(even_far, 24.0, 16.0), jnp.where(even_far, far_even, far_odd)),
     ]
     lane = iota((1, 128), 1)
     target = lane.astype(jnp.float32)
@@ -164,27 +152,33 @@
         jnp.sum(jnp.where(lane == table[:, k : k + 1], target, 0.0), axis=1, keepdims=True)
         for k in range(4)
     ]
-    groups = [(lane == at[k] + float(8 * c)).astype(jnp.float32) for k in range(4) for c in range(COMPS)]
-    return jnp.concatenate(groups, axis=0).astype(jnp.bfloat16)
+    return jnp.concatenate([jnp.broadcast_to(x, (8, 128)) for x in at], axis=0).astype(jnp.int32)
 
 
 def multiply(choose, pieces, shift, high, low):
     rows = 8 * COMPS
-    ext = jnp.concatenate(pieces + [jnp.zeros((128 - 5 * rows, 128), jnp.float32)], axis=0)
-    top = ext.astype(jnp.bfloat16).astype(jnp.float32)
-    x = dot(choose, jnp.concatenate([top, ext - top], axis=1).astype(jnp.bfloat16))
-    front = iota((rows, 256), 1) % 128 < BLOCK
-    pairs = [
-        jnp.where(front, x[2 * t * rows : (2 * t + 1) * rows], x[(2 * t + 1) * rows : (2 * t + 2) * rows])
-        for t in range(2)
+    front = iota((8, 128), 1) < BLOCK
+    picked = []
+    for k in range(4):
+        code = choose[8 * k : 8 * k + 8]
+        index, place = code & 7, code >> 3
+        blocks = []
+        for c in range(COMPS):
+            block = jnp.zeros((8, 128), jnp.float32)
+            for p, piece in enumerate(pieces):
+                found = jnp.take_along_axis(piece[8 * c : 8 * c + 8], index, axis=0)
+                block = jnp.where(place == p, found, block)
+            blocks.append(block)
+        picked.append(blocks)
+    x = [
+        jnp.concatenate(
+            [jnp.where(front, picked[2 * t][c], picked[2 * t + 1][c]) for t in range(2)], axis=1
+        )
+        for c in range(COMPS)
     ]
-    left = jnp.concatenate(
-        [
-            jnp.concatenate([pair[:, half * 128 : (half + 1) * 128] for pair in pairs], axis=1)
-            for half in range(2)
-        ],
-        axis=0,
-    ).astype(jnp.bfloat16)
+    x = jnp.concatenate(x, axis=0)
+    top = x.astype(jnp.bfloat16).astype(jnp.float32)
+    left = jnp.concatenate([top, x - top], axis=0).astype(jnp.bfloat16)
     both = dot(left, high) + dot(left, low)
     image = both[:rows] + both[rows:]
     image = fold(jnp.where(own_lanes(rows, image.shape[1]), image, 0.0))
@@ -228,7 +222,7 @@
         tiles[t] = jnp.where((lane >= first) & (lane < first + vecs - 8 * g), piece, tiles[t])
     gram_ref[:16, :] = jnp.concatenate(tiles, axis=0)
     against = jnp.concatenate([prev, lines, jnp.zeros((8, rows), jnp.float32)], axis=0)
-    for ref, part in zip(split_refs, split(against.T) + split(prev)):
+    for ref, part in zip(split_refs, split(against.T)):
         ref[...] = part
     gram = dot(lines, against, NT, HIGHEST)
     result = jnp.zeros((8, 128), jnp.float32)
@@ -255,8 +249,8 @@
     )
 
 
-def finish_kernel(total, vecs, gram_in, p0, p1, p2, lines, last, basis_ref, factors_ref):
-    comps = COMPS
+def finish_kernel(total, gram_in, prev_ref, lines, last, basis_ref, factors_ref):
+    comps, vecs, rows = prev_ref.shape
     width = comps * vecs
     gram = gram_in[...] * (1.0 / total)
     small = gram[16:]
@@ -268,19 +262,24 @@
         coef.append(jnp.where(in_prev, line, 0.0))
         cross.append([jnp.where(lane == width + 8 * l + comp, line, 0.0) for l in range(k + 1)])
     coefs = jnp.concatenate(coef, axis=0)
-    pieces = []
+    pieces, turns = [], {}
     for c in range(comps):
         for g in range(vecs // 8):
             t, first = PLACES[c, g]
             at = c * vecs + 8 * g
-            piece = pltpu.roll(gram[8 * t : 8 * t + 8], (at - first) % 128, 1)
+            turn = t, (at - first) % 128
+            if turn not in turns:
+                piece = gram[8 * t : 8 * t + 8]
+                turns[turn] = pltpu.roll(piece, turn[1], 1) if turn[1] else piece
+            piece = turns[turn]
             piece = jnp.where(lane < at + 8, 0.5 * piece, piece)
             piece = jnp.where((lane >= at) & (lane < (c + 1) * vecs), piece, 0.0)
             pieces.append(piece - jnp.where(lane == at + comp, 1.0, 0.0))
-    half = split(jnp.concatenate(pieces, axis=0))
-    turned = split_dot(coefs[:, :width], half)
+    half = jnp.concatenate(pieces, axis=0)
+    turned = dot(coefs[:, :width], half, precision=HIGHEST)
+    prev = prev_ref[...].reshape(width, rows)
     basis = jnp.concatenate([lines[...], last[...]], axis=0)
-    projected = basis - split_dot(coefs[:, :width], (p0[...], p1[...], p2[...]))
+    projected = basis - dot(coefs[:, :width], prev, precision=HIGHEST)
     unit, scale = {}, {}
     for l in range(S):
         for k in range(l, S):
@@ -416,7 +415,7 @@
     length = lax.axis_size("dom")
     tile, choose = call(
         lambda *refs: first_kernel(length, *refs),
-        [tile_out, ((4 * comps * blocks, 128), bf16)],
+        [tile_out, ((4 * blocks, 128), jnp.int32)],
         [VMEM] * 8,
         50000000,
         600000,
@@ -431,7 +430,7 @@
     gram_out = ((24, 128), f32)
     lines, early, *parts = call(
         early_kernel,
-        [((8 * S - 8, rows), f32), gram_out] + [((rows, 128), bf16)] * 3 + [((comps * vecs, rows), bf16)] * 3,
+        [((8 * S - 8, rows), f32), gram_out] + [((rows, 128), bf16)] * 3,
         [VMEM] * 4,
         60000000,
         250000,
@@ -442,15 +441,15 @@
         [VMEM] * 13,
         80000000,
         900000,
-    )(tile, *received, choose, aux, high, low, early, *parts[:3])
+    )(tile, *received, choose, aux, high, low, early, *parts)
     total = float(length * rows)
     basis, factors = call(
-        lambda *refs: finish_kernel(total, vecs, *refs),
+        lambda *refs: finish_kernel(total, *refs),
         [((comps, S, rows), f32), ((comps, S, vecs + S), f32)],
-        [VMEM] * 6,
+        [VMEM] * 4,
         50000000,
         400000,
-    )(summed(gram), *parts[3:], lines, last)
+    )(summed(gram), prev_basis, lines, last)
     return basis, jnp.swapaxes(factors, 1, 2)
 
 

time: 41.4 us -> 40.9 us (0.988)
  Pallas kernels: 6.04 us -> 5.48 us
where the time goes in v12:
time: 40.9 us; the launch traced here: 40.7 us
  starting transfers between devices  21.1 us (52%)
  waiting for transfers between devices  13.4 us (33%)
  Pallas kernels  5.48 us (13%)
  between operations  0.72 us (2%)
    ppermute x23, starting transfers between devices, send(): lax.ppermute(value, 'dom', [(d, target[d]) for d in range(lax.axis_size('...  21.1 us
    ppermute x23, waiting for transfers between devices, send(): lax.ppermute(value, 'dom', [(d, target[d]) for d in range(lax.axis_size('...  13.4 us
    pallas_call x1, Pallas kernels, local(): call(prepare_kernel, [((width, rows), bf16), ((width, rows), bf16), ((8 *...  1.39 us
    pallas_call x1, Pallas kernels, local(): call(start_kernel, [((comps * blocks + 8, 128), f32)], [HBM] * 4, 600000,...  1.08 us
    pallas_call x1, Pallas kernels, local(): call(lambda *refs: finish_kernel(total, *refs), [((comps, S, rows), f32),...  1.02 us
  transfers between devices with their start and end apart: 23, of which 14 were waited for; matrix products, arithmetic and copies ran while one was open for 0% of the time, Pallas kernels for 5%

profile of v12, /device:TPU:0, one launch (start us, length us, event | category | flops | bytes accessed | tf_op | source)
XLA Modules:
  0.0 40.7 jit_solution(6643204216337430347)
XLA Ops:
  0.6 1.1 %shard_map.86.refs_0_ = f32[32,128]{1,0:T(8,128)S(1)} custom-call(f32[3,32,512]{2,1,0:T(8,128)} %refs_1_.1, f32[3,32]{1,0:T(4,128)} %mix_in.1, s32[1,4,8]{2,1,0:T(4,128)} %list_in.1, s32[1,4]{1,0:T(1,128)} %count_in.1), custom_call_target="tpu_custom_call" | custom-call | flops 600000 | bytes 250000 | tf_op jit(solution)/shard_map/pallas_call | solution.py:387
  1.7 3.0 %collective-permute-start.3 = (f32[32,128]{1,0:T(8,128)S(1)}, f32[32,128]{1,0:T(8,128)S(1)}, u32[]{:S(2)}, u32[]{:S(2)}) collective-permute-start(f32[32,128]{1,0:T(8,128)S(1)} %shard_map.86.refs_0_), channel_id=1, source_target_pairs={{0,2},{1,0},{2,1},{3,4},{4,3},{5,6},{6,5},{7,8},{8,7},{9,10},{10,9... | collective-permute-start | bytes 49160 | tf_op jit(solution)/shard_map/ppermute | solution.py:337
  4.7 1.9 %collective-permute-start.2 = (f32[32,128]{1,0:T(8,128)S(1)}, f32[32,128]{1,0:T(8,128)S(1)}, u32[]{:S(2)}, u32[]{:S(2)}) collective-permute-start(f32[32,128]{1,0:T(8,128)S(1)} %shard_map.86.refs_0_), channel_id=1, source_target_pairs={{0,8},{1,9},{2,10},{3,11},{4,12},{5,13},{6,14},{7,15},{8,0},{9,1},... | collective-permute-start | bytes 49160 | tf_op jit(solution)/shard_map/ppermute | solution.py:337
  6.6 0.0 collective-permute-start.1
  6.6 0.0 collective-permute-start
  6.6 1.4 %shard_map.87 = (bf16[256,512]{1,0:T(8,128)(2,1)S(1)}, bf16[256,512]{1,0:T(8,128)(2,1)S(1)}, f32[40,128]{1,0:T(8,128)S(1)}) custom-call(f32[512,256]{1,0:T(8,128)} %strips_in.1, s32[4,8]{1,0:T(4,128)} %bitcast.2, f32[4]{0:T(128)} %shifts_in.1), custom_call_target="tpu_custom_call" | custom-call | flops 1000000 | bytes 1000000 | tf_op jit(solution)/shard_map/pallas_call | solution.py:401
  8.0 0.0 collective-permute-done.3.refs_4_
  8.0 0.5 %collective-permute-done.2.refs_3_ = f32[32,128]{1,0:T(8,128)S(1)} collective-permute-done((f32[32,128]{1,0:T(8,128)S(1)}, f32[32,128]{1,0:T(8,128)S(1)}, u32[]{:S(2)}, u32[]{:S(2)}) %collective-permute-start.2) | collective-permute-done | bytes 16416 | tf_op jit(solution)/shard_map/ppermute | solution.py:337
  8.5 1.3 %collective-permute-done.1.refs_2_ = f32[32,128]{1,0:T(8,128)S(1)} collective-permute-done((f32[32,128]{1,0:T(8,128)S(1)}, f32[32,128]{1,0:T(8,128)S(1)}, u32[]{:S(2)}, u32[]{:S(2)}) %collective-permute-start.1) | collective-permute-done | bytes 16416 | tf_op jit(solution)/shard_map/ppermute | solution.py:337
  9.7 0.0 collective-permute-done.refs_1_
  9.7 0.4 shard_map.88
  10.1 0.4 %collective-permute-start.7 = (f32[24,128]{1,0:T(8,128)S(1)}, f32[24,128]{1,0:T(8,128)S(1)}, u32[]{:S(2)}, u32[]{:S(2)}) collective-permute-start(f32[24,128]{1,0:T(8,128)S(1)} %get-tuple-element.19.refs_0_.t0), channel_id=1, source_target_pairs={{0,2},{1,0},{2,1},{3,4},{4,3},{5,6},{6,5},{7,8},{8,7},{9,10},{10,9... | collective-permute-start | bytes 36872 | tf_op jit(solution)/shard_map/ppermute | solution.py:337
  10.6 1.4 %collective-permute-start.6 = (f32[24,128]{1,0:T(8,128)S(1)}, f32[24,128]{1,0:T(8,128)S(1)}, u32[]{:S(2)}, u32[]{:S(2)}) collective-permute-start(f32[24,128]{1,0:T(8,128)S(1)} %get-tuple-element.19.refs_0_.t0), channel_id=1, source_target_pairs={{0,8},{1,9},{2,10},{3,11},{4,12},{5,13},{6,14},{7,15},{8,0},{9,1},... | collective-permute-start | bytes 36872 | tf_op jit(solution)/shard_map/ppermute | solution.py:337
  12.0 0.2 collective-permute-start.5
  12.2 1.7 %collective-permute-start.4 = (f32[24,128]{1,0:T(8,128)S(1)}, f32[24,128]{1,0:T(8,128)S(1)}, u32[]{:S(2)}, u32[]{:S(2)}) collective-permute-start(f32[24,128]{1,0:T(8,128)S(1)} %get-tuple-element.19.refs_0_.t0), channel_id=1, source_target_pairs={{0,1},{1,0},{2,3},{3,2},{4,5},{5,4},{6,7},{7,6},{8,9},{9,8},{10,11... | collective-permute-start | bytes 36872 | tf_op jit(solution)/shard_map/ppermute | solution.py:337
  13.8 0.0 collective-permute-done.7.refs_4_
  13.8 0.4 %collective-permute-done.6.refs_3_ = f32[24,128]{1,0:T(8,128)S(1)} collective-permute-done((f32[24,128]{1,0:T(8,128)S(1)}, f32[24,128]{1,0:T(8,128)S(1)}, u32[]{:S(2)}, u32[]{:S(2)}) %collective-permute-start.6) | collective-permute-done | bytes 12320 | tf_op jit(solution)/shard_map/ppermute | solution.py:337
  14.3 0.9 %collective-permute-done.5.refs_2_ = f32[24,128]{1,0:T(8,128)S(1)} collective-permute-done((f32[24,128]{1,0:T(8,128)S(1)}, f32[24,128]{1,0:T(8,128)S(1)}, u32[]{:S(2)}, u32[]{:S(2)}) %collective-permute-start.5) | collective-permute-done | bytes 12320 | tf_op jit(solution)/shard_map/ppermute | solution.py:337
  15.1 0.0 collective-permute-done.4.refs_1_
  15.1 0.3 shard_map.89.refs_0_.t1
  15.4 0.0 copy-start
  15.4 1.7 %collective-permute-start.11 = (f32[24,128]{1,0:T(8,128)S(1)}, f32[24,128]{1,0:T(8,128)S(1)}, u32[]{:S(2)}, u32[]{:S(2)}) collective-permute-start(f32[24,128]{1,0:T(8,128)S(1)} %shard_map.89.refs_0_.t1), channel_id=1, source_target_pairs={{0,2},{1,0},{2,1},{3,4},{4,3},{5,6},{6,5},{7,8},{8,7},{9,10},{10,9... | collective-permute-start | bytes 36872 | tf_op jit(solution)/shard_map/ppermute | solution.py:337
  17.1 1.6 %collective-permute-start.10 = (f32[24,128]{1,0:T(8,128)S(1)}, f32[24,128]{1,0:T(8,128)S(1)}, u32[]{:S(2)}, u32[]{:S(2)}) collective-permute-start(f32[24,128]{1,0:T(8,128)S(1)} %shard_map.89.refs_0_.t1), channel_id=1, source_target_pairs={{0,8},{1,9},{2,10},{3,11},{4,12},{5,13},{6,14},{7,15},{8,0},{9,1},... | collective-permute-start | bytes 36872 | tf_op jit(solution)/shard_map/ppermute | solution.py:337
  18.8 0.0 collective-permute-start.9
  18.8 0.0 collective-permute-start.8
  18.8 0.0 collective-permute-done.11.refs_4_
  18.8 2.0 %collective-permute-done.10.refs_3_ = f32[24,128]{1,0:T(8,128)S(1)} collective-permute-done((f32[24,128]{1,0:T(8,128)S(1)}, f32[24,128]{1,0:T(8,128)S(1)}, u32[]{:S(2)}, u32[]{:S(2)}) %collective-permute-start.10) | collective-permute-done | bytes 12320 | tf_op jit(solution)/shard_map/ppermute | solution.py:337
  20.8 1.1 %collective-permute-done.9.refs_2_ = f32[24,128]{1,0:T(8,128)S(1)} collective-permute-done((f32[24,128]{1,0:T(8,128)S(1)}, f32[24,128]{1,0:T(8,128)S(1)}, u32[]{:S(2)}, u32[]{:S(2)}) %collective-permute-start.9) | collective-permute-done | bytes 12320 | tf_op jit(solution)/shard_map/ppermute | solution.py:337
  21.9 0.0 collective-permute-done.8.refs_1_
  21.9 0.3 shard_map.90.t2.refs_0_
  22.2 0.0 collective-permute-start.15
  22.2 1.8 %collective-permute-start.14 = (f32[24,128]{1,0:T(8,128)S(1)}, f32[24,128]{1,0:T(8,128)S(1)}, u32[]{:S(2)}, u32[]{:S(2)}) collective-permute-start(f32[24,128]{1,0:T(8,128)S(1)} %shard_map.90.t2.refs_0_), channel_id=1, source_target_pairs={{0,8},{1,9},{2,10},{3,11},{4,12},{5,13},{6,14},{7,15},{8,0},{9,1},... | collective-permute-start | bytes 36872 | tf_op jit(solution)/shard_map/ppermute | solution.py:337
  24.0 0.0 collective-permute-start.13
  24.0 0.4 collective-permute-start.12
  24.4 0.0 copy-done
  24.4 0.6 %shard_map.91 = (f32[24,512]{1,0:T(8,128)S(1)}, f32[24,128]{1,0:T(8,128)S(1)}, bf16[512,128]{1,0:T(8,128)(2,1)S(1)}, bf16[512,128]{1,0:T(8,128)(2,1)S(1)}, bf16[512,128]{1,0:T(8,128)(2,1)S(1)}) custom-call(f32[3,32,512]{2,1,0:T(8,128)S(1)} %copy-done, f32[24,128]{1,0:T(8,128)S(1)} %get-tuple-element.19.refs_0_.t0, f32[24,128]{1,0:T(8,128)S(1)} %shard_map.89.refs_0_.t1, ...), custom_call_target="tpu_custom_call" | custom-call | flops 60000000 | bytes 250000 | tf_op jit(solution)/shard_map/pallas_call | solution.py:431
  25.0 0.0 collective-permute-done.15.refs_4_
  25.0 0.9 %collective-permute-done.14.refs_3_ = f32[24,128]{1,0:T(8,128)S(1)} collective-permute-done((f32[24,128]{1,0:T(8,128)S(1)}, f32[24,128]{1,0:T(8,128)S(1)}, u32[]{:S(2)}, u32[]{:S(2)}) %collective-permute-start.14) | collective-permute-done | bytes 12320 | tf_op jit(solution)/shard_map/ppermute | solution.py:337
  25.9 1.2 %collective-permute-done.13.refs_2_ = f32[24,128]{1,0:T(8,128)S(1)} collective-permute-done((f32[24,128]{1,0:T(8,128)S(1)}, f32[24,128]{1,0:T(8,128)S(1)}, u32[]{:S(2)}, u32[]{:S(2)}) %collective-permute-start.13) | collective-permute-done | bytes 12320 | tf_op jit(solution)/shard_map/ppermute | solution.py:337
  27.1 0.0 collective-permute-done.12.refs_1_
  27.1 0.5 %shard_map.92 = (f32[8,512]{1,0:T(8,128)S(1)}, f32[24,128]{1,0:T(8,128)S(1)}) custom-call(f32[24,128]{1,0:T(8,128)S(1)} %shard_map.90.t2.refs_0_, f32[24,128]{1,0:T(8,128)S(1)} %collective-permute-done.12.refs_1_, f32[24,128]{1,0:T(8,128)S(1)} %collective-permute-done.13.refs_2_, f32[24,128]{1,0:T(8,128)S(1)} %collective-permute-done.14.refs_3_, ...), custom_call_target="tpu_custom_call" | custom-call | flops 80000000 | bytes 900000 | tf_op jit(solution)/shard_map/pallas_call | solution.py:438
  27.6 0.1 collective-permute-start.16
  27.7 1.2 %collective-permute-done.16 = f32[24,128]{1,0:T(8,128)S(1)} collective-permute-done((f32[24,128]{1,0:T(8,128)S(1)}, f32[24,128]{1,0:T(8,128)S(1)}, u32[]{:S(2)}, u32[]{:S(2)}) %collective-permute-start.16) | collective-permute-done | bytes 12320 | tf_op jit(solution)/shard_map/ppermute | solution.py:337
  28.9 1.0 %collective-permute-start.19 = (f32[24,128]{1,0:T(8,128)S(1)}, f32[24,128]{1,0:T(8,128)S(1)}, u32[]{:S(2)}, u32[]{:S(2)}) collective-permute-start(f32[24,128]{1,0:T(8,128)S(1)} %add.21), channel_id=1, source_target_pairs={{0,7},{1,6},{2,5},{3,4},{4,3},{5,2},{6,1},{7,0},{8,15},{9,14},{10,... | collective-permute-start | bytes 36872 | tf_op jit(solution)/shard_map/ppermute | solution.py:337
  29.9 0.4 %collective-permute-start.18 = (f32[24,128]{1,0:T(8,128)S(1)}, f32[24,128]{1,0:T(8,128)S(1)}, u32[]{:S(2)}, u32[]{:S(2)}) collective-permute-start(f32[24,128]{1,0:T(8,128)S(1)} %add.21), channel_id=1, source_target_pairs={{0,5},{1,4},{2,7},{3,6},{4,1},{5,0},{6,3},{7,2},{8,13},{9,12},{10,... | collective-permute-start | bytes 36872 | tf_op jit(solution)/shard_map/ppermute | solution.py:337
  30.3 1.5 %collective-permute-start.17 = (f32[24,128]{1,0:T(8,128)S(1)}, f32[24,128]{1,0:T(8,128)S(1)}, u32[]{:S(2)}, u32[]{:S(2)}) collective-permute-start(f32[24,128]{1,0:T(8,128)S(1)} %add.21), channel_id=1, source_target_pairs={{0,3},{1,2},{2,1},{3,0},{4,7},{5,6},{6,5},{7,4},{8,11},{9,10},{10,... | collective-permute-start | bytes 36872 | tf_op jit(solution)/shard_map/ppermute | solution.py:337
  31.8 1.0 %collective-permute-done.19 = f32[24,128]{1,0:T(8,128)S(1)} collective-permute-done((f32[24,128]{1,0:T(8,128)S(1)}, f32[24,128]{1,0:T(8,128)S(1)}, u32[]{:S(2)}, u32[]{:S(2)}) %collective-permute-start.19) | collective-permute-done | bytes 12320 | tf_op jit(solution)/shard_map/ppermute | solution.py:337
  32.9 0.1 collective-permute-done.18
  33.0 0.4 %collective-permute-done.17 = f32[24,128]{1,0:T(8,128)S(1)} collective-permute-done((f32[24,128]{1,0:T(8,128)S(1)}, f32[24,128]{1,0:T(8,128)S(1)}, u32[]{:S(2)}, u32[]{:S(2)}) %collective-permute-start.17) | collective-permute-done | bytes 12320 | tf_op jit(solution)/shard_map/ppermute | solution.py:337
  33.5 2.1 %collective-permute-start.22 = (f32[24,128]{1,0:T(8,128)S(1)}, f32[24,128]{1,0:T(8,128)S(1)}, u32[]{:S(2)}, u32[]{:S(2)}) collective-permute-start(f32[24,128]{1,0:T(8,128)S(1)} %add_add_fusion.1), channel_id=1, source_target_pairs={{0,25},{1,24},{2,27},{3,26},{4,29},{5,28},{6,31},{7,30},{8,17},{9,... | collective-permute-start | bytes 36872 | tf_op jit(solution)/shard_map/ppermute | solution.py:337
  35.5 0.2 collective-permute-start.21
  35.8 1.6 %collective-permute-start.20 = (f32[24,128]{1,0:T(8,128)S(1)}, f32[24,128]{1,0:T(8,128)S(1)}, u32[]{:S(2)}, u32[]{:S(2)}) collective-permute-start(f32[24,128]{1,0:T(8,128)S(1)} %add_add_fusion.1), channel_id=1, source_target_pairs={{0,9},{1,8},{2,11},{3,10},{4,13},{5,12},{6,15},{7,14},{8,1},{9,0},... | collective-permute-start | bytes 36872 | tf_op jit(solution)/shard_map/ppermute | solution.py:337
  37.4 1.0 %collective-permute-done.22 = f32[24,128]{1,0:T(8,128)S(1)} collective-permute-done((f32[24,128]{1,0:T(8,128)S(1)}, f32[24,128]{1,0:T(8,128)S(1)}, u32[]{:S(2)}, u32[]{:S(2)}) %collective-permute-start.22) | collective-permute-done | bytes 12320 | tf_op jit(solution)/shard_map/ppermute | solution.py:337
  38.4 1.3 %collective-permute-done.21 = f32[24,128]{1,0:T(8,128)S(1)} collective-permute-done((f32[24,128]{1,0:T(8,128)S(1)}, f32[24,128]{1,0:T(8,128)S(1)}, u32[]{:S(2)}, u32[]{:S(2)}) %collective-permute-start.21) | collective-permute-done | bytes 12320 | tf_op jit(solution)/shard_map/ppermute | solution.py:337
  39.7 0.0 collective-permute-done.20
  39.7 1.0 %shard_map.93 = (f32[3,4,512]{2,1,0:T(4,128)}, f32[3,4,36]{2,1,0:T(4,128)}) custom-call(f32[24,128]{1,0:T(8,128)S(1)} %add_add_fusion.refs_0_, f32[3,32,512]{2,1,0:T(8,128)S(1)} %copy-done, f32[24,512]{1,0:T(8,128)S(1)} %get-tuple-element.26.refs_2_, f32[8,512]{1,0:T(8,128)S(1)} %get-tuple-element.27.refs_3_), custom_call_target="tpu_custom_call" | custom-call | flops 50000000 | bytes 400000 | tf_op jit(solution)/shard_map/pallas_call | solution.py:446
  (3 shorter events, 0.0 us)
Async XLA Ops:
  1.7 6.3 %collective-permute-start.3 = (f32[32,128]{1,0:T(8,128)S(1)}, f32[32,128]{1,0:T(8,128)S(1)}, u32[]{:S(2)}, u32[]{:S(2)}) collective-permute-start(f32[32,128]{1,0:T(8,128)S(1)} %shard_map.86.refs_0_), channel_id=1, source_target_pairs={{0,2},{1,0},{2,1},{3,4},{4,3},{5,6},{6,5},{7,8},{8,7},{9,10},{10,9... | collective-permute-start | bytes 49160 | tf_op jit(solution)/shard_map/ppermute | solution.py:337
  4.7 3.7 %collective-permute-start.2 = (f32[32,128]{1,0:T(8,128)S(1)}, f32[32,128]{1,0:T(8,128)S(1)}, u32[]{:S(2)}, u32[]{:S(2)}) collective-permute-start(f32[32,128]{1,0:T(8,128)S(1)} %shard_map.86.refs_0_), channel_id=1, source_target_pairs={{0,8},{1,9},{2,10},{3,11},{4,12},{5,13},{6,14},{7,15},{8,0},{9,1},... | collective-permute-start | bytes 49160 | tf_op jit(solution)/shard_map/ppermute | solution.py:337
  6.6 3.2 %collective-permute-start.1 = (f32[32,128]{1,0:T(8,128)S(1)}, f32[32,128]{1,0:T(8,128)S(1)}, u32[]{:S(2)}, u32[]{:S(2)}) collective-permute-start(f32[32,128]{1,0:T(8,128)S(1)} %shard_map.86.refs_0_), channel_id=1, source_target_pairs={{0,1},{1,2},{2,3},{3,0},{4,5},{5,4},{6,7},{7,6},{8,16},{9,17},{10,... | collective-permute-start | bytes 49160 | tf_op jit(solution)/shard_map/ppermute | solution.py:337
  6.6 3.2 %collective-permute-start = (f32[32,128]{1,0:T(8,128)S(1)}, f32[32,128]{1,0:T(8,128)S(1)}, u32[]{:S(2)}, u32[]{:S(2)}) collective-permute-start(f32[32,128]{1,0:T(8,128)S(1)} %shard_map.86.refs_0_), channel_id=1, source_target_pairs={{0,1},{1,0},{2,3},{3,2},{4,5},{5,4},{6,7},{7,6},{8,9},{9,8},{10,11... | collective-permute-start | bytes 49160 | tf_op jit(solution)/shard_map/ppermute | solution.py:337
  10.1 3.7 %collective-permute-start.7 = (f32[24,128]{1,0:T(8,128)S(1)}, f32[24,128]{1,0:T(8,128)S(1)}, u32[]{:S(2)}, u32[]{:S(2)}) collective-permute-start(f32[24,128]{1,0:T(8,128)S(1)} %get-tuple-element.19.refs_0_.t0), channel_id=1, source_target_pairs={{0,2},{1,0},{2,1},{3,4},{4,3},{5,6},{6,5},{7,8},{8,7},{9,10},{10,9... | collective-permute-start | bytes 36872 | tf_op jit(solution)/shard_map/ppermute | solution.py:337
  10.6 3.7 %collective-permute-start.6 = (f32[24,128]{1,0:T(8,128)S(1)}, f32[24,128]{1,0:T(8,128)S(1)}, u32[]{:S(2)}, u32[]{:S(2)}) collective-permute-start(f32[24,128]{1,0:T(8,128)S(1)} %get-tuple-element.19.refs_0_.t0), channel_id=1, source_target_pairs={{0,8},{1,9},{2,10},{3,11},{4,12},{5,13},{6,14},{7,15},{8,0},{9,1},... | collective-permute-start | bytes 36872 | tf_op jit(solution)/shard_map/ppermute | solution.py:337
  12.0 3.1 %collective-permute-start.5 = (f32[24,128]{1,0:T(8,128)S(1)}, f32[24,128]{1,0:T(8,128)S(1)}, u32[]{:S(2)}, u32[]{:S(2)}) collective-permute-start(f32[24,128]{1,0:T(8,128)S(1)} %get-tuple-element.19.refs_0_.t0), channel_id=1, source_target_pairs={{0,1},{1,2},{2,3},{3,0},{4,5},{5,4},{6,7},{7,6},{8,16},{9,17},{10,... | collective-permute-start | bytes 36872 | tf_op jit(solution)/shard_map/ppermute | solution.py:337
  12.2 2.9 %collective-permute-start.4 = (f32[24,128]{1,0:T(8,128)S(1)}, f32[24,128]{1,0:T(8,128)S(1)}, u32[]{:S(2)}, u32[]{:S(2)}) collective-permute-start(f32[24,128]{1,0:T(8,128)S(1)} %get-tuple-element.19.refs_0_.t0), channel_id=1, source_target_pairs={{0,1},{1,0},{2,3},{3,2},{4,5},{5,4},{6,7},{7,6},{8,9},{9,8},{10,11... | collective-permute-start | bytes 36872 | tf_op jit(solution)/shard_map/ppermute | solution.py:337
  15.4 9.0 %copy-start = (f32[3,32,512]{2,1,0:T(8,128)S(1)}, f32[3,32,512]{2,1,0:T(8,128)}, u32[]{:S(2)}) copy-start(f32[3,32,512]{2,1,0:T(8,128)} %refs_1_.1) | copy-start | bytes 589828
  15.4 3.4 %collective-permute-start.11 = (f32[24,128]{1,0:T(8,128)S(1)}, f32[24,128]{1,0:T(8,128)S(1)}, u32[]{:S(2)}, u32[]{:S(2)}) collective-permute-start(f32[24,128]{1,0:T(8,128)S(1)} %shard_map.89.refs_0_.t1), channel_id=1, source_target_pairs={{0,2},{1,0},{2,1},{3,4},{4,3},{5,6},{6,5},{7,8},{8,7},{9,10},{10,9... | collective-permute-start | bytes 36872 | tf_op jit(solution)/shard_map/ppermute | solution.py:337
  17.1 3.7 %collective-permute-start.10 = (f32[24,128]{1,0:T(8,128)S(1)}, f32[24,128]{1,0:T(8,128)S(1)}, u32[]{:S(2)}, u32[]{:S(2)}) collective-permute-start(f32[24,128]{1,0:T(8,128)S(1)} %shard_map.89.refs_0_.t1), channel_id=1, source_target_pairs={{0,8},{1,9},{2,10},{3,11},{4,12},{5,13},{6,14},{7,15},{8,0},{9,1},... | collective-permute-start | bytes 36872 | tf_op jit(solution)/shard_map/ppermute | solution.py:337
  18.8 3.1 %collective-permute-start.9 = (f32[24,128]{1,0:T(8,128)S(1)}, f32[24,128]{1,0:T(8,128)S(1)}, u32[]{:S(2)}, u32[]{:S(2)}) collective-permute-start(f32[24,128]{1,0:T(8,128)S(1)} %shard_map.89.refs_0_.t1), channel_id=1, source_target_pairs={{0,1},{1,2},{2,3},{3,0},{4,5},{5,4},{6,7},{7,6},{8,16},{9,17},{10,... | collective-permute-start | bytes 36872 | tf_op jit(solution)/shard_map/ppermute | solution.py:337
  18.8 3.1 %collective-permute-start.8 = (f32[24,128]{1,0:T(8,128)S(1)}, f32[24,128]{1,0:T(8,128)S(1)}, u32[]{:S(2)}, u32[]{:S(2)}) collective-permute-start(f32[24,128]{1,0:T(8,128)S(1)} %shard_map.89.refs_0_.t1), channel_id=1, source_target_pairs={{0,1},{1,0},{2,3},{3,2},{4,5},{5,4},{6,7},{7,6},{8,9},{9,8},{10,11... | collective-permute-start | bytes 36872 | tf_op jit(solution)/shard_map/ppermute | solution.py:337
  22.2 2.8 %collective-permute-start.15 = (f32[24,128]{1,0:T(8,128)S(1)}, f32[24,128]{1,0:T(8,128)S(1)}, u32[]{:S(2)}, u32[]{:S(2)}) collective-permute-start(f32[24,128]{1,0:T(8,128)S(1)} %shard_map.90.t2.refs_0_), channel_id=1, source_target_pairs={{0,2},{1,0},{2,1},{3,4},{4,3},{5,6},{6,5},{7,8},{8,7},{9,10},{10,9... | collective-permute-start | bytes 36872 | tf_op jit(solution)/shard_map/ppermute | solution.py:337
  22.2 3.8 %collective-permute-start.14 = (f32[24,128]{1,0:T(8,128)S(1)}, f32[24,128]{1,0:T(8,128)S(1)}, u32[]{:S(2)}, u32[]{:S(2)}) collective-permute-start(f32[24,128]{1,0:T(8,128)S(1)} %shard_map.90.t2.refs_0_), channel_id=1, source_target_pairs={{0,8},{1,9},{2,10},{3,11},{4,12},{5,13},{6,14},{7,15},{8,0},{9,1},... | collective-permute-start | bytes 36872 | tf_op jit(solution)/shard_map/ppermute | solution.py:337
  24.0 3.1 %collective-permute-start.13 = (f32[24,128]{1,0:T(8,128)S(1)}, f32[24,128]{1,0:T(8,128)S(1)}, u32[]{:S(2)}, u32[]{:S(2)}) collective-permute-start(f32[24,128]{1,0:T(8,128)S(1)} %shard_map.90.t2.refs_0_), channel_id=1, source_target_pairs={{0,1},{1,2},{2,3},{3,0},{4,5},{5,4},{6,7},{7,6},{8,16},{9,17},{10,... | collective-permute-start | bytes 36872 | tf_op jit(solution)/shard_map/ppermute | solution.py:337
  24.0 3.1 %collective-permute-start.12 = (f32[24,128]{1,0:T(8,128)S(1)}, f32[24,128]{1,0:T(8,128)S(1)}, u32[]{:S(2)}, u32[]{:S(2)}) collective-permute-start(f32[24,128]{1,0:T(8,128)S(1)} %shard_map.90.t2.refs_0_), channel_id=1, source_target_pairs={{0,1},{1,0},{2,3},{3,2},{4,5},{5,4},{6,7},{7,6},{8,9},{9,8},{10,11... | collective-permute-start | bytes 36872 | tf_op jit(solution)/shard_map/ppermute | solution.py:337
  27.6 1.2 %collective-permute-start.16 = (f32[24,128]{1,0:T(8,128)S(1)}, f32[24,128]{1,0:T(8,128)S(1)}, u32[]{:S(2)}, u32[]{:S(2)}) collective-permute-start(f32[24,128]{1,0:T(8,128)S(1)} %get-tuple-element.25), channel_id=1, source_target_pairs={{0,1},{1,0},{2,3},{3,2},{4,5},{5,4},{6,7},{7,6},{8,9},{9,8},{10,11... | collective-permute-start | bytes 36872 | tf_op jit(solution)/shard_map/ppermute | solution.py:337
  28.9 4.0 %collective-permute-start.19 = (f32[24,128]{1,0:T(8,128)S(1)}, f32[24,128]{1,0:T(8,128)S(1)}, u32[]{:S(2)}, u32[]{:S(2)}) collective-permute-start(f32[24,128]{1,0:T(8,128)S(1)} %add.21), channel_id=1, source_target_pairs={{0,7},{1,6},{2,5},{3,4},{4,3},{5,2},{6,1},{7,0},{8,15},{9,14},{10,... | collective-permute-start | bytes 36872 | tf_op jit(solution)/shard_map/ppermute | solution.py:337
  29.9 3.1 %collective-permute-start.18 = (f32[24,128]{1,0:T(8,128)S(1)}, f32[24,128]{1,0:T(8,128)S(1)}, u32[]{:S(2)}, u32[]{:S(2)}) collective-permute-start(f32[24,128]{1,0:T(8,128)S(1)} %add.21), channel_id=1, source_target_pairs={{0,5},{1,4},{2,7},{3,6},{4,1},{5,0},{6,3},{7,2},{8,13},{9,12},{10,... | collective-permute-start | bytes 36872 | tf_op jit(solution)/shard_map/ppermute | solution.py:337
  30.3 3.1 %collective-permute-start.17 = (f32[24,128]{1,0:T(8,128)S(1)}, f32[24,128]{1,0:T(8,128)S(1)}, u32[]{:S(2)}, u32[]{:S(2)}) collective-permute-start(f32[24,128]{1,0:T(8,128)S(1)} %add.21), channel_id=1, source_target_pairs={{0,3},{1,2},{2,1},{3,0},{4,7},{5,6},{6,5},{7,4},{8,11},{9,10},{10,... | collective-permute-start | bytes 36872 | tf_op jit(solution)/shard_map/ppermute | solution.py:337
  33.5 4.9 %collective-permute-start.22 = (f32[24,128]{1,0:T(8,128)S(1)}, f32[24,128]{1,0:T(8,128)S(1)}, u32[]{:S(2)}, u32[]{:S(2)}) collective-permute-start(f32[24,128]{1,0:T(8,128)S(1)} %add_add_fusion.1), channel_id=1, source_target_pairs={{0,25},{1,24},{2,27},{3,26},{4,29},{5,28},{6,31},{7,30},{8,17},{9,... | collective-permute-start | bytes 36872 | tf_op jit(solution)/shard_map/ppermute | solution.py:337
  35.5 4.1 %collective-permute-start.21 = (f32[24,128]{1,0:T(8,128)S(1)}, f32[24,128]{1,0:T(8,128)S(1)}, u32[]{:S(2)}, u32[]{:S(2)}) collective-permute-start(f32[24,128]{1,0:T(8,128)S(1)} %add_add_fusion.1), channel_id=1, source_target_pairs={{0,17},{1,16},{2,19},{3,18},{4,21},{5,20},{6,23},{7,22},{8,25},{9,... | collective-permute-start | bytes 36872 | tf_op jit(solution)/shard_map/ppermute | solution.py:337
  35.8 3.9 %collective-permute-start.20 = (f32[24,128]{1,0:T(8,128)S(1)}, f32[24,128]{1,0:T(8,128)S(1)}, u32[]{:S(2)}, u32[]{:S(2)}) collective-permute-start(f32[24,128]{1,0:T(8,128)S(1)} %add_add_fusion.1), channel_id=1, source_target_pairs={{0,9},{1,8},{2,11},{3,10},{4,13},{5,12},{6,15},{7,14},{8,1},{9,0},... | collective-permute-start | bytes 36872 | tf_op jit(solution)/shard_map/ppermute | solution.py:337

commit v13 on v12

--- a/solution.py
+++ b/solution.py
@@ -249,7 +249,7 @@
     )
 
 
-def finish_kernel(total, gram_in, prev_ref, lines, last, basis_ref, factors_ref):
+def finish_kernel(total, gram_in, prev_ref, lines, last, basis_out, factors_out, basis_ref, factors_ref, sems):
     comps, vecs, rows = prev_ref.shape
     width = comps * vecs
     gram = gram_in[...] * (1.0 / total)
@@ -293,15 +293,6 @@
                 unit[k, l] = value / scale[l]
     roots = [jnp.sqrt(scale[k]) for k in range(S)]
     lower = {(k, l): unit[k, l] * roots[l] if l < k else roots[k] for k in range(S) for l in range(k + 1)}
-    vectors = []
-    for k in range(S):
-        value = projected[k * 8 : (k + 1) * 8]
-        for l in range(k):
-            value = value - unit[k, l] * vectors[l]
-        vectors.append(value)
-        value = value / roots[k]
-        for c in range(comps):
-            basis_ref[c, k : k + 1, :] = value[c : c + 1]
     for c in range(comps):
         factors_ref[c, :, :vecs] = small[:S, c * vecs : (c + 1) * vecs]
     for k in range(S):
@@ -310,6 +301,21 @@
             line = jnp.where(lane == l, lower[k, l], line)
         for c in range(comps):
             factors_ref[c, k : k + 1, vecs:] = line[c : c + 1, :S]
+    factors_copy = pltpu.make_async_copy(factors_ref, factors_out, sems.at[0])
+    factors_copy.start()
+    vectors = []
+    for k in range(S):
+        value = projected[k * 8 : (k + 1) * 8]
+        for l in range(k):
+            value = value - unit[k, l] * vectors[l]
+        vectors.append(value)
+        value = value * (1.0 / roots[k])
+        for c in range(comps):
+            basis_ref[c, k : k + 1, :] = value[c : c + 1]
+    basis_copy = pltpu.make_async_copy(basis_ref, basis_out, sems.at[1])
+    basis_copy.start()
+    factors_copy.wait()
+    basis_copy.wait()
 
 
 VMEM = pl.BlockSpec(memory_space=pltpu.VMEM)
@@ -320,13 +326,13 @@
     return [pltpu.with_memory_space_constraint(x, pltpu.HBM) for x in arrays]
 
 
-def call(kernel, outs, specs, flops, moved, scratch=()):
+def call(kernel, outs, specs, flops, moved, scratch=(), home=None):
     shapes = [jax.ShapeDtypeStruct(shape, kind) for shape, kind in outs]
     return pl.pallas_call(
         kernel,
         out_shape=shapes if len(shapes) > 1 else shapes[0],
         in_specs=specs,
-        out_specs=[VMEM] * len(shapes) if len(shapes) > 1 else VMEM,
+        out_specs=[home or VMEM] * len(shapes) if len(shapes) > 1 else VMEM,
         scratch_shapes=list(scratch),
         compiler_params=pltpu.CompilerParams(vmem_limit_bytes=24 * 1024 * 1024),
         cost_estimate=pl.CostEstimate(flops=flops, bytes_accessed=moved, transcendentals=0),
@@ -449,6 +455,12 @@
         [VMEM] * 4,
         50000000,
         400000,
+        [
+            pltpu.VMEM((comps, S, rows), f32),
+            pltpu.VMEM((comps, S, vecs + S), f32),
+            dma((2,)),
+        ],
+        HBM,
     )(summed(gram), prev_basis, lines, last)
     return basis, jnp.swapaxes(factors, 1, 2)
 

time: 40.9 us -> 40.9 us (level)
  no operation moved by 1% of the time
where the time goes in v13:
time: 40.9 us; the launch traced here: 40.7 us
  starting transfers between devices  21.1 us (52%)
  waiting for transfers between devices  13.4 us (33%)
  Pallas kernels  5.51 us (13%)
  between operations  0.72 us (2%)
    ppermute x23, starting transfers between devices, send(): lax.ppermute(value, 'dom', [(d, target[d]) for d in range(lax.axis_size('...  21.1 us
    ppermute x23, waiting for transfers between devices, send(): lax.ppermute(value, 'dom', [(d, target[d]) for d in range(lax.axis_size('...  13.4 us
    pallas_call x1, Pallas kernels, local(): call(prepare_kernel, [((width, rows), bf16), ((width, rows), bf16), ((8 *...  1.39 us
    pallas_call x1, Pallas kernels, local(): call(start_kernel, [((comps * blocks + 8, 128), f32)], [HBM] * 4, 600000,...  1.08 us
    pallas_call x1, Pallas kernels, local(): call(lambda *refs: finish_kernel(total, *refs), [((comps, S, rows), f32),...  1.05 us
  transfers between devices with their start and end apart: 23, of which 14 were waited for; matrix products, arithmetic and copies ran while one was open for 0% of the time, Pallas kernels for 5%

profile of v13, /device:TPU:0, one launch (start us, length us, event | category | flops | bytes accessed | tf_op | source)
XLA Modules:
  0.0 40.7 jit_solution(12160666037606295096)
XLA Ops:
  0.6 1.1 %shard_map.86.refs_0_ = f32[32,128]{1,0:T(8,128)S(1)} custom-call(f32[3,32,512]{2,1,0:T(8,128)} %refs_1_.1, f32[3,32]{1,0:T(4,128)} %mix_in.1, s32[1,4,8]{2,1,0:T(4,128)} %list_in.1, s32[1,4]{1,0:T(1,128)} %count_in.1), custom_call_target="tpu_custom_call" | custom-call | flops 600000 | bytes 250000 | tf_op jit(solution)/shard_map/pallas_call | solution.py:393
  1.7 3.0 %collective-permute-start.3 = (f32[32,128]{1,0:T(8,128)S(1)}, f32[32,128]{1,0:T(8,128)S(1)}, u32[]{:S(2)}, u32[]{:S(2)}) collective-permute-start(f32[32,128]{1,0:T(8,128)S(1)} %shard_map.86.refs_0_), channel_id=1, source_target_pairs={{0,2},{1,0},{2,1},{3,4},{4,3},{5,6},{6,5},{7,8},{8,7},{9,10},{10,9... | collective-permute-start | bytes 49160 | tf_op jit(solution)/shard_map/ppermute | solution.py:343
  4.7 1.9 %collective-permute-start.2 = (f32[32,128]{1,0:T(8,128)S(1)}, f32[32,128]{1,0:T(8,128)S(1)}, u32[]{:S(2)}, u32[]{:S(2)}) collective-permute-start(f32[32,128]{1,0:T(8,128)S(1)} %shard_map.86.refs_0_), channel_id=1, source_target_pairs={{0,8},{1,9},{2,10},{3,11},{4,12},{5,13},{6,14},{7,15},{8,0},{9,1},... | collective-permute-start | bytes 49160 | tf_op jit(solution)/shard_map/ppermute | solution.py:343
  6.6 0.0 collective-permute-start.1
  6.6 0.0 collective-permute-start
  6.6 1.4 %shard_map.87 = (bf16[256,512]{1,0:T(8,128)(2,1)S(1)}, bf16[256,512]{1,0:T(8,128)(2,1)S(1)}, f32[40,128]{1,0:T(8,128)S(1)}) custom-call(f32[512,256]{1,0:T(8,128)} %strips_in.1, s32[4,8]{1,0:T(4,128)} %bitcast.2, f32[4]{0:T(128)} %shifts_in.1), custom_call_target="tpu_custom_call" | custom-call | flops 1000000 | bytes 1000000 | tf_op jit(solution)/shard_map/pallas_call | solution.py:407
  8.0 0.0 collective-permute-done.3.refs_4_
  8.0 0.5 %collective-permute-done.2.refs_3_ = f32[32,128]{1,0:T(8,128)S(1)} collective-permute-done((f32[32,128]{1,0:T(8,128)S(1)}, f32[32,128]{1,0:T(8,128)S(1)}, u32[]{:S(2)}, u32[]{:S(2)}) %collective-permute-start.2) | collective-permute-done | bytes 16416 | tf_op jit(solution)/shard_map/ppermute | solution.py:343
  8.5 1.3 %collective-permute-done.1.refs_2_ = f32[32,128]{1,0:T(8,128)S(1)} collective-permute-done((f32[32,128]{1,0:T(8,128)S(1)}, f32[32,128]{1,0:T(8,128)S(1)}, u32[]{:S(2)}, u32[]{:S(2)}) %collective-permute-start.1) | collective-permute-done | bytes 16416 | tf_op jit(solution)/shard_map/ppermute | solution.py:343
  9.7 0.0 collective-permute-done.refs_1_
  9.7 0.4 shard_map.88
  10.1 0.4 %collective-permute-start.7 = (f32[24,128]{1,0:T(8,128)S(1)}, f32[24,128]{1,0:T(8,128)S(1)}, u32[]{:S(2)}, u32[]{:S(2)}) collective-permute-start(f32[24,128]{1,0:T(8,128)S(1)} %get-tuple-element.19.refs_0_.t0), channel_id=1, source_target_pairs={{0,2},{1,0},{2,1},{3,4},{4,3},{5,6},{6,5},{7,8},{8,7},{9,10},{10,9... | collective-permute-start | bytes 36872 | tf_op jit(solution)/shard_map/ppermute | solution.py:343
  10.6 1.4 %collective-permute-start.6 = (f32[24,128]{1,0:T(8,128)S(1)}, f32[24,128]{1,0:T(8,128)S(1)}, u32[]{:S(2)}, u32[]{:S(2)}) collective-permute-start(f32[24,128]{1,0:T(8,128)S(1)} %get-tuple-element.19.refs_0_.t0), channel_id=1, source_target_pairs={{0,8},{1,9},{2,10},{3,11},{4,12},{5,13},{6,14},{7,15},{8,0},{9,1},... | collective-permute-start | bytes 36872 | tf_op jit(solution)/shard_map/ppermute | solution.py:343
  12.0 0.2 collective-permute-start.5
  12.2 1.7 %collective-permute-start.4 = (f32[24,128]{1,0:T(8,128)S(1)}, f32[24,128]{1,0:T(8,128)S(1)}, u32[]{:S(2)}, u32[]{:S(2)}) collective-permute-start(f32[24,128]{1,0:T(8,128)S(1)} %get-tuple-element.19.refs_0_.t0), channel_id=1, source_target_pairs={{0,1},{1,0},{2,3},{3,2},{4,5},{5,4},{6,7},{7,6},{8,9},{9,8},{10,11... | collective-permute-start | bytes 36872 | tf_op jit(solution)/shard_map/ppermute | solution.py:343
  13.8 0.0 collective-permute-done.7.refs_4_
  13.8 0.4 %collective-permute-done.6.refs_3_ = f32[24,128]{1,0:T(8,128)S(1)} collective-permute-done((f32[24,128]{1,0:T(8,128)S(1)}, f32[24,128]{1,0:T(8,128)S(1)}, u32[]{:S(2)}, u32[]{:S(2)}) %collective-permute-start.6) | collective-permute-done | bytes 12320 | tf_op jit(solution)/shard_map/ppermute | solution.py:343
  14.3 0.9 %collective-permute-done.5.refs_2_ = f32[24,128]{1,0:T(8,128)S(1)} collective-permute-done((f32[24,128]{1,0:T(8,128)S(1)}, f32[24,128]{1,0:T(8,128)S(1)}, u32[]{:S(2)}, u32[]{:S(2)}) %collective-permute-start.5) | collective-permute-done | bytes 12320 | tf_op jit(solution)/shard_map/ppermute | solution.py:343
  15.1 0.0 collective-permute-done.4.refs_1_
  15.1 0.3 shard_map.89.refs_0_.t1
  15.4 0.0 copy-start
  15.4 1.7 %collective-permute-start.11 = (f32[24,128]{1,0:T(8,128)S(1)}, f32[24,128]{1,0:T(8,128)S(1)}, u32[]{:S(2)}, u32[]{:S(2)}) collective-permute-start(f32[24,128]{1,0:T(8,128)S(1)} %shard_map.89.refs_0_.t1), channel_id=1, source_target_pairs={{0,2},{1,0},{2,1},{3,4},{4,3},{5,6},{6,5},{7,8},{8,7},{9,10},{10,9... | collective-permute-start | bytes 36872 | tf_op jit(solution)/shard_map/ppermute | solution.py:343
  17.1 1.6 %collective-permute-start.10 = (f32[24,128]{1,0:T(8,128)S(1)}, f32[24,128]{1,0:T(8,128)S(1)}, u32[]{:S(2)}, u32[]{:S(2)}) collective-permute-start(f32[24,128]{1,0:T(8,128)S(1)} %shard_map.89.refs_0_.t1), channel_id=1, source_target_pairs={{0,8},{1,9},{2,10},{3,11},{4,12},{5,13},{6,14},{7,15},{8,0},{9,1},... | collective-permute-start | bytes 36872 | tf_op jit(solution)/shard_map/ppermute | solution.py:343
  18.8 0.0 collective-permute-start.9
  18.8 0.0 collective-permute-start.8
  18.8 0.0 collective-permute-done.11.refs_4_
  18.8 2.0 %collective-permute-done.10.refs_3_ = f32[24,128]{1,0:T(8,128)S(1)} collective-permute-done((f32[24,128]{1,0:T(8,128)S(1)}, f32[24,128]{1,0:T(8,128)S(1)}, u32[]{:S(2)}, u32[]{:S(2)}) %collective-permute-start.10) | collective-permute-done | bytes 12320 | tf_op jit(solution)/shard_map/ppermute | solution.py:343
  20.8 1.1 %collective-permute-done.9.refs_2_ = f32[24,128]{1,0:T(8,128)S(1)} collective-permute-done((f32[24,128]{1,0:T(8,128)S(1)}, f32[24,128]{1,0:T(8,128)S(1)}, u32[]{:S(2)}, u32[]{:S(2)}) %collective-permute-start.9) | collective-permute-done | bytes 12320 | tf_op jit(solution)/shard_map/ppermute | solution.py:343
  21.9 0.0 collective-permute-done.8.refs_1_
  21.9 0.3 shard_map.90.t2.refs_0_
  22.2 0.0 collective-permute-start.15
  22.2 1.8 %collective-permute-start.14 = (f32[24,128]{1,0:T(8,128)S(1)}, f32[24,128]{1,0:T(8,128)S(1)}, u32[]{:S(2)}, u32[]{:S(2)}) collective-permute-start(f32[24,128]{1,0:T(8,128)S(1)} %shard_map.90.t2.refs_0_), channel_id=1, source_target_pairs={{0,8},{1,9},{2,10},{3,11},{4,12},{5,13},{6,14},{7,15},{8,0},{9,1},... | collective-permute-start | bytes 36872 | tf_op jit(solution)/shard_map/ppermute | solution.py:343
  24.0 0.0 collective-permute-start.13
  24.0 0.4 collective-permute-start.12
  24.4 0.0 copy-done
  24.4 0.6 %shard_map.91 = (f32[24,512]{1,0:T(8,128)S(1)}, f32[24,128]{1,0:T(8,128)S(1)}, bf16[512,128]{1,0:T(8,128)(2,1)S(1)}, bf16[512,128]{1,0:T(8,128)(2,1)S(1)}, bf16[512,128]{1,0:T(8,128)(2,1)S(1)}) custom-call(f32[3,32,512]{2,1,0:T(8,128)S(1)} %copy-done, f32[24,128]{1,0:T(8,128)S(1)} %get-tuple-element.19.refs_0_.t0, f32[24,128]{1,0:T(8,128)S(1)} %shard_map.89.refs_0_.t1, ...), custom_call_target="tpu_custom_call" | custom-call | flops 60000000 | bytes 250000 | tf_op jit(solution)/shard_map/pallas_call | solution.py:437
  25.0 0.0 collective-permute-done.15.refs_4_
  25.0 0.9 %collective-permute-done.14.refs_3_ = f32[24,128]{1,0:T(8,128)S(1)} collective-permute-done((f32[24,128]{1,0:T(8,128)S(1)}, f32[24,128]{1,0:T(8,128)S(1)}, u32[]{:S(2)}, u32[]{:S(2)}) %collective-permute-start.14) | collective-permute-done | bytes 12320 | tf_op jit(solution)/shard_map/ppermute | solution.py:343
  25.9 1.2 %collective-permute-done.13.refs_2_ = f32[24,128]{1,0:T(8,128)S(1)} collective-permute-done((f32[24,128]{1,0:T(8,128)S(1)}, f32[24,128]{1,0:T(8,128)S(1)}, u32[]{:S(2)}, u32[]{:S(2)}) %collective-permute-start.13) | collective-permute-done | bytes 12320 | tf_op jit(solution)/shard_map/ppermute | solution.py:343
  27.1 0.0 collective-permute-done.12.refs_1_
  27.1 0.5 %shard_map.92 = (f32[8,512]{1,0:T(8,128)S(1)}, f32[24,128]{1,0:T(8,128)S(1)}) custom-call(f32[24,128]{1,0:T(8,128)S(1)} %shard_map.90.t2.refs_0_, f32[24,128]{1,0:T(8,128)S(1)} %collective-permute-done.12.refs_1_, f32[24,128]{1,0:T(8,128)S(1)} %collective-permute-done.13.refs_2_, f32[24,128]{1,0:T(8,128)S(1)} %collective-permute-done.14.refs_3_, ...), custom_call_target="tpu_custom_call" | custom-call | flops 80000000 | bytes 900000 | tf_op jit(solution)/shard_map/pallas_call | solution.py:444
  27.6 0.1 collective-permute-start.16
  27.7 1.2 %collective-permute-done.16 = f32[24,128]{1,0:T(8,128)S(1)} collective-permute-done((f32[24,128]{1,0:T(8,128)S(1)}, f32[24,128]{1,0:T(8,128)S(1)}, u32[]{:S(2)}, u32[]{:S(2)}) %collective-permute-start.16) | collective-permute-done | bytes 12320 | tf_op jit(solution)/shard_map/ppermute | solution.py:343
  28.9 1.0 %collective-permute-start.19 = (f32[24,128]{1,0:T(8,128)S(1)}, f32[24,128]{1,0:T(8,128)S(1)}, u32[]{:S(2)}, u32[]{:S(2)}) collective-permute-start(f32[24,128]{1,0:T(8,128)S(1)} %add.21), channel_id=1, source_target_pairs={{0,7},{1,6},{2,5},{3,4},{4,3},{5,2},{6,1},{7,0},{8,15},{9,14},{10,... | collective-permute-start | bytes 36872 | tf_op jit(solution)/shard_map/ppermute | solution.py:343
  29.9 0.4 %collective-permute-start.18 = (f32[24,128]{1,0:T(8,128)S(1)}, f32[24,128]{1,0:T(8,128)S(1)}, u32[]{:S(2)}, u32[]{:S(2)}) collective-permute-start(f32[24,128]{1,0:T(8,128)S(1)} %add.21), channel_id=1, source_target_pairs={{0,5},{1,4},{2,7},{3,6},{4,1},{5,0},{6,3},{7,2},{8,13},{9,12},{10,... | collective-permute-start | bytes 36872 | tf_op jit(solution)/shard_map/ppermute | solution.py:343
  30.3 1.5 %collective-permute-start.17 = (f32[24,128]{1,0:T(8,128)S(1)}, f32[24,128]{1,0:T(8,128)S(1)}, u32[]{:S(2)}, u32[]{:S(2)}) collective-permute-start(f32[24,128]{1,0:T(8,128)S(1)} %add.21), channel_id=1, source_target_pairs={{0,3},{1,2},{2,1},{3,0},{4,7},{5,6},{6,5},{7,4},{8,11},{9,10},{10,... | collective-permute-start | bytes 36872 | tf_op jit(solution)/shard_map/ppermute | solution.py:343
  31.8 1.0 %collective-permute-done.19 = f32[24,128]{1,0:T(8,128)S(1)} collective-permute-done((f32[24,128]{1,0:T(8,128)S(1)}, f32[24,128]{1,0:T(8,128)S(1)}, u32[]{:S(2)}, u32[]{:S(2)}) %collective-permute-start.19) | collective-permute-done | bytes 12320 | tf_op jit(solution)/shard_map/ppermute | solution.py:343
  32.9 0.1 collective-permute-done.18
  33.0 0.4 %collective-permute-done.17 = f32[24,128]{1,0:T(8,128)S(1)} collective-permute-done((f32[24,128]{1,0:T(8,128)S(1)}, f32[24,128]{1,0:T(8,128)S(1)}, u32[]{:S(2)}, u32[]{:S(2)}) %collective-permute-start.17) | collective-permute-done | bytes 12320 | tf_op jit(solution)/shard_map/ppermute | solution.py:343
  33.5 2.1 %collective-permute-start.22 = (f32[24,128]{1,0:T(8,128)S(1)}, f32[24,128]{1,0:T(8,128)S(1)}, u32[]{:S(2)}, u32[]{:S(2)}) collective-permute-start(f32[24,128]{1,0:T(8,128)S(1)} %add_add_fusion.1), channel_id=1, source_target_pairs={{0,25},{1,24},{2,27},{3,26},{4,29},{5,28},{6,31},{7,30},{8,17},{9,... | collective-permute-start | bytes 36872 | tf_op jit(solution)/shard_map/ppermute | solution.py:343
  35.5 0.2 collective-permute-start.21
  35.8 1.6 %collective-permute-start.20 = (f32[24,128]{1,0:T(8,128)S(1)}, f32[24,128]{1,0:T(8,128)S(1)}, u32[]{:S(2)}, u32[]{:S(2)}) collective-permute-start(f32[24,128]{1,0:T(8,128)S(1)} %add_add_fusion.1), channel_id=1, source_target_pairs={{0,9},{1,8},{2,11},{3,10},{4,13},{5,12},{6,15},{7,14},{8,1},{9,0},... | collective-permute-start | bytes 36872 | tf_op jit(solution)/shard_map/ppermute | solution.py:343
  37.4 1.0 %collective-permute-done.22 = f32[24,128]{1,0:T(8,128)S(1)} collective-permute-done((f32[24,128]{1,0:T(8,128)S(1)}, f32[24,128]{1,0:T(8,128)S(1)}, u32[]{:S(2)}, u32[]{:S(2)}) %collective-permute-start.22) | collective-permute-done | bytes 12320 | tf_op jit(solution)/shard_map/ppermute | solution.py:343
  38.4 1.3 %collective-permute-done.21 = f32[24,128]{1,0:T(8,128)S(1)} collective-permute-done((f32[24,128]{1,0:T(8,128)S(1)}, f32[24,128]{1,0:T(8,128)S(1)}, u32[]{:S(2)}, u32[]{:S(2)}) %collective-permute-start.21) | collective-permute-done | bytes 12320 | tf_op jit(solution)/shard_map/ppermute | solution.py:343
  39.7 0.0 collective-permute-done.20
  39.7 1.1 %shard_map.93 = (f32[3,4,512]{2,1,0:T(4,128)}, f32[3,4,36]{2,1,0:T(4,128)}) custom-call(f32[24,128]{1,0:T(8,128)S(1)} %add_add_fusion.refs_0_, f32[3,32,512]{2,1,0:T(8,128)S(1)} %copy-done, f32[24,512]{1,0:T(8,128)S(1)} %get-tuple-element.26.refs_2_, f32[8,512]{1,0:T(8,128)S(1)} %get-tuple-element.27.refs_3_), custom_call_target="tpu_custom_call" | custom-call | flops 50000000 | bytes 400000 | tf_op jit(solution)/shard_map/pallas_call | solution.py:452
  (3 shorter events, 0.0 us)
Async XLA Ops:
  1.7 6.3 %collective-permute-start.3 = (f32[32,128]{1,0:T(8,128)S(1)}, f32[32,128]{1,0:T(8,128)S(1)}, u32[]{:S(2)}, u32[]{:S(2)}) collective-permute-start(f32[32,128]{1,0:T(8,128)S(1)} %shard_map.86.refs_0_), channel_id=1, source_target_pairs={{0,2},{1,0},{2,1},{3,4},{4,3},{5,6},{6,5},{7,8},{8,7},{9,10},{10,9... | collective-permute-start | bytes 49160 | tf_op jit(solution)/shard_map/ppermute | solution.py:343
  4.7 3.7 %collective-permute-start.2 = (f32[32,128]{1,0:T(8,128)S(1)}, f32[32,128]{1,0:T(8,128)S(1)}, u32[]{:S(2)}, u32[]{:S(2)}) collective-permute-start(f32[32,128]{1,0:T(8,128)S(1)} %shard_map.86.refs_0_), channel_id=1, source_target_pairs={{0,8},{1,9},{2,10},{3,11},{4,12},{5,13},{6,14},{7,15},{8,0},{9,1},... | collective-permute-start | bytes 49160 | tf_op jit(solution)/shard_map/ppermute | solution.py:343
  6.6 3.2 %collective-permute-start.1 = (f32[32,128]{1,0:T(8,128)S(1)}, f32[32,128]{1,0:T(8,128)S(1)}, u32[]{:S(2)}, u32[]{:S(2)}) collective-permute-start(f32[32,128]{1,0:T(8,128)S(1)} %shard_map.86.refs_0_), channel_id=1, source_target_pairs={{0,1},{1,2},{2,3},{3,0},{4,5},{5,4},{6,7},{7,6},{8,16},{9,17},{10,... | collective-permute-start | bytes 49160 | tf_op jit(solution)/shard_map/ppermute | solution.py:343
  6.6 3.2 %collective-permute-start = (f32[32,128]{1,0:T(8,128)S(1)}, f32[32,128]{1,0:T(8,128)S(1)}, u32[]{:S(2)}, u32[]{:S(2)}) collective-permute-start(f32[32,128]{1,0:T(8,128)S(1)} %shard_map.86.refs_0_), channel_id=1, source_target_pairs={{0,1},{1,0},{2,3},{3,2},{4,5},{5,4},{6,7},{7,6},{8,9},{9,8},{10,11... | collective-permute-start | bytes 49160 | tf_op jit(solution)/shard_map/ppermute | solution.py:343
  10.1 3.7 %collective-permute-start.7 = (f32[24,128]{1,0:T(8,128)S(1)}, f32[24,128]{1,0:T(8,128)S(1)}, u32[]{:S(2)}, u32[]{:S(2)}) collective-permute-start(f32[24,128]{1,0:T(8,128)S(1)} %get-tuple-element.19.refs_0_.t0), channel_id=1, source_target_pairs={{0,2},{1,0},{2,1},{3,4},{4,3},{5,6},{6,5},{7,8},{8,7},{9,10},{10,9... | collective-permute-start | bytes 36872 | tf_op jit(solution)/shard_map/ppermute | solution.py:343
  10.6 3.7 %collective-permute-start.6 = (f32[24,128]{1,0:T(8,128)S(1)}, f32[24,128]{1,0:T(8,128)S(1)}, u32[]{:S(2)}, u32[]{:S(2)}) collective-permute-start(f32[24,128]{1,0:T(8,128)S(1)} %get-tuple-element.19.refs_0_.t0), channel_id=1, source_target_pairs={{0,8},{1,9},{2,10},{3,11},{4,12},{5,13},{6,14},{7,15},{8,0},{9,1},... | collective-permute-start | bytes 36872 | tf_op jit(solution)/shard_map/ppermute | solution.py:343
  12.0 3.1 %collective-permute-start.5 = (f32[24,128]{1,0:T(8,128)S(1)}, f32[24,128]{1,0:T(8,128)S(1)}, u32[]{:S(2)}, u32[]{:S(2)}) collective-permute-start(f32[24,128]{1,0:T(8,128)S(1)} %get-tuple-element.19.refs_0_.t0), channel_id=1, source_target_pairs={{0,1},{1,2},{2,3},{3,0},{4,5},{5,4},{6,7},{7,6},{8,16},{9,17},{10,... | collective-permute-start | bytes 36872 | tf_op jit(solution)/shard_map/ppermute | solution.py:343
  12.2 2.9 %collective-permute-start.4 = (f32[24,128]{1,0:T(8,128)S(1)}, f32[24,128]{1,0:T(8,128)S(1)}, u32[]{:S(2)}, u32[]{:S(2)}) collective-permute-start(f32[24,128]{1,0:T(8,128)S(1)} %get-tuple-element.19.refs_0_.t0), channel_id=1, source_target_pairs={{0,1},{1,0},{2,3},{3,2},{4,5},{5,4},{6,7},{7,6},{8,9},{9,8},{10,11... | collective-permute-start | bytes 36872 | tf_op jit(solution)/shard_map/ppermute | solution.py:343
  15.4 9.0 %copy-start = (f32[3,32,512]{2,1,0:T(8,128)S(1)}, f32[3,32,512]{2,1,0:T(8,128)}, u32[]{:S(2)}) copy-start(f32[3,32,512]{2,1,0:T(8,128)} %refs_1_.1) | copy-start | bytes 589828
  15.4 3.4 %collective-permute-start.11 = (f32[24,128]{1,0:T(8,128)S(1)}, f32[24,128]{1,0:T(8,128)S(1)}, u32[]{:S(2)}, u32[]{:S(2)}) collective-permute-start(f32[24,128]{1,0:T(8,128)S(1)} %shard_map.89.refs_0_.t1), channel_id=1, source_target_pairs={{0,2},{1,0},{2,1},{3,4},{4,3},{5,6},{6,5},{7,8},{8,7},{9,10},{10,9... | collective-permute-start | bytes 36872 | tf_op jit(solution)/shard_map/ppermute | solution.py:343
  17.1 3.7 %collective-permute-start.10 = (f32[24,128]{1,0:T(8,128)S(1)}, f32[24,128]{1,0:T(8,128)S(1)}, u32[]{:S(2)}, u32[]{:S(2)}) collective-permute-start(f32[24,128]{1,0:T(8,128)S(1)} %shard_map.89.refs_0_.t1), channel_id=1, source_target_pairs={{0,8},{1,9},{2,10},{3,11},{4,12},{5,13},{6,14},{7,15},{8,0},{9,1},... | collective-permute-start | bytes 36872 | tf_op jit(solution)/shard_map/ppermute | solution.py:343
  18.8 3.1 %collective-permute-start.9 = (f32[24,128]{1,0:T(8,128)S(1)}, f32[24,128]{1,0:T(8,128)S(1)}, u32[]{:S(2)}, u32[]{:S(2)}) collective-permute-start(f32[24,128]{1,0:T(8,128)S(1)} %shard_map.89.refs_0_.t1), channel_id=1, source_target_pairs={{0,1},{1,2},{2,3},{3,0},{4,5},{5,4},{6,7},{7,6},{8,16},{9,17},{10,... | collective-permute-start | bytes 36872 | tf_op jit(solution)/shard_map/ppermute | solution.py:343
  18.8 3.1 %collective-permute-start.8 = (f32[24,128]{1,0:T(8,128)S(1)}, f32[24,128]{1,0:T(8,128)S(1)}, u32[]{:S(2)}, u32[]{:S(2)}) collective-permute-start(f32[24,128]{1,0:T(8,128)S(1)} %shard_map.89.refs_0_.t1), channel_id=1, source_target_pairs={{0,1},{1,0},{2,3},{3,2},{4,5},{5,4},{6,7},{7,6},{8,9},{9,8},{10,11... | collective-permute-start | bytes 36872 | tf_op jit(solution)/shard_map/ppermute | solution.py:343
  22.2 2.8 %collective-permute-start.15 = (f32[24,128]{1,0:T(8,128)S(1)}, f32[24,128]{1,0:T(8,128)S(1)}, u32[]{:S(2)}, u32[]{:S(2)}) collective-permute-start(f32[24,128]{1,0:T(8,128)S(1)} %shard_map.90.t2.refs_0_), channel_id=1, source_target_pairs={{0,2},{1,0},{2,1},{3,4},{4,3},{5,6},{6,5},{7,8},{8,7},{9,10},{10,9... | collective-permute-start | bytes 36872 | tf_op jit(solution)/shard_map/ppermute | solution.py:343
  22.2 3.8 %collective-permute-start.14 = (f32[24,128]{1,0:T(8,128)S(1)}, f32[24,128]{1,0:T(8,128)S(1)}, u32[]{:S(2)}, u32[]{:S(2)}) collective-permute-start(f32[24,128]{1,0:T(8,128)S(1)} %shard_map.90.t2.refs_0_), channel_id=1, source_target_pairs={{0,8},{1,9},{2,10},{3,11},{4,12},{5,13},{6,14},{7,15},{8,0},{9,1},... | collective-permute-start | bytes 36872 | tf_op jit(solution)/shard_map/ppermute | solution.py:343
  24.0 3.1 %collective-permute-start.13 = (f32[24,128]{1,0:T(8,128)S(1)}, f32[24,128]{1,0:T(8,128)S(1)}, u32[]{:S(2)}, u32[]{:S(2)}) collective-permute-start(f32[24,128]{1,0:T(8,128)S(1)} %shard_map.90.t2.refs_0_), channel_id=1, source_target_pairs={{0,1},{1,2},{2,3},{3,0},{4,5},{5,4},{6,7},{7,6},{8,16},{9,17},{10,... | collective-permute-start | bytes 36872 | tf_op jit(solution)/shard_map/ppermute | solution.py:343
  24.0 3.1 %collective-permute-start.12 = (f32[24,128]{1,0:T(8,128)S(1)}, f32[24,128]{1,0:T(8,128)S(1)}, u32[]{:S(2)}, u32[]{:S(2)}) collective-permute-start(f32[24,128]{1,0:T(8,128)S(1)} %shard_map.90.t2.refs_0_), channel_id=1, source_target_pairs={{0,1},{1,0},{2,3},{3,2},{4,5},{5,4},{6,7},{7,6},{8,9},{9,8},{10,11... | collective-permute-start | bytes 36872 | tf_op jit(solution)/shard_map/ppermute | solution.py:343
  27.6 1.2 %collective-permute-start.16 = (f32[24,128]{1,0:T(8,128)S(1)}, f32[24,128]{1,0:T(8,128)S(1)}, u32[]{:S(2)}, u32[]{:S(2)}) collective-permute-start(f32[24,128]{1,0:T(8,128)S(1)} %get-tuple-element.25), channel_id=1, source_target_pairs={{0,1},{1,0},{2,3},{3,2},{4,5},{5,4},{6,7},{7,6},{8,9},{9,8},{10,11... | collective-permute-start | bytes 36872 | tf_op jit(solution)/shard_map/ppermute | solution.py:343
  28.9 4.0 %collective-permute-start.19 = (f32[24,128]{1,0:T(8,128)S(1)}, f32[24,128]{1,0:T(8,128)S(1)}, u32[]{:S(2)}, u32[]{:S(2)}) collective-permute-start(f32[24,128]{1,0:T(8,128)S(1)} %add.21), channel_id=1, source_target_pairs={{0,7},{1,6},{2,5},{3,4},{4,3},{5,2},{6,1},{7,0},{8,15},{9,14},{10,... | collective-permute-start | bytes 36872 | tf_op jit(solution)/shard_map/ppermute | solution.py:343
  29.9 3.1 %collective-permute-start.18 = (f32[24,128]{1,0:T(8,128)S(1)}, f32[24,128]{1,0:T(8,128)S(1)}, u32[]{:S(2)}, u32[]{:S(2)}) collective-permute-start(f32[24,128]{1,0:T(8,128)S(1)} %add.21), channel_id=1, source_target_pairs={{0,5},{1,4},{2,7},{3,6},{4,1},{5,0},{6,3},{7,2},{8,13},{9,12},{10,... | collective-permute-start | bytes 36872 | tf_op jit(solution)/shard_map/ppermute | solution.py:343
  30.3 3.1 %collective-permute-start.17 = (f32[24,128]{1,0:T(8,128)S(1)}, f32[24,128]{1,0:T(8,128)S(1)}, u32[]{:S(2)}, u32[]{:S(2)}) collective-permute-start(f32[24,128]{1,0:T(8,128)S(1)} %add.21), channel_id=1, source_target_pairs={{0,3},{1,2},{2,1},{3,0},{4,7},{5,6},{6,5},{7,4},{8,11},{9,10},{10,... | collective-permute-start | bytes 36872 | tf_op jit(solution)/shard_map/ppermute | solution.py:343
  33.5 4.9 %collective-permute-start.22 = (f32[24,128]{1,0:T(8,128)S(1)}, f32[24,128]{1,0:T(8,128)S(1)}, u32[]{:S(2)}, u32[]{:S(2)}) collective-permute-start(f32[24,128]{1,0:T(8,128)S(1)} %add_add_fusion.1), channel_id=1, source_target_pairs={{0,25},{1,24},{2,27},{3,26},{4,29},{5,28},{6,31},{7,30},{8,17},{9,... | collective-permute-start | bytes 36872 | tf_op jit(solution)/shard_map/ppermute | solution.py:343
  35.5 4.1 %collective-permute-start.21 = (f32[24,128]{1,0:T(8,128)S(1)}, f32[24,128]{1,0:T(8,128)S(1)}, u32[]{:S(2)}, u32[]{:S(2)}) collective-permute-start(f32[24,128]{1,0:T(8,128)S(1)} %add_add_fusion.1), channel_id=1, source_target_pairs={{0,17},{1,16},{2,19},{3,18},{4,21},{5,20},{6,23},{7,22},{8,25},{9,... | collective-permute-start | bytes 36872 | tf_op jit(solution)/shard_map/ppermute | solution.py:343
  35.8 3.9 %collective-permute-start.20 = (f32[24,128]{1,0:T(8,128)S(1)}, f32[24,128]{1,0:T(8,128)S(1)}, u32[]{:S(2)}, u32[]{:S(2)}) collective-permute-start(f32[24,128]{1,0:T(8,128)S(1)} %add_add_fusion.1), channel_id=1, source_target_pairs={{0,9},{1,8},{2,11},{3,10},{4,13},{5,12},{6,15},{7,14},{8,1},{9,0},... | collective-permute-start | bytes 36872 | tf_op jit(solution)/shard_map/ppermute | solution.py:343

commit v14 on v12

--- a/solution.py
+++ b/solution.py
@@ -40,7 +40,11 @@
 
 def lines_of(tile, width):
     wide = jnp.concatenate([tile] * (width // 128), axis=1)
-    wide = jnp.where(own_lanes(wide.shape[0], width), wide, 0.0)
+    return joined(jnp.where(own_lanes(wide.shape[0], width), wide, 0.0))
+
+
+def joined(wide):
+    width = wide.shape[1]
     where = iota((8, width), 0)
     result = jnp.zeros((8, width), jnp.float32)
     for c in range(COMPS):
@@ -155,7 +159,7 @@
     return jnp.concatenate([jnp.broadcast_to(x, (8, 128)) for x in at], axis=0).astype(jnp.int32)
 
 
-def multiply(choose, pieces, shift, high, low):
+def product(choose, pieces, high, low):
     rows = 8 * COMPS
     front = iota((8, 128), 1) < BLOCK
     picked = []
@@ -181,7 +185,11 @@
     left = jnp.concatenate([top, x - top], axis=0).astype(jnp.bfloat16)
     both = dot(left, high) + dot(left, low)
     image = both[:rows] + both[rows:]
-    image = fold(jnp.where(own_lanes(rows, image.shape[1]), image, 0.0))
+    return jnp.where(own_lanes(rows, image.shape[1]), image, 0.0)
+
+
+def multiply(choose, pieces, shift, high, low):
+    image = fold(product(choose, pieces, high, low))
     return image - jnp.concatenate([shift] * COMPS, axis=0) * pieces[0]
 
 
@@ -232,12 +240,14 @@
     gram_ref[16:, :] = result
 
 
-def last_kernel(vecs, own, a, b, c, d, choose, aux, high, low, early, t0, t1, t2, line_ref, gram_ref):
+def last_kernel(
+    vecs, own, a, b, c, d, choose, aux, high, low, early, t0, t1, t2, lines, line_ref, gram_ref
+):
     pieces = [ref[...] for ref in (own, a, b, c, d)]
-    tile = multiply(choose[...], pieces, aux[8 * S - 8 : 8 * S, :], high[...], low[...])
-    rows = line_ref.shape[1]
+    image = joined(product(choose[...], pieces, high[...], low[...]))
     width = COMPS * vecs
-    last = lines_of(tile, rows)
+    shift = aux[8 * S - 8 : 8 * S, :1]
+    last = image - shift * lines[8 * S - 16 :, :]
     line_ref[...] = last
     gram = split_dot(last, (t0[...], t1[...], t2[...]))
     square = jnp.sum(last * last, axis=1, keepdims=True)
@@ -299,7 +309,7 @@
         for l in range(k):
             value = value - unit[k, l] * vectors[l]
         vectors.append(value)
-        value = value / roots[k]
+        value = value * (1.0 / roots[k])
         for c in range(comps):
             basis_ref[c, k : k + 1, :] = value[c : c + 1]
     for c in range(comps):
@@ -438,10 +448,10 @@
     last, gram = call(
         lambda *refs: last_kernel(vecs, *refs),
         [((8, rows), f32), gram_out],
-        [VMEM] * 13,
+        [VMEM] * 14,
         80000000,
         900000,
-    )(tile, *received, choose, aux, high, low, early, *parts)
+    )(tile, *received, choose, aux, high, low, early, *parts, lines)
     total = float(length * rows)
     basis, factors = call(
         lambda *refs: finish_kernel(total, *refs),

time: 40.9 us -> 40.8 us (level)
  no operation moved by 1% of the time
where the time goes in v14:
time: 40.8 us; the launch traced here: 40.6 us
  starting transfers between devices  21.1 us (52%)
  waiting for transfers between devices  13.4 us (33%)
  Pallas kernels  5.41 us (13%)
  between operations  0.72 us (2%)
    ppermute x23, starting transfers between devices, send(): lax.ppermute(value, 'dom', [(d, target[d]) for d in range(lax.axis_size('...  21.1 us
    ppermute x23, waiting for transfers between devices, send(): lax.ppermute(value, 'dom', [(d, target[d]) for d in range(lax.axis_size('...  13.4 us
    pallas_call x1, Pallas kernels, local(): call(prepare_kernel, [((width, rows), bf16), ((width, rows), bf16), ((8 *...  1.39 us
    pallas_call x1, Pallas kernels, local(): call(start_kernel, [((comps * blocks + 8, 128), f32)], [HBM] * 4, 600000,...  1.08 us
    pallas_call x1, Pallas kernels, local(): call(lambda *refs: finish_kernel(total, *refs), [((comps, S, rows), f32),...  1.02 us
  transfers between devices with their start and end apart: 23, of which 14 were waited for; matrix products, arithmetic and copies ran while one was open for 0% of the time, Pallas kernels for 5%

profile of v14, /device:TPU:0, one launch (start us, length us, event | category | flops | bytes accessed | tf_op | source)
XLA Modules:
  0.0 40.6 jit_solution(14751884779448671150)
XLA Ops:
  0.6 1.1 %shard_map.86.refs_0_ = f32[32,128]{1,0:T(8,128)S(1)} custom-call(f32[3,32,512]{2,1,0:T(8,128)} %refs_1_.1, f32[3,32]{1,0:T(4,128)} %mix_in.1, s32[1,4,8]{2,1,0:T(4,128)} %list_in.1, s32[1,4]{1,0:T(1,128)} %count_in.1), custom_call_target="tpu_custom_call" | custom-call | flops 600000 | bytes 250000 | tf_op jit(solution)/shard_map/pallas_call | solution.py:397
  1.7 3.0 %collective-permute-start.3 = (f32[32,128]{1,0:T(8,128)S(1)}, f32[32,128]{1,0:T(8,128)S(1)}, u32[]{:S(2)}, u32[]{:S(2)}) collective-permute-start(f32[32,128]{1,0:T(8,128)S(1)} %shard_map.86.refs_0_), channel_id=1, source_target_pairs={{0,2},{1,0},{2,1},{3,4},{4,3},{5,6},{6,5},{7,8},{8,7},{9,10},{10,9... | collective-permute-start | bytes 49160 | tf_op jit(solution)/shard_map/ppermute | solution.py:347
  4.7 1.9 %collective-permute-start.2 = (f32[32,128]{1,0:T(8,128)S(1)}, f32[32,128]{1,0:T(8,128)S(1)}, u32[]{:S(2)}, u32[]{:S(2)}) collective-permute-start(f32[32,128]{1,0:T(8,128)S(1)} %shard_map.86.refs_0_), channel_id=1, source_target_pairs={{0,8},{1,9},{2,10},{3,11},{4,12},{5,13},{6,14},{7,15},{8,0},{9,1},... | collective-permute-start | bytes 49160 | tf_op jit(solution)/shard_map/ppermute | solution.py:347
  6.6 0.0 collective-permute-start.1
  6.6 0.0 collective-permute-start
  6.6 1.4 %shard_map.87 = (bf16[256,512]{1,0:T(8,128)(2,1)S(1)}, bf16[256,512]{1,0:T(8,128)(2,1)S(1)}, f32[40,128]{1,0:T(8,128)S(1)}) custom-call(f32[512,256]{1,0:T(8,128)} %strips_in.1, s32[4,8]{1,0:T(4,128)} %bitcast.2, f32[4]{0:T(128)} %shifts_in.1), custom_call_target="tpu_custom_call" | custom-call | flops 1000000 | bytes 1000000 | tf_op jit(solution)/shard_map/pallas_call | solution.py:411
  8.0 0.0 collective-permute-done.3.refs_4_
  8.0 0.5 %collective-permute-done.2.refs_3_ = f32[32,128]{1,0:T(8,128)S(1)} collective-permute-done((f32[32,128]{1,0:T(8,128)S(1)}, f32[32,128]{1,0:T(8,128)S(1)}, u32[]{:S(2)}, u32[]{:S(2)}) %collective-permute-start.2) | collective-permute-done | bytes 16416 | tf_op jit(solution)/shard_map/ppermute | solution.py:347
  8.5 1.3 %collective-permute-done.1.refs_2_ = f32[32,128]{1,0:T(8,128)S(1)} collective-permute-done((f32[32,128]{1,0:T(8,128)S(1)}, f32[32,128]{1,0:T(8,128)S(1)}, u32[]{:S(2)}, u32[]{:S(2)}) %collective-permute-start.1) | collective-permute-done | bytes 16416 | tf_op jit(solution)/shard_map/ppermute | solution.py:347
  9.7 0.0 collective-permute-done.refs_1_
  9.7 0.4 shard_map.88
  10.1 0.4 %collective-permute-start.7 = (f32[24,128]{1,0:T(8,128)S(1)}, f32[24,128]{1,0:T(8,128)S(1)}, u32[]{:S(2)}, u32[]{:S(2)}) collective-permute-start(f32[24,128]{1,0:T(8,128)S(1)} %get-tuple-element.19.refs_0_.t0), channel_id=1, source_target_pairs={{0,2},{1,0},{2,1},{3,4},{4,3},{5,6},{6,5},{7,8},{8,7},{9,10},{10,9... | collective-permute-start | bytes 36872 | tf_op jit(solution)/shard_map/ppermute | solution.py:347
  10.6 1.4 %collective-permute-start.6 = (f32[24,128]{1,0:T(8,128)S(1)}, f32[24,128]{1,0:T(8,128)S(1)}, u32[]{:S(2)}, u32[]{:S(2)}) collective-permute-start(f32[24,128]{1,0:T(8,128)S(1)} %get-tuple-element.19.refs_0_.t0), channel_id=1, source_target_pairs={{0,8},{1,9},{2,10},{3,11},{4,12},{5,13},{6,14},{7,15},{8,0},{9,1},... | collective-permute-start | bytes 36872 | tf_op jit(solution)/shard_map/ppermute | solution.py:347
  12.0 0.2 collective-permute-start.5
  12.2 1.7 %collective-permute-start.4 = (f32[24,128]{1,0:T(8,128)S(1)}, f32[24,128]{1,0:T(8,128)S(1)}, u32[]{:S(2)}, u32[]{:S(2)}) collective-permute-start(f32[24,128]{1,0:T(8,128)S(1)} %get-tuple-element.19.refs_0_.t0), channel_id=1, source_target_pairs={{0,1},{1,0},{2,3},{3,2},{4,5},{5,4},{6,7},{7,6},{8,9},{9,8},{10,11... | collective-permute-start | bytes 36872 | tf_op jit(solution)/shard_map/ppermute | solution.py:347
  13.8 0.0 collective-permute-done.7.refs_4_
  13.8 0.4 %collective-permute-done.6.refs_3_ = f32[24,128]{1,0:T(8,128)S(1)} collective-permute-done((f32[24,128]{1,0:T(8,128)S(1)}, f32[24,128]{1,0:T(8,128)S(1)}, u32[]{:S(2)}, u32[]{:S(2)}) %collective-permute-start.6) | collective-permute-done | bytes 12320 | tf_op jit(solution)/shard_map/ppermute | solution.py:347
  14.3 0.9 %collective-permute-done.5.refs_2_ = f32[24,128]{1,0:T(8,128)S(1)} collective-permute-done((f32[24,128]{1,0:T(8,128)S(1)}, f32[24,128]{1,0:T(8,128)S(1)}, u32[]{:S(2)}, u32[]{:S(2)}) %collective-permute-start.5) | collective-permute-done | bytes 12320 | tf_op jit(solution)/shard_map/ppermute | solution.py:347
  15.1 0.0 collective-permute-done.4.refs_1_
  15.1 0.3 shard_map.89.refs_0_.t1
  15.4 0.0 copy-start
  15.4 1.7 %collective-permute-start.11 = (f32[24,128]{1,0:T(8,128)S(1)}, f32[24,128]{1,0:T(8,128)S(1)}, u32[]{:S(2)}, u32[]{:S(2)}) collective-permute-start(f32[24,128]{1,0:T(8,128)S(1)} %shard_map.89.refs_0_.t1), channel_id=1, source_target_pairs={{0,2},{1,0},{2,1},{3,4},{4,3},{5,6},{6,5},{7,8},{8,7},{9,10},{10,9... | collective-permute-start | bytes 36872 | tf_op jit(solution)/shard_map/ppermute | solution.py:347
  17.1 1.6 %collective-permute-start.10 = (f32[24,128]{1,0:T(8,128)S(1)}, f32[24,128]{1,0:T(8,128)S(1)}, u32[]{:S(2)}, u32[]{:S(2)}) collective-permute-start(f32[24,128]{1,0:T(8,128)S(1)} %shard_map.89.refs_0_.t1), channel_id=1, source_target_pairs={{0,8},{1,9},{2,10},{3,11},{4,12},{5,13},{6,14},{7,15},{8,0},{9,1},... | collective-permute-start | bytes 36872 | tf_op jit(solution)/shard_map/ppermute | solution.py:347
  18.8 0.0 collective-permute-start.9
  18.8 0.0 collective-permute-start.8
  18.8 0.0 collective-permute-done.11.refs_4_
  18.8 2.0 %collective-permute-done.10.refs_3_ = f32[24,128]{1,0:T(8,128)S(1)} collective-permute-done((f32[24,128]{1,0:T(8,128)S(1)}, f32[24,128]{1,0:T(8,128)S(1)}, u32[]{:S(2)}, u32[]{:S(2)}) %collective-permute-start.10) | collective-permute-done | bytes 12320 | tf_op jit(solution)/shard_map/ppermute | solution.py:347
  20.8 1.1 %collective-permute-done.9.refs_2_ = f32[24,128]{1,0:T(8,128)S(1)} collective-permute-done((f32[24,128]{1,0:T(8,128)S(1)}, f32[24,128]{1,0:T(8,128)S(1)}, u32[]{:S(2)}, u32[]{:S(2)}) %collective-permute-start.9) | collective-permute-done | bytes 12320 | tf_op jit(solution)/shard_map/ppermute | solution.py:347
  21.9 0.0 collective-permute-done.8.refs_1_
  21.9 0.3 shard_map.90.t2.refs_0_
  22.2 0.0 collective-permute-start.15
  22.2 1.8 %collective-permute-start.14 = (f32[24,128]{1,0:T(8,128)S(1)}, f32[24,128]{1,0:T(8,128)S(1)}, u32[]{:S(2)}, u32[]{:S(2)}) collective-permute-start(f32[24,128]{1,0:T(8,128)S(1)} %shard_map.90.t2.refs_0_), channel_id=1, source_target_pairs={{0,8},{1,9},{2,10},{3,11},{4,12},{5,13},{6,14},{7,15},{8,0},{9,1},... | collective-permute-start | bytes 36872 | tf_op jit(solution)/shard_map/ppermute | solution.py:347
  24.0 0.0 collective-permute-start.13
  24.0 0.4 collective-permute-start.12
  24.4 0.0 copy-done
  24.4 0.6 %shard_map.91 = (f32[24,512]{1,0:T(8,128)S(1)}, f32[24,128]{1,0:T(8,128)S(1)}, bf16[512,128]{1,0:T(8,128)(2,1)S(1)}, bf16[512,128]{1,0:T(8,128)(2,1)S(1)}, bf16[512,128]{1,0:T(8,128)(2,1)S(1)}) custom-call(f32[3,32,512]{2,1,0:T(8,128)S(1)} %copy-done, f32[24,128]{1,0:T(8,128)S(1)} %get-tuple-element.19.refs_0_.t0, f32[24,128]{1,0:T(8,128)S(1)} %shard_map.89.refs_0_.t1, ...), custom_call_target="tpu_custom_call" | custom-call | flops 60000000 | bytes 250000 | tf_op jit(solution)/shard_map/pallas_call | solution.py:441
  25.0 0.0 collective-permute-done.15.refs_4_
  25.0 0.9 %collective-permute-done.14.refs_3_ = f32[24,128]{1,0:T(8,128)S(1)} collective-permute-done((f32[24,128]{1,0:T(8,128)S(1)}, f32[24,128]{1,0:T(8,128)S(1)}, u32[]{:S(2)}, u32[]{:S(2)}) %collective-permute-start.14) | collective-permute-done | bytes 12320 | tf_op jit(solution)/shard_map/ppermute | solution.py:347
  25.9 1.2 %collective-permute-done.13.refs_2_ = f32[24,128]{1,0:T(8,128)S(1)} collective-permute-done((f32[24,128]{1,0:T(8,128)S(1)}, f32[24,128]{1,0:T(8,128)S(1)}, u32[]{:S(2)}, u32[]{:S(2)}) %collective-permute-start.13) | collective-permute-done | bytes 12320 | tf_op jit(solution)/shard_map/ppermute | solution.py:347
  27.1 0.0 collective-permute-done.12.refs_1_
  27.1 0.4 shard_map.92
  27.5 0.1 collective-permute-start.16
  27.6 1.2 %collective-permute-done.16 = f32[24,128]{1,0:T(8,128)S(1)} collective-permute-done((f32[24,128]{1,0:T(8,128)S(1)}, f32[24,128]{1,0:T(8,128)S(1)}, u32[]{:S(2)}, u32[]{:S(2)}) %collective-permute-start.16) | collective-permute-done | bytes 12320 | tf_op jit(solution)/shard_map/ppermute | solution.py:347
  28.8 1.0 %collective-permute-start.19 = (f32[24,128]{1,0:T(8,128)S(1)}, f32[24,128]{1,0:T(8,128)S(1)}, u32[]{:S(2)}, u32[]{:S(2)}) collective-permute-start(f32[24,128]{1,0:T(8,128)S(1)} %add.21), channel_id=1, source_target_pairs={{0,7},{1,6},{2,5},{3,4},{4,3},{5,2},{6,1},{7,0},{8,15},{9,14},{10,... | collective-permute-start | bytes 36872 | tf_op jit(solution)/shard_map/ppermute | solution.py:347
  29.8 0.4 %collective-permute-start.18 = (f32[24,128]{1,0:T(8,128)S(1)}, f32[24,128]{1,0:T(8,128)S(1)}, u32[]{:S(2)}, u32[]{:S(2)}) collective-permute-start(f32[24,128]{1,0:T(8,128)S(1)} %add.21), channel_id=1, source_target_pairs={{0,5},{1,4},{2,7},{3,6},{4,1},{5,0},{6,3},{7,2},{8,13},{9,12},{10,... | collective-permute-start | bytes 36872 | tf_op jit(solution)/shard_map/ppermute | solution.py:347
  30.3 1.5 %collective-permute-start.17 = (f32[24,128]{1,0:T(8,128)S(1)}, f32[24,128]{1,0:T(8,128)S(1)}, u32[]{:S(2)}, u32[]{:S(2)}) collective-permute-start(f32[24,128]{1,0:T(8,128)S(1)} %add.21), channel_id=1, source_target_pairs={{0,3},{1,2},{2,1},{3,0},{4,7},{5,6},{6,5},{7,4},{8,11},{9,10},{10,... | collective-permute-start | bytes 36872 | tf_op jit(solution)/shard_map/ppermute | solution.py:347
  31.8 1.0 %collective-permute-done.19 = f32[24,128]{1,0:T(8,128)S(1)} collective-permute-done((f32[24,128]{1,0:T(8,128)S(1)}, f32[24,128]{1,0:T(8,128)S(1)}, u32[]{:S(2)}, u32[]{:S(2)}) %collective-permute-start.19) | collective-permute-done | bytes 12320 | tf_op jit(solution)/shard_map/ppermute | solution.py:347
  32.8 0.1 collective-permute-done.18
  32.9 0.4 %collective-permute-done.17 = f32[24,128]{1,0:T(8,128)S(1)} collective-permute-done((f32[24,128]{1,0:T(8,128)S(1)}, f32[24,128]{1,0:T(8,128)S(1)}, u32[]{:S(2)}, u32[]{:S(2)}) %collective-permute-start.17) | collective-permute-done | bytes 12320 | tf_op jit(solution)/shard_map/ppermute | solution.py:347
  33.4 2.1 %collective-permute-start.22 = (f32[24,128]{1,0:T(8,128)S(1)}, f32[24,128]{1,0:T(8,128)S(1)}, u32[]{:S(2)}, u32[]{:S(2)}) collective-permute-start(f32[24,128]{1,0:T(8,128)S(1)} %add_add_fusion.1), channel_id=1, source_target_pairs={{0,25},{1,24},{2,27},{3,26},{4,29},{5,28},{6,31},{7,30},{8,17},{9,... | collective-permute-start | bytes 36872 | tf_op jit(solution)/shard_map/ppermute | solution.py:347
  35.5 0.2 collective-permute-start.21
  35.7 1.6 %collective-permute-start.20 = (f32[24,128]{1,0:T(8,128)S(1)}, f32[24,128]{1,0:T(8,128)S(1)}, u32[]{:S(2)}, u32[]{:S(2)}) collective-permute-start(f32[24,128]{1,0:T(8,128)S(1)} %add_add_fusion.1), channel_id=1, source_target_pairs={{0,9},{1,8},{2,11},{3,10},{4,13},{5,12},{6,15},{7,14},{8,1},{9,0},... | collective-permute-start | bytes 36872 | tf_op jit(solution)/shard_map/ppermute | solution.py:347
  37.3 1.0 %collective-permute-done.22 = f32[24,128]{1,0:T(8,128)S(1)} collective-permute-done((f32[24,128]{1,0:T(8,128)S(1)}, f32[24,128]{1,0:T(8,128)S(1)}, u32[]{:S(2)}, u32[]{:S(2)}) %collective-permute-start.22) | collective-permute-done | bytes 12320 | tf_op jit(solution)/shard_map/ppermute | solution.py:347
  38.3 1.3 %collective-permute-done.21 = f32[24,128]{1,0:T(8,128)S(1)} collective-permute-done((f32[24,128]{1,0:T(8,128)S(1)}, f32[24,128]{1,0:T(8,128)S(1)}, u32[]{:S(2)}, u32[]{:S(2)}) %collective-permute-start.21) | collective-permute-done | bytes 12320 | tf_op jit(solution)/shard_map/ppermute | solution.py:347
  39.6 0.0 collective-permute-done.20
  39.6 1.0 %shard_map.93 = (f32[3,4,512]{2,1,0:T(4,128)}, f32[3,4,36]{2,1,0:T(4,128)}) custom-call(f32[24,128]{1,0:T(8,128)S(1)} %add_add_fusion.refs_0_, f32[3,32,512]{2,1,0:T(8,128)S(1)} %copy-done, f32[24,512]{1,0:T(8,128)S(1)} %get-tuple-element.25.refs_13_.refs_2_, f32[8,512]{1,0:T(8,128)S(1)} %get-tuple-element.27.refs_3_), custom_call_target="tpu_custom_call" | custom-call | flops 50000000 | bytes 400000 | tf_op jit(solution)/shard_map/pallas_call | solution.py:456
  (3 shorter events, 0.0 us)
Async XLA Ops:
  1.7 6.3 %collective-permute-start.3 = (f32[32,128]{1,0:T(8,128)S(1)}, f32[32,128]{1,0:T(8,128)S(1)}, u32[]{:S(2)}, u32[]{:S(2)}) collective-permute-start(f32[32,128]{1,0:T(8,128)S(1)} %shard_map.86.refs_0_), channel_id=1, source_target_pairs={{0,2},{1,0},{2,1},{3,4},{4,3},{5,6},{6,5},{7,8},{8,7},{9,10},{10,9... | collective-permute-start | bytes 49160 | tf_op jit(solution)/shard_map/ppermute | solution.py:347
  4.7 3.7 %collective-permute-start.2 = (f32[32,128]{1,0:T(8,128)S(1)}, f32[32,128]{1,0:T(8,128)S(1)}, u32[]{:S(2)}, u32[]{:S(2)}) collective-permute-start(f32[32,128]{1,0:T(8,128)S(1)} %shard_map.86.refs_0_), channel_id=1, source_target_pairs={{0,8},{1,9},{2,10},{3,11},{4,12},{5,13},{6,14},{7,15},{8,0},{9,1},... | collective-permute-start | bytes 49160 | tf_op jit(solution)/shard_map/ppermute | solution.py:347
  6.6 3.2 %collective-permute-start.1 = (f32[32,128]{1,0:T(8,128)S(1)}, f32[32,128]{1,0:T(8,128)S(1)}, u32[]{:S(2)}, u32[]{:S(2)}) collective-permute-start(f32[32,128]{1,0:T(8,128)S(1)} %shard_map.86.refs_0_), channel_id=1, source_target_pairs={{0,1},{1,2},{2,3},{3,0},{4,5},{5,4},{6,7},{7,6},{8,16},{9,17},{10,... | collective-permute-start | bytes 49160 | tf_op jit(solution)/shard_map/ppermute | solution.py:347
  6.6 3.2 %collective-permute-start = (f32[32,128]{1,0:T(8,128)S(1)}, f32[32,128]{1,0:T(8,128)S(1)}, u32[]{:S(2)}, u32[]{:S(2)}) collective-permute-start(f32[32,128]{1,0:T(8,128)S(1)} %shard_map.86.refs_0_), channel_id=1, source_target_pairs={{0,1},{1,0},{2,3},{3,2},{4,5},{5,4},{6,7},{7,6},{8,9},{9,8},{10,11... | collective-permute-start | bytes 49160 | tf_op jit(solution)/shard_map/ppermute | solution.py:347
  10.1 3.7 %collective-permute-start.7 = (f32[24,128]{1,0:T(8,128)S(1)}, f32[24,128]{1,0:T(8,128)S(1)}, u32[]{:S(2)}, u32[]{:S(2)}) collective-permute-start(f32[24,128]{1,0:T(8,128)S(1)} %get-tuple-element.19.refs_0_.t0), channel_id=1, source_target_pairs={{0,2},{1,0},{2,1},{3,4},{4,3},{5,6},{6,5},{7,8},{8,7},{9,10},{10,9... | collective-permute-start | bytes 36872 | tf_op jit(solution)/shard_map/ppermute | solution.py:347
  10.6 3.7 %collective-permute-start.6 = (f32[24,128]{1,0:T(8,128)S(1)}, f32[24,128]{1,0:T(8,128)S(1)}, u32[]{:S(2)}, u32[]{:S(2)}) collective-permute-start(f32[24,128]{1,0:T(8,128)S(1)} %get-tuple-element.19.refs_0_.t0), channel_id=1, source_target_pairs={{0,8},{1,9},{2,10},{3,11},{4,12},{5,13},{6,14},{7,15},{8,0},{9,1},... | collective-permute-start | bytes 36872 | tf_op jit(solution)/shard_map/ppermute | solution.py:347
  12.0 3.1 %collective-permute-start.5 = (f32[24,128]{1,0:T(8,128)S(1)}, f32[24,128]{1,0:T(8,128)S(1)}, u32[]{:S(2)}, u32[]{:S(2)}) collective-permute-start(f32[24,128]{1,0:T(8,128)S(1)} %get-tuple-element.19.refs_0_.t0), channel_id=1, source_target_pairs={{0,1},{1,2},{2,3},{3,0},{4,5},{5,4},{6,7},{7,6},{8,16},{9,17},{10,... | collective-permute-start | bytes 36872 | tf_op jit(solution)/shard_map/ppermute | solution.py:347
  12.2 2.9 %collective-permute-start.4 = (f32[24,128]{1,0:T(8,128)S(1)}, f32[24,128]{1,0:T(8,128)S(1)}, u32[]{:S(2)}, u32[]{:S(2)}) collective-permute-start(f32[24,128]{1,0:T(8,128)S(1)} %get-tuple-element.19.refs_0_.t0), channel_id=1, source_target_pairs={{0,1},{1,0},{2,3},{3,2},{4,5},{5,4},{6,7},{7,6},{8,9},{9,8},{10,11... | collective-permute-start | bytes 36872 | tf_op jit(solution)/shard_map/ppermute | solution.py:347
  15.4 9.0 %copy-start = (f32[3,32,512]{2,1,0:T(8,128)S(1)}, f32[3,32,512]{2,1,0:T(8,128)}, u32[]{:S(2)}) copy-start(f32[3,32,512]{2,1,0:T(8,128)} %refs_1_.1) | copy-start | bytes 589828
  15.4 3.4 %collective-permute-start.11 = (f32[24,128]{1,0:T(8,128)S(1)}, f32[24,128]{1,0:T(8,128)S(1)}, u32[]{:S(2)}, u32[]{:S(2)}) collective-permute-start(f32[24,128]{1,0:T(8,128)S(1)} %shard_map.89.refs_0_.t1), channel_id=1, source_target_pairs={{0,2},{1,0},{2,1},{3,4},{4,3},{5,6},{6,5},{7,8},{8,7},{9,10},{10,9... | collective-permute-start | bytes 36872 | tf_op jit(solution)/shard_map/ppermute | solution.py:347
  17.1 3.7 %collective-permute-start.10 = (f32[24,128]{1,0:T(8,128)S(1)}, f32[24,128]{1,0:T(8,128)S(1)}, u32[]{:S(2)}, u32[]{:S(2)}) collective-permute-start(f32[24,128]{1,0:T(8,128)S(1)} %shard_map.89.refs_0_.t1), channel_id=1, source_target_pairs={{0,8},{1,9},{2,10},{3,11},{4,12},{5,13},{6,14},{7,15},{8,0},{9,1},... | collective-permute-start | bytes 36872 | tf_op jit(solution)/shard_map/ppermute | solution.py:347
  18.8 3.1 %collective-permute-start.9 = (f32[24,128]{1,0:T(8,128)S(1)}, f32[24,128]{1,0:T(8,128)S(1)}, u32[]{:S(2)}, u32[]{:S(2)}) collective-permute-start(f32[24,128]{1,0:T(8,128)S(1)} %shard_map.89.refs_0_.t1), channel_id=1, source_target_pairs={{0,1},{1,2},{2,3},{3,0},{4,5},{5,4},{6,7},{7,6},{8,16},{9,17},{10,... | collective-permute-start | bytes 36872 | tf_op jit(solution)/shard_map/ppermute | solution.py:347
  18.8 3.1 %collective-permute-start.8 = (f32[24,128]{1,0:T(8,128)S(1)}, f32[24,128]{1,0:T(8,128)S(1)}, u32[]{:S(2)}, u32[]{:S(2)}) collective-permute-start(f32[24,128]{1,0:T(8,128)S(1)} %shard_map.89.refs_0_.t1), channel_id=1, source_target_pairs={{0,1},{1,0},{2,3},{3,2},{4,5},{5,4},{6,7},{7,6},{8,9},{9,8},{10,11... | collective-permute-start | bytes 36872 | tf_op jit(solution)/shard_map/ppermute | solution.py:347
  22.2 2.8 %collective-permute-start.15 = (f32[24,128]{1,0:T(8,128)S(1)}, f32[24,128]{1,0:T(8,128)S(1)}, u32[]{:S(2)}, u32[]{:S(2)}) collective-permute-start(f32[24,128]{1,0:T(8,128)S(1)} %shard_map.90.t2.refs_0_), channel_id=1, source_target_pairs={{0,2},{1,0},{2,1},{3,4},{4,3},{5,6},{6,5},{7,8},{8,7},{9,10},{10,9... | collective-permute-start | bytes 36872 | tf_op jit(solution)/shard_map/ppermute | solution.py:347
  22.2 3.8 %collective-permute-start.14 = (f32[24,128]{1,0:T(8,128)S(1)}, f32[24,128]{1,0:T(8,128)S(1)}, u32[]{:S(2)}, u32[]{:S(2)}) collective-permute-start(f32[24,128]{1,0:T(8,128)S(1)} %shard_map.90.t2.refs_0_), channel_id=1, source_target_pairs={{0,8},{1,9},{2,10},{3,11},{4,12},{5,13},{6,14},{7,15},{8,0},{9,1},... | collective-permute-start | bytes 36872 | tf_op jit(solution)/shard_map/ppermute | solution.py:347
  24.0 3.1 %collective-permute-start.13 = (f32[24,128]{1,0:T(8,128)S(1)}, f32[24,128]{1,0:T(8,128)S(1)}, u32[]{:S(2)}, u32[]{:S(2)}) collective-permute-start(f32[24,128]{1,0:T(8,128)S(1)} %shard_map.90.t2.refs_0_), channel_id=1, source_target_pairs={{0,1},{1,2},{2,3},{3,0},{4,5},{5,4},{6,7},{7,6},{8,16},{9,17},{10,... | collective-permute-start | bytes 36872 | tf_op jit(solution)/shard_map/ppermute | solution.py:347
  24.0 3.1 %collective-permute-start.12 = (f32[24,128]{1,0:T(8,128)S(1)}, f32[24,128]{1,0:T(8,128)S(1)}, u32[]{:S(2)}, u32[]{:S(2)}) collective-permute-start(f32[24,128]{1,0:T(8,128)S(1)} %shard_map.90.t2.refs_0_), channel_id=1, source_target_pairs={{0,1},{1,0},{2,3},{3,2},{4,5},{5,4},{6,7},{7,6},{8,9},{9,8},{10,11... | collective-permute-start | bytes 36872 | tf_op jit(solution)/shard_map/ppermute | solution.py:347
  27.5 1.2 %collective-permute-start.16 = (f32[24,128]{1,0:T(8,128)S(1)}, f32[24,128]{1,0:T(8,128)S(1)}, u32[]{:S(2)}, u32[]{:S(2)}) collective-permute-start(f32[24,128]{1,0:T(8,128)S(1)} %get-tuple-element.26), channel_id=1, source_target_pairs={{0,1},{1,0},{2,3},{3,2},{4,5},{5,4},{6,7},{7,6},{8,9},{9,8},{10,11... | collective-permute-start | bytes 36872 | tf_op jit(solution)/shard_map/ppermute | solution.py:347
  28.8 4.0 %collective-permute-start.19 = (f32[24,128]{1,0:T(8,128)S(1)}, f32[24,128]{1,0:T(8,128)S(1)}, u32[]{:S(2)}, u32[]{:S(2)}) collective-permute-start(f32[24,128]{1,0:T(8,128)S(1)} %add.21), channel_id=1, source_target_pairs={{0,7},{1,6},{2,5},{3,4},{4,3},{5,2},{6,1},{7,0},{8,15},{9,14},{10,... | collective-permute-start | bytes 36872 | tf_op jit(solution)/shard_map/ppermute | solution.py:347
  29.8 3.1 %collective-permute-start.18 = (f32[24,128]{1,0:T(8,128)S(1)}, f32[24,128]{1,0:T(8,128)S(1)}, u32[]{:S(2)}, u32[]{:S(2)}) collective-permute-start(f32[24,128]{1,0:T(8,128)S(1)} %add.21), channel_id=1, source_target_pairs={{0,5},{1,4},{2,7},{3,6},{4,1},{5,0},{6,3},{7,2},{8,13},{9,12},{10,... | collective-permute-start | bytes 36872 | tf_op jit(solution)/shard_map/ppermute | solution.py:347
  30.3 3.1 %collective-permute-start.17 = (f32[24,128]{1,0:T(8,128)S(1)}, f32[24,128]{1,0:T(8,128)S(1)}, u32[]{:S(2)}, u32[]{:S(2)}) collective-permute-start(f32[24,128]{1,0:T(8,128)S(1)} %add.21), channel_id=1, source_target_pairs={{0,3},{1,2},{2,1},{3,0},{4,7},{5,6},{6,5},{7,4},{8,11},{9,10},{10,... | collective-permute-start | bytes 36872 | tf_op jit(solution)/shard_map/ppermute | solution.py:347
  33.4 4.9 %collective-permute-start.22 = (f32[24,128]{1,0:T(8,128)S(1)}, f32[24,128]{1,0:T(8,128)S(1)}, u32[]{:S(2)}, u32[]{:S(2)}) collective-permute-start(f32[24,128]{1,0:T(8,128)S(1)} %add_add_fusion.1), channel_id=1, source_target_pairs={{0,25},{1,24},{2,27},{3,26},{4,29},{5,28},{6,31},{7,30},{8,17},{9,... | collective-permute-start | bytes 36872 | tf_op jit(solution)/shard_map/ppermute | solution.py:347
  35.5 4.1 %collective-permute-start.21 = (f32[24,128]{1,0:T(8,128)S(1)}, f32[24,128]{1,0:T(8,128)S(1)}, u32[]{:S(2)}, u32[]{:S(2)}) collective-permute-start(f32[24,128]{1,0:T(8,128)S(1)} %add_add_fusion.1), channel_id=1, source_target_pairs={{0,17},{1,16},{2,19},{3,18},{4,21},{5,20},{6,23},{7,22},{8,25},{9,... | collective-permute-start | bytes 36872 | tf_op jit(solution)/shard_map/ppermute | solution.py:347
  35.7 3.9 %collective-permute-start.20 = (f32[24,128]{1,0:T(8,128)S(1)}, f32[24,128]{1,0:T(8,128)S(1)}, u32[]{:S(2)}, u32[]{:S(2)}) collective-permute-start(f32[24,128]{1,0:T(8,128)S(1)} %add_add_fusion.1), channel_id=1, source_target_pairs={{0,9},{1,8},{2,11},{3,10},{4,13},{5,12},{6,15},{7,14},{8,1},{9,0},... | collective-permute-start | bytes 36872 | tf_op jit(solution)/shard_map/ppermute | solution.py:347

commit v15 on v14

--- a/solution.py
+++ b/solution.py
@@ -376,15 +376,15 @@
         return send(value, {d: d ^ (step | 1) for d in range(length)})
 
     value = value + fetched(1)
-    step = 2
-    while step < length:
-        if 2 * step < length:
-            farthest = fetched(3 * step)
-            first, second = fetched(step), fetched(2 * step)
+    step = length // 2
+    while step > 1:
+        if step > 2:
+            farthest = fetched(step | step // 2)
+            first, second = fetched(step // 2), fetched(step)
             value = (value + first) + (second + farthest)
         else:
             value = value + fetched(step)
-        step *= 4
+        step //= 4
     return value
 
 

time: 40.8 us -> 40.7 us (level)
  transfers between devices with their start and end apart: 23 -> 23, of which waited for: 14 -> 13; matrix products, arithmetic and copies ran while one was open for 0% -> 0% of each run, Pallas kernels for 5% -> 5%
where the time goes in v15:
time: 40.7 us; the launch traced here: 40.5 us
  starting transfers between devices  21.3 us (52%)
  waiting for transfers between devices  13 us (32%)
  Pallas kernels  5.41 us (13%)
  between operations  0.72 us (2%)
    ppermute x23, starting transfers between devices, send(): lax.ppermute(value, 'dom', [(d, target[d]) for d in range(lax.axis_size('...  21.3 us
    ppermute x23, waiting for transfers between devices, send(): lax.ppermute(value, 'dom', [(d, target[d]) for d in range(lax.axis_size('...  13 us
    pallas_call x1, Pallas kernels, local(): call(prepare_kernel, [((width, rows), bf16), ((width, rows), bf16), ((8 *...  1.39 us
    pallas_call x1, Pallas kernels, local(): call(start_kernel, [((comps * blocks + 8, 128), f32)], [HBM] * 4, 600000,...  1.08 us
    pallas_call x1, Pallas kernels, local(): call(lambda *refs: finish_kernel(total, *refs), [((comps, S, rows), f32),...  1.02 us
  transfers between devices with their start and end apart: 23, of which 13 were waited for; matrix products, arithmetic and copies ran while one was open for 0% of the time, Pallas kernels for 5%

profile of v15, /device:TPU:0, one launch (start us, length us, event | category | flops | bytes accessed | tf_op | source)
XLA Modules:
  0.0 40.5 jit_solution(15900099610907168759)
XLA Ops:
  0.6 1.1 %shard_map.86.refs_0_ = f32[32,128]{1,0:T(8,128)S(1)} custom-call(f32[3,32,512]{2,1,0:T(8,128)} %refs_1_.1, f32[3,32]{1,0:T(4,128)} %mix_in.1, s32[1,4,8]{2,1,0:T(4,128)} %list_in.1, s32[1,4]{1,0:T(1,128)} %count_in.1), custom_call_target="tpu_custom_call" | custom-call | flops 600000 | bytes 250000 | tf_op jit(solution)/shard_map/pallas_call | solution.py:397
  1.7 3.0 %collective-permute-start.3 = (f32[32,128]{1,0:T(8,128)S(1)}, f32[32,128]{1,0:T(8,128)S(1)}, u32[]{:S(2)}, u32[]{:S(2)}) collective-permute-start(f32[32,128]{1,0:T(8,128)S(1)} %shard_map.86.refs_0_), channel_id=1, source_target_pairs={{0,2},{1,0},{2,1},{3,4},{4,3},{5,6},{6,5},{7,8},{8,7},{9,10},{10,9... | collective-permute-start | bytes 49160 | tf_op jit(solution)/shard_map/ppermute | solution.py:347
  4.7 1.9 %collective-permute-start.2 = (f32[32,128]{1,0:T(8,128)S(1)}, f32[32,128]{1,0:T(8,128)S(1)}, u32[]{:S(2)}, u32[]{:S(2)}) collective-permute-start(f32[32,128]{1,0:T(8,128)S(1)} %shard_map.86.refs_0_), channel_id=1, source_target_pairs={{0,8},{1,9},{2,10},{3,11},{4,12},{5,13},{6,14},{7,15},{8,0},{9,1},... | collective-permute-start | bytes 49160 | tf_op jit(solution)/shard_map/ppermute | solution.py:347
  6.6 0.0 collective-permute-start.1
  6.6 0.0 collective-permute-start
  6.6 1.4 %shard_map.87 = (bf16[256,512]{1,0:T(8,128)(2,1)S(1)}, bf16[256,512]{1,0:T(8,128)(2,1)S(1)}, f32[40,128]{1,0:T(8,128)S(1)}) custom-call(f32[512,256]{1,0:T(8,128)} %strips_in.1, s32[4,8]{1,0:T(4,128)} %bitcast.2, f32[4]{0:T(128)} %shifts_in.1), custom_call_target="tpu_custom_call" | custom-call | flops 1000000 | bytes 1000000 | tf_op jit(solution)/shard_map/pallas_call | solution.py:411
  8.0 0.0 collective-permute-done.3.refs_4_
  8.0 0.5 %collective-permute-done.2.refs_3_ = f32[32,128]{1,0:T(8,128)S(1)} collective-permute-done((f32[32,128]{1,0:T(8,128)S(1)}, f32[32,128]{1,0:T(8,128)S(1)}, u32[]{:S(2)}, u32[]{:S(2)}) %collective-permute-start.2) | collective-permute-done | bytes 16416 | tf_op jit(solution)/shard_map/ppermute | solution.py:347
  8.5 1.3 %collective-permute-done.1.refs_2_ = f32[32,128]{1,0:T(8,128)S(1)} collective-permute-done((f32[32,128]{1,0:T(8,128)S(1)}, f32[32,128]{1,0:T(8,128)S(1)}, u32[]{:S(2)}, u32[]{:S(2)}) %collective-permute-start.1) | collective-permute-done | bytes 16416 | tf_op jit(solution)/shard_map/ppermute | solution.py:347
  9.7 0.0 collective-permute-done.refs_1_
  9.7 0.4 %shard_map.88 = (f32[24,128]{1,0:T(8,128)S(1)}, s32[32,128]{1,0:T(8,128)S(1)}) custom-call(f32[32,128]{1,0:T(8,128)S(1)} %shard_map.86.refs_0_, f32[32,128]{1,0:T(8,128)S(1)} %collective-permute-done.refs_1_, f32[32,128]{1,0:T(8,128)S(1)} %collective-permute-done.1.refs_2_, f32[32,128]{1,0:T(8,128)S(1)} %collective-permute-done.2.refs_3_, ...), custom_call_target="tpu_custom_call" | custom-call | flops 50000000 | bytes 600000 | tf_op jit(solution)/shard_map/pallas_call | solution.py:426
  10.1 0.4 %collective-permute-start.7 = (f32[24,128]{1,0:T(8,128)S(1)}, f32[24,128]{1,0:T(8,128)S(1)}, u32[]{:S(2)}, u32[]{:S(2)}) collective-permute-start(f32[24,128]{1,0:T(8,128)S(1)} %get-tuple-element.19.refs_0_.t0), channel_id=1, source_target_pairs={{0,2},{1,0},{2,1},{3,4},{4,3},{5,6},{6,5},{7,8},{8,7},{9,10},{10,9... | collective-permute-start | bytes 36872 | tf_op jit(solution)/shard_map/ppermute | solution.py:347
  10.6 1.4 %collective-permute-start.6 = (f32[24,128]{1,0:T(8,128)S(1)}, f32[24,128]{1,0:T(8,128)S(1)}, u32[]{:S(2)}, u32[]{:S(2)}) collective-permute-start(f32[24,128]{1,0:T(8,128)S(1)} %get-tuple-element.19.refs_0_.t0), channel_id=1, source_target_pairs={{0,8},{1,9},{2,10},{3,11},{4,12},{5,13},{6,14},{7,15},{8,0},{9,1},... | collective-permute-start | bytes 36872 | tf_op jit(solution)/shard_map/ppermute | solution.py:347
  12.0 0.2 collective-permute-start.5
  12.2 1.7 %collective-permute-start.4 = (f32[24,128]{1,0:T(8,128)S(1)}, f32[24,128]{1,0:T(8,128)S(1)}, u32[]{:S(2)}, u32[]{:S(2)}) collective-permute-start(f32[24,128]{1,0:T(8,128)S(1)} %get-tuple-element.19.refs_0_.t0), channel_id=1, source_target_pairs={{0,1},{1,0},{2,3},{3,2},{4,5},{5,4},{6,7},{7,6},{8,9},{9,8},{10,11... | collective-permute-start | bytes 36872 | tf_op jit(solution)/shard_map/ppermute | solution.py:347
  13.8 0.0 collective-permute-done.7.refs_4_
  13.8 0.4 %collective-permute-done.6.refs_3_ = f32[24,128]{1,0:T(8,128)S(1)} collective-permute-done((f32[24,128]{1,0:T(8,128)S(1)}, f32[24,128]{1,0:T(8,128)S(1)}, u32[]{:S(2)}, u32[]{:S(2)}) %collective-permute-start.6) | collective-permute-done | bytes 12320 | tf_op jit(solution)/shard_map/ppermute | solution.py:347
  14.3 0.9 %collective-permute-done.5.refs_2_ = f32[24,128]{1,0:T(8,128)S(1)} collective-permute-done((f32[24,128]{1,0:T(8,128)S(1)}, f32[24,128]{1,0:T(8,128)S(1)}, u32[]{:S(2)}, u32[]{:S(2)}) %collective-permute-start.5) | collective-permute-done | bytes 12320 | tf_op jit(solution)/shard_map/ppermute | solution.py:347
  15.1 0.0 collective-permute-done.4.refs_1_
  15.1 0.3 shard_map.89.refs_0_.t1
  15.4 0.0 copy-start
  15.4 1.7 %collective-permute-start.11 = (f32[24,128]{1,0:T(8,128)S(1)}, f32[24,128]{1,0:T(8,128)S(1)}, u32[]{:S(2)}, u32[]{:S(2)}) collective-permute-start(f32[24,128]{1,0:T(8,128)S(1)} %shard_map.89.refs_0_.t1), channel_id=1, source_target_pairs={{0,2},{1,0},{2,1},{3,4},{4,3},{5,6},{6,5},{7,8},{8,7},{9,10},{10,9... | collective-permute-start | bytes 36872 | tf_op jit(solution)/shard_map/ppermute | solution.py:347
  17.1 1.6 %collective-permute-start.10 = (f32[24,128]{1,0:T(8,128)S(1)}, f32[24,128]{1,0:T(8,128)S(1)}, u32[]{:S(2)}, u32[]{:S(2)}) collective-permute-start(f32[24,128]{1,0:T(8,128)S(1)} %shard_map.89.refs_0_.t1), channel_id=1, source_target_pairs={{0,8},{1,9},{2,10},{3,11},{4,12},{5,13},{6,14},{7,15},{8,0},{9,1},... | collective-permute-start | bytes 36872 | tf_op jit(solution)/shard_map/ppermute | solution.py:347
  18.8 0.0 collective-permute-start.9
  18.8 0.0 collective-permute-start.8
  18.8 0.0 collective-permute-done.11.refs_4_
  18.8 2.0 %collective-permute-done.10.refs_3_ = f32[24,128]{1,0:T(8,128)S(1)} collective-permute-done((f32[24,128]{1,0:T(8,128)S(1)}, f32[24,128]{1,0:T(8,128)S(1)}, u32[]{:S(2)}, u32[]{:S(2)}) %collective-permute-start.10) | collective-permute-done | bytes 12320 | tf_op jit(solution)/shard_map/ppermute | solution.py:347
  20.8 1.1 %collective-permute-done.9.refs_2_ = f32[24,128]{1,0:T(8,128)S(1)} collective-permute-done((f32[24,128]{1,0:T(8,128)S(1)}, f32[24,128]{1,0:T(8,128)S(1)}, u32[]{:S(2)}, u32[]{:S(2)}) %collective-permute-start.9) | collective-permute-done | bytes 12320 | tf_op jit(solution)/shard_map/ppermute | solution.py:347
  21.9 0.0 collective-permute-done.8.refs_1_
  21.9 0.3 shard_map.90.t2.refs_0_
  22.2 0.0 collective-permute-start.15
  22.2 1.8 %collective-permute-start.14 = (f32[24,128]{1,0:T(8,128)S(1)}, f32[24,128]{1,0:T(8,128)S(1)}, u32[]{:S(2)}, u32[]{:S(2)}) collective-permute-start(f32[24,128]{1,0:T(8,128)S(1)} %shard_map.90.t2.refs_0_), channel_id=1, source_target_pairs={{0,8},{1,9},{2,10},{3,11},{4,12},{5,13},{6,14},{7,15},{8,0},{9,1},... | collective-permute-start | bytes 36872 | tf_op jit(solution)/shard_map/ppermute | solution.py:347
  24.0 0.0 collective-permute-start.13
  24.0 0.4 collective-permute-start.12
  24.4 0.0 copy-done
  24.4 0.6 %shard_map.91 = (f32[24,512]{1,0:T(8,128)S(1)}, f32[24,128]{1,0:T(8,128)S(1)}, bf16[512,128]{1,0:T(8,128)(2,1)S(1)}, bf16[512,128]{1,0:T(8,128)(2,1)S(1)}, bf16[512,128]{1,0:T(8,128)(2,1)S(1)}) custom-call(f32[3,32,512]{2,1,0:T(8,128)S(1)} %copy-done, f32[24,128]{1,0:T(8,128)S(1)} %get-tuple-element.19.refs_0_.t0, f32[24,128]{1,0:T(8,128)S(1)} %shard_map.89.refs_0_.t1, ...), custom_call_target="tpu_custom_call" | custom-call | flops 60000000 | bytes 250000 | tf_op jit(solution)/shard_map/pallas_call | solution.py:441
  25.0 0.0 collective-permute-done.15.refs_4_
  25.0 0.9 %collective-permute-done.14.refs_3_ = f32[24,128]{1,0:T(8,128)S(1)} collective-permute-done((f32[24,128]{1,0:T(8,128)S(1)}, f32[24,128]{1,0:T(8,128)S(1)}, u32[]{:S(2)}, u32[]{:S(2)}) %collective-permute-start.14) | collective-permute-done | bytes 12320 | tf_op jit(solution)/shard_map/ppermute | solution.py:347
  25.9 1.2 %collective-permute-done.13.refs_2_ = f32[24,128]{1,0:T(8,128)S(1)} collective-permute-done((f32[24,128]{1,0:T(8,128)S(1)}, f32[24,128]{1,0:T(8,128)S(1)}, u32[]{:S(2)}, u32[]{:S(2)}) %collective-permute-start.13) | collective-permute-done | bytes 12320 | tf_op jit(solution)/shard_map/ppermute | solution.py:347
  27.1 0.0 collective-permute-done.12.refs_1_
  27.1 0.4 shard_map.92
  27.5 0.1 collective-permute-start.16
  27.6 1.2 %collective-permute-done.16 = f32[24,128]{1,0:T(8,128)S(1)} collective-permute-done((f32[24,128]{1,0:T(8,128)S(1)}, f32[24,128]{1,0:T(8,128)S(1)}, u32[]{:S(2)}, u32[]{:S(2)}) %collective-permute-start.16) | collective-permute-done | bytes 12320 | tf_op jit(solution)/shard_map/ppermute | solution.py:347
  28.8 1.6 %collective-permute-start.19 = (f32[24,128]{1,0:T(8,128)S(1)}, f32[24,128]{1,0:T(8,128)S(1)}, u32[]{:S(2)}, u32[]{:S(2)}) collective-permute-start(f32[24,128]{1,0:T(8,128)S(1)} %add.21), channel_id=1, source_target_pairs={{0,25},{1,24},{2,27},{3,26},{4,29},{5,28},{6,31},{7,30},{8,17},{9,... | collective-permute-start | bytes 36872 | tf_op jit(solution)/shard_map/ppermute | solution.py:347
  30.3 0.6 %collective-permute-start.18 = (f32[24,128]{1,0:T(8,128)S(1)}, f32[24,128]{1,0:T(8,128)S(1)}, u32[]{:S(2)}, u32[]{:S(2)}) collective-permute-start(f32[24,128]{1,0:T(8,128)S(1)} %add.21), channel_id=1, source_target_pairs={{0,17},{1,16},{2,19},{3,18},{4,21},{5,20},{6,23},{7,22},{8,25},{9,... | collective-permute-start | bytes 36872 | tf_op jit(solution)/shard_map/ppermute | solution.py:347
  30.9 1.8 %collective-permute-start.17 = (f32[24,128]{1,0:T(8,128)S(1)}, f32[24,128]{1,0:T(8,128)S(1)}, u32[]{:S(2)}, u32[]{:S(2)}) collective-permute-start(f32[24,128]{1,0:T(8,128)S(1)} %add.21), channel_id=1, source_target_pairs={{0,9},{1,8},{2,11},{3,10},{4,13},{5,12},{6,15},{7,14},{8,1},{9,0},... | collective-permute-start | bytes 36872 | tf_op jit(solution)/shard_map/ppermute | solution.py:347
  32.7 1.0 %collective-permute-done.19 = f32[24,128]{1,0:T(8,128)S(1)} collective-permute-done((f32[24,128]{1,0:T(8,128)S(1)}, f32[24,128]{1,0:T(8,128)S(1)}, u32[]{:S(2)}, u32[]{:S(2)}) %collective-permute-start.19) | collective-permute-done | bytes 12320 | tf_op jit(solution)/shard_map/ppermute | solution.py:347
  33.7 0.7 %collective-permute-done.18 = f32[24,128]{1,0:T(8,128)S(1)} collective-permute-done((f32[24,128]{1,0:T(8,128)S(1)}, f32[24,128]{1,0:T(8,128)S(1)}, u32[]{:S(2)}, u32[]{:S(2)}) %collective-permute-start.18) | collective-permute-done | bytes 12320 | tf_op jit(solution)/shard_map/ppermute | solution.py:347
  34.4 0.0 collective-permute-done.17
  34.4 2.0 %collective-permute-start.22 = (f32[24,128]{1,0:T(8,128)S(1)}, f32[24,128]{1,0:T(8,128)S(1)}, u32[]{:S(2)}, u32[]{:S(2)}) collective-permute-start(f32[24,128]{1,0:T(8,128)S(1)} %add_add_fusion.1), channel_id=1, source_target_pairs={{0,7},{1,6},{2,5},{3,4},{4,3},{5,2},{6,1},{7,0},{8,15},{9,14},{10,... | collective-permute-start | bytes 36872 | tf_op jit(solution)/shard_map/ppermute | solution.py:347
  36.4 0.0 collective-permute-start.21
  36.4 1.2 %collective-permute-start.20 = (f32[24,128]{1,0:T(8,128)S(1)}, f32[24,128]{1,0:T(8,128)S(1)}, u32[]{:S(2)}, u32[]{:S(2)}) collective-permute-start(f32[24,128]{1,0:T(8,128)S(1)} %add_add_fusion.1), channel_id=1, source_target_pairs={{0,3},{1,2},{2,1},{3,0},{4,7},{5,6},{6,5},{7,4},{8,11},{9,10},{10,... | collective-permute-start | bytes 36872 | tf_op jit(solution)/shard_map/ppermute | solution.py:347
  37.6 0.8 %collective-permute-done.22 = f32[24,128]{1,0:T(8,128)S(1)} collective-permute-done((f32[24,128]{1,0:T(8,128)S(1)}, f32[24,128]{1,0:T(8,128)S(1)}, u32[]{:S(2)}, u32[]{:S(2)}) %collective-permute-start.22) | collective-permute-done | bytes 12320 | tf_op jit(solution)/shard_map/ppermute | solution.py:347
  38.5 1.0 %collective-permute-done.21 = f32[24,128]{1,0:T(8,128)S(1)} collective-permute-done((f32[24,128]{1,0:T(8,128)S(1)}, f32[24,128]{1,0:T(8,128)S(1)}, u32[]{:S(2)}, u32[]{:S(2)}) %collective-permute-start.21) | collective-permute-done | bytes 12320 | tf_op jit(solution)/shard_map/ppermute | solution.py:347
  39.5 0.0 collective-permute-done.20
  39.5 1.0 %shard_map.93 = (f32[3,4,512]{2,1,0:T(4,128)}, f32[3,4,36]{2,1,0:T(4,128)}) custom-call(f32[24,128]{1,0:T(8,128)S(1)} %add_add_fusion.refs_0_, f32[3,32,512]{2,1,0:T(8,128)S(1)} %copy-done, f32[24,512]{1,0:T(8,128)S(1)} %get-tuple-element.25.refs_13_.refs_2_, f32[8,512]{1,0:T(8,128)S(1)} %get-tuple-element.27.refs_3_), custom_call_target="tpu_custom_call" | custom-call | flops 50000000 | bytes 400000 | tf_op jit(solution)/shard_map/pallas_call | solution.py:456
  (3 shorter events, 0.0 us)
Async XLA Ops:
  1.7 6.3 %collective-permute-start.3 = (f32[32,128]{1,0:T(8,128)S(1)}, f32[32,128]{1,0:T(8,128)S(1)}, u32[]{:S(2)}, u32[]{:S(2)}) collective-permute-start(f32[32,128]{1,0:T(8,128)S(1)} %shard_map.86.refs_0_), channel_id=1, source_target_pairs={{0,2},{1,0},{2,1},{3,4},{4,3},{5,6},{6,5},{7,8},{8,7},{9,10},{10,9... | collective-permute-start | bytes 49160 | tf_op jit(solution)/shard_map/ppermute | solution.py:347
  4.7 3.7 %collective-permute-start.2 = (f32[32,128]{1,0:T(8,128)S(1)}, f32[32,128]{1,0:T(8,128)S(1)}, u32[]{:S(2)}, u32[]{:S(2)}) collective-permute-start(f32[32,128]{1,0:T(8,128)S(1)} %shard_map.86.refs_0_), channel_id=1, source_target_pairs={{0,8},{1,9},{2,10},{3,11},{4,12},{5,13},{6,14},{7,15},{8,0},{9,1},... | collective-permute-start | bytes 49160 | tf_op jit(solution)/shard_map/ppermute | solution.py:347
  6.6 3.2 %collective-permute-start.1 = (f32[32,128]{1,0:T(8,128)S(1)}, f32[32,128]{1,0:T(8,128)S(1)}, u32[]{:S(2)}, u32[]{:S(2)}) collective-permute-start(f32[32,128]{1,0:T(8,128)S(1)} %shard_map.86.refs_0_), channel_id=1, source_target_pairs={{0,1},{1,2},{2,3},{3,0},{4,5},{5,4},{6,7},{7,6},{8,16},{9,17},{10,... | collective-permute-start | bytes 49160 | tf_op jit(solution)/shard_map/ppermute | solution.py:347
  6.6 3.2 %collective-permute-start = (f32[32,128]{1,0:T(8,128)S(1)}, f32[32,128]{1,0:T(8,128)S(1)}, u32[]{:S(2)}, u32[]{:S(2)}) collective-permute-start(f32[32,128]{1,0:T(8,128)S(1)} %shard_map.86.refs_0_), channel_id=1, source_target_pairs={{0,1},{1,0},{2,3},{3,2},{4,5},{5,4},{6,7},{7,6},{8,9},{9,8},{10,11... | collective-permute-start | bytes 49160 | tf_op jit(solution)/shard_map/ppermute | solution.py:347
  10.1 3.7 %collective-permute-start.7 = (f32[24,128]{1,0:T(8,128)S(1)}, f32[24,128]{1,0:T(8,128)S(1)}, u32[]{:S(2)}, u32[]{:S(2)}) collective-permute-start(f32[24,128]{1,0:T(8,128)S(1)} %get-tuple-element.19.refs_0_.t0), channel_id=1, source_target_pairs={{0,2},{1,0},{2,1},{3,4},{4,3},{5,6},{6,5},{7,8},{8,7},{9,10},{10,9... | collective-permute-start | bytes 36872 | tf_op jit(solution)/shard_map/ppermute | solution.py:347
  10.6 3.7 %collective-permute-start.6 = (f32[24,128]{1,0:T(8,128)S(1)}, f32[24,128]{1,0:T(8,128)S(1)}, u32[]{:S(2)}, u32[]{:S(2)}) collective-permute-start(f32[24,128]{1,0:T(8,128)S(1)} %get-tuple-element.19.refs_0_.t0), channel_id=1, source_target_pairs={{0,8},{1,9},{2,10},{3,11},{4,12},{5,13},{6,14},{7,15},{8,0},{9,1},... | collective-permute-start | bytes 36872 | tf_op jit(solution)/shard_map/ppermute | solution.py:347
  12.0 3.1 %collective-permute-start.5 = (f32[24,128]{1,0:T(8,128)S(1)}, f32[24,128]{1,0:T(8,128)S(1)}, u32[]{:S(2)}, u32[]{:S(2)}) collective-permute-start(f32[24,128]{1,0:T(8,128)S(1)} %get-tuple-element.19.refs_0_.t0), channel_id=1, source_target_pairs={{0,1},{1,2},{2,3},{3,0},{4,5},{5,4},{6,7},{7,6},{8,16},{9,17},{10,... | collective-permute-start | bytes 36872 | tf_op jit(solution)/shard_map/ppermute | solution.py:347
  12.2 2.9 %collective-permute-start.4 = (f32[24,128]{1,0:T(8,128)S(1)}, f32[24,128]{1,0:T(8,128)S(1)}, u32[]{:S(2)}, u32[]{:S(2)}) collective-permute-start(f32[24,128]{1,0:T(8,128)S(1)} %get-tuple-element.19.refs_0_.t0), channel_id=1, source_target_pairs={{0,1},{1,0},{2,3},{3,2},{4,5},{5,4},{6,7},{7,6},{8,9},{9,8},{10,11... | collective-permute-start | bytes 36872 | tf_op jit(solution)/shard_map/ppermute | solution.py:347
  15.4 9.0 %copy-start = (f32[3,32,512]{2,1,0:T(8,128)S(1)}, f32[3,32,512]{2,1,0:T(8,128)}, u32[]{:S(2)}) copy-start(f32[3,32,512]{2,1,0:T(8,128)} %refs_1_.1) | copy-start | bytes 589828
  15.4 3.4 %collective-permute-start.11 = (f32[24,128]{1,0:T(8,128)S(1)}, f32[24,128]{1,0:T(8,128)S(1)}, u32[]{:S(2)}, u32[]{:S(2)}) collective-permute-start(f32[24,128]{1,0:T(8,128)S(1)} %shard_map.89.refs_0_.t1), channel_id=1, source_target_pairs={{0,2},{1,0},{2,1},{3,4},{4,3},{5,6},{6,5},{7,8},{8,7},{9,10},{10,9... | collective-permute-start | bytes 36872 | tf_op jit(solution)/shard_map/ppermute | solution.py:347
  17.1 3.7 %collective-permute-start.10 = (f32[24,128]{1,0:T(8,128)S(1)}, f32[24,128]{1,0:T(8,128)S(1)}, u32[]{:S(2)}, u32[]{:S(2)}) collective-permute-start(f32[24,128]{1,0:T(8,128)S(1)} %shard_map.89.refs_0_.t1), channel_id=1, source_target_pairs={{0,8},{1,9},{2,10},{3,11},{4,12},{5,13},{6,14},{7,15},{8,0},{9,1},... | collective-permute-start | bytes 36872 | tf_op jit(solution)/shard_map/ppermute | solution.py:347
  18.8 3.1 %collective-permute-start.9 = (f32[24,128]{1,0:T(8,128)S(1)}, f32[24,128]{1,0:T(8,128)S(1)}, u32[]{:S(2)}, u32[]{:S(2)}) collective-permute-start(f32[24,128]{1,0:T(8,128)S(1)} %shard_map.89.refs_0_.t1), channel_id=1, source_target_pairs={{0,1},{1,2},{2,3},{3,0},{4,5},{5,4},{6,7},{7,6},{8,16},{9,17},{10,... | collective-permute-start | bytes 36872 | tf_op jit(solution)/shard_map/ppermute | solution.py:347
  18.8 3.1 %collective-permute-start.8 = (f32[24,128]{1,0:T(8,128)S(1)}, f32[24,128]{1,0:T(8,128)S(1)}, u32[]{:S(2)}, u32[]{:S(2)}) collective-permute-start(f32[24,128]{1,0:T(8,128)S(1)} %shard_map.89.refs_0_.t1), channel_id=1, source_target_pairs={{0,1},{1,0},{2,3},{3,2},{4,5},{5,4},{6,7},{7,6},{8,9},{9,8},{10,11... | collective-permute-start | bytes 36872 | tf_op jit(solution)/shard_map/ppermute | solution.py:347
  22.2 2.8 %collective-permute-start.15 = (f32[24,128]{1,0:T(8,128)S(1)}, f32[24,128]{1,0:T(8,128)S(1)}, u32[]{:S(2)}, u32[]{:S(2)}) collective-permute-start(f32[24,128]{1,0:T(8,128)S(1)} %shard_map.90.t2.refs_0_), channel_id=1, source_target_pairs={{0,2},{1,0},{2,1},{3,4},{4,3},{5,6},{6,5},{7,8},{8,7},{9,10},{10,9... | collective-permute-start | bytes 36872 | tf_op jit(solution)/shard_map/ppermute | solution.py:347
  22.2 3.8 %collective-permute-start.14 = (f32[24,128]{1,0:T(8,128)S(1)}, f32[24,128]{1,0:T(8,128)S(1)}, u32[]{:S(2)}, u32[]{:S(2)}) collective-permute-start(f32[24,128]{1,0:T(8,128)S(1)} %shard_map.90.t2.refs_0_), channel_id=1, source_target_pairs={{0,8},{1,9},{2,10},{3,11},{4,12},{5,13},{6,14},{7,15},{8,0},{9,1},... | collective-permute-start | bytes 36872 | tf_op jit(solution)/shard_map/ppermute | solution.py:347
  24.0 3.1 %collective-permute-start.13 = (f32[24,128]{1,0:T(8,128)S(1)}, f32[24,128]{1,0:T(8,128)S(1)}, u32[]{:S(2)}, u32[]{:S(2)}) collective-permute-start(f32[24,128]{1,0:T(8,128)S(1)} %shard_map.90.t2.refs_0_), channel_id=1, source_target_pairs={{0,1},{1,2},{2,3},{3,0},{4,5},{5,4},{6,7},{7,6},{8,16},{9,17},{10,... | collective-permute-start | bytes 36872 | tf_op jit(solution)/shard_map/ppermute | solution.py:347
  24.0 3.1 %collective-permute-start.12 = (f32[24,128]{1,0:T(8,128)S(1)}, f32[24,128]{1,0:T(8,128)S(1)}, u32[]{:S(2)}, u32[]{:S(2)}) collective-permute-start(f32[24,128]{1,0:T(8,128)S(1)} %shard_map.90.t2.refs_0_), channel_id=1, source_target_pairs={{0,1},{1,0},{2,3},{3,2},{4,5},{5,4},{6,7},{7,6},{8,9},{9,8},{10,11... | collective-permute-start | bytes 36872 | tf_op jit(solution)/shard_map/ppermute | solution.py:347
  27.5 1.2 %collective-permute-start.16 = (f32[24,128]{1,0:T(8,128)S(1)}, f32[24,128]{1,0:T(8,128)S(1)}, u32[]{:S(2)}, u32[]{:S(2)}) collective-permute-start(f32[24,128]{1,0:T(8,128)S(1)} %get-tuple-element.26), channel_id=1, source_target_pairs={{0,1},{1,0},{2,3},{3,2},{4,5},{5,4},{6,7},{7,6},{8,9},{9,8},{10,11... | collective-permute-start | bytes 36872 | tf_op jit(solution)/shard_map/ppermute | solution.py:347
  28.8 4.9 %collective-permute-start.19 = (f32[24,128]{1,0:T(8,128)S(1)}, f32[24,128]{1,0:T(8,128)S(1)}, u32[]{:S(2)}, u32[]{:S(2)}) collective-permute-start(f32[24,128]{1,0:T(8,128)S(1)} %add.21), channel_id=1, source_target_pairs={{0,25},{1,24},{2,27},{3,26},{4,29},{5,28},{6,31},{7,30},{8,17},{9,... | collective-permute-start | bytes 36872 | tf_op jit(solution)/shard_map/ppermute | solution.py:347
  30.3 4.0 %collective-permute-start.18 = (f32[24,128]{1,0:T(8,128)S(1)}, f32[24,128]{1,0:T(8,128)S(1)}, u32[]{:S(2)}, u32[]{:S(2)}) collective-permute-start(f32[24,128]{1,0:T(8,128)S(1)} %add.21), channel_id=1, source_target_pairs={{0,17},{1,16},{2,19},{3,18},{4,21},{5,20},{6,23},{7,22},{8,25},{9,... | collective-permute-start | bytes 36872 | tf_op jit(solution)/shard_map/ppermute | solution.py:347
  30.9 3.5 %collective-permute-start.17 = (f32[24,128]{1,0:T(8,128)S(1)}, f32[24,128]{1,0:T(8,128)S(1)}, u32[]{:S(2)}, u32[]{:S(2)}) collective-permute-start(f32[24,128]{1,0:T(8,128)S(1)} %add.21), channel_id=1, source_target_pairs={{0,9},{1,8},{2,11},{3,10},{4,13},{5,12},{6,15},{7,14},{8,1},{9,0},... | collective-permute-start | bytes 36872 | tf_op jit(solution)/shard_map/ppermute | solution.py:347
  34.4 4.1 %collective-permute-start.22 = (f32[24,128]{1,0:T(8,128)S(1)}, f32[24,128]{1,0:T(8,128)S(1)}, u32[]{:S(2)}, u32[]{:S(2)}) collective-permute-start(f32[24,128]{1,0:T(8,128)S(1)} %add_add_fusion.1), channel_id=1, source_target_pairs={{0,7},{1,6},{2,5},{3,4},{4,3},{5,2},{6,1},{7,0},{8,15},{9,14},{10,... | collective-permute-start | bytes 36872 | tf_op jit(solution)/shard_map/ppermute | solution.py:347
  36.4 3.1 %collective-permute-start.21 = (f32[24,128]{1,0:T(8,128)S(1)}, f32[24,128]{1,0:T(8,128)S(1)}, u32[]{:S(2)}, u32[]{:S(2)}) collective-permute-start(f32[24,128]{1,0:T(8,128)S(1)} %add_add_fusion.1), channel_id=1, source_target_pairs={{0,5},{1,4},{2,7},{3,6},{4,1},{5,0},{6,3},{7,2},{8,13},{9,12},{10,... | collective-permute-start | bytes 36872 | tf_op jit(solution)/shard_map/ppermute | solution.py:347
  36.4 3.1 %collective-permute-start.20 = (f32[24,128]{1,0:T(8,128)S(1)}, f32[24,128]{1,0:T(8,128)S(1)}, u32[]{:S(2)}, u32[]{:S(2)}) collective-permute-start(f32[24,128]{1,0:T(8,128)S(1)} %add_add_fusion.1), channel_id=1, source_target_pairs={{0,3},{1,2},{2,1},{3,0},{4,7},{5,6},{6,5},{7,4},{8,11},{9,10},{10,... | collective-permute-start | bytes 36872 | tf_op jit(solution)/shard_map/ppermute | solution.py:347

commit v16 on v14

--- a/solution.py
+++ b/solution.py
@@ -154,7 +154,7 @@
     lane = iota((8, 128), 1).astype(jnp.float32)
     at = [
         jnp.sum(jnp.where(lane == table[:, k : k + 1], target, 0.0), axis=1, keepdims=True)
-        for k in range(4)
+        for k in range(1, 4)
     ]
     return jnp.concatenate([jnp.broadcast_to(x, (8, 128)) for x in at], axis=0).astype(jnp.int32)
 
@@ -162,8 +162,8 @@
 def product(choose, pieces, high, low):
     rows = 8 * COMPS
     front = iota((8, 128), 1) < BLOCK
-    picked = []
-    for k in range(4):
+    picked = [[pieces[0][8 * c : 8 * c + 8] for c in range(COMPS)]]
+    for k in range(3):
         code = choose[8 * k : 8 * k + 8]
         index, place = code & 7, code >> 3
         blocks = []
@@ -425,7 +425,7 @@
     length = lax.axis_size("dom")
     tile, choose = call(
         lambda *refs: first_kernel(length, *refs),
-        [tile_out, ((4 * blocks, 128), jnp.int32)],
+        [tile_out, ((3 * blocks, 128), jnp.int32)],
         [VMEM] * 8,
         50000000,
         600000,

time: 40.8 us -> 40.8 us (level)
  no operation moved by 1% of the time
where the time goes in v16:
time: 40.8 us; the launch traced here: 40.6 us
  starting transfers between devices  21.1 us (52%)
  waiting for transfers between devices  13.4 us (33%)
  Pallas kernels  5.4 us (13%)
  between operations  0.72 us (2%)
    ppermute x23, starting transfers between devices, send(): lax.ppermute(value, 'dom', [(d, target[d]) for d in range(lax.axis_size('...  21.1 us
    ppermute x23, waiting for transfers between devices, send(): lax.ppermute(value, 'dom', [(d, target[d]) for d in range(lax.axis_size('...  13.4 us
    pallas_call x1, Pallas kernels, local(): call(prepare_kernel, [((width, rows), bf16), ((width, rows), bf16), ((8 *...  1.39 us
    pallas_call x1, Pallas kernels, local(): call(start_kernel, [((comps * blocks + 8, 128), f32)], [HBM] * 4, 600000,...  1.08 us
    pallas_call x1, Pallas kernels, local(): call(lambda *refs: finish_kernel(total, *refs), [((comps, S, rows), f32),...  1.02 us
  transfers between devices with their start and end apart: 23, of which 14 were waited for; matrix products, arithmetic and copies ran while one was open for 0% of the time, Pallas kernels for 5%

profile of v16, /device:TPU:0, one launch (start us, length us, event | category | flops | bytes accessed | tf_op | source)
XLA Modules:
  0.0 40.6 jit_solution(17948236491784637272)
XLA Ops:
  0.6 1.1 %shard_map.86.refs_0_ = f32[32,128]{1,0:T(8,128)S(1)} custom-call(f32[3,32,512]{2,1,0:T(8,128)} %refs_1_.1, f32[3,32]{1,0:T(4,128)} %mix_in.1, s32[1,4,8]{2,1,0:T(4,128)} %list_in.1, s32[1,4]{1,0:T(1,128)} %count_in.1), custom_call_target="tpu_custom_call" | custom-call | flops 600000 | bytes 250000 | tf_op jit(solution)/shard_map/pallas_call | solution.py:397
  1.7 3.0 %collective-permute-start.3 = (f32[32,128]{1,0:T(8,128)S(1)}, f32[32,128]{1,0:T(8,128)S(1)}, u32[]{:S(2)}, u32[]{:S(2)}) collective-permute-start(f32[32,128]{1,0:T(8,128)S(1)} %shard_map.86.refs_0_), channel_id=1, source_target_pairs={{0,2},{1,0},{2,1},{3,4},{4,3},{5,6},{6,5},{7,8},{8,7},{9,10},{10,9... | collective-permute-start | bytes 49160 | tf_op jit(solution)/shard_map/ppermute | solution.py:347
  4.7 1.9 %collective-permute-start.2 = (f32[32,128]{1,0:T(8,128)S(1)}, f32[32,128]{1,0:T(8,128)S(1)}, u32[]{:S(2)}, u32[]{:S(2)}) collective-permute-start(f32[32,128]{1,0:T(8,128)S(1)} %shard_map.86.refs_0_), channel_id=1, source_target_pairs={{0,8},{1,9},{2,10},{3,11},{4,12},{5,13},{6,14},{7,15},{8,0},{9,1},... | collective-permute-start | bytes 49160 | tf_op jit(solution)/shard_map/ppermute | solution.py:347
  6.6 0.0 collective-permute-start.1
  6.6 0.0 collective-permute-start
  6.6 1.4 %shard_map.87 = (bf16[256,512]{1,0:T(8,128)(2,1)S(1)}, bf16[256,512]{1,0:T(8,128)(2,1)S(1)}, f32[40,128]{1,0:T(8,128)S(1)}) custom-call(f32[512,256]{1,0:T(8,128)} %strips_in.1, s32[4,8]{1,0:T(4,128)} %bitcast.2, f32[4]{0:T(128)} %shifts_in.1), custom_call_target="tpu_custom_call" | custom-call | flops 1000000 | bytes 1000000 | tf_op jit(solution)/shard_map/pallas_call | solution.py:411
  8.0 0.0 collective-permute-done.3.refs_4_
  8.0 0.5 %collective-permute-done.2.refs_3_ = f32[32,128]{1,0:T(8,128)S(1)} collective-permute-done((f32[32,128]{1,0:T(8,128)S(1)}, f32[32,128]{1,0:T(8,128)S(1)}, u32[]{:S(2)}, u32[]{:S(2)}) %collective-permute-start.2) | collective-permute-done | bytes 16416 | tf_op jit(solution)/shard_map/ppermute | solution.py:347
  8.5 1.3 %collective-permute-done.1.refs_2_ = f32[32,128]{1,0:T(8,128)S(1)} collective-permute-done((f32[32,128]{1,0:T(8,128)S(1)}, f32[32,128]{1,0:T(8,128)S(1)}, u32[]{:S(2)}, u32[]{:S(2)}) %collective-permute-start.1) | collective-permute-done | bytes 16416 | tf_op jit(solution)/shard_map/ppermute | solution.py:347
  9.7 0.0 collective-permute-done.refs_1_
  9.7 0.4 shard_map.88
  10.1 0.4 %collective-permute-start.7 = (f32[24,128]{1,0:T(8,128)S(1)}, f32[24,128]{1,0:T(8,128)S(1)}, u32[]{:S(2)}, u32[]{:S(2)}) collective-permute-start(f32[24,128]{1,0:T(8,128)S(1)} %get-tuple-element.19.refs_0_.t0), channel_id=1, source_target_pairs={{0,2},{1,0},{2,1},{3,4},{4,3},{5,6},{6,5},{7,8},{8,7},{9,10},{10,9... | collective-permute-start | bytes 36872 | tf_op jit(solution)/shard_map/ppermute | solution.py:347
  10.6 1.4 %collective-permute-start.6 = (f32[24,128]{1,0:T(8,128)S(1)}, f32[24,128]{1,0:T(8,128)S(1)}, u32[]{:S(2)}, u32[]{:S(2)}) collective-permute-start(f32[24,128]{1,0:T(8,128)S(1)} %get-tuple-element.19.refs_0_.t0), channel_id=1, source_target_pairs={{0,8},{1,9},{2,10},{3,11},{4,12},{5,13},{6,14},{7,15},{8,0},{9,1},... | collective-permute-start | bytes 36872 | tf_op jit(solution)/shard_map/ppermute | solution.py:347
  12.0 0.2 collective-permute-start.5
  12.2 1.7 %collective-permute-start.4 = (f32[24,128]{1,0:T(8,128)S(1)}, f32[24,128]{1,0:T(8,128)S(1)}, u32[]{:S(2)}, u32[]{:S(2)}) collective-permute-start(f32[24,128]{1,0:T(8,128)S(1)} %get-tuple-element.19.refs_0_.t0), channel_id=1, source_target_pairs={{0,1},{1,0},{2,3},{3,2},{4,5},{5,4},{6,7},{7,6},{8,9},{9,8},{10,11... | collective-permute-start | bytes 36872 | tf_op jit(solution)/shard_map/ppermute | solution.py:347
  13.8 0.0 collective-permute-done.7.refs_4_
  13.8 0.4 %collective-permute-done.6.refs_3_ = f32[24,128]{1,0:T(8,128)S(1)} collective-permute-done((f32[24,128]{1,0:T(8,128)S(1)}, f32[24,128]{1,0:T(8,128)S(1)}, u32[]{:S(2)}, u32[]{:S(2)}) %collective-permute-start.6) | collective-permute-done | bytes 12320 | tf_op jit(solution)/shard_map/ppermute | solution.py:347
  14.3 0.9 %collective-permute-done.5.refs_2_ = f32[24,128]{1,0:T(8,128)S(1)} collective-permute-done((f32[24,128]{1,0:T(8,128)S(1)}, f32[24,128]{1,0:T(8,128)S(1)}, u32[]{:S(2)}, u32[]{:S(2)}) %collective-permute-start.5) | collective-permute-done | bytes 12320 | tf_op jit(solution)/shard_map/ppermute | solution.py:347
  15.1 0.0 collective-permute-done.4.refs_1_
  15.1 0.3 shard_map.89.refs_0_.t1
  15.4 0.0 copy-start
  15.4 1.7 %collective-permute-start.11 = (f32[24,128]{1,0:T(8,128)S(1)}, f32[24,128]{1,0:T(8,128)S(1)}, u32[]{:S(2)}, u32[]{:S(2)}) collective-permute-start(f32[24,128]{1,0:T(8,128)S(1)} %shard_map.89.refs_0_.t1), channel_id=1, source_target_pairs={{0,2},{1,0},{2,1},{3,4},{4,3},{5,6},{6,5},{7,8},{8,7},{9,10},{10,9... | collective-permute-start | bytes 36872 | tf_op jit(solution)/shard_map/ppermute | solution.py:347
  17.1 1.6 %collective-permute-start.10 = (f32[24,128]{1,0:T(8,128)S(1)}, f32[24,128]{1,0:T(8,128)S(1)}, u32[]{:S(2)}, u32[]{:S(2)}) collective-permute-start(f32[24,128]{1,0:T(8,128)S(1)} %shard_map.89.refs_0_.t1), channel_id=1, source_target_pairs={{0,8},{1,9},{2,10},{3,11},{4,12},{5,13},{6,14},{7,15},{8,0},{9,1},... | collective-permute-start | bytes 36872 | tf_op jit(solution)/shard_map/ppermute | solution.py:347
  18.8 0.0 collective-permute-start.9
  18.8 0.0 collective-permute-start.8
  18.8 0.0 collective-permute-done.11.refs_4_
  18.8 2.0 %collective-permute-done.10.refs_3_ = f32[24,128]{1,0:T(8,128)S(1)} collective-permute-done((f32[24,128]{1,0:T(8,128)S(1)}, f32[24,128]{1,0:T(8,128)S(1)}, u32[]{:S(2)}, u32[]{:S(2)}) %collective-permute-start.10) | collective-permute-done | bytes 12320 | tf_op jit(solution)/shard_map/ppermute | solution.py:347
  20.8 1.1 %collective-permute-done.9.refs_2_ = f32[24,128]{1,0:T(8,128)S(1)} collective-permute-done((f32[24,128]{1,0:T(8,128)S(1)}, f32[24,128]{1,0:T(8,128)S(1)}, u32[]{:S(2)}, u32[]{:S(2)}) %collective-permute-start.9) | collective-permute-done | bytes 12320 | tf_op jit(solution)/shard_map/ppermute | solution.py:347
  21.9 0.0 collective-permute-done.8.refs_1_
  21.9 0.3 shard_map.90.t2.refs_0_
  22.2 0.0 collective-permute-start.15
  22.2 1.8 %collective-permute-start.14 = (f32[24,128]{1,0:T(8,128)S(1)}, f32[24,128]{1,0:T(8,128)S(1)}, u32[]{:S(2)}, u32[]{:S(2)}) collective-permute-start(f32[24,128]{1,0:T(8,128)S(1)} %shard_map.90.t2.refs_0_), channel_id=1, source_target_pairs={{0,8},{1,9},{2,10},{3,11},{4,12},{5,13},{6,14},{7,15},{8,0},{9,1},... | collective-permute-start | bytes 36872 | tf_op jit(solution)/shard_map/ppermute | solution.py:347
  24.0 0.0 collective-permute-start.13
  24.0 0.4 collective-permute-start.12
  24.4 0.0 copy-done
  24.4 0.6 %shard_map.91 = (f32[24,512]{1,0:T(8,128)S(1)}, f32[24,128]{1,0:T(8,128)S(1)}, bf16[512,128]{1,0:T(8,128)(2,1)S(1)}, bf16[512,128]{1,0:T(8,128)(2,1)S(1)}, bf16[512,128]{1,0:T(8,128)(2,1)S(1)}) custom-call(f32[3,32,512]{2,1,0:T(8,128)S(1)} %copy-done, f32[24,128]{1,0:T(8,128)S(1)} %get-tuple-element.19.refs_0_.t0, f32[24,128]{1,0:T(8,128)S(1)} %shard_map.89.refs_0_.t1, ...), custom_call_target="tpu_custom_call" | custom-call | flops 60000000 | bytes 250000 | tf_op jit(solution)/shard_map/pallas_call | solution.py:441
  25.0 0.0 collective-permute-done.15.refs_4_
  25.0 0.9 %collective-permute-done.14.refs_3_ = f32[24,128]{1,0:T(8,128)S(1)} collective-permute-done((f32[24,128]{1,0:T(8,128)S(1)}, f32[24,128]{1,0:T(8,128)S(1)}, u32[]{:S(2)}, u32[]{:S(2)}) %collective-permute-start.14) | collective-permute-done | bytes 12320 | tf_op jit(solution)/shard_map/ppermute | solution.py:347
  25.9 1.2 %collective-permute-done.13.refs_2_ = f32[24,128]{1,0:T(8,128)S(1)} collective-permute-done((f32[24,128]{1,0:T(8,128)S(1)}, f32[24,128]{1,0:T(8,128)S(1)}, u32[]{:S(2)}, u32[]{:S(2)}) %collective-permute-start.13) | collective-permute-done | bytes 12320 | tf_op jit(solution)/shard_map/ppermute | solution.py:347
  27.1 0.0 collective-permute-done.12.refs_1_
  27.1 0.4 shard_map.92
  27.5 0.1 collective-permute-start.16
  27.6 1.2 %collective-permute-done.16 = f32[24,128]{1,0:T(8,128)S(1)} collective-permute-done((f32[24,128]{1,0:T(8,128)S(1)}, f32[24,128]{1,0:T(8,128)S(1)}, u32[]{:S(2)}, u32[]{:S(2)}) %collective-permute-start.16) | collective-permute-done | bytes 12320 | tf_op jit(solution)/shard_map/ppermute | solution.py:347
  28.8 1.0 %collective-permute-start.19 = (f32[24,128]{1,0:T(8,128)S(1)}, f32[24,128]{1,0:T(8,128)S(1)}, u32[]{:S(2)}, u32[]{:S(2)}) collective-permute-start(f32[24,128]{1,0:T(8,128)S(1)} %add.21), channel_id=1, source_target_pairs={{0,7},{1,6},{2,5},{3,4},{4,3},{5,2},{6,1},{7,0},{8,15},{9,14},{10,... | collective-permute-start | bytes 36872 | tf_op jit(solution)/shard_map/ppermute | solution.py:347
  29.8 0.4 %collective-permute-start.18 = (f32[24,128]{1,0:T(8,128)S(1)}, f32[24,128]{1,0:T(8,128)S(1)}, u32[]{:S(2)}, u32[]{:S(2)}) collective-permute-start(f32[24,128]{1,0:T(8,128)S(1)} %add.21), channel_id=1, source_target_pairs={{0,5},{1,4},{2,7},{3,6},{4,1},{5,0},{6,3},{7,2},{8,13},{9,12},{10,... | collective-permute-start | bytes 36872 | tf_op jit(solution)/shard_map/ppermute | solution.py:347
  30.3 1.5 %collective-permute-start.17 = (f32[24,128]{1,0:T(8,128)S(1)}, f32[24,128]{1,0:T(8,128)S(1)}, u32[]{:S(2)}, u32[]{:S(2)}) collective-permute-start(f32[24,128]{1,0:T(8,128)S(1)} %add.21), channel_id=1, source_target_pairs={{0,3},{1,2},{2,1},{3,0},{4,7},{5,6},{6,5},{7,4},{8,11},{9,10},{10,... | collective-permute-start | bytes 36872 | tf_op jit(solution)/shard_map/ppermute | solution.py:347
  31.8 1.0 %collective-permute-done.19 = f32[24,128]{1,0:T(8,128)S(1)} collective-permute-done((f32[24,128]{1,0:T(8,128)S(1)}, f32[24,128]{1,0:T(8,128)S(1)}, u32[]{:S(2)}, u32[]{:S(2)}) %collective-permute-start.19) | collective-permute-done | bytes 12320 | tf_op jit(solution)/shard_map/ppermute | solution.py:347
  32.8 0.1 collective-permute-done.18
  32.9 0.4 %collective-permute-done.17 = f32[24,128]{1,0:T(8,128)S(1)} collective-permute-done((f32[24,128]{1,0:T(8,128)S(1)}, f32[24,128]{1,0:T(8,128)S(1)}, u32[]{:S(2)}, u32[]{:S(2)}) %collective-permute-start.17) | collective-permute-done | bytes 12320 | tf_op jit(solution)/shard_map/ppermute | solution.py:347
  33.4 2.1 %collective-permute-start.22 = (f32[24,128]{1,0:T(8,128)S(1)}, f32[24,128]{1,0:T(8,128)S(1)}, u32[]{:S(2)}, u32[]{:S(2)}) collective-permute-start(f32[24,128]{1,0:T(8,128)S(1)} %add_add_fusion.1), channel_id=1, source_target_pairs={{0,25},{1,24},{2,27},{3,26},{4,29},{5,28},{6,31},{7,30},{8,17},{9,... | collective-permute-start | bytes 36872 | tf_op jit(solution)/shard_map/ppermute | solution.py:347
  35.5 0.2 collective-permute-start.21
  35.7 1.6 %collective-permute-start.20 = (f32[24,128]{1,0:T(8,128)S(1)}, f32[24,128]{1,0:T(8,128)S(1)}, u32[]{:S(2)}, u32[]{:S(2)}) collective-permute-start(f32[24,128]{1,0:T(8,128)S(1)} %add_add_fusion.1), channel_id=1, source_target_pairs={{0,9},{1,8},{2,11},{3,10},{4,13},{5,12},{6,15},{7,14},{8,1},{9,0},... | collective-permute-start | bytes 36872 | tf_op jit(solution)/shard_map/ppermute | solution.py:347
  37.3 1.0 %collective-permute-done.22 = f32[24,128]{1,0:T(8,128)S(1)} collective-permute-done((f32[24,128]{1,0:T(8,128)S(1)}, f32[24,128]{1,0:T(8,128)S(1)}, u32[]{:S(2)}, u32[]{:S(2)}) %collective-permute-start.22) | collective-permute-done | bytes 12320 | tf_op jit(solution)/shard_map/ppermute | solution.py:347
  38.3 1.3 %collective-permute-done.21 = f32[24,128]{1,0:T(8,128)S(1)} collective-permute-done((f32[24,128]{1,0:T(8,128)S(1)}, f32[24,128]{1,0:T(8,128)S(1)}, u32[]{:S(2)}, u32[]{:S(2)}) %collective-permute-start.21) | collective-permute-done | bytes 12320 | tf_op jit(solution)/shard_map/ppermute | solution.py:347
  39.6 0.0 collective-permute-done.20
  39.6 1.0 %shard_map.93 = (f32[3,4,512]{2,1,0:T(4,128)}, f32[3,4,36]{2,1,0:T(4,128)}) custom-call(f32[24,128]{1,0:T(8,128)S(1)} %add_add_fusion.refs_0_, f32[3,32,512]{2,1,0:T(8,128)S(1)} %copy-done, f32[24,512]{1,0:T(8,128)S(1)} %get-tuple-element.25.refs_13_.refs_2_, f32[8,512]{1,0:T(8,128)S(1)} %get-tuple-element.27.refs_3_), custom_call_target="tpu_custom_call" | custom-call | flops 50000000 | bytes 400000 | tf_op jit(solution)/shard_map/pallas_call | solution.py:456
  (3 shorter events, 0.0 us)
Async XLA Ops:
  1.7 6.3 %collective-permute-start.3 = (f32[32,128]{1,0:T(8,128)S(1)}, f32[32,128]{1,0:T(8,128)S(1)}, u32[]{:S(2)}, u32[]{:S(2)}) collective-permute-start(f32[32,128]{1,0:T(8,128)S(1)} %shard_map.86.refs_0_), channel_id=1, source_target_pairs={{0,2},{1,0},{2,1},{3,4},{4,3},{5,6},{6,5},{7,8},{8,7},{9,10},{10,9... | collective-permute-start | bytes 49160 | tf_op jit(solution)/shard_map/ppermute | solution.py:347
  4.7 3.7 %collective-permute-start.2 = (f32[32,128]{1,0:T(8,128)S(1)}, f32[32,128]{1,0:T(8,128)S(1)}, u32[]{:S(2)}, u32[]{:S(2)}) collective-permute-start(f32[32,128]{1,0:T(8,128)S(1)} %shard_map.86.refs_0_), channel_id=1, source_target_pairs={{0,8},{1,9},{2,10},{3,11},{4,12},{5,13},{6,14},{7,15},{8,0},{9,1},... | collective-permute-start | bytes 49160 | tf_op jit(solution)/shard_map/ppermute | solution.py:347
  6.6 3.2 %collective-permute-start.1 = (f32[32,128]{1,0:T(8,128)S(1)}, f32[32,128]{1,0:T(8,128)S(1)}, u32[]{:S(2)}, u32[]{:S(2)}) collective-permute-start(f32[32,128]{1,0:T(8,128)S(1)} %shard_map.86.refs_0_), channel_id=1, source_target_pairs={{0,1},{1,2},{2,3},{3,0},{4,5},{5,4},{6,7},{7,6},{8,16},{9,17},{10,... | collective-permute-start | bytes 49160 | tf_op jit(solution)/shard_map/ppermute | solution.py:347
  6.6 3.2 %collective-permute-start = (f32[32,128]{1,0:T(8,128)S(1)}, f32[32,128]{1,0:T(8,128)S(1)}, u32[]{:S(2)}, u32[]{:S(2)}) collective-permute-start(f32[32,128]{1,0:T(8,128)S(1)} %shard_map.86.refs_0_), channel_id=1, source_target_pairs={{0,1},{1,0},{2,3},{3,2},{4,5},{5,4},{6,7},{7,6},{8,9},{9,8},{10,11... | collective-permute-start | bytes 49160 | tf_op jit(solution)/shard_map/ppermute | solution.py:347
  10.1 3.7 %collective-permute-start.7 = (f32[24,128]{1,0:T(8,128)S(1)}, f32[24,128]{1,0:T(8,128)S(1)}, u32[]{:S(2)}, u32[]{:S(2)}) collective-permute-start(f32[24,128]{1,0:T(8,128)S(1)} %get-tuple-element.19.refs_0_.t0), channel_id=1, source_target_pairs={{0,2},{1,0},{2,1},{3,4},{4,3},{5,6},{6,5},{7,8},{8,7},{9,10},{10,9... | collective-permute-start | bytes 36872 | tf_op jit(solution)/shard_map/ppermute | solution.py:347
  10.6 3.7 %collective-permute-start.6 = (f32[24,128]{1,0:T(8,128)S(1)}, f32[24,128]{1,0:T(8,128)S(1)}, u32[]{:S(2)}, u32[]{:S(2)}) collective-permute-start(f32[24,128]{1,0:T(8,128)S(1)} %get-tuple-element.19.refs_0_.t0), channel_id=1, source_target_pairs={{0,8},{1,9},{2,10},{3,11},{4,12},{5,13},{6,14},{7,15},{8,0},{9,1},... | collective-permute-start | bytes 36872 | tf_op jit(solution)/shard_map/ppermute | solution.py:347
  12.0 3.1 %collective-permute-start.5 = (f32[24,128]{1,0:T(8,128)S(1)}, f32[24,128]{1,0:T(8,128)S(1)}, u32[]{:S(2)}, u32[]{:S(2)}) collective-permute-start(f32[24,128]{1,0:T(8,128)S(1)} %get-tuple-element.19.refs_0_.t0), channel_id=1, source_target_pairs={{0,1},{1,2},{2,3},{3,0},{4,5},{5,4},{6,7},{7,6},{8,16},{9,17},{10,... | collective-permute-start | bytes 36872 | tf_op jit(solution)/shard_map/ppermute | solution.py:347
  12.2 2.9 %collective-permute-start.4 = (f32[24,128]{1,0:T(8,128)S(1)}, f32[24,128]{1,0:T(8,128)S(1)}, u32[]{:S(2)}, u32[]{:S(2)}) collective-permute-start(f32[24,128]{1,0:T(8,128)S(1)} %get-tuple-element.19.refs_0_.t0), channel_id=1, source_target_pairs={{0,1},{1,0},{2,3},{3,2},{4,5},{5,4},{6,7},{7,6},{8,9},{9,8},{10,11... | collective-permute-start | bytes 36872 | tf_op jit(solution)/shard_map/ppermute | solution.py:347
  15.4 9.0 %copy-start = (f32[3,32,512]{2,1,0:T(8,128)S(1)}, f32[3,32,512]{2,1,0:T(8,128)}, u32[]{:S(2)}) copy-start(f32[3,32,512]{2,1,0:T(8,128)} %refs_1_.1) | copy-start | bytes 589828
  15.4 3.4 %collective-permute-start.11 = (f32[24,128]{1,0:T(8,128)S(1)}, f32[24,128]{1,0:T(8,128)S(1)}, u32[]{:S(2)}, u32[]{:S(2)}) collective-permute-start(f32[24,128]{1,0:T(8,128)S(1)} %shard_map.89.refs_0_.t1), channel_id=1, source_target_pairs={{0,2},{1,0},{2,1},{3,4},{4,3},{5,6},{6,5},{7,8},{8,7},{9,10},{10,9... | collective-permute-start | bytes 36872 | tf_op jit(solution)/shard_map/ppermute | solution.py:347
  17.1 3.7 %collective-permute-start.10 = (f32[24,128]{1,0:T(8,128)S(1)}, f32[24,128]{1,0:T(8,128)S(1)}, u32[]{:S(2)}, u32[]{:S(2)}) collective-permute-start(f32[24,128]{1,0:T(8,128)S(1)} %shard_map.89.refs_0_.t1), channel_id=1, source_target_pairs={{0,8},{1,9},{2,10},{3,11},{4,12},{5,13},{6,14},{7,15},{8,0},{9,1},... | collective-permute-start | bytes 36872 | tf_op jit(solution)/shard_map/ppermute | solution.py:347
  18.8 3.1 %collective-permute-start.9 = (f32[24,128]{1,0:T(8,128)S(1)}, f32[24,128]{1,0:T(8,128)S(1)}, u32[]{:S(2)}, u32[]{:S(2)}) collective-permute-start(f32[24,128]{1,0:T(8,128)S(1)} %shard_map.89.refs_0_.t1), channel_id=1, source_target_pairs={{0,1},{1,2},{2,3},{3,0},{4,5},{5,4},{6,7},{7,6},{8,16},{9,17},{10,... | collective-permute-start | bytes 36872 | tf_op jit(solution)/shard_map/ppermute | solution.py:347
  18.8 3.1 %collective-permute-start.8 = (f32[24,128]{1,0:T(8,128)S(1)}, f32[24,128]{1,0:T(8,128)S(1)}, u32[]{:S(2)}, u32[]{:S(2)}) collective-permute-start(f32[24,128]{1,0:T(8,128)S(1)} %shard_map.89.refs_0_.t1), channel_id=1, source_target_pairs={{0,1},{1,0},{2,3},{3,2},{4,5},{5,4},{6,7},{7,6},{8,9},{9,8},{10,11... | collective-permute-start | bytes 36872 | tf_op jit(solution)/shard_map/ppermute | solution.py:347
  22.2 2.8 %collective-permute-start.15 = (f32[24,128]{1,0:T(8,128)S(1)}, f32[24,128]{1,0:T(8,128)S(1)}, u32[]{:S(2)}, u32[]{:S(2)}) collective-permute-start(f32[24,128]{1,0:T(8,128)S(1)} %shard_map.90.t2.refs_0_), channel_id=1, source_target_pairs={{0,2},{1,0},{2,1},{3,4},{4,3},{5,6},{6,5},{7,8},{8,7},{9,10},{10,9... | collective-permute-start | bytes 36872 | tf_op jit(solution)/shard_map/ppermute | solution.py:347
  22.2 3.8 %collective-permute-start.14 = (f32[24,128]{1,0:T(8,128)S(1)}, f32[24,128]{1,0:T(8,128)S(1)}, u32[]{:S(2)}, u32[]{:S(2)}) collective-permute-start(f32[24,128]{1,0:T(8,128)S(1)} %shard_map.90.t2.refs_0_), channel_id=1, source_target_pairs={{0,8},{1,9},{2,10},{3,11},{4,12},{5,13},{6,14},{7,15},{8,0},{9,1},... | collective-permute-start | bytes 36872 | tf_op jit(solution)/shard_map/ppermute | solution.py:347
  24.0 3.1 %collective-permute-start.13 = (f32[24,128]{1,0:T(8,128)S(1)}, f32[24,128]{1,0:T(8,128)S(1)}, u32[]{:S(2)}, u32[]{:S(2)}) collective-permute-start(f32[24,128]{1,0:T(8,128)S(1)} %shard_map.90.t2.refs_0_), channel_id=1, source_target_pairs={{0,1},{1,2},{2,3},{3,0},{4,5},{5,4},{6,7},{7,6},{8,16},{9,17},{10,... | collective-permute-start | bytes 36872 | tf_op jit(solution)/shard_map/ppermute | solution.py:347
  24.0 3.1 %collective-permute-start.12 = (f32[24,128]{1,0:T(8,128)S(1)}, f32[24,128]{1,0:T(8,128)S(1)}, u32[]{:S(2)}, u32[]{:S(2)}) collective-permute-start(f32[24,128]{1,0:T(8,128)S(1)} %shard_map.90.t2.refs_0_), channel_id=1, source_target_pairs={{0,1},{1,0},{2,3},{3,2},{4,5},{5,4},{6,7},{7,6},{8,9},{9,8},{10,11... | collective-permute-start | bytes 36872 | tf_op jit(solution)/shard_map/ppermute | solution.py:347
  27.5 1.2 %collective-permute-start.16 = (f32[24,128]{1,0:T(8,128)S(1)}, f32[24,128]{1,0:T(8,128)S(1)}, u32[]{:S(2)}, u32[]{:S(2)}) collective-permute-start(f32[24,128]{1,0:T(8,128)S(1)} %get-tuple-element.26), channel_id=1, source_target_pairs={{0,1},{1,0},{2,3},{3,2},{4,5},{5,4},{6,7},{7,6},{8,9},{9,8},{10,11... | collective-permute-start | bytes 36872 | tf_op jit(solution)/shard_map/ppermute | solution.py:347
  28.8 4.0 %collective-permute-start.19 = (f32[24,128]{1,0:T(8,128)S(1)}, f32[24,128]{1,0:T(8,128)S(1)}, u32[]{:S(2)}, u32[]{:S(2)}) collective-permute-start(f32[24,128]{1,0:T(8,128)S(1)} %add.21), channel_id=1, source_target_pairs={{0,7},{1,6},{2,5},{3,4},{4,3},{5,2},{6,1},{7,0},{8,15},{9,14},{10,... | collective-permute-start | bytes 36872 | tf_op jit(solution)/shard_map/ppermute | solution.py:347
  29.8 3.1 %collective-permute-start.18 = (f32[24,128]{1,0:T(8,128)S(1)}, f32[24,128]{1,0:T(8,128)S(1)}, u32[]{:S(2)}, u32[]{:S(2)}) collective-permute-start(f32[24,128]{1,0:T(8,128)S(1)} %add.21), channel_id=1, source_target_pairs={{0,5},{1,4},{2,7},{3,6},{4,1},{5,0},{6,3},{7,2},{8,13},{9,12},{10,... | collective-permute-start | bytes 36872 | tf_op jit(solution)/shard_map/ppermute | solution.py:347
  30.3 3.1 %collective-permute-start.17 = (f32[24,128]{1,0:T(8,128)S(1)}, f32[24,128]{1,0:T(8,128)S(1)}, u32[]{:S(2)}, u32[]{:S(2)}) collective-permute-start(f32[24,128]{1,0:T(8,128)S(1)} %add.21), channel_id=1, source_target_pairs={{0,3},{1,2},{2,1},{3,0},{4,7},{5,6},{6,5},{7,4},{8,11},{9,10},{10,... | collective-permute-start | bytes 36872 | tf_op jit(solution)/shard_map/ppermute | solution.py:347
  33.4 4.9 %collective-permute-start.22 = (f32[24,128]{1,0:T(8,128)S(1)}, f32[24,128]{1,0:T(8,128)S(1)}, u32[]{:S(2)}, u32[]{:S(2)}) collective-permute-start(f32[24,128]{1,0:T(8,128)S(1)} %add_add_fusion.1), channel_id=1, source_target_pairs={{0,25},{1,24},{2,27},{3,26},{4,29},{5,28},{6,31},{7,30},{8,17},{9,... | collective-permute-start | bytes 36872 | tf_op jit(solution)/shard_map/ppermute | solution.py:347
  35.5 4.1 %collective-permute-start.21 = (f32[24,128]{1,0:T(8,128)S(1)}, f32[24,128]{1,0:T(8,128)S(1)}, u32[]{:S(2)}, u32[]{:S(2)}) collective-permute-start(f32[24,128]{1,0:T(8,128)S(1)} %add_add_fusion.1), channel_id=1, source_target_pairs={{0,17},{1,16},{2,19},{3,18},{4,21},{5,20},{6,23},{7,22},{8,25},{9,... | collective-permute-start | bytes 36872 | tf_op jit(solution)/shard_map/ppermute | solution.py:347
  35.7 3.9 %collective-permute-start.20 = (f32[24,128]{1,0:T(8,128)S(1)}, f32[24,128]{1,0:T(8,128)S(1)}, u32[]{:S(2)}, u32[]{:S(2)}) collective-permute-start(f32[24,128]{1,0:T(8,128)S(1)} %add_add_fusion.1), channel_id=1, source_target_pairs={{0,9},{1,8},{2,11},{3,10},{4,13},{5,12},{6,15},{7,14},{8,1},{9,0},... | collective-permute-start | bytes 36872 | tf_op jit(solution)/shard_map/ppermute | solution.py:347

commit v17 on v16

--- a/solution.py
+++ b/solution.py
@@ -77,11 +77,20 @@
     return copies
 
 
-def start_kernel(prev_in, mix_in, list_in, count_in, out_ref, prev_ref, mix_ref, list_ref, count_ref, sems):
+def start_kernel(
+    prev_in, mix_in, list_in, count_in, strips_in, out_ref, head_ref, prev_ref, mix_ref, list_ref, count_ref, sems
+):
     copies = fetch(
-        [(prev_in, prev_ref), (mix_in, mix_ref), (list_in, list_ref), (count_in, count_ref)], sems
+        [
+            (prev_in, prev_ref),
+            (mix_in, mix_ref),
+            (list_in, list_ref),
+            (count_in, count_ref),
+            (strips_in.at[pl.ds(0, head_ref.shape[0])], head_ref),
+        ],
+        sems,
     )
-    for copy in copies[1:]:
+    for copy in copies[1:4]:
         copy.wait()
     comps, vecs, rows = prev_ref.shape
     eye = iota((vecs, vecs), 0) == iota((vecs, vecs), 1)
@@ -105,14 +114,25 @@
         start = jnp.sum(weights[c] * prev_ref[c], axis=0, keepdims=True)
         line = jnp.broadcast_to(start, own.shape)
         out_ref[c * 8 : (c + 1) * 8, :] = fold(jnp.where(own, line, 0.0))
-
-
-def prepare_kernel(strips_in, columns_in, shifts_in, high_ref, low_ref, aux_ref, strips, columns, shifts, sems):
-    parts = strips.shape[0]
-    depth = strips.shape[1]
-    pairs = [(columns_in, columns), (shifts_in, shifts)]
-    pairs += [(strips_in.at[pl.ds(p * depth, depth)], strips.at[p]) for p in range(parts)]
-    copies = fetch(pairs, sems)
+    copies[4].wait()
+
+
+def prepare_kernel(
+    head, strips_in, columns_in, shifts_in, high_ref, low_ref, aux_ref, strips, columns, shifts, sems
+):
+    parts, depth = strips.shape[:2]
+    first = head.shape[0]
+    pairs = [(strips_in.at[pl.ds(first + p * depth, depth)], strips.at[p]) for p in range(parts)]
+    copies = fetch([(columns_in, columns), (shifts_in, shifts)] + pairs, sems)
+
+    def turn(block, at):
+        turned = block.T
+        high = turned.astype(jnp.bfloat16)
+        columns = pl.ds(at, block.shape[0])
+        high_ref[:, columns] = high
+        low_ref[:, columns] = (turned - high.astype(jnp.float32)).astype(jnp.bfloat16)
+
+    turn(head[...], 0)
     copies[0].wait()
     copies[1].wait()
     where = iota((8, 128), 1)
@@ -127,10 +147,7 @@
     aux_ref[8 * S :, :] = table
     for p in range(parts):
         copies[2 + p].wait()
-        turned = strips[p].T
-        high = turned.astype(jnp.bfloat16)
-        high_ref[:, p * depth : (p + 1) * depth] = high
-        low_ref[:, p * depth : (p + 1) * depth] = (turned - high.astype(jnp.float32)).astype(jnp.bfloat16)
+        turn(strips[p], first + p * depth)
 
 
 def selection(table, metas, place, length):
@@ -394,10 +411,10 @@
     width = strips.shape[1]
     f32, bf16, dma = jnp.float32, jnp.bfloat16, pltpu.SemaphoreType.DMA
     tile_out = ((comps * blocks, 128), f32)
-    tile = call(
+    tile, head = call(
         start_kernel,
-        [((comps * blocks + 8, 128), f32)],
-        [HBM] * 4,
+        [((comps * blocks + 8, 128), f32), ((rows // 2, width), f32)],
+        [HBM] * 5,
         600000,
         250000,
         [
@@ -405,22 +422,22 @@
             pltpu.VMEM(mix.shape, f32),
             pltpu.VMEM(send_list.shape, jnp.int32),
             pltpu.VMEM(send_count.shape, jnp.int32),
-            dma((4,)),
+            dma((5,)),
         ],
-    )(*in_hbm(prev_basis, mix, send_list, send_count))
+    )(*in_hbm(prev_basis, mix, send_list, send_count, strips))
     high, low, aux = call(
         prepare_kernel,
         [((width, rows), bf16), ((width, rows), bf16), ((8 * S + 8, 128), f32)],
-        [HBM] * 3,
+        [VMEM] + [HBM] * 3,
         1000000,
         1000000,
         [
-            pltpu.VMEM((4, rows // 4, width), f32),
+            pltpu.VMEM((2, rows // 4, width), f32),
             pltpu.VMEM(columns.shape[::-1], jnp.int32),
             pltpu.SMEM(shifts.shape, f32),
-            dma((6,)),
+            dma((4,)),
         ],
-    )(*in_hbm(strips, columns.T, shifts))
+    )(head, *in_hbm(strips, columns.T, shifts))
     tiles = []
     length = lax.axis_size("dom")
     tile, choose = call(

time: 40.8 us -> 40.9 us (level)
  transfers between devices with their start and end apart: 23 -> 23, of which waited for: 14 -> 14; matrix products, arithmetic and copies ran while one was open for 0% -> 0% of each run, Pallas kernels for 5% -> 4%
where the time goes in v17:
time: 40.9 us; the launch traced here: 40.7 us
  starting transfers between devices  20.9 us (51%)
  waiting for transfers between devices  13.8 us (34%)
  Pallas kernels  5.25 us (13%)
  between operations  0.72 us (2%)
    ppermute x23, starting transfers between devices, send(): lax.ppermute(value, 'dom', [(d, target[d]) for d in range(lax.axis_size('...  20.9 us
    ppermute x23, waiting for transfers between devices, send(): lax.ppermute(value, 'dom', [(d, target[d]) for d in range(lax.axis_size('...  13.8 us
    pallas_call x1, Pallas kernels, local(): call(prepare_kernel, [((width, rows), bf16), ((width, rows), bf16), ((8 *...  1.17 us
    pallas_call x1, Pallas kernels, local(): call(start_kernel, [((comps * blocks + 8, 128), f32), ((rows // 2, width)...  1.15 us
    pallas_call x1, Pallas kernels, local(): call(lambda *refs: finish_kernel(total, *refs), [((comps, S, rows), f32),...  1.02 us
  transfers between devices with their start and end apart: 23, of which 14 were waited for; matrix products, arithmetic and copies ran while one was open for 0% of the time, Pallas kernels for 4%

profile of v17, /device:TPU:0, one launch (start us, length us, event | category | flops | bytes accessed | tf_op | source)
XLA Modules:
  0.0 40.7 jit_solution(15277194532770359911)
XLA Ops:
  0.6 1.1 %shard_map.86 = (f32[32,128]{1,0:T(8,128)S(1)}, f32[256,256]{1,0:T(8,128)S(1)}) custom-call(f32[3,32,512]{2,1,0:T(8,128)} %refs_1_.1, f32[3,32]{1,0:T(4,128)} %mix_in.1, s32[1,4,8]{2,1,0:T(4,128)} %list_in.1, s32[1,4]{1,0:T(1,128)} %count_in.1, f32[512,256]{1,0:T(8,128)} %strips_in.3), custom_call_target="tpu_custom_call" | custom-call | flops 600000 | bytes 250000 | tf_op jit(solution)/shard_map/pallas_call | solution.py:414
  1.8 3.0 %collective-permute-start.3 = (f32[32,128]{1,0:T(8,128)S(1)}, f32[32,128]{1,0:T(8,128)S(1)}, u32[]{:S(2)}, u32[]{:S(2)}) collective-permute-start(f32[32,128]{1,0:T(8,128)S(1)} %get-tuple-element.18.refs_0_), channel_id=1, source_target_pairs={{0,2},{1,0},{2,1},{3,4},{4,3},{5,6},{6,5},{7,8},{8,7},{9,10},{10,9... | collective-permute-start | bytes 49160 | tf_op jit(solution)/shard_map/ppermute | solution.py:364
  4.8 1.9 %collective-permute-start.2 = (f32[32,128]{1,0:T(8,128)S(1)}, f32[32,128]{1,0:T(8,128)S(1)}, u32[]{:S(2)}, u32[]{:S(2)}) collective-permute-start(f32[32,128]{1,0:T(8,128)S(1)} %get-tuple-element.18.refs_0_), channel_id=1, source_target_pairs={{0,8},{1,9},{2,10},{3,11},{4,12},{5,13},{6,14},{7,15},{8,0},{9,1},... | collective-permute-start | bytes 49160 | tf_op jit(solution)/shard_map/ppermute | solution.py:364
  6.6 0.0 collective-permute-start.1
  6.6 0.0 collective-permute-start
  6.6 1.2 %shard_map.87 = (bf16[256,512]{1,0:T(8,128)(2,1)S(1)}, bf16[256,512]{1,0:T(8,128)(2,1)S(1)}, f32[40,128]{1,0:T(8,128)S(1)}) custom-call(f32[256,256]{1,0:T(8,128)S(1)} %get-tuple-element.19.head, f32[512,256]{1,0:T(8,128)} %strips_in.3, s32[4,8]{1,0:T(4,128)} %bitcast.2, f32[4]{0:T(128)} %shifts_in.1), custom_call_target="tpu_custom_call" | custom-call | flops 1000000 | bytes 1000000 | tf_op jit(solution)/shard_map/pallas_call | solution.py:428
  7.8 0.0 collective-permute-done.3.refs_4_
  7.8 0.7 %collective-permute-done.2.refs_3_ = f32[32,128]{1,0:T(8,128)S(1)} collective-permute-done((f32[32,128]{1,0:T(8,128)S(1)}, f32[32,128]{1,0:T(8,128)S(1)}, u32[]{:S(2)}, u32[]{:S(2)}) %collective-permute-start.2) | collective-permute-done | bytes 16416 | tf_op jit(solution)/shard_map/ppermute | solution.py:364
  8.5 1.3 %collective-permute-done.1.refs_2_ = f32[32,128]{1,0:T(8,128)S(1)} collective-permute-done((f32[32,128]{1,0:T(8,128)S(1)}, f32[32,128]{1,0:T(8,128)S(1)}, u32[]{:S(2)}, u32[]{:S(2)}) %collective-permute-start.1) | collective-permute-done | bytes 16416 | tf_op jit(solution)/shard_map/ppermute | solution.py:364
  9.8 0.0 collective-permute-done.refs_1_
  9.8 0.4 shard_map.88
  10.2 0.2 collective-permute-start.7
  10.4 1.6 %collective-permute-start.6 = (f32[24,128]{1,0:T(8,128)S(1)}, f32[24,128]{1,0:T(8,128)S(1)}, u32[]{:S(2)}, u32[]{:S(2)}) collective-permute-start(f32[24,128]{1,0:T(8,128)S(1)} %get-tuple-element.23.refs_0_.t0), channel_id=1, source_target_pairs={{0,8},{1,9},{2,10},{3,11},{4,12},{5,13},{6,14},{7,15},{8,0},{9,1},... | collective-permute-start | bytes 36872 | tf_op jit(solution)/shard_map/ppermute | solution.py:364
  12.0 0.0 collective-permute-start.5
  12.0 1.6 %collective-permute-start.4 = (f32[24,128]{1,0:T(8,128)S(1)}, f32[24,128]{1,0:T(8,128)S(1)}, u32[]{:S(2)}, u32[]{:S(2)}) collective-permute-start(f32[24,128]{1,0:T(8,128)S(1)} %get-tuple-element.23.refs_0_.t0), channel_id=1, source_target_pairs={{0,1},{1,0},{2,3},{3,2},{4,5},{5,4},{6,7},{7,6},{8,9},{9,8},{10,11... | collective-permute-start | bytes 36872 | tf_op jit(solution)/shard_map/ppermute | solution.py:364
  13.7 0.0 collective-permute-done.7.refs_4_
  13.7 0.4 %collective-permute-done.6.refs_3_ = f32[24,128]{1,0:T(8,128)S(1)} collective-permute-done((f32[24,128]{1,0:T(8,128)S(1)}, f32[24,128]{1,0:T(8,128)S(1)}, u32[]{:S(2)}, u32[]{:S(2)}) %collective-permute-start.6) | collective-permute-done | bytes 12320 | tf_op jit(solution)/shard_map/ppermute | solution.py:364
  14.1 1.0 %collective-permute-done.5.refs_2_ = f32[24,128]{1,0:T(8,128)S(1)} collective-permute-done((f32[24,128]{1,0:T(8,128)S(1)}, f32[24,128]{1,0:T(8,128)S(1)}, u32[]{:S(2)}, u32[]{:S(2)}) %collective-permute-start.5) | collective-permute-done | bytes 12320 | tf_op jit(solution)/shard_map/ppermute | solution.py:364
  15.1 0.0 collective-permute-done.4.refs_1_
  15.1 0.3 shard_map.89.refs_0_.t1
  15.4 0.0 copy-start
  15.4 1.5 %collective-permute-start.11 = (f32[24,128]{1,0:T(8,128)S(1)}, f32[24,128]{1,0:T(8,128)S(1)}, u32[]{:S(2)}, u32[]{:S(2)}) collective-permute-start(f32[24,128]{1,0:T(8,128)S(1)} %shard_map.89.refs_0_.t1), channel_id=1, source_target_pairs={{0,2},{1,0},{2,1},{3,4},{4,3},{5,6},{6,5},{7,8},{8,7},{9,10},{10,9... | collective-permute-start | bytes 36872 | tf_op jit(solution)/shard_map/ppermute | solution.py:364
  17.0 1.9 %collective-permute-start.10 = (f32[24,128]{1,0:T(8,128)S(1)}, f32[24,128]{1,0:T(8,128)S(1)}, u32[]{:S(2)}, u32[]{:S(2)}) collective-permute-start(f32[24,128]{1,0:T(8,128)S(1)} %shard_map.89.refs_0_.t1), channel_id=1, source_target_pairs={{0,8},{1,9},{2,10},{3,11},{4,12},{5,13},{6,14},{7,15},{8,0},{9,1},... | collective-permute-start | bytes 36872 | tf_op jit(solution)/shard_map/ppermute | solution.py:364
  18.8 0.0 collective-permute-start.9
  18.8 0.0 collective-permute-start.8
  18.8 0.0 collective-permute-done.11.refs_4_
  18.8 1.8 %collective-permute-done.10.refs_3_ = f32[24,128]{1,0:T(8,128)S(1)} collective-permute-done((f32[24,128]{1,0:T(8,128)S(1)}, f32[24,128]{1,0:T(8,128)S(1)}, u32[]{:S(2)}, u32[]{:S(2)}) %collective-permute-start.10) | collective-permute-done | bytes 12320 | tf_op jit(solution)/shard_map/ppermute | solution.py:364
  20.7 1.3 %collective-permute-done.9.refs_2_ = f32[24,128]{1,0:T(8,128)S(1)} collective-permute-done((f32[24,128]{1,0:T(8,128)S(1)}, f32[24,128]{1,0:T(8,128)S(1)}, u32[]{:S(2)}, u32[]{:S(2)}) %collective-permute-start.9) | collective-permute-done | bytes 12320 | tf_op jit(solution)/shard_map/ppermute | solution.py:364
  21.9 0.0 collective-permute-done.8.refs_1_
  22.0 0.3 shard_map.90.t2.refs_0_
  22.2 0.0 collective-permute-start.15
  22.2 1.8 %collective-permute-start.14 = (f32[24,128]{1,0:T(8,128)S(1)}, f32[24,128]{1,0:T(8,128)S(1)}, u32[]{:S(2)}, u32[]{:S(2)}) collective-permute-start(f32[24,128]{1,0:T(8,128)S(1)} %shard_map.90.t2.refs_0_), channel_id=1, source_target_pairs={{0,8},{1,9},{2,10},{3,11},{4,12},{5,13},{6,14},{7,15},{8,0},{9,1},... | collective-permute-start | bytes 36872 | tf_op jit(solution)/shard_map/ppermute | solution.py:364
  24.1 0.0 collective-permute-start.13
  24.1 0.4 collective-permute-start.12
  24.5 0.0 copy-done
  24.5 0.6 %shard_map.91 = (f32[24,512]{1,0:T(8,128)S(1)}, f32[24,128]{1,0:T(8,128)S(1)}, bf16[512,128]{1,0:T(8,128)(2,1)S(1)}, bf16[512,128]{1,0:T(8,128)(2,1)S(1)}, bf16[512,128]{1,0:T(8,128)(2,1)S(1)}) custom-call(f32[3,32,512]{2,1,0:T(8,128)S(1)} %copy-done, f32[24,128]{1,0:T(8,128)S(1)} %get-tuple-element.23.refs_0_.t0, f32[24,128]{1,0:T(8,128)S(1)} %shard_map.89.refs_0_.t1, ...), custom_call_target="tpu_custom_call" | custom-call | flops 60000000 | bytes 250000 | tf_op jit(solution)/shard_map/pallas_call | solution.py:458
  25.1 0.0 collective-permute-done.15.refs_4_
  25.1 0.9 %collective-permute-done.14.refs_3_ = f32[24,128]{1,0:T(8,128)S(1)} collective-permute-done((f32[24,128]{1,0:T(8,128)S(1)}, f32[24,128]{1,0:T(8,128)S(1)}, u32[]{:S(2)}, u32[]{:S(2)}) %collective-permute-start.14) | collective-permute-done | bytes 12320 | tf_op jit(solution)/shard_map/ppermute | solution.py:364
  26.0 1.2 %collective-permute-done.13.refs_2_ = f32[24,128]{1,0:T(8,128)S(1)} collective-permute-done((f32[24,128]{1,0:T(8,128)S(1)}, f32[24,128]{1,0:T(8,128)S(1)}, u32[]{:S(2)}, u32[]{:S(2)}) %collective-permute-start.13) | collective-permute-done | bytes 12320 | tf_op jit(solution)/shard_map/ppermute | solution.py:364
  27.2 0.0 collective-permute-done.12.refs_1_
  27.2 0.4 shard_map.92
  27.6 0.1 collective-permute-start.16
  27.7 1.2 %collective-permute-done.16 = f32[24,128]{1,0:T(8,128)S(1)} collective-permute-done((f32[24,128]{1,0:T(8,128)S(1)}, f32[24,128]{1,0:T(8,128)S(1)}, u32[]{:S(2)}, u32[]{:S(2)}) %collective-permute-start.16) | collective-permute-done | bytes 12320 | tf_op jit(solution)/shard_map/ppermute | solution.py:364
  28.9 1.0 %collective-permute-start.19 = (f32[24,128]{1,0:T(8,128)S(1)}, f32[24,128]{1,0:T(8,128)S(1)}, u32[]{:S(2)}, u32[]{:S(2)}) collective-permute-start(f32[24,128]{1,0:T(8,128)S(1)} %add.21), channel_id=1, source_target_pairs={{0,7},{1,6},{2,5},{3,4},{4,3},{5,2},{6,1},{7,0},{8,15},{9,14},{10,... | collective-permute-start | bytes 36872 | tf_op jit(solution)/shard_map/ppermute | solution.py:364
  29.9 0.4 %collective-permute-start.18 = (f32[24,128]{1,0:T(8,128)S(1)}, f32[24,128]{1,0:T(8,128)S(1)}, u32[]{:S(2)}, u32[]{:S(2)}) collective-permute-start(f32[24,128]{1,0:T(8,128)S(1)} %add.21), channel_id=1, source_target_pairs={{0,5},{1,4},{2,7},{3,6},{4,1},{5,0},{6,3},{7,2},{8,13},{9,12},{10,... | collective-permute-start | bytes 36872 | tf_op jit(solution)/shard_map/ppermute | solution.py:364
  30.3 1.5 %collective-permute-start.17 = (f32[24,128]{1,0:T(8,128)S(1)}, f32[24,128]{1,0:T(8,128)S(1)}, u32[]{:S(2)}, u32[]{:S(2)}) collective-permute-start(f32[24,128]{1,0:T(8,128)S(1)} %add.21), channel_id=1, source_target_pairs={{0,3},{1,2},{2,1},{3,0},{4,7},{5,6},{6,5},{7,4},{8,11},{9,10},{10,... | collective-permute-start | bytes 36872 | tf_op jit(solution)/shard_map/ppermute | solution.py:364
  31.8 1.0 %collective-permute-done.19 = f32[24,128]{1,0:T(8,128)S(1)} collective-permute-done((f32[24,128]{1,0:T(8,128)S(1)}, f32[24,128]{1,0:T(8,128)S(1)}, u32[]{:S(2)}, u32[]{:S(2)}) %collective-permute-start.19) | collective-permute-done | bytes 12320 | tf_op jit(solution)/shard_map/ppermute | solution.py:364
  32.9 0.1 collective-permute-done.18
  33.0 0.4 %collective-permute-done.17 = f32[24,128]{1,0:T(8,128)S(1)} collective-permute-done((f32[24,128]{1,0:T(8,128)S(1)}, f32[24,128]{1,0:T(8,128)S(1)}, u32[]{:S(2)}, u32[]{:S(2)}) %collective-permute-start.17) | collective-permute-done | bytes 12320 | tf_op jit(solution)/shard_map/ppermute | solution.py:364
  33.5 2.1 %collective-permute-start.22 = (f32[24,128]{1,0:T(8,128)S(1)}, f32[24,128]{1,0:T(8,128)S(1)}, u32[]{:S(2)}, u32[]{:S(2)}) collective-permute-start(f32[24,128]{1,0:T(8,128)S(1)} %add_add_fusion.1), channel_id=1, source_target_pairs={{0,25},{1,24},{2,27},{3,26},{4,29},{5,28},{6,31},{7,30},{8,17},{9,... | collective-permute-start | bytes 36872 | tf_op jit(solution)/shard_map/ppermute | solution.py:364
  35.5 0.2 collective-permute-start.21
  35.8 1.6 %collective-permute-start.20 = (f32[24,128]{1,0:T(8,128)S(1)}, f32[24,128]{1,0:T(8,128)S(1)}, u32[]{:S(2)}, u32[]{:S(2)}) collective-permute-start(f32[24,128]{1,0:T(8,128)S(1)} %add_add_fusion.1), channel_id=1, source_target_pairs={{0,9},{1,8},{2,11},{3,10},{4,13},{5,12},{6,15},{7,14},{8,1},{9,0},... | collective-permute-start | bytes 36872 | tf_op jit(solution)/shard_map/ppermute | solution.py:364
  37.4 1.0 %collective-permute-done.22 = f32[24,128]{1,0:T(8,128)S(1)} collective-permute-done((f32[24,128]{1,0:T(8,128)S(1)}, f32[24,128]{1,0:T(8,128)S(1)}, u32[]{:S(2)}, u32[]{:S(2)}) %collective-permute-start.22) | collective-permute-done | bytes 12320 | tf_op jit(solution)/shard_map/ppermute | solution.py:364
  38.4 1.3 %collective-permute-done.21 = f32[24,128]{1,0:T(8,128)S(1)} collective-permute-done((f32[24,128]{1,0:T(8,128)S(1)}, f32[24,128]{1,0:T(8,128)S(1)}, u32[]{:S(2)}, u32[]{:S(2)}) %collective-permute-start.21) | collective-permute-done | bytes 12320 | tf_op jit(solution)/shard_map/ppermute | solution.py:364
  39.7 0.0 collective-permute-done.20
  39.7 1.0 %shard_map.93 = (f32[3,4,512]{2,1,0:T(4,128)}, f32[3,4,36]{2,1,0:T(4,128)}) custom-call(f32[24,128]{1,0:T(8,128)S(1)} %add_add_fusion.refs_0_, f32[3,32,512]{2,1,0:T(8,128)S(1)} %copy-done, f32[24,512]{1,0:T(8,128)S(1)} %get-tuple-element.29.refs_13_.refs_2_, f32[8,512]{1,0:T(8,128)S(1)} %get-tuple-element.31.refs_3_), custom_call_target="tpu_custom_call" | custom-call | flops 50000000 | bytes 400000 | tf_op jit(solution)/shard_map/pallas_call | solution.py:473
  (3 shorter events, 0.0 us)
Async XLA Ops:
  1.8 6.0 %collective-permute-start.3 = (f32[32,128]{1,0:T(8,128)S(1)}, f32[32,128]{1,0:T(8,128)S(1)}, u32[]{:S(2)}, u32[]{:S(2)}) collective-permute-start(f32[32,128]{1,0:T(8,128)S(1)} %get-tuple-element.18.refs_0_), channel_id=1, source_target_pairs={{0,2},{1,0},{2,1},{3,4},{4,3},{5,6},{6,5},{7,8},{8,7},{9,10},{10,9... | collective-permute-start | bytes 49160 | tf_op jit(solution)/shard_map/ppermute | solution.py:364
  4.8 3.7 %collective-permute-start.2 = (f32[32,128]{1,0:T(8,128)S(1)}, f32[32,128]{1,0:T(8,128)S(1)}, u32[]{:S(2)}, u32[]{:S(2)}) collective-permute-start(f32[32,128]{1,0:T(8,128)S(1)} %get-tuple-element.18.refs_0_), channel_id=1, source_target_pairs={{0,8},{1,9},{2,10},{3,11},{4,12},{5,13},{6,14},{7,15},{8,0},{9,1},... | collective-permute-start | bytes 49160 | tf_op jit(solution)/shard_map/ppermute | solution.py:364
  6.6 3.2 %collective-permute-start.1 = (f32[32,128]{1,0:T(8,128)S(1)}, f32[32,128]{1,0:T(8,128)S(1)}, u32[]{:S(2)}, u32[]{:S(2)}) collective-permute-start(f32[32,128]{1,0:T(8,128)S(1)} %get-tuple-element.18.refs_0_), channel_id=1, source_target_pairs={{0,1},{1,2},{2,3},{3,0},{4,5},{5,4},{6,7},{7,6},{8,16},{9,17},{10,... | collective-permute-start | bytes 49160 | tf_op jit(solution)/shard_map/ppermute | solution.py:364
  6.6 3.2 %collective-permute-start = (f32[32,128]{1,0:T(8,128)S(1)}, f32[32,128]{1,0:T(8,128)S(1)}, u32[]{:S(2)}, u32[]{:S(2)}) collective-permute-start(f32[32,128]{1,0:T(8,128)S(1)} %get-tuple-element.18.refs_0_), channel_id=1, source_target_pairs={{0,1},{1,0},{2,3},{3,2},{4,5},{5,4},{6,7},{7,6},{8,9},{9,8},{10,11... | collective-permute-start | bytes 49160 | tf_op jit(solution)/shard_map/ppermute | solution.py:364
  10.2 3.5 %collective-permute-start.7 = (f32[24,128]{1,0:T(8,128)S(1)}, f32[24,128]{1,0:T(8,128)S(1)}, u32[]{:S(2)}, u32[]{:S(2)}) collective-permute-start(f32[24,128]{1,0:T(8,128)S(1)} %get-tuple-element.23.refs_0_.t0), channel_id=1, source_target_pairs={{0,2},{1,0},{2,1},{3,4},{4,3},{5,6},{6,5},{7,8},{8,7},{9,10},{10,9... | collective-permute-start | bytes 36872 | tf_op jit(solution)/shard_map/ppermute | solution.py:364
  10.4 3.7 %collective-permute-start.6 = (f32[24,128]{1,0:T(8,128)S(1)}, f32[24,128]{1,0:T(8,128)S(1)}, u32[]{:S(2)}, u32[]{:S(2)}) collective-permute-start(f32[24,128]{1,0:T(8,128)S(1)} %get-tuple-element.23.refs_0_.t0), channel_id=1, source_target_pairs={{0,8},{1,9},{2,10},{3,11},{4,12},{5,13},{6,14},{7,15},{8,0},{9,1},... | collective-permute-start | bytes 36872 | tf_op jit(solution)/shard_map/ppermute | solution.py:364
  12.0 3.1 %collective-permute-start.5 = (f32[24,128]{1,0:T(8,128)S(1)}, f32[24,128]{1,0:T(8,128)S(1)}, u32[]{:S(2)}, u32[]{:S(2)}) collective-permute-start(f32[24,128]{1,0:T(8,128)S(1)} %get-tuple-element.23.refs_0_.t0), channel_id=1, source_target_pairs={{0,1},{1,2},{2,3},{3,0},{4,5},{5,4},{6,7},{7,6},{8,16},{9,17},{10,... | collective-permute-start | bytes 36872 | tf_op jit(solution)/shard_map/ppermute | solution.py:364
  12.0 3.1 %collective-permute-start.4 = (f32[24,128]{1,0:T(8,128)S(1)}, f32[24,128]{1,0:T(8,128)S(1)}, u32[]{:S(2)}, u32[]{:S(2)}) collective-permute-start(f32[24,128]{1,0:T(8,128)S(1)} %get-tuple-element.23.refs_0_.t0), channel_id=1, source_target_pairs={{0,1},{1,0},{2,3},{3,2},{4,5},{5,4},{6,7},{7,6},{8,9},{9,8},{10,11... | collective-permute-start | bytes 36872 | tf_op jit(solution)/shard_map/ppermute | solution.py:364
  15.4 9.1 %copy-start = (f32[3,32,512]{2,1,0:T(8,128)S(1)}, f32[3,32,512]{2,1,0:T(8,128)}, u32[]{:S(2)}) copy-start(f32[3,32,512]{2,1,0:T(8,128)} %refs_1_.1) | copy-start | bytes 589828
  15.4 3.4 %collective-permute-start.11 = (f32[24,128]{1,0:T(8,128)S(1)}, f32[24,128]{1,0:T(8,128)S(1)}, u32[]{:S(2)}, u32[]{:S(2)}) collective-permute-start(f32[24,128]{1,0:T(8,128)S(1)} %shard_map.89.refs_0_.t1), channel_id=1, source_target_pairs={{0,2},{1,0},{2,1},{3,4},{4,3},{5,6},{6,5},{7,8},{8,7},{9,10},{10,9... | collective-permute-start | bytes 36872 | tf_op jit(solution)/shard_map/ppermute | solution.py:364
  17.0 3.7 %collective-permute-start.10 = (f32[24,128]{1,0:T(8,128)S(1)}, f32[24,128]{1,0:T(8,128)S(1)}, u32[]{:S(2)}, u32[]{:S(2)}) collective-permute-start(f32[24,128]{1,0:T(8,128)S(1)} %shard_map.89.refs_0_.t1), channel_id=1, source_target_pairs={{0,8},{1,9},{2,10},{3,11},{4,12},{5,13},{6,14},{7,15},{8,0},{9,1},... | collective-permute-start | bytes 36872 | tf_op jit(solution)/shard_map/ppermute | solution.py:364
  18.8 3.1 %collective-permute-start.9 = (f32[24,128]{1,0:T(8,128)S(1)}, f32[24,128]{1,0:T(8,128)S(1)}, u32[]{:S(2)}, u32[]{:S(2)}) collective-permute-start(f32[24,128]{1,0:T(8,128)S(1)} %shard_map.89.refs_0_.t1), channel_id=1, source_target_pairs={{0,1},{1,2},{2,3},{3,0},{4,5},{5,4},{6,7},{7,6},{8,16},{9,17},{10,... | collective-permute-start | bytes 36872 | tf_op jit(solution)/shard_map/ppermute | solution.py:364
  18.8 3.1 %collective-permute-start.8 = (f32[24,128]{1,0:T(8,128)S(1)}, f32[24,128]{1,0:T(8,128)S(1)}, u32[]{:S(2)}, u32[]{:S(2)}) collective-permute-start(f32[24,128]{1,0:T(8,128)S(1)} %shard_map.89.refs_0_.t1), channel_id=1, source_target_pairs={{0,1},{1,0},{2,3},{3,2},{4,5},{5,4},{6,7},{7,6},{8,9},{9,8},{10,11... | collective-permute-start | bytes 36872 | tf_op jit(solution)/shard_map/ppermute | solution.py:364
  22.2 2.8 %collective-permute-start.15 = (f32[24,128]{1,0:T(8,128)S(1)}, f32[24,128]{1,0:T(8,128)S(1)}, u32[]{:S(2)}, u32[]{:S(2)}) collective-permute-start(f32[24,128]{1,0:T(8,128)S(1)} %shard_map.90.t2.refs_0_), channel_id=1, source_target_pairs={{0,2},{1,0},{2,1},{3,4},{4,3},{5,6},{6,5},{7,8},{8,7},{9,10},{10,9... | collective-permute-start | bytes 36872 | tf_op jit(solution)/shard_map/ppermute | solution.py:364
  22.2 3.8 %collective-permute-start.14 = (f32[24,128]{1,0:T(8,128)S(1)}, f32[24,128]{1,0:T(8,128)S(1)}, u32[]{:S(2)}, u32[]{:S(2)}) collective-permute-start(f32[24,128]{1,0:T(8,128)S(1)} %shard_map.90.t2.refs_0_), channel_id=1, source_target_pairs={{0,8},{1,9},{2,10},{3,11},{4,12},{5,13},{6,14},{7,15},{8,0},{9,1},... | collective-permute-start | bytes 36872 | tf_op jit(solution)/shard_map/ppermute | solution.py:364
  24.1 3.1 %collective-permute-start.13 = (f32[24,128]{1,0:T(8,128)S(1)}, f32[24,128]{1,0:T(8,128)S(1)}, u32[]{:S(2)}, u32[]{:S(2)}) collective-permute-start(f32[24,128]{1,0:T(8,128)S(1)} %shard_map.90.t2.refs_0_), channel_id=1, source_target_pairs={{0,1},{1,2},{2,3},{3,0},{4,5},{5,4},{6,7},{7,6},{8,16},{9,17},{10,... | collective-permute-start | bytes 36872 | tf_op jit(solution)/shard_map/ppermute | solution.py:364
  24.1 3.1 %collective-permute-start.12 = (f32[24,128]{1,0:T(8,128)S(1)}, f32[24,128]{1,0:T(8,128)S(1)}, u32[]{:S(2)}, u32[]{:S(2)}) collective-permute-start(f32[24,128]{1,0:T(8,128)S(1)} %shard_map.90.t2.refs_0_), channel_id=1, source_target_pairs={{0,1},{1,0},{2,3},{3,2},{4,5},{5,4},{6,7},{7,6},{8,9},{9,8},{10,11... | collective-permute-start | bytes 36872 | tf_op jit(solution)/shard_map/ppermute | solution.py:364
  27.6 1.2 %collective-permute-start.16 = (f32[24,128]{1,0:T(8,128)S(1)}, f32[24,128]{1,0:T(8,128)S(1)}, u32[]{:S(2)}, u32[]{:S(2)}) collective-permute-start(f32[24,128]{1,0:T(8,128)S(1)} %get-tuple-element.30), channel_id=1, source_target_pairs={{0,1},{1,0},{2,3},{3,2},{4,5},{5,4},{6,7},{7,6},{8,9},{9,8},{10,11... | collective-permute-start | bytes 36872 | tf_op jit(solution)/shard_map/ppermute | solution.py:364
  28.9 4.0 %collective-permute-start.19 = (f32[24,128]{1,0:T(8,128)S(1)}, f32[24,128]{1,0:T(8,128)S(1)}, u32[]{:S(2)}, u32[]{:S(2)}) collective-permute-start(f32[24,128]{1,0:T(8,128)S(1)} %add.21), channel_id=1, source_target_pairs={{0,7},{1,6},{2,5},{3,4},{4,3},{5,2},{6,1},{7,0},{8,15},{9,14},{10,... | collective-permute-start | bytes 36872 | tf_op jit(solution)/shard_map/ppermute | solution.py:364
  29.9 3.1 %collective-permute-start.18 = (f32[24,128]{1,0:T(8,128)S(1)}, f32[24,128]{1,0:T(8,128)S(1)}, u32[]{:S(2)}, u32[]{:S(2)}) collective-permute-start(f32[24,128]{1,0:T(8,128)S(1)} %add.21), channel_id=1, source_target_pairs={{0,5},{1,4},{2,7},{3,6},{4,1},{5,0},{6,3},{7,2},{8,13},{9,12},{10,... | collective-permute-start | bytes 36872 | tf_op jit(solution)/shard_map/ppermute | solution.py:364
  30.3 3.1 %collective-permute-start.17 = (f32[24,128]{1,0:T(8,128)S(1)}, f32[24,128]{1,0:T(8,128)S(1)}, u32[]{:S(2)}, u32[]{:S(2)}) collective-permute-start(f32[24,128]{1,0:T(8,128)S(1)} %add.21), channel_id=1, source_target_pairs={{0,3},{1,2},{2,1},{3,0},{4,7},{5,6},{6,5},{7,4},{8,11},{9,10},{10,... | collective-permute-start | bytes 36872 | tf_op jit(solution)/shard_map/ppermute | solution.py:364
  33.5 4.9 %collective-permute-start.22 = (f32[24,128]{1,0:T(8,128)S(1)}, f32[24,128]{1,0:T(8,128)S(1)}, u32[]{:S(2)}, u32[]{:S(2)}) collective-permute-start(f32[24,128]{1,0:T(8,128)S(1)} %add_add_fusion.1), channel_id=1, source_target_pairs={{0,25},{1,24},{2,27},{3,26},{4,29},{5,28},{6,31},{7,30},{8,17},{9,... | collective-permute-start | bytes 36872 | tf_op jit(solution)/shard_map/ppermute | solution.py:364
  35.5 4.1 %collective-permute-start.21 = (f32[24,128]{1,0:T(8,128)S(1)}, f32[24,128]{1,0:T(8,128)S(1)}, u32[]{:S(2)}, u32[]{:S(2)}) collective-permute-start(f32[24,128]{1,0:T(8,128)S(1)} %add_add_fusion.1), channel_id=1, source_target_pairs={{0,17},{1,16},{2,19},{3,18},{4,21},{5,20},{6,23},{7,22},{8,25},{9,... | collective-permute-start | bytes 36872 | tf_op jit(solution)/shard_map/ppermute | solution.py:364
  35.8 3.9 %collective-permute-start.20 = (f32[24,128]{1,0:T(8,128)S(1)}, f32[24,128]{1,0:T(8,128)S(1)}, u32[]{:S(2)}, u32[]{:S(2)}) collective-permute-start(f32[24,128]{1,0:T(8,128)S(1)} %add_add_fusion.1), channel_id=1, source_target_pairs={{0,9},{1,8},{2,11},{3,10},{4,13},{5,12},{6,15},{7,14},{8,1},{9,0},... | collective-permute-start | bytes 36872 | tf_op jit(solution)/shard_map/ppermute | solution.py:364

commit v18 on v16

--- a/solution.py
+++ b/solution.py
@@ -115,16 +115,14 @@
     copies = fetch(pairs, sems)
     copies[0].wait()
     copies[1].wait()
-    where = iota((8, 128), 1)
-    table = jnp.zeros((8, 128), jnp.float32)
     eye = iota((8, 8), 0) == iota((8, 8), 1)
-    for k in range(columns.shape[0]):
+    for k in range(1, columns.shape[0]):
         line = jnp.broadcast_to(columns[k : k + 1, :].astype(jnp.float32), (8, 8))
         column = jnp.sum(jnp.where(eye, line, 0.0), axis=1, keepdims=True)
-        table = jnp.where(where == k, column, table)
+        at = 8 * S + 8 * (k - 1)
+        aux_ref[at : at + 8, :] = jnp.broadcast_to(column, (8, 128))
     for k in range(S):
         aux_ref[8 * k : 8 * k + 8, :] = jnp.full((8, 128), shifts[k], jnp.float32)
-    aux_ref[8 * S :, :] = table
     for p in range(parts):
         copies[2 + p].wait()
         turned = strips[p].T
@@ -151,12 +149,9 @@
         order = order + jnp.where(valid, base, DEAD)
         target = jnp.where(lane // 8 == link + 1, order, target)
     target = jnp.broadcast_to(target, (8, 128))
-    lane = iota((8, 128), 1).astype(jnp.float32)
-    at = [
-        jnp.sum(jnp.where(lane == table[:, k : k + 1], target, 0.0), axis=1, keepdims=True)
-        for k in range(1, 4)
-    ]
-    return jnp.concatenate([jnp.broadcast_to(x, (8, 128)) for x in at], axis=0).astype(jnp.int32)
+    index = table.astype(jnp.int32)
+    at = [jnp.take_along_axis(target, index[8 * k : 8 * k + 8], axis=1) for k in range(3)]
+    return jnp.concatenate(at, axis=0).astype(jnp.int32)
 
 
 def product(choose, pieces, high, low):
@@ -259,10 +254,10 @@
     )
 
 
-def finish_kernel(total, gram_in, prev_ref, lines, last, basis_ref, factors_ref):
+def finish_kernel(total, gram_ins, prev_ref, lines, last, basis_ref, factors_ref):
     comps, vecs, rows = prev_ref.shape
     width = comps * vecs
-    gram = gram_in[...] * (1.0 / total)
+    gram = added([ref[...] for ref in gram_ins]) * (1.0 / total)
     small = gram[16:]
     lane, comp = iota((8, 128), 1), iota((8, 128), 0)
     in_prev = (lane < width) & (lane // vecs == comp)
@@ -375,17 +370,21 @@
     def fetched(step):
         return send(value, {d: d ^ (step | 1) for d in range(length)})
 
-    value = value + fetched(1)
+    parts = [value, fetched(1)]
     step = 2
     while step < length:
-        if 2 * step < length:
-            farthest = fetched(3 * step)
-            first, second = fetched(step), fetched(2 * step)
-            value = (value + first) + (second + farthest)
-        else:
-            value = value + fetched(step)
+        value = added(parts)
+        steps = (3 * step, step, 2 * step) if 2 * step < length else (step,)
+        got = [fetched(s) for s in steps]
+        parts = [value] + got[1:] + got[:1]
         step *= 4
-    return value
+    return parts
+
+
+def added(parts):
+    if len(parts) == 2:
+        return parts[0] + parts[1]
+    return (parts[0] + parts[1]) + (parts[2] + parts[3])
 
 
 def local(strips, columns, send_list, send_count, shifts, prev_basis, mix):
@@ -410,7 +409,7 @@
     )(*in_hbm(prev_basis, mix, send_list, send_count))
     high, low, aux = call(
         prepare_kernel,
-        [((width, rows), bf16), ((width, rows), bf16), ((8 * S + 8, 128), f32)],
+        [((width, rows), bf16), ((width, rows), bf16), ((8 * S + 24, 128), f32)],
         [HBM] * 3,
         1000000,
         1000000,
@@ -453,13 +452,15 @@
         900000,
     )(tile, *received, choose, aux, high, low, early, *parts, lines)
     total = float(length * rows)
+    parts = summed(gram)
+    count = len(parts)
     basis, factors = call(
-        lambda *refs: finish_kernel(total, *refs),
+        lambda *refs: finish_kernel(total, refs[:count], *refs[count:]),
         [((comps, S, rows), f32), ((comps, S, vecs + S), f32)],
-        [VMEM] * 4,
+        [VMEM] * (count + 3),
         50000000,
         400000,
-    )(summed(gram), prev_basis, lines, last)
+    )(*parts, prev_basis, lines, last)
     return basis, jnp.swapaxes(factors, 1, 2)
 
 

time: 40.8 us -> 40.8 us (level)
  no operation moved by 1% of the time
where the time goes in v18:
time: 40.8 us; the launch traced here: 40.6 us
  starting transfers between devices  21.1 us (52%)
  waiting for transfers between devices  13.4 us (33%)
  Pallas kernels  5.36 us (13%)
  between operations  0.72 us (2%)
    ppermute x23, starting transfers between devices, send(): lax.ppermute(value, 'dom', [(d, target[d]) for d in range(lax.axis_size('...  21.1 us
    ppermute x23, waiting for transfers between devices, send(): lax.ppermute(value, 'dom', [(d, target[d]) for d in range(lax.axis_size('...  13.4 us
    pallas_call x1, Pallas kernels, local(): call(prepare_kernel, [((width, rows), bf16), ((width, rows), bf16), ((8 *...  1.39 us
    pallas_call x1, Pallas kernels, local(): call(start_kernel, [((comps * blocks + 8, 128), f32)], [HBM] * 4, 600000,...  1.08 us
    pallas_call x1, Pallas kernels, local(): call(lambda *refs: finish_kernel(total, refs[:count], *refs[count:]), [((...  1.02 us
  transfers between devices with their start and end apart: 23, of which 14 were waited for; matrix products, arithmetic and copies ran while one was open for 0% of the time, Pallas kernels for 5%

profile of v18, /device:TPU:0, one launch (start us, length us, event | category | flops | bytes accessed | tf_op | source)
XLA Modules:
  0.0 40.6 jit_solution(2098654572276413567)
XLA Ops:
  0.6 1.1 %shard_map.86.refs_0_ = f32[32,128]{1,0:T(8,128)S(1)} custom-call(f32[3,32,512]{2,1,0:T(8,128)} %refs_4_.1, f32[3,32]{1,0:T(4,128)} %mix_in.1, s32[1,4,8]{2,1,0:T(4,128)} %list_in.1, s32[1,4]{1,0:T(1,128)} %count_in.1), custom_call_target="tpu_custom_call" | custom-call | flops 600000 | bytes 250000 | tf_op jit(solution)/shard_map/pallas_call | solution.py:396
  1.7 3.0 %collective-permute-start.3 = (f32[32,128]{1,0:T(8,128)S(1)}, f32[32,128]{1,0:T(8,128)S(1)}, u32[]{:S(2)}, u32[]{:S(2)}) collective-permute-start(f32[32,128]{1,0:T(8,128)S(1)} %shard_map.86.refs_0_), channel_id=1, source_target_pairs={{0,2},{1,0},{2,1},{3,4},{4,3},{5,6},{6,5},{7,8},{8,7},{9,10},{10,9... | collective-permute-start | bytes 49160 | tf_op jit(solution)/shard_map/ppermute | solution.py:342
  4.7 1.9 %collective-permute-start.2 = (f32[32,128]{1,0:T(8,128)S(1)}, f32[32,128]{1,0:T(8,128)S(1)}, u32[]{:S(2)}, u32[]{:S(2)}) collective-permute-start(f32[32,128]{1,0:T(8,128)S(1)} %shard_map.86.refs_0_), channel_id=1, source_target_pairs={{0,8},{1,9},{2,10},{3,11},{4,12},{5,13},{6,14},{7,15},{8,0},{9,1},... | collective-permute-start | bytes 49160 | tf_op jit(solution)/shard_map/ppermute | solution.py:342
  6.6 0.0 collective-permute-start.1
  6.6 0.0 collective-permute-start
  6.6 1.4 %shard_map.87 = (bf16[256,512]{1,0:T(8,128)(2,1)S(1)}, bf16[256,512]{1,0:T(8,128)(2,1)S(1)}, f32[56,128]{1,0:T(8,128)S(1)}) custom-call(f32[512,256]{1,0:T(8,128)} %strips_in.1, s32[4,8]{1,0:T(4,128)} %bitcast.2, f32[4]{0:T(128)} %shifts_in.1), custom_call_target="tpu_custom_call" | custom-call | flops 1000000 | bytes 1000000 | tf_op jit(solution)/shard_map/pallas_call | solution.py:410
  8.0 0.0 collective-permute-done.3.refs_4_
  8.0 0.5 %collective-permute-done.2.refs_3_ = f32[32,128]{1,0:T(8,128)S(1)} collective-permute-done((f32[32,128]{1,0:T(8,128)S(1)}, f32[32,128]{1,0:T(8,128)S(1)}, u32[]{:S(2)}, u32[]{:S(2)}) %collective-permute-start.2) | collective-permute-done | bytes 16416 | tf_op jit(solution)/shard_map/ppermute | solution.py:342
  8.5 1.3 %collective-permute-done.1.refs_2_ = f32[32,128]{1,0:T(8,128)S(1)} collective-permute-done((f32[32,128]{1,0:T(8,128)S(1)}, f32[32,128]{1,0:T(8,128)S(1)}, u32[]{:S(2)}, u32[]{:S(2)}) %collective-permute-start.1) | collective-permute-done | bytes 16416 | tf_op jit(solution)/shard_map/ppermute | solution.py:342
  9.7 0.0 collective-permute-done.refs_1_
  9.7 0.4 shard_map.88
  10.1 0.4 %collective-permute-start.7 = (f32[24,128]{1,0:T(8,128)S(1)}, f32[24,128]{1,0:T(8,128)S(1)}, u32[]{:S(2)}, u32[]{:S(2)}) collective-permute-start(f32[24,128]{1,0:T(8,128)S(1)} %get-tuple-element.19.refs_0_.t0), channel_id=1, source_target_pairs={{0,2},{1,0},{2,1},{3,4},{4,3},{5,6},{6,5},{7,8},{8,7},{9,10},{10,9... | collective-permute-start | bytes 36872 | tf_op jit(solution)/shard_map/ppermute | solution.py:342
  10.5 1.4 %collective-permute-start.6 = (f32[24,128]{1,0:T(8,128)S(1)}, f32[24,128]{1,0:T(8,128)S(1)}, u32[]{:S(2)}, u32[]{:S(2)}) collective-permute-start(f32[24,128]{1,0:T(8,128)S(1)} %get-tuple-element.19.refs_0_.t0), channel_id=1, source_target_pairs={{0,8},{1,9},{2,10},{3,11},{4,12},{5,13},{6,14},{7,15},{8,0},{9,1},... | collective-permute-start | bytes 36872 | tf_op jit(solution)/shard_map/ppermute | solution.py:342
  11.9 0.2 collective-permute-start.5
  12.1 1.7 %collective-permute-start.4 = (f32[24,128]{1,0:T(8,128)S(1)}, f32[24,128]{1,0:T(8,128)S(1)}, u32[]{:S(2)}, u32[]{:S(2)}) collective-permute-start(f32[24,128]{1,0:T(8,128)S(1)} %get-tuple-element.19.refs_0_.t0), channel_id=1, source_target_pairs={{0,1},{1,0},{2,3},{3,2},{4,5},{5,4},{6,7},{7,6},{8,9},{9,8},{10,11... | collective-permute-start | bytes 36872 | tf_op jit(solution)/shard_map/ppermute | solution.py:342
  13.8 0.0 collective-permute-done.7.refs_4_
  13.8 0.4 %collective-permute-done.6.refs_3_ = f32[24,128]{1,0:T(8,128)S(1)} collective-permute-done((f32[24,128]{1,0:T(8,128)S(1)}, f32[24,128]{1,0:T(8,128)S(1)}, u32[]{:S(2)}, u32[]{:S(2)}) %collective-permute-start.6) | collective-permute-done | bytes 12320 | tf_op jit(solution)/shard_map/ppermute | solution.py:342
  14.2 0.9 %collective-permute-done.5.refs_2_ = f32[24,128]{1,0:T(8,128)S(1)} collective-permute-done((f32[24,128]{1,0:T(8,128)S(1)}, f32[24,128]{1,0:T(8,128)S(1)}, u32[]{:S(2)}, u32[]{:S(2)}) %collective-permute-start.5) | collective-permute-done | bytes 12320 | tf_op jit(solution)/shard_map/ppermute | solution.py:342
  15.1 0.0 collective-permute-done.4.refs_1_
  15.1 0.3 shard_map.89.refs_0_.t1
  15.3 0.0 copy-start
  15.3 1.7 %collective-permute-start.11 = (f32[24,128]{1,0:T(8,128)S(1)}, f32[24,128]{1,0:T(8,128)S(1)}, u32[]{:S(2)}, u32[]{:S(2)}) collective-permute-start(f32[24,128]{1,0:T(8,128)S(1)} %shard_map.89.refs_0_.t1), channel_id=1, source_target_pairs={{0,2},{1,0},{2,1},{3,4},{4,3},{5,6},{6,5},{7,8},{8,7},{9,10},{10,9... | collective-permute-start | bytes 36872 | tf_op jit(solution)/shard_map/ppermute | solution.py:342
  17.1 1.6 %collective-permute-start.10 = (f32[24,128]{1,0:T(8,128)S(1)}, f32[24,128]{1,0:T(8,128)S(1)}, u32[]{:S(2)}, u32[]{:S(2)}) collective-permute-start(f32[24,128]{1,0:T(8,128)S(1)} %shard_map.89.refs_0_.t1), channel_id=1, source_target_pairs={{0,8},{1,9},{2,10},{3,11},{4,12},{5,13},{6,14},{7,15},{8,0},{9,1},... | collective-permute-start | bytes 36872 | tf_op jit(solution)/shard_map/ppermute | solution.py:342
  18.7 0.0 collective-permute-start.9
  18.7 0.0 collective-permute-start.8
  18.7 0.0 collective-permute-done.11.refs_4_
  18.7 2.0 %collective-permute-done.10.refs_3_ = f32[24,128]{1,0:T(8,128)S(1)} collective-permute-done((f32[24,128]{1,0:T(8,128)S(1)}, f32[24,128]{1,0:T(8,128)S(1)}, u32[]{:S(2)}, u32[]{:S(2)}) %collective-permute-start.10) | collective-permute-done | bytes 12320 | tf_op jit(solution)/shard_map/ppermute | solution.py:342
  20.8 1.1 %collective-permute-done.9.refs_2_ = f32[24,128]{1,0:T(8,128)S(1)} collective-permute-done((f32[24,128]{1,0:T(8,128)S(1)}, f32[24,128]{1,0:T(8,128)S(1)}, u32[]{:S(2)}, u32[]{:S(2)}) %collective-permute-start.9) | collective-permute-done | bytes 12320 | tf_op jit(solution)/shard_map/ppermute | solution.py:342
  21.8 0.0 collective-permute-done.8.refs_1_
  21.8 0.3 shard_map.90.t2.refs_0_
  22.1 0.0 collective-permute-start.15
  22.1 1.8 %collective-permute-start.14 = (f32[24,128]{1,0:T(8,128)S(1)}, f32[24,128]{1,0:T(8,128)S(1)}, u32[]{:S(2)}, u32[]{:S(2)}) collective-permute-start(f32[24,128]{1,0:T(8,128)S(1)} %shard_map.90.t2.refs_0_), channel_id=1, source_target_pairs={{0,8},{1,9},{2,10},{3,11},{4,12},{5,13},{6,14},{7,15},{8,0},{9,1},... | collective-permute-start | bytes 36872 | tf_op jit(solution)/shard_map/ppermute | solution.py:342
  24.0 0.0 collective-permute-start.13
  24.0 0.4 collective-permute-start.12
  24.4 0.0 copy-done
  24.4 0.6 %shard_map.91 = (f32[24,512]{1,0:T(8,128)S(1)}, f32[24,128]{1,0:T(8,128)S(1)}, bf16[512,128]{1,0:T(8,128)(2,1)S(1)}, bf16[512,128]{1,0:T(8,128)(2,1)S(1)}, bf16[512,128]{1,0:T(8,128)(2,1)S(1)}) custom-call(f32[3,32,512]{2,1,0:T(8,128)S(1)} %copy-done, f32[24,128]{1,0:T(8,128)S(1)} %get-tuple-element.19.refs_0_.t0, f32[24,128]{1,0:T(8,128)S(1)} %shard_map.89.refs_0_.t1, ...), custom_call_target="tpu_custom_call" | custom-call | flops 60000000 | bytes 250000 | tf_op jit(solution)/shard_map/pallas_call | solution.py:440
  24.9 0.0 collective-permute-done.15.refs_4_
  24.9 0.9 %collective-permute-done.14.refs_3_ = f32[24,128]{1,0:T(8,128)S(1)} collective-permute-done((f32[24,128]{1,0:T(8,128)S(1)}, f32[24,128]{1,0:T(8,128)S(1)}, u32[]{:S(2)}, u32[]{:S(2)}) %collective-permute-start.14) | collective-permute-done | bytes 12320 | tf_op jit(solution)/shard_map/ppermute | solution.py:342
  25.9 1.2 %collective-permute-done.13.refs_2_ = f32[24,128]{1,0:T(8,128)S(1)} collective-permute-done((f32[24,128]{1,0:T(8,128)S(1)}, f32[24,128]{1,0:T(8,128)S(1)}, u32[]{:S(2)}, u32[]{:S(2)}) %collective-permute-start.13) | collective-permute-done | bytes 12320 | tf_op jit(solution)/shard_map/ppermute | solution.py:342
  27.1 0.0 collective-permute-done.12.refs_1_
  27.1 0.4 shard_map.92
  27.5 0.1 collective-permute-start.16
  27.6 1.2 %collective-permute-done.16 = f32[24,128]{1,0:T(8,128)S(1)} collective-permute-done((f32[24,128]{1,0:T(8,128)S(1)}, f32[24,128]{1,0:T(8,128)S(1)}, u32[]{:S(2)}, u32[]{:S(2)}) %collective-permute-start.16) | collective-permute-done | bytes 12320 | tf_op jit(solution)/shard_map/ppermute | solution.py:342
  28.7 1.0 %collective-permute-start.19 = (f32[24,128]{1,0:T(8,128)S(1)}, f32[24,128]{1,0:T(8,128)S(1)}, u32[]{:S(2)}, u32[]{:S(2)}) collective-permute-start(f32[24,128]{1,0:T(8,128)S(1)} %add.12), channel_id=1, source_target_pairs={{0,7},{1,6},{2,5},{3,4},{4,3},{5,2},{6,1},{7,0},{8,15},{9,14},{10,... | collective-permute-start | bytes 36872 | tf_op jit(solution)/shard_map/ppermute | solution.py:342
  29.8 0.4 %collective-permute-start.18 = (f32[24,128]{1,0:T(8,128)S(1)}, f32[24,128]{1,0:T(8,128)S(1)}, u32[]{:S(2)}, u32[]{:S(2)}) collective-permute-start(f32[24,128]{1,0:T(8,128)S(1)} %add.12), channel_id=1, source_target_pairs={{0,5},{1,4},{2,7},{3,6},{4,1},{5,0},{6,3},{7,2},{8,13},{9,12},{10,... | collective-permute-start | bytes 36872 | tf_op jit(solution)/shard_map/ppermute | solution.py:342
  30.2 1.5 %collective-permute-start.17 = (f32[24,128]{1,0:T(8,128)S(1)}, f32[24,128]{1,0:T(8,128)S(1)}, u32[]{:S(2)}, u32[]{:S(2)}) collective-permute-start(f32[24,128]{1,0:T(8,128)S(1)} %add.12), channel_id=1, source_target_pairs={{0,3},{1,2},{2,1},{3,0},{4,7},{5,6},{6,5},{7,4},{8,11},{9,10},{10,... | collective-permute-start | bytes 36872 | tf_op jit(solution)/shard_map/ppermute | solution.py:342
  31.7 1.0 %collective-permute-done.19 = f32[24,128]{1,0:T(8,128)S(1)} collective-permute-done((f32[24,128]{1,0:T(8,128)S(1)}, f32[24,128]{1,0:T(8,128)S(1)}, u32[]{:S(2)}, u32[]{:S(2)}) %collective-permute-start.19) | collective-permute-done | bytes 12320 | tf_op jit(solution)/shard_map/ppermute | solution.py:342
  32.8 0.1 collective-permute-done.18
  32.9 0.4 %collective-permute-done.17 = f32[24,128]{1,0:T(8,128)S(1)} collective-permute-done((f32[24,128]{1,0:T(8,128)S(1)}, f32[24,128]{1,0:T(8,128)S(1)}, u32[]{:S(2)}, u32[]{:S(2)}) %collective-permute-start.17) | collective-permute-done | bytes 12320 | tf_op jit(solution)/shard_map/ppermute | solution.py:342
  33.3 2.1 %collective-permute-start.22 = (f32[24,128]{1,0:T(8,128)S(1)}, f32[24,128]{1,0:T(8,128)S(1)}, u32[]{:S(2)}, u32[]{:S(2)}) collective-permute-start(f32[24,128]{1,0:T(8,128)S(1)} %add_add_fusion.refs_0_), channel_id=1, source_target_pairs={{0,25},{1,24},{2,27},{3,26},{4,29},{5,28},{6,31},{7,30},{8,17},{9,... | collective-permute-start | bytes 36872 | tf_op jit(solution)/shard_map/ppermute | solution.py:342
  35.4 0.2 collective-permute-start.21
  35.6 1.6 %collective-permute-start.20 = (f32[24,128]{1,0:T(8,128)S(1)}, f32[24,128]{1,0:T(8,128)S(1)}, u32[]{:S(2)}, u32[]{:S(2)}) collective-permute-start(f32[24,128]{1,0:T(8,128)S(1)} %add_add_fusion.refs_0_), channel_id=1, source_target_pairs={{0,9},{1,8},{2,11},{3,10},{4,13},{5,12},{6,15},{7,14},{8,1},{9,0},... | collective-permute-start | bytes 36872 | tf_op jit(solution)/shard_map/ppermute | solution.py:342
  37.2 1.0 %collective-permute-done.22.refs_3_ = f32[24,128]{1,0:T(8,128)S(1)} collective-permute-done((f32[24,128]{1,0:T(8,128)S(1)}, f32[24,128]{1,0:T(8,128)S(1)}, u32[]{:S(2)}, u32[]{:S(2)}) %collective-permute-start.22) | collective-permute-done | bytes 12320 | tf_op jit(solution)/shard_map/ppermute | solution.py:342
  38.2 1.3 %collective-permute-done.21.refs_2_ = f32[24,128]{1,0:T(8,128)S(1)} collective-permute-done((f32[24,128]{1,0:T(8,128)S(1)}, f32[24,128]{1,0:T(8,128)S(1)}, u32[]{:S(2)}, u32[]{:S(2)}) %collective-permute-start.21) | collective-permute-done | bytes 12320 | tf_op jit(solution)/shard_map/ppermute | solution.py:342
  39.5 0.0 collective-permute-done.20.refs_1_
  39.5 1.0 %shard_map.93 = (f32[3,4,512]{2,1,0:T(4,128)}, f32[3,4,36]{2,1,0:T(4,128)}) custom-call(f32[24,128]{1,0:T(8,128)S(1)} %add_add_fusion.refs_0_, f32[24,128]{1,0:T(8,128)S(1)} %collective-permute-done.20.refs_1_, f32[24,128]{1,0:T(8,128)S(1)} %collective-permute-done.21.refs_2_, f32[24,128]{1,0:T(8,128)S(1)} %collective-permute-done.22.refs_3_, ...), custom_call_target="tpu_custom_call" | custom-call | flops 50000000 | bytes 400000 | tf_op jit(solution)/shard_map/pallas_call | solution.py:457
  (2 shorter events, 0.0 us)
Async XLA Ops:
  1.7 6.3 %collective-permute-start.3 = (f32[32,128]{1,0:T(8,128)S(1)}, f32[32,128]{1,0:T(8,128)S(1)}, u32[]{:S(2)}, u32[]{:S(2)}) collective-permute-start(f32[32,128]{1,0:T(8,128)S(1)} %shard_map.86.refs_0_), channel_id=1, source_target_pairs={{0,2},{1,0},{2,1},{3,4},{4,3},{5,6},{6,5},{7,8},{8,7},{9,10},{10,9... | collective-permute-start | bytes 49160 | tf_op jit(solution)/shard_map/ppermute | solution.py:342
  4.7 3.7 %collective-permute-start.2 = (f32[32,128]{1,0:T(8,128)S(1)}, f32[32,128]{1,0:T(8,128)S(1)}, u32[]{:S(2)}, u32[]{:S(2)}) collective-permute-start(f32[32,128]{1,0:T(8,128)S(1)} %shard_map.86.refs_0_), channel_id=1, source_target_pairs={{0,8},{1,9},{2,10},{3,11},{4,12},{5,13},{6,14},{7,15},{8,0},{9,1},... | collective-permute-start | bytes 49160 | tf_op jit(solution)/shard_map/ppermute | solution.py:342
  6.6 3.2 %collective-permute-start.1 = (f32[32,128]{1,0:T(8,128)S(1)}, f32[32,128]{1,0:T(8,128)S(1)}, u32[]{:S(2)}, u32[]{:S(2)}) collective-permute-start(f32[32,128]{1,0:T(8,128)S(1)} %shard_map.86.refs_0_), channel_id=1, source_target_pairs={{0,1},{1,2},{2,3},{3,0},{4,5},{5,4},{6,7},{7,6},{8,16},{9,17},{10,... | collective-permute-start | bytes 49160 | tf_op jit(solution)/shard_map/ppermute | solution.py:342
  6.6 3.2 %collective-permute-start = (f32[32,128]{1,0:T(8,128)S(1)}, f32[32,128]{1,0:T(8,128)S(1)}, u32[]{:S(2)}, u32[]{:S(2)}) collective-permute-start(f32[32,128]{1,0:T(8,128)S(1)} %shard_map.86.refs_0_), channel_id=1, source_target_pairs={{0,1},{1,0},{2,3},{3,2},{4,5},{5,4},{6,7},{7,6},{8,9},{9,8},{10,11... | collective-permute-start | bytes 49160 | tf_op jit(solution)/shard_map/ppermute | solution.py:342
  10.1 3.7 %collective-permute-start.7 = (f32[24,128]{1,0:T(8,128)S(1)}, f32[24,128]{1,0:T(8,128)S(1)}, u32[]{:S(2)}, u32[]{:S(2)}) collective-permute-start(f32[24,128]{1,0:T(8,128)S(1)} %get-tuple-element.19.refs_0_.t0), channel_id=1, source_target_pairs={{0,2},{1,0},{2,1},{3,4},{4,3},{5,6},{6,5},{7,8},{8,7},{9,10},{10,9... | collective-permute-start | bytes 36872 | tf_op jit(solution)/shard_map/ppermute | solution.py:342
  10.5 3.7 %collective-permute-start.6 = (f32[24,128]{1,0:T(8,128)S(1)}, f32[24,128]{1,0:T(8,128)S(1)}, u32[]{:S(2)}, u32[]{:S(2)}) collective-permute-start(f32[24,128]{1,0:T(8,128)S(1)} %get-tuple-element.19.refs_0_.t0), channel_id=1, source_target_pairs={{0,8},{1,9},{2,10},{3,11},{4,12},{5,13},{6,14},{7,15},{8,0},{9,1},... | collective-permute-start | bytes 36872 | tf_op jit(solution)/shard_map/ppermute | solution.py:342
  11.9 3.1 %collective-permute-start.5 = (f32[24,128]{1,0:T(8,128)S(1)}, f32[24,128]{1,0:T(8,128)S(1)}, u32[]{:S(2)}, u32[]{:S(2)}) collective-permute-start(f32[24,128]{1,0:T(8,128)S(1)} %get-tuple-element.19.refs_0_.t0), channel_id=1, source_target_pairs={{0,1},{1,2},{2,3},{3,0},{4,5},{5,4},{6,7},{7,6},{8,16},{9,17},{10,... | collective-permute-start | bytes 36872 | tf_op jit(solution)/shard_map/ppermute | solution.py:342
  12.1 2.9 %collective-permute-start.4 = (f32[24,128]{1,0:T(8,128)S(1)}, f32[24,128]{1,0:T(8,128)S(1)}, u32[]{:S(2)}, u32[]{:S(2)}) collective-permute-start(f32[24,128]{1,0:T(8,128)S(1)} %get-tuple-element.19.refs_0_.t0), channel_id=1, source_target_pairs={{0,1},{1,0},{2,3},{3,2},{4,5},{5,4},{6,7},{7,6},{8,9},{9,8},{10,11... | collective-permute-start | bytes 36872 | tf_op jit(solution)/shard_map/ppermute | solution.py:342
  15.3 9.0 %copy-start = (f32[3,32,512]{2,1,0:T(8,128)S(1)}, f32[3,32,512]{2,1,0:T(8,128)}, u32[]{:S(2)}) copy-start(f32[3,32,512]{2,1,0:T(8,128)} %refs_4_.1) | copy-start | bytes 589828
  15.3 3.4 %collective-permute-start.11 = (f32[24,128]{1,0:T(8,128)S(1)}, f32[24,128]{1,0:T(8,128)S(1)}, u32[]{:S(2)}, u32[]{:S(2)}) collective-permute-start(f32[24,128]{1,0:T(8,128)S(1)} %shard_map.89.refs_0_.t1), channel_id=1, source_target_pairs={{0,2},{1,0},{2,1},{3,4},{4,3},{5,6},{6,5},{7,8},{8,7},{9,10},{10,9... | collective-permute-start | bytes 36872 | tf_op jit(solution)/shard_map/ppermute | solution.py:342
  17.1 3.7 %collective-permute-start.10 = (f32[24,128]{1,0:T(8,128)S(1)}, f32[24,128]{1,0:T(8,128)S(1)}, u32[]{:S(2)}, u32[]{:S(2)}) collective-permute-start(f32[24,128]{1,0:T(8,128)S(1)} %shard_map.89.refs_0_.t1), channel_id=1, source_target_pairs={{0,8},{1,9},{2,10},{3,11},{4,12},{5,13},{6,14},{7,15},{8,0},{9,1},... | collective-permute-start | bytes 36872 | tf_op jit(solution)/shard_map/ppermute | solution.py:342
  18.7 3.1 %collective-permute-start.9 = (f32[24,128]{1,0:T(8,128)S(1)}, f32[24,128]{1,0:T(8,128)S(1)}, u32[]{:S(2)}, u32[]{:S(2)}) collective-permute-start(f32[24,128]{1,0:T(8,128)S(1)} %shard_map.89.refs_0_.t1), channel_id=1, source_target_pairs={{0,1},{1,2},{2,3},{3,0},{4,5},{5,4},{6,7},{7,6},{8,16},{9,17},{10,... | collective-permute-start | bytes 36872 | tf_op jit(solution)/shard_map/ppermute | solution.py:342
  18.7 3.1 %collective-permute-start.8 = (f32[24,128]{1,0:T(8,128)S(1)}, f32[24,128]{1,0:T(8,128)S(1)}, u32[]{:S(2)}, u32[]{:S(2)}) collective-permute-start(f32[24,128]{1,0:T(8,128)S(1)} %shard_map.89.refs_0_.t1), channel_id=1, source_target_pairs={{0,1},{1,0},{2,3},{3,2},{4,5},{5,4},{6,7},{7,6},{8,9},{9,8},{10,11... | collective-permute-start | bytes 36872 | tf_op jit(solution)/shard_map/ppermute | solution.py:342
  22.1 2.8 %collective-permute-start.15 = (f32[24,128]{1,0:T(8,128)S(1)}, f32[24,128]{1,0:T(8,128)S(1)}, u32[]{:S(2)}, u32[]{:S(2)}) collective-permute-start(f32[24,128]{1,0:T(8,128)S(1)} %shard_map.90.t2.refs_0_), channel_id=1, source_target_pairs={{0,2},{1,0},{2,1},{3,4},{4,3},{5,6},{6,5},{7,8},{8,7},{9,10},{10,9... | collective-permute-start | bytes 36872 | tf_op jit(solution)/shard_map/ppermute | solution.py:342
  22.1 3.8 %collective-permute-start.14 = (f32[24,128]{1,0:T(8,128)S(1)}, f32[24,128]{1,0:T(8,128)S(1)}, u32[]{:S(2)}, u32[]{:S(2)}) collective-permute-start(f32[24,128]{1,0:T(8,128)S(1)} %shard_map.90.t2.refs_0_), channel_id=1, source_target_pairs={{0,8},{1,9},{2,10},{3,11},{4,12},{5,13},{6,14},{7,15},{8,0},{9,1},... | collective-permute-start | bytes 36872 | tf_op jit(solution)/shard_map/ppermute | solution.py:342
  24.0 3.1 %collective-permute-start.13 = (f32[24,128]{1,0:T(8,128)S(1)}, f32[24,128]{1,0:T(8,128)S(1)}, u32[]{:S(2)}, u32[]{:S(2)}) collective-permute-start(f32[24,128]{1,0:T(8,128)S(1)} %shard_map.90.t2.refs_0_), channel_id=1, source_target_pairs={{0,1},{1,2},{2,3},{3,0},{4,5},{5,4},{6,7},{7,6},{8,16},{9,17},{10,... | collective-permute-start | bytes 36872 | tf_op jit(solution)/shard_map/ppermute | solution.py:342
  24.0 3.1 %collective-permute-start.12 = (f32[24,128]{1,0:T(8,128)S(1)}, f32[24,128]{1,0:T(8,128)S(1)}, u32[]{:S(2)}, u32[]{:S(2)}) collective-permute-start(f32[24,128]{1,0:T(8,128)S(1)} %shard_map.90.t2.refs_0_), channel_id=1, source_target_pairs={{0,1},{1,0},{2,3},{3,2},{4,5},{5,4},{6,7},{7,6},{8,9},{9,8},{10,11... | collective-permute-start | bytes 36872 | tf_op jit(solution)/shard_map/ppermute | solution.py:342
  27.5 1.2 %collective-permute-start.16 = (f32[24,128]{1,0:T(8,128)S(1)}, f32[24,128]{1,0:T(8,128)S(1)}, u32[]{:S(2)}, u32[]{:S(2)}) collective-permute-start(f32[24,128]{1,0:T(8,128)S(1)} %get-tuple-element.26), channel_id=1, source_target_pairs={{0,1},{1,0},{2,3},{3,2},{4,5},{5,4},{6,7},{7,6},{8,9},{9,8},{10,11... | collective-permute-start | bytes 36872 | tf_op jit(solution)/shard_map/ppermute | solution.py:342
  28.7 4.0 %collective-permute-start.19 = (f32[24,128]{1,0:T(8,128)S(1)}, f32[24,128]{1,0:T(8,128)S(1)}, u32[]{:S(2)}, u32[]{:S(2)}) collective-permute-start(f32[24,128]{1,0:T(8,128)S(1)} %add.12), channel_id=1, source_target_pairs={{0,7},{1,6},{2,5},{3,4},{4,3},{5,2},{6,1},{7,0},{8,15},{9,14},{10,... | collective-permute-start | bytes 36872 | tf_op jit(solution)/shard_map/ppermute | solution.py:342
  29.8 3.1 %collective-permute-start.18 = (f32[24,128]{1,0:T(8,128)S(1)}, f32[24,128]{1,0:T(8,128)S(1)}, u32[]{:S(2)}, u32[]{:S(2)}) collective-permute-start(f32[24,128]{1,0:T(8,128)S(1)} %add.12), channel_id=1, source_target_pairs={{0,5},{1,4},{2,7},{3,6},{4,1},{5,0},{6,3},{7,2},{8,13},{9,12},{10,... | collective-permute-start | bytes 36872 | tf_op jit(solution)/shard_map/ppermute | solution.py:342
  30.2 3.1 %collective-permute-start.17 = (f32[24,128]{1,0:T(8,128)S(1)}, f32[24,128]{1,0:T(8,128)S(1)}, u32[]{:S(2)}, u32[]{:S(2)}) collective-permute-start(f32[24,128]{1,0:T(8,128)S(1)} %add.12), channel_id=1, source_target_pairs={{0,3},{1,2},{2,1},{3,0},{4,7},{5,6},{6,5},{7,4},{8,11},{9,10},{10,... | collective-permute-start | bytes 36872 | tf_op jit(solution)/shard_map/ppermute | solution.py:342
  33.3 4.9 %collective-permute-start.22 = (f32[24,128]{1,0:T(8,128)S(1)}, f32[24,128]{1,0:T(8,128)S(1)}, u32[]{:S(2)}, u32[]{:S(2)}) collective-permute-start(f32[24,128]{1,0:T(8,128)S(1)} %add_add_fusion.refs_0_), channel_id=1, source_target_pairs={{0,25},{1,24},{2,27},{3,26},{4,29},{5,28},{6,31},{7,30},{8,17},{9,... | collective-permute-start | bytes 36872 | tf_op jit(solution)/shard_map/ppermute | solution.py:342
  35.4 4.1 %collective-permute-start.21 = (f32[24,128]{1,0:T(8,128)S(1)}, f32[24,128]{1,0:T(8,128)S(1)}, u32[]{:S(2)}, u32[]{:S(2)}) collective-permute-start(f32[24,128]{1,0:T(8,128)S(1)} %add_add_fusion.refs_0_), channel_id=1, source_target_pairs={{0,17},{1,16},{2,19},{3,18},{4,21},{5,20},{6,23},{7,22},{8,25},{9,... | collective-permute-start | bytes 36872 | tf_op jit(solution)/shard_map/ppermute | solution.py:342
  35.6 3.9 %collective-permute-start.20 = (f32[24,128]{1,0:T(8,128)S(1)}, f32[24,128]{1,0:T(8,128)S(1)}, u32[]{:S(2)}, u32[]{:S(2)}) collective-permute-start(f32[24,128]{1,0:T(8,128)S(1)} %add_add_fusion.refs_0_), channel_id=1, source_target_pairs={{0,9},{1,8},{2,11},{3,10},{4,13},{5,12},{6,15},{7,14},{8,1},{9,0},... | collective-permute-start | bytes 36872 | tf_op jit(solution)/shard_map/ppermute | solution.py:342

commit v19 on v18

--- a/solution.py
+++ b/solution.py
@@ -188,7 +188,7 @@
     return image - jnp.concatenate([shift] * COMPS, axis=0) * pieces[0]
 
 
-def first_kernel(length, own, a, b, c, d, aux, high, low, tile_ref, choose_ref):
+def first_kernel(length, own, a, c, d, b, aux, high, low, tile_ref, choose_ref):
     rows = 8 * COMPS
     refs = (own, a, b, c, d)
     pieces = [ref[:rows, :] for ref in refs]
@@ -422,13 +422,14 @@
     )(*in_hbm(strips, columns.T, shifts))
     tiles = []
     length = lax.axis_size("dom")
+    near, far_odd, far_even, across = ghosts(tile)
     tile, choose = call(
         lambda *refs: first_kernel(length, *refs),
         [tile_out, ((3 * blocks, 128), jnp.int32)],
         [VMEM] * 8,
         50000000,
         600000,
-    )(tile, *ghosts(tile), aux, high, low)
+    )(tile, near, far_even, across, far_odd, aux, high, low)
     tiles.append(tile)
     for step in (1, 2):
         tile = call(

time: 40.8 us -> 40.1 us (0.983)
  waiting for transfers between devices: 13.4 us -> 12.9 us
    ppermute x23, waiting for transfers between devices: 13.4 us -> 12.9 us  [send(): lax.ppermute(value, 'dom', [(d, target[d]) for d in range(lax.axis_size('...]
  transfers between devices with their start and end apart: 23 -> 23, of which waited for: 14 -> 12; matrix products, arithmetic and copies ran while one was open for 0% -> 0% of each run, Pallas kernels for 5% -> 5%
where the time goes in v19:
time: 40.1 us; the launch traced here: 39.9 us
  starting transfers between devices  20.9 us (52%)
  waiting for transfers between devices  12.9 us (32%)
  Pallas kernels  5.36 us (13%)
  between operations  0.72 us (2%)
    ppermute x23, starting transfers between devices, send(): lax.ppermute(value, 'dom', [(d, target[d]) for d in range(lax.axis_size('...  20.9 us
    ppermute x23, waiting for transfers between devices, send(): lax.ppermute(value, 'dom', [(d, target[d]) for d in range(lax.axis_size('...  12.9 us
    pallas_call x1, Pallas kernels, local(): call(prepare_kernel, [((width, rows), bf16), ((width, rows), bf16), ((8 *...  1.39 us
    pallas_call x1, Pallas kernels, local(): call(start_kernel, [((comps * blocks + 8, 128), f32)], [HBM] * 4, 600000,...  1.08 us
    pallas_call x1, Pallas kernels, local(): call(lambda *refs: finish_kernel(total, refs[:count], *refs[count:]), [((...  1.02 us
  transfers between devices with their start and end apart: 23, of which 12 were waited for; matrix products, arithmetic and copies ran while one was open for 0% of the time, Pallas kernels for 5%

profile of v19, /device:TPU:0, one launch (start us, length us, event | category | flops | bytes accessed | tf_op | source)
XLA Modules:
  0.0 39.9 jit_solution(9251104042095485186)
XLA Ops:
  0.6 1.1 %shard_map.86.refs_0_ = f32[32,128]{1,0:T(8,128)S(1)} custom-call(f32[3,32,512]{2,1,0:T(8,128)} %refs_4_.1, f32[3,32]{1,0:T(4,128)} %mix_in.1, s32[1,4,8]{2,1,0:T(4,128)} %list_in.1, s32[1,4]{1,0:T(1,128)} %count_in.1), custom_call_target="tpu_custom_call" | custom-call | flops 600000 | bytes 250000 | tf_op jit(solution)/shard_map/pallas_call | solution.py:396
  1.7 0.5 %collective-permute-start.3 = (f32[32,128]{1,0:T(8,128)S(1)}, f32[32,128]{1,0:T(8,128)S(1)}, u32[]{:S(2)}, u32[]{:S(2)}) collective-permute-start(f32[32,128]{1,0:T(8,128)S(1)} %shard_map.86.refs_0_), channel_id=1, source_target_pairs={{0,1},{1,2},{2,3},{3,0},{4,5},{5,4},{6,7},{7,6},{8,16},{9,17},{10,... | collective-permute-start | bytes 49160 | tf_op jit(solution)/shard_map/ppermute | solution.py:342
  2.2 2.5 %collective-permute-start.2 = (f32[32,128]{1,0:T(8,128)S(1)}, f32[32,128]{1,0:T(8,128)S(1)}, u32[]{:S(2)}, u32[]{:S(2)}) collective-permute-start(f32[32,128]{1,0:T(8,128)S(1)} %shard_map.86.refs_0_), channel_id=1, source_target_pairs={{0,2},{1,0},{2,1},{3,4},{4,3},{5,6},{6,5},{7,8},{8,7},{9,10},{10,9... | collective-permute-start | bytes 49160 | tf_op jit(solution)/shard_map/ppermute | solution.py:342
  4.8 2.5 %collective-permute-start.1 = (f32[32,128]{1,0:T(8,128)S(1)}, f32[32,128]{1,0:T(8,128)S(1)}, u32[]{:S(2)}, u32[]{:S(2)}) collective-permute-start(f32[32,128]{1,0:T(8,128)S(1)} %shard_map.86.refs_0_), channel_id=1, source_target_pairs={{0,8},{1,9},{2,10},{3,11},{4,12},{5,13},{6,14},{7,15},{8,0},{9,1},... | collective-permute-start | bytes 49160 | tf_op jit(solution)/shard_map/ppermute | solution.py:342
  7.2 0.5 %collective-permute-start = (f32[32,128]{1,0:T(8,128)S(1)}, f32[32,128]{1,0:T(8,128)S(1)}, u32[]{:S(2)}, u32[]{:S(2)}) collective-permute-start(f32[32,128]{1,0:T(8,128)S(1)} %shard_map.86.refs_0_), channel_id=1, source_target_pairs={{0,1},{1,0},{2,3},{3,2},{4,5},{5,4},{6,7},{7,6},{8,9},{9,8},{10,11... | collective-permute-start | bytes 49160 | tf_op jit(solution)/shard_map/ppermute | solution.py:342
  7.7 1.4 %shard_map.87 = (bf16[256,512]{1,0:T(8,128)(2,1)S(1)}, bf16[256,512]{1,0:T(8,128)(2,1)S(1)}, f32[56,128]{1,0:T(8,128)S(1)}) custom-call(f32[512,256]{1,0:T(8,128)} %strips_in.1, s32[4,8]{1,0:T(4,128)} %bitcast.2, f32[4]{0:T(128)} %shifts_in.1), custom_call_target="tpu_custom_call" | custom-call | flops 1000000 | bytes 1000000 | tf_op jit(solution)/shard_map/pallas_call | solution.py:410
  9.1 0.0 collective-permute-done.3.refs_4_
  9.1 0.0 collective-permute-done.2.refs_3_
  9.1 0.2 collective-permute-done.1.refs_2_
  9.3 0.0 collective-permute-done.refs_1_
  9.3 0.4 shard_map.88
  9.7 1.3 %collective-permute-start.7 = (f32[24,128]{1,0:T(8,128)S(1)}, f32[24,128]{1,0:T(8,128)S(1)}, u32[]{:S(2)}, u32[]{:S(2)}) collective-permute-start(f32[24,128]{1,0:T(8,128)S(1)} %get-tuple-element.19.refs_0_.t0), channel_id=1, source_target_pairs={{0,2},{1,0},{2,1},{3,4},{4,3},{5,6},{6,5},{7,8},{8,7},{9,10},{10,9... | collective-permute-start | bytes 36872 | tf_op jit(solution)/shard_map/ppermute | solution.py:342
  11.0 1.9 %collective-permute-start.6 = (f32[24,128]{1,0:T(8,128)S(1)}, f32[24,128]{1,0:T(8,128)S(1)}, u32[]{:S(2)}, u32[]{:S(2)}) collective-permute-start(f32[24,128]{1,0:T(8,128)S(1)} %get-tuple-element.19.refs_0_.t0), channel_id=1, source_target_pairs={{0,8},{1,9},{2,10},{3,11},{4,12},{5,13},{6,14},{7,15},{8,0},{9,1},... | collective-permute-start | bytes 36872 | tf_op jit(solution)/shard_map/ppermute | solution.py:342
  12.9 0.0 collective-permute-start.5
  12.9 0.1 collective-permute-start.4
  13.0 0.0 collective-permute-done.7.refs_4_
  13.0 1.7 %collective-permute-done.6.refs_3_ = f32[24,128]{1,0:T(8,128)S(1)} collective-permute-done((f32[24,128]{1,0:T(8,128)S(1)}, f32[24,128]{1,0:T(8,128)S(1)}, u32[]{:S(2)}, u32[]{:S(2)}) %collective-permute-start.6) | collective-permute-done | bytes 12320 | tf_op jit(solution)/shard_map/ppermute | solution.py:342
  14.7 1.3 %collective-permute-done.5.refs_2_ = f32[24,128]{1,0:T(8,128)S(1)} collective-permute-done((f32[24,128]{1,0:T(8,128)S(1)}, f32[24,128]{1,0:T(8,128)S(1)}, u32[]{:S(2)}, u32[]{:S(2)}) %collective-permute-start.5) | collective-permute-done | bytes 12320 | tf_op jit(solution)/shard_map/ppermute | solution.py:342
  16.0 0.0 collective-permute-done.4.refs_1_
  16.0 0.3 shard_map.89.refs_0_.t1
  16.3 0.0 copy-start
  16.3 0.1 collective-permute-start.11
  16.4 2.0 %collective-permute-start.10 = (f32[24,128]{1,0:T(8,128)S(1)}, f32[24,128]{1,0:T(8,128)S(1)}, u32[]{:S(2)}, u32[]{:S(2)}) collective-permute-start(f32[24,128]{1,0:T(8,128)S(1)} %shard_map.89.refs_0_.t1), channel_id=1, source_target_pairs={{0,8},{1,9},{2,10},{3,11},{4,12},{5,13},{6,14},{7,15},{8,0},{9,1},... | collective-permute-start | bytes 36872 | tf_op jit(solution)/shard_map/ppermute | solution.py:342
  18.4 0.0 collective-permute-start.9
  18.4 0.2 collective-permute-start.8
  18.6 0.0 collective-permute-done.11.refs_4_
  18.6 1.6 %collective-permute-done.10.refs_3_ = f32[24,128]{1,0:T(8,128)S(1)} collective-permute-done((f32[24,128]{1,0:T(8,128)S(1)}, f32[24,128]{1,0:T(8,128)S(1)}, u32[]{:S(2)}, u32[]{:S(2)}) %collective-permute-start.10) | collective-permute-done | bytes 12320 | tf_op jit(solution)/shard_map/ppermute | solution.py:342
  20.2 1.3 %collective-permute-done.9.refs_2_ = f32[24,128]{1,0:T(8,128)S(1)} collective-permute-done((f32[24,128]{1,0:T(8,128)S(1)}, f32[24,128]{1,0:T(8,128)S(1)}, u32[]{:S(2)}, u32[]{:S(2)}) %collective-permute-start.9) | collective-permute-done | bytes 12320 | tf_op jit(solution)/shard_map/ppermute | solution.py:342
  21.5 0.0 collective-permute-done.8.refs_1_
  21.5 0.3 shard_map.90.t2.refs_0_
  21.8 0.1 collective-permute-start.15
  22.0 2.1 %collective-permute-start.14 = (f32[24,128]{1,0:T(8,128)S(1)}, f32[24,128]{1,0:T(8,128)S(1)}, u32[]{:S(2)}, u32[]{:S(2)}) collective-permute-start(f32[24,128]{1,0:T(8,128)S(1)} %shard_map.90.t2.refs_0_), channel_id=1, source_target_pairs={{0,8},{1,9},{2,10},{3,11},{4,12},{5,13},{6,14},{7,15},{8,0},{9,1},... | collective-permute-start | bytes 36872 | tf_op jit(solution)/shard_map/ppermute | solution.py:342
  24.1 0.0 collective-permute-start.13
  24.1 0.0 collective-permute-start.12
  24.1 0.0 copy-done
  24.1 0.6 %shard_map.91 = (f32[24,512]{1,0:T(8,128)S(1)}, f32[24,128]{1,0:T(8,128)S(1)}, bf16[512,128]{1,0:T(8,128)(2,1)S(1)}, bf16[512,128]{1,0:T(8,128)(2,1)S(1)}, bf16[512,128]{1,0:T(8,128)(2,1)S(1)}) custom-call(f32[3,32,512]{2,1,0:T(8,128)S(1)} %copy-done, f32[24,128]{1,0:T(8,128)S(1)} %get-tuple-element.19.refs_0_.t0, f32[24,128]{1,0:T(8,128)S(1)} %shard_map.89.refs_0_.t1, ...), custom_call_target="tpu_custom_call" | custom-call | flops 60000000 | bytes 250000 | tf_op jit(solution)/shard_map/pallas_call | solution.py:441
  24.7 0.0 collective-permute-done.15.refs_4_
  24.7 1.2 %collective-permute-done.14.refs_3_ = f32[24,128]{1,0:T(8,128)S(1)} collective-permute-done((f32[24,128]{1,0:T(8,128)S(1)}, f32[24,128]{1,0:T(8,128)S(1)}, u32[]{:S(2)}, u32[]{:S(2)}) %collective-permute-start.14) | collective-permute-done | bytes 12320 | tf_op jit(solution)/shard_map/ppermute | solution.py:342
  25.9 1.3 %collective-permute-done.13.refs_2_ = f32[24,128]{1,0:T(8,128)S(1)} collective-permute-done((f32[24,128]{1,0:T(8,128)S(1)}, f32[24,128]{1,0:T(8,128)S(1)}, u32[]{:S(2)}, u32[]{:S(2)}) %collective-permute-start.13) | collective-permute-done | bytes 12320 | tf_op jit(solution)/shard_map/ppermute | solution.py:342
  27.2 0.0 collective-permute-done.12.refs_1_
  27.2 0.4 shard_map.92
  27.6 0.1 collective-permute-start.16
  27.7 1.2 %collective-permute-done.16 = f32[24,128]{1,0:T(8,128)S(1)} collective-permute-done((f32[24,128]{1,0:T(8,128)S(1)}, f32[24,128]{1,0:T(8,128)S(1)}, u32[]{:S(2)}, u32[]{:S(2)}) %collective-permute-start.16) | collective-permute-done | bytes 12320 | tf_op jit(solution)/shard_map/ppermute | solution.py:342
  28.9 0.4 collective-permute-start.19
  29.2 0.7 %collective-permute-start.18 = (f32[24,128]{1,0:T(8,128)S(1)}, f32[24,128]{1,0:T(8,128)S(1)}, u32[]{:S(2)}, u32[]{:S(2)}) collective-permute-start(f32[24,128]{1,0:T(8,128)S(1)} %add.12), channel_id=1, source_target_pairs={{0,5},{1,4},{2,7},{3,6},{4,1},{5,0},{6,3},{7,2},{8,13},{9,12},{10,... | collective-permute-start | bytes 36872 | tf_op jit(solution)/shard_map/ppermute | solution.py:342
  29.9 1.9 %collective-permute-start.17 = (f32[24,128]{1,0:T(8,128)S(1)}, f32[24,128]{1,0:T(8,128)S(1)}, u32[]{:S(2)}, u32[]{:S(2)}) collective-permute-start(f32[24,128]{1,0:T(8,128)S(1)} %add.12), channel_id=1, source_target_pairs={{0,3},{1,2},{2,1},{3,0},{4,7},{5,6},{6,5},{7,4},{8,11},{9,10},{10,... | collective-permute-start | bytes 36872 | tf_op jit(solution)/shard_map/ppermute | solution.py:342
  31.8 1.1 %collective-permute-done.19 = f32[24,128]{1,0:T(8,128)S(1)} collective-permute-done((f32[24,128]{1,0:T(8,128)S(1)}, f32[24,128]{1,0:T(8,128)S(1)}, u32[]{:S(2)}, u32[]{:S(2)}) %collective-permute-start.19) | collective-permute-done | bytes 12320 | tf_op jit(solution)/shard_map/ppermute | solution.py:342
  33.0 0.0 collective-permute-done.18
  33.0 0.3 collective-permute-done.17
  33.3 1.6 %collective-permute-start.22 = (f32[24,128]{1,0:T(8,128)S(1)}, f32[24,128]{1,0:T(8,128)S(1)}, u32[]{:S(2)}, u32[]{:S(2)}) collective-permute-start(f32[24,128]{1,0:T(8,128)S(1)} %add_add_fusion.refs_0_), channel_id=1, source_target_pairs={{0,25},{1,24},{2,27},{3,26},{4,29},{5,28},{6,31},{7,30},{8,17},{9,... | collective-permute-start | bytes 36872 | tf_op jit(solution)/shard_map/ppermute | solution.py:342
  34.9 0.3 collective-permute-start.21
  35.2 2.1 %collective-permute-start.20 = (f32[24,128]{1,0:T(8,128)S(1)}, f32[24,128]{1,0:T(8,128)S(1)}, u32[]{:S(2)}, u32[]{:S(2)}) collective-permute-start(f32[24,128]{1,0:T(8,128)S(1)} %add_add_fusion.refs_0_), channel_id=1, source_target_pairs={{0,9},{1,8},{2,11},{3,10},{4,13},{5,12},{6,15},{7,14},{8,1},{9,0},... | collective-permute-start | bytes 36872 | tf_op jit(solution)/shard_map/ppermute | solution.py:342
  37.3 0.9 %collective-permute-done.22.refs_3_ = f32[24,128]{1,0:T(8,128)S(1)} collective-permute-done((f32[24,128]{1,0:T(8,128)S(1)}, f32[24,128]{1,0:T(8,128)S(1)}, u32[]{:S(2)}, u32[]{:S(2)}) %collective-permute-start.22) | collective-permute-done | bytes 12320 | tf_op jit(solution)/shard_map/ppermute | solution.py:342
  38.2 0.7 %collective-permute-done.21.refs_2_ = f32[24,128]{1,0:T(8,128)S(1)} collective-permute-done((f32[24,128]{1,0:T(8,128)S(1)}, f32[24,128]{1,0:T(8,128)S(1)}, u32[]{:S(2)}, u32[]{:S(2)}) %collective-permute-start.21) | collective-permute-done | bytes 12320 | tf_op jit(solution)/shard_map/ppermute | solution.py:342
  38.9 0.0 collective-permute-done.20.refs_1_
  38.9 1.0 %shard_map.93 = (f32[3,4,512]{2,1,0:T(4,128)}, f32[3,4,36]{2,1,0:T(4,128)}) custom-call(f32[24,128]{1,0:T(8,128)S(1)} %add_add_fusion.refs_0_, f32[24,128]{1,0:T(8,128)S(1)} %collective-permute-done.20.refs_1_, f32[24,128]{1,0:T(8,128)S(1)} %collective-permute-done.21.refs_2_, f32[24,128]{1,0:T(8,128)S(1)} %collective-permute-done.22.refs_3_, ...), custom_call_target="tpu_custom_call" | custom-call | flops 50000000 | bytes 400000 | tf_op jit(solution)/shard_map/pallas_call | solution.py:458
  (2 shorter events, 0.0 us)
Async XLA Ops:
  1.7 7.4 %collective-permute-start.3 = (f32[32,128]{1,0:T(8,128)S(1)}, f32[32,128]{1,0:T(8,128)S(1)}, u32[]{:S(2)}, u32[]{:S(2)}) collective-permute-start(f32[32,128]{1,0:T(8,128)S(1)} %shard_map.86.refs_0_), channel_id=1, source_target_pairs={{0,1},{1,2},{2,3},{3,0},{4,5},{5,4},{6,7},{7,6},{8,16},{9,17},{10,... | collective-permute-start | bytes 49160 | tf_op jit(solution)/shard_map/ppermute | solution.py:342
  2.2 6.9 %collective-permute-start.2 = (f32[32,128]{1,0:T(8,128)S(1)}, f32[32,128]{1,0:T(8,128)S(1)}, u32[]{:S(2)}, u32[]{:S(2)}) collective-permute-start(f32[32,128]{1,0:T(8,128)S(1)} %shard_map.86.refs_0_), channel_id=1, source_target_pairs={{0,2},{1,0},{2,1},{3,4},{4,3},{5,6},{6,5},{7,8},{8,7},{9,10},{10,9... | collective-permute-start | bytes 49160 | tf_op jit(solution)/shard_map/ppermute | solution.py:342
  4.8 4.5 %collective-permute-start.1 = (f32[32,128]{1,0:T(8,128)S(1)}, f32[32,128]{1,0:T(8,128)S(1)}, u32[]{:S(2)}, u32[]{:S(2)}) collective-permute-start(f32[32,128]{1,0:T(8,128)S(1)} %shard_map.86.refs_0_), channel_id=1, source_target_pairs={{0,8},{1,9},{2,10},{3,11},{4,12},{5,13},{6,14},{7,15},{8,0},{9,1},... | collective-permute-start | bytes 49160 | tf_op jit(solution)/shard_map/ppermute | solution.py:342
  7.2 2.1 %collective-permute-start = (f32[32,128]{1,0:T(8,128)S(1)}, f32[32,128]{1,0:T(8,128)S(1)}, u32[]{:S(2)}, u32[]{:S(2)}) collective-permute-start(f32[32,128]{1,0:T(8,128)S(1)} %shard_map.86.refs_0_), channel_id=1, source_target_pairs={{0,1},{1,0},{2,3},{3,2},{4,5},{5,4},{6,7},{7,6},{8,9},{9,8},{10,11... | collective-permute-start | bytes 49160 | tf_op jit(solution)/shard_map/ppermute | solution.py:342
  9.7 3.3 %collective-permute-start.7 = (f32[24,128]{1,0:T(8,128)S(1)}, f32[24,128]{1,0:T(8,128)S(1)}, u32[]{:S(2)}, u32[]{:S(2)}) collective-permute-start(f32[24,128]{1,0:T(8,128)S(1)} %get-tuple-element.19.refs_0_.t0), channel_id=1, source_target_pairs={{0,2},{1,0},{2,1},{3,4},{4,3},{5,6},{6,5},{7,8},{8,7},{9,10},{10,9... | collective-permute-start | bytes 36872 | tf_op jit(solution)/shard_map/ppermute | solution.py:342
  11.0 3.7 %collective-permute-start.6 = (f32[24,128]{1,0:T(8,128)S(1)}, f32[24,128]{1,0:T(8,128)S(1)}, u32[]{:S(2)}, u32[]{:S(2)}) collective-permute-start(f32[24,128]{1,0:T(8,128)S(1)} %get-tuple-element.19.refs_0_.t0), channel_id=1, source_target_pairs={{0,8},{1,9},{2,10},{3,11},{4,12},{5,13},{6,14},{7,15},{8,0},{9,1},... | collective-permute-start | bytes 36872 | tf_op jit(solution)/shard_map/ppermute | solution.py:342
  12.9 3.1 %collective-permute-start.5 = (f32[24,128]{1,0:T(8,128)S(1)}, f32[24,128]{1,0:T(8,128)S(1)}, u32[]{:S(2)}, u32[]{:S(2)}) collective-permute-start(f32[24,128]{1,0:T(8,128)S(1)} %get-tuple-element.19.refs_0_.t0), channel_id=1, source_target_pairs={{0,1},{1,2},{2,3},{3,0},{4,5},{5,4},{6,7},{7,6},{8,16},{9,17},{10,... | collective-permute-start | bytes 36872 | tf_op jit(solution)/shard_map/ppermute | solution.py:342
  12.9 3.1 %collective-permute-start.4 = (f32[24,128]{1,0:T(8,128)S(1)}, f32[24,128]{1,0:T(8,128)S(1)}, u32[]{:S(2)}, u32[]{:S(2)}) collective-permute-start(f32[24,128]{1,0:T(8,128)S(1)} %get-tuple-element.19.refs_0_.t0), channel_id=1, source_target_pairs={{0,1},{1,0},{2,3},{3,2},{4,5},{5,4},{6,7},{7,6},{8,9},{9,8},{10,11... | collective-permute-start | bytes 36872 | tf_op jit(solution)/shard_map/ppermute | solution.py:342
  16.3 7.8 %copy-start = (f32[3,32,512]{2,1,0:T(8,128)S(1)}, f32[3,32,512]{2,1,0:T(8,128)}, u32[]{:S(2)}) copy-start(f32[3,32,512]{2,1,0:T(8,128)} %refs_4_.1) | copy-start | bytes 589828
  16.3 2.3 %collective-permute-start.11 = (f32[24,128]{1,0:T(8,128)S(1)}, f32[24,128]{1,0:T(8,128)S(1)}, u32[]{:S(2)}, u32[]{:S(2)}) collective-permute-start(f32[24,128]{1,0:T(8,128)S(1)} %shard_map.89.refs_0_.t1), channel_id=1, source_target_pairs={{0,2},{1,0},{2,1},{3,4},{4,3},{5,6},{6,5},{7,8},{8,7},{9,10},{10,9... | collective-permute-start | bytes 36872 | tf_op jit(solution)/shard_map/ppermute | solution.py:342
  16.4 3.8 %collective-permute-start.10 = (f32[24,128]{1,0:T(8,128)S(1)}, f32[24,128]{1,0:T(8,128)S(1)}, u32[]{:S(2)}, u32[]{:S(2)}) collective-permute-start(f32[24,128]{1,0:T(8,128)S(1)} %shard_map.89.refs_0_.t1), channel_id=1, source_target_pairs={{0,8},{1,9},{2,10},{3,11},{4,12},{5,13},{6,14},{7,15},{8,0},{9,1},... | collective-permute-start | bytes 36872 | tf_op jit(solution)/shard_map/ppermute | solution.py:342
  18.4 3.1 %collective-permute-start.9 = (f32[24,128]{1,0:T(8,128)S(1)}, f32[24,128]{1,0:T(8,128)S(1)}, u32[]{:S(2)}, u32[]{:S(2)}) collective-permute-start(f32[24,128]{1,0:T(8,128)S(1)} %shard_map.89.refs_0_.t1), channel_id=1, source_target_pairs={{0,1},{1,2},{2,3},{3,0},{4,5},{5,4},{6,7},{7,6},{8,16},{9,17},{10,... | collective-permute-start | bytes 36872 | tf_op jit(solution)/shard_map/ppermute | solution.py:342
  18.4 3.1 %collective-permute-start.8 = (f32[24,128]{1,0:T(8,128)S(1)}, f32[24,128]{1,0:T(8,128)S(1)}, u32[]{:S(2)}, u32[]{:S(2)}) collective-permute-start(f32[24,128]{1,0:T(8,128)S(1)} %shard_map.89.refs_0_.t1), channel_id=1, source_target_pairs={{0,1},{1,0},{2,3},{3,2},{4,5},{5,4},{6,7},{7,6},{8,9},{9,8},{10,11... | collective-permute-start | bytes 36872 | tf_op jit(solution)/shard_map/ppermute | solution.py:342
  21.8 2.9 %collective-permute-start.15 = (f32[24,128]{1,0:T(8,128)S(1)}, f32[24,128]{1,0:T(8,128)S(1)}, u32[]{:S(2)}, u32[]{:S(2)}) collective-permute-start(f32[24,128]{1,0:T(8,128)S(1)} %shard_map.90.t2.refs_0_), channel_id=1, source_target_pairs={{0,2},{1,0},{2,1},{3,4},{4,3},{5,6},{6,5},{7,8},{8,7},{9,10},{10,9... | collective-permute-start | bytes 36872 | tf_op jit(solution)/shard_map/ppermute | solution.py:342
  22.0 3.9 %collective-permute-start.14 = (f32[24,128]{1,0:T(8,128)S(1)}, f32[24,128]{1,0:T(8,128)S(1)}, u32[]{:S(2)}, u32[]{:S(2)}) collective-permute-start(f32[24,128]{1,0:T(8,128)S(1)} %shard_map.90.t2.refs_0_), channel_id=1, source_target_pairs={{0,8},{1,9},{2,10},{3,11},{4,12},{5,13},{6,14},{7,15},{8,0},{9,1},... | collective-permute-start | bytes 36872 | tf_op jit(solution)/shard_map/ppermute | solution.py:342
  24.1 3.1 %collective-permute-start.13 = (f32[24,128]{1,0:T(8,128)S(1)}, f32[24,128]{1,0:T(8,128)S(1)}, u32[]{:S(2)}, u32[]{:S(2)}) collective-permute-start(f32[24,128]{1,0:T(8,128)S(1)} %shard_map.90.t2.refs_0_), channel_id=1, source_target_pairs={{0,1},{1,2},{2,3},{3,0},{4,5},{5,4},{6,7},{7,6},{8,16},{9,17},{10,... | collective-permute-start | bytes 36872 | tf_op jit(solution)/shard_map/ppermute | solution.py:342
  24.1 3.1 %collective-permute-start.12 = (f32[24,128]{1,0:T(8,128)S(1)}, f32[24,128]{1,0:T(8,128)S(1)}, u32[]{:S(2)}, u32[]{:S(2)}) collective-permute-start(f32[24,128]{1,0:T(8,128)S(1)} %shard_map.90.t2.refs_0_), channel_id=1, source_target_pairs={{0,1},{1,0},{2,3},{3,2},{4,5},{5,4},{6,7},{7,6},{8,9},{9,8},{10,11... | collective-permute-start | bytes 36872 | tf_op jit(solution)/shard_map/ppermute | solution.py:342
  27.6 1.2 %collective-permute-start.16 = (f32[24,128]{1,0:T(8,128)S(1)}, f32[24,128]{1,0:T(8,128)S(1)}, u32[]{:S(2)}, u32[]{:S(2)}) collective-permute-start(f32[24,128]{1,0:T(8,128)S(1)} %get-tuple-element.26), channel_id=1, source_target_pairs={{0,1},{1,0},{2,3},{3,2},{4,5},{5,4},{6,7},{7,6},{8,9},{9,8},{10,11... | collective-permute-start | bytes 36872 | tf_op jit(solution)/shard_map/ppermute | solution.py:342
  28.9 4.1 %collective-permute-start.19 = (f32[24,128]{1,0:T(8,128)S(1)}, f32[24,128]{1,0:T(8,128)S(1)}, u32[]{:S(2)}, u32[]{:S(2)}) collective-permute-start(f32[24,128]{1,0:T(8,128)S(1)} %add.12), channel_id=1, source_target_pairs={{0,7},{1,6},{2,5},{3,4},{4,3},{5,2},{6,1},{7,0},{8,15},{9,14},{10,... | collective-permute-start | bytes 36872 | tf_op jit(solution)/shard_map/ppermute | solution.py:342
  29.2 3.8 %collective-permute-start.18 = (f32[24,128]{1,0:T(8,128)S(1)}, f32[24,128]{1,0:T(8,128)S(1)}, u32[]{:S(2)}, u32[]{:S(2)}) collective-permute-start(f32[24,128]{1,0:T(8,128)S(1)} %add.12), channel_id=1, source_target_pairs={{0,5},{1,4},{2,7},{3,6},{4,1},{5,0},{6,3},{7,2},{8,13},{9,12},{10,... | collective-permute-start | bytes 36872 | tf_op jit(solution)/shard_map/ppermute | solution.py:342
  29.9 3.3 %collective-permute-start.17 = (f32[24,128]{1,0:T(8,128)S(1)}, f32[24,128]{1,0:T(8,128)S(1)}, u32[]{:S(2)}, u32[]{:S(2)}) collective-permute-start(f32[24,128]{1,0:T(8,128)S(1)} %add.12), channel_id=1, source_target_pairs={{0,3},{1,2},{2,1},{3,0},{4,7},{5,6},{6,5},{7,4},{8,11},{9,10},{10,... | collective-permute-start | bytes 36872 | tf_op jit(solution)/shard_map/ppermute | solution.py:342
  33.3 4.9 %collective-permute-start.22 = (f32[24,128]{1,0:T(8,128)S(1)}, f32[24,128]{1,0:T(8,128)S(1)}, u32[]{:S(2)}, u32[]{:S(2)}) collective-permute-start(f32[24,128]{1,0:T(8,128)S(1)} %add_add_fusion.refs_0_), channel_id=1, source_target_pairs={{0,25},{1,24},{2,27},{3,26},{4,29},{5,28},{6,31},{7,30},{8,17},{9,... | collective-permute-start | bytes 36872 | tf_op jit(solution)/shard_map/ppermute | solution.py:342
  34.9 4.1 %collective-permute-start.21 = (f32[24,128]{1,0:T(8,128)S(1)}, f32[24,128]{1,0:T(8,128)S(1)}, u32[]{:S(2)}, u32[]{:S(2)}) collective-permute-start(f32[24,128]{1,0:T(8,128)S(1)} %add_add_fusion.refs_0_), channel_id=1, source_target_pairs={{0,17},{1,16},{2,19},{3,18},{4,21},{5,20},{6,23},{7,22},{8,25},{9,... | collective-permute-start | bytes 36872 | tf_op jit(solution)/shard_map/ppermute | solution.py:342
  35.2 3.7 %collective-permute-start.20 = (f32[24,128]{1,0:T(8,128)S(1)}, f32[24,128]{1,0:T(8,128)S(1)}, u32[]{:S(2)}, u32[]{:S(2)}) collective-permute-start(f32[24,128]{1,0:T(8,128)S(1)} %add_add_fusion.refs_0_), channel_id=1, source_target_pairs={{0,9},{1,8},{2,11},{3,10},{4,13},{5,12},{6,15},{7,14},{8,1},{9,0},... | collective-permute-start | bytes 36872 | tf_op jit(solution)/shard_map/ppermute | solution.py:342

commit v20 on v19

--- a/solution.py
+++ b/solution.py
@@ -312,9 +312,9 @@
     for k in range(S):
         line = jnp.zeros((8, 128), jnp.float32)
         for l in range(k + 1):
-            line = jnp.where(lane == l, lower[k, l], line)
+            line = jnp.where(lane == vecs + l, lower[k, l], line)
         for c in range(comps):
-            factors_ref[c, k : k + 1, vecs:] = line[c : c + 1, :S]
+            factors_ref[c, k : k + 1, vecs:] = line[c : c + 1, vecs : vecs + S]
 
 
 VMEM = pl.BlockSpec(memory_space=pltpu.VMEM)
@@ -414,10 +414,10 @@
         1000000,
         1000000,
         [
-            pltpu.VMEM((4, rows // 4, width), f32),
+            pltpu.VMEM((2, rows // 2, width), f32),
             pltpu.VMEM(columns.shape[::-1], jnp.int32),
             pltpu.SMEM(shifts.shape, f32),
-            dma((6,)),
+            dma((4,)),
         ],
     )(*in_hbm(strips, columns.T, shifts))
     tiles = []

time: 40.1 us -> 40.1 us (level)
  no operation moved by 1% of the time
where the time goes in v20:
time: 40.1 us; the launch traced here: 39.9 us
  starting transfers between devices  20.9 us (52%)
  waiting for transfers between devices  13 us (32%)
  Pallas kernels  5.2 us (13%)
  between operations  0.72 us (2%)
    ppermute x23, starting transfers between devices, send(): lax.ppermute(value, 'dom', [(d, target[d]) for d in range(lax.axis_size('...  20.9 us
    ppermute x23, waiting for transfers between devices, send(): lax.ppermute(value, 'dom', [(d, target[d]) for d in range(lax.axis_size('...  13 us
    pallas_call x1, Pallas kernels, local(): call(prepare_kernel, [((width, rows), bf16), ((width, rows), bf16), ((8 *...  1.28 us
    pallas_call x1, Pallas kernels, local(): call(start_kernel, [((comps * blocks + 8, 128), f32)], [HBM] * 4, 600000,...  1.08 us
    pallas_call x1, Pallas kernels, local(): call(lambda *refs: finish_kernel(total, refs[:count], *refs[count:]), [((...  0.97 us
  transfers between devices with their start and end apart: 23, of which 12 were waited for; matrix products, arithmetic and copies ran while one was open for 0% of the time, Pallas kernels for 5%

profile of v20, /device:TPU:0, one launch (start us, length us, event | category | flops | bytes accessed | tf_op | source)
XLA Modules:
  0.0 39.9 jit_solution(5877671708821235284)
XLA Ops:
  0.6 1.1 %shard_map.86.refs_0_ = f32[32,128]{1,0:T(8,128)S(1)} custom-call(f32[3,32,512]{2,1,0:T(8,128)} %refs_4_.1, f32[3,32]{1,0:T(4,128)} %mix_in.1, s32[1,4,8]{2,1,0:T(4,128)} %list_in.1, s32[1,4]{1,0:T(1,128)} %count_in.1), custom_call_target="tpu_custom_call" | custom-call | flops 600000 | bytes 250000 | tf_op jit(solution)/shard_map/pallas_call | solution.py:396
  1.7 0.5 %collective-permute-start.3 = (f32[32,128]{1,0:T(8,128)S(1)}, f32[32,128]{1,0:T(8,128)S(1)}, u32[]{:S(2)}, u32[]{:S(2)}) collective-permute-start(f32[32,128]{1,0:T(8,128)S(1)} %shard_map.86.refs_0_), channel_id=1, source_target_pairs={{0,1},{1,2},{2,3},{3,0},{4,5},{5,4},{6,7},{7,6},{8,16},{9,17},{10,... | collective-permute-start | bytes 49160 | tf_op jit(solution)/shard_map/ppermute | solution.py:342
  2.2 2.5 %collective-permute-start.2 = (f32[32,128]{1,0:T(8,128)S(1)}, f32[32,128]{1,0:T(8,128)S(1)}, u32[]{:S(2)}, u32[]{:S(2)}) collective-permute-start(f32[32,128]{1,0:T(8,128)S(1)} %shard_map.86.refs_0_), channel_id=1, source_target_pairs={{0,2},{1,0},{2,1},{3,4},{4,3},{5,6},{6,5},{7,8},{8,7},{9,10},{10,9... | collective-permute-start | bytes 49160 | tf_op jit(solution)/shard_map/ppermute | solution.py:342
  4.8 2.5 %collective-permute-start.1 = (f32[32,128]{1,0:T(8,128)S(1)}, f32[32,128]{1,0:T(8,128)S(1)}, u32[]{:S(2)}, u32[]{:S(2)}) collective-permute-start(f32[32,128]{1,0:T(8,128)S(1)} %shard_map.86.refs_0_), channel_id=1, source_target_pairs={{0,8},{1,9},{2,10},{3,11},{4,12},{5,13},{6,14},{7,15},{8,0},{9,1},... | collective-permute-start | bytes 49160 | tf_op jit(solution)/shard_map/ppermute | solution.py:342
  7.2 0.5 %collective-permute-start = (f32[32,128]{1,0:T(8,128)S(1)}, f32[32,128]{1,0:T(8,128)S(1)}, u32[]{:S(2)}, u32[]{:S(2)}) collective-permute-start(f32[32,128]{1,0:T(8,128)S(1)} %shard_map.86.refs_0_), channel_id=1, source_target_pairs={{0,1},{1,0},{2,3},{3,2},{4,5},{5,4},{6,7},{7,6},{8,9},{9,8},{10,11... | collective-permute-start | bytes 49160 | tf_op jit(solution)/shard_map/ppermute | solution.py:342
  7.7 1.3 %shard_map.87 = (bf16[256,512]{1,0:T(8,128)(2,1)S(1)}, bf16[256,512]{1,0:T(8,128)(2,1)S(1)}, f32[56,128]{1,0:T(8,128)S(1)}) custom-call(f32[512,256]{1,0:T(8,128)} %strips_in.1, s32[4,8]{1,0:T(4,128)} %bitcast.2, f32[4]{0:T(128)} %shifts_in.1), custom_call_target="tpu_custom_call" | custom-call | flops 1000000 | bytes 1000000 | tf_op jit(solution)/shard_map/pallas_call | solution.py:410
  9.0 0.0 collective-permute-done.3.refs_4_
  9.0 0.0 collective-permute-done.2.refs_3_
  9.0 0.3 collective-permute-done.1.refs_2_
  9.3 0.0 collective-permute-done.refs_1_
  9.3 0.4 shard_map.88
  9.7 1.2 %collective-permute-start.7 = (f32[24,128]{1,0:T(8,128)S(1)}, f32[24,128]{1,0:T(8,128)S(1)}, u32[]{:S(2)}, u32[]{:S(2)}) collective-permute-start(f32[24,128]{1,0:T(8,128)S(1)} %get-tuple-element.19.refs_0_.t0), channel_id=1, source_target_pairs={{0,2},{1,0},{2,1},{3,4},{4,3},{5,6},{6,5},{7,8},{8,7},{9,10},{10,9... | collective-permute-start | bytes 36872 | tf_op jit(solution)/shard_map/ppermute | solution.py:342
  10.9 2.0 %collective-permute-start.6 = (f32[24,128]{1,0:T(8,128)S(1)}, f32[24,128]{1,0:T(8,128)S(1)}, u32[]{:S(2)}, u32[]{:S(2)}) collective-permute-start(f32[24,128]{1,0:T(8,128)S(1)} %get-tuple-element.19.refs_0_.t0), channel_id=1, source_target_pairs={{0,8},{1,9},{2,10},{3,11},{4,12},{5,13},{6,14},{7,15},{8,0},{9,1},... | collective-permute-start | bytes 36872 | tf_op jit(solution)/shard_map/ppermute | solution.py:342
  12.9 0.0 collective-permute-start.5
  12.9 0.1 collective-permute-start.4
  13.0 0.0 collective-permute-done.7.refs_4_
  13.0 1.7 %collective-permute-done.6.refs_3_ = f32[24,128]{1,0:T(8,128)S(1)} collective-permute-done((f32[24,128]{1,0:T(8,128)S(1)}, f32[24,128]{1,0:T(8,128)S(1)}, u32[]{:S(2)}, u32[]{:S(2)}) %collective-permute-start.6) | collective-permute-done | bytes 12320 | tf_op jit(solution)/shard_map/ppermute | solution.py:342
  14.7 1.3 %collective-permute-done.5.refs_2_ = f32[24,128]{1,0:T(8,128)S(1)} collective-permute-done((f32[24,128]{1,0:T(8,128)S(1)}, f32[24,128]{1,0:T(8,128)S(1)}, u32[]{:S(2)}, u32[]{:S(2)}) %collective-permute-start.5) | collective-permute-done | bytes 12320 | tf_op jit(solution)/shard_map/ppermute | solution.py:342
  16.0 0.0 collective-permute-done.4.refs_1_
  16.0 0.3 shard_map.89.refs_0_.t1
  16.3 0.0 copy-start
  16.3 0.1 collective-permute-start.11
  16.4 2.0 %collective-permute-start.10 = (f32[24,128]{1,0:T(8,128)S(1)}, f32[24,128]{1,0:T(8,128)S(1)}, u32[]{:S(2)}, u32[]{:S(2)}) collective-permute-start(f32[24,128]{1,0:T(8,128)S(1)} %shard_map.89.refs_0_.t1), channel_id=1, source_target_pairs={{0,8},{1,9},{2,10},{3,11},{4,12},{5,13},{6,14},{7,15},{8,0},{9,1},... | collective-permute-start | bytes 36872 | tf_op jit(solution)/shard_map/ppermute | solution.py:342
  18.4 0.0 collective-permute-start.9
  18.4 0.2 collective-permute-start.8
  18.6 0.0 collective-permute-done.11.refs_4_
  18.6 1.6 %collective-permute-done.10.refs_3_ = f32[24,128]{1,0:T(8,128)S(1)} collective-permute-done((f32[24,128]{1,0:T(8,128)S(1)}, f32[24,128]{1,0:T(8,128)S(1)}, u32[]{:S(2)}, u32[]{:S(2)}) %collective-permute-start.10) | collective-permute-done | bytes 12320 | tf_op jit(solution)/shard_map/ppermute | solution.py:342
  20.2 1.3 %collective-permute-done.9.refs_2_ = f32[24,128]{1,0:T(8,128)S(1)} collective-permute-done((f32[24,128]{1,0:T(8,128)S(1)}, f32[24,128]{1,0:T(8,128)S(1)}, u32[]{:S(2)}, u32[]{:S(2)}) %collective-permute-start.9) | collective-permute-done | bytes 12320 | tf_op jit(solution)/shard_map/ppermute | solution.py:342
  21.5 0.0 collective-permute-done.8.refs_1_
  21.5 0.3 shard_map.90.t2.refs_0_
  21.8 0.1 collective-permute-start.15
  22.0 2.1 %collective-permute-start.14 = (f32[24,128]{1,0:T(8,128)S(1)}, f32[24,128]{1,0:T(8,128)S(1)}, u32[]{:S(2)}, u32[]{:S(2)}) collective-permute-start(f32[24,128]{1,0:T(8,128)S(1)} %shard_map.90.t2.refs_0_), channel_id=1, source_target_pairs={{0,8},{1,9},{2,10},{3,11},{4,12},{5,13},{6,14},{7,15},{8,0},{9,1},... | collective-permute-start | bytes 36872 | tf_op jit(solution)/shard_map/ppermute | solution.py:342
  24.1 0.0 collective-permute-start.13
  24.1 0.0 collective-permute-start.12
  24.1 0.0 copy-done
  24.1 0.6 %shard_map.91 = (f32[24,512]{1,0:T(8,128)S(1)}, f32[24,128]{1,0:T(8,128)S(1)}, bf16[512,128]{1,0:T(8,128)(2,1)S(1)}, bf16[512,128]{1,0:T(8,128)(2,1)S(1)}, bf16[512,128]{1,0:T(8,128)(2,1)S(1)}) custom-call(f32[3,32,512]{2,1,0:T(8,128)S(1)} %copy-done, f32[24,128]{1,0:T(8,128)S(1)} %get-tuple-element.19.refs_0_.t0, f32[24,128]{1,0:T(8,128)S(1)} %shard_map.89.refs_0_.t1, ...), custom_call_target="tpu_custom_call" | custom-call | flops 60000000 | bytes 250000 | tf_op jit(solution)/shard_map/pallas_call | solution.py:441
  24.7 0.0 collective-permute-done.15.refs_4_
  24.7 1.2 %collective-permute-done.14.refs_3_ = f32[24,128]{1,0:T(8,128)S(1)} collective-permute-done((f32[24,128]{1,0:T(8,128)S(1)}, f32[24,128]{1,0:T(8,128)S(1)}, u32[]{:S(2)}, u32[]{:S(2)}) %collective-permute-start.14) | collective-permute-done | bytes 12320 | tf_op jit(solution)/shard_map/ppermute | solution.py:342
  25.9 1.3 %collective-permute-done.13.refs_2_ = f32[24,128]{1,0:T(8,128)S(1)} collective-permute-done((f32[24,128]{1,0:T(8,128)S(1)}, f32[24,128]{1,0:T(8,128)S(1)}, u32[]{:S(2)}, u32[]{:S(2)}) %collective-permute-start.13) | collective-permute-done | bytes 12320 | tf_op jit(solution)/shard_map/ppermute | solution.py:342
  27.2 0.0 collective-permute-done.12.refs_1_
  27.2 0.4 shard_map.92
  27.6 0.1 collective-permute-start.16
  27.7 1.2 %collective-permute-done.16 = f32[24,128]{1,0:T(8,128)S(1)} collective-permute-done((f32[24,128]{1,0:T(8,128)S(1)}, f32[24,128]{1,0:T(8,128)S(1)}, u32[]{:S(2)}, u32[]{:S(2)}) %collective-permute-start.16) | collective-permute-done | bytes 12320 | tf_op jit(solution)/shard_map/ppermute | solution.py:342
  28.9 0.4 collective-permute-start.19
  29.2 0.7 %collective-permute-start.18 = (f32[24,128]{1,0:T(8,128)S(1)}, f32[24,128]{1,0:T(8,128)S(1)}, u32[]{:S(2)}, u32[]{:S(2)}) collective-permute-start(f32[24,128]{1,0:T(8,128)S(1)} %add.12), channel_id=1, source_target_pairs={{0,5},{1,4},{2,7},{3,6},{4,1},{5,0},{6,3},{7,2},{8,13},{9,12},{10,... | collective-permute-start | bytes 36872 | tf_op jit(solution)/shard_map/ppermute | solution.py:342
  29.9 1.9 %collective-permute-start.17 = (f32[24,128]{1,0:T(8,128)S(1)}, f32[24,128]{1,0:T(8,128)S(1)}, u32[]{:S(2)}, u32[]{:S(2)}) collective-permute-start(f32[24,128]{1,0:T(8,128)S(1)} %add.12), channel_id=1, source_target_pairs={{0,3},{1,2},{2,1},{3,0},{4,7},{5,6},{6,5},{7,4},{8,11},{9,10},{10,... | collective-permute-start | bytes 36872 | tf_op jit(solution)/shard_map/ppermute | solution.py:342
  31.8 1.1 %collective-permute-done.19 = f32[24,128]{1,0:T(8,128)S(1)} collective-permute-done((f32[24,128]{1,0:T(8,128)S(1)}, f32[24,128]{1,0:T(8,128)S(1)}, u32[]{:S(2)}, u32[]{:S(2)}) %collective-permute-start.19) | collective-permute-done | bytes 12320 | tf_op jit(solution)/shard_map/ppermute | solution.py:342
  33.0 0.0 collective-permute-done.18
  33.0 0.3 collective-permute-done.17
  33.3 1.6 %collective-permute-start.22 = (f32[24,128]{1,0:T(8,128)S(1)}, f32[24,128]{1,0:T(8,128)S(1)}, u32[]{:S(2)}, u32[]{:S(2)}) collective-permute-start(f32[24,128]{1,0:T(8,128)S(1)} %add_add_fusion.refs_0_), channel_id=1, source_target_pairs={{0,25},{1,24},{2,27},{3,26},{4,29},{5,28},{6,31},{7,30},{8,17},{9,... | collective-permute-start | bytes 36872 | tf_op jit(solution)/shard_map/ppermute | solution.py:342
  34.9 0.3 collective-permute-start.21
  35.2 2.1 %collective-permute-start.20 = (f32[24,128]{1,0:T(8,128)S(1)}, f32[24,128]{1,0:T(8,128)S(1)}, u32[]{:S(2)}, u32[]{:S(2)}) collective-permute-start(f32[24,128]{1,0:T(8,128)S(1)} %add_add_fusion.refs_0_), channel_id=1, source_target_pairs={{0,9},{1,8},{2,11},{3,10},{4,13},{5,12},{6,15},{7,14},{8,1},{9,0},... | collective-permute-start | bytes 36872 | tf_op jit(solution)/shard_map/ppermute | solution.py:342
  37.3 0.9 %collective-permute-done.22.refs_3_ = f32[24,128]{1,0:T(8,128)S(1)} collective-permute-done((f32[24,128]{1,0:T(8,128)S(1)}, f32[24,128]{1,0:T(8,128)S(1)}, u32[]{:S(2)}, u32[]{:S(2)}) %collective-permute-start.22) | collective-permute-done | bytes 12320 | tf_op jit(solution)/shard_map/ppermute | solution.py:342
  38.2 0.7 %collective-permute-done.21.refs_2_ = f32[24,128]{1,0:T(8,128)S(1)} collective-permute-done((f32[24,128]{1,0:T(8,128)S(1)}, f32[24,128]{1,0:T(8,128)S(1)}, u32[]{:S(2)}, u32[]{:S(2)}) %collective-permute-start.21) | collective-permute-done | bytes 12320 | tf_op jit(solution)/shard_map/ppermute | solution.py:342
  38.9 0.0 collective-permute-done.20.refs_1_
  38.9 1.0 %shard_map.93 = (f32[3,4,512]{2,1,0:T(4,128)}, f32[3,4,36]{2,1,0:T(4,128)}) custom-call(f32[24,128]{1,0:T(8,128)S(1)} %add_add_fusion.refs_0_, f32[24,128]{1,0:T(8,128)S(1)} %collective-permute-done.20.refs_1_, f32[24,128]{1,0:T(8,128)S(1)} %collective-permute-done.21.refs_2_, f32[24,128]{1,0:T(8,128)S(1)} %collective-permute-done.22.refs_3_, ...), custom_call_target="tpu_custom_call" | custom-call | flops 50000000 | bytes 400000 | tf_op jit(solution)/shard_map/pallas_call | solution.py:458
  (2 shorter events, 0.0 us)
Async XLA Ops:
  1.7 7.3 %collective-permute-start.3 = (f32[32,128]{1,0:T(8,128)S(1)}, f32[32,128]{1,0:T(8,128)S(1)}, u32[]{:S(2)}, u32[]{:S(2)}) collective-permute-start(f32[32,128]{1,0:T(8,128)S(1)} %shard_map.86.refs_0_), channel_id=1, source_target_pairs={{0,1},{1,2},{2,3},{3,0},{4,5},{5,4},{6,7},{7,6},{8,16},{9,17},{10,... | collective-permute-start | bytes 49160 | tf_op jit(solution)/shard_map/ppermute | solution.py:342
  2.2 6.8 %collective-permute-start.2 = (f32[32,128]{1,0:T(8,128)S(1)}, f32[32,128]{1,0:T(8,128)S(1)}, u32[]{:S(2)}, u32[]{:S(2)}) collective-permute-start(f32[32,128]{1,0:T(8,128)S(1)} %shard_map.86.refs_0_), channel_id=1, source_target_pairs={{0,2},{1,0},{2,1},{3,4},{4,3},{5,6},{6,5},{7,8},{8,7},{9,10},{10,9... | collective-permute-start | bytes 49160 | tf_op jit(solution)/shard_map/ppermute | solution.py:342
  4.8 4.5 %collective-permute-start.1 = (f32[32,128]{1,0:T(8,128)S(1)}, f32[32,128]{1,0:T(8,128)S(1)}, u32[]{:S(2)}, u32[]{:S(2)}) collective-permute-start(f32[32,128]{1,0:T(8,128)S(1)} %shard_map.86.refs_0_), channel_id=1, source_target_pairs={{0,8},{1,9},{2,10},{3,11},{4,12},{5,13},{6,14},{7,15},{8,0},{9,1},... | collective-permute-start | bytes 49160 | tf_op jit(solution)/shard_map/ppermute | solution.py:342
  7.2 2.1 %collective-permute-start = (f32[32,128]{1,0:T(8,128)S(1)}, f32[32,128]{1,0:T(8,128)S(1)}, u32[]{:S(2)}, u32[]{:S(2)}) collective-permute-start(f32[32,128]{1,0:T(8,128)S(1)} %shard_map.86.refs_0_), channel_id=1, source_target_pairs={{0,1},{1,0},{2,3},{3,2},{4,5},{5,4},{6,7},{7,6},{8,9},{9,8},{10,11... | collective-permute-start | bytes 49160 | tf_op jit(solution)/shard_map/ppermute | solution.py:342
  9.7 3.3 %collective-permute-start.7 = (f32[24,128]{1,0:T(8,128)S(1)}, f32[24,128]{1,0:T(8,128)S(1)}, u32[]{:S(2)}, u32[]{:S(2)}) collective-permute-start(f32[24,128]{1,0:T(8,128)S(1)} %get-tuple-element.19.refs_0_.t0), channel_id=1, source_target_pairs={{0,2},{1,0},{2,1},{3,4},{4,3},{5,6},{6,5},{7,8},{8,7},{9,10},{10,9... | collective-permute-start | bytes 36872 | tf_op jit(solution)/shard_map/ppermute | solution.py:342
  10.9 3.8 %collective-permute-start.6 = (f32[24,128]{1,0:T(8,128)S(1)}, f32[24,128]{1,0:T(8,128)S(1)}, u32[]{:S(2)}, u32[]{:S(2)}) collective-permute-start(f32[24,128]{1,0:T(8,128)S(1)} %get-tuple-element.19.refs_0_.t0), channel_id=1, source_target_pairs={{0,8},{1,9},{2,10},{3,11},{4,12},{5,13},{6,14},{7,15},{8,0},{9,1},... | collective-permute-start | bytes 36872 | tf_op jit(solution)/shard_map/ppermute | solution.py:342
  12.9 3.1 %collective-permute-start.5 = (f32[24,128]{1,0:T(8,128)S(1)}, f32[24,128]{1,0:T(8,128)S(1)}, u32[]{:S(2)}, u32[]{:S(2)}) collective-permute-start(f32[24,128]{1,0:T(8,128)S(1)} %get-tuple-element.19.refs_0_.t0), channel_id=1, source_target_pairs={{0,1},{1,2},{2,3},{3,0},{4,5},{5,4},{6,7},{7,6},{8,16},{9,17},{10,... | collective-permute-start | bytes 36872 | tf_op jit(solution)/shard_map/ppermute | solution.py:342
  12.9 3.1 %collective-permute-start.4 = (f32[24,128]{1,0:T(8,128)S(1)}, f32[24,128]{1,0:T(8,128)S(1)}, u32[]{:S(2)}, u32[]{:S(2)}) collective-permute-start(f32[24,128]{1,0:T(8,128)S(1)} %get-tuple-element.19.refs_0_.t0), channel_id=1, source_target_pairs={{0,1},{1,0},{2,3},{3,2},{4,5},{5,4},{6,7},{7,6},{8,9},{9,8},{10,11... | collective-permute-start | bytes 36872 | tf_op jit(solution)/shard_map/ppermute | solution.py:342
  16.3 7.8 %copy-start = (f32[3,32,512]{2,1,0:T(8,128)S(1)}, f32[3,32,512]{2,1,0:T(8,128)}, u32[]{:S(2)}) copy-start(f32[3,32,512]{2,1,0:T(8,128)} %refs_4_.1) | copy-start | bytes 589828
  16.3 2.3 %collective-permute-start.11 = (f32[24,128]{1,0:T(8,128)S(1)}, f32[24,128]{1,0:T(8,128)S(1)}, u32[]{:S(2)}, u32[]{:S(2)}) collective-permute-start(f32[24,128]{1,0:T(8,128)S(1)} %shard_map.89.refs_0_.t1), channel_id=1, source_target_pairs={{0,2},{1,0},{2,1},{3,4},{4,3},{5,6},{6,5},{7,8},{8,7},{9,10},{10,9... | collective-permute-start | bytes 36872 | tf_op jit(solution)/shard_map/ppermute | solution.py:342
  16.4 3.8 %collective-permute-start.10 = (f32[24,128]{1,0:T(8,128)S(1)}, f32[24,128]{1,0:T(8,128)S(1)}, u32[]{:S(2)}, u32[]{:S(2)}) collective-permute-start(f32[24,128]{1,0:T(8,128)S(1)} %shard_map.89.refs_0_.t1), channel_id=1, source_target_pairs={{0,8},{1,9},{2,10},{3,11},{4,12},{5,13},{6,14},{7,15},{8,0},{9,1},... | collective-permute-start | bytes 36872 | tf_op jit(solution)/shard_map/ppermute | solution.py:342
  18.4 3.1 %collective-permute-start.9 = (f32[24,128]{1,0:T(8,128)S(1)}, f32[24,128]{1,0:T(8,128)S(1)}, u32[]{:S(2)}, u32[]{:S(2)}) collective-permute-start(f32[24,128]{1,0:T(8,128)S(1)} %shard_map.89.refs_0_.t1), channel_id=1, source_target_pairs={{0,1},{1,2},{2,3},{3,0},{4,5},{5,4},{6,7},{7,6},{8,16},{9,17},{10,... | collective-permute-start | bytes 36872 | tf_op jit(solution)/shard_map/ppermute | solution.py:342
  18.4 3.1 %collective-permute-start.8 = (f32[24,128]{1,0:T(8,128)S(1)}, f32[24,128]{1,0:T(8,128)S(1)}, u32[]{:S(2)}, u32[]{:S(2)}) collective-permute-start(f32[24,128]{1,0:T(8,128)S(1)} %shard_map.89.refs_0_.t1), channel_id=1, source_target_pairs={{0,1},{1,0},{2,3},{3,2},{4,5},{5,4},{6,7},{7,6},{8,9},{9,8},{10,11... | collective-permute-start | bytes 36872 | tf_op jit(solution)/shard_map/ppermute | solution.py:342
  21.8 2.9 %collective-permute-start.15 = (f32[24,128]{1,0:T(8,128)S(1)}, f32[24,128]{1,0:T(8,128)S(1)}, u32[]{:S(2)}, u32[]{:S(2)}) collective-permute-start(f32[24,128]{1,0:T(8,128)S(1)} %shard_map.90.t2.refs_0_), channel_id=1, source_target_pairs={{0,2},{1,0},{2,1},{3,4},{4,3},{5,6},{6,5},{7,8},{8,7},{9,10},{10,9... | collective-permute-start | bytes 36872 | tf_op jit(solution)/shard_map/ppermute | solution.py:342
  22.0 3.9 %collective-permute-start.14 = (f32[24,128]{1,0:T(8,128)S(1)}, f32[24,128]{1,0:T(8,128)S(1)}, u32[]{:S(2)}, u32[]{:S(2)}) collective-permute-start(f32[24,128]{1,0:T(8,128)S(1)} %shard_map.90.t2.refs_0_), channel_id=1, source_target_pairs={{0,8},{1,9},{2,10},{3,11},{4,12},{5,13},{6,14},{7,15},{8,0},{9,1},... | collective-permute-start | bytes 36872 | tf_op jit(solution)/shard_map/ppermute | solution.py:342
  24.1 3.1 %collective-permute-start.13 = (f32[24,128]{1,0:T(8,128)S(1)}, f32[24,128]{1,0:T(8,128)S(1)}, u32[]{:S(2)}, u32[]{:S(2)}) collective-permute-start(f32[24,128]{1,0:T(8,128)S(1)} %shard_map.90.t2.refs_0_), channel_id=1, source_target_pairs={{0,1},{1,2},{2,3},{3,0},{4,5},{5,4},{6,7},{7,6},{8,16},{9,17},{10,... | collective-permute-start | bytes 36872 | tf_op jit(solution)/shard_map/ppermute | solution.py:342
  24.1 3.1 %collective-permute-start.12 = (f32[24,128]{1,0:T(8,128)S(1)}, f32[24,128]{1,0:T(8,128)S(1)}, u32[]{:S(2)}, u32[]{:S(2)}) collective-permute-start(f32[24,128]{1,0:T(8,128)S(1)} %shard_map.90.t2.refs_0_), channel_id=1, source_target_pairs={{0,1},{1,0},{2,3},{3,2},{4,5},{5,4},{6,7},{7,6},{8,9},{9,8},{10,11... | collective-permute-start | bytes 36872 | tf_op jit(solution)/shard_map/ppermute | solution.py:342
  27.6 1.2 %collective-permute-start.16 = (f32[24,128]{1,0:T(8,128)S(1)}, f32[24,128]{1,0:T(8,128)S(1)}, u32[]{:S(2)}, u32[]{:S(2)}) collective-permute-start(f32[24,128]{1,0:T(8,128)S(1)} %get-tuple-element.26), channel_id=1, source_target_pairs={{0,1},{1,0},{2,3},{3,2},{4,5},{5,4},{6,7},{7,6},{8,9},{9,8},{10,11... | collective-permute-start | bytes 36872 | tf_op jit(solution)/shard_map/ppermute | solution.py:342
  28.9 4.1 %collective-permute-start.19 = (f32[24,128]{1,0:T(8,128)S(1)}, f32[24,128]{1,0:T(8,128)S(1)}, u32[]{:S(2)}, u32[]{:S(2)}) collective-permute-start(f32[24,128]{1,0:T(8,128)S(1)} %add.12), channel_id=1, source_target_pairs={{0,7},{1,6},{2,5},{3,4},{4,3},{5,2},{6,1},{7,0},{8,15},{9,14},{10,... | collective-permute-start | bytes 36872 | tf_op jit(solution)/shard_map/ppermute | solution.py:342
  29.2 3.8 %collective-permute-start.18 = (f32[24,128]{1,0:T(8,128)S(1)}, f32[24,128]{1,0:T(8,128)S(1)}, u32[]{:S(2)}, u32[]{:S(2)}) collective-permute-start(f32[24,128]{1,0:T(8,128)S(1)} %add.12), channel_id=1, source_target_pairs={{0,5},{1,4},{2,7},{3,6},{4,1},{5,0},{6,3},{7,2},{8,13},{9,12},{10,... | collective-permute-start | bytes 36872 | tf_op jit(solution)/shard_map/ppermute | solution.py:342
  29.9 3.3 %collective-permute-start.17 = (f32[24,128]{1,0:T(8,128)S(1)}, f32[24,128]{1,0:T(8,128)S(1)}, u32[]{:S(2)}, u32[]{:S(2)}) collective-permute-start(f32[24,128]{1,0:T(8,128)S(1)} %add.12), channel_id=1, source_target_pairs={{0,3},{1,2},{2,1},{3,0},{4,7},{5,6},{6,5},{7,4},{8,11},{9,10},{10,... | collective-permute-start | bytes 36872 | tf_op jit(solution)/shard_map/ppermute | solution.py:342
  33.3 4.9 %collective-permute-start.22 = (f32[24,128]{1,0:T(8,128)S(1)}, f32[24,128]{1,0:T(8,128)S(1)}, u32[]{:S(2)}, u32[]{:S(2)}) collective-permute-start(f32[24,128]{1,0:T(8,128)S(1)} %add_add_fusion.refs_0_), channel_id=1, source_target_pairs={{0,25},{1,24},{2,27},{3,26},{4,29},{5,28},{6,31},{7,30},{8,17},{9,... | collective-permute-start | bytes 36872 | tf_op jit(solution)/shard_map/ppermute | solution.py:342
  34.9 4.1 %collective-permute-start.21 = (f32[24,128]{1,0:T(8,128)S(1)}, f32[24,128]{1,0:T(8,128)S(1)}, u32[]{:S(2)}, u32[]{:S(2)}) collective-permute-start(f32[24,128]{1,0:T(8,128)S(1)} %add_add_fusion.refs_0_), channel_id=1, source_target_pairs={{0,17},{1,16},{2,19},{3,18},{4,21},{5,20},{6,23},{7,22},{8,25},{9,... | collective-permute-start | bytes 36872 | tf_op jit(solution)/shard_map/ppermute | solution.py:342
  35.2 3.7 %collective-permute-start.20 = (f32[24,128]{1,0:T(8,128)S(1)}, f32[24,128]{1,0:T(8,128)S(1)}, u32[]{:S(2)}, u32[]{:S(2)}) collective-permute-start(f32[24,128]{1,0:T(8,128)S(1)} %add_add_fusion.refs_0_), channel_id=1, source_target_pairs={{0,9},{1,8},{2,11},{3,10},{4,13},{5,12},{6,15},{7,14},{8,1},{9,0},... | collective-permute-start | bytes 36872 | tf_op jit(solution)/shard_map/ppermute | solution.py:342

commit v21 on v20

--- a/solution.py
+++ b/solution.py
@@ -108,13 +108,12 @@
 
 
 def prepare_kernel(strips_in, columns_in, shifts_in, high_ref, low_ref, aux_ref, strips, columns, shifts, sems):
-    parts = strips.shape[0]
-    depth = strips.shape[1]
-    pairs = [(columns_in, columns), (shifts_in, shifts)]
-    pairs += [(strips_in.at[pl.ds(p * depth, depth)], strips.at[p]) for p in range(parts)]
-    copies = fetch(pairs, sems)
-    copies[0].wait()
-    copies[1].wait()
+    rows = strips.shape[0]
+    cuts = [(0, rows * 3 // 4), (rows * 3 // 4, rows)]
+    pairs = [(strips_in.at[pl.ds(a, b - a)], strips.at[pl.ds(a, b - a)]) for a, b in cuts]
+    copies = fetch(pairs + [(columns_in, columns), (shifts_in, shifts)], sems)
+    copies[2].wait()
+    copies[3].wait()
     eye = iota((8, 8), 0) == iota((8, 8), 1)
     for k in range(1, columns.shape[0]):
         line = jnp.broadcast_to(columns[k : k + 1, :].astype(jnp.float32), (8, 8))
@@ -123,12 +122,12 @@
         aux_ref[at : at + 8, :] = jnp.broadcast_to(column, (8, 128))
     for k in range(S):
         aux_ref[8 * k : 8 * k + 8, :] = jnp.full((8, 128), shifts[k], jnp.float32)
-    for p in range(parts):
-        copies[2 + p].wait()
-        turned = strips[p].T
+    for copy, (a, b) in zip(copies, cuts):
+        copy.wait()
+        turned = strips[a:b, :].T
         high = turned.astype(jnp.bfloat16)
-        high_ref[:, p * depth : (p + 1) * depth] = high
-        low_ref[:, p * depth : (p + 1) * depth] = (turned - high.astype(jnp.float32)).astype(jnp.bfloat16)
+        high_ref[:, a:b] = high
+        low_ref[:, a:b] = (turned - high.astype(jnp.float32)).astype(jnp.bfloat16)
 
 
 def selection(table, metas, place, length):
@@ -414,7 +413,7 @@
         1000000,
         1000000,
         [
-            pltpu.VMEM((2, rows // 2, width), f32),
+            pltpu.VMEM((rows, width), f32),
             pltpu.VMEM(columns.shape[::-1], jnp.int32),
             pltpu.SMEM(shifts.shape, f32),
             dma((4,)),

time: 40.1 us -> 40.1 us (level)
  no operation moved by 1% of the time
where the time goes in v21:
time: 40.1 us; the launch traced here: 39.9 us
  starting transfers between devices  20.9 us (52%)
  waiting for transfers between devices  13 us (32%)
  Pallas kernels  5.23 us (13%)
  between operations  0.72 us (2%)
    ppermute x23, starting transfers between devices, send(): lax.ppermute(value, 'dom', [(d, target[d]) for d in range(lax.axis_size('...  20.9 us
    ppermute x23, waiting for transfers between devices, send(): lax.ppermute(value, 'dom', [(d, target[d]) for d in range(lax.axis_size('...  13 us
    pallas_call x1, Pallas kernels, local(): call(prepare_kernel, [((width, rows), bf16), ((width, rows), bf16), ((8 *...  1.31 us
    pallas_call x1, Pallas kernels, local(): call(start_kernel, [((comps * blocks + 8, 128), f32)], [HBM] * 4, 600000,...  1.08 us
    pallas_call x1, Pallas kernels, local(): call(lambda *refs: finish_kernel(total, refs[:count], *refs[count:]), [((...  0.97 us
  transfers between devices with their start and end apart: 23, of which 12 were waited for; matrix products, arithmetic and copies ran while one was open for 0% of the time, Pallas kernels for 5%

profile of v21, /device:TPU:0, one launch (start us, length us, event | category | flops | bytes accessed | tf_op | source)
XLA Modules:
  0.0 39.9 jit_solution(4290598045704991488)
XLA Ops:
  0.6 1.1 %shard_map.86.refs_0_ = f32[32,128]{1,0:T(8,128)S(1)} custom-call(f32[3,32,512]{2,1,0:T(8,128)} %refs_4_.1, f32[3,32]{1,0:T(4,128)} %mix_in.1, s32[1,4,8]{2,1,0:T(4,128)} %list_in.1, s32[1,4]{1,0:T(1,128)} %count_in.1), custom_call_target="tpu_custom_call" | custom-call | flops 600000 | bytes 250000 | tf_op jit(solution)/shard_map/pallas_call | solution.py:395
  1.7 0.5 %collective-permute-start.3 = (f32[32,128]{1,0:T(8,128)S(1)}, f32[32,128]{1,0:T(8,128)S(1)}, u32[]{:S(2)}, u32[]{:S(2)}) collective-permute-start(f32[32,128]{1,0:T(8,128)S(1)} %shard_map.86.refs_0_), channel_id=1, source_target_pairs={{0,1},{1,2},{2,3},{3,0},{4,5},{5,4},{6,7},{7,6},{8,16},{9,17},{10,... | collective-permute-start | bytes 49160 | tf_op jit(solution)/shard_map/ppermute | solution.py:341
  2.2 2.5 %collective-permute-start.2 = (f32[32,128]{1,0:T(8,128)S(1)}, f32[32,128]{1,0:T(8,128)S(1)}, u32[]{:S(2)}, u32[]{:S(2)}) collective-permute-start(f32[32,128]{1,0:T(8,128)S(1)} %shard_map.86.refs_0_), channel_id=1, source_target_pairs={{0,2},{1,0},{2,1},{3,4},{4,3},{5,6},{6,5},{7,8},{8,7},{9,10},{10,9... | collective-permute-start | bytes 49160 | tf_op jit(solution)/shard_map/ppermute | solution.py:341
  4.8 2.5 %collective-permute-start.1 = (f32[32,128]{1,0:T(8,128)S(1)}, f32[32,128]{1,0:T(8,128)S(1)}, u32[]{:S(2)}, u32[]{:S(2)}) collective-permute-start(f32[32,128]{1,0:T(8,128)S(1)} %shard_map.86.refs_0_), channel_id=1, source_target_pairs={{0,8},{1,9},{2,10},{3,11},{4,12},{5,13},{6,14},{7,15},{8,0},{9,1},... | collective-permute-start | bytes 49160 | tf_op jit(solution)/shard_map/ppermute | solution.py:341
  7.2 0.5 %collective-permute-start = (f32[32,128]{1,0:T(8,128)S(1)}, f32[32,128]{1,0:T(8,128)S(1)}, u32[]{:S(2)}, u32[]{:S(2)}) collective-permute-start(f32[32,128]{1,0:T(8,128)S(1)} %shard_map.86.refs_0_), channel_id=1, source_target_pairs={{0,1},{1,0},{2,3},{3,2},{4,5},{5,4},{6,7},{7,6},{8,9},{9,8},{10,11... | collective-permute-start | bytes 49160 | tf_op jit(solution)/shard_map/ppermute | solution.py:341
  7.7 1.3 %shard_map.87 = (bf16[256,512]{1,0:T(8,128)(2,1)S(1)}, bf16[256,512]{1,0:T(8,128)(2,1)S(1)}, f32[56,128]{1,0:T(8,128)S(1)}) custom-call(f32[512,256]{1,0:T(8,128)} %strips_in.1, s32[4,8]{1,0:T(4,128)} %bitcast.2, f32[4]{0:T(128)} %shifts_in.1), custom_call_target="tpu_custom_call" | custom-call | flops 1000000 | bytes 1000000 | tf_op jit(solution)/shard_map/pallas_call | solution.py:409
  9.0 0.0 collective-permute-done.3.refs_4_
  9.0 0.0 collective-permute-done.2.refs_3_
  9.0 0.3 collective-permute-done.1.refs_2_
  9.3 0.0 collective-permute-done.refs_1_
  9.3 0.4 shard_map.88
  9.7 1.2 %collective-permute-start.7 = (f32[24,128]{1,0:T(8,128)S(1)}, f32[24,128]{1,0:T(8,128)S(1)}, u32[]{:S(2)}, u32[]{:S(2)}) collective-permute-start(f32[24,128]{1,0:T(8,128)S(1)} %get-tuple-element.19.refs_0_.t0), channel_id=1, source_target_pairs={{0,2},{1,0},{2,1},{3,4},{4,3},{5,6},{6,5},{7,8},{8,7},{9,10},{10,9... | collective-permute-start | bytes 36872 | tf_op jit(solution)/shard_map/ppermute | solution.py:341
  10.9 2.0 %collective-permute-start.6 = (f32[24,128]{1,0:T(8,128)S(1)}, f32[24,128]{1,0:T(8,128)S(1)}, u32[]{:S(2)}, u32[]{:S(2)}) collective-permute-start(f32[24,128]{1,0:T(8,128)S(1)} %get-tuple-element.19.refs_0_.t0), channel_id=1, source_target_pairs={{0,8},{1,9},{2,10},{3,11},{4,12},{5,13},{6,14},{7,15},{8,0},{9,1},... | collective-permute-start | bytes 36872 | tf_op jit(solution)/shard_map/ppermute | solution.py:341
  12.9 0.0 collective-permute-start.5
  12.9 0.1 collective-permute-start.4
  13.0 0.0 collective-permute-done.7.refs_4_
  13.0 1.7 %collective-permute-done.6.refs_3_ = f32[24,128]{1,0:T(8,128)S(1)} collective-permute-done((f32[24,128]{1,0:T(8,128)S(1)}, f32[24,128]{1,0:T(8,128)S(1)}, u32[]{:S(2)}, u32[]{:S(2)}) %collective-permute-start.6) | collective-permute-done | bytes 12320 | tf_op jit(solution)/shard_map/ppermute | solution.py:341
  14.7 1.3 %collective-permute-done.5.refs_2_ = f32[24,128]{1,0:T(8,128)S(1)} collective-permute-done((f32[24,128]{1,0:T(8,128)S(1)}, f32[24,128]{1,0:T(8,128)S(1)}, u32[]{:S(2)}, u32[]{:S(2)}) %collective-permute-start.5) | collective-permute-done | bytes 12320 | tf_op jit(solution)/shard_map/ppermute | solution.py:341
  16.0 0.0 collective-permute-done.4.refs_1_
  16.0 0.3 shard_map.89.refs_0_.t1
  16.3 0.0 copy-start
  16.3 0.1 collective-permute-start.11
  16.4 2.0 %collective-permute-start.10 = (f32[24,128]{1,0:T(8,128)S(1)}, f32[24,128]{1,0:T(8,128)S(1)}, u32[]{:S(2)}, u32[]{:S(2)}) collective-permute-start(f32[24,128]{1,0:T(8,128)S(1)} %shard_map.89.refs_0_.t1), channel_id=1, source_target_pairs={{0,8},{1,9},{2,10},{3,11},{4,12},{5,13},{6,14},{7,15},{8,0},{9,1},... | collective-permute-start | bytes 36872 | tf_op jit(solution)/shard_map/ppermute | solution.py:341
  18.4 0.0 collective-permute-start.9
  18.4 0.2 collective-permute-start.8
  18.6 0.0 collective-permute-done.11.refs_4_
  18.6 1.6 %collective-permute-done.10.refs_3_ = f32[24,128]{1,0:T(8,128)S(1)} collective-permute-done((f32[24,128]{1,0:T(8,128)S(1)}, f32[24,128]{1,0:T(8,128)S(1)}, u32[]{:S(2)}, u32[]{:S(2)}) %collective-permute-start.10) | collective-permute-done | bytes 12320 | tf_op jit(solution)/shard_map/ppermute | solution.py:341
  20.2 1.3 %collective-permute-done.9.refs_2_ = f32[24,128]{1,0:T(8,128)S(1)} collective-permute-done((f32[24,128]{1,0:T(8,128)S(1)}, f32[24,128]{1,0:T(8,128)S(1)}, u32[]{:S(2)}, u32[]{:S(2)}) %collective-permute-start.9) | collective-permute-done | bytes 12320 | tf_op jit(solution)/shard_map/ppermute | solution.py:341
  21.5 0.0 collective-permute-done.8.refs_1_
  21.5 0.3 shard_map.90.t2.refs_0_
  21.8 0.1 collective-permute-start.15
  22.0 2.1 %collective-permute-start.14 = (f32[24,128]{1,0:T(8,128)S(1)}, f32[24,128]{1,0:T(8,128)S(1)}, u32[]{:S(2)}, u32[]{:S(2)}) collective-permute-start(f32[24,128]{1,0:T(8,128)S(1)} %shard_map.90.t2.refs_0_), channel_id=1, source_target_pairs={{0,8},{1,9},{2,10},{3,11},{4,12},{5,13},{6,14},{7,15},{8,0},{9,1},... | collective-permute-start | bytes 36872 | tf_op jit(solution)/shard_map/ppermute | solution.py:341
  24.1 0.0 collective-permute-start.13
  24.1 0.0 collective-permute-start.12
  24.1 0.0 copy-done
  24.1 0.6 %shard_map.91 = (f32[24,512]{1,0:T(8,128)S(1)}, f32[24,128]{1,0:T(8,128)S(1)}, bf16[512,128]{1,0:T(8,128)(2,1)S(1)}, bf16[512,128]{1,0:T(8,128)(2,1)S(1)}, bf16[512,128]{1,0:T(8,128)(2,1)S(1)}) custom-call(f32[3,32,512]{2,1,0:T(8,128)S(1)} %copy-done, f32[24,128]{1,0:T(8,128)S(1)} %get-tuple-element.19.refs_0_.t0, f32[24,128]{1,0:T(8,128)S(1)} %shard_map.89.refs_0_.t1, ...), custom_call_target="tpu_custom_call" | custom-call | flops 60000000 | bytes 250000 | tf_op jit(solution)/shard_map/pallas_call | solution.py:440
  24.7 0.0 collective-permute-done.15.refs_4_
  24.7 1.2 %collective-permute-done.14.refs_3_ = f32[24,128]{1,0:T(8,128)S(1)} collective-permute-done((f32[24,128]{1,0:T(8,128)S(1)}, f32[24,128]{1,0:T(8,128)S(1)}, u32[]{:S(2)}, u32[]{:S(2)}) %collective-permute-start.14) | collective-permute-done | bytes 12320 | tf_op jit(solution)/shard_map/ppermute | solution.py:341
  25.9 1.3 %collective-permute-done.13.refs_2_ = f32[24,128]{1,0:T(8,128)S(1)} collective-permute-done((f32[24,128]{1,0:T(8,128)S(1)}, f32[24,128]{1,0:T(8,128)S(1)}, u32[]{:S(2)}, u32[]{:S(2)}) %collective-permute-start.13) | collective-permute-done | bytes 12320 | tf_op jit(solution)/shard_map/ppermute | solution.py:341
  27.2 0.0 collective-permute-done.12.refs_1_
  27.2 0.4 shard_map.92
  27.6 0.1 collective-permute-start.16
  27.7 1.2 %collective-permute-done.16 = f32[24,128]{1,0:T(8,128)S(1)} collective-permute-done((f32[24,128]{1,0:T(8,128)S(1)}, f32[24,128]{1,0:T(8,128)S(1)}, u32[]{:S(2)}, u32[]{:S(2)}) %collective-permute-start.16) | collective-permute-done | bytes 12320 | tf_op jit(solution)/shard_map/ppermute | solution.py:341
  28.9 0.4 collective-permute-start.19
  29.2 0.7 %collective-permute-start.18 = (f32[24,128]{1,0:T(8,128)S(1)}, f32[24,128]{1,0:T(8,128)S(1)}, u32[]{:S(2)}, u32[]{:S(2)}) collective-permute-start(f32[24,128]{1,0:T(8,128)S(1)} %add.12), channel_id=1, source_target_pairs={{0,5},{1,4},{2,7},{3,6},{4,1},{5,0},{6,3},{7,2},{8,13},{9,12},{10,... | collective-permute-start | bytes 36872 | tf_op jit(solution)/shard_map/ppermute | solution.py:341
  29.9 1.9 %collective-permute-start.17 = (f32[24,128]{1,0:T(8,128)S(1)}, f32[24,128]{1,0:T(8,128)S(1)}, u32[]{:S(2)}, u32[]{:S(2)}) collective-permute-start(f32[24,128]{1,0:T(8,128)S(1)} %add.12), channel_id=1, source_target_pairs={{0,3},{1,2},{2,1},{3,0},{4,7},{5,6},{6,5},{7,4},{8,11},{9,10},{10,... | collective-permute-start | bytes 36872 | tf_op jit(solution)/shard_map/ppermute | solution.py:341
  31.8 1.1 %collective-permute-done.19 = f32[24,128]{1,0:T(8,128)S(1)} collective-permute-done((f32[24,128]{1,0:T(8,128)S(1)}, f32[24,128]{1,0:T(8,128)S(1)}, u32[]{:S(2)}, u32[]{:S(2)}) %collective-permute-start.19) | collective-permute-done | bytes 12320 | tf_op jit(solution)/shard_map/ppermute | solution.py:341
  33.0 0.0 collective-permute-done.18
  33.0 0.3 collective-permute-done.17
  33.3 1.6 %collective-permute-start.22 = (f32[24,128]{1,0:T(8,128)S(1)}, f32[24,128]{1,0:T(8,128)S(1)}, u32[]{:S(2)}, u32[]{:S(2)}) collective-permute-start(f32[24,128]{1,0:T(8,128)S(1)} %add_add_fusion.refs_0_), channel_id=1, source_target_pairs={{0,25},{1,24},{2,27},{3,26},{4,29},{5,28},{6,31},{7,30},{8,17},{9,... | collective-permute-start | bytes 36872 | tf_op jit(solution)/shard_map/ppermute | solution.py:341
  34.9 0.3 collective-permute-start.21
  35.2 2.1 %collective-permute-start.20 = (f32[24,128]{1,0:T(8,128)S(1)}, f32[24,128]{1,0:T(8,128)S(1)}, u32[]{:S(2)}, u32[]{:S(2)}) collective-permute-start(f32[24,128]{1,0:T(8,128)S(1)} %add_add_fusion.refs_0_), channel_id=1, source_target_pairs={{0,9},{1,8},{2,11},{3,10},{4,13},{5,12},{6,15},{7,14},{8,1},{9,0},... | collective-permute-start | bytes 36872 | tf_op jit(solution)/shard_map/ppermute | solution.py:341
  37.3 0.9 %collective-permute-done.22.refs_3_ = f32[24,128]{1,0:T(8,128)S(1)} collective-permute-done((f32[24,128]{1,0:T(8,128)S(1)}, f32[24,128]{1,0:T(8,128)S(1)}, u32[]{:S(2)}, u32[]{:S(2)}) %collective-permute-start.22) | collective-permute-done | bytes 12320 | tf_op jit(solution)/shard_map/ppermute | solution.py:341
  38.2 0.7 %collective-permute-done.21.refs_2_ = f32[24,128]{1,0:T(8,128)S(1)} collective-permute-done((f32[24,128]{1,0:T(8,128)S(1)}, f32[24,128]{1,0:T(8,128)S(1)}, u32[]{:S(2)}, u32[]{:S(2)}) %collective-permute-start.21) | collective-permute-done | bytes 12320 | tf_op jit(solution)/shard_map/ppermute | solution.py:341
  38.9 0.0 collective-permute-done.20.refs_1_
  38.9 1.0 %shard_map.93 = (f32[3,4,512]{2,1,0:T(4,128)}, f32[3,4,36]{2,1,0:T(4,128)}) custom-call(f32[24,128]{1,0:T(8,128)S(1)} %add_add_fusion.refs_0_, f32[24,128]{1,0:T(8,128)S(1)} %collective-permute-done.20.refs_1_, f32[24,128]{1,0:T(8,128)S(1)} %collective-permute-done.21.refs_2_, f32[24,128]{1,0:T(8,128)S(1)} %collective-permute-done.22.refs_3_, ...), custom_call_target="tpu_custom_call" | custom-call | flops 50000000 | bytes 400000 | tf_op jit(solution)/shard_map/pallas_call | solution.py:457
  (2 shorter events, 0.0 us)
Async XLA Ops:
  1.7 7.3 %collective-permute-start.3 = (f32[32,128]{1,0:T(8,128)S(1)}, f32[32,128]{1,0:T(8,128)S(1)}, u32[]{:S(2)}, u32[]{:S(2)}) collective-permute-start(f32[32,128]{1,0:T(8,128)S(1)} %shard_map.86.refs_0_), channel_id=1, source_target_pairs={{0,1},{1,2},{2,3},{3,0},{4,5},{5,4},{6,7},{7,6},{8,16},{9,17},{10,... | collective-permute-start | bytes 49160 | tf_op jit(solution)/shard_map/ppermute | solution.py:341
  2.2 6.8 %collective-permute-start.2 = (f32[32,128]{1,0:T(8,128)S(1)}, f32[32,128]{1,0:T(8,128)S(1)}, u32[]{:S(2)}, u32[]{:S(2)}) collective-permute-start(f32[32,128]{1,0:T(8,128)S(1)} %shard_map.86.refs_0_), channel_id=1, source_target_pairs={{0,2},{1,0},{2,1},{3,4},{4,3},{5,6},{6,5},{7,8},{8,7},{9,10},{10,9... | collective-permute-start | bytes 49160 | tf_op jit(solution)/shard_map/ppermute | solution.py:341
  4.8 4.5 %collective-permute-start.1 = (f32[32,128]{1,0:T(8,128)S(1)}, f32[32,128]{1,0:T(8,128)S(1)}, u32[]{:S(2)}, u32[]{:S(2)}) collective-permute-start(f32[32,128]{1,0:T(8,128)S(1)} %shard_map.86.refs_0_), channel_id=1, source_target_pairs={{0,8},{1,9},{2,10},{3,11},{4,12},{5,13},{6,14},{7,15},{8,0},{9,1},... | collective-permute-start | bytes 49160 | tf_op jit(solution)/shard_map/ppermute | solution.py:341
  7.2 2.1 %collective-permute-start = (f32[32,128]{1,0:T(8,128)S(1)}, f32[32,128]{1,0:T(8,128)S(1)}, u32[]{:S(2)}, u32[]{:S(2)}) collective-permute-start(f32[32,128]{1,0:T(8,128)S(1)} %shard_map.86.refs_0_), channel_id=1, source_target_pairs={{0,1},{1,0},{2,3},{3,2},{4,5},{5,4},{6,7},{7,6},{8,9},{9,8},{10,11... | collective-permute-start | bytes 49160 | tf_op jit(solution)/shard_map/ppermute | solution.py:341
  9.7 3.3 %collective-permute-start.7 = (f32[24,128]{1,0:T(8,128)S(1)}, f32[24,128]{1,0:T(8,128)S(1)}, u32[]{:S(2)}, u32[]{:S(2)}) collective-permute-start(f32[24,128]{1,0:T(8,128)S(1)} %get-tuple-element.19.refs_0_.t0), channel_id=1, source_target_pairs={{0,2},{1,0},{2,1},{3,4},{4,3},{5,6},{6,5},{7,8},{8,7},{9,10},{10,9... | collective-permute-start | bytes 36872 | tf_op jit(solution)/shard_map/ppermute | solution.py:341
  10.9 3.8 %collective-permute-start.6 = (f32[24,128]{1,0:T(8,128)S(1)}, f32[24,128]{1,0:T(8,128)S(1)}, u32[]{:S(2)}, u32[]{:S(2)}) collective-permute-start(f32[24,128]{1,0:T(8,128)S(1)} %get-tuple-element.19.refs_0_.t0), channel_id=1, source_target_pairs={{0,8},{1,9},{2,10},{3,11},{4,12},{5,13},{6,14},{7,15},{8,0},{9,1},... | collective-permute-start | bytes 36872 | tf_op jit(solution)/shard_map/ppermute | solution.py:341
  12.9 3.1 %collective-permute-start.5 = (f32[24,128]{1,0:T(8,128)S(1)}, f32[24,128]{1,0:T(8,128)S(1)}, u32[]{:S(2)}, u32[]{:S(2)}) collective-permute-start(f32[24,128]{1,0:T(8,128)S(1)} %get-tuple-element.19.refs_0_.t0), channel_id=1, source_target_pairs={{0,1},{1,2},{2,3},{3,0},{4,5},{5,4},{6,7},{7,6},{8,16},{9,17},{10,... | collective-permute-start | bytes 36872 | tf_op jit(solution)/shard_map/ppermute | solution.py:341
  12.9 3.1 %collective-permute-start.4 = (f32[24,128]{1,0:T(8,128)S(1)}, f32[24,128]{1,0:T(8,128)S(1)}, u32[]{:S(2)}, u32[]{:S(2)}) collective-permute-start(f32[24,128]{1,0:T(8,128)S(1)} %get-tuple-element.19.refs_0_.t0), channel_id=1, source_target_pairs={{0,1},{1,0},{2,3},{3,2},{4,5},{5,4},{6,7},{7,6},{8,9},{9,8},{10,11... | collective-permute-start | bytes 36872 | tf_op jit(solution)/shard_map/ppermute | solution.py:341
  16.3 7.8 %copy-start = (f32[3,32,512]{2,1,0:T(8,128)S(1)}, f32[3,32,512]{2,1,0:T(8,128)}, u32[]{:S(2)}) copy-start(f32[3,32,512]{2,1,0:T(8,128)} %refs_4_.1) | copy-start | bytes 589828
  16.3 2.3 %collective-permute-start.11 = (f32[24,128]{1,0:T(8,128)S(1)}, f32[24,128]{1,0:T(8,128)S(1)}, u32[]{:S(2)}, u32[]{:S(2)}) collective-permute-start(f32[24,128]{1,0:T(8,128)S(1)} %shard_map.89.refs_0_.t1), channel_id=1, source_target_pairs={{0,2},{1,0},{2,1},{3,4},{4,3},{5,6},{6,5},{7,8},{8,7},{9,10},{10,9... | collective-permute-start | bytes 36872 | tf_op jit(solution)/shard_map/ppermute | solution.py:341
  16.4 3.8 %collective-permute-start.10 = (f32[24,128]{1,0:T(8,128)S(1)}, f32[24,128]{1,0:T(8,128)S(1)}, u32[]{:S(2)}, u32[]{:S(2)}) collective-permute-start(f32[24,128]{1,0:T(8,128)S(1)} %shard_map.89.refs_0_.t1), channel_id=1, source_target_pairs={{0,8},{1,9},{2,10},{3,11},{4,12},{5,13},{6,14},{7,15},{8,0},{9,1},... | collective-permute-start | bytes 36872 | tf_op jit(solution)/shard_map/ppermute | solution.py:341
  18.4 3.1 %collective-permute-start.9 = (f32[24,128]{1,0:T(8,128)S(1)}, f32[24,128]{1,0:T(8,128)S(1)}, u32[]{:S(2)}, u32[]{:S(2)}) collective-permute-start(f32[24,128]{1,0:T(8,128)S(1)} %shard_map.89.refs_0_.t1), channel_id=1, source_target_pairs={{0,1},{1,2},{2,3},{3,0},{4,5},{5,4},{6,7},{7,6},{8,16},{9,17},{10,... | collective-permute-start | bytes 36872 | tf_op jit(solution)/shard_map/ppermute | solution.py:341
  18.4 3.1 %collective-permute-start.8 = (f32[24,128]{1,0:T(8,128)S(1)}, f32[24,128]{1,0:T(8,128)S(1)}, u32[]{:S(2)}, u32[]{:S(2)}) collective-permute-start(f32[24,128]{1,0:T(8,128)S(1)} %shard_map.89.refs_0_.t1), channel_id=1, source_target_pairs={{0,1},{1,0},{2,3},{3,2},{4,5},{5,4},{6,7},{7,6},{8,9},{9,8},{10,11... | collective-permute-start | bytes 36872 | tf_op jit(solution)/shard_map/ppermute | solution.py:341
  21.8 2.9 %collective-permute-start.15 = (f32[24,128]{1,0:T(8,128)S(1)}, f32[24,128]{1,0:T(8,128)S(1)}, u32[]{:S(2)}, u32[]{:S(2)}) collective-permute-start(f32[24,128]{1,0:T(8,128)S(1)} %shard_map.90.t2.refs_0_), channel_id=1, source_target_pairs={{0,2},{1,0},{2,1},{3,4},{4,3},{5,6},{6,5},{7,8},{8,7},{9,10},{10,9... | collective-permute-start | bytes 36872 | tf_op jit(solution)/shard_map/ppermute | solution.py:341
  22.0 3.9 %collective-permute-start.14 = (f32[24,128]{1,0:T(8,128)S(1)}, f32[24,128]{1,0:T(8,128)S(1)}, u32[]{:S(2)}, u32[]{:S(2)}) collective-permute-start(f32[24,128]{1,0:T(8,128)S(1)} %shard_map.90.t2.refs_0_), channel_id=1, source_target_pairs={{0,8},{1,9},{2,10},{3,11},{4,12},{5,13},{6,14},{7,15},{8,0},{9,1},... | collective-permute-start | bytes 36872 | tf_op jit(solution)/shard_map/ppermute | solution.py:341
  24.1 3.1 %collective-permute-start.13 = (f32[24,128]{1,0:T(8,128)S(1)}, f32[24,128]{1,0:T(8,128)S(1)}, u32[]{:S(2)}, u32[]{:S(2)}) collective-permute-start(f32[24,128]{1,0:T(8,128)S(1)} %shard_map.90.t2.refs_0_), channel_id=1, source_target_pairs={{0,1},{1,2},{2,3},{3,0},{4,5},{5,4},{6,7},{7,6},{8,16},{9,17},{10,... | collective-permute-start | bytes 36872 | tf_op jit(solution)/shard_map/ppermute | solution.py:341
  24.1 3.1 %collective-permute-start.12 = (f32[24,128]{1,0:T(8,128)S(1)}, f32[24,128]{1,0:T(8,128)S(1)}, u32[]{:S(2)}, u32[]{:S(2)}) collective-permute-start(f32[24,128]{1,0:T(8,128)S(1)} %shard_map.90.t2.refs_0_), channel_id=1, source_target_pairs={{0,1},{1,0},{2,3},{3,2},{4,5},{5,4},{6,7},{7,6},{8,9},{9,8},{10,11... | collective-permute-start | bytes 36872 | tf_op jit(solution)/shard_map/ppermute | solution.py:341
  27.6 1.2 %collective-permute-start.16 = (f32[24,128]{1,0:T(8,128)S(1)}, f32[24,128]{1,0:T(8,128)S(1)}, u32[]{:S(2)}, u32[]{:S(2)}) collective-permute-start(f32[24,128]{1,0:T(8,128)S(1)} %get-tuple-element.26), channel_id=1, source_target_pairs={{0,1},{1,0},{2,3},{3,2},{4,5},{5,4},{6,7},{7,6},{8,9},{9,8},{10,11... | collective-permute-start | bytes 36872 | tf_op jit(solution)/shard_map/ppermute | solution.py:341
  28.9 4.1 %collective-permute-start.19 = (f32[24,128]{1,0:T(8,128)S(1)}, f32[24,128]{1,0:T(8,128)S(1)}, u32[]{:S(2)}, u32[]{:S(2)}) collective-permute-start(f32[24,128]{1,0:T(8,128)S(1)} %add.12), channel_id=1, source_target_pairs={{0,7},{1,6},{2,5},{3,4},{4,3},{5,2},{6,1},{7,0},{8,15},{9,14},{10,... | collective-permute-start | bytes 36872 | tf_op jit(solution)/shard_map/ppermute | solution.py:341
  29.2 3.8 %collective-permute-start.18 = (f32[24,128]{1,0:T(8,128)S(1)}, f32[24,128]{1,0:T(8,128)S(1)}, u32[]{:S(2)}, u32[]{:S(2)}) collective-permute-start(f32[24,128]{1,0:T(8,128)S(1)} %add.12), channel_id=1, source_target_pairs={{0,5},{1,4},{2,7},{3,6},{4,1},{5,0},{6,3},{7,2},{8,13},{9,12},{10,... | collective-permute-start | bytes 36872 | tf_op jit(solution)/shard_map/ppermute | solution.py:341
  29.9 3.3 %collective-permute-start.17 = (f32[24,128]{1,0:T(8,128)S(1)}, f32[24,128]{1,0:T(8,128)S(1)}, u32[]{:S(2)}, u32[]{:S(2)}) collective-permute-start(f32[24,128]{1,0:T(8,128)S(1)} %add.12), channel_id=1, source_target_pairs={{0,3},{1,2},{2,1},{3,0},{4,7},{5,6},{6,5},{7,4},{8,11},{9,10},{10,... | collective-permute-start | bytes 36872 | tf_op jit(solution)/shard_map/ppermute | solution.py:341
  33.3 4.9 %collective-permute-start.22 = (f32[24,128]{1,0:T(8,128)S(1)}, f32[24,128]{1,0:T(8,128)S(1)}, u32[]{:S(2)}, u32[]{:S(2)}) collective-permute-start(f32[24,128]{1,0:T(8,128)S(1)} %add_add_fusion.refs_0_), channel_id=1, source_target_pairs={{0,25},{1,24},{2,27},{3,26},{4,29},{5,28},{6,31},{7,30},{8,17},{9,... | collective-permute-start | bytes 36872 | tf_op jit(solution)/shard_map/ppermute | solution.py:341
  34.9 4.1 %collective-permute-start.21 = (f32[24,128]{1,0:T(8,128)S(1)}, f32[24,128]{1,0:T(8,128)S(1)}, u32[]{:S(2)}, u32[]{:S(2)}) collective-permute-start(f32[24,128]{1,0:T(8,128)S(1)} %add_add_fusion.refs_0_), channel_id=1, source_target_pairs={{0,17},{1,16},{2,19},{3,18},{4,21},{5,20},{6,23},{7,22},{8,25},{9,... | collective-permute-start | bytes 36872 | tf_op jit(solution)/shard_map/ppermute | solution.py:341
  35.2 3.7 %collective-permute-start.20 = (f32[24,128]{1,0:T(8,128)S(1)}, f32[24,128]{1,0:T(8,128)S(1)}, u32[]{:S(2)}, u32[]{:S(2)}) collective-permute-start(f32[24,128]{1,0:T(8,128)S(1)} %add_add_fusion.refs_0_), channel_id=1, source_target_pairs={{0,9},{1,8},{2,11},{3,10},{4,13},{5,12},{6,15},{7,14},{8,1},{9,0},... | collective-permute-start | bytes 36872 | tf_op jit(solution)/shard_map/ppermute | solution.py:341

commit v22 on v21

--- a/solution.py
+++ b/solution.py
@@ -109,7 +109,7 @@
 
 def prepare_kernel(strips_in, columns_in, shifts_in, high_ref, low_ref, aux_ref, strips, columns, shifts, sems):
     rows = strips.shape[0]
-    cuts = [(0, rows * 3 // 4), (rows * 3 // 4, rows)]
+    cuts = [(0, rows // 2), (rows // 2, rows)]
     pairs = [(strips_in.at[pl.ds(a, b - a)], strips.at[pl.ds(a, b - a)]) for a, b in cuts]
     copies = fetch(pairs + [(columns_in, columns), (shifts_in, shifts)], sems)
     copies[2].wait()

time: 40.1 us -> 40.1 us (level)
  no operation moved by 1% of the time
where the time goes in v22:
time: 40.1 us; the launch traced here: 39.9 us
  starting transfers between devices  20.9 us (52%)
  waiting for transfers between devices  13 us (32%)
  Pallas kernels  5.18 us (13%)
  between operations  0.72 us (2%)
    ppermute x23, starting transfers between devices, send(): lax.ppermute(value, 'dom', [(d, target[d]) for d in range(lax.axis_size('...  20.9 us
    ppermute x23, waiting for transfers between devices, send(): lax.ppermute(value, 'dom', [(d, target[d]) for d in range(lax.axis_size('...  13 us
    pallas_call x1, Pallas kernels, local(): call(prepare_kernel, [((width, rows), bf16), ((width, rows), bf16), ((8 *...  1.26 us
    pallas_call x1, Pallas kernels, local(): call(start_kernel, [((comps * blocks + 8, 128), f32)], [HBM] * 4, 600000,...  1.08 us
    pallas_call x1, Pallas kernels, local(): call(lambda *refs: finish_kernel(total, refs[:count], *refs[count:]), [((...  0.97 us
  transfers between devices with their start and end apart: 23, of which 12 were waited for; matrix products, arithmetic and copies ran while one was open for 0% of the time, Pallas kernels for 5%

profile of v22, /device:TPU:0, one launch (start us, length us, event | category | flops | bytes accessed | tf_op | source)
XLA Modules:
  0.0 39.9 jit_solution(5776940929990617795)
XLA Ops:
  0.6 1.1 %shard_map.86.refs_0_ = f32[32,128]{1,0:T(8,128)S(1)} custom-call(f32[3,32,512]{2,1,0:T(8,128)} %refs_4_.1, f32[3,32]{1,0:T(4,128)} %mix_in.1, s32[1,4,8]{2,1,0:T(4,128)} %list_in.1, s32[1,4]{1,0:T(1,128)} %count_in.1), custom_call_target="tpu_custom_call" | custom-call | flops 600000 | bytes 250000 | tf_op jit(solution)/shard_map/pallas_call | solution.py:395
  1.7 0.5 %collective-permute-start.3 = (f32[32,128]{1,0:T(8,128)S(1)}, f32[32,128]{1,0:T(8,128)S(1)}, u32[]{:S(2)}, u32[]{:S(2)}) collective-permute-start(f32[32,128]{1,0:T(8,128)S(1)} %shard_map.86.refs_0_), channel_id=1, source_target_pairs={{0,1},{1,2},{2,3},{3,0},{4,5},{5,4},{6,7},{7,6},{8,16},{9,17},{10,... | collective-permute-start | bytes 49160 | tf_op jit(solution)/shard_map/ppermute | solution.py:341
  2.2 2.5 %collective-permute-start.2 = (f32[32,128]{1,0:T(8,128)S(1)}, f32[32,128]{1,0:T(8,128)S(1)}, u32[]{:S(2)}, u32[]{:S(2)}) collective-permute-start(f32[32,128]{1,0:T(8,128)S(1)} %shard_map.86.refs_0_), channel_id=1, source_target_pairs={{0,2},{1,0},{2,1},{3,4},{4,3},{5,6},{6,5},{7,8},{8,7},{9,10},{10,9... | collective-permute-start | bytes 49160 | tf_op jit(solution)/shard_map/ppermute | solution.py:341
  4.8 2.5 %collective-permute-start.1 = (f32[32,128]{1,0:T(8,128)S(1)}, f32[32,128]{1,0:T(8,128)S(1)}, u32[]{:S(2)}, u32[]{:S(2)}) collective-permute-start(f32[32,128]{1,0:T(8,128)S(1)} %shard_map.86.refs_0_), channel_id=1, source_target_pairs={{0,8},{1,9},{2,10},{3,11},{4,12},{5,13},{6,14},{7,15},{8,0},{9,1},... | collective-permute-start | bytes 49160 | tf_op jit(solution)/shard_map/ppermute | solution.py:341
  7.2 0.5 %collective-permute-start = (f32[32,128]{1,0:T(8,128)S(1)}, f32[32,128]{1,0:T(8,128)S(1)}, u32[]{:S(2)}, u32[]{:S(2)}) collective-permute-start(f32[32,128]{1,0:T(8,128)S(1)} %shard_map.86.refs_0_), channel_id=1, source_target_pairs={{0,1},{1,0},{2,3},{3,2},{4,5},{5,4},{6,7},{7,6},{8,9},{9,8},{10,11... | collective-permute-start | bytes 49160 | tf_op jit(solution)/shard_map/ppermute | solution.py:341
  7.7 1.3 %shard_map.87 = (bf16[256,512]{1,0:T(8,128)(2,1)S(1)}, bf16[256,512]{1,0:T(8,128)(2,1)S(1)}, f32[56,128]{1,0:T(8,128)S(1)}) custom-call(f32[512,256]{1,0:T(8,128)} %strips_in.1, s32[4,8]{1,0:T(4,128)} %bitcast.2, f32[4]{0:T(128)} %shifts_in.1), custom_call_target="tpu_custom_call" | custom-call | flops 1000000 | bytes 1000000 | tf_op jit(solution)/shard_map/pallas_call | solution.py:409
  9.0 0.0 collective-permute-done.3.refs_4_
  9.0 0.0 collective-permute-done.2.refs_3_
  9.0 0.3 collective-permute-done.1.refs_2_
  9.3 0.0 collective-permute-done.refs_1_
  9.3 0.4 shard_map.88
  9.7 1.2 %collective-permute-start.7 = (f32[24,128]{1,0:T(8,128)S(1)}, f32[24,128]{1,0:T(8,128)S(1)}, u32[]{:S(2)}, u32[]{:S(2)}) collective-permute-start(f32[24,128]{1,0:T(8,128)S(1)} %get-tuple-element.19.refs_0_.t0), channel_id=1, source_target_pairs={{0,2},{1,0},{2,1},{3,4},{4,3},{5,6},{6,5},{7,8},{8,7},{9,10},{10,9... | collective-permute-start | bytes 36872 | tf_op jit(solution)/shard_map/ppermute | solution.py:341
  10.9 2.0 %collective-permute-start.6 = (f32[24,128]{1,0:T(8,128)S(1)}, f32[24,128]{1,0:T(8,128)S(1)}, u32[]{:S(2)}, u32[]{:S(2)}) collective-permute-start(f32[24,128]{1,0:T(8,128)S(1)} %get-tuple-element.19.refs_0_.t0), channel_id=1, source_target_pairs={{0,8},{1,9},{2,10},{3,11},{4,12},{5,13},{6,14},{7,15},{8,0},{9,1},... | collective-permute-start | bytes 36872 | tf_op jit(solution)/shard_map/ppermute | solution.py:341
  12.9 0.0 collective-permute-start.5
  12.9 0.1 collective-permute-start.4
  13.0 0.0 collective-permute-done.7.refs_4_
  13.0 1.7 %collective-permute-done.6.refs_3_ = f32[24,128]{1,0:T(8,128)S(1)} collective-permute-done((f32[24,128]{1,0:T(8,128)S(1)}, f32[24,128]{1,0:T(8,128)S(1)}, u32[]{:S(2)}, u32[]{:S(2)}) %collective-permute-start.6) | collective-permute-done | bytes 12320 | tf_op jit(solution)/shard_map/ppermute | solution.py:341
  14.7 1.3 %collective-permute-done.5.refs_2_ = f32[24,128]{1,0:T(8,128)S(1)} collective-permute-done((f32[24,128]{1,0:T(8,128)S(1)}, f32[24,128]{1,0:T(8,128)S(1)}, u32[]{:S(2)}, u32[]{:S(2)}) %collective-permute-start.5) | collective-permute-done | bytes 12320 | tf_op jit(solution)/shard_map/ppermute | solution.py:341
  16.0 0.0 collective-permute-done.4.refs_1_
  16.0 0.3 shard_map.89.refs_0_.t1
  16.3 0.0 copy-start
  16.3 0.1 collective-permute-start.11
  16.4 2.0 %collective-permute-start.10 = (f32[24,128]{1,0:T(8,128)S(1)}, f32[24,128]{1,0:T(8,128)S(1)}, u32[]{:S(2)}, u32[]{:S(2)}) collective-permute-start(f32[24,128]{1,0:T(8,128)S(1)} %shard_map.89.refs_0_.t1), channel_id=1, source_target_pairs={{0,8},{1,9},{2,10},{3,11},{4,12},{5,13},{6,14},{7,15},{8,0},{9,1},... | collective-permute-start | bytes 36872 | tf_op jit(solution)/shard_map/ppermute | solution.py:341
  18.4 0.0 collective-permute-start.9
  18.4 0.2 collective-permute-start.8
  18.6 0.0 collective-permute-done.11.refs_4_
  18.6 1.6 %collective-permute-done.10.refs_3_ = f32[24,128]{1,0:T(8,128)S(1)} collective-permute-done((f32[24,128]{1,0:T(8,128)S(1)}, f32[24,128]{1,0:T(8,128)S(1)}, u32[]{:S(2)}, u32[]{:S(2)}) %collective-permute-start.10) | collective-permute-done | bytes 12320 | tf_op jit(solution)/shard_map/ppermute | solution.py:341
  20.2 1.3 %collective-permute-done.9.refs_2_ = f32[24,128]{1,0:T(8,128)S(1)} collective-permute-done((f32[24,128]{1,0:T(8,128)S(1)}, f32[24,128]{1,0:T(8,128)S(1)}, u32[]{:S(2)}, u32[]{:S(2)}) %collective-permute-start.9) | collective-permute-done | bytes 12320 | tf_op jit(solution)/shard_map/ppermute | solution.py:341
  21.5 0.0 collective-permute-done.8.refs_1_
  21.5 0.3 shard_map.90.t2.refs_0_
  21.8 0.1 collective-permute-start.15
  22.0 2.1 %collective-permute-start.14 = (f32[24,128]{1,0:T(8,128)S(1)}, f32[24,128]{1,0:T(8,128)S(1)}, u32[]{:S(2)}, u32[]{:S(2)}) collective-permute-start(f32[24,128]{1,0:T(8,128)S(1)} %shard_map.90.t2.refs_0_), channel_id=1, source_target_pairs={{0,8},{1,9},{2,10},{3,11},{4,12},{5,13},{6,14},{7,15},{8,0},{9,1},... | collective-permute-start | bytes 36872 | tf_op jit(solution)/shard_map/ppermute | solution.py:341
  24.1 0.0 collective-permute-start.13
  24.1 0.0 collective-permute-start.12
  24.1 0.0 copy-done
  24.1 0.6 %shard_map.91 = (f32[24,512]{1,0:T(8,128)S(1)}, f32[24,128]{1,0:T(8,128)S(1)}, bf16[512,128]{1,0:T(8,128)(2,1)S(1)}, bf16[512,128]{1,0:T(8,128)(2,1)S(1)}, bf16[512,128]{1,0:T(8,128)(2,1)S(1)}) custom-call(f32[3,32,512]{2,1,0:T(8,128)S(1)} %copy-done, f32[24,128]{1,0:T(8,128)S(1)} %get-tuple-element.19.refs_0_.t0, f32[24,128]{1,0:T(8,128)S(1)} %shard_map.89.refs_0_.t1, ...), custom_call_target="tpu_custom_call" | custom-call | flops 60000000 | bytes 250000 | tf_op jit(solution)/shard_map/pallas_call | solution.py:440
  24.7 0.0 collective-permute-done.15.refs_4_
  24.7 1.2 %collective-permute-done.14.refs_3_ = f32[24,128]{1,0:T(8,128)S(1)} collective-permute-done((f32[24,128]{1,0:T(8,128)S(1)}, f32[24,128]{1,0:T(8,128)S(1)}, u32[]{:S(2)}, u32[]{:S(2)}) %collective-permute-start.14) | collective-permute-done | bytes 12320 | tf_op jit(solution)/shard_map/ppermute | solution.py:341
  25.9 1.3 %collective-permute-done.13.refs_2_ = f32[24,128]{1,0:T(8,128)S(1)} collective-permute-done((f32[24,128]{1,0:T(8,128)S(1)}, f32[24,128]{1,0:T(8,128)S(1)}, u32[]{:S(2)}, u32[]{:S(2)}) %collective-permute-start.13) | collective-permute-done | bytes 12320 | tf_op jit(solution)/shard_map/ppermute | solution.py:341
  27.2 0.0 collective-permute-done.12.refs_1_
  27.2 0.4 shard_map.92
  27.6 0.1 collective-permute-start.16
  27.7 1.2 %collective-permute-done.16 = f32[24,128]{1,0:T(8,128)S(1)} collective-permute-done((f32[24,128]{1,0:T(8,128)S(1)}, f32[24,128]{1,0:T(8,128)S(1)}, u32[]{:S(2)}, u32[]{:S(2)}) %collective-permute-start.16) | collective-permute-done | bytes 12320 | tf_op jit(solution)/shard_map/ppermute | solution.py:341
  28.9 0.4 collective-permute-start.19
  29.2 0.7 %collective-permute-start.18 = (f32[24,128]{1,0:T(8,128)S(1)}, f32[24,128]{1,0:T(8,128)S(1)}, u32[]{:S(2)}, u32[]{:S(2)}) collective-permute-start(f32[24,128]{1,0:T(8,128)S(1)} %add.12), channel_id=1, source_target_pairs={{0,5},{1,4},{2,7},{3,6},{4,1},{5,0},{6,3},{7,2},{8,13},{9,12},{10,... | collective-permute-start | bytes 36872 | tf_op jit(solution)/shard_map/ppermute | solution.py:341
  29.9 1.9 %collective-permute-start.17 = (f32[24,128]{1,0:T(8,128)S(1)}, f32[24,128]{1,0:T(8,128)S(1)}, u32[]{:S(2)}, u32[]{:S(2)}) collective-permute-start(f32[24,128]{1,0:T(8,128)S(1)} %add.12), channel_id=1, source_target_pairs={{0,3},{1,2},{2,1},{3,0},{4,7},{5,6},{6,5},{7,4},{8,11},{9,10},{10,... | collective-permute-start | bytes 36872 | tf_op jit(solution)/shard_map/ppermute | solution.py:341
  31.8 1.1 %collective-permute-done.19 = f32[24,128]{1,0:T(8,128)S(1)} collective-permute-done((f32[24,128]{1,0:T(8,128)S(1)}, f32[24,128]{1,0:T(8,128)S(1)}, u32[]{:S(2)}, u32[]{:S(2)}) %collective-permute-start.19) | collective-permute-done | bytes 12320 | tf_op jit(solution)/shard_map/ppermute | solution.py:341
  33.0 0.0 collective-permute-done.18
  33.0 0.3 collective-permute-done.17
  33.3 1.6 %collective-permute-start.22 = (f32[24,128]{1,0:T(8,128)S(1)}, f32[24,128]{1,0:T(8,128)S(1)}, u32[]{:S(2)}, u32[]{:S(2)}) collective-permute-start(f32[24,128]{1,0:T(8,128)S(1)} %add_add_fusion.refs_0_), channel_id=1, source_target_pairs={{0,25},{1,24},{2,27},{3,26},{4,29},{5,28},{6,31},{7,30},{8,17},{9,... | collective-permute-start | bytes 36872 | tf_op jit(solution)/shard_map/ppermute | solution.py:341
  34.9 0.3 collective-permute-start.21
  35.2 2.1 %collective-permute-start.20 = (f32[24,128]{1,0:T(8,128)S(1)}, f32[24,128]{1,0:T(8,128)S(1)}, u32[]{:S(2)}, u32[]{:S(2)}) collective-permute-start(f32[24,128]{1,0:T(8,128)S(1)} %add_add_fusion.refs_0_), channel_id=1, source_target_pairs={{0,9},{1,8},{2,11},{3,10},{4,13},{5,12},{6,15},{7,14},{8,1},{9,0},... | collective-permute-start | bytes 36872 | tf_op jit(solution)/shard_map/ppermute | solution.py:341
  37.3 0.9 %collective-permute-done.22.refs_3_ = f32[24,128]{1,0:T(8,128)S(1)} collective-permute-done((f32[24,128]{1,0:T(8,128)S(1)}, f32[24,128]{1,0:T(8,128)S(1)}, u32[]{:S(2)}, u32[]{:S(2)}) %collective-permute-start.22) | collective-permute-done | bytes 12320 | tf_op jit(solution)/shard_map/ppermute | solution.py:341
  38.2 0.7 %collective-permute-done.21.refs_2_ = f32[24,128]{1,0:T(8,128)S(1)} collective-permute-done((f32[24,128]{1,0:T(8,128)S(1)}, f32[24,128]{1,0:T(8,128)S(1)}, u32[]{:S(2)}, u32[]{:S(2)}) %collective-permute-start.21) | collective-permute-done | bytes 12320 | tf_op jit(solution)/shard_map/ppermute | solution.py:341
  38.9 0.0 collective-permute-done.20.refs_1_
  38.9 1.0 %shard_map.93 = (f32[3,4,512]{2,1,0:T(4,128)}, f32[3,4,36]{2,1,0:T(4,128)}) custom-call(f32[24,128]{1,0:T(8,128)S(1)} %add_add_fusion.refs_0_, f32[24,128]{1,0:T(8,128)S(1)} %collective-permute-done.20.refs_1_, f32[24,128]{1,0:T(8,128)S(1)} %collective-permute-done.21.refs_2_, f32[24,128]{1,0:T(8,128)S(1)} %collective-permute-done.22.refs_3_, ...), custom_call_target="tpu_custom_call" | custom-call | flops 50000000 | bytes 400000 | tf_op jit(solution)/shard_map/pallas_call | solution.py:457
  (2 shorter events, 0.0 us)
Async XLA Ops:
  1.7 7.2 %collective-permute-start.3 = (f32[32,128]{1,0:T(8,128)S(1)}, f32[32,128]{1,0:T(8,128)S(1)}, u32[]{:S(2)}, u32[]{:S(2)}) collective-permute-start(f32[32,128]{1,0:T(8,128)S(1)} %shard_map.86.refs_0_), channel_id=1, source_target_pairs={{0,1},{1,2},{2,3},{3,0},{4,5},{5,4},{6,7},{7,6},{8,16},{9,17},{10,... | collective-permute-start | bytes 49160 | tf_op jit(solution)/shard_map/ppermute | solution.py:341
  2.2 6.8 %collective-permute-start.2 = (f32[32,128]{1,0:T(8,128)S(1)}, f32[32,128]{1,0:T(8,128)S(1)}, u32[]{:S(2)}, u32[]{:S(2)}) collective-permute-start(f32[32,128]{1,0:T(8,128)S(1)} %shard_map.86.refs_0_), channel_id=1, source_target_pairs={{0,2},{1,0},{2,1},{3,4},{4,3},{5,6},{6,5},{7,8},{8,7},{9,10},{10,9... | collective-permute-start | bytes 49160 | tf_op jit(solution)/shard_map/ppermute | solution.py:341
  4.8 4.5 %collective-permute-start.1 = (f32[32,128]{1,0:T(8,128)S(1)}, f32[32,128]{1,0:T(8,128)S(1)}, u32[]{:S(2)}, u32[]{:S(2)}) collective-permute-start(f32[32,128]{1,0:T(8,128)S(1)} %shard_map.86.refs_0_), channel_id=1, source_target_pairs={{0,8},{1,9},{2,10},{3,11},{4,12},{5,13},{6,14},{7,15},{8,0},{9,1},... | collective-permute-start | bytes 49160 | tf_op jit(solution)/shard_map/ppermute | solution.py:341
  7.2 2.1 %collective-permute-start = (f32[32,128]{1,0:T(8,128)S(1)}, f32[32,128]{1,0:T(8,128)S(1)}, u32[]{:S(2)}, u32[]{:S(2)}) collective-permute-start(f32[32,128]{1,0:T(8,128)S(1)} %shard_map.86.refs_0_), channel_id=1, source_target_pairs={{0,1},{1,0},{2,3},{3,2},{4,5},{5,4},{6,7},{7,6},{8,9},{9,8},{10,11... | collective-permute-start | bytes 49160 | tf_op jit(solution)/shard_map/ppermute | solution.py:341
  9.7 3.3 %collective-permute-start.7 = (f32[24,128]{1,0:T(8,128)S(1)}, f32[24,128]{1,0:T(8,128)S(1)}, u32[]{:S(2)}, u32[]{:S(2)}) collective-permute-start(f32[24,128]{1,0:T(8,128)S(1)} %get-tuple-element.19.refs_0_.t0), channel_id=1, source_target_pairs={{0,2},{1,0},{2,1},{3,4},{4,3},{5,6},{6,5},{7,8},{8,7},{9,10},{10,9... | collective-permute-start | bytes 36872 | tf_op jit(solution)/shard_map/ppermute | solution.py:341
  10.9 3.8 %collective-permute-start.6 = (f32[24,128]{1,0:T(8,128)S(1)}, f32[24,128]{1,0:T(8,128)S(1)}, u32[]{:S(2)}, u32[]{:S(2)}) collective-permute-start(f32[24,128]{1,0:T(8,128)S(1)} %get-tuple-element.19.refs_0_.t0), channel_id=1, source_target_pairs={{0,8},{1,9},{2,10},{3,11},{4,12},{5,13},{6,14},{7,15},{8,0},{9,1},... | collective-permute-start | bytes 36872 | tf_op jit(solution)/shard_map/ppermute | solution.py:341
  12.9 3.1 %collective-permute-start.5 = (f32[24,128]{1,0:T(8,128)S(1)}, f32[24,128]{1,0:T(8,128)S(1)}, u32[]{:S(2)}, u32[]{:S(2)}) collective-permute-start(f32[24,128]{1,0:T(8,128)S(1)} %get-tuple-element.19.refs_0_.t0), channel_id=1, source_target_pairs={{0,1},{1,2},{2,3},{3,0},{4,5},{5,4},{6,7},{7,6},{8,16},{9,17},{10,... | collective-permute-start | bytes 36872 | tf_op jit(solution)/shard_map/ppermute | solution.py:341
  12.9 3.1 %collective-permute-start.4 = (f32[24,128]{1,0:T(8,128)S(1)}, f32[24,128]{1,0:T(8,128)S(1)}, u32[]{:S(2)}, u32[]{:S(2)}) collective-permute-start(f32[24,128]{1,0:T(8,128)S(1)} %get-tuple-element.19.refs_0_.t0), channel_id=1, source_target_pairs={{0,1},{1,0},{2,3},{3,2},{4,5},{5,4},{6,7},{7,6},{8,9},{9,8},{10,11... | collective-permute-start | bytes 36872 | tf_op jit(solution)/shard_map/ppermute | solution.py:341
  16.3 7.8 %copy-start = (f32[3,32,512]{2,1,0:T(8,128)S(1)}, f32[3,32,512]{2,1,0:T(8,128)}, u32[]{:S(2)}) copy-start(f32[3,32,512]{2,1,0:T(8,128)} %refs_4_.1) | copy-start | bytes 589828
  16.3 2.3 %collective-permute-start.11 = (f32[24,128]{1,0:T(8,128)S(1)}, f32[24,128]{1,0:T(8,128)S(1)}, u32[]{:S(2)}, u32[]{:S(2)}) collective-permute-start(f32[24,128]{1,0:T(8,128)S(1)} %shard_map.89.refs_0_.t1), channel_id=1, source_target_pairs={{0,2},{1,0},{2,1},{3,4},{4,3},{5,6},{6,5},{7,8},{8,7},{9,10},{10,9... | collective-permute-start | bytes 36872 | tf_op jit(solution)/shard_map/ppermute | solution.py:341
  16.4 3.8 %collective-permute-start.10 = (f32[24,128]{1,0:T(8,128)S(1)}, f32[24,128]{1,0:T(8,128)S(1)}, u32[]{:S(2)}, u32[]{:S(2)}) collective-permute-start(f32[24,128]{1,0:T(8,128)S(1)} %shard_map.89.refs_0_.t1), channel_id=1, source_target_pairs={{0,8},{1,9},{2,10},{3,11},{4,12},{5,13},{6,14},{7,15},{8,0},{9,1},... | collective-permute-start | bytes 36872 | tf_op jit(solution)/shard_map/ppermute | solution.py:341
  18.4 3.1 %collective-permute-start.9 = (f32[24,128]{1,0:T(8,128)S(1)}, f32[24,128]{1,0:T(8,128)S(1)}, u32[]{:S(2)}, u32[]{:S(2)}) collective-permute-start(f32[24,128]{1,0:T(8,128)S(1)} %shard_map.89.refs_0_.t1), channel_id=1, source_target_pairs={{0,1},{1,2},{2,3},{3,0},{4,5},{5,4},{6,7},{7,6},{8,16},{9,17},{10,... | collective-permute-start | bytes 36872 | tf_op jit(solution)/shard_map/ppermute | solution.py:341
  18.4 3.1 %collective-permute-start.8 = (f32[24,128]{1,0:T(8,128)S(1)}, f32[24,128]{1,0:T(8,128)S(1)}, u32[]{:S(2)}, u32[]{:S(2)}) collective-permute-start(f32[24,128]{1,0:T(8,128)S(1)} %shard_map.89.refs_0_.t1), channel_id=1, source_target_pairs={{0,1},{1,0},{2,3},{3,2},{4,5},{5,4},{6,7},{7,6},{8,9},{9,8},{10,11... | collective-permute-start | bytes 36872 | tf_op jit(solution)/shard_map/ppermute | solution.py:341
  21.8 2.9 %collective-permute-start.15 = (f32[24,128]{1,0:T(8,128)S(1)}, f32[24,128]{1,0:T(8,128)S(1)}, u32[]{:S(2)}, u32[]{:S(2)}) collective-permute-start(f32[24,128]{1,0:T(8,128)S(1)} %shard_map.90.t2.refs_0_), channel_id=1, source_target_pairs={{0,2},{1,0},{2,1},{3,4},{4,3},{5,6},{6,5},{7,8},{8,7},{9,10},{10,9... | collective-permute-start | bytes 36872 | tf_op jit(solution)/shard_map/ppermute | solution.py:341
  22.0 3.9 %collective-permute-start.14 = (f32[24,128]{1,0:T(8,128)S(1)}, f32[24,128]{1,0:T(8,128)S(1)}, u32[]{:S(2)}, u32[]{:S(2)}) collective-permute-start(f32[24,128]{1,0:T(8,128)S(1)} %shard_map.90.t2.refs_0_), channel_id=1, source_target_pairs={{0,8},{1,9},{2,10},{3,11},{4,12},{5,13},{6,14},{7,15},{8,0},{9,1},... | collective-permute-start | bytes 36872 | tf_op jit(solution)/shard_map/ppermute | solution.py:341
  24.1 3.1 %collective-permute-start.13 = (f32[24,128]{1,0:T(8,128)S(1)}, f32[24,128]{1,0:T(8,128)S(1)}, u32[]{:S(2)}, u32[]{:S(2)}) collective-permute-start(f32[24,128]{1,0:T(8,128)S(1)} %shard_map.90.t2.refs_0_), channel_id=1, source_target_pairs={{0,1},{1,2},{2,3},{3,0},{4,5},{5,4},{6,7},{7,6},{8,16},{9,17},{10,... | collective-permute-start | bytes 36872 | tf_op jit(solution)/shard_map/ppermute | solution.py:341
  24.1 3.1 %collective-permute-start.12 = (f32[24,128]{1,0:T(8,128)S(1)}, f32[24,128]{1,0:T(8,128)S(1)}, u32[]{:S(2)}, u32[]{:S(2)}) collective-permute-start(f32[24,128]{1,0:T(8,128)S(1)} %shard_map.90.t2.refs_0_), channel_id=1, source_target_pairs={{0,1},{1,0},{2,3},{3,2},{4,5},{5,4},{6,7},{7,6},{8,9},{9,8},{10,11... | collective-permute-start | bytes 36872 | tf_op jit(solution)/shard_map/ppermute | solution.py:341
  27.6 1.2 %collective-permute-start.16 = (f32[24,128]{1,0:T(8,128)S(1)}, f32[24,128]{1,0:T(8,128)S(1)}, u32[]{:S(2)}, u32[]{:S(2)}) collective-permute-start(f32[24,128]{1,0:T(8,128)S(1)} %get-tuple-element.26), channel_id=1, source_target_pairs={{0,1},{1,0},{2,3},{3,2},{4,5},{5,4},{6,7},{7,6},{8,9},{9,8},{10,11... | collective-permute-start | bytes 36872 | tf_op jit(solution)/shard_map/ppermute | solution.py:341
  28.9 4.1 %collective-permute-start.19 = (f32[24,128]{1,0:T(8,128)S(1)}, f32[24,128]{1,0:T(8,128)S(1)}, u32[]{:S(2)}, u32[]{:S(2)}) collective-permute-start(f32[24,128]{1,0:T(8,128)S(1)} %add.12), channel_id=1, source_target_pairs={{0,7},{1,6},{2,5},{3,4},{4,3},{5,2},{6,1},{7,0},{8,15},{9,14},{10,... | collective-permute-start | bytes 36872 | tf_op jit(solution)/shard_map/ppermute | solution.py:341
  29.2 3.8 %collective-permute-start.18 = (f32[24,128]{1,0:T(8,128)S(1)}, f32[24,128]{1,0:T(8,128)S(1)}, u32[]{:S(2)}, u32[]{:S(2)}) collective-permute-start(f32[24,128]{1,0:T(8,128)S(1)} %add.12), channel_id=1, source_target_pairs={{0,5},{1,4},{2,7},{3,6},{4,1},{5,0},{6,3},{7,2},{8,13},{9,12},{10,... | collective-permute-start | bytes 36872 | tf_op jit(solution)/shard_map/ppermute | solution.py:341
  29.9 3.3 %collective-permute-start.17 = (f32[24,128]{1,0:T(8,128)S(1)}, f32[24,128]{1,0:T(8,128)S(1)}, u32[]{:S(2)}, u32[]{:S(2)}) collective-permute-start(f32[24,128]{1,0:T(8,128)S(1)} %add.12), channel_id=1, source_target_pairs={{0,3},{1,2},{2,1},{3,0},{4,7},{5,6},{6,5},{7,4},{8,11},{9,10},{10,... | collective-permute-start | bytes 36872 | tf_op jit(solution)/shard_map/ppermute | solution.py:341
  33.3 4.9 %collective-permute-start.22 = (f32[24,128]{1,0:T(8,128)S(1)}, f32[24,128]{1,0:T(8,128)S(1)}, u32[]{:S(2)}, u32[]{:S(2)}) collective-permute-start(f32[24,128]{1,0:T(8,128)S(1)} %add_add_fusion.refs_0_), channel_id=1, source_target_pairs={{0,25},{1,24},{2,27},{3,26},{4,29},{5,28},{6,31},{7,30},{8,17},{9,... | collective-permute-start | bytes 36872 | tf_op jit(solution)/shard_map/ppermute | solution.py:341
  34.9 4.1 %collective-permute-start.21 = (f32[24,128]{1,0:T(8,128)S(1)}, f32[24,128]{1,0:T(8,128)S(1)}, u32[]{:S(2)}, u32[]{:S(2)}) collective-permute-start(f32[24,128]{1,0:T(8,128)S(1)} %add_add_fusion.refs_0_), channel_id=1, source_target_pairs={{0,17},{1,16},{2,19},{3,18},{4,21},{5,20},{6,23},{7,22},{8,25},{9,... | collective-permute-start | bytes 36872 | tf_op jit(solution)/shard_map/ppermute | solution.py:341
  35.2 3.7 %collective-permute-start.20 = (f32[24,128]{1,0:T(8,128)S(1)}, f32[24,128]{1,0:T(8,128)S(1)}, u32[]{:S(2)}, u32[]{:S(2)}) collective-permute-start(f32[24,128]{1,0:T(8,128)S(1)} %add_add_fusion.refs_0_), channel_id=1, source_target_pairs={{0,9},{1,8},{2,11},{3,10},{4,13},{5,12},{6,15},{7,14},{8,1},{9,0},... | collective-permute-start | bytes 36872 | tf_op jit(solution)/shard_map/ppermute | solution.py:341

commit v23 on v22

--- a/solution.py
+++ b/solution.py
@@ -96,15 +96,17 @@
     for link in range(4):
         live = slot < jnp.broadcast_to(count_ref[0:1, link : link + 1], slot.shape)
         line = jnp.where(live, order[link : link + 1], DEAD)
-        line = pltpu.roll(jnp.broadcast_to(line, (8, 128)), 8 + 8 * link, 1)
-        meta = jnp.where(iota((8, 128), 1) // 8 == link + 1, line, meta)
-    out_ref[8 * comps :, :] = meta
+        line = pltpu.roll(jnp.broadcast_to(line, (8, 128)), BLOCK + 8 + 8 * link, 1)
+        meta = jnp.where(iota((8, 128), 1) // 8 == BLOCK // 8 + link + 1, line, meta)
     copies[0].wait()
     own = own_lanes(8, rows)
     for c in range(comps):
         start = jnp.sum(weights[c] * prev_ref[c], axis=0, keepdims=True)
         line = jnp.broadcast_to(start, own.shape)
-        out_ref[c * 8 : (c + 1) * 8, :] = fold(jnp.where(own, line, 0.0))
+        part = fold(jnp.where(own, line, 0.0))
+        if c == comps - 1:
+            part = jnp.where(iota((8, 128), 1) < BLOCK, part, meta)
+        out_ref[c * 8 : (c + 1) * 8, :] = part
 
 
 def prepare_kernel(strips_in, columns_in, shifts_in, high_ref, low_ref, aux_ref, strips, columns, shifts, sems):
@@ -188,10 +190,14 @@
 
 
 def first_kernel(length, own, a, c, d, b, aux, high, low, tile_ref, choose_ref):
-    rows = 8 * COMPS
-    refs = (own, a, b, c, d)
-    pieces = [ref[:rows, :] for ref in refs]
-    metas = [ref[rows : rows + 1, :] for ref in refs[1:]]
+    pieces, metas = [], []
+    for ref in (own, a, b, c, d):
+        last = ref[8 * COMPS - 8 :, :]
+        turned = pltpu.roll(last, BLOCK, 1)
+        last = jnp.where(iota((8, 128), 1) < BLOCK, last, turned)
+        pieces.append(jnp.concatenate([ref[: 8 * COMPS - 8, :], last], axis=0))
+        metas.append(turned[:1])
+    metas = metas[1:]
     choose = selection(aux[8 * S :, :], metas, lax.axis_index("dom"), length)
     choose_ref[...] = choose
     tile_ref[...] = multiply(choose, pieces, aux[:8, :], high[...], low[...])
@@ -394,7 +400,7 @@
     tile_out = ((comps * blocks, 128), f32)
     tile = call(
         start_kernel,
-        [((comps * blocks + 8, 128), f32)],
+        [tile_out],
         [HBM] * 4,
         600000,
         250000,

time: 40.1 us -> 40.1 us (level)
  no operation moved by 1% of the time
where the time goes in v23:
time: 40.1 us; the launch traced here: 39.9 us
  starting transfers between devices  21 us (52%)
  waiting for transfers between devices  12.9 us (32%)
  Pallas kernels  5.23 us (13%)
  between operations  0.72 us (2%)
    ppermute x23, starting transfers between devices, send(): lax.ppermute(value, 'dom', [(d, target[d]) for d in range(lax.axis_size('...  21 us
    ppermute x23, waiting for transfers between devices, send(): lax.ppermute(value, 'dom', [(d, target[d]) for d in range(lax.axis_size('...  12.9 us
    pallas_call x1, Pallas kernels, local(): call(prepare_kernel, [((width, rows), bf16), ((width, rows), bf16), ((8 *...  1.26 us
    pallas_call x1, Pallas kernels, local(): call(start_kernel, [tile_out], [HBM] * 4, 600000, 250000, [pltpu.VMEM(pre...  1.08 us
    pallas_call x1, Pallas kernels, local(): call(lambda *refs: finish_kernel(total, refs[:count], *refs[count:]), [((...  0.97 us
  transfers between devices with their start and end apart: 23, of which 12 were waited for; matrix products, arithmetic and copies ran while one was open for 0% of the time, Pallas kernels for 5%

profile of v23, /device:TPU:0, one launch (start us, length us, event | category | flops | bytes accessed | tf_op | source)
XLA Modules:
  0.0 39.9 jit_solution(18060306793581685555)
XLA Ops:
  0.6 1.1 %shard_map.86.refs_0_ = f32[24,128]{1,0:T(8,128)S(1)} custom-call(f32[3,32,512]{2,1,0:T(8,128)} %refs_4_.1, f32[3,32]{1,0:T(4,128)} %mix_in.1, s32[1,4,8]{2,1,0:T(4,128)} %list_in.1, s32[1,4]{1,0:T(1,128)} %count_in.1), custom_call_target="tpu_custom_call" | custom-call | flops 600000 | bytes 250000 | tf_op jit(solution)/shard_map/pallas_call | solution.py:401
  1.7 0.5 %collective-permute-start.3 = (f32[24,128]{1,0:T(8,128)S(1)}, f32[24,128]{1,0:T(8,128)S(1)}, u32[]{:S(2)}, u32[]{:S(2)}) collective-permute-start(f32[24,128]{1,0:T(8,128)S(1)} %shard_map.86.refs_0_), channel_id=1, source_target_pairs={{0,1},{1,2},{2,3},{3,0},{4,5},{5,4},{6,7},{7,6},{8,16},{9,17},{10,... | collective-permute-start | bytes 36872 | tf_op jit(solution)/shard_map/ppermute | solution.py:347
  2.2 2.5 %collective-permute-start.2 = (f32[24,128]{1,0:T(8,128)S(1)}, f32[24,128]{1,0:T(8,128)S(1)}, u32[]{:S(2)}, u32[]{:S(2)}) collective-permute-start(f32[24,128]{1,0:T(8,128)S(1)} %shard_map.86.refs_0_), channel_id=1, source_target_pairs={{0,2},{1,0},{2,1},{3,4},{4,3},{5,6},{6,5},{7,8},{8,7},{9,10},{10,9... | collective-permute-start | bytes 36872 | tf_op jit(solution)/shard_map/ppermute | solution.py:347
  4.8 2.5 %collective-permute-start.1 = (f32[24,128]{1,0:T(8,128)S(1)}, f32[24,128]{1,0:T(8,128)S(1)}, u32[]{:S(2)}, u32[]{:S(2)}) collective-permute-start(f32[24,128]{1,0:T(8,128)S(1)} %shard_map.86.refs_0_), channel_id=1, source_target_pairs={{0,8},{1,9},{2,10},{3,11},{4,12},{5,13},{6,14},{7,15},{8,0},{9,1},... | collective-permute-start | bytes 36872 | tf_op jit(solution)/shard_map/ppermute | solution.py:347
  7.2 0.5 %collective-permute-start = (f32[24,128]{1,0:T(8,128)S(1)}, f32[24,128]{1,0:T(8,128)S(1)}, u32[]{:S(2)}, u32[]{:S(2)}) collective-permute-start(f32[24,128]{1,0:T(8,128)S(1)} %shard_map.86.refs_0_), channel_id=1, source_target_pairs={{0,1},{1,0},{2,3},{3,2},{4,5},{5,4},{6,7},{7,6},{8,9},{9,8},{10,11... | collective-permute-start | bytes 36872 | tf_op jit(solution)/shard_map/ppermute | solution.py:347
  7.7 1.3 %shard_map.87 = (bf16[256,512]{1,0:T(8,128)(2,1)S(1)}, bf16[256,512]{1,0:T(8,128)(2,1)S(1)}, f32[56,128]{1,0:T(8,128)S(1)}) custom-call(f32[512,256]{1,0:T(8,128)} %strips_in.1, s32[4,8]{1,0:T(4,128)} %bitcast.2, f32[4]{0:T(128)} %shifts_in.1), custom_call_target="tpu_custom_call" | custom-call | flops 1000000 | bytes 1000000 | tf_op jit(solution)/shard_map/pallas_call | solution.py:415
  9.0 0.0 collective-permute-done.3.refs_4_
  9.0 0.0 collective-permute-done.2.refs_3_
  9.0 0.2 collective-permute-done.1.refs_2_
  9.2 0.0 collective-permute-done.refs_1_
  9.2 0.4 %shard_map.88 = (f32[24,128]{1,0:T(8,128)S(1)}, s32[24,128]{1,0:T(8,128)S(1)}) custom-call(f32[24,128]{1,0:T(8,128)S(1)} %shard_map.86.refs_0_, f32[24,128]{1,0:T(8,128)S(1)} %collective-permute-done.refs_1_, f32[24,128]{1,0:T(8,128)S(1)} %collective-permute-done.1.refs_2_, f32[24,128]{1,0:T(8,128)S(1)} %collective-permute-done.2.refs_3_, ...), custom_call_target="tpu_custom_call" | custom-call | flops 50000000 | bytes 600000 | tf_op jit(solution)/shard_map/pallas_call | solution.py:431
  9.6 1.3 %collective-permute-start.7 = (f32[24,128]{1,0:T(8,128)S(1)}, f32[24,128]{1,0:T(8,128)S(1)}, u32[]{:S(2)}, u32[]{:S(2)}) collective-permute-start(f32[24,128]{1,0:T(8,128)S(1)} %get-tuple-element.19.refs_0_.t0), channel_id=1, source_target_pairs={{0,2},{1,0},{2,1},{3,4},{4,3},{5,6},{6,5},{7,8},{8,7},{9,10},{10,9... | collective-permute-start | bytes 36872 | tf_op jit(solution)/shard_map/ppermute | solution.py:347
  10.9 2.0 %collective-permute-start.6 = (f32[24,128]{1,0:T(8,128)S(1)}, f32[24,128]{1,0:T(8,128)S(1)}, u32[]{:S(2)}, u32[]{:S(2)}) collective-permute-start(f32[24,128]{1,0:T(8,128)S(1)} %get-tuple-element.19.refs_0_.t0), channel_id=1, source_target_pairs={{0,8},{1,9},{2,10},{3,11},{4,12},{5,13},{6,14},{7,15},{8,0},{9,1},... | collective-permute-start | bytes 36872 | tf_op jit(solution)/shard_map/ppermute | solution.py:347
  12.9 0.0 collective-permute-start.5
  12.9 0.1 collective-permute-start.4
  13.0 0.0 collective-permute-done.7.refs_4_
  13.0 1.7 %collective-permute-done.6.refs_3_ = f32[24,128]{1,0:T(8,128)S(1)} collective-permute-done((f32[24,128]{1,0:T(8,128)S(1)}, f32[24,128]{1,0:T(8,128)S(1)}, u32[]{:S(2)}, u32[]{:S(2)}) %collective-permute-start.6) | collective-permute-done | bytes 12320 | tf_op jit(solution)/shard_map/ppermute | solution.py:347
  14.7 1.3 %collective-permute-done.5.refs_2_ = f32[24,128]{1,0:T(8,128)S(1)} collective-permute-done((f32[24,128]{1,0:T(8,128)S(1)}, f32[24,128]{1,0:T(8,128)S(1)}, u32[]{:S(2)}, u32[]{:S(2)}) %collective-permute-start.5) | collective-permute-done | bytes 12320 | tf_op jit(solution)/shard_map/ppermute | solution.py:347
  16.0 0.0 collective-permute-done.4.refs_1_
  16.0 0.3 shard_map.89.refs_0_.t1
  16.3 0.0 copy-start
  16.3 0.1 collective-permute-start.11
  16.4 2.0 %collective-permute-start.10 = (f32[24,128]{1,0:T(8,128)S(1)}, f32[24,128]{1,0:T(8,128)S(1)}, u32[]{:S(2)}, u32[]{:S(2)}) collective-permute-start(f32[24,128]{1,0:T(8,128)S(1)} %shard_map.89.refs_0_.t1), channel_id=1, source_target_pairs={{0,8},{1,9},{2,10},{3,11},{4,12},{5,13},{6,14},{7,15},{8,0},{9,1},... | collective-permute-start | bytes 36872 | tf_op jit(solution)/shard_map/ppermute | solution.py:347
  18.4 0.0 collective-permute-start.9
  18.4 0.2 collective-permute-start.8
  18.6 0.0 collective-permute-done.11.refs_4_
  18.6 1.6 %collective-permute-done.10.refs_3_ = f32[24,128]{1,0:T(8,128)S(1)} collective-permute-done((f32[24,128]{1,0:T(8,128)S(1)}, f32[24,128]{1,0:T(8,128)S(1)}, u32[]{:S(2)}, u32[]{:S(2)}) %collective-permute-start.10) | collective-permute-done | bytes 12320 | tf_op jit(solution)/shard_map/ppermute | solution.py:347
  20.2 1.3 %collective-permute-done.9.refs_2_ = f32[24,128]{1,0:T(8,128)S(1)} collective-permute-done((f32[24,128]{1,0:T(8,128)S(1)}, f32[24,128]{1,0:T(8,128)S(1)}, u32[]{:S(2)}, u32[]{:S(2)}) %collective-permute-start.9) | collective-permute-done | bytes 12320 | tf_op jit(solution)/shard_map/ppermute | solution.py:347
  21.6 0.0 collective-permute-done.8.refs_1_
  21.6 0.3 shard_map.90.t2.refs_0_
  21.8 0.1 collective-permute-start.15
  22.0 2.1 %collective-permute-start.14 = (f32[24,128]{1,0:T(8,128)S(1)}, f32[24,128]{1,0:T(8,128)S(1)}, u32[]{:S(2)}, u32[]{:S(2)}) collective-permute-start(f32[24,128]{1,0:T(8,128)S(1)} %shard_map.90.t2.refs_0_), channel_id=1, source_target_pairs={{0,8},{1,9},{2,10},{3,11},{4,12},{5,13},{6,14},{7,15},{8,0},{9,1},... | collective-permute-start | bytes 36872 | tf_op jit(solution)/shard_map/ppermute | solution.py:347
  24.1 0.0 collective-permute-start.13
  24.1 0.0 collective-permute-start.12
  24.1 0.0 copy-done
  24.1 0.6 %shard_map.91 = (f32[24,512]{1,0:T(8,128)S(1)}, f32[24,128]{1,0:T(8,128)S(1)}, bf16[512,128]{1,0:T(8,128)(2,1)S(1)}, bf16[512,128]{1,0:T(8,128)(2,1)S(1)}, bf16[512,128]{1,0:T(8,128)(2,1)S(1)}) custom-call(f32[3,32,512]{2,1,0:T(8,128)S(1)} %copy-done, f32[24,128]{1,0:T(8,128)S(1)} %get-tuple-element.19.refs_0_.t0, f32[24,128]{1,0:T(8,128)S(1)} %shard_map.89.refs_0_.t1, ...), custom_call_target="tpu_custom_call" | custom-call | flops 60000000 | bytes 250000 | tf_op jit(solution)/shard_map/pallas_call | solution.py:446
  24.7 0.0 collective-permute-done.15.refs_4_
  24.7 1.2 %collective-permute-done.14.refs_3_ = f32[24,128]{1,0:T(8,128)S(1)} collective-permute-done((f32[24,128]{1,0:T(8,128)S(1)}, f32[24,128]{1,0:T(8,128)S(1)}, u32[]{:S(2)}, u32[]{:S(2)}) %collective-permute-start.14) | collective-permute-done | bytes 12320 | tf_op jit(solution)/shard_map/ppermute | solution.py:347
  25.9 1.3 %collective-permute-done.13.refs_2_ = f32[24,128]{1,0:T(8,128)S(1)} collective-permute-done((f32[24,128]{1,0:T(8,128)S(1)}, f32[24,128]{1,0:T(8,128)S(1)}, u32[]{:S(2)}, u32[]{:S(2)}) %collective-permute-start.13) | collective-permute-done | bytes 12320 | tf_op jit(solution)/shard_map/ppermute | solution.py:347
  27.2 0.0 collective-permute-done.12.refs_1_
  27.2 0.4 shard_map.92
  27.6 0.1 collective-permute-start.16
  27.7 1.2 %collective-permute-done.16 = f32[24,128]{1,0:T(8,128)S(1)} collective-permute-done((f32[24,128]{1,0:T(8,128)S(1)}, f32[24,128]{1,0:T(8,128)S(1)}, u32[]{:S(2)}, u32[]{:S(2)}) %collective-permute-start.16) | collective-permute-done | bytes 12320 | tf_op jit(solution)/shard_map/ppermute | solution.py:347
  28.9 0.4 collective-permute-start.19
  29.2 0.7 %collective-permute-start.18 = (f32[24,128]{1,0:T(8,128)S(1)}, f32[24,128]{1,0:T(8,128)S(1)}, u32[]{:S(2)}, u32[]{:S(2)}) collective-permute-start(f32[24,128]{1,0:T(8,128)S(1)} %add.12), channel_id=1, source_target_pairs={{0,5},{1,4},{2,7},{3,6},{4,1},{5,0},{6,3},{7,2},{8,13},{9,12},{10,... | collective-permute-start | bytes 36872 | tf_op jit(solution)/shard_map/ppermute | solution.py:347
  29.9 1.9 %collective-permute-start.17 = (f32[24,128]{1,0:T(8,128)S(1)}, f32[24,128]{1,0:T(8,128)S(1)}, u32[]{:S(2)}, u32[]{:S(2)}) collective-permute-start(f32[24,128]{1,0:T(8,128)S(1)} %add.12), channel_id=1, source_target_pairs={{0,3},{1,2},{2,1},{3,0},{4,7},{5,6},{6,5},{7,4},{8,11},{9,10},{10,... | collective-permute-start | bytes 36872 | tf_op jit(solution)/shard_map/ppermute | solution.py:347
  31.8 1.1 %collective-permute-done.19 = f32[24,128]{1,0:T(8,128)S(1)} collective-permute-done((f32[24,128]{1,0:T(8,128)S(1)}, f32[24,128]{1,0:T(8,128)S(1)}, u32[]{:S(2)}, u32[]{:S(2)}) %collective-permute-start.19) | collective-permute-done | bytes 12320 | tf_op jit(solution)/shard_map/ppermute | solution.py:347
  33.0 0.0 collective-permute-done.18
  33.0 0.3 collective-permute-done.17
  33.3 1.6 %collective-permute-start.22 = (f32[24,128]{1,0:T(8,128)S(1)}, f32[24,128]{1,0:T(8,128)S(1)}, u32[]{:S(2)}, u32[]{:S(2)}) collective-permute-start(f32[24,128]{1,0:T(8,128)S(1)} %add_add_fusion.refs_0_), channel_id=1, source_target_pairs={{0,25},{1,24},{2,27},{3,26},{4,29},{5,28},{6,31},{7,30},{8,17},{9,... | collective-permute-start | bytes 36872 | tf_op jit(solution)/shard_map/ppermute | solution.py:347
  34.9 0.3 collective-permute-start.21
  35.2 2.1 %collective-permute-start.20 = (f32[24,128]{1,0:T(8,128)S(1)}, f32[24,128]{1,0:T(8,128)S(1)}, u32[]{:S(2)}, u32[]{:S(2)}) collective-permute-start(f32[24,128]{1,0:T(8,128)S(1)} %add_add_fusion.refs_0_), channel_id=1, source_target_pairs={{0,9},{1,8},{2,11},{3,10},{4,13},{5,12},{6,15},{7,14},{8,1},{9,0},... | collective-permute-start | bytes 36872 | tf_op jit(solution)/shard_map/ppermute | solution.py:347
  37.3 0.9 %collective-permute-done.22.refs_3_ = f32[24,128]{1,0:T(8,128)S(1)} collective-permute-done((f32[24,128]{1,0:T(8,128)S(1)}, f32[24,128]{1,0:T(8,128)S(1)}, u32[]{:S(2)}, u32[]{:S(2)}) %collective-permute-start.22) | collective-permute-done | bytes 12320 | tf_op jit(solution)/shard_map/ppermute | solution.py:347
  38.2 0.7 %collective-permute-done.21.refs_2_ = f32[24,128]{1,0:T(8,128)S(1)} collective-permute-done((f32[24,128]{1,0:T(8,128)S(1)}, f32[24,128]{1,0:T(8,128)S(1)}, u32[]{:S(2)}, u32[]{:S(2)}) %collective-permute-start.21) | collective-permute-done | bytes 12320 | tf_op jit(solution)/shard_map/ppermute | solution.py:347
  38.9 0.0 collective-permute-done.20.refs_1_
  38.9 1.0 %shard_map.93 = (f32[3,4,512]{2,1,0:T(4,128)}, f32[3,4,36]{2,1,0:T(4,128)}) custom-call(f32[24,128]{1,0:T(8,128)S(1)} %add_add_fusion.refs_0_, f32[24,128]{1,0:T(8,128)S(1)} %collective-permute-done.20.refs_1_, f32[24,128]{1,0:T(8,128)S(1)} %collective-permute-done.21.refs_2_, f32[24,128]{1,0:T(8,128)S(1)} %collective-permute-done.22.refs_3_, ...), custom_call_target="tpu_custom_call" | custom-call | flops 50000000 | bytes 400000 | tf_op jit(solution)/shard_map/pallas_call | solution.py:463
  (2 shorter events, 0.0 us)
Async XLA Ops:
  1.7 7.2 %collective-permute-start.3 = (f32[24,128]{1,0:T(8,128)S(1)}, f32[24,128]{1,0:T(8,128)S(1)}, u32[]{:S(2)}, u32[]{:S(2)}) collective-permute-start(f32[24,128]{1,0:T(8,128)S(1)} %shard_map.86.refs_0_), channel_id=1, source_target_pairs={{0,1},{1,2},{2,3},{3,0},{4,5},{5,4},{6,7},{7,6},{8,16},{9,17},{10,... | collective-permute-start | bytes 36872 | tf_op jit(solution)/shard_map/ppermute | solution.py:347
  2.2 6.8 %collective-permute-start.2 = (f32[24,128]{1,0:T(8,128)S(1)}, f32[24,128]{1,0:T(8,128)S(1)}, u32[]{:S(2)}, u32[]{:S(2)}) collective-permute-start(f32[24,128]{1,0:T(8,128)S(1)} %shard_map.86.refs_0_), channel_id=1, source_target_pairs={{0,2},{1,0},{2,1},{3,4},{4,3},{5,6},{6,5},{7,8},{8,7},{9,10},{10,9... | collective-permute-start | bytes 36872 | tf_op jit(solution)/shard_map/ppermute | solution.py:347
  4.8 4.4 %collective-permute-start.1 = (f32[24,128]{1,0:T(8,128)S(1)}, f32[24,128]{1,0:T(8,128)S(1)}, u32[]{:S(2)}, u32[]{:S(2)}) collective-permute-start(f32[24,128]{1,0:T(8,128)S(1)} %shard_map.86.refs_0_), channel_id=1, source_target_pairs={{0,8},{1,9},{2,10},{3,11},{4,12},{5,13},{6,14},{7,15},{8,0},{9,1},... | collective-permute-start | bytes 36872 | tf_op jit(solution)/shard_map/ppermute | solution.py:347
  7.2 1.9 %collective-permute-start = (f32[24,128]{1,0:T(8,128)S(1)}, f32[24,128]{1,0:T(8,128)S(1)}, u32[]{:S(2)}, u32[]{:S(2)}) collective-permute-start(f32[24,128]{1,0:T(8,128)S(1)} %shard_map.86.refs_0_), channel_id=1, source_target_pairs={{0,1},{1,0},{2,3},{3,2},{4,5},{5,4},{6,7},{7,6},{8,9},{9,8},{10,11... | collective-permute-start | bytes 36872 | tf_op jit(solution)/shard_map/ppermute | solution.py:347
  9.6 3.4 %collective-permute-start.7 = (f32[24,128]{1,0:T(8,128)S(1)}, f32[24,128]{1,0:T(8,128)S(1)}, u32[]{:S(2)}, u32[]{:S(2)}) collective-permute-start(f32[24,128]{1,0:T(8,128)S(1)} %get-tuple-element.19.refs_0_.t0), channel_id=1, source_target_pairs={{0,2},{1,0},{2,1},{3,4},{4,3},{5,6},{6,5},{7,8},{8,7},{9,10},{10,9... | collective-permute-start | bytes 36872 | tf_op jit(solution)/shard_map/ppermute | solution.py:347
  10.9 3.8 %collective-permute-start.6 = (f32[24,128]{1,0:T(8,128)S(1)}, f32[24,128]{1,0:T(8,128)S(1)}, u32[]{:S(2)}, u32[]{:S(2)}) collective-permute-start(f32[24,128]{1,0:T(8,128)S(1)} %get-tuple-element.19.refs_0_.t0), channel_id=1, source_target_pairs={{0,8},{1,9},{2,10},{3,11},{4,12},{5,13},{6,14},{7,15},{8,0},{9,1},... | collective-permute-start | bytes 36872 | tf_op jit(solution)/shard_map/ppermute | solution.py:347
  12.9 3.1 %collective-permute-start.5 = (f32[24,128]{1,0:T(8,128)S(1)}, f32[24,128]{1,0:T(8,128)S(1)}, u32[]{:S(2)}, u32[]{:S(2)}) collective-permute-start(f32[24,128]{1,0:T(8,128)S(1)} %get-tuple-element.19.refs_0_.t0), channel_id=1, source_target_pairs={{0,1},{1,2},{2,3},{3,0},{4,5},{5,4},{6,7},{7,6},{8,16},{9,17},{10,... | collective-permute-start | bytes 36872 | tf_op jit(solution)/shard_map/ppermute | solution.py:347
  12.9 3.1 %collective-permute-start.4 = (f32[24,128]{1,0:T(8,128)S(1)}, f32[24,128]{1,0:T(8,128)S(1)}, u32[]{:S(2)}, u32[]{:S(2)}) collective-permute-start(f32[24,128]{1,0:T(8,128)S(1)} %get-tuple-element.19.refs_0_.t0), channel_id=1, source_target_pairs={{0,1},{1,0},{2,3},{3,2},{4,5},{5,4},{6,7},{7,6},{8,9},{9,8},{10,11... | collective-permute-start | bytes 36872 | tf_op jit(solution)/shard_map/ppermute | solution.py:347
  16.3 7.8 %copy-start = (f32[3,32,512]{2,1,0:T(8,128)S(1)}, f32[3,32,512]{2,1,0:T(8,128)}, u32[]{:S(2)}) copy-start(f32[3,32,512]{2,1,0:T(8,128)} %refs_4_.1) | copy-start | bytes 589828
  16.3 2.3 %collective-permute-start.11 = (f32[24,128]{1,0:T(8,128)S(1)}, f32[24,128]{1,0:T(8,128)S(1)}, u32[]{:S(2)}, u32[]{:S(2)}) collective-permute-start(f32[24,128]{1,0:T(8,128)S(1)} %shard_map.89.refs_0_.t1), channel_id=1, source_target_pairs={{0,2},{1,0},{2,1},{3,4},{4,3},{5,6},{6,5},{7,8},{8,7},{9,10},{10,9... | collective-permute-start | bytes 36872 | tf_op jit(solution)/shard_map/ppermute | solution.py:347
  16.4 3.8 %collective-permute-start.10 = (f32[24,128]{1,0:T(8,128)S(1)}, f32[24,128]{1,0:T(8,128)S(1)}, u32[]{:S(2)}, u32[]{:S(2)}) collective-permute-start(f32[24,128]{1,0:T(8,128)S(1)} %shard_map.89.refs_0_.t1), channel_id=1, source_target_pairs={{0,8},{1,9},{2,10},{3,11},{4,12},{5,13},{6,14},{7,15},{8,0},{9,1},... | collective-permute-start | bytes 36872 | tf_op jit(solution)/shard_map/ppermute | solution.py:347
  18.4 3.1 %collective-permute-start.9 = (f32[24,128]{1,0:T(8,128)S(1)}, f32[24,128]{1,0:T(8,128)S(1)}, u32[]{:S(2)}, u32[]{:S(2)}) collective-permute-start(f32[24,128]{1,0:T(8,128)S(1)} %shard_map.89.refs_0_.t1), channel_id=1, source_target_pairs={{0,1},{1,2},{2,3},{3,0},{4,5},{5,4},{6,7},{7,6},{8,16},{9,17},{10,... | collective-permute-start | bytes 36872 | tf_op jit(solution)/shard_map/ppermute | solution.py:347
  18.4 3.1 %collective-permute-start.8 = (f32[24,128]{1,0:T(8,128)S(1)}, f32[24,128]{1,0:T(8,128)S(1)}, u32[]{:S(2)}, u32[]{:S(2)}) collective-permute-start(f32[24,128]{1,0:T(8,128)S(1)} %shard_map.89.refs_0_.t1), channel_id=1, source_target_pairs={{0,1},{1,0},{2,3},{3,2},{4,5},{5,4},{6,7},{7,6},{8,9},{9,8},{10,11... | collective-permute-start | bytes 36872 | tf_op jit(solution)/shard_map/ppermute | solution.py:347
  21.8 2.9 %collective-permute-start.15 = (f32[24,128]{1,0:T(8,128)S(1)}, f32[24,128]{1,0:T(8,128)S(1)}, u32[]{:S(2)}, u32[]{:S(2)}) collective-permute-start(f32[24,128]{1,0:T(8,128)S(1)} %shard_map.90.t2.refs_0_), channel_id=1, source_target_pairs={{0,2},{1,0},{2,1},{3,4},{4,3},{5,6},{6,5},{7,8},{8,7},{9,10},{10,9... | collective-permute-start | bytes 36872 | tf_op jit(solution)/shard_map/ppermute | solution.py:347
  22.0 3.9 %collective-permute-start.14 = (f32[24,128]{1,0:T(8,128)S(1)}, f32[24,128]{1,0:T(8,128)S(1)}, u32[]{:S(2)}, u32[]{:S(2)}) collective-permute-start(f32[24,128]{1,0:T(8,128)S(1)} %shard_map.90.t2.refs_0_), channel_id=1, source_target_pairs={{0,8},{1,9},{2,10},{3,11},{4,12},{5,13},{6,14},{7,15},{8,0},{9,1},... | collective-permute-start | bytes 36872 | tf_op jit(solution)/shard_map/ppermute | solution.py:347
  24.1 3.1 %collective-permute-start.13 = (f32[24,128]{1,0:T(8,128)S(1)}, f32[24,128]{1,0:T(8,128)S(1)}, u32[]{:S(2)}, u32[]{:S(2)}) collective-permute-start(f32[24,128]{1,0:T(8,128)S(1)} %shard_map.90.t2.refs_0_), channel_id=1, source_target_pairs={{0,1},{1,2},{2,3},{3,0},{4,5},{5,4},{6,7},{7,6},{8,16},{9,17},{10,... | collective-permute-start | bytes 36872 | tf_op jit(solution)/shard_map/ppermute | solution.py:347
  24.1 3.1 %collective-permute-start.12 = (f32[24,128]{1,0:T(8,128)S(1)}, f32[24,128]{1,0:T(8,128)S(1)}, u32[]{:S(2)}, u32[]{:S(2)}) collective-permute-start(f32[24,128]{1,0:T(8,128)S(1)} %shard_map.90.t2.refs_0_), channel_id=1, source_target_pairs={{0,1},{1,0},{2,3},{3,2},{4,5},{5,4},{6,7},{7,6},{8,9},{9,8},{10,11... | collective-permute-start | bytes 36872 | tf_op jit(solution)/shard_map/ppermute | solution.py:347
  27.6 1.2 %collective-permute-start.16 = (f32[24,128]{1,0:T(8,128)S(1)}, f32[24,128]{1,0:T(8,128)S(1)}, u32[]{:S(2)}, u32[]{:S(2)}) collective-permute-start(f32[24,128]{1,0:T(8,128)S(1)} %get-tuple-element.26), channel_id=1, source_target_pairs={{0,1},{1,0},{2,3},{3,2},{4,5},{5,4},{6,7},{7,6},{8,9},{9,8},{10,11... | collective-permute-start | bytes 36872 | tf_op jit(solution)/shard_map/ppermute | solution.py:347
  28.9 4.1 %collective-permute-start.19 = (f32[24,128]{1,0:T(8,128)S(1)}, f32[24,128]{1,0:T(8,128)S(1)}, u32[]{:S(2)}, u32[]{:S(2)}) collective-permute-start(f32[24,128]{1,0:T(8,128)S(1)} %add.12), channel_id=1, source_target_pairs={{0,7},{1,6},{2,5},{3,4},{4,3},{5,2},{6,1},{7,0},{8,15},{9,14},{10,... | collective-permute-start | bytes 36872 | tf_op jit(solution)/shard_map/ppermute | solution.py:347
  29.2 3.8 %collective-permute-start.18 = (f32[24,128]{1,0:T(8,128)S(1)}, f32[24,128]{1,0:T(8,128)S(1)}, u32[]{:S(2)}, u32[]{:S(2)}) collective-permute-start(f32[24,128]{1,0:T(8,128)S(1)} %add.12), channel_id=1, source_target_pairs={{0,5},{1,4},{2,7},{3,6},{4,1},{5,0},{6,3},{7,2},{8,13},{9,12},{10,... | collective-permute-start | bytes 36872 | tf_op jit(solution)/shard_map/ppermute | solution.py:347
  29.9 3.3 %collective-permute-start.17 = (f32[24,128]{1,0:T(8,128)S(1)}, f32[24,128]{1,0:T(8,128)S(1)}, u32[]{:S(2)}, u32[]{:S(2)}) collective-permute-start(f32[24,128]{1,0:T(8,128)S(1)} %add.12), channel_id=1, source_target_pairs={{0,3},{1,2},{2,1},{3,0},{4,7},{5,6},{6,5},{7,4},{8,11},{9,10},{10,... | collective-permute-start | bytes 36872 | tf_op jit(solution)/shard_map/ppermute | solution.py:347
  33.3 4.9 %collective-permute-start.22 = (f32[24,128]{1,0:T(8,128)S(1)}, f32[24,128]{1,0:T(8,128)S(1)}, u32[]{:S(2)}, u32[]{:S(2)}) collective-permute-start(f32[24,128]{1,0:T(8,128)S(1)} %add_add_fusion.refs_0_), channel_id=1, source_target_pairs={{0,25},{1,24},{2,27},{3,26},{4,29},{5,28},{6,31},{7,30},{8,17},{9,... | collective-permute-start | bytes 36872 | tf_op jit(solution)/shard_map/ppermute | solution.py:347
  34.9 4.1 %collective-permute-start.21 = (f32[24,128]{1,0:T(8,128)S(1)}, f32[24,128]{1,0:T(8,128)S(1)}, u32[]{:S(2)}, u32[]{:S(2)}) collective-permute-start(f32[24,128]{1,0:T(8,128)S(1)} %add_add_fusion.refs_0_), channel_id=1, source_target_pairs={{0,17},{1,16},{2,19},{3,18},{4,21},{5,20},{6,23},{7,22},{8,25},{9,... | collective-permute-start | bytes 36872 | tf_op jit(solution)/shard_map/ppermute | solution.py:347
  35.2 3.7 %collective-permute-start.20 = (f32[24,128]{1,0:T(8,128)S(1)}, f32[24,128]{1,0:T(8,128)S(1)}, u32[]{:S(2)}, u32[]{:S(2)}) collective-permute-start(f32[24,128]{1,0:T(8,128)S(1)} %add_add_fusion.refs_0_), channel_id=1, source_target_pairs={{0,9},{1,8},{2,11},{3,10},{4,13},{5,12},{6,15},{7,14},{8,1},{9,0},... | collective-permute-start | bytes 36872 | tf_op jit(solution)/shard_map/ppermute | solution.py:347

commit v24 on v22

--- a/solution.py
+++ b/solution.py
@@ -78,10 +78,11 @@
 
 
 def start_kernel(prev_in, mix_in, list_in, count_in, out_ref, prev_ref, mix_ref, list_ref, count_ref, sems):
-    copies = fetch(
-        [(prev_in, prev_ref), (mix_in, mix_ref), (list_in, list_ref), (count_in, count_ref)], sems
-    )
-    for copy in copies[1:]:
+    comps = prev_ref.shape[0]
+    cuts = [pl.ds(0, comps - 1), pl.ds(comps - 1, 1)]
+    pairs = [(prev_in.at[cut], prev_ref.at[cut]) for cut in cuts]
+    copies = fetch(pairs + [(mix_in, mix_ref), (list_in, list_ref), (count_in, count_ref)], sems)
+    for copy in copies[2:]:
         copy.wait()
     comps, vecs, rows = prev_ref.shape
     eye = iota((vecs, vecs), 0) == iota((vecs, vecs), 1)
@@ -102,6 +103,8 @@
     copies[0].wait()
     own = own_lanes(8, rows)
     for c in range(comps):
+        if c == comps - 1:
+            copies[1].wait()
         start = jnp.sum(weights[c] * prev_ref[c], axis=0, keepdims=True)
         line = jnp.broadcast_to(start, own.shape)
         out_ref[c * 8 : (c + 1) * 8, :] = fold(jnp.where(own, line, 0.0))
@@ -403,7 +406,7 @@
             pltpu.VMEM(mix.shape, f32),
             pltpu.VMEM(send_list.shape, jnp.int32),
             pltpu.VMEM(send_count.shape, jnp.int32),
-            dma((4,)),
+            dma((5,)),
         ],
     )(*in_hbm(prev_basis, mix, send_list, send_count))
     high, low, aux = call(

time: 40.1 us -> 40.1 us (level)
  no operation moved by 1% of the time
where the time goes in v24:
time: 40.1 us; the launch traced here: 40 us
  starting transfers between devices  20.9 us (52%)
  waiting for transfers between devices  13 us (32%)
  Pallas kernels  5.26 us (13%)
  between operations  0.72 us (2%)
    ppermute x23, starting transfers between devices, send(): lax.ppermute(value, 'dom', [(d, target[d]) for d in range(lax.axis_size('...  20.9 us
    ppermute x23, waiting for transfers between devices, send(): lax.ppermute(value, 'dom', [(d, target[d]) for d in range(lax.axis_size('...  13 us
    pallas_call x1, Pallas kernels, local(): call(prepare_kernel, [((width, rows), bf16), ((width, rows), bf16), ((8 *...  1.26 us
    pallas_call x1, Pallas kernels, local(): call(start_kernel, [((comps * blocks + 8, 128), f32)], [HBM] * 4, 600000,...  1.16 us
    pallas_call x1, Pallas kernels, local(): call(lambda *refs: finish_kernel(total, refs[:count], *refs[count:]), [((...  0.97 us
  transfers between devices with their start and end apart: 23, of which 12 were waited for; matrix products, arithmetic and copies ran while one was open for 0% of the time, Pallas kernels for 5%

profile of v24, /device:TPU:0, one launch (start us, length us, event | category | flops | bytes accessed | tf_op | source)
XLA Modules:
  0.0 40.0 jit_solution(748863840716872588)
XLA Ops:
  0.6 1.2 %shard_map.86.refs_0_ = f32[32,128]{1,0:T(8,128)S(1)} custom-call(f32[3,32,512]{2,1,0:T(8,128)} %refs_4_.1, f32[3,32]{1,0:T(4,128)} %mix_in.1, s32[1,4,8]{2,1,0:T(4,128)} %list_in.1, s32[1,4]{1,0:T(1,128)} %count_in.1), custom_call_target="tpu_custom_call" | custom-call | flops 600000 | bytes 250000 | tf_op jit(solution)/shard_map/pallas_call | solution.py:398
  1.8 0.5 %collective-permute-start.3 = (f32[32,128]{1,0:T(8,128)S(1)}, f32[32,128]{1,0:T(8,128)S(1)}, u32[]{:S(2)}, u32[]{:S(2)}) collective-permute-start(f32[32,128]{1,0:T(8,128)S(1)} %shard_map.86.refs_0_), channel_id=1, source_target_pairs={{0,1},{1,2},{2,3},{3,0},{4,5},{5,4},{6,7},{7,6},{8,16},{9,17},{10,... | collective-permute-start | bytes 49160 | tf_op jit(solution)/shard_map/ppermute | solution.py:344
  2.3 2.5 %collective-permute-start.2 = (f32[32,128]{1,0:T(8,128)S(1)}, f32[32,128]{1,0:T(8,128)S(1)}, u32[]{:S(2)}, u32[]{:S(2)}) collective-permute-start(f32[32,128]{1,0:T(8,128)S(1)} %shard_map.86.refs_0_), channel_id=1, source_target_pairs={{0,2},{1,0},{2,1},{3,4},{4,3},{5,6},{6,5},{7,8},{8,7},{9,10},{10,9... | collective-permute-start | bytes 49160 | tf_op jit(solution)/shard_map/ppermute | solution.py:344
  4.8 2.5 %collective-permute-start.1 = (f32[32,128]{1,0:T(8,128)S(1)}, f32[32,128]{1,0:T(8,128)S(1)}, u32[]{:S(2)}, u32[]{:S(2)}) collective-permute-start(f32[32,128]{1,0:T(8,128)S(1)} %shard_map.86.refs_0_), channel_id=1, source_target_pairs={{0,8},{1,9},{2,10},{3,11},{4,12},{5,13},{6,14},{7,15},{8,0},{9,1},... | collective-permute-start | bytes 49160 | tf_op jit(solution)/shard_map/ppermute | solution.py:344
  7.3 0.5 %collective-permute-start = (f32[32,128]{1,0:T(8,128)S(1)}, f32[32,128]{1,0:T(8,128)S(1)}, u32[]{:S(2)}, u32[]{:S(2)}) collective-permute-start(f32[32,128]{1,0:T(8,128)S(1)} %shard_map.86.refs_0_), channel_id=1, source_target_pairs={{0,1},{1,0},{2,3},{3,2},{4,5},{5,4},{6,7},{7,6},{8,9},{9,8},{10,11... | collective-permute-start | bytes 49160 | tf_op jit(solution)/shard_map/ppermute | solution.py:344
  7.8 1.3 %shard_map.87 = (bf16[256,512]{1,0:T(8,128)(2,1)S(1)}, bf16[256,512]{1,0:T(8,128)(2,1)S(1)}, f32[56,128]{1,0:T(8,128)S(1)}) custom-call(f32[512,256]{1,0:T(8,128)} %strips_in.1, s32[4,8]{1,0:T(4,128)} %bitcast.2, f32[4]{0:T(128)} %shifts_in.1), custom_call_target="tpu_custom_call" | custom-call | flops 1000000 | bytes 1000000 | tf_op jit(solution)/shard_map/pallas_call | solution.py:412
  9.0 0.0 collective-permute-done.3.refs_4_
  9.1 0.0 collective-permute-done.2.refs_3_
  9.1 0.3 collective-permute-done.1.refs_2_
  9.4 0.0 collective-permute-done.refs_1_
  9.4 0.4 shard_map.88
  9.7 1.2 %collective-permute-start.7 = (f32[24,128]{1,0:T(8,128)S(1)}, f32[24,128]{1,0:T(8,128)S(1)}, u32[]{:S(2)}, u32[]{:S(2)}) collective-permute-start(f32[24,128]{1,0:T(8,128)S(1)} %get-tuple-element.19.refs_0_.t0), channel_id=1, source_target_pairs={{0,2},{1,0},{2,1},{3,4},{4,3},{5,6},{6,5},{7,8},{8,7},{9,10},{10,9... | collective-permute-start | bytes 36872 | tf_op jit(solution)/shard_map/ppermute | solution.py:344
  10.9 2.0 %collective-permute-start.6 = (f32[24,128]{1,0:T(8,128)S(1)}, f32[24,128]{1,0:T(8,128)S(1)}, u32[]{:S(2)}, u32[]{:S(2)}) collective-permute-start(f32[24,128]{1,0:T(8,128)S(1)} %get-tuple-element.19.refs_0_.t0), channel_id=1, source_target_pairs={{0,8},{1,9},{2,10},{3,11},{4,12},{5,13},{6,14},{7,15},{8,0},{9,1},... | collective-permute-start | bytes 36872 | tf_op jit(solution)/shard_map/ppermute | solution.py:344
  12.9 0.0 collective-permute-start.5
  12.9 0.1 collective-permute-start.4
  13.0 0.0 collective-permute-done.7.refs_4_
  13.1 1.7 %collective-permute-done.6.refs_3_ = f32[24,128]{1,0:T(8,128)S(1)} collective-permute-done((f32[24,128]{1,0:T(8,128)S(1)}, f32[24,128]{1,0:T(8,128)S(1)}, u32[]{:S(2)}, u32[]{:S(2)}) %collective-permute-start.6) | collective-permute-done | bytes 12320 | tf_op jit(solution)/shard_map/ppermute | solution.py:344
  14.7 1.3 %collective-permute-done.5.refs_2_ = f32[24,128]{1,0:T(8,128)S(1)} collective-permute-done((f32[24,128]{1,0:T(8,128)S(1)}, f32[24,128]{1,0:T(8,128)S(1)}, u32[]{:S(2)}, u32[]{:S(2)}) %collective-permute-start.5) | collective-permute-done | bytes 12320 | tf_op jit(solution)/shard_map/ppermute | solution.py:344
  16.1 0.0 collective-permute-done.4.refs_1_
  16.1 0.3 shard_map.89.refs_0_.t1
  16.3 0.0 copy-start
  16.3 0.1 collective-permute-start.11
  16.5 2.0 %collective-permute-start.10 = (f32[24,128]{1,0:T(8,128)S(1)}, f32[24,128]{1,0:T(8,128)S(1)}, u32[]{:S(2)}, u32[]{:S(2)}) collective-permute-start(f32[24,128]{1,0:T(8,128)S(1)} %shard_map.89.refs_0_.t1), channel_id=1, source_target_pairs={{0,8},{1,9},{2,10},{3,11},{4,12},{5,13},{6,14},{7,15},{8,0},{9,1},... | collective-permute-start | bytes 36872 | tf_op jit(solution)/shard_map/ppermute | solution.py:344
  18.5 0.0 collective-permute-start.9
  18.5 0.2 collective-permute-start.8
  18.7 0.0 collective-permute-done.11.refs_4_
  18.7 1.6 %collective-permute-done.10.refs_3_ = f32[24,128]{1,0:T(8,128)S(1)} collective-permute-done((f32[24,128]{1,0:T(8,128)S(1)}, f32[24,128]{1,0:T(8,128)S(1)}, u32[]{:S(2)}, u32[]{:S(2)}) %collective-permute-start.10) | collective-permute-done | bytes 12320 | tf_op jit(solution)/shard_map/ppermute | solution.py:344
  20.3 1.3 %collective-permute-done.9.refs_2_ = f32[24,128]{1,0:T(8,128)S(1)} collective-permute-done((f32[24,128]{1,0:T(8,128)S(1)}, f32[24,128]{1,0:T(8,128)S(1)}, u32[]{:S(2)}, u32[]{:S(2)}) %collective-permute-start.9) | collective-permute-done | bytes 12320 | tf_op jit(solution)/shard_map/ppermute | solution.py:344
  21.6 0.0 collective-permute-done.8.refs_1_
  21.6 0.3 shard_map.90.t2.refs_0_
  21.9 0.1 collective-permute-start.15
  22.1 2.1 %collective-permute-start.14 = (f32[24,128]{1,0:T(8,128)S(1)}, f32[24,128]{1,0:T(8,128)S(1)}, u32[]{:S(2)}, u32[]{:S(2)}) collective-permute-start(f32[24,128]{1,0:T(8,128)S(1)} %shard_map.90.t2.refs_0_), channel_id=1, source_target_pairs={{0,8},{1,9},{2,10},{3,11},{4,12},{5,13},{6,14},{7,15},{8,0},{9,1},... | collective-permute-start | bytes 36872 | tf_op jit(solution)/shard_map/ppermute | solution.py:344
  24.2 0.0 collective-permute-start.13
  24.2 0.0 collective-permute-start.12
  24.2 0.0 copy-done
  24.2 0.6 %shard_map.91 = (f32[24,512]{1,0:T(8,128)S(1)}, f32[24,128]{1,0:T(8,128)S(1)}, bf16[512,128]{1,0:T(8,128)(2,1)S(1)}, bf16[512,128]{1,0:T(8,128)(2,1)S(1)}, bf16[512,128]{1,0:T(8,128)(2,1)S(1)}) custom-call(f32[3,32,512]{2,1,0:T(8,128)S(1)} %copy-done, f32[24,128]{1,0:T(8,128)S(1)} %get-tuple-element.19.refs_0_.t0, f32[24,128]{1,0:T(8,128)S(1)} %shard_map.89.refs_0_.t1, ...), custom_call_target="tpu_custom_call" | custom-call | flops 60000000 | bytes 250000 | tf_op jit(solution)/shard_map/pallas_call | solution.py:443
  24.8 0.0 collective-permute-done.15.refs_4_
  24.8 1.2 %collective-permute-done.14.refs_3_ = f32[24,128]{1,0:T(8,128)S(1)} collective-permute-done((f32[24,128]{1,0:T(8,128)S(1)}, f32[24,128]{1,0:T(8,128)S(1)}, u32[]{:S(2)}, u32[]{:S(2)}) %collective-permute-start.14) | collective-permute-done | bytes 12320 | tf_op jit(solution)/shard_map/ppermute | solution.py:344
  26.0 1.3 %collective-permute-done.13.refs_2_ = f32[24,128]{1,0:T(8,128)S(1)} collective-permute-done((f32[24,128]{1,0:T(8,128)S(1)}, f32[24,128]{1,0:T(8,128)S(1)}, u32[]{:S(2)}, u32[]{:S(2)}) %collective-permute-start.13) | collective-permute-done | bytes 12320 | tf_op jit(solution)/shard_map/ppermute | solution.py:344
  27.3 0.0 collective-permute-done.12.refs_1_
  27.3 0.4 shard_map.92
  27.7 0.1 collective-permute-start.16
  27.8 1.2 %collective-permute-done.16 = f32[24,128]{1,0:T(8,128)S(1)} collective-permute-done((f32[24,128]{1,0:T(8,128)S(1)}, f32[24,128]{1,0:T(8,128)S(1)}, u32[]{:S(2)}, u32[]{:S(2)}) %collective-permute-start.16) | collective-permute-done | bytes 12320 | tf_op jit(solution)/shard_map/ppermute | solution.py:344
  28.9 0.4 collective-permute-start.19
  29.3 0.7 %collective-permute-start.18 = (f32[24,128]{1,0:T(8,128)S(1)}, f32[24,128]{1,0:T(8,128)S(1)}, u32[]{:S(2)}, u32[]{:S(2)}) collective-permute-start(f32[24,128]{1,0:T(8,128)S(1)} %add.12), channel_id=1, source_target_pairs={{0,5},{1,4},{2,7},{3,6},{4,1},{5,0},{6,3},{7,2},{8,13},{9,12},{10,... | collective-permute-start | bytes 36872 | tf_op jit(solution)/shard_map/ppermute | solution.py:344
  30.0 1.9 %collective-permute-start.17 = (f32[24,128]{1,0:T(8,128)S(1)}, f32[24,128]{1,0:T(8,128)S(1)}, u32[]{:S(2)}, u32[]{:S(2)}) collective-permute-start(f32[24,128]{1,0:T(8,128)S(1)} %add.12), channel_id=1, source_target_pairs={{0,3},{1,2},{2,1},{3,0},{4,7},{5,6},{6,5},{7,4},{8,11},{9,10},{10,... | collective-permute-start | bytes 36872 | tf_op jit(solution)/shard_map/ppermute | solution.py:344
  31.9 1.1 %collective-permute-done.19 = f32[24,128]{1,0:T(8,128)S(1)} collective-permute-done((f32[24,128]{1,0:T(8,128)S(1)}, f32[24,128]{1,0:T(8,128)S(1)}, u32[]{:S(2)}, u32[]{:S(2)}) %collective-permute-start.19) | collective-permute-done | bytes 12320 | tf_op jit(solution)/shard_map/ppermute | solution.py:344
  33.1 0.0 collective-permute-done.18
  33.1 0.3 collective-permute-done.17
  33.3 1.6 %collective-permute-start.22 = (f32[24,128]{1,0:T(8,128)S(1)}, f32[24,128]{1,0:T(8,128)S(1)}, u32[]{:S(2)}, u32[]{:S(2)}) collective-permute-start(f32[24,128]{1,0:T(8,128)S(1)} %add_add_fusion.refs_0_), channel_id=1, source_target_pairs={{0,25},{1,24},{2,27},{3,26},{4,29},{5,28},{6,31},{7,30},{8,17},{9,... | collective-permute-start | bytes 36872 | tf_op jit(solution)/shard_map/ppermute | solution.py:344
  34.9 0.3 collective-permute-start.21
  35.3 2.1 %collective-permute-start.20 = (f32[24,128]{1,0:T(8,128)S(1)}, f32[24,128]{1,0:T(8,128)S(1)}, u32[]{:S(2)}, u32[]{:S(2)}) collective-permute-start(f32[24,128]{1,0:T(8,128)S(1)} %add_add_fusion.refs_0_), channel_id=1, source_target_pairs={{0,9},{1,8},{2,11},{3,10},{4,13},{5,12},{6,15},{7,14},{8,1},{9,0},... | collective-permute-start | bytes 36872 | tf_op jit(solution)/shard_map/ppermute | solution.py:344
  37.4 0.9 %collective-permute-done.22.refs_3_ = f32[24,128]{1,0:T(8,128)S(1)} collective-permute-done((f32[24,128]{1,0:T(8,128)S(1)}, f32[24,128]{1,0:T(8,128)S(1)}, u32[]{:S(2)}, u32[]{:S(2)}) %collective-permute-start.22) | collective-permute-done | bytes 12320 | tf_op jit(solution)/shard_map/ppermute | solution.py:344
  38.3 0.7 %collective-permute-done.21.refs_2_ = f32[24,128]{1,0:T(8,128)S(1)} collective-permute-done((f32[24,128]{1,0:T(8,128)S(1)}, f32[24,128]{1,0:T(8,128)S(1)}, u32[]{:S(2)}, u32[]{:S(2)}) %collective-permute-start.21) | collective-permute-done | bytes 12320 | tf_op jit(solution)/shard_map/ppermute | solution.py:344
  39.0 0.0 collective-permute-done.20.refs_1_
  39.0 1.0 %shard_map.93 = (f32[3,4,512]{2,1,0:T(4,128)}, f32[3,4,36]{2,1,0:T(4,128)}) custom-call(f32[24,128]{1,0:T(8,128)S(1)} %add_add_fusion.refs_0_, f32[24,128]{1,0:T(8,128)S(1)} %collective-permute-done.20.refs_1_, f32[24,128]{1,0:T(8,128)S(1)} %collective-permute-done.21.refs_2_, f32[24,128]{1,0:T(8,128)S(1)} %collective-permute-done.22.refs_3_, ...), custom_call_target="tpu_custom_call" | custom-call | flops 50000000 | bytes 400000 | tf_op jit(solution)/shard_map/pallas_call | solution.py:460
  (2 shorter events, 0.0 us)
Async XLA Ops:
  1.8 7.2 %collective-permute-start.3 = (f32[32,128]{1,0:T(8,128)S(1)}, f32[32,128]{1,0:T(8,128)S(1)}, u32[]{:S(2)}, u32[]{:S(2)}) collective-permute-start(f32[32,128]{1,0:T(8,128)S(1)} %shard_map.86.refs_0_), channel_id=1, source_target_pairs={{0,1},{1,2},{2,3},{3,0},{4,5},{5,4},{6,7},{7,6},{8,16},{9,17},{10,... | collective-permute-start | bytes 49160 | tf_op jit(solution)/shard_map/ppermute | solution.py:344
  2.3 6.8 %collective-permute-start.2 = (f32[32,128]{1,0:T(8,128)S(1)}, f32[32,128]{1,0:T(8,128)S(1)}, u32[]{:S(2)}, u32[]{:S(2)}) collective-permute-start(f32[32,128]{1,0:T(8,128)S(1)} %shard_map.86.refs_0_), channel_id=1, source_target_pairs={{0,2},{1,0},{2,1},{3,4},{4,3},{5,6},{6,5},{7,8},{8,7},{9,10},{10,9... | collective-permute-start | bytes 49160 | tf_op jit(solution)/shard_map/ppermute | solution.py:344
  4.8 4.5 %collective-permute-start.1 = (f32[32,128]{1,0:T(8,128)S(1)}, f32[32,128]{1,0:T(8,128)S(1)}, u32[]{:S(2)}, u32[]{:S(2)}) collective-permute-start(f32[32,128]{1,0:T(8,128)S(1)} %shard_map.86.refs_0_), channel_id=1, source_target_pairs={{0,8},{1,9},{2,10},{3,11},{4,12},{5,13},{6,14},{7,15},{8,0},{9,1},... | collective-permute-start | bytes 49160 | tf_op jit(solution)/shard_map/ppermute | solution.py:344
  7.3 2.1 %collective-permute-start = (f32[32,128]{1,0:T(8,128)S(1)}, f32[32,128]{1,0:T(8,128)S(1)}, u32[]{:S(2)}, u32[]{:S(2)}) collective-permute-start(f32[32,128]{1,0:T(8,128)S(1)} %shard_map.86.refs_0_), channel_id=1, source_target_pairs={{0,1},{1,0},{2,3},{3,2},{4,5},{5,4},{6,7},{7,6},{8,9},{9,8},{10,11... | collective-permute-start | bytes 49160 | tf_op jit(solution)/shard_map/ppermute | solution.py:344
  9.7 3.3 %collective-permute-start.7 = (f32[24,128]{1,0:T(8,128)S(1)}, f32[24,128]{1,0:T(8,128)S(1)}, u32[]{:S(2)}, u32[]{:S(2)}) collective-permute-start(f32[24,128]{1,0:T(8,128)S(1)} %get-tuple-element.19.refs_0_.t0), channel_id=1, source_target_pairs={{0,2},{1,0},{2,1},{3,4},{4,3},{5,6},{6,5},{7,8},{8,7},{9,10},{10,9... | collective-permute-start | bytes 36872 | tf_op jit(solution)/shard_map/ppermute | solution.py:344
  10.9 3.8 %collective-permute-start.6 = (f32[24,128]{1,0:T(8,128)S(1)}, f32[24,128]{1,0:T(8,128)S(1)}, u32[]{:S(2)}, u32[]{:S(2)}) collective-permute-start(f32[24,128]{1,0:T(8,128)S(1)} %get-tuple-element.19.refs_0_.t0), channel_id=1, source_target_pairs={{0,8},{1,9},{2,10},{3,11},{4,12},{5,13},{6,14},{7,15},{8,0},{9,1},... | collective-permute-start | bytes 36872 | tf_op jit(solution)/shard_map/ppermute | solution.py:344
  12.9 3.1 %collective-permute-start.5 = (f32[24,128]{1,0:T(8,128)S(1)}, f32[24,128]{1,0:T(8,128)S(1)}, u32[]{:S(2)}, u32[]{:S(2)}) collective-permute-start(f32[24,128]{1,0:T(8,128)S(1)} %get-tuple-element.19.refs_0_.t0), channel_id=1, source_target_pairs={{0,1},{1,2},{2,3},{3,0},{4,5},{5,4},{6,7},{7,6},{8,16},{9,17},{10,... | collective-permute-start | bytes 36872 | tf_op jit(solution)/shard_map/ppermute | solution.py:344
  12.9 3.1 %collective-permute-start.4 = (f32[24,128]{1,0:T(8,128)S(1)}, f32[24,128]{1,0:T(8,128)S(1)}, u32[]{:S(2)}, u32[]{:S(2)}) collective-permute-start(f32[24,128]{1,0:T(8,128)S(1)} %get-tuple-element.19.refs_0_.t0), channel_id=1, source_target_pairs={{0,1},{1,0},{2,3},{3,2},{4,5},{5,4},{6,7},{7,6},{8,9},{9,8},{10,11... | collective-permute-start | bytes 36872 | tf_op jit(solution)/shard_map/ppermute | solution.py:344
  16.3 7.8 %copy-start = (f32[3,32,512]{2,1,0:T(8,128)S(1)}, f32[3,32,512]{2,1,0:T(8,128)}, u32[]{:S(2)}) copy-start(f32[3,32,512]{2,1,0:T(8,128)} %refs_4_.1) | copy-start | bytes 589828
  16.3 2.3 %collective-permute-start.11 = (f32[24,128]{1,0:T(8,128)S(1)}, f32[24,128]{1,0:T(8,128)S(1)}, u32[]{:S(2)}, u32[]{:S(2)}) collective-permute-start(f32[24,128]{1,0:T(8,128)S(1)} %shard_map.89.refs_0_.t1), channel_id=1, source_target_pairs={{0,2},{1,0},{2,1},{3,4},{4,3},{5,6},{6,5},{7,8},{8,7},{9,10},{10,9... | collective-permute-start | bytes 36872 | tf_op jit(solution)/shard_map/ppermute | solution.py:344
  16.5 3.8 %collective-permute-start.10 = (f32[24,128]{1,0:T(8,128)S(1)}, f32[24,128]{1,0:T(8,128)S(1)}, u32[]{:S(2)}, u32[]{:S(2)}) collective-permute-start(f32[24,128]{1,0:T(8,128)S(1)} %shard_map.89.refs_0_.t1), channel_id=1, source_target_pairs={{0,8},{1,9},{2,10},{3,11},{4,12},{5,13},{6,14},{7,15},{8,0},{9,1},... | collective-permute-start | bytes 36872 | tf_op jit(solution)/shard_map/ppermute | solution.py:344
  18.5 3.1 %collective-permute-start.9 = (f32[24,128]{1,0:T(8,128)S(1)}, f32[24,128]{1,0:T(8,128)S(1)}, u32[]{:S(2)}, u32[]{:S(2)}) collective-permute-start(f32[24,128]{1,0:T(8,128)S(1)} %shard_map.89.refs_0_.t1), channel_id=1, source_target_pairs={{0,1},{1,2},{2,3},{3,0},{4,5},{5,4},{6,7},{7,6},{8,16},{9,17},{10,... | collective-permute-start | bytes 36872 | tf_op jit(solution)/shard_map/ppermute | solution.py:344
  18.5 3.1 %collective-permute-start.8 = (f32[24,128]{1,0:T(8,128)S(1)}, f32[24,128]{1,0:T(8,128)S(1)}, u32[]{:S(2)}, u32[]{:S(2)}) collective-permute-start(f32[24,128]{1,0:T(8,128)S(1)} %shard_map.89.refs_0_.t1), channel_id=1, source_target_pairs={{0,1},{1,0},{2,3},{3,2},{4,5},{5,4},{6,7},{7,6},{8,9},{9,8},{10,11... | collective-permute-start | bytes 36872 | tf_op jit(solution)/shard_map/ppermute | solution.py:344
  21.9 2.9 %collective-permute-start.15 = (f32[24,128]{1,0:T(8,128)S(1)}, f32[24,128]{1,0:T(8,128)S(1)}, u32[]{:S(2)}, u32[]{:S(2)}) collective-permute-start(f32[24,128]{1,0:T(8,128)S(1)} %shard_map.90.t2.refs_0_), channel_id=1, source_target_pairs={{0,2},{1,0},{2,1},{3,4},{4,3},{5,6},{6,5},{7,8},{8,7},{9,10},{10,9... | collective-permute-start | bytes 36872 | tf_op jit(solution)/shard_map/ppermute | solution.py:344
  22.1 3.9 %collective-permute-start.14 = (f32[24,128]{1,0:T(8,128)S(1)}, f32[24,128]{1,0:T(8,128)S(1)}, u32[]{:S(2)}, u32[]{:S(2)}) collective-permute-start(f32[24,128]{1,0:T(8,128)S(1)} %shard_map.90.t2.refs_0_), channel_id=1, source_target_pairs={{0,8},{1,9},{2,10},{3,11},{4,12},{5,13},{6,14},{7,15},{8,0},{9,1},... | collective-permute-start | bytes 36872 | tf_op jit(solution)/shard_map/ppermute | solution.py:344
  24.2 3.1 %collective-permute-start.13 = (f32[24,128]{1,0:T(8,128)S(1)}, f32[24,128]{1,0:T(8,128)S(1)}, u32[]{:S(2)}, u32[]{:S(2)}) collective-permute-start(f32[24,128]{1,0:T(8,128)S(1)} %shard_map.90.t2.refs_0_), channel_id=1, source_target_pairs={{0,1},{1,2},{2,3},{3,0},{4,5},{5,4},{6,7},{7,6},{8,16},{9,17},{10,... | collective-permute-start | bytes 36872 | tf_op jit(solution)/shard_map/ppermute | solution.py:344
  24.2 3.1 %collective-permute-start.12 = (f32[24,128]{1,0:T(8,128)S(1)}, f32[24,128]{1,0:T(8,128)S(1)}, u32[]{:S(2)}, u32[]{:S(2)}) collective-permute-start(f32[24,128]{1,0:T(8,128)S(1)} %shard_map.90.t2.refs_0_), channel_id=1, source_target_pairs={{0,1},{1,0},{2,3},{3,2},{4,5},{5,4},{6,7},{7,6},{8,9},{9,8},{10,11... | collective-permute-start | bytes 36872 | tf_op jit(solution)/shard_map/ppermute | solution.py:344
  27.7 1.2 %collective-permute-start.16 = (f32[24,128]{1,0:T(8,128)S(1)}, f32[24,128]{1,0:T(8,128)S(1)}, u32[]{:S(2)}, u32[]{:S(2)}) collective-permute-start(f32[24,128]{1,0:T(8,128)S(1)} %get-tuple-element.26), channel_id=1, source_target_pairs={{0,1},{1,0},{2,3},{3,2},{4,5},{5,4},{6,7},{7,6},{8,9},{9,8},{10,11... | collective-permute-start | bytes 36872 | tf_op jit(solution)/shard_map/ppermute | solution.py:344
  28.9 4.1 %collective-permute-start.19 = (f32[24,128]{1,0:T(8,128)S(1)}, f32[24,128]{1,0:T(8,128)S(1)}, u32[]{:S(2)}, u32[]{:S(2)}) collective-permute-start(f32[24,128]{1,0:T(8,128)S(1)} %add.12), channel_id=1, source_target_pairs={{0,7},{1,6},{2,5},{3,4},{4,3},{5,2},{6,1},{7,0},{8,15},{9,14},{10,... | collective-permute-start | bytes 36872 | tf_op jit(solution)/shard_map/ppermute | solution.py:344
  29.3 3.8 %collective-permute-start.18 = (f32[24,128]{1,0:T(8,128)S(1)}, f32[24,128]{1,0:T(8,128)S(1)}, u32[]{:S(2)}, u32[]{:S(2)}) collective-permute-start(f32[24,128]{1,0:T(8,128)S(1)} %add.12), channel_id=1, source_target_pairs={{0,5},{1,4},{2,7},{3,6},{4,1},{5,0},{6,3},{7,2},{8,13},{9,12},{10,... | collective-permute-start | bytes 36872 | tf_op jit(solution)/shard_map/ppermute | solution.py:344
  30.0 3.3 %collective-permute-start.17 = (f32[24,128]{1,0:T(8,128)S(1)}, f32[24,128]{1,0:T(8,128)S(1)}, u32[]{:S(2)}, u32[]{:S(2)}) collective-permute-start(f32[24,128]{1,0:T(8,128)S(1)} %add.12), channel_id=1, source_target_pairs={{0,3},{1,2},{2,1},{3,0},{4,7},{5,6},{6,5},{7,4},{8,11},{9,10},{10,... | collective-permute-start | bytes 36872 | tf_op jit(solution)/shard_map/ppermute | solution.py:344
  33.3 4.9 %collective-permute-start.22 = (f32[24,128]{1,0:T(8,128)S(1)}, f32[24,128]{1,0:T(8,128)S(1)}, u32[]{:S(2)}, u32[]{:S(2)}) collective-permute-start(f32[24,128]{1,0:T(8,128)S(1)} %add_add_fusion.refs_0_), channel_id=1, source_target_pairs={{0,25},{1,24},{2,27},{3,26},{4,29},{5,28},{6,31},{7,30},{8,17},{9,... | collective-permute-start | bytes 36872 | tf_op jit(solution)/shard_map/ppermute | solution.py:344
  34.9 4.1 %collective-permute-start.21 = (f32[24,128]{1,0:T(8,128)S(1)}, f32[24,128]{1,0:T(8,128)S(1)}, u32[]{:S(2)}, u32[]{:S(2)}) collective-permute-start(f32[24,128]{1,0:T(8,128)S(1)} %add_add_fusion.refs_0_), channel_id=1, source_target_pairs={{0,17},{1,16},{2,19},{3,18},{4,21},{5,20},{6,23},{7,22},{8,25},{9,... | collective-permute-start | bytes 36872 | tf_op jit(solution)/shard_map/ppermute | solution.py:344
  35.3 3.7 %collective-permute-start.20 = (f32[24,128]{1,0:T(8,128)S(1)}, f32[24,128]{1,0:T(8,128)S(1)}, u32[]{:S(2)}, u32[]{:S(2)}) collective-permute-start(f32[24,128]{1,0:T(8,128)S(1)} %add_add_fusion.refs_0_), channel_id=1, source_target_pairs={{0,9},{1,8},{2,11},{3,10},{4,13},{5,12},{6,15},{7,14},{8,1},{9,0},... | collective-permute-start | bytes 36872 | tf_op jit(solution)/shard_map/ppermute | solution.py:344

commit v25 on v21

--- a/solution.py
+++ b/solution.py
@@ -297,15 +297,15 @@
                 unit[k, l] = value / scale[l]
     roots = [jnp.sqrt(scale[k]) for k in range(S)]
     lower = {(k, l): unit[k, l] * roots[l] if l < k else roots[k] for k in range(S) for l in range(k + 1)}
-    vectors = []
+    vectors, results = [], []
     for k in range(S):
         value = projected[k * 8 : (k + 1) * 8]
         for l in range(k):
             value = value - unit[k, l] * vectors[l]
         vectors.append(value)
-        value = value * (1.0 / roots[k])
-        for c in range(comps):
-            basis_ref[c, k : k + 1, :] = value[c : c + 1]
+        results.append(value * (1.0 / roots[k]))
+    for c in range(comps):
+        basis_ref[c] = jnp.concatenate([value[c : c + 1] for value in results], axis=0)
     for c in range(comps):
         factors_ref[c, :, :vecs] = small[:S, c * vecs : (c + 1) * vecs]
     for k in range(S):

time: 40.1 us -> 40.1 us (level)
  no operation moved by 1% of the time
where the time goes in v25:
time: 40.1 us; the launch traced here: 39.9 us
  starting transfers between devices  20.9 us (52%)
  waiting for transfers between devices  13 us (32%)
  Pallas kernels  5.23 us (13%)
  between operations  0.72 us (2%)
    ppermute x23, starting transfers between devices, send(): lax.ppermute(value, 'dom', [(d, target[d]) for d in range(lax.axis_size('...  20.9 us
    ppermute x23, waiting for transfers between devices, send(): lax.ppermute(value, 'dom', [(d, target[d]) for d in range(lax.axis_size('...  13 us
    pallas_call x1, Pallas kernels, local(): call(prepare_kernel, [((width, rows), bf16), ((width, rows), bf16), ((8 *...  1.31 us
    pallas_call x1, Pallas kernels, local(): call(start_kernel, [((comps * blocks + 8, 128), f32)], [HBM] * 4, 600000,...  1.08 us
    pallas_call x1, Pallas kernels, local(): call(lambda *refs: finish_kernel(total, refs[:count], *refs[count:]), [((...  0.97 us
  transfers between devices with their start and end apart: 23, of which 12 were waited for; matrix products, arithmetic and copies ran while one was open for 0% of the time, Pallas kernels for 5%

profile of v25, /device:TPU:0, one launch (start us, length us, event | category | flops | bytes accessed | tf_op | source)
XLA Modules:
  0.0 39.9 jit_solution(16559023561675924014)
XLA Ops:
  0.6 1.1 %shard_map.86.refs_0_ = f32[32,128]{1,0:T(8,128)S(1)} custom-call(f32[3,32,512]{2,1,0:T(8,128)} %refs_4_.1, f32[3,32]{1,0:T(4,128)} %mix_in.1, s32[1,4,8]{2,1,0:T(4,128)} %list_in.1, s32[1,4]{1,0:T(1,128)} %count_in.1), custom_call_target="tpu_custom_call" | custom-call | flops 600000 | bytes 250000 | tf_op jit(solution)/shard_map/pallas_call | solution.py:395
  1.7 0.5 %collective-permute-start.3 = (f32[32,128]{1,0:T(8,128)S(1)}, f32[32,128]{1,0:T(8,128)S(1)}, u32[]{:S(2)}, u32[]{:S(2)}) collective-permute-start(f32[32,128]{1,0:T(8,128)S(1)} %shard_map.86.refs_0_), channel_id=1, source_target_pairs={{0,1},{1,2},{2,3},{3,0},{4,5},{5,4},{6,7},{7,6},{8,16},{9,17},{10,... | collective-permute-start | bytes 49160 | tf_op jit(solution)/shard_map/ppermute | solution.py:341
  2.2 2.5 %collective-permute-start.2 = (f32[32,128]{1,0:T(8,128)S(1)}, f32[32,128]{1,0:T(8,128)S(1)}, u32[]{:S(2)}, u32[]{:S(2)}) collective-permute-start(f32[32,128]{1,0:T(8,128)S(1)} %shard_map.86.refs_0_), channel_id=1, source_target_pairs={{0,2},{1,0},{2,1},{3,4},{4,3},{5,6},{6,5},{7,8},{8,7},{9,10},{10,9... | collective-permute-start | bytes 49160 | tf_op jit(solution)/shard_map/ppermute | solution.py:341
  4.8 2.5 %collective-permute-start.1 = (f32[32,128]{1,0:T(8,128)S(1)}, f32[32,128]{1,0:T(8,128)S(1)}, u32[]{:S(2)}, u32[]{:S(2)}) collective-permute-start(f32[32,128]{1,0:T(8,128)S(1)} %shard_map.86.refs_0_), channel_id=1, source_target_pairs={{0,8},{1,9},{2,10},{3,11},{4,12},{5,13},{6,14},{7,15},{8,0},{9,1},... | collective-permute-start | bytes 49160 | tf_op jit(solution)/shard_map/ppermute | solution.py:341
  7.2 0.5 %collective-permute-start = (f32[32,128]{1,0:T(8,128)S(1)}, f32[32,128]{1,0:T(8,128)S(1)}, u32[]{:S(2)}, u32[]{:S(2)}) collective-permute-start(f32[32,128]{1,0:T(8,128)S(1)} %shard_map.86.refs_0_), channel_id=1, source_target_pairs={{0,1},{1,0},{2,3},{3,2},{4,5},{5,4},{6,7},{7,6},{8,9},{9,8},{10,11... | collective-permute-start | bytes 49160 | tf_op jit(solution)/shard_map/ppermute | solution.py:341
  7.7 1.3 %shard_map.87 = (bf16[256,512]{1,0:T(8,128)(2,1)S(1)}, bf16[256,512]{1,0:T(8,128)(2,1)S(1)}, f32[56,128]{1,0:T(8,128)S(1)}) custom-call(f32[512,256]{1,0:T(8,128)} %strips_in.1, s32[4,8]{1,0:T(4,128)} %bitcast.2, f32[4]{0:T(128)} %shifts_in.1), custom_call_target="tpu_custom_call" | custom-call | flops 1000000 | bytes 1000000 | tf_op jit(solution)/shard_map/pallas_call | solution.py:409
  9.0 0.0 collective-permute-done.3.refs_4_
  9.0 0.0 collective-permute-done.2.refs_3_
  9.0 0.3 collective-permute-done.1.refs_2_
  9.3 0.0 collective-permute-done.refs_1_
  9.3 0.4 shard_map.88
  9.7 1.2 %collective-permute-start.7 = (f32[24,128]{1,0:T(8,128)S(1)}, f32[24,128]{1,0:T(8,128)S(1)}, u32[]{:S(2)}, u32[]{:S(2)}) collective-permute-start(f32[24,128]{1,0:T(8,128)S(1)} %get-tuple-element.19.refs_0_.t0), channel_id=1, source_target_pairs={{0,2},{1,0},{2,1},{3,4},{4,3},{5,6},{6,5},{7,8},{8,7},{9,10},{10,9... | collective-permute-start | bytes 36872 | tf_op jit(solution)/shard_map/ppermute | solution.py:341
  10.9 2.0 %collective-permute-start.6 = (f32[24,128]{1,0:T(8,128)S(1)}, f32[24,128]{1,0:T(8,128)S(1)}, u32[]{:S(2)}, u32[]{:S(2)}) collective-permute-start(f32[24,128]{1,0:T(8,128)S(1)} %get-tuple-element.19.refs_0_.t0), channel_id=1, source_target_pairs={{0,8},{1,9},{2,10},{3,11},{4,12},{5,13},{6,14},{7,15},{8,0},{9,1},... | collective-permute-start | bytes 36872 | tf_op jit(solution)/shard_map/ppermute | solution.py:341
  12.9 0.0 collective-permute-start.5
  12.9 0.1 collective-permute-start.4
  13.0 0.0 collective-permute-done.7.refs_4_
  13.0 1.7 %collective-permute-done.6.refs_3_ = f32[24,128]{1,0:T(8,128)S(1)} collective-permute-done((f32[24,128]{1,0:T(8,128)S(1)}, f32[24,128]{1,0:T(8,128)S(1)}, u32[]{:S(2)}, u32[]{:S(2)}) %collective-permute-start.6) | collective-permute-done | bytes 12320 | tf_op jit(solution)/shard_map/ppermute | solution.py:341
  14.7 1.3 %collective-permute-done.5.refs_2_ = f32[24,128]{1,0:T(8,128)S(1)} collective-permute-done((f32[24,128]{1,0:T(8,128)S(1)}, f32[24,128]{1,0:T(8,128)S(1)}, u32[]{:S(2)}, u32[]{:S(2)}) %collective-permute-start.5) | collective-permute-done | bytes 12320 | tf_op jit(solution)/shard_map/ppermute | solution.py:341
  16.0 0.0 collective-permute-done.4.refs_1_
  16.0 0.3 shard_map.89.refs_0_.t1
  16.3 0.0 copy-start
  16.3 0.1 collective-permute-start.11
  16.4 2.0 %collective-permute-start.10 = (f32[24,128]{1,0:T(8,128)S(1)}, f32[24,128]{1,0:T(8,128)S(1)}, u32[]{:S(2)}, u32[]{:S(2)}) collective-permute-start(f32[24,128]{1,0:T(8,128)S(1)} %shard_map.89.refs_0_.t1), channel_id=1, source_target_pairs={{0,8},{1,9},{2,10},{3,11},{4,12},{5,13},{6,14},{7,15},{8,0},{9,1},... | collective-permute-start | bytes 36872 | tf_op jit(solution)/shard_map/ppermute | solution.py:341
  18.4 0.0 collective-permute-start.9
  18.4 0.2 collective-permute-start.8
  18.6 0.0 collective-permute-done.11.refs_4_
  18.6 1.6 %collective-permute-done.10.refs_3_ = f32[24,128]{1,0:T(8,128)S(1)} collective-permute-done((f32[24,128]{1,0:T(8,128)S(1)}, f32[24,128]{1,0:T(8,128)S(1)}, u32[]{:S(2)}, u32[]{:S(2)}) %collective-permute-start.10) | collective-permute-done | bytes 12320 | tf_op jit(solution)/shard_map/ppermute | solution.py:341
  20.2 1.3 %collective-permute-done.9.refs_2_ = f32[24,128]{1,0:T(8,128)S(1)} collective-permute-done((f32[24,128]{1,0:T(8,128)S(1)}, f32[24,128]{1,0:T(8,128)S(1)}, u32[]{:S(2)}, u32[]{:S(2)}) %collective-permute-start.9) | collective-permute-done | bytes 12320 | tf_op jit(solution)/shard_map/ppermute | solution.py:341
  21.5 0.0 collective-permute-done.8.refs_1_
  21.5 0.3 shard_map.90.t2.refs_0_
  21.8 0.1 collective-permute-start.15
  22.0 2.1 %collective-permute-start.14 = (f32[24,128]{1,0:T(8,128)S(1)}, f32[24,128]{1,0:T(8,128)S(1)}, u32[]{:S(2)}, u32[]{:S(2)}) collective-permute-start(f32[24,128]{1,0:T(8,128)S(1)} %shard_map.90.t2.refs_0_), channel_id=1, source_target_pairs={{0,8},{1,9},{2,10},{3,11},{4,12},{5,13},{6,14},{7,15},{8,0},{9,1},... | collective-permute-start | bytes 36872 | tf_op jit(solution)/shard_map/ppermute | solution.py:341
  24.1 0.0 collective-permute-start.13
  24.1 0.0 collective-permute-start.12
  24.1 0.0 copy-done
  24.1 0.6 %shard_map.91 = (f32[24,512]{1,0:T(8,128)S(1)}, f32[24,128]{1,0:T(8,128)S(1)}, bf16[512,128]{1,0:T(8,128)(2,1)S(1)}, bf16[512,128]{1,0:T(8,128)(2,1)S(1)}, bf16[512,128]{1,0:T(8,128)(2,1)S(1)}) custom-call(f32[3,32,512]{2,1,0:T(8,128)S(1)} %copy-done, f32[24,128]{1,0:T(8,128)S(1)} %get-tuple-element.19.refs_0_.t0, f32[24,128]{1,0:T(8,128)S(1)} %shard_map.89.refs_0_.t1, ...), custom_call_target="tpu_custom_call" | custom-call | flops 60000000 | bytes 250000 | tf_op jit(solution)/shard_map/pallas_call | solution.py:440
  24.7 0.0 collective-permute-done.15.refs_4_
  24.7 1.2 %collective-permute-done.14.refs_3_ = f32[24,128]{1,0:T(8,128)S(1)} collective-permute-done((f32[24,128]{1,0:T(8,128)S(1)}, f32[24,128]{1,0:T(8,128)S(1)}, u32[]{:S(2)}, u32[]{:S(2)}) %collective-permute-start.14) | collective-permute-done | bytes 12320 | tf_op jit(solution)/shard_map/ppermute | solution.py:341
  25.9 1.3 %collective-permute-done.13.refs_2_ = f32[24,128]{1,0:T(8,128)S(1)} collective-permute-done((f32[24,128]{1,0:T(8,128)S(1)}, f32[24,128]{1,0:T(8,128)S(1)}, u32[]{:S(2)}, u32[]{:S(2)}) %collective-permute-start.13) | collective-permute-done | bytes 12320 | tf_op jit(solution)/shard_map/ppermute | solution.py:341
  27.2 0.0 collective-permute-done.12.refs_1_
  27.2 0.4 shard_map.92
  27.6 0.1 collective-permute-start.16
  27.7 1.2 %collective-permute-done.16 = f32[24,128]{1,0:T(8,128)S(1)} collective-permute-done((f32[24,128]{1,0:T(8,128)S(1)}, f32[24,128]{1,0:T(8,128)S(1)}, u32[]{:S(2)}, u32[]{:S(2)}) %collective-permute-start.16) | collective-permute-done | bytes 12320 | tf_op jit(solution)/shard_map/ppermute | solution.py:341
  28.9 0.4 collective-permute-start.19
  29.2 0.7 %collective-permute-start.18 = (f32[24,128]{1,0:T(8,128)S(1)}, f32[24,128]{1,0:T(8,128)S(1)}, u32[]{:S(2)}, u32[]{:S(2)}) collective-permute-start(f32[24,128]{1,0:T(8,128)S(1)} %add.12), channel_id=1, source_target_pairs={{0,5},{1,4},{2,7},{3,6},{4,1},{5,0},{6,3},{7,2},{8,13},{9,12},{10,... | collective-permute-start | bytes 36872 | tf_op jit(solution)/shard_map/ppermute | solution.py:341
  29.9 1.9 %collective-permute-start.17 = (f32[24,128]{1,0:T(8,128)S(1)}, f32[24,128]{1,0:T(8,128)S(1)}, u32[]{:S(2)}, u32[]{:S(2)}) collective-permute-start(f32[24,128]{1,0:T(8,128)S(1)} %add.12), channel_id=1, source_target_pairs={{0,3},{1,2},{2,1},{3,0},{4,7},{5,6},{6,5},{7,4},{8,11},{9,10},{10,... | collective-permute-start | bytes 36872 | tf_op jit(solution)/shard_map/ppermute | solution.py:341
  31.8 1.1 %collective-permute-done.19 = f32[24,128]{1,0:T(8,128)S(1)} collective-permute-done((f32[24,128]{1,0:T(8,128)S(1)}, f32[24,128]{1,0:T(8,128)S(1)}, u32[]{:S(2)}, u32[]{:S(2)}) %collective-permute-start.19) | collective-permute-done | bytes 12320 | tf_op jit(solution)/shard_map/ppermute | solution.py:341
  33.0 0.0 collective-permute-done.18
  33.0 0.3 collective-permute-done.17
  33.3 1.6 %collective-permute-start.22 = (f32[24,128]{1,0:T(8,128)S(1)}, f32[24,128]{1,0:T(8,128)S(1)}, u32[]{:S(2)}, u32[]{:S(2)}) collective-permute-start(f32[24,128]{1,0:T(8,128)S(1)} %add_add_fusion.refs_0_), channel_id=1, source_target_pairs={{0,25},{1,24},{2,27},{3,26},{4,29},{5,28},{6,31},{7,30},{8,17},{9,... | collective-permute-start | bytes 36872 | tf_op jit(solution)/shard_map/ppermute | solution.py:341
  34.9 0.3 collective-permute-start.21
  35.2 2.1 %collective-permute-start.20 = (f32[24,128]{1,0:T(8,128)S(1)}, f32[24,128]{1,0:T(8,128)S(1)}, u32[]{:S(2)}, u32[]{:S(2)}) collective-permute-start(f32[24,128]{1,0:T(8,128)S(1)} %add_add_fusion.refs_0_), channel_id=1, source_target_pairs={{0,9},{1,8},{2,11},{3,10},{4,13},{5,12},{6,15},{7,14},{8,1},{9,0},... | collective-permute-start | bytes 36872 | tf_op jit(solution)/shard_map/ppermute | solution.py:341
  37.3 0.9 %collective-permute-done.22.refs_3_ = f32[24,128]{1,0:T(8,128)S(1)} collective-permute-done((f32[24,128]{1,0:T(8,128)S(1)}, f32[24,128]{1,0:T(8,128)S(1)}, u32[]{:S(2)}, u32[]{:S(2)}) %collective-permute-start.22) | collective-permute-done | bytes 12320 | tf_op jit(solution)/shard_map/ppermute | solution.py:341
  38.2 0.7 %collective-permute-done.21.refs_2_ = f32[24,128]{1,0:T(8,128)S(1)} collective-permute-done((f32[24,128]{1,0:T(8,128)S(1)}, f32[24,128]{1,0:T(8,128)S(1)}, u32[]{:S(2)}, u32[]{:S(2)}) %collective-permute-start.21) | collective-permute-done | bytes 12320 | tf_op jit(solution)/shard_map/ppermute | solution.py:341
  38.9 0.0 collective-permute-done.20.refs_1_
  38.9 1.0 %shard_map.93 = (f32[3,4,512]{2,1,0:T(4,128)}, f32[3,4,36]{2,1,0:T(4,128)}) custom-call(f32[24,128]{1,0:T(8,128)S(1)} %add_add_fusion.refs_0_, f32[24,128]{1,0:T(8,128)S(1)} %collective-permute-done.20.refs_1_, f32[24,128]{1,0:T(8,128)S(1)} %collective-permute-done.21.refs_2_, f32[24,128]{1,0:T(8,128)S(1)} %collective-permute-done.22.refs_3_, ...), custom_call_target="tpu_custom_call" | custom-call | flops 50000000 | bytes 400000 | tf_op jit(solution)/shard_map/pallas_call | solution.py:457
  (2 shorter events, 0.0 us)
Async XLA Ops:
  1.7 7.3 %collective-permute-start.3 = (f32[32,128]{1,0:T(8,128)S(1)}, f32[32,128]{1,0:T(8,128)S(1)}, u32[]{:S(2)}, u32[]{:S(2)}) collective-permute-start(f32[32,128]{1,0:T(8,128)S(1)} %shard_map.86.refs_0_), channel_id=1, source_target_pairs={{0,1},{1,2},{2,3},{3,0},{4,5},{5,4},{6,7},{7,6},{8,16},{9,17},{10,... | collective-permute-start | bytes 49160 | tf_op jit(solution)/shard_map/ppermute | solution.py:341
  2.2 6.8 %collective-permute-start.2 = (f32[32,128]{1,0:T(8,128)S(1)}, f32[32,128]{1,0:T(8,128)S(1)}, u32[]{:S(2)}, u32[]{:S(2)}) collective-permute-start(f32[32,128]{1,0:T(8,128)S(1)} %shard_map.86.refs_0_), channel_id=1, source_target_pairs={{0,2},{1,0},{2,1},{3,4},{4,3},{5,6},{6,5},{7,8},{8,7},{9,10},{10,9... | collective-permute-start | bytes 49160 | tf_op jit(solution)/shard_map/ppermute | solution.py:341
  4.8 4.5 %collective-permute-start.1 = (f32[32,128]{1,0:T(8,128)S(1)}, f32[32,128]{1,0:T(8,128)S(1)}, u32[]{:S(2)}, u32[]{:S(2)}) collective-permute-start(f32[32,128]{1,0:T(8,128)S(1)} %shard_map.86.refs_0_), channel_id=1, source_target_pairs={{0,8},{1,9},{2,10},{3,11},{4,12},{5,13},{6,14},{7,15},{8,0},{9,1},... | collective-permute-start | bytes 49160 | tf_op jit(solution)/shard_map/ppermute | solution.py:341
  7.2 2.1 %collective-permute-start = (f32[32,128]{1,0:T(8,128)S(1)}, f32[32,128]{1,0:T(8,128)S(1)}, u32[]{:S(2)}, u32[]{:S(2)}) collective-permute-start(f32[32,128]{1,0:T(8,128)S(1)} %shard_map.86.refs_0_), channel_id=1, source_target_pairs={{0,1},{1,0},{2,3},{3,2},{4,5},{5,4},{6,7},{7,6},{8,9},{9,8},{10,11... | collective-permute-start | bytes 49160 | tf_op jit(solution)/shard_map/ppermute | solution.py:341
  9.7 3.3 %collective-permute-start.7 = (f32[24,128]{1,0:T(8,128)S(1)}, f32[24,128]{1,0:T(8,128)S(1)}, u32[]{:S(2)}, u32[]{:S(2)}) collective-permute-start(f32[24,128]{1,0:T(8,128)S(1)} %get-tuple-element.19.refs_0_.t0), channel_id=1, source_target_pairs={{0,2},{1,0},{2,1},{3,4},{4,3},{5,6},{6,5},{7,8},{8,7},{9,10},{10,9... | collective-permute-start | bytes 36872 | tf_op jit(solution)/shard_map/ppermute | solution.py:341
  10.9 3.8 %collective-permute-start.6 = (f32[24,128]{1,0:T(8,128)S(1)}, f32[24,128]{1,0:T(8,128)S(1)}, u32[]{:S(2)}, u32[]{:S(2)}) collective-permute-start(f32[24,128]{1,0:T(8,128)S(1)} %get-tuple-element.19.refs_0_.t0), channel_id=1, source_target_pairs={{0,8},{1,9},{2,10},{3,11},{4,12},{5,13},{6,14},{7,15},{8,0},{9,1},... | collective-permute-start | bytes 36872 | tf_op jit(solution)/shard_map/ppermute | solution.py:341
  12.9 3.1 %collective-permute-start.5 = (f32[24,128]{1,0:T(8,128)S(1)}, f32[24,128]{1,0:T(8,128)S(1)}, u32[]{:S(2)}, u32[]{:S(2)}) collective-permute-start(f32[24,128]{1,0:T(8,128)S(1)} %get-tuple-element.19.refs_0_.t0), channel_id=1, source_target_pairs={{0,1},{1,2},{2,3},{3,0},{4,5},{5,4},{6,7},{7,6},{8,16},{9,17},{10,... | collective-permute-start | bytes 36872 | tf_op jit(solution)/shard_map/ppermute | solution.py:341
  12.9 3.1 %collective-permute-start.4 = (f32[24,128]{1,0:T(8,128)S(1)}, f32[24,128]{1,0:T(8,128)S(1)}, u32[]{:S(2)}, u32[]{:S(2)}) collective-permute-start(f32[24,128]{1,0:T(8,128)S(1)} %get-tuple-element.19.refs_0_.t0), channel_id=1, source_target_pairs={{0,1},{1,0},{2,3},{3,2},{4,5},{5,4},{6,7},{7,6},{8,9},{9,8},{10,11... | collective-permute-start | bytes 36872 | tf_op jit(solution)/shard_map/ppermute | solution.py:341
  16.3 7.8 %copy-start = (f32[3,32,512]{2,1,0:T(8,128)S(1)}, f32[3,32,512]{2,1,0:T(8,128)}, u32[]{:S(2)}) copy-start(f32[3,32,512]{2,1,0:T(8,128)} %refs_4_.1) | copy-start | bytes 589828
  16.3 2.3 %collective-permute-start.11 = (f32[24,128]{1,0:T(8,128)S(1)}, f32[24,128]{1,0:T(8,128)S(1)}, u32[]{:S(2)}, u32[]{:S(2)}) collective-permute-start(f32[24,128]{1,0:T(8,128)S(1)} %shard_map.89.refs_0_.t1), channel_id=1, source_target_pairs={{0,2},{1,0},{2,1},{3,4},{4,3},{5,6},{6,5},{7,8},{8,7},{9,10},{10,9... | collective-permute-start | bytes 36872 | tf_op jit(solution)/shard_map/ppermute | solution.py:341
  16.4 3.8 %collective-permute-start.10 = (f32[24,128]{1,0:T(8,128)S(1)}, f32[24,128]{1,0:T(8,128)S(1)}, u32[]{:S(2)}, u32[]{:S(2)}) collective-permute-start(f32[24,128]{1,0:T(8,128)S(1)} %shard_map.89.refs_0_.t1), channel_id=1, source_target_pairs={{0,8},{1,9},{2,10},{3,11},{4,12},{5,13},{6,14},{7,15},{8,0},{9,1},... | collective-permute-start | bytes 36872 | tf_op jit(solution)/shard_map/ppermute | solution.py:341
  18.4 3.1 %collective-permute-start.9 = (f32[24,128]{1,0:T(8,128)S(1)}, f32[24,128]{1,0:T(8,128)S(1)}, u32[]{:S(2)}, u32[]{:S(2)}) collective-permute-start(f32[24,128]{1,0:T(8,128)S(1)} %shard_map.89.refs_0_.t1), channel_id=1, source_target_pairs={{0,1},{1,2},{2,3},{3,0},{4,5},{5,4},{6,7},{7,6},{8,16},{9,17},{10,... | collective-permute-start | bytes 36872 | tf_op jit(solution)/shard_map/ppermute | solution.py:341
  18.4 3.1 %collective-permute-start.8 = (f32[24,128]{1,0:T(8,128)S(1)}, f32[24,128]{1,0:T(8,128)S(1)}, u32[]{:S(2)}, u32[]{:S(2)}) collective-permute-start(f32[24,128]{1,0:T(8,128)S(1)} %shard_map.89.refs_0_.t1), channel_id=1, source_target_pairs={{0,1},{1,0},{2,3},{3,2},{4,5},{5,4},{6,7},{7,6},{8,9},{9,8},{10,11... | collective-permute-start | bytes 36872 | tf_op jit(solution)/shard_map/ppermute | solution.py:341
  21.8 2.9 %collective-permute-start.15 = (f32[24,128]{1,0:T(8,128)S(1)}, f32[24,128]{1,0:T(8,128)S(1)}, u32[]{:S(2)}, u32[]{:S(2)}) collective-permute-start(f32[24,128]{1,0:T(8,128)S(1)} %shard_map.90.t2.refs_0_), channel_id=1, source_target_pairs={{0,2},{1,0},{2,1},{3,4},{4,3},{5,6},{6,5},{7,8},{8,7},{9,10},{10,9... | collective-permute-start | bytes 36872 | tf_op jit(solution)/shard_map/ppermute | solution.py:341
  22.0 3.9 %collective-permute-start.14 = (f32[24,128]{1,0:T(8,128)S(1)}, f32[24,128]{1,0:T(8,128)S(1)}, u32[]{:S(2)}, u32[]{:S(2)}) collective-permute-start(f32[24,128]{1,0:T(8,128)S(1)} %shard_map.90.t2.refs_0_), channel_id=1, source_target_pairs={{0,8},{1,9},{2,10},{3,11},{4,12},{5,13},{6,14},{7,15},{8,0},{9,1},... | collective-permute-start | bytes 36872 | tf_op jit(solution)/shard_map/ppermute | solution.py:341
  24.1 3.1 %collective-permute-start.13 = (f32[24,128]{1,0:T(8,128)S(1)}, f32[24,128]{1,0:T(8,128)S(1)}, u32[]{:S(2)}, u32[]{:S(2)}) collective-permute-start(f32[24,128]{1,0:T(8,128)S(1)} %shard_map.90.t2.refs_0_), channel_id=1, source_target_pairs={{0,1},{1,2},{2,3},{3,0},{4,5},{5,4},{6,7},{7,6},{8,16},{9,17},{10,... | collective-permute-start | bytes 36872 | tf_op jit(solution)/shard_map/ppermute | solution.py:341
  24.1 3.1 %collective-permute-start.12 = (f32[24,128]{1,0:T(8,128)S(1)}, f32[24,128]{1,0:T(8,128)S(1)}, u32[]{:S(2)}, u32[]{:S(2)}) collective-permute-start(f32[24,128]{1,0:T(8,128)S(1)} %shard_map.90.t2.refs_0_), channel_id=1, source_target_pairs={{0,1},{1,0},{2,3},{3,2},{4,5},{5,4},{6,7},{7,6},{8,9},{9,8},{10,11... | collective-permute-start | bytes 36872 | tf_op jit(solution)/shard_map/ppermute | solution.py:341
  27.6 1.2 %collective-permute-start.16 = (f32[24,128]{1,0:T(8,128)S(1)}, f32[24,128]{1,0:T(8,128)S(1)}, u32[]{:S(2)}, u32[]{:S(2)}) collective-permute-start(f32[24,128]{1,0:T(8,128)S(1)} %get-tuple-element.26), channel_id=1, source_target_pairs={{0,1},{1,0},{2,3},{3,2},{4,5},{5,4},{6,7},{7,6},{8,9},{9,8},{10,11... | collective-permute-start | bytes 36872 | tf_op jit(solution)/shard_map/ppermute | solution.py:341
  28.9 4.1 %collective-permute-start.19 = (f32[24,128]{1,0:T(8,128)S(1)}, f32[24,128]{1,0:T(8,128)S(1)}, u32[]{:S(2)}, u32[]{:S(2)}) collective-permute-start(f32[24,128]{1,0:T(8,128)S(1)} %add.12), channel_id=1, source_target_pairs={{0,7},{1,6},{2,5},{3,4},{4,3},{5,2},{6,1},{7,0},{8,15},{9,14},{10,... | collective-permute-start | bytes 36872 | tf_op jit(solution)/shard_map/ppermute | solution.py:341
  29.2 3.8 %collective-permute-start.18 = (f32[24,128]{1,0:T(8,128)S(1)}, f32[24,128]{1,0:T(8,128)S(1)}, u32[]{:S(2)}, u32[]{:S(2)}) collective-permute-start(f32[24,128]{1,0:T(8,128)S(1)} %add.12), channel_id=1, source_target_pairs={{0,5},{1,4},{2,7},{3,6},{4,1},{5,0},{6,3},{7,2},{8,13},{9,12},{10,... | collective-permute-start | bytes 36872 | tf_op jit(solution)/shard_map/ppermute | solution.py:341
  29.9 3.3 %collective-permute-start.17 = (f32[24,128]{1,0:T(8,128)S(1)}, f32[24,128]{1,0:T(8,128)S(1)}, u32[]{:S(2)}, u32[]{:S(2)}) collective-permute-start(f32[24,128]{1,0:T(8,128)S(1)} %add.12), channel_id=1, source_target_pairs={{0,3},{1,2},{2,1},{3,0},{4,7},{5,6},{6,5},{7,4},{8,11},{9,10},{10,... | collective-permute-start | bytes 36872 | tf_op jit(solution)/shard_map/ppermute | solution.py:341
  33.3 4.9 %collective-permute-start.22 = (f32[24,128]{1,0:T(8,128)S(1)}, f32[24,128]{1,0:T(8,128)S(1)}, u32[]{:S(2)}, u32[]{:S(2)}) collective-permute-start(f32[24,128]{1,0:T(8,128)S(1)} %add_add_fusion.refs_0_), channel_id=1, source_target_pairs={{0,25},{1,24},{2,27},{3,26},{4,29},{5,28},{6,31},{7,30},{8,17},{9,... | collective-permute-start | bytes 36872 | tf_op jit(solution)/shard_map/ppermute | solution.py:341
  34.9 4.1 %collective-permute-start.21 = (f32[24,128]{1,0:T(8,128)S(1)}, f32[24,128]{1,0:T(8,128)S(1)}, u32[]{:S(2)}, u32[]{:S(2)}) collective-permute-start(f32[24,128]{1,0:T(8,128)S(1)} %add_add_fusion.refs_0_), channel_id=1, source_target_pairs={{0,17},{1,16},{2,19},{3,18},{4,21},{5,20},{6,23},{7,22},{8,25},{9,... | collective-permute-start | bytes 36872 | tf_op jit(solution)/shard_map/ppermute | solution.py:341
  35.2 3.7 %collective-permute-start.20 = (f32[24,128]{1,0:T(8,128)S(1)}, f32[24,128]{1,0:T(8,128)S(1)}, u32[]{:S(2)}, u32[]{:S(2)}) collective-permute-start(f32[24,128]{1,0:T(8,128)S(1)} %add_add_fusion.refs_0_), channel_id=1, source_target_pairs={{0,9},{1,8},{2,11},{3,10},{4,13},{5,12},{6,15},{7,14},{8,1},{9,0},... | collective-permute-start | bytes 36872 | tf_op jit(solution)/shard_map/ppermute | solution.py:341

commit v26 on v21

--- a/solution.py
+++ b/solution.py
@@ -63,8 +63,7 @@
 
 def split_dot(x, parts):
     left = [part.astype(jnp.float32) for part in split(x)]
-    left.append(jnp.zeros((-3 * x.shape[0] % 16, x.shape[1]), jnp.float32))
-    left = jnp.concatenate([part for part in left if part.shape[0]], axis=0).astype(jnp.bfloat16)
+    left = jnp.concatenate(left, axis=0).astype(jnp.bfloat16)
     products = dot(left, parts[0]) + dot(left, parts[1]) + dot(left, parts[2])
     rows = x.shape[0]
     return products[:rows] + (products[rows : 2 * rows] + products[2 * rows : 3 * rows])

time: 40.1 us -> 40.1 us (level)
  no operation moved by 1% of the time
where the time goes in v26:
time: 40.1 us; the launch traced here: 39.9 us
  starting transfers between devices  20.9 us (52%)
  waiting for transfers between devices  13 us (32%)
  Pallas kernels  5.23 us (13%)
  between operations  0.72 us (2%)
    ppermute x23, starting transfers between devices, send(): lax.ppermute(value, 'dom', [(d, target[d]) for d in range(lax.axis_size('...  20.9 us
    ppermute x23, waiting for transfers between devices, send(): lax.ppermute(value, 'dom', [(d, target[d]) for d in range(lax.axis_size('...  13 us
    pallas_call x1, Pallas kernels, local(): call(prepare_kernel, [((width, rows), bf16), ((width, rows), bf16), ((8 *...  1.31 us
    pallas_call x1, Pallas kernels, local(): call(start_kernel, [((comps * blocks + 8, 128), f32)], [HBM] * 4, 600000,...  1.08 us
    pallas_call x1, Pallas kernels, local(): call(lambda *refs: finish_kernel(total, refs[:count], *refs[count:]), [((...  0.97 us
  transfers between devices with their start and end apart: 23, of which 12 were waited for; matrix products, arithmetic and copies ran while one was open for 0% of the time, Pallas kernels for 5%

profile of v26, /device:TPU:0, one launch (start us, length us, event | category | flops | bytes accessed | tf_op | source)
XLA Modules:
  0.0 39.9 jit_solution(76606375252684087)
XLA Ops:
  0.6 1.1 %shard_map.86.refs_0_ = f32[32,128]{1,0:T(8,128)S(1)} custom-call(f32[3,32,512]{2,1,0:T(8,128)} %refs_4_.1, f32[3,32]{1,0:T(4,128)} %mix_in.1, s32[1,4,8]{2,1,0:T(4,128)} %list_in.1, s32[1,4]{1,0:T(1,128)} %count_in.1), custom_call_target="tpu_custom_call" | custom-call | flops 600000 | bytes 250000 | tf_op jit(solution)/shard_map/pallas_call | solution.py:394
  1.7 0.5 %collective-permute-start.3 = (f32[32,128]{1,0:T(8,128)S(1)}, f32[32,128]{1,0:T(8,128)S(1)}, u32[]{:S(2)}, u32[]{:S(2)}) collective-permute-start(f32[32,128]{1,0:T(8,128)S(1)} %shard_map.86.refs_0_), channel_id=1, source_target_pairs={{0,1},{1,2},{2,3},{3,0},{4,5},{5,4},{6,7},{7,6},{8,16},{9,17},{10,... | collective-permute-start | bytes 49160 | tf_op jit(solution)/shard_map/ppermute | solution.py:340
  2.2 2.5 %collective-permute-start.2 = (f32[32,128]{1,0:T(8,128)S(1)}, f32[32,128]{1,0:T(8,128)S(1)}, u32[]{:S(2)}, u32[]{:S(2)}) collective-permute-start(f32[32,128]{1,0:T(8,128)S(1)} %shard_map.86.refs_0_), channel_id=1, source_target_pairs={{0,2},{1,0},{2,1},{3,4},{4,3},{5,6},{6,5},{7,8},{8,7},{9,10},{10,9... | collective-permute-start | bytes 49160 | tf_op jit(solution)/shard_map/ppermute | solution.py:340
  4.8 2.5 %collective-permute-start.1 = (f32[32,128]{1,0:T(8,128)S(1)}, f32[32,128]{1,0:T(8,128)S(1)}, u32[]{:S(2)}, u32[]{:S(2)}) collective-permute-start(f32[32,128]{1,0:T(8,128)S(1)} %shard_map.86.refs_0_), channel_id=1, source_target_pairs={{0,8},{1,9},{2,10},{3,11},{4,12},{5,13},{6,14},{7,15},{8,0},{9,1},... | collective-permute-start | bytes 49160 | tf_op jit(solution)/shard_map/ppermute | solution.py:340
  7.2 0.5 %collective-permute-start = (f32[32,128]{1,0:T(8,128)S(1)}, f32[32,128]{1,0:T(8,128)S(1)}, u32[]{:S(2)}, u32[]{:S(2)}) collective-permute-start(f32[32,128]{1,0:T(8,128)S(1)} %shard_map.86.refs_0_), channel_id=1, source_target_pairs={{0,1},{1,0},{2,3},{3,2},{4,5},{5,4},{6,7},{7,6},{8,9},{9,8},{10,11... | collective-permute-start | bytes 49160 | tf_op jit(solution)/shard_map/ppermute | solution.py:340
  7.7 1.3 %shard_map.87 = (bf16[256,512]{1,0:T(8,128)(2,1)S(1)}, bf16[256,512]{1,0:T(8,128)(2,1)S(1)}, f32[56,128]{1,0:T(8,128)S(1)}) custom-call(f32[512,256]{1,0:T(8,128)} %strips_in.1, s32[4,8]{1,0:T(4,128)} %bitcast.2, f32[4]{0:T(128)} %shifts_in.1), custom_call_target="tpu_custom_call" | custom-call | flops 1000000 | bytes 1000000 | tf_op jit(solution)/shard_map/pallas_call | solution.py:408
  9.0 0.0 collective-permute-done.3.refs_4_
  9.0 0.0 collective-permute-done.2.refs_3_
  9.0 0.3 collective-permute-done.1.refs_2_
  9.3 0.0 collective-permute-done.refs_1_
  9.3 0.4 shard_map.88
  9.7 1.2 %collective-permute-start.7 = (f32[24,128]{1,0:T(8,128)S(1)}, f32[24,128]{1,0:T(8,128)S(1)}, u32[]{:S(2)}, u32[]{:S(2)}) collective-permute-start(f32[24,128]{1,0:T(8,128)S(1)} %get-tuple-element.19.refs_0_.t0), channel_id=1, source_target_pairs={{0,2},{1,0},{2,1},{3,4},{4,3},{5,6},{6,5},{7,8},{8,7},{9,10},{10,9... | collective-permute-start | bytes 36872 | tf_op jit(solution)/shard_map/ppermute | solution.py:340
  10.9 2.0 %collective-permute-start.6 = (f32[24,128]{1,0:T(8,128)S(1)}, f32[24,128]{1,0:T(8,128)S(1)}, u32[]{:S(2)}, u32[]{:S(2)}) collective-permute-start(f32[24,128]{1,0:T(8,128)S(1)} %get-tuple-element.19.refs_0_.t0), channel_id=1, source_target_pairs={{0,8},{1,9},{2,10},{3,11},{4,12},{5,13},{6,14},{7,15},{8,0},{9,1},... | collective-permute-start | bytes 36872 | tf_op jit(solution)/shard_map/ppermute | solution.py:340
  12.9 0.0 collective-permute-start.5
  12.9 0.1 collective-permute-start.4
  13.0 0.0 collective-permute-done.7.refs_4_
  13.0 1.7 %collective-permute-done.6.refs_3_ = f32[24,128]{1,0:T(8,128)S(1)} collective-permute-done((f32[24,128]{1,0:T(8,128)S(1)}, f32[24,128]{1,0:T(8,128)S(1)}, u32[]{:S(2)}, u32[]{:S(2)}) %collective-permute-start.6) | collective-permute-done | bytes 12320 | tf_op jit(solution)/shard_map/ppermute | solution.py:340
  14.7 1.3 %collective-permute-done.5.refs_2_ = f32[24,128]{1,0:T(8,128)S(1)} collective-permute-done((f32[24,128]{1,0:T(8,128)S(1)}, f32[24,128]{1,0:T(8,128)S(1)}, u32[]{:S(2)}, u32[]{:S(2)}) %collective-permute-start.5) | collective-permute-done | bytes 12320 | tf_op jit(solution)/shard_map/ppermute | solution.py:340
  16.0 0.0 collective-permute-done.4.refs_1_
  16.0 0.3 shard_map.89.refs_0_.t1
  16.3 0.0 copy-start
  16.3 0.1 collective-permute-start.11
  16.4 2.0 %collective-permute-start.10 = (f32[24,128]{1,0:T(8,128)S(1)}, f32[24,128]{1,0:T(8,128)S(1)}, u32[]{:S(2)}, u32[]{:S(2)}) collective-permute-start(f32[24,128]{1,0:T(8,128)S(1)} %shard_map.89.refs_0_.t1), channel_id=1, source_target_pairs={{0,8},{1,9},{2,10},{3,11},{4,12},{5,13},{6,14},{7,15},{8,0},{9,1},... | collective-permute-start | bytes 36872 | tf_op jit(solution)/shard_map/ppermute | solution.py:340
  18.4 0.0 collective-permute-start.9
  18.4 0.2 collective-permute-start.8
  18.6 0.0 collective-permute-done.11.refs_4_
  18.6 1.6 %collective-permute-done.10.refs_3_ = f32[24,128]{1,0:T(8,128)S(1)} collective-permute-done((f32[24,128]{1,0:T(8,128)S(1)}, f32[24,128]{1,0:T(8,128)S(1)}, u32[]{:S(2)}, u32[]{:S(2)}) %collective-permute-start.10) | collective-permute-done | bytes 12320 | tf_op jit(solution)/shard_map/ppermute | solution.py:340
  20.2 1.3 %collective-permute-done.9.refs_2_ = f32[24,128]{1,0:T(8,128)S(1)} collective-permute-done((f32[24,128]{1,0:T(8,128)S(1)}, f32[24,128]{1,0:T(8,128)S(1)}, u32[]{:S(2)}, u32[]{:S(2)}) %collective-permute-start.9) | collective-permute-done | bytes 12320 | tf_op jit(solution)/shard_map/ppermute | solution.py:340
  21.5 0.0 collective-permute-done.8.refs_1_
  21.5 0.3 shard_map.90.t2.refs_0_
  21.8 0.1 collective-permute-start.15
  22.0 2.1 %collective-permute-start.14 = (f32[24,128]{1,0:T(8,128)S(1)}, f32[24,128]{1,0:T(8,128)S(1)}, u32[]{:S(2)}, u32[]{:S(2)}) collective-permute-start(f32[24,128]{1,0:T(8,128)S(1)} %shard_map.90.t2.refs_0_), channel_id=1, source_target_pairs={{0,8},{1,9},{2,10},{3,11},{4,12},{5,13},{6,14},{7,15},{8,0},{9,1},... | collective-permute-start | bytes 36872 | tf_op jit(solution)/shard_map/ppermute | solution.py:340
  24.1 0.0 collective-permute-start.13
  24.1 0.0 collective-permute-start.12
  24.1 0.0 copy-done
  24.1 0.6 %shard_map.91 = (f32[24,512]{1,0:T(8,128)S(1)}, f32[24,128]{1,0:T(8,128)S(1)}, bf16[512,128]{1,0:T(8,128)(2,1)S(1)}, bf16[512,128]{1,0:T(8,128)(2,1)S(1)}, bf16[512,128]{1,0:T(8,128)(2,1)S(1)}) custom-call(f32[3,32,512]{2,1,0:T(8,128)S(1)} %copy-done, f32[24,128]{1,0:T(8,128)S(1)} %get-tuple-element.19.refs_0_.t0, f32[24,128]{1,0:T(8,128)S(1)} %shard_map.89.refs_0_.t1, ...), custom_call_target="tpu_custom_call" | custom-call | flops 60000000 | bytes 250000 | tf_op jit(solution)/shard_map/pallas_call | solution.py:439
  24.7 0.0 collective-permute-done.15.refs_4_
  24.7 1.2 %collective-permute-done.14.refs_3_ = f32[24,128]{1,0:T(8,128)S(1)} collective-permute-done((f32[24,128]{1,0:T(8,128)S(1)}, f32[24,128]{1,0:T(8,128)S(1)}, u32[]{:S(2)}, u32[]{:S(2)}) %collective-permute-start.14) | collective-permute-done | bytes 12320 | tf_op jit(solution)/shard_map/ppermute | solution.py:340
  25.9 1.3 %collective-permute-done.13.refs_2_ = f32[24,128]{1,0:T(8,128)S(1)} collective-permute-done((f32[24,128]{1,0:T(8,128)S(1)}, f32[24,128]{1,0:T(8,128)S(1)}, u32[]{:S(2)}, u32[]{:S(2)}) %collective-permute-start.13) | collective-permute-done | bytes 12320 | tf_op jit(solution)/shard_map/ppermute | solution.py:340
  27.2 0.0 collective-permute-done.12.refs_1_
  27.2 0.4 shard_map.92
  27.6 0.1 collective-permute-start.16
  27.7 1.2 %collective-permute-done.16 = f32[24,128]{1,0:T(8,128)S(1)} collective-permute-done((f32[24,128]{1,0:T(8,128)S(1)}, f32[24,128]{1,0:T(8,128)S(1)}, u32[]{:S(2)}, u32[]{:S(2)}) %collective-permute-start.16) | collective-permute-done | bytes 12320 | tf_op jit(solution)/shard_map/ppermute | solution.py:340
  28.9 0.4 collective-permute-start.19
  29.2 0.7 %collective-permute-start.18 = (f32[24,128]{1,0:T(8,128)S(1)}, f32[24,128]{1,0:T(8,128)S(1)}, u32[]{:S(2)}, u32[]{:S(2)}) collective-permute-start(f32[24,128]{1,0:T(8,128)S(1)} %add.12), channel_id=1, source_target_pairs={{0,5},{1,4},{2,7},{3,6},{4,1},{5,0},{6,3},{7,2},{8,13},{9,12},{10,... | collective-permute-start | bytes 36872 | tf_op jit(solution)/shard_map/ppermute | solution.py:340
  29.9 1.9 %collective-permute-start.17 = (f32[24,128]{1,0:T(8,128)S(1)}, f32[24,128]{1,0:T(8,128)S(1)}, u32[]{:S(2)}, u32[]{:S(2)}) collective-permute-start(f32[24,128]{1,0:T(8,128)S(1)} %add.12), channel_id=1, source_target_pairs={{0,3},{1,2},{2,1},{3,0},{4,7},{5,6},{6,5},{7,4},{8,11},{9,10},{10,... | collective-permute-start | bytes 36872 | tf_op jit(solution)/shard_map/ppermute | solution.py:340
  31.8 1.1 %collective-permute-done.19 = f32[24,128]{1,0:T(8,128)S(1)} collective-permute-done((f32[24,128]{1,0:T(8,128)S(1)}, f32[24,128]{1,0:T(8,128)S(1)}, u32[]{:S(2)}, u32[]{:S(2)}) %collective-permute-start.19) | collective-permute-done | bytes 12320 | tf_op jit(solution)/shard_map/ppermute | solution.py:340
  33.0 0.0 collective-permute-done.18
  33.0 0.3 collective-permute-done.17
  33.3 1.6 %collective-permute-start.22 = (f32[24,128]{1,0:T(8,128)S(1)}, f32[24,128]{1,0:T(8,128)S(1)}, u32[]{:S(2)}, u32[]{:S(2)}) collective-permute-start(f32[24,128]{1,0:T(8,128)S(1)} %add_add_fusion.refs_0_), channel_id=1, source_target_pairs={{0,25},{1,24},{2,27},{3,26},{4,29},{5,28},{6,31},{7,30},{8,17},{9,... | collective-permute-start | bytes 36872 | tf_op jit(solution)/shard_map/ppermute | solution.py:340
  34.9 0.3 collective-permute-start.21
  35.2 2.1 %collective-permute-start.20 = (f32[24,128]{1,0:T(8,128)S(1)}, f32[24,128]{1,0:T(8,128)S(1)}, u32[]{:S(2)}, u32[]{:S(2)}) collective-permute-start(f32[24,128]{1,0:T(8,128)S(1)} %add_add_fusion.refs_0_), channel_id=1, source_target_pairs={{0,9},{1,8},{2,11},{3,10},{4,13},{5,12},{6,15},{7,14},{8,1},{9,0},... | collective-permute-start | bytes 36872 | tf_op jit(solution)/shard_map/ppermute | solution.py:340
  37.3 0.9 %collective-permute-done.22.refs_3_ = f32[24,128]{1,0:T(8,128)S(1)} collective-permute-done((f32[24,128]{1,0:T(8,128)S(1)}, f32[24,128]{1,0:T(8,128)S(1)}, u32[]{:S(2)}, u32[]{:S(2)}) %collective-permute-start.22) | collective-permute-done | bytes 12320 | tf_op jit(solution)/shard_map/ppermute | solution.py:340
  38.2 0.7 %collective-permute-done.21.refs_2_ = f32[24,128]{1,0:T(8,128)S(1)} collective-permute-done((f32[24,128]{1,0:T(8,128)S(1)}, f32[24,128]{1,0:T(8,128)S(1)}, u32[]{:S(2)}, u32[]{:S(2)}) %collective-permute-start.21) | collective-permute-done | bytes 12320 | tf_op jit(solution)/shard_map/ppermute | solution.py:340
  38.9 0.0 collective-permute-done.20.refs_1_
  38.9 1.0 %shard_map.93 = (f32[3,4,512]{2,1,0:T(4,128)}, f32[3,4,36]{2,1,0:T(4,128)}) custom-call(f32[24,128]{1,0:T(8,128)S(1)} %add_add_fusion.refs_0_, f32[24,128]{1,0:T(8,128)S(1)} %collective-permute-done.20.refs_1_, f32[24,128]{1,0:T(8,128)S(1)} %collective-permute-done.21.refs_2_, f32[24,128]{1,0:T(8,128)S(1)} %collective-permute-done.22.refs_3_, ...), custom_call_target="tpu_custom_call" | custom-call | flops 50000000 | bytes 400000 | tf_op jit(solution)/shard_map/pallas_call | solution.py:456
  (2 shorter events, 0.0 us)
Async XLA Ops:
  1.7 7.3 %collective-permute-start.3 = (f32[32,128]{1,0:T(8,128)S(1)}, f32[32,128]{1,0:T(8,128)S(1)}, u32[]{:S(2)}, u32[]{:S(2)}) collective-permute-start(f32[32,128]{1,0:T(8,128)S(1)} %shard_map.86.refs_0_), channel_id=1, source_target_pairs={{0,1},{1,2},{2,3},{3,0},{4,5},{5,4},{6,7},{7,6},{8,16},{9,17},{10,... | collective-permute-start | bytes 49160 | tf_op jit(solution)/shard_map/ppermute | solution.py:340
  2.2 6.8 %collective-permute-start.2 = (f32[32,128]{1,0:T(8,128)S(1)}, f32[32,128]{1,0:T(8,128)S(1)}, u32[]{:S(2)}, u32[]{:S(2)}) collective-permute-start(f32[32,128]{1,0:T(8,128)S(1)} %shard_map.86.refs_0_), channel_id=1, source_target_pairs={{0,2},{1,0},{2,1},{3,4},{4,3},{5,6},{6,5},{7,8},{8,7},{9,10},{10,9... | collective-permute-start | bytes 49160 | tf_op jit(solution)/shard_map/ppermute | solution.py:340
  4.8 4.5 %collective-permute-start.1 = (f32[32,128]{1,0:T(8,128)S(1)}, f32[32,128]{1,0:T(8,128)S(1)}, u32[]{:S(2)}, u32[]{:S(2)}) collective-permute-start(f32[32,128]{1,0:T(8,128)S(1)} %shard_map.86.refs_0_), channel_id=1, source_target_pairs={{0,8},{1,9},{2,10},{3,11},{4,12},{5,13},{6,14},{7,15},{8,0},{9,1},... | collective-permute-start | bytes 49160 | tf_op jit(solution)/shard_map/ppermute | solution.py:340
  7.2 2.1 %collective-permute-start = (f32[32,128]{1,0:T(8,128)S(1)}, f32[32,128]{1,0:T(8,128)S(1)}, u32[]{:S(2)}, u32[]{:S(2)}) collective-permute-start(f32[32,128]{1,0:T(8,128)S(1)} %shard_map.86.refs_0_), channel_id=1, source_target_pairs={{0,1},{1,0},{2,3},{3,2},{4,5},{5,4},{6,7},{7,6},{8,9},{9,8},{10,11... | collective-permute-start | bytes 49160 | tf_op jit(solution)/shard_map/ppermute | solution.py:340
  9.7 3.3 %collective-permute-start.7 = (f32[24,128]{1,0:T(8,128)S(1)}, f32[24,128]{1,0:T(8,128)S(1)}, u32[]{:S(2)}, u32[]{:S(2)}) collective-permute-start(f32[24,128]{1,0:T(8,128)S(1)} %get-tuple-element.19.refs_0_.t0), channel_id=1, source_target_pairs={{0,2},{1,0},{2,1},{3,4},{4,3},{5,6},{6,5},{7,8},{8,7},{9,10},{10,9... | collective-permute-start | bytes 36872 | tf_op jit(solution)/shard_map/ppermute | solution.py:340
  10.9 3.8 %collective-permute-start.6 = (f32[24,128]{1,0:T(8,128)S(1)}, f32[24,128]{1,0:T(8,128)S(1)}, u32[]{:S(2)}, u32[]{:S(2)}) collective-permute-start(f32[24,128]{1,0:T(8,128)S(1)} %get-tuple-element.19.refs_0_.t0), channel_id=1, source_target_pairs={{0,8},{1,9},{2,10},{3,11},{4,12},{5,13},{6,14},{7,15},{8,0},{9,1},... | collective-permute-start | bytes 36872 | tf_op jit(solution)/shard_map/ppermute | solution.py:340
  12.9 3.1 %collective-permute-start.5 = (f32[24,128]{1,0:T(8,128)S(1)}, f32[24,128]{1,0:T(8,128)S(1)}, u32[]{:S(2)}, u32[]{:S(2)}) collective-permute-start(f32[24,128]{1,0:T(8,128)S(1)} %get-tuple-element.19.refs_0_.t0), channel_id=1, source_target_pairs={{0,1},{1,2},{2,3},{3,0},{4,5},{5,4},{6,7},{7,6},{8,16},{9,17},{10,... | collective-permute-start | bytes 36872 | tf_op jit(solution)/shard_map/ppermute | solution.py:340
  12.9 3.1 %collective-permute-start.4 = (f32[24,128]{1,0:T(8,128)S(1)}, f32[24,128]{1,0:T(8,128)S(1)}, u32[]{:S(2)}, u32[]{:S(2)}) collective-permute-start(f32[24,128]{1,0:T(8,128)S(1)} %get-tuple-element.19.refs_0_.t0), channel_id=1, source_target_pairs={{0,1},{1,0},{2,3},{3,2},{4,5},{5,4},{6,7},{7,6},{8,9},{9,8},{10,11... | collective-permute-start | bytes 36872 | tf_op jit(solution)/shard_map/ppermute | solution.py:340
  16.3 7.8 %copy-start = (f32[3,32,512]{2,1,0:T(8,128)S(1)}, f32[3,32,512]{2,1,0:T(8,128)}, u32[]{:S(2)}) copy-start(f32[3,32,512]{2,1,0:T(8,128)} %refs_4_.1) | copy-start | bytes 589828
  16.3 2.3 %collective-permute-start.11 = (f32[24,128]{1,0:T(8,128)S(1)}, f32[24,128]{1,0:T(8,128)S(1)}, u32[]{:S(2)}, u32[]{:S(2)}) collective-permute-start(f32[24,128]{1,0:T(8,128)S(1)} %shard_map.89.refs_0_.t1), channel_id=1, source_target_pairs={{0,2},{1,0},{2,1},{3,4},{4,3},{5,6},{6,5},{7,8},{8,7},{9,10},{10,9... | collective-permute-start | bytes 36872 | tf_op jit(solution)/shard_map/ppermute | solution.py:340
  16.4 3.8 %collective-permute-start.10 = (f32[24,128]{1,0:T(8,128)S(1)}, f32[24,128]{1,0:T(8,128)S(1)}, u32[]{:S(2)}, u32[]{:S(2)}) collective-permute-start(f32[24,128]{1,0:T(8,128)S(1)} %shard_map.89.refs_0_.t1), channel_id=1, source_target_pairs={{0,8},{1,9},{2,10},{3,11},{4,12},{5,13},{6,14},{7,15},{8,0},{9,1},... | collective-permute-start | bytes 36872 | tf_op jit(solution)/shard_map/ppermute | solution.py:340
  18.4 3.1 %collective-permute-start.9 = (f32[24,128]{1,0:T(8,128)S(1)}, f32[24,128]{1,0:T(8,128)S(1)}, u32[]{:S(2)}, u32[]{:S(2)}) collective-permute-start(f32[24,128]{1,0:T(8,128)S(1)} %shard_map.89.refs_0_.t1), channel_id=1, source_target_pairs={{0,1},{1,2},{2,3},{3,0},{4,5},{5,4},{6,7},{7,6},{8,16},{9,17},{10,... | collective-permute-start | bytes 36872 | tf_op jit(solution)/shard_map/ppermute | solution.py:340
  18.4 3.1 %collective-permute-start.8 = (f32[24,128]{1,0:T(8,128)S(1)}, f32[24,128]{1,0:T(8,128)S(1)}, u32[]{:S(2)}, u32[]{:S(2)}) collective-permute-start(f32[24,128]{1,0:T(8,128)S(1)} %shard_map.89.refs_0_.t1), channel_id=1, source_target_pairs={{0,1},{1,0},{2,3},{3,2},{4,5},{5,4},{6,7},{7,6},{8,9},{9,8},{10,11... | collective-permute-start | bytes 36872 | tf_op jit(solution)/shard_map/ppermute | solution.py:340
  21.8 2.9 %collective-permute-start.15 = (f32[24,128]{1,0:T(8,128)S(1)}, f32[24,128]{1,0:T(8,128)S(1)}, u32[]{:S(2)}, u32[]{:S(2)}) collective-permute-start(f32[24,128]{1,0:T(8,128)S(1)} %shard_map.90.t2.refs_0_), channel_id=1, source_target_pairs={{0,2},{1,0},{2,1},{3,4},{4,3},{5,6},{6,5},{7,8},{8,7},{9,10},{10,9... | collective-permute-start | bytes 36872 | tf_op jit(solution)/shard_map/ppermute | solution.py:340
  22.0 3.9 %collective-permute-start.14 = (f32[24,128]{1,0:T(8,128)S(1)}, f32[24,128]{1,0:T(8,128)S(1)}, u32[]{:S(2)}, u32[]{:S(2)}) collective-permute-start(f32[24,128]{1,0:T(8,128)S(1)} %shard_map.90.t2.refs_0_), channel_id=1, source_target_pairs={{0,8},{1,9},{2,10},{3,11},{4,12},{5,13},{6,14},{7,15},{8,0},{9,1},... | collective-permute-start | bytes 36872 | tf_op jit(solution)/shard_map/ppermute | solution.py:340
  24.1 3.1 %collective-permute-start.13 = (f32[24,128]{1,0:T(8,128)S(1)}, f32[24,128]{1,0:T(8,128)S(1)}, u32[]{:S(2)}, u32[]{:S(2)}) collective-permute-start(f32[24,128]{1,0:T(8,128)S(1)} %shard_map.90.t2.refs_0_), channel_id=1, source_target_pairs={{0,1},{1,2},{2,3},{3,0},{4,5},{5,4},{6,7},{7,6},{8,16},{9,17},{10,... | collective-permute-start | bytes 36872 | tf_op jit(solution)/shard_map/ppermute | solution.py:340
  24.1 3.1 %collective-permute-start.12 = (f32[24,128]{1,0:T(8,128)S(1)}, f32[24,128]{1,0:T(8,128)S(1)}, u32[]{:S(2)}, u32[]{:S(2)}) collective-permute-start(f32[24,128]{1,0:T(8,128)S(1)} %shard_map.90.t2.refs_0_), channel_id=1, source_target_pairs={{0,1},{1,0},{2,3},{3,2},{4,5},{5,4},{6,7},{7,6},{8,9},{9,8},{10,11... | collective-permute-start | bytes 36872 | tf_op jit(solution)/shard_map/ppermute | solution.py:340
  27.6 1.2 %collective-permute-start.16 = (f32[24,128]{1,0:T(8,128)S(1)}, f32[24,128]{1,0:T(8,128)S(1)}, u32[]{:S(2)}, u32[]{:S(2)}) collective-permute-start(f32[24,128]{1,0:T(8,128)S(1)} %get-tuple-element.26), channel_id=1, source_target_pairs={{0,1},{1,0},{2,3},{3,2},{4,5},{5,4},{6,7},{7,6},{8,9},{9,8},{10,11... | collective-permute-start | bytes 36872 | tf_op jit(solution)/shard_map/ppermute | solution.py:340
  28.9 4.1 %collective-permute-start.19 = (f32[24,128]{1,0:T(8,128)S(1)}, f32[24,128]{1,0:T(8,128)S(1)}, u32[]{:S(2)}, u32[]{:S(2)}) collective-permute-start(f32[24,128]{1,0:T(8,128)S(1)} %add.12), channel_id=1, source_target_pairs={{0,7},{1,6},{2,5},{3,4},{4,3},{5,2},{6,1},{7,0},{8,15},{9,14},{10,... | collective-permute-start | bytes 36872 | tf_op jit(solution)/shard_map/ppermute | solution.py:340
  29.2 3.8 %collective-permute-start.18 = (f32[24,128]{1,0:T(8,128)S(1)}, f32[24,128]{1,0:T(8,128)S(1)}, u32[]{:S(2)}, u32[]{:S(2)}) collective-permute-start(f32[24,128]{1,0:T(8,128)S(1)} %add.12), channel_id=1, source_target_pairs={{0,5},{1,4},{2,7},{3,6},{4,1},{5,0},{6,3},{7,2},{8,13},{9,12},{10,... | collective-permute-start | bytes 36872 | tf_op jit(solution)/shard_map/ppermute | solution.py:340
  29.9 3.3 %collective-permute-start.17 = (f32[24,128]{1,0:T(8,128)S(1)}, f32[24,128]{1,0:T(8,128)S(1)}, u32[]{:S(2)}, u32[]{:S(2)}) collective-permute-start(f32[24,128]{1,0:T(8,128)S(1)} %add.12), channel_id=1, source_target_pairs={{0,3},{1,2},{2,1},{3,0},{4,7},{5,6},{6,5},{7,4},{8,11},{9,10},{10,... | collective-permute-start | bytes 36872 | tf_op jit(solution)/shard_map/ppermute | solution.py:340
  33.3 4.9 %collective-permute-start.22 = (f32[24,128]{1,0:T(8,128)S(1)}, f32[24,128]{1,0:T(8,128)S(1)}, u32[]{:S(2)}, u32[]{:S(2)}) collective-permute-start(f32[24,128]{1,0:T(8,128)S(1)} %add_add_fusion.refs_0_), channel_id=1, source_target_pairs={{0,25},{1,24},{2,27},{3,26},{4,29},{5,28},{6,31},{7,30},{8,17},{9,... | collective-permute-start | bytes 36872 | tf_op jit(solution)/shard_map/ppermute | solution.py:340
  34.9 4.1 %collective-permute-start.21 = (f32[24,128]{1,0:T(8,128)S(1)}, f32[24,128]{1,0:T(8,128)S(1)}, u32[]{:S(2)}, u32[]{:S(2)}) collective-permute-start(f32[24,128]{1,0:T(8,128)S(1)} %add_add_fusion.refs_0_), channel_id=1, source_target_pairs={{0,17},{1,16},{2,19},{3,18},{4,21},{5,20},{6,23},{7,22},{8,25},{9,... | collective-permute-start | bytes 36872 | tf_op jit(solution)/shard_map/ppermute | solution.py:340
  35.2 3.7 %collective-permute-start.20 = (f32[24,128]{1,0:T(8,128)S(1)}, f32[24,128]{1,0:T(8,128)S(1)}, u32[]{:S(2)}, u32[]{:S(2)}) collective-permute-start(f32[24,128]{1,0:T(8,128)S(1)} %add_add_fusion.refs_0_), channel_id=1, source_target_pairs={{0,9},{1,8},{2,11},{3,10},{4,13},{5,12},{6,15},{7,14},{8,1},{9,0},... | collective-permute-start | bytes 36872 | tf_op jit(solution)/shard_map/ppermute | solution.py:340

commit v27 on v21

--- a/solution.py
+++ b/solution.py
@@ -284,17 +284,17 @@
     prev = prev_ref[...].reshape(width, rows)
     basis = jnp.concatenate([lines[...], last[...]], axis=0)
     projected = basis - dot(coefs[:, :width], prev, precision=HIGHEST)
-    unit, scale = {}, {}
+    unit, scale, entry = {}, {}, {}
     for l in range(S):
         for k in range(l, S):
             value = turned[k * 8 : (k + 1) * 8] * coef[l] + turned[l * 8 : (l + 1) * 8] * coef[k] + cross[k][l]
             value = jnp.sum(value, axis=1, keepdims=True)
             for m in range(l):
-                value = value - (unit[k, m] * scale[m]) * unit[l, m]
+                value = value - entry[k, m] * unit[l, m]
             if k == l:
-                scale[l] = value
+                scale[l] = entry[l, l] = value
             else:
-                unit[k, l] = value / scale[l]
+                entry[k, l], unit[k, l] = value, value / scale[l]
     roots = [jnp.sqrt(scale[k]) for k in range(S)]
     lower = {(k, l): unit[k, l] * roots[l] if l < k else roots[k] for k in range(S) for l in range(k + 1)}
     vectors = []

time: 40.1 us -> 40.1 us (level)
  no operation moved by 1% of the time
where the time goes in v27:
time: 40.1 us; the launch traced here: 39.9 us
  starting transfers between devices  20.9 us (52%)
  waiting for transfers between devices  13 us (32%)
  Pallas kernels  5.23 us (13%)
  between operations  0.72 us (2%)
    ppermute x23, starting transfers between devices, send(): lax.ppermute(value, 'dom', [(d, target[d]) for d in range(lax.axis_size('...  20.9 us
    ppermute x23, waiting for transfers between devices, send(): lax.ppermute(value, 'dom', [(d, target[d]) for d in range(lax.axis_size('...  13 us
    pallas_call x1, Pallas kernels, local(): call(prepare_kernel, [((width, rows), bf16), ((width, rows), bf16), ((8 *...  1.31 us
    pallas_call x1, Pallas kernels, local(): call(start_kernel, [((comps * blocks + 8, 128), f32)], [HBM] * 4, 600000,...  1.08 us
    pallas_call x1, Pallas kernels, local(): call(lambda *refs: finish_kernel(total, refs[:count], *refs[count:]), [((...  0.97 us
  transfers between devices with their start and end apart: 23, of which 12 were waited for; matrix products, arithmetic and copies ran while one was open for 0% of the time, Pallas kernels for 5%

profile of v27, /device:TPU:0, one launch (start us, length us, event | category | flops | bytes accessed | tf_op | source)
XLA Modules:
  0.0 39.9 jit_solution(10641955282165931977)
XLA Ops:
  0.6 1.1 %shard_map.86.refs_0_ = f32[32,128]{1,0:T(8,128)S(1)} custom-call(f32[3,32,512]{2,1,0:T(8,128)} %refs_4_.1, f32[3,32]{1,0:T(4,128)} %mix_in.1, s32[1,4,8]{2,1,0:T(4,128)} %list_in.1, s32[1,4]{1,0:T(1,128)} %count_in.1), custom_call_target="tpu_custom_call" | custom-call | flops 600000 | bytes 250000 | tf_op jit(solution)/shard_map/pallas_call | solution.py:395
  1.7 0.5 %collective-permute-start.3 = (f32[32,128]{1,0:T(8,128)S(1)}, f32[32,128]{1,0:T(8,128)S(1)}, u32[]{:S(2)}, u32[]{:S(2)}) collective-permute-start(f32[32,128]{1,0:T(8,128)S(1)} %shard_map.86.refs_0_), channel_id=1, source_target_pairs={{0,1},{1,2},{2,3},{3,0},{4,5},{5,4},{6,7},{7,6},{8,16},{9,17},{10,... | collective-permute-start | bytes 49160 | tf_op jit(solution)/shard_map/ppermute | solution.py:341
  2.2 2.5 %collective-permute-start.2 = (f32[32,128]{1,0:T(8,128)S(1)}, f32[32,128]{1,0:T(8,128)S(1)}, u32[]{:S(2)}, u32[]{:S(2)}) collective-permute-start(f32[32,128]{1,0:T(8,128)S(1)} %shard_map.86.refs_0_), channel_id=1, source_target_pairs={{0,2},{1,0},{2,1},{3,4},{4,3},{5,6},{6,5},{7,8},{8,7},{9,10},{10,9... | collective-permute-start | bytes 49160 | tf_op jit(solution)/shard_map/ppermute | solution.py:341
  4.8 2.5 %collective-permute-start.1 = (f32[32,128]{1,0:T(8,128)S(1)}, f32[32,128]{1,0:T(8,128)S(1)}, u32[]{:S(2)}, u32[]{:S(2)}) collective-permute-start(f32[32,128]{1,0:T(8,128)S(1)} %shard_map.86.refs_0_), channel_id=1, source_target_pairs={{0,8},{1,9},{2,10},{3,11},{4,12},{5,13},{6,14},{7,15},{8,0},{9,1},... | collective-permute-start | bytes 49160 | tf_op jit(solution)/shard_map/ppermute | solution.py:341
  7.2 0.5 %collective-permute-start = (f32[32,128]{1,0:T(8,128)S(1)}, f32[32,128]{1,0:T(8,128)S(1)}, u32[]{:S(2)}, u32[]{:S(2)}) collective-permute-start(f32[32,128]{1,0:T(8,128)S(1)} %shard_map.86.refs_0_), channel_id=1, source_target_pairs={{0,1},{1,0},{2,3},{3,2},{4,5},{5,4},{6,7},{7,6},{8,9},{9,8},{10,11... | collective-permute-start | bytes 49160 | tf_op jit(solution)/shard_map/ppermute | solution.py:341
  7.7 1.3 %shard_map.87 = (bf16[256,512]{1,0:T(8,128)(2,1)S(1)}, bf16[256,512]{1,0:T(8,128)(2,1)S(1)}, f32[56,128]{1,0:T(8,128)S(1)}) custom-call(f32[512,256]{1,0:T(8,128)} %strips_in.1, s32[4,8]{1,0:T(4,128)} %bitcast.2, f32[4]{0:T(128)} %shifts_in.1), custom_call_target="tpu_custom_call" | custom-call | flops 1000000 | bytes 1000000 | tf_op jit(solution)/shard_map/pallas_call | solution.py:409
  9.0 0.0 collective-permute-done.3.refs_4_
  9.0 0.0 collective-permute-done.2.refs_3_
  9.0 0.3 collective-permute-done.1.refs_2_
  9.3 0.0 collective-permute-done.refs_1_
  9.3 0.4 shard_map.88
  9.7 1.2 %collective-permute-start.7 = (f32[24,128]{1,0:T(8,128)S(1)}, f32[24,128]{1,0:T(8,128)S(1)}, u32[]{:S(2)}, u32[]{:S(2)}) collective-permute-start(f32[24,128]{1,0:T(8,128)S(1)} %get-tuple-element.19.refs_0_.t0), channel_id=1, source_target_pairs={{0,2},{1,0},{2,1},{3,4},{4,3},{5,6},{6,5},{7,8},{8,7},{9,10},{10,9... | collective-permute-start | bytes 36872 | tf_op jit(solution)/shard_map/ppermute | solution.py:341
  10.9 2.0 %collective-permute-start.6 = (f32[24,128]{1,0:T(8,128)S(1)}, f32[24,128]{1,0:T(8,128)S(1)}, u32[]{:S(2)}, u32[]{:S(2)}) collective-permute-start(f32[24,128]{1,0:T(8,128)S(1)} %get-tuple-element.19.refs_0_.t0), channel_id=1, source_target_pairs={{0,8},{1,9},{2,10},{3,11},{4,12},{5,13},{6,14},{7,15},{8,0},{9,1},... | collective-permute-start | bytes 36872 | tf_op jit(solution)/shard_map/ppermute | solution.py:341
  12.9 0.0 collective-permute-start.5
  12.9 0.1 collective-permute-start.4
  13.0 0.0 collective-permute-done.7.refs_4_
  13.0 1.7 %collective-permute-done.6.refs_3_ = f32[24,128]{1,0:T(8,128)S(1)} collective-permute-done((f32[24,128]{1,0:T(8,128)S(1)}, f32[24,128]{1,0:T(8,128)S(1)}, u32[]{:S(2)}, u32[]{:S(2)}) %collective-permute-start.6) | collective-permute-done | bytes 12320 | tf_op jit(solution)/shard_map/ppermute | solution.py:341
  14.7 1.3 %collective-permute-done.5.refs_2_ = f32[24,128]{1,0:T(8,128)S(1)} collective-permute-done((f32[24,128]{1,0:T(8,128)S(1)}, f32[24,128]{1,0:T(8,128)S(1)}, u32[]{:S(2)}, u32[]{:S(2)}) %collective-permute-start.5) | collective-permute-done | bytes 12320 | tf_op jit(solution)/shard_map/ppermute | solution.py:341
  16.0 0.0 collective-permute-done.4.refs_1_
  16.0 0.3 shard_map.89.refs_0_.t1
  16.3 0.0 copy-start
  16.3 0.1 collective-permute-start.11
  16.4 2.0 %collective-permute-start.10 = (f32[24,128]{1,0:T(8,128)S(1)}, f32[24,128]{1,0:T(8,128)S(1)}, u32[]{:S(2)}, u32[]{:S(2)}) collective-permute-start(f32[24,128]{1,0:T(8,128)S(1)} %shard_map.89.refs_0_.t1), channel_id=1, source_target_pairs={{0,8},{1,9},{2,10},{3,11},{4,12},{5,13},{6,14},{7,15},{8,0},{9,1},... | collective-permute-start | bytes 36872 | tf_op jit(solution)/shard_map/ppermute | solution.py:341
  18.4 0.0 collective-permute-start.9
  18.4 0.2 collective-permute-start.8
  18.6 0.0 collective-permute-done.11.refs_4_
  18.6 1.6 %collective-permute-done.10.refs_3_ = f32[24,128]{1,0:T(8,128)S(1)} collective-permute-done((f32[24,128]{1,0:T(8,128)S(1)}, f32[24,128]{1,0:T(8,128)S(1)}, u32[]{:S(2)}, u32[]{:S(2)}) %collective-permute-start.10) | collective-permute-done | bytes 12320 | tf_op jit(solution)/shard_map/ppermute | solution.py:341
  20.2 1.3 %collective-permute-done.9.refs_2_ = f32[24,128]{1,0:T(8,128)S(1)} collective-permute-done((f32[24,128]{1,0:T(8,128)S(1)}, f32[24,128]{1,0:T(8,128)S(1)}, u32[]{:S(2)}, u32[]{:S(2)}) %collective-permute-start.9) | collective-permute-done | bytes 12320 | tf_op jit(solution)/shard_map/ppermute | solution.py:341
  21.5 0.0 collective-permute-done.8.refs_1_
  21.5 0.3 shard_map.90.t2.refs_0_
  21.8 0.1 collective-permute-start.15
  22.0 2.1 %collective-permute-start.14 = (f32[24,128]{1,0:T(8,128)S(1)}, f32[24,128]{1,0:T(8,128)S(1)}, u32[]{:S(2)}, u32[]{:S(2)}) collective-permute-start(f32[24,128]{1,0:T(8,128)S(1)} %shard_map.90.t2.refs_0_), channel_id=1, source_target_pairs={{0,8},{1,9},{2,10},{3,11},{4,12},{5,13},{6,14},{7,15},{8,0},{9,1},... | collective-permute-start | bytes 36872 | tf_op jit(solution)/shard_map/ppermute | solution.py:341
  24.1 0.0 collective-permute-start.13
  24.1 0.0 collective-permute-start.12
  24.1 0.0 copy-done
  24.1 0.6 %shard_map.91 = (f32[24,512]{1,0:T(8,128)S(1)}, f32[24,128]{1,0:T(8,128)S(1)}, bf16[512,128]{1,0:T(8,128)(2,1)S(1)}, bf16[512,128]{1,0:T(8,128)(2,1)S(1)}, bf16[512,128]{1,0:T(8,128)(2,1)S(1)}) custom-call(f32[3,32,512]{2,1,0:T(8,128)S(1)} %copy-done, f32[24,128]{1,0:T(8,128)S(1)} %get-tuple-element.19.refs_0_.t0, f32[24,128]{1,0:T(8,128)S(1)} %shard_map.89.refs_0_.t1, ...), custom_call_target="tpu_custom_call" | custom-call | flops 60000000 | bytes 250000 | tf_op jit(solution)/shard_map/pallas_call | solution.py:440
  24.7 0.0 collective-permute-done.15.refs_4_
  24.7 1.2 %collective-permute-done.14.refs_3_ = f32[24,128]{1,0:T(8,128)S(1)} collective-permute-done((f32[24,128]{1,0:T(8,128)S(1)}, f32[24,128]{1,0:T(8,128)S(1)}, u32[]{:S(2)}, u32[]{:S(2)}) %collective-permute-start.14) | collective-permute-done | bytes 12320 | tf_op jit(solution)/shard_map/ppermute | solution.py:341
  25.9 1.3 %collective-permute-done.13.refs_2_ = f32[24,128]{1,0:T(8,128)S(1)} collective-permute-done((f32[24,128]{1,0:T(8,128)S(1)}, f32[24,128]{1,0:T(8,128)S(1)}, u32[]{:S(2)}, u32[]{:S(2)}) %collective-permute-start.13) | collective-permute-done | bytes 12320 | tf_op jit(solution)/shard_map/ppermute | solution.py:341
  27.2 0.0 collective-permute-done.12.refs_1_
  27.2 0.4 shard_map.92
  27.6 0.1 collective-permute-start.16
  27.7 1.2 %collective-permute-done.16 = f32[24,128]{1,0:T(8,128)S(1)} collective-permute-done((f32[24,128]{1,0:T(8,128)S(1)}, f32[24,128]{1,0:T(8,128)S(1)}, u32[]{:S(2)}, u32[]{:S(2)}) %collective-permute-start.16) | collective-permute-done | bytes 12320 | tf_op jit(solution)/shard_map/ppermute | solution.py:341
  28.9 0.4 collective-permute-start.19
  29.2 0.7 %collective-permute-start.18 = (f32[24,128]{1,0:T(8,128)S(1)}, f32[24,128]{1,0:T(8,128)S(1)}, u32[]{:S(2)}, u32[]{:S(2)}) collective-permute-start(f32[24,128]{1,0:T(8,128)S(1)} %add.12), channel_id=1, source_target_pairs={{0,5},{1,4},{2,7},{3,6},{4,1},{5,0},{6,3},{7,2},{8,13},{9,12},{10,... | collective-permute-start | bytes 36872 | tf_op jit(solution)/shard_map/ppermute | solution.py:341
  29.9 1.9 %collective-permute-start.17 = (f32[24,128]{1,0:T(8,128)S(1)}, f32[24,128]{1,0:T(8,128)S(1)}, u32[]{:S(2)}, u32[]{:S(2)}) collective-permute-start(f32[24,128]{1,0:T(8,128)S(1)} %add.12), channel_id=1, source_target_pairs={{0,3},{1,2},{2,1},{3,0},{4,7},{5,6},{6,5},{7,4},{8,11},{9,10},{10,... | collective-permute-start | bytes 36872 | tf_op jit(solution)/shard_map/ppermute | solution.py:341
  31.8 1.1 %collective-permute-done.19 = f32[24,128]{1,0:T(8,128)S(1)} collective-permute-done((f32[24,128]{1,0:T(8,128)S(1)}, f32[24,128]{1,0:T(8,128)S(1)}, u32[]{:S(2)}, u32[]{:S(2)}) %collective-permute-start.19) | collective-permute-done | bytes 12320 | tf_op jit(solution)/shard_map/ppermute | solution.py:341
  33.0 0.0 collective-permute-done.18
  33.0 0.3 collective-permute-done.17
  33.3 1.6 %collective-permute-start.22 = (f32[24,128]{1,0:T(8,128)S(1)}, f32[24,128]{1,0:T(8,128)S(1)}, u32[]{:S(2)}, u32[]{:S(2)}) collective-permute-start(f32[24,128]{1,0:T(8,128)S(1)} %add_add_fusion.refs_0_), channel_id=1, source_target_pairs={{0,25},{1,24},{2,27},{3,26},{4,29},{5,28},{6,31},{7,30},{8,17},{9,... | collective-permute-start | bytes 36872 | tf_op jit(solution)/shard_map/ppermute | solution.py:341
  34.9 0.3 collective-permute-start.21
  35.2 2.1 %collective-permute-start.20 = (f32[24,128]{1,0:T(8,128)S(1)}, f32[24,128]{1,0:T(8,128)S(1)}, u32[]{:S(2)}, u32[]{:S(2)}) collective-permute-start(f32[24,128]{1,0:T(8,128)S(1)} %add_add_fusion.refs_0_), channel_id=1, source_target_pairs={{0,9},{1,8},{2,11},{3,10},{4,13},{5,12},{6,15},{7,14},{8,1},{9,0},... | collective-permute-start | bytes 36872 | tf_op jit(solution)/shard_map/ppermute | solution.py:341
  37.3 0.9 %collective-permute-done.22.refs_3_ = f32[24,128]{1,0:T(8,128)S(1)} collective-permute-done((f32[24,128]{1,0:T(8,128)S(1)}, f32[24,128]{1,0:T(8,128)S(1)}, u32[]{:S(2)}, u32[]{:S(2)}) %collective-permute-start.22) | collective-permute-done | bytes 12320 | tf_op jit(solution)/shard_map/ppermute | solution.py:341
  38.2 0.7 %collective-permute-done.21.refs_2_ = f32[24,128]{1,0:T(8,128)S(1)} collective-permute-done((f32[24,128]{1,0:T(8,128)S(1)}, f32[24,128]{1,0:T(8,128)S(1)}, u32[]{:S(2)}, u32[]{:S(2)}) %collective-permute-start.21) | collective-permute-done | bytes 12320 | tf_op jit(solution)/shard_map/ppermute | solution.py:341
  38.9 0.0 collective-permute-done.20.refs_1_
  38.9 1.0 %shard_map.93 = (f32[3,4,512]{2,1,0:T(4,128)}, f32[3,4,36]{2,1,0:T(4,128)}) custom-call(f32[24,128]{1,0:T(8,128)S(1)} %add_add_fusion.refs_0_, f32[24,128]{1,0:T(8,128)S(1)} %collective-permute-done.20.refs_1_, f32[24,128]{1,0:T(8,128)S(1)} %collective-permute-done.21.refs_2_, f32[24,128]{1,0:T(8,128)S(1)} %collective-permute-done.22.refs_3_, ...), custom_call_target="tpu_custom_call" | custom-call | flops 50000000 | bytes 400000 | tf_op jit(solution)/shard_map/pallas_call | solution.py:457
  (2 shorter events, 0.0 us)
Async XLA Ops:
  1.7 7.3 %collective-permute-start.3 = (f32[32,128]{1,0:T(8,128)S(1)}, f32[32,128]{1,0:T(8,128)S(1)}, u32[]{:S(2)}, u32[]{:S(2)}) collective-permute-start(f32[32,128]{1,0:T(8,128)S(1)} %shard_map.86.refs_0_), channel_id=1, source_target_pairs={{0,1},{1,2},{2,3},{3,0},{4,5},{5,4},{6,7},{7,6},{8,16},{9,17},{10,... | collective-permute-start | bytes 49160 | tf_op jit(solution)/shard_map/ppermute | solution.py:341
  2.2 6.8 %collective-permute-start.2 = (f32[32,128]{1,0:T(8,128)S(1)}, f32[32,128]{1,0:T(8,128)S(1)}, u32[]{:S(2)}, u32[]{:S(2)}) collective-permute-start(f32[32,128]{1,0:T(8,128)S(1)} %shard_map.86.refs_0_), channel_id=1, source_target_pairs={{0,2},{1,0},{2,1},{3,4},{4,3},{5,6},{6,5},{7,8},{8,7},{9,10},{10,9... | collective-permute-start | bytes 49160 | tf_op jit(solution)/shard_map/ppermute | solution.py:341
  4.8 4.5 %collective-permute-start.1 = (f32[32,128]{1,0:T(8,128)S(1)}, f32[32,128]{1,0:T(8,128)S(1)}, u32[]{:S(2)}, u32[]{:S(2)}) collective-permute-start(f32[32,128]{1,0:T(8,128)S(1)} %shard_map.86.refs_0_), channel_id=1, source_target_pairs={{0,8},{1,9},{2,10},{3,11},{4,12},{5,13},{6,14},{7,15},{8,0},{9,1},... | collective-permute-start | bytes 49160 | tf_op jit(solution)/shard_map/ppermute | solution.py:341
  7.2 2.1 %collective-permute-start = (f32[32,128]{1,0:T(8,128)S(1)}, f32[32,128]{1,0:T(8,128)S(1)}, u32[]{:S(2)}, u32[]{:S(2)}) collective-permute-start(f32[32,128]{1,0:T(8,128)S(1)} %shard_map.86.refs_0_), channel_id=1, source_target_pairs={{0,1},{1,0},{2,3},{3,2},{4,5},{5,4},{6,7},{7,6},{8,9},{9,8},{10,11... | collective-permute-start | bytes 49160 | tf_op jit(solution)/shard_map/ppermute | solution.py:341
  9.7 3.3 %collective-permute-start.7 = (f32[24,128]{1,0:T(8,128)S(1)}, f32[24,128]{1,0:T(8,128)S(1)}, u32[]{:S(2)}, u32[]{:S(2)}) collective-permute-start(f32[24,128]{1,0:T(8,128)S(1)} %get-tuple-element.19.refs_0_.t0), channel_id=1, source_target_pairs={{0,2},{1,0},{2,1},{3,4},{4,3},{5,6},{6,5},{7,8},{8,7},{9,10},{10,9... | collective-permute-start | bytes 36872 | tf_op jit(solution)/shard_map/ppermute | solution.py:341
  10.9 3.8 %collective-permute-start.6 = (f32[24,128]{1,0:T(8,128)S(1)}, f32[24,128]{1,0:T(8,128)S(1)}, u32[]{:S(2)}, u32[]{:S(2)}) collective-permute-start(f32[24,128]{1,0:T(8,128)S(1)} %get-tuple-element.19.refs_0_.t0), channel_id=1, source_target_pairs={{0,8},{1,9},{2,10},{3,11},{4,12},{5,13},{6,14},{7,15},{8,0},{9,1},... | collective-permute-start | bytes 36872 | tf_op jit(solution)/shard_map/ppermute | solution.py:341
  12.9 3.1 %collective-permute-start.5 = (f32[24,128]{1,0:T(8,128)S(1)}, f32[24,128]{1,0:T(8,128)S(1)}, u32[]{:S(2)}, u32[]{:S(2)}) collective-permute-start(f32[24,128]{1,0:T(8,128)S(1)} %get-tuple-element.19.refs_0_.t0), channel_id=1, source_target_pairs={{0,1},{1,2},{2,3},{3,0},{4,5},{5,4},{6,7},{7,6},{8,16},{9,17},{10,... | collective-permute-start | bytes 36872 | tf_op jit(solution)/shard_map/ppermute | solution.py:341
  12.9 3.1 %collective-permute-start.4 = (f32[24,128]{1,0:T(8,128)S(1)}, f32[24,128]{1,0:T(8,128)S(1)}, u32[]{:S(2)}, u32[]{:S(2)}) collective-permute-start(f32[24,128]{1,0:T(8,128)S(1)} %get-tuple-element.19.refs_0_.t0), channel_id=1, source_target_pairs={{0,1},{1,0},{2,3},{3,2},{4,5},{5,4},{6,7},{7,6},{8,9},{9,8},{10,11... | collective-permute-start | bytes 36872 | tf_op jit(solution)/shard_map/ppermute | solution.py:341
  16.3 7.8 %copy-start = (f32[3,32,512]{2,1,0:T(8,128)S(1)}, f32[3,32,512]{2,1,0:T(8,128)}, u32[]{:S(2)}) copy-start(f32[3,32,512]{2,1,0:T(8,128)} %refs_4_.1) | copy-start | bytes 589828
  16.3 2.3 %collective-permute-start.11 = (f32[24,128]{1,0:T(8,128)S(1)}, f32[24,128]{1,0:T(8,128)S(1)}, u32[]{:S(2)}, u32[]{:S(2)}) collective-permute-start(f32[24,128]{1,0:T(8,128)S(1)} %shard_map.89.refs_0_.t1), channel_id=1, source_target_pairs={{0,2},{1,0},{2,1},{3,4},{4,3},{5,6},{6,5},{7,8},{8,7},{9,10},{10,9... | collective-permute-start | bytes 36872 | tf_op jit(solution)/shard_map/ppermute | solution.py:341
  16.4 3.8 %collective-permute-start.10 = (f32[24,128]{1,0:T(8,128)S(1)}, f32[24,128]{1,0:T(8,128)S(1)}, u32[]{:S(2)}, u32[]{:S(2)}) collective-permute-start(f32[24,128]{1,0:T(8,128)S(1)} %shard_map.89.refs_0_.t1), channel_id=1, source_target_pairs={{0,8},{1,9},{2,10},{3,11},{4,12},{5,13},{6,14},{7,15},{8,0},{9,1},... | collective-permute-start | bytes 36872 | tf_op jit(solution)/shard_map/ppermute | solution.py:341
  18.4 3.1 %collective-permute-start.9 = (f32[24,128]{1,0:T(8,128)S(1)}, f32[24,128]{1,0:T(8,128)S(1)}, u32[]{:S(2)}, u32[]{:S(2)}) collective-permute-start(f32[24,128]{1,0:T(8,128)S(1)} %shard_map.89.refs_0_.t1), channel_id=1, source_target_pairs={{0,1},{1,2},{2,3},{3,0},{4,5},{5,4},{6,7},{7,6},{8,16},{9,17},{10,... | collective-permute-start | bytes 36872 | tf_op jit(solution)/shard_map/ppermute | solution.py:341
  18.4 3.1 %collective-permute-start.8 = (f32[24,128]{1,0:T(8,128)S(1)}, f32[24,128]{1,0:T(8,128)S(1)}, u32[]{:S(2)}, u32[]{:S(2)}) collective-permute-start(f32[24,128]{1,0:T(8,128)S(1)} %shard_map.89.refs_0_.t1), channel_id=1, source_target_pairs={{0,1},{1,0},{2,3},{3,2},{4,5},{5,4},{6,7},{7,6},{8,9},{9,8},{10,11... | collective-permute-start | bytes 36872 | tf_op jit(solution)/shard_map/ppermute | solution.py:341
  21.8 2.9 %collective-permute-start.15 = (f32[24,128]{1,0:T(8,128)S(1)}, f32[24,128]{1,0:T(8,128)S(1)}, u32[]{:S(2)}, u32[]{:S(2)}) collective-permute-start(f32[24,128]{1,0:T(8,128)S(1)} %shard_map.90.t2.refs_0_), channel_id=1, source_target_pairs={{0,2},{1,0},{2,1},{3,4},{4,3},{5,6},{6,5},{7,8},{8,7},{9,10},{10,9... | collective-permute-start | bytes 36872 | tf_op jit(solution)/shard_map/ppermute | solution.py:341
  22.0 3.9 %collective-permute-start.14 = (f32[24,128]{1,0:T(8,128)S(1)}, f32[24,128]{1,0:T(8,128)S(1)}, u32[]{:S(2)}, u32[]{:S(2)}) collective-permute-start(f32[24,128]{1,0:T(8,128)S(1)} %shard_map.90.t2.refs_0_), channel_id=1, source_target_pairs={{0,8},{1,9},{2,10},{3,11},{4,12},{5,13},{6,14},{7,15},{8,0},{9,1},... | collective-permute-start | bytes 36872 | tf_op jit(solution)/shard_map/ppermute | solution.py:341
  24.1 3.1 %collective-permute-start.13 = (f32[24,128]{1,0:T(8,128)S(1)}, f32[24,128]{1,0:T(8,128)S(1)}, u32[]{:S(2)}, u32[]{:S(2)}) collective-permute-start(f32[24,128]{1,0:T(8,128)S(1)} %shard_map.90.t2.refs_0_), channel_id=1, source_target_pairs={{0,1},{1,2},{2,3},{3,0},{4,5},{5,4},{6,7},{7,6},{8,16},{9,17},{10,... | collective-permute-start | bytes 36872 | tf_op jit(solution)/shard_map/ppermute | solution.py:341
  24.1 3.1 %collective-permute-start.12 = (f32[24,128]{1,0:T(8,128)S(1)}, f32[24,128]{1,0:T(8,128)S(1)}, u32[]{:S(2)}, u32[]{:S(2)}) collective-permute-start(f32[24,128]{1,0:T(8,128)S(1)} %shard_map.90.t2.refs_0_), channel_id=1, source_target_pairs={{0,1},{1,0},{2,3},{3,2},{4,5},{5,4},{6,7},{7,6},{8,9},{9,8},{10,11... | collective-permute-start | bytes 36872 | tf_op jit(solution)/shard_map/ppermute | solution.py:341
  27.6 1.2 %collective-permute-start.16 = (f32[24,128]{1,0:T(8,128)S(1)}, f32[24,128]{1,0:T(8,128)S(1)}, u32[]{:S(2)}, u32[]{:S(2)}) collective-permute-start(f32[24,128]{1,0:T(8,128)S(1)} %get-tuple-element.26), channel_id=1, source_target_pairs={{0,1},{1,0},{2,3},{3,2},{4,5},{5,4},{6,7},{7,6},{8,9},{9,8},{10,11... | collective-permute-start | bytes 36872 | tf_op jit(solution)/shard_map/ppermute | solution.py:341
  28.9 4.1 %collective-permute-start.19 = (f32[24,128]{1,0:T(8,128)S(1)}, f32[24,128]{1,0:T(8,128)S(1)}, u32[]{:S(2)}, u32[]{:S(2)}) collective-permute-start(f32[24,128]{1,0:T(8,128)S(1)} %add.12), channel_id=1, source_target_pairs={{0,7},{1,6},{2,5},{3,4},{4,3},{5,2},{6,1},{7,0},{8,15},{9,14},{10,... | collective-permute-start | bytes 36872 | tf_op jit(solution)/shard_map/ppermute | solution.py:341
  29.2 3.8 %collective-permute-start.18 = (f32[24,128]{1,0:T(8,128)S(1)}, f32[24,128]{1,0:T(8,128)S(1)}, u32[]{:S(2)}, u32[]{:S(2)}) collective-permute-start(f32[24,128]{1,0:T(8,128)S(1)} %add.12), channel_id=1, source_target_pairs={{0,5},{1,4},{2,7},{3,6},{4,1},{5,0},{6,3},{7,2},{8,13},{9,12},{10,... | collective-permute-start | bytes 36872 | tf_op jit(solution)/shard_map/ppermute | solution.py:341
  29.9 3.3 %collective-permute-start.17 = (f32[24,128]{1,0:T(8,128)S(1)}, f32[24,128]{1,0:T(8,128)S(1)}, u32[]{:S(2)}, u32[]{:S(2)}) collective-permute-start(f32[24,128]{1,0:T(8,128)S(1)} %add.12), channel_id=1, source_target_pairs={{0,3},{1,2},{2,1},{3,0},{4,7},{5,6},{6,5},{7,4},{8,11},{9,10},{10,... | collective-permute-start | bytes 36872 | tf_op jit(solution)/shard_map/ppermute | solution.py:341
  33.3 4.9 %collective-permute-start.22 = (f32[24,128]{1,0:T(8,128)S(1)}, f32[24,128]{1,0:T(8,128)S(1)}, u32[]{:S(2)}, u32[]{:S(2)}) collective-permute-start(f32[24,128]{1,0:T(8,128)S(1)} %add_add_fusion.refs_0_), channel_id=1, source_target_pairs={{0,25},{1,24},{2,27},{3,26},{4,29},{5,28},{6,31},{7,30},{8,17},{9,... | collective-permute-start | bytes 36872 | tf_op jit(solution)/shard_map/ppermute | solution.py:341
  34.9 4.1 %collective-permute-start.21 = (f32[24,128]{1,0:T(8,128)S(1)}, f32[24,128]{1,0:T(8,128)S(1)}, u32[]{:S(2)}, u32[]{:S(2)}) collective-permute-start(f32[24,128]{1,0:T(8,128)S(1)} %add_add_fusion.refs_0_), channel_id=1, source_target_pairs={{0,17},{1,16},{2,19},{3,18},{4,21},{5,20},{6,23},{7,22},{8,25},{9,... | collective-permute-start | bytes 36872 | tf_op jit(solution)/shard_map/ppermute | solution.py:341
  35.2 3.7 %collective-permute-start.20 = (f32[24,128]{1,0:T(8,128)S(1)}, f32[24,128]{1,0:T(8,128)S(1)}, u32[]{:S(2)}, u32[]{:S(2)}) collective-permute-start(f32[24,128]{1,0:T(8,128)S(1)} %add_add_fusion.refs_0_), channel_id=1, source_target_pairs={{0,9},{1,8},{2,11},{3,10},{4,13},{5,12},{6,15},{7,14},{8,1},{9,0},... | collective-permute-start | bytes 36872 | tf_op jit(solution)/shard_map/ppermute | solution.py:341
